TPU v7x, 32 devices: a whole 2x2x4 slice. The times are simulated.
32 devices in a mesh: fsdp: 8 (over y, x, core), seq: 4 (over z).
Axes of the slice: x: 2, y: 2, z: 4, core: 2. Of those that a mesh axis runs over, the one named last changes fastest.
Arguments:
- inputs: bfloat16 [8, 2048, 1536], P('fsdp', 'seq'), may hold values from -6 to 6
- teacher: bfloat16 [8, 2048, 1536], P('fsdp', 'seq'), may hold values from -6 to 6
- routes: int32 [8, 2048, 8], P('fsdp', 'seq'), may hold values from 0 to 39, all different within a row; in each aligned block of 512 rows (0 to 511, 512 to 1023, ..., all dimensions but the last counted through in order) at most 153 rows name the same one
- valid_mask: int32 [8, 2048], P('fsdp', 'seq'), may hold values from 0 to 1, as said below
- block_lengths: int32 [8, 16], P('fsdp'), may hold values from 1 to 256, 2048 in all within a row
- gain_one: bfloat16 [1536], P('fsdp'), may hold values from 0.5 to 1.5
- w_qkv: bfloat16 [1536, 2560], P('fsdp'), may hold values from -0.5 to 0.5
- w_out: bfloat16 [1536, 1536], P('fsdp'), may hold values from -2.5 to 2.5
- gain_two: bfloat16 [1536], P('fsdp'), may hold values from 0.5 to 1.5
- w_router: bfloat16 [1536, 40], P('fsdp'), may hold values from -0.078125 to 0.078125
- w_gate: bfloat16 [40, 1536, 512], P('seq', 'fsdp'), may hold values from -0.3125 to 0.3125
- w_up: bfloat16 [40, 1536, 512], P('seq', 'fsdp'), may hold values from -0.3125 to 0.3125
- w_down: bfloat16 [40, 512, 1536], P('seq', 'fsdp'), may hold values from -1 to 1
Outputs:
- activations: bfloat16 [8, 2048, 1536], P('fsdp', 'seq')
- loss: float32 [], replicated
- input_grad: float32 [8, 2048, 1536], P('fsdp', 'seq')
- gain_one_grad: float32 [1536], P('fsdp')
- qkv_grad: float32 [1536, 2560], P('fsdp')
- out_grad: float32 [1536, 1536], P('fsdp')
- gain_two_grad: float32 [1536], P('fsdp')
- router_grad: float32 [1536, 40], P('fsdp')
- gate_grad: float32 [40, 1536, 512], P('seq', 'fsdp')
- up_grad: float32 [40, 1536, 512], P('seq', 'fsdp')
- down_grad: float32 [40, 512, 1536], P('seq', 'fsdp')
Inputs may be any that keep to these rules, and one draw needn't show every extreme that they name: In each aligned block of 512 rows (one sequence's positions on one index of seq), no expert is named by more than 153 routes; in some block one expert is named by exactly 153; a token's 8 experts differ. `block_lengths`: each row sums to 2048, and its longest block is 256. `valid_mask`: 1 marks a token that the loss counts.
All inputs are finite; a program needn't handle non-finite values.
Results may differ from a plain program's by a relative error of at most 0.019.
Values may be sent and summed in bfloat16 or wider, within the bound.
No kernel may reach another device: no remote copies, remote signals or barrier semaphores. Data moves between devices by JAX's collectives and lax.ppermute only.
A program may use at most 512 MiB of HBM per device.

v0:
```python
from functools import partial

import jax
import jax.numpy as jnp
from jax import lax
from jax.sharding import PartitionSpec as P

HEADS = 24
KV_HEADS = 8
HEAD_DIM = 64
BLOCK = 256
GROUP = 3
QKV_W = 2560


epsilon = 1e-06
attn_mult = 0.015625
resid_mult = 0.22
rope_base = 10000.0
masked_score = -1e30


def rms_norm(values, gain_vec):
    inv_rms = lax.rsqrt(jnp.mean(values * values, axis=-1, keepdims=True) + epsilon)
    return values * inv_rms * gain_vec


def rope_tables(positions, head_dim):
    half_dim = head_dim // 2
    frequency = rope_base ** (-(2.0 * jnp.arange(half_dim, dtype=jnp.float32)) / head_dim)
    angles = positions[:, None] * frequency[None, :]
    return (jnp.cos(angles), jnp.sin(angles))


def rotate(values, cosine, sine_vals):
    half_dim = values.shape[-1] // 2
    front_half = values[..., :half_dim]
    back_half = values[..., half_dim:]
    return jnp.concatenate(
        [front_half * cosine - back_half * sine_vals, back_half * cosine + front_half * sine_vals],
        axis=-1,
    )


def block_ids(lengths_row, positions):
    block_ends = jnp.cumsum(lengths_row)
    return jnp.sum((positions[:, None] >= block_ends[None, :]).astype(jnp.int32), axis=1)


def route_slots(route_block, expert_count):
    flat_ids = route_block.reshape(-1)
    onehot = (flat_ids[:, None] == jnp.arange(expert_count, dtype=jnp.int32)[None, :]).astype(
        jnp.int32
    )
    rank_ids = jnp.cumsum(onehot, axis=0) - 1
    return jnp.sum(rank_ids * onehot, axis=1).reshape(route_block.shape)


def slot_table(route_block, slot_ids, expert_count, capacity):
    row_total = route_block.shape[0]
    token_ids = jnp.broadcast_to(jnp.arange(row_total, dtype=jnp.int32)[:, None], route_block.shape)
    slot_map = jnp.full((expert_count, capacity), row_total, jnp.int32)
    return slot_map.at[route_block.reshape(-1), slot_ids.reshape(-1)].set(token_ids.reshape(-1))


def swiglu(gate_act, up_act):
    return jax.nn.silu(gate_act) * up_act


def shards(
    inputs,
    teacher,
    routes,
    valid_mask,
    block_lengths,
    gain_one,
    w_qkv,
    w_out,
    gain_two,
    w_router,
    w_gate,
    w_up,
    w_down,
):
    seq_devs = lax.axis_size("seq")
    seqs_here, shard_len, model_width = inputs.shape
    seq_len = shard_len * seq_devs
    tokens_all = seqs_here * lax.axis_size("fsdp") * seq_len
    kv_here = KV_HEADS // seq_devs
    expert_total = w_gate.shape[0] * seq_devs
    top_count = routes.shape[2]
    capacity = 3 * shard_len * top_count // (2 * expert_total)
    row_count = seqs_here * shard_len
    slot_rows = seqs_here * capacity
    gathered = (
        lax.all_gather(gain_one, "fsdp", axis=0, tiled=True),
        lax.all_gather(w_qkv, "fsdp", axis=0, tiled=True),
        lax.all_gather(w_out, "fsdp", axis=0, tiled=True),
        lax.all_gather(gain_two, "fsdp", axis=0, tiled=True),
        lax.all_gather(w_router, "fsdp", axis=0, tiled=True),
        lax.all_gather(w_gate, "fsdp", axis=1, tiled=True),
        lax.all_gather(w_up, "fsdp", axis=1, tiled=True),
        lax.all_gather(w_down, "fsdp", axis=1, tiled=True),
    )
    full_g1, full_qkv, full_out, full_g2, full_router, full_gate, full_up, full_down = gathered
    x_rows = inputs.astype(jnp.float32).reshape(row_count, model_width)
    normed_one, norm_one_pull = jax.vjp(rms_norm, x_rows, full_g1.astype(jnp.float32))
    normed_low = normed_one.astype(jnp.bfloat16)
    qkv_rows = jnp.dot(normed_low, full_qkv, preferred_element_type=jnp.float32)
    qkv_rows = qkv_rows.reshape(seqs_here, shard_len, KV_HEADS, GROUP + 2, HEAD_DIM)
    positions = lax.axis_index("seq") * shard_len + jnp.arange(shard_len, dtype=jnp.int32)
    cosine, sine_vals = rope_tables(positions.astype(jnp.float32), HEAD_DIM)
    cos_rows = cosine[None, :, None, None, :]
    sin_rows = sine_vals[None, :, None, None, :]
    turned = rotate(qkv_rows[:, :, :, : GROUP + 1], cos_rows, sin_rows)
    packed = jnp.concatenate([turned, qkv_rows[:, :, :, GROUP + 1 :]], axis=3).astype(jnp.bfloat16)
    packed = packed.reshape(seqs_here, shard_len, KV_HEADS, (GROUP + 2) * HEAD_DIM)
    head_rows = lax.all_to_all(packed, "seq", split_axis=2, concat_axis=1, tiled=True)
    head_rows = head_rows.reshape(seqs_here, seq_len, kv_here, GROUP + 2, HEAD_DIM)
    head_query = head_rows[:, :, :, :GROUP]
    head_key = head_rows[:, :, :, GROUP]
    head_value = head_rows[:, :, :, GROUP + 1]
    seq_positions = jnp.arange(seq_len, dtype=jnp.int32)
    blocks = jax.vmap(block_ids, in_axes=(0, None))(block_lengths, seq_positions)
    query_rows = min(512, seq_len)
    row_starts = list(range(0, seq_len, query_rows))

    def masked_scores(row_start, row_stop):
        query_blk = head_query[:, row_start : row_start + query_rows]
        scores = (
            jnp.einsum(
                "sqghd,skgd->sghqk",
                query_blk,
                head_key[:, :row_stop],
                preferred_element_type=jnp.float32,
            )
            * attn_mult
        )
        allowed = (
            blocks[:, None, None, None, :row_stop]
            <= blocks[:, None, None, row_start : row_start + query_rows, None]
        )
        return jnp.where(allowed, scores, masked_score)

    attended_list = []
    lse_list = []
    for row_start in row_starts:
        row_stop = min(seq_len, row_start + query_rows + BLOCK)
        scores = masked_scores(row_start, row_stop)
        row_peak = jnp.max(scores, axis=-1, keepdims=True)
        exp_rows = jnp.exp(scores - row_peak)
        exp_sum = jnp.sum(exp_rows, axis=-1, keepdims=True)
        prob_low = (exp_rows / exp_sum).astype(jnp.bfloat16)
        attended_list.append(
            jnp.einsum(
                "sghqk,skgd->sqghd",
                prob_low,
                head_value[:, :row_stop],
                preferred_element_type=jnp.float32,
            )
        )
        lse_list.append(row_peak + jnp.log(exp_sum))
    attended = jnp.concatenate(attended_list, axis=1).astype(jnp.bfloat16)
    attended = attended.reshape(seqs_here, seq_len, kv_here, GROUP * HEAD_DIM)
    back_rows = lax.all_to_all(attended, "seq", split_axis=1, concat_axis=2, tiled=True)
    attn_rows = back_rows.reshape(row_count, HEADS * HEAD_DIM)
    projected = jnp.dot(attn_rows, full_out, preferred_element_type=jnp.float32)
    hidden = x_rows + resid_mult * projected
    normed_two, norm_two_pull = jax.vjp(rms_norm, hidden, full_g2.astype(jnp.float32))
    router_in = normed_two.astype(jnp.bfloat16)
    logits = jnp.dot(router_in, full_router, preferred_element_type=jnp.float32)
    route_rows = routes.reshape(row_count, top_count)
    expert_ids = jnp.arange(expert_total, dtype=jnp.int32)
    onehot = (route_rows[:, :, None] == expert_ids[None, None, :]).astype(jnp.float32)

    def gate_softmax(logit_rows):
        chosen = jnp.sum(onehot * logit_rows[:, None, :], axis=2)
        return jax.nn.softmax(chosen, axis=-1)

    gate_vals, gate_pull = jax.vjp(gate_softmax, logits)
    slot_ids = jax.vmap(partial(route_slots, expert_count=expert_total))(routes)
    tables = jax.vmap(
        partial(slot_table, expert_count=expert_total, capacity=capacity), out_axes=1
    )(routes, slot_ids)
    tables = tables + (jnp.arange(seqs_here, dtype=jnp.int32) * (shard_len + 1))[None, :, None]
    padded = jnp.concatenate(
        [
            router_in.reshape(seqs_here, shard_len, model_width),
            jnp.zeros((seqs_here, 1, model_width), jnp.bfloat16),
        ],
        axis=1,
    )
    padded = padded.reshape(seqs_here * (shard_len + 1), model_width)
    send_rows = padded[tables].reshape(expert_total, slot_rows, model_width)
    expert_in = lax.all_to_all(send_rows, "seq", split_axis=0, concat_axis=1, tiled=True)
    gate_act = jnp.einsum("erd,edf->erf", expert_in, full_gate, preferred_element_type=jnp.float32)
    up_act = jnp.einsum("erd,edf->erf", expert_in, full_up, preferred_element_type=jnp.float32)
    act_out, act_pull = jax.vjp(swiglu, gate_act, up_act)
    act_low = act_out.astype(jnp.bfloat16)
    expert_out = jnp.einsum(
        "erf,efd->erd", act_low, full_down, preferred_element_type=jnp.float32
    ).astype(jnp.bfloat16)
    returned = lax.all_to_all(expert_out, "seq", split_axis=1, concat_axis=0, tiled=True)
    flat_returned = returned.reshape(expert_total * slot_rows, model_width)
    block_of = (jnp.arange(row_count, dtype=jnp.int32) // shard_len)[:, None]
    flat_index = (
        route_rows * slot_rows + block_of * capacity + slot_ids.reshape(row_count, top_count)
    )
    picked = flat_returned[flat_index].astype(jnp.float32)
    mixture = jnp.sum(gate_vals[:, :, None] * picked, axis=1)
    output_f32 = hidden + resid_mult * mixture
    activations = output_f32.astype(jnp.bfloat16).reshape(seqs_here, shard_len, model_width)
    valid_rows = valid_mask.reshape(row_count).astype(jnp.float32)
    error_rows = output_f32 - teacher.astype(jnp.float32).reshape(row_count, model_width)
    weighted = valid_rows[:, None] * error_rows
    valid_count, squares = lax.psum(
        (jnp.sum(valid_rows), jnp.sum(weighted * error_rows)), ("fsdp", "seq")
    )
    loss_value = squares / (valid_count * model_width)
    d_out = weighted * (tokens_all / valid_count)
    back_weights = (
        lax.all_gather(gain_one, "fsdp", axis=0, tiled=True),
        lax.all_gather(w_qkv, "fsdp", axis=0, tiled=True),
        lax.all_gather(w_out, "fsdp", axis=0, tiled=True),
        lax.all_gather(gain_two, "fsdp", axis=0, tiled=True),
        lax.all_gather(w_router, "fsdp", axis=0, tiled=True),
        lax.all_gather(w_gate, "fsdp", axis=1, tiled=True),
        lax.all_gather(w_up, "fsdp", axis=1, tiled=True),
        lax.all_gather(w_down, "fsdp", axis=1, tiled=True),
    )
    back_qkv = back_weights[1]
    back_out = back_weights[2]
    back_router = back_weights[4]
    back_gate = back_weights[5]
    back_up = back_weights[6]
    back_down = back_weights[7]
    d_mix = resid_mult * d_out
    d_gates = jnp.sum(picked * d_mix[:, None, :], axis=2)
    d_picked = (gate_vals[:, :, None] * d_mix[:, None, :]).astype(jnp.bfloat16)
    grad_slots = (
        jnp.zeros((expert_total * slot_rows, model_width), jnp.bfloat16)
        .at[flat_index.reshape(-1)]
        .set(d_picked.reshape(row_count * top_count, model_width))
    )
    grad_slots = grad_slots.reshape(expert_total, slot_rows, model_width)
    grad_expert = lax.all_to_all(grad_slots, "seq", split_axis=0, concat_axis=1, tiled=True)
    d_act = jnp.einsum("erd,efd->erf", grad_expert, back_down, preferred_element_type=jnp.float32)
    down_part = jnp.einsum("erf,erd->efd", act_low, grad_expert, preferred_element_type=jnp.float32)
    d_gate_act, d_up_act = act_pull(d_act)
    d_gate_low = d_gate_act.astype(jnp.bfloat16)
    d_up_low = d_up_act.astype(jnp.bfloat16)
    gate_part = jnp.einsum(
        "erd,erf->edf", expert_in, d_gate_low, preferred_element_type=jnp.float32
    )
    up_part = jnp.einsum("erd,erf->edf", expert_in, d_up_low, preferred_element_type=jnp.float32)
    d_expert_in = jnp.einsum(
        "erf,edf->erd", d_gate_low, back_gate, preferred_element_type=jnp.float32
    )
    d_expert_in = (
        d_expert_in
        + jnp.einsum("erf,edf->erd", d_up_low, back_up, preferred_element_type=jnp.float32)
    ).astype(jnp.bfloat16)
    grad_rows = lax.all_to_all(d_expert_in, "seq", split_axis=1, concat_axis=0, tiled=True)
    grad_rows = grad_rows.reshape(expert_total * slot_rows, model_width)
    d_logits = gate_pull(d_gates)[0].astype(jnp.bfloat16)
    router_part = jnp.einsum("td,te->de", router_in, d_logits, preferred_element_type=jnp.float32)
    d_normed_two = jnp.sum(grad_rows[flat_index].astype(jnp.float32), axis=1)
    d_normed_two = d_normed_two + jnp.einsum(
        "te,de->td", d_logits, back_router, preferred_element_type=jnp.float32
    )
    d_hidden_norm, gain_two_part = norm_two_pull(d_normed_two)
    d_hidden = d_out + d_hidden_norm
    d_proj = (resid_mult * d_hidden).astype(jnp.bfloat16)
    out_part = jnp.einsum("ti,td->id", attn_rows, d_proj, preferred_element_type=jnp.float32)
    d_attended = jnp.einsum(
        "td,id->ti", d_proj, back_out, preferred_element_type=jnp.float32
    ).astype(jnp.bfloat16)
    d_heads = lax.all_to_all(
        d_attended.reshape(seqs_here, shard_len, KV_HEADS, GROUP * HEAD_DIM),
        "seq",
        split_axis=2,
        concat_axis=1,
        tiled=True,
    )
    d_heads = d_heads.reshape(seqs_here, seq_len, kv_here, GROUP, HEAD_DIM)
    key_grad = jnp.zeros((seqs_here, seq_len, kv_here, HEAD_DIM), jnp.float32)
    value_grad = jnp.zeros((seqs_here, seq_len, kv_here, HEAD_DIM), jnp.float32)
    query_grads = []
    for block_number, row_start in enumerate(row_starts):
        row_stop = min(seq_len, row_start + query_rows + BLOCK)
        scores = masked_scores(row_start, row_stop)
        prob_rows = jnp.exp(scores - lse_list[block_number])
        d_out_blk = d_heads[:, row_start : row_start + query_rows]
        d_probs = jnp.einsum(
            "sqghd,skgd->sghqk",
            d_out_blk,
            head_value[:, :row_stop],
            preferred_element_type=jnp.float32,
        )
        row_delta = jnp.sum(prob_rows * d_probs, axis=-1, keepdims=True)
        d_scores = (prob_rows * (d_probs - row_delta)).astype(jnp.bfloat16)
        query_blk = head_query[:, row_start : row_start + query_rows]
        query_grads.append(
            jnp.einsum(
                "sghqk,skgd->sqghd",
                d_scores,
                head_key[:, :row_stop],
                preferred_element_type=jnp.float32,
            )
            * attn_mult
        )
        key_grad = key_grad.at[:, :row_stop].add(
            jnp.einsum("sghqk,sqghd->skgd", d_scores, query_blk, preferred_element_type=jnp.float32)
            * attn_mult
        )
        value_grad = value_grad.at[:, :row_stop].add(
            jnp.einsum(
                "sghqk,sqghd->skgd",
                prob_rows.astype(jnp.bfloat16),
                d_out_blk,
                preferred_element_type=jnp.float32,
            )
        )
    query_grad = jnp.concatenate(query_grads, axis=1)
    d_packed = jnp.concatenate(
        [query_grad, key_grad[:, :, :, None], value_grad[:, :, :, None]], axis=3
    ).astype(jnp.bfloat16)
    d_packed = d_packed.reshape(seqs_here, seq_len, kv_here, (GROUP + 2) * HEAD_DIM)
    d_local = lax.all_to_all(d_packed, "seq", split_axis=1, concat_axis=2, tiled=True)
    d_local = d_local.reshape(seqs_here, shard_len, KV_HEADS, GROUP + 2, HEAD_DIM).astype(
        jnp.float32
    )
    d_turned = rotate(d_local[:, :, :, : GROUP + 1], cos_rows, -sin_rows)
    d_qkv = (
        jnp.concatenate([d_turned, d_local[:, :, :, GROUP + 1 :]], axis=3)
        .astype(jnp.bfloat16)
        .reshape(row_count, QKV_W)
    )
    qkv_part = jnp.einsum("td,tc->dc", normed_low, d_qkv, preferred_element_type=jnp.float32)
    d_normed_one = jnp.einsum("tc,dc->td", d_qkv, back_qkv, preferred_element_type=jnp.float32)
    d_input_norm, gain_one_part = norm_one_pull(d_normed_one)
    input_grad = (d_hidden + d_input_norm).reshape(seqs_here, shard_len, model_width)
    dense_parts = (
        lax.psum(gain_one_part.astype(jnp.bfloat16), "seq").astype(jnp.float32),
        lax.psum(qkv_part.astype(jnp.bfloat16), "seq").astype(jnp.float32),
        lax.psum(out_part.astype(jnp.bfloat16), "seq").astype(jnp.float32),
        lax.psum(gain_two_part.astype(jnp.bfloat16), "seq").astype(jnp.float32),
        lax.psum(router_part.astype(jnp.bfloat16), "seq").astype(jnp.float32),
    )
    reduced = (
        lax.psum_scatter(
            dense_parts[0].astype(jnp.bfloat16), "fsdp", scatter_dimension=0, tiled=True
        ).astype(jnp.float32),
        lax.psum_scatter(
            dense_parts[1].astype(jnp.bfloat16), "fsdp", scatter_dimension=0, tiled=True
        ).astype(jnp.float32),
        lax.psum_scatter(
            dense_parts[2].astype(jnp.bfloat16), "fsdp", scatter_dimension=0, tiled=True
        ).astype(jnp.float32),
        lax.psum_scatter(
            dense_parts[3].astype(jnp.bfloat16), "fsdp", scatter_dimension=0, tiled=True
        ).astype(jnp.float32),
        lax.psum_scatter(
            dense_parts[4].astype(jnp.bfloat16), "fsdp", scatter_dimension=0, tiled=True
        ).astype(jnp.float32),
        lax.psum_scatter(
            gate_part.astype(jnp.bfloat16), "fsdp", scatter_dimension=1, tiled=True
        ).astype(jnp.float32),
        lax.psum_scatter(
            up_part.astype(jnp.bfloat16), "fsdp", scatter_dimension=1, tiled=True
        ).astype(jnp.float32),
        lax.psum_scatter(
            down_part.astype(jnp.bfloat16), "fsdp", scatter_dimension=1, tiled=True
        ).astype(jnp.float32),
    )
    dense_shards = (reduced[0], reduced[1], reduced[2], reduced[3], reduced[4])
    return (
        activations,
        loss_value,
        input_grad,
        dense_shards[0],
        dense_shards[1],
        dense_shards[2],
        dense_shards[3],
        dense_shards[4],
        reduced[5],
        reduced[6],
        reduced[7],
    )


def solution(mesh):
    return jax.shard_map(
        shards,
        mesh=mesh,
        in_specs=(
            P("fsdp", "seq", None),
            P("fsdp", "seq", None),
            P("fsdp", "seq", None),
            P("fsdp", "seq"),
            P("fsdp", None),
            P("fsdp"),
            P("fsdp", None),
            P("fsdp", None),
            P("fsdp"),
            P("fsdp", None),
            P("seq", "fsdp", None),
            P("seq", "fsdp", None),
            P("seq", "fsdp", None),
        ),
        out_specs=(
            P("fsdp", "seq", None),
            P(),
            P("fsdp", "seq", None),
            P("fsdp"),
            P("fsdp", None),
            P("fsdp", None),
            P("fsdp"),
            P("fsdp", None),
            P("seq", "fsdp", None),
            P("seq", "fsdp", None),
            P("seq", "fsdp", None),
        ),
        check_vma=False,
    )
```

profile of v0, /device:TPU:0, one launch (start us, length us, event | category | flops | bytes accessed | tf_op | source)
XLA Modules:
  0.0 3681.1 jit_solution(8373944617494248218)
XLA Ops:
  13.1 16.4 all-reduce.8
  32.8 32.1 all-gather.7.cloned.1.call-done
  92.1 22.6 reduce-window.6
  124.5 25.4 all-to-all-done
  247.1 32.0 pad_maximum_fusion.2
  286.2 15.5 scatter_custom_fusion.1
  302.1 27.9 all-to-all-done.1
  345.4 28.4 gather_fusion
  373.8 16.8 reshape.1616
  398.8 423.5 %all-to-all-done.2 = bf16[40,153,1536]{2,1,0:T(8,128)(2,1)} async-done(((bf16[40,153,1536]{2,1,0:T(8,128)(2,1)}), bf16[40,153,1536]{2,1,0:T(8,128)(2,1)}, u32[]{:S(2)}, u32[]{:S(2)}) %all-to-all-start.2) | async-done | bytes 18800672 | tf_op jit(solution)/shard_map/all_to_all | solution.py:195
  822.3 16.4 copy.276
  838.7 17.7 all_to_all.97
  856.3 21.2 fusion.187
  877.5 26.8 multiply_convert_fusion.1
  904.4 19.6 convolution_convert_fusion
  924.0 36.8 copy.277
  971.0 666.1 %psum.50 = f32[]{:T(128)} all-reduce(f32[]{:T(128)} %convert_reduce_fusion.2), channel_id=1, replica_groups=mesh['fsdp'=8,'seq'=4] {'fsdp','seq'}, use_global_device_ids=true, to_apply=%region_23.24 | all-reduce | flops 1 | bytes 8 | tf_op jit(solution)/shard_map/psum | solution.py:216
  1665.4 23.5 copy.279
  1688.9 17.1 reshape.1617
  1706.0 34.1 gather_fusion.1
  1740.1 30.0 fusion
  1772.7 30.9 scatter_custom_fusion
  1803.7 16.9 reshape.1622
  1842.6 411.3 %all-to-all-done.4 = bf16[40,153,1536]{2,1,0:T(8,128)(2,1)} async-done(((bf16[40,153,1536]{2,1,0:T(8,128)(2,1)}), bf16[40,153,1536]{2,1,0:T(8,128)(2,1)}, u32[]{:S(2)}, u32[]{:S(2)}) %all-to-all-start.4) | async-done | bytes 18800672 | tf_op jit(solution)/shard_map/all_to_all | solution.py:246
  2253.9 16.5 copy.282
  2270.4 17.7 all_to_all.104
  2288.0 27.8 multiply_convert_fusion
  2315.8 20.2 convolution_convert_fusion.3
  2336.3 23.6 convolution_convert_fusion.2
  2359.9 22.8 fusion.188
  2382.8 27.6 add_convert_fusion
  2410.4 36.8 copy.283
  2457.1 24.1 convolution_convert_fusion.1
  2481.2 623.9 %all-to-all-done.5 = bf16[10,612,1536]{2,0,1:T(8,128)(2,1)} async-done(((bf16[10,612,1536]{2,0,1:T(8,128)(2,1)}), bf16[10,612,1536]{2,0,1:T(8,128)(2,1)}, u32[]{:S(2)}, u32[]{:S(2)}) %all-to-all-start.5) | async-done | bytes 18800672 | tf_op jit(solution)/shard_map/all_to_all | solution.py:263
  3105.2 23.5 copy.285
  3128.7 17.0 reshape.1623
  3145.7 34.1 gather_fusion.2
  3212.9 30.7 all-to-all-done.6
  3273.4 13.7 fusion.7
  3312.9 16.9 fusion.36
  3352.2 16.5 fusion.2
  3368.6 16.8 fusion.26
  3427.9 73.5 %all_to_all.120 = bf16[1,2048,2,320]{3,2,0,1:T(2,128)(2,1)} all-to-all(bf16[1,2048,2,320]{3,2,0,1:T(2,128)(2,1)S(1)} %copy.303), channel_id=1, replica_groups=mesh['fsdp'=8,'seq'=4] {'seq'}, dimensions={1} | all-to-all | bytes 5242880 | tf_op jit(solution)/shard_map/all_to_all | solution.py:329
  3543.8 38.0 %psum.49 = f32[]{:T(128)} all-reduce(f32[]{:T(128)} %get-tuple-element.127), channel_id=1, replica_groups=mesh['fsdp'=8,'seq'=4] {'fsdp','seq'}, use_global_device_ids=true, to_apply=%region_21.22 | all-reduce | flops 1 | bytes 8 | tf_op jit(solution)/shard_map/psum | solution.py:216
  3582.4 12.9 reduce-scatter.15.cloned.1.call-done
  3606.2 13.7 all-reduce.7
  3620.1 19.8 all-reduce.9
  3646.5 21.5 all-reduce.13.cloned.1.call-done
  (406 shorter events, 462.1 us)
Async XLA Ops:
  7.2 57.7 %all-gather.7.cloned.1.call-start = ((), (), s32[]{:S(2)}) async-start(), calls=%async_computation.14 | async-start | bytes 8847360 | tf_op jit(solution)/shard_map/all_gather | solution.py:97
  7.9 328.9 %all-gather.9.cloned.1.call-start = ((), (), s32[]{:S(2)}) async-start(), calls=%async_computation.15 | async-start | bytes 5308416 | tf_op jit(solution)/shard_map/all_gather | solution.py:98
  8.7 847.7 %all-gather.11.cloned.1.call-start = ((), (), s32[]{:S(2)}) async-start(), calls=%async_computation.16 | async-start | bytes 17694720 | tf_op jit(solution)/shard_map/all_gather | solution.py:101
  29.4 46.3 %copy-start.71 = (f32[1536]{0:T(1024)}, f32[1536]{0:T(1024)S(1)}, u32[]{:S(2)}) copy-start(f32[1536]{0:T(1024)S(1)} %convert_element_type.266) | copy-start | bytes 18436
  31.8 43.9 %copy-start.80 = (f32[512]{0:T(512)}, f32[512]{0:T(512)S(1)}, u32[]{:S(2)}) copy-start(f32[512]{0:T(512)S(1)} %fusion.176) | copy-start | bytes 6148
  32.8 50.2 %copy-start.40 = (f32[512,32]{0,1:T(8,128)}, f32[512,32]{0,1:T(8,128)S(1)}, u32[]{:S(2)}) copy-start(f32[512,32]{0,1:T(8,128)S(1)} %get-tuple-element.153) | copy-start | bytes 196612
  85.5 64.4 %all-to-all-start = ((bf16[1,512,8,320]{1,3,0,2:T(8,128)(2,1)}), bf16[1,512,8,320]{1,3,0,2:T(8,128)(2,1)S(1)}, u32[]{:S(2)}, u32[]{:S(2)}) async-start(bf16[1,512,8,320]{1,3,0,2:T(8,128)(2,1)} %bitcast.610), calls=%async_computation | async-start | bytes 5242880 | tf_op jit(solution)/shard_map/all_to_all | solution.py:118
  90.1 787.4 %all-gather.13.cloned.1.call-start = ((), (), s32[]{:S(2)}) async-start(), calls=%async_computation.17 | async-start | bytes 17694720 | tf_op jit(solution)/shard_map/all_gather | solution.py:102
  90.8 192.9 %copy-start.20 = (s32[1,512,8]{2,1,0:T(8,128)}, s32[1,512,8]{2,1,0:T(8,128)S(1)}, u32[]{:S(2)}) copy-start(s32[1,512,8]{2,1,0:T(8,128)S(1)} %copy.272) | copy-start | bytes 49156
  177.0 14.0 copy-start.9
  245.6 37.1 %copy-start.24 = (s32[1,40,32,128]{3,2,1,0:T(8,128)S(1)}, s32[1,40,32,128]{3,2,1,0:T(8,128)}, u32[]{:S(2)}) copy-start(s32[1,40,32,128]{3,2,1,0:T(8,128)} %reduce-window.6) | copy-start | bytes 1966084
  245.6 38.2 %copy-start.85 = (bf16[1536]{0:T(1024)(128)(2,1)S(1)}, bf16[1536]{0:T(1024)(128)(2,1)}, u32[]{:S(2)}) copy-start(bf16[1536]{0:T(1024)(128)(2,1)} %get-tuple-element.131) | copy-start | bytes 9220
  247.0 38.7 %copy-start.87 = (s32[3]{0:T(128)S(1)}, s32[3]{0:T(128)}, u32[]{:S(2)}) copy-start(s32[3]{0:T(128)} %constant.308) | copy-start | bytes 40
  247.0 38.8 %copy-start.86 = (s32[3]{0:T(128)S(1)}, s32[3]{0:T(128)}, u32[]{:S(2)}) copy-start(s32[3]{0:T(128)} %constant.311) | copy-start | bytes 40
  279.1 51.0 %all-to-all-start.1 = ((bf16[1,2048,2,192]{3,2,0,1:T(2,128)(2,1)}), bf16[1,2048,2,192]{3,2,0,1:T(2,128)(2,1)S(1)}, u32[]{:S(2)}, u32[]{:S(2)}) async-start(bf16[1,2048,2,192]{3,2,0,1:T(2,128)(2,1)} %pad_maximum_fusion.2), calls=%async_computation.1 | async-start | bytes 4194304 | tf_op jit(solution)/shard_map/all_to_all | solution.py:165
  283.8 59.5 %copy-start.47 = (f32[1536]{0:T(1024)}, f32[1536]{0:T(1024)S(1)}, u32[]{:S(2)}) copy-start(f32[1536]{0:T(1024)S(1)} %convert_element_type.275) | copy-start | bytes 18436
  343.4 30.5 copy-start.69
  390.6 431.7 %all-to-all-start.2 = ((bf16[40,153,1536]{2,1,0:T(8,128)(2,1)}), bf16[40,153,1536]{2,1,0:T(8,128)(2,1)}, u32[]{:S(2)}, u32[]{:S(2)}) async-start(bf16[40,153,1536]{2,1,0:T(8,128)(2,1)} %reshape.1616), calls=%async_computation.2 | async-start | bytes 39321600 | tf_op jit(solution)/shard_map/all_to_all | solution.py:195
  398.2 506.2 %all-gather.15.cloned.1.call-start = ((), (), s32[]{:S(2)}) async-start(), calls=%async_computation.18 | async-start | bytes 17694720 | tf_op jit(solution)/shard_map/all_gather | solution.py:103
  960.7 676.4 %copy-start.46 = (s32[4096]{0:T(1024)S(1)}, s32[4096]{0:T(1024)}, u32[]{:S(2)}) copy-start(s32[4096]{0:T(1024)} %copy-done.45) | copy-start | bytes 49156
  960.7 677.8 %copy-start.21 = (s32[1,512,8]{2,1,0:T(8,128)S(1)}, s32[1,512,8]{2,1,0:T(8,128)}, u32[]{:S(2)}) copy-start(s32[1,512,8]{2,1,0:T(8,128)} %copy-done.20) | copy-start | bytes 49156
  960.8 681.3 %copy-start.75 = (bf16[192,40]{0,1:T(8,128)(2,1)S(1)}, bf16[192,40]{0,1:T(8,128)(2,1)}, u32[]{:S(2)}) copy-start(bf16[192,40]{0,1:T(8,128)(2,1)} %param.42) | copy-start | bytes 46084
  960.8 700.1 %copy-start.4 = (f32[512,1536]{1,0:T(8,128)S(1)}, f32[512,1536]{1,0:T(8,128)}, u32[]{:S(2)}) copy-start(f32[512,1536]{1,0:T(8,128)} %copy-done.3) | copy-start | bytes 9437188
  960.8 700.1 %copy-start.48 = (f32[1536]{0:T(1024)S(1)}, f32[1536]{0:T(1024)}, u32[]{:S(2)}) copy-start(f32[1536]{0:T(1024)} %copy-done.47) | copy-start | bytes 18436
  960.8 704.6 %all-to-all-start.3 = ((bf16[10,612,1536]{2,0,1:T(8,128)(2,1)}), bf16[10,612,1536]{2,0,1:T(8,128)(2,1)}, u32[]{:S(2)}, u32[]{:S(2)}) async-start(bf16[10,612,1536]{2,0,1:T(8,128)(2,1)} %copy.277), calls=%async_computation.3 | async-start | bytes 60162048 | tf_op jit(solution)/shard_map/all_to_all | solution.py:203
  1659.5 46.5 %copy-start.10 = (s32[4096]{0:T(1024)}, s32[4096]{0:T(1024)S(1)}, u32[]{:S(2)}) copy-start(s32[4096]{0:T(1024)S(1)} %broadcast_clamp_fusion) | copy-start | bytes 49156
  1740.1 30.0 copy-start.13
  1740.1 30.0 copy-start.73
  1820.6 433.3 %all-to-all-start.4 = ((bf16[40,153,1536]{2,1,0:T(8,128)(2,1)}), bf16[40,153,1536]{2,1,0:T(8,128)(2,1)}, u32[]{:S(2)}, u32[]{:S(2)}) async-start(bf16[40,153,1536]{2,1,0:T(8,128)(2,1)} %reshape.1622), calls=%async_computation.4 | async-start | bytes 39321600 | tf_op jit(solution)/shard_map/all_to_all | solution.py:246
  1828.5 1700.9 %reduce-scatter.19.cloned.1.call-start = ((), (), s32[]{:S(2)}) async-start(), calls=%async_computation.24 | async-start | bytes 442368
  1842.6 1687.6 %reduce-scatter.9.cloned.1.call-start = ((), (), s32[]{:S(2)}) async-start(), calls=%async_computation.19 | async-start | bytes 17694720 | tf_op jit(solution)/shard_map/reduce_scatter | solution.py:366
  2336.0 1198.9 %reduce-scatter.11.cloned.1.call-start = ((), (), s32[]{:S(2)}) async-start(), calls=%async_computation.20 | async-start | bytes 17694720 | tf_op jit(solution)/shard_map/reduce_scatter | solution.py:369
  2447.1 658.0 %all-to-all-start.5 = ((bf16[10,612,1536]{2,0,1:T(8,128)(2,1)}), bf16[10,612,1536]{2,0,1:T(8,128)(2,1)}, u32[]{:S(2)}, u32[]{:S(2)}) async-start(bf16[10,612,1536]{2,0,1:T(8,128)(2,1)} %copy.283), calls=%async_computation.5 | async-start | bytes 60162048 | tf_op jit(solution)/shard_map/all_to_all | solution.py:263
  2456.7 1082.8 %reduce-scatter.13.cloned.1.call-start = ((), (), s32[]{:S(2)}) async-start(), calls=%async_computation.21 | async-start | bytes 17694720 | tf_op jit(solution)/shard_map/reduce_scatter | solution.py:372
  3128.7 17.0 copy-start.11
  3202.5 41.1 %all-to-all-start.6 = ((bf16[1,512,8,192]{1,3,0,2:T(8,128)(2,1)}), bf16[1,512,8,192]{1,3,0,2:T(8,128)(2,1)}, u32[]{:S(2)}, u32[]{:S(2)}) async-start(bf16[1,512,8,192]{1,3,0,2:T(8,128)(2,1)} %bitcast.616), calls=%async_computation.6 | async-start | bytes 3145728 | tf_op jit(solution)/shard_map/all_to_all | solution.py:278
  3206.9 375.5 %reduce-scatter.17.cloned.1.call-start = ((), (), s32[]{:S(2)}) async-start(), calls=%async_computation.23 | async-start | bytes 5308416 | tf_op jit(solution)/shard_map/reduce_scatter | solution.py:357
  3212.8 382.4 %reduce-scatter.15.cloned.1.call-start = ((), (), s32[]{:S(2)}) async-start(), calls=%async_computation.22 | async-start | bytes 8847360 | tf_op jit(solution)/shard_map/reduce_scatter | solution.py:354
  3247.6 39.5 %copy-start.12 = (bf16[1,2048,2,3,64]{1,4,3,2,0:T(8,128)(2,1)}, bf16[1,2048,2,3,64]{1,4,3,2,0:T(8,128)(2,1)S(1)}, u32[]{:S(2)}) copy-start(bf16[1,2048,2,3,64]{1,4,3,2,0:T(8,128)(2,1)S(1)} %reshape.1625) | copy-start | bytes 4718596
  3247.6 14.0 slice-start
  3312.8 18.9 slice-start.4
  3312.8 17.0 copy-start.29
  3312.8 18.9 slice-start.5
  3312.9 18.9 slice-start.6
  3312.9 18.9 slice-start.7
  3527.9 140.0 %all-reduce.13.cloned.1.call-start = ((), (), s32[]{:S(2)}) async-start(), calls=%async_computation.25 | async-start | bytes 3145728 | tf_op jit(solution)/shard_map/psum | solution.py:345
  3595.3 46.3 %copy-start.78 = (f32[512]{0:T(512)S(1)}, f32[512]{0:T(512)}, u32[]{:S(2)}) copy-start(f32[512]{0:T(512)} %copy-done.77) | copy-start | bytes 6148
  3595.3 46.3 %copy-start.19 = (f32[512,1536]{1,0:T(8,128)S(1)}, f32[512,1536]{1,0:T(8,128)}, u32[]{:S(2)}) copy-start(f32[512,1536]{1,0:T(8,128)} %copy-done.18) | copy-start | bytes 9437188
  (70 other events, 516.4 us)
Sparse Core Ops, SparseCore 0:
  9.9 54.9 all-gather.6
  66.8 38.9 all-gather.8
  107.6 85.4 all-gather.10
  194.9 85.4 all-gather.12
  400.6 85.9 all-gather.14
  1842.7 34.3 reduce-scatter.18
  2336.2 107.4 reduce-scatter.8
  2447.1 109.1 reduce-scatter.10
  2559.9 109.1 reduce-scatter.12
  3213.0 53.8 reduce-scatter.16
  3528.1 67.1 reduce-scatter.14
  3597.6 70.3 all-reduce.12
where the time goes:
time: 3690 us; the launch traced here: 3680 us
  waiting for transfers between devices  1610 us (44%)
  blocking collectives  838 us (23%)
  local copies, waits for them, and re-layouts  479 us (13%)
  matrix products  420 us (11%)
  other arithmetic  263 us (7%)
  starting transfers between devices  48.1 us (1%)
    psum x2, blocking collectives, shards(): lax.psum((jnp.sum(valid_rows), jnp.sum(weighted * error_rows)), ('fsdp',...  704 us
    all_to_all x1, waiting for transfers between devices, shards(): lax.all_to_all(d_expert_in, 'seq', split_axis=1, concat_axis=0, tiled=True)  624 us
    all_to_all x1, waiting for transfers between devices, shards(): lax.all_to_all(send_rows, 'seq', split_axis=0, concat_axis=1, tiled=True)  424 us
    all_to_all x1, waiting for transfers between devices, shards(): lax.all_to_all(grad_slots, 'seq', split_axis=0, concat_axis=1, tiled=True)  411 us
    another operation x7, other arithmetic  78.5 us
  transfers between devices with their start and end apart: 19, of which 9 were waited for; matrix products, arithmetic and copies ran while one was open for 24% of the time, Pallas kernels for 0%

commit v1 on v0

v1 whole, which is shorter than its diff:
```python
import jax
import jax.numpy as jnp
from jax import lax
from jax.sharding import PartitionSpec as P

HEADS = 24
KV_HEADS = 8
HEAD_DIM = 64
BLOCK = 256
GROUP = 3
QKV_W = 2560


epsilon = 1e-06
attn_mult = 0.015625
resid_mult = 0.22
rope_base = 10000.0
masked_score = -1e30

low = jnp.bfloat16
full = jnp.float32


def dot(spec, left, right):
    return jnp.einsum(spec, left, right, preferred_element_type=full)


def rms_norm(values, gain_vec):
    inv_rms = lax.rsqrt(jnp.mean(values * values, axis=-1, keepdims=True) + epsilon)
    return values * inv_rms * gain_vec


def rope_tables(positions, head_dim):
    half_dim = head_dim // 2
    frequency = rope_base ** (-(2.0 * jnp.arange(half_dim, dtype=full)) / head_dim)
    angles = positions[:, None] * frequency[None, :]
    return (jnp.cos(angles), jnp.sin(angles))


def rotate(values, cosine, sine_vals):
    half_dim = values.shape[-1] // 2
    front_half = values[..., :half_dim]
    back_half = values[..., half_dim:]
    return jnp.concatenate(
        [front_half * cosine - back_half * sine_vals, back_half * cosine + front_half * sine_vals],
        axis=-1,
    )


def block_ids(lengths_row, positions):
    block_ends = jnp.cumsum(lengths_row)
    return jnp.sum((positions[:, None] >= block_ends[None, :]).astype(jnp.int32), axis=1)


def swiglu(gate_act, up_act):
    return jax.nn.silu(gate_act) * up_act


def line_gather(block):
    n = lax.axis_size("seq")
    me = lax.axis_index("seq")
    rights, lefts = [block], [block]
    for k in range(1, n):
        rights.append(lax.ppermute(rights[-1], "seq", [(i, i + 1) for i in range(k - 1, n - 1)]))
        lefts.append(lax.ppermute(lefts[-1], "seq", [(i, i - 1) for i in range(1, n - k + 1)]))
    return [block] + [jnp.where(me >= k, rights[k], lefts[n - k]) for k in range(1, n)]


def line_scatter(parts):
    n = lax.axis_size("seq")
    right = left = None
    for k in range(n - 1, 0, -1):
        to_right, to_left = parts[n - k], parts[k]
        if right is not None:
            to_right = to_right + right.astype(full)
            to_left = to_left + left.astype(full)
        right = lax.ppermute(to_right.astype(low), "seq", [(i, i + 1) for i in range(n - k)])
        left = lax.ppermute(to_left.astype(low), "seq", [(i, i - 1) for i in range(k, n)])
    return parts[0] + (right.astype(full) + left.astype(full))


def by_place(blocks):
    n = lax.axis_size("seq")
    me = lax.axis_index("seq")
    return jnp.stack(blocks)[(me - jnp.arange(n)) % n]


def attention_forward(query, key, value, blocks, query_rows):
    seq_len = key.shape[0]
    attended_list = []
    lse_list = []
    for row_start in range(0, seq_len, query_rows):
        row_stop = min(seq_len, row_start + query_rows + BLOCK)
        scores = masked_scores(query, key, blocks, row_start, row_stop, query_rows)
        row_peak = jnp.max(scores, axis=-1, keepdims=True)
        exp_rows = jnp.exp(scores - row_peak)
        exp_sum = jnp.sum(exp_rows, axis=-1, keepdims=True)
        prob_low = (exp_rows / exp_sum).astype(low)
        attended_list.append(dot("ghqk,kgd->qghd", prob_low, value[:row_stop]))
        lse_list.append(row_peak + jnp.log(exp_sum))
    return jnp.concatenate(attended_list, axis=0).astype(low), lse_list


def masked_scores(query, key, blocks, row_start, row_stop, query_rows):
    query_blk = query[row_start : row_start + query_rows]
    scores = dot("qghd,kgd->ghqk", query_blk, key[:row_stop]) * attn_mult
    allowed = blocks[None, :row_stop] <= blocks[row_start : row_start + query_rows, None]
    return jnp.where(allowed, scores, masked_score)


def attention_backward(query, key, value, blocks, lse_list, d_heads, query_rows):
    seq_len, kv_here = key.shape[:2]
    key_grad = jnp.zeros((seq_len, kv_here, HEAD_DIM), full)
    value_grad = jnp.zeros((seq_len, kv_here, HEAD_DIM), full)
    query_grads = []
    for block_number, row_start in enumerate(range(0, seq_len, query_rows)):
        row_stop = min(seq_len, row_start + query_rows + BLOCK)
        scores = masked_scores(query, key, blocks, row_start, row_stop, query_rows)
        prob_rows = jnp.exp(scores - lse_list[block_number])
        d_out_blk = d_heads[row_start : row_start + query_rows]
        d_probs = dot("qghd,kgd->ghqk", d_out_blk, value[:row_stop])
        row_delta = jnp.sum(prob_rows * d_probs, axis=-1, keepdims=True)
        d_scores = (prob_rows * (d_probs - row_delta)).astype(low)
        query_blk = query[row_start : row_start + query_rows]
        query_grads.append(dot("ghqk,kgd->qghd", d_scores, key[:row_stop]) * attn_mult)
        key_grad = key_grad.at[:row_stop].add(
            dot("ghqk,qghd->kgd", d_scores, query_blk) * attn_mult
        )
        value_grad = value_grad.at[:row_stop].add(
            dot("ghqk,qghd->kgd", prob_rows.astype(low), d_out_blk)
        )
    return jnp.concatenate(query_grads, axis=0), key_grad, value_grad


def shards(
    inputs,
    teacher,
    routes,
    valid_mask,
    block_lengths,
    gain_one,
    w_qkv,
    w_out,
    gain_two,
    w_router,
    w_gate,
    w_up,
    w_down,
):
    seq_devs = lax.axis_size("seq")
    me = lax.axis_index("seq")
    seqs_here, shard_len, width = inputs.shape
    assert seqs_here == 1
    seq_len = shard_len * seq_devs
    tokens_all = lax.axis_size("fsdp") * seq_len
    kv_here = KV_HEADS // seq_devs
    heads_w = kv_here * GROUP * HEAD_DIM
    group_w = kv_here * (GROUP + 2) * HEAD_DIM
    experts_here = w_gate.shape[0]
    expert_total = experts_here * seq_devs
    top_count = routes.shape[2]
    capacity = 3 * shard_len * top_count // (2 * expert_total)
    slots = -(-capacity // 16) * 16
    x_low = inputs.reshape(shard_len, width)

    own_qkv = lax.dynamic_slice_in_dim(w_qkv, me * group_w, group_w, 1)
    small = jnp.concatenate(
        [gain_one[:, None], gain_two[:, None], w_router], axis=1
    )
    small = lax.all_gather(small, "fsdp", axis=0, tiled=True)
    full_qkv = lax.all_gather(own_qkv, "fsdp", axis=0, tiled=True)
    full_out = lax.all_gather(w_out, "fsdp", axis=0, tiled=True)
    full_gate = lax.all_gather(w_gate, "fsdp", axis=1, tiled=True)
    full_up = lax.all_gather(w_up, "fsdp", axis=1, tiled=True)
    full_down = lax.all_gather(w_down, "fsdp", axis=1, tiled=True)
    full_g1 = small[:, 0].astype(full)
    full_g2 = small[:, 1].astype(full)
    full_router = small[:, 2:]
    valid_rows = valid_mask.reshape(shard_len).astype(full)
    valid_count = lax.psum(jnp.sum(valid_rows), ("fsdp", "seq"))

    routes_all = lax.all_gather(routes.reshape(shard_len, top_count), "seq", axis=0)
    routes_rel = routes_all[(me - jnp.arange(seq_devs)) % seq_devs]
    expert_ids = jnp.arange(expert_total, dtype=jnp.int32)
    member = jnp.any(routes_rel[:, :, :, None] == expert_ids, axis=2)
    own_member = lax.dynamic_slice_in_dim(member, me * experts_here, experts_here, 2)
    own_member = jnp.transpose(own_member, (2, 0, 1)).astype(low)
    earlier = jnp.arange(shard_len)[:, None] < jnp.arange(shard_len)[None, :]
    slot_of = dot("ent,tu->enu", own_member, earlier.astype(low)).astype(jnp.int32)
    slot_of = jnp.where(own_member > 0, slot_of, -1)
    onehot = slot_of[:, :, None, :] == jnp.arange(slots, dtype=jnp.int32)[None, None, :, None]
    pick = onehot.astype(low)

    x_all = by_place(line_gather(x_low)).reshape(seq_len, width).astype(full)
    normed_one = rms_norm(x_all, full_g1).astype(low)
    qkv_rows = dot("td,dc->tc", normed_one, full_qkv)
    qkv_rows = qkv_rows.reshape(seq_len, kv_here, GROUP + 2, HEAD_DIM)
    positions = jnp.arange(seq_len, dtype=jnp.int32)
    cosine, sine_vals = rope_tables(positions.astype(full), HEAD_DIM)
    cos_rows = cosine[:, None, None, :]
    sin_rows = sine_vals[:, None, None, :]
    turned = rotate(qkv_rows[:, :, : GROUP + 1], cos_rows, sin_rows).astype(low)
    query = turned[:, :, :GROUP]
    key = turned[:, :, GROUP]
    value = qkv_rows[:, :, GROUP + 1].astype(low)
    blocks = block_ids(block_lengths[0], positions)
    query_rows = min(512, seq_len)
    attended, lse_list = attention_forward(query, key, value, blocks, query_rows)
    attended = attended.reshape(seq_devs, shard_len, heads_w)
    attn_rows = lax.all_to_all(attended, "seq", split_axis=0, concat_axis=0, tiled=True)
    out_rows = full_out.reshape(seq_devs, heads_w, width)
    projected = dot("gtk,gkd->td", attn_rows, out_rows)
    hidden = x_low.astype(full) + resid_mult * projected
    normed_two, norm_two_pull = jax.vjp(rms_norm, hidden, full_g2)

    tokens = jnp.stack(line_gather(normed_two.astype(low)))
    logits = dot("ntd,de->nte", tokens, full_router)
    chosen = jnp.where(member, logits, masked_score)
    gate_exp = jnp.where(member, jnp.exp(chosen - jnp.max(chosen, axis=2, keepdims=True)), 0.0)
    gates = gate_exp / jnp.sum(gate_exp, axis=2, keepdims=True)
    own_gates = lax.dynamic_slice_in_dim(gates, me * experts_here, experts_here, 2)
    slot_gates = jnp.sum(
        onehot.astype(full) * jnp.transpose(own_gates, (2, 0, 1))[:, :, None, :], axis=3
    )
    expert_in = dot("enct,ntd->encd", pick, tokens).astype(low)
    expert_in = expert_in.reshape(experts_here, seq_devs * slots, width)
    gate_act = dot("erd,edf->erf", expert_in, full_gate)
    up_act = dot("erd,edf->erf", expert_in, full_up)
    act_out, act_pull = jax.vjp(swiglu, gate_act, up_act)
    act_low = act_out.astype(low)
    expert_out = dot("erf,efd->erd", act_low, full_down).astype(low)
    expert_out = expert_out.reshape(experts_here, seq_devs, slots, width)
    gated_pick = pick * slot_gates.astype(low)[..., None]
    mix_parts = dot("enct,encd->ntd", gated_pick, expert_out)
    mixture = line_scatter([mix_parts[k] for k in range(seq_devs)])
    output_f32 = hidden + resid_mult * mixture
    activations = output_f32.astype(low).reshape(1, shard_len, width)
    error_rows = output_f32 - teacher.astype(full).reshape(shard_len, width)
    weighted = valid_rows[:, None] * error_rows
    squares = lax.psum(jnp.sum(weighted * error_rows), ("fsdp", "seq"))
    loss_value = squares / (valid_count * width)
    d_out = weighted * (tokens_all / valid_count)

    d_mix = resid_mult * d_out
    mix_dot = lax.all_gather(jnp.sum(d_mix * mixture, axis=1), "seq", axis=0)
    mix_dot = mix_dot[(me - jnp.arange(seq_devs)) % seq_devs]
    d_tokens = jnp.stack(line_gather(d_mix.astype(low)))
    d_rows = dot("enct,ntd->encd", pick, d_tokens).astype(low)
    d_rows = d_rows.reshape(experts_here, seq_devs * slots, width)
    d_act_raw = dot("erd,efd->erf", d_rows, full_down)
    row_gates = slot_gates.reshape(experts_here, seq_devs * slots, 1)
    d_slot_gates = jnp.sum(d_act_raw * act_low.astype(full), axis=2)
    down_part = dot("erf,erd->efd", (act_low.astype(full) * row_gates).astype(low), d_rows)
    d_gate_act, d_up_act = act_pull(d_act_raw * row_gates)
    d_gate_low = d_gate_act.astype(low)
    d_up_low = d_up_act.astype(low)
    gate_part = dot("erd,erf->edf", expert_in, d_gate_low)
    up_part = dot("erd,erf->edf", expert_in, d_up_low)
    d_expert_in = dot("erf,edf->erd", d_gate_low, full_gate)
    d_expert_in = (d_expert_in + dot("erf,edf->erd", d_up_low, full_up)).astype(low)
    d_expert_in = d_expert_in.reshape(experts_here, seq_devs, slots, width)
    d_gates = jnp.sum(
        onehot.astype(full)
        * d_slot_gates.reshape(experts_here, seq_devs, slots)[..., None],
        axis=2,
    )
    d_gates = jnp.transpose(d_gates, (1, 2, 0))
    d_logits = (own_gates * (d_gates - mix_dot[:, :, None])).astype(low)
    own_router = lax.dynamic_slice_in_dim(full_router, me * experts_here, experts_here, 1)
    d_normed_parts = dot("enct,encd->ntd", pick, d_expert_in) + dot(
        "nte,de->ntd", d_logits, own_router
    )
    router_part = dot("ntd,nte->de", tokens, d_logits)
    d_normed_two = line_scatter([d_normed_parts[k] for k in range(seq_devs)])

    d_hidden_norm, gain_two_part = norm_two_pull(d_normed_two)
    d_hidden = d_out + d_hidden_norm
    d_proj = (resid_mult * d_hidden).astype(low)
    d_attended = dot("td,gkd->gtk", d_proj, out_rows).astype(low)
    d_heads = lax.all_to_all(d_attended, "seq", split_axis=0, concat_axis=0, tiled=True)
    out_part = dot("gtk,td->gkd", attn_rows, d_proj).astype(low).reshape(HEADS * HEAD_DIM, width)
    d_heads = d_heads.reshape(seq_len, kv_here, GROUP, HEAD_DIM)
    query_grad, key_grad, value_grad = attention_backward(
        query, key, value, blocks, lse_list, d_heads, query_rows
    )
    d_turned = jnp.concatenate([query_grad, key_grad[:, :, None]], axis=2).astype(low).astype(full)
    d_turned = rotate(d_turned, cos_rows, -sin_rows).astype(low)
    d_qkv = jnp.concatenate([d_turned, value_grad[:, :, None].astype(low)], axis=2)
    d_qkv = d_qkv.reshape(seq_len, group_w)
    qkv_part = dot("td,tc->dc", normed_one, d_qkv).astype(low)
    d_normed_parts = dot("tc,dc->td", d_qkv, full_qkv).reshape(seq_devs, shard_len, width)
    d_normed_parts = d_normed_parts[(me - jnp.arange(seq_devs)) % seq_devs]
    d_normed_one = line_scatter([d_normed_parts[k] for k in range(seq_devs)])
    x_rows = x_low.astype(full)
    _, norm_one_pull = jax.vjp(lambda v: rms_norm(v, full_g1), x_rows)
    input_grad = (d_hidden + norm_one_pull(d_normed_one)[0]).reshape(1, shard_len, width)

    def rows_sum(part, dim):
        return lax.psum_scatter(part, "fsdp", scatter_dimension=dim, tiled=True)

    gate_grad = rows_sum(gate_part.astype(low), 1).astype(full)
    up_grad = rows_sum(up_part.astype(low), 1).astype(full)
    down_grad = rows_sum(down_part.astype(low), 1).astype(full)
    own_columns = jnp.zeros((width, expert_total), full)
    own_columns = lax.dynamic_update_slice_in_dim(
        own_columns, router_part, me * experts_here, 1
    )
    dense_part = jnp.concatenate(
        [out_part, own_columns.astype(low), gain_two_part[:, None].astype(low)], axis=1
    )
    dense_part = lax.psum(rows_sum(dense_part, 0), "seq").astype(full)
    out_grad = dense_part[:, :width]
    router_grad = dense_part[:, width : width + expert_total]
    gain_two_grad = dense_part[:, width + expert_total]
    qkv_grad = lax.all_gather(rows_sum(qkv_part, 0), "seq", axis=1, tiled=True).astype(full)
    gain_one_grad = jnp.sum(qkv_grad * w_qkv.astype(full), axis=1) / gain_one.astype(full)
    return (
        activations,
        loss_value,
        input_grad,
        gain_one_grad,
        qkv_grad,
        out_grad,
        gain_two_grad,
        router_grad,
        gate_grad,
        up_grad,
        down_grad,
    )


def solution(mesh):
    return jax.shard_map(
        shards,
        mesh=mesh,
        in_specs=(
            P("fsdp", "seq", None),
            P("fsdp", "seq", None),
            P("fsdp", "seq", None),
            P("fsdp", "seq"),
            P("fsdp", None),
            P("fsdp"),
            P("fsdp", None),
            P("fsdp", None),
            P("fsdp"),
            P("fsdp", None),
            P("seq", "fsdp", None),
            P("seq", "fsdp", None),
            P("seq", "fsdp", None),
        ),
        out_specs=(
            P("fsdp", "seq", None),
            P(),
            P("fsdp", "seq", None),
            P("fsdp"),
            P("fsdp", None),
            P("fsdp", None),
            P("fsdp"),
            P("fsdp", None),
            P("seq", "fsdp", None),
            P("seq", "fsdp", None),
            P("seq", "fsdp", None),
        ),
        check_vma=False,
    )
```

time: 3690 us -> 1750 us (0.47)
  waiting for transfers between devices: 1610 us -> 552 us
  blocking collectives: 838 us -> 266 us
  local copies, waits for them, and re-layouts: 479 us -> 113 us
  matrix products: 420 us -> 512 us
  other arithmetic: 263 us -> 182 us
  starting transfers between devices: 48.1 us -> 97.3 us
    all_to_all x7 -> x1, waiting for transfers between devices: 1540 us -> 0.01 us  [shards(): lax.all_to_all(d_attended, 'seq', split_axis=0, concat_axis=0, tiled=True)]
    psum x3 -> x2, blocking collectives: 724 us -> 91.9 us  [the longest x1 47.3 us: shards(): valid_count = lax.psum(jnp.sum(valid_rows), ('fsdp', 'seq'))]
    ppermute x0 -> x36, waiting for transfers between devices: none -> 388 us  [the longest x9 160 us: line_scatter(): lax.ppermute(to_right.astype(low), 'seq', [(i, i + 1) for i in range(n -...]
    reduce_scatter x5 -> x4, waiting for transfers between devices: 12.9 us -> 162 us  [rows_sum(): return lax.psum_scatter(part, 'fsdp', scatter_dimension=dim, tiled=True)]
    all_to_all x11 -> x0, local copies, waits for them, and re-layouts: 135 us -> none  [the longest x2 34.1 us: shards(): lax.all_to_all(grad_slots, 'seq', split_axis=0, concat_axis=1, tiled=True)]
    all_gather x1 -> x4, blocking collectives: 10.2 us -> 136 us  [the longest x1 72.2 us: shards(): lax.all_gather(routes.reshape(shard_len, top_count), 'seq', axis=0)]
    dot_general x42 -> x47, matrix products: 420 us -> 512 us  [dot(): return jnp.einsum(spec, left, right, preferred_element_type=full)]
    ppermute x0 -> x36, starting transfers between devices: none -> 92 us  [the longest x9 49.6 us: line_scatter(): lax.ppermute(to_right.astype(low), 'seq', [(i, i + 1) for i in range(n -...]
  transfers between devices with their start and end apart: 19 -> 48, of which waited for: 9 -> 20; matrix products, arithmetic and copies ran while one was open for 24% -> 33% of each run, Pallas kernels for 0% -> 0%
where the time goes in v1:
time: 1750 us; the launch traced here: 1740 us
  waiting for transfers between devices  552 us (32%)
  matrix products  512 us (29%)
  blocking collectives  266 us (15%)
  other arithmetic  182 us (10%)
  local copies, waits for them, and re-layouts  113 us (6%)
  starting transfers between devices  97.3 us (6%)
  between operations  19.3 us (1%)
    dot_general x47, matrix products, dot(): return jnp.einsum(spec, left, right, preferred_element_type=full)  512 us
    reduce_scatter x4, waiting for transfers between devices, rows_sum(): return lax.psum_scatter(part, 'fsdp', scatter_dimension=dim, tiled=True)  162 us
    ppermute x9, waiting for transfers between devices, line_scatter(): lax.ppermute(to_right.astype(low), 'seq', [(i, i + 1) for i in range(n -...  160 us
    ppermute x9, waiting for transfers between devices, line_gather(): lax.ppermute(lefts[-1], 'seq', [(i, i - 1) for i in range(1, n - k + 1)])  123 us
    ppermute x9, waiting for transfers between devices, line_gather(): lax.ppermute(rights[-1], 'seq', [(i, i + 1) for i in range(k - 1, n - 1)])  82.2 us
    all_gather x1, blocking collectives, shards(): lax.all_gather(routes.reshape(shard_len, top_count), 'seq', axis=0)  72.2 us
    convert_element_type x4, other arithmetic, attention_backward(): d_scores = (prob_rows * (d_probs - row_delta)).astype(low)  52.1 us
    ppermute x9, starting transfers between devices, line_scatter(): lax.ppermute(to_right.astype(low), 'seq', [(i, i + 1) for i in range(n -...  49.6 us
  transfers between devices with their start and end apart: 48, of which 20 were waited for; matrix products, arithmetic and copies ran while one was open for 33% of the time, Pallas kernels for 0%

profile of v1, /device:TPU:0, one launch (start us, length us, event | category | flops | bytes accessed | tf_op | source)
XLA Modules:
  0.0 1741.6 jit_solution(487067580772973361)
XLA Ops:
  29.2 20.6 %collective-permute-done = bf16[512,1536]{1,0:T(8,128)(2,1)} collective-permute-done((bf16[512,1536]{1,0:T(8,128)(2,1)S(1)}, bf16[512,1536]{1,0:T(8,128)(2,1)}, u32[]{:S(2)}, u32[]{:S(2)}) %collective-permute-start) | collective-permute-done | bytes 1572896 | tf_op jit(solution)/shard_map/ppermute | solution.py:64
  61.2 32.4 %collective-permute-done.2 = bf16[512,1536]{1,0:T(8,128)(2,1)} collective-permute-done((bf16[512,1536]{1,0:T(8,128)(2,1)}, bf16[512,1536]{1,0:T(8,128)(2,1)}, u32[]{:S(2)}, u32[]{:S(2)}) %collective-permute-start.2) | collective-permute-done | bytes 1572896 | tf_op jit(solution)/shard_map/ppermute | solution.py:65
  105.1 25.0 %collective-permute-done.3 = bf16[512,1536]{1,0:T(8,128)(2,1)} collective-permute-done((bf16[512,1536]{1,0:T(8,128)(2,1)}, bf16[512,1536]{1,0:T(8,128)(2,1)}, u32[]{:S(2)}, u32[]{:S(2)}) %collective-permute-start.3) | collective-permute-done | bytes 1572896 | tf_op jit(solution)/shard_map/ppermute | solution.py:65
  167.6 14.1 fusion.215
  181.8 11.2 fusion.4
  233.0 11.1 fusion.157
  247.0 38.2 %all_to_all.10 = bf16[4,512,384]{2,1,0:T(8,128)(2,1)} all-to-all(bf16[4,512,384]{2,1,0:T(8,128)(2,1)S(1)} %copy.158), channel_id=1, replica_groups=mesh['fsdp'=8,'seq'=4] {'seq'}, dimensions={0} | all-to-all | bytes 3145728 | tf_op jit(solution)/shard_map/all_to_all | solution.py:210
  295.2 30.4 %collective-permute-done.6 = bf16[512,1536]{1,0:T(8,128)(2,1)S(1)} collective-permute-done((bf16[512,1536]{1,0:T(8,128)(2,1)S(1)}, bf16[512,1536]{1,0:T(8,128)(2,1)S(1)}, u32[]{:S(2)}, u32[]{:S(2)}) %collective-permute-start.6) | collective-permute-done | bytes 1572896 | tf_op jit(solution)/shard_map/ppermute | solution.py:64
  333.1 72.2 %all_gather.33 = s32[4,512,8]{1,2,0:T(8,128)S(1)} all-gather(s32[1,512,8]{1,2,0:T(8,128)S(1)} %copy-done.85), channel_id=1, replica_groups=mesh['fsdp'=8,'seq'=4] {'seq'}, dimensions={0}, use_global_device_ids=true | all-gather | bytes 81920 | tf_op jit(solution)/shard_map/all_gather | solution.py:182
  413.3 26.1 %collective-permute-done.9 = bf16[512,1536]{1,0:T(8,128)(2,1)S(1)} collective-permute-done((bf16[512,1536]{1,0:T(8,128)(2,1)}, bf16[512,1536]{1,0:T(8,128)(2,1)S(1)}, u32[]{:S(2)}, u32[]{:S(2)}) %collective-permute-start.9) | collective-permute-done | bytes 1572896 | tf_op jit(solution)/shard_map/ppermute | solution.py:65
  439.7 14.0 convert_bitcast_fusion.1
  453.7 16.4 copy.159
  475.1 22.0 %fusion.221 = f32[10,640,512]{1,2,0:T(8,128)} fusion(bf16[10,640,1536]{2,1,0:T(8,128)(2,1)} %bitcast.504, bf16[10,1536,512]{2,1,0:T(8,128)(2,1)} %all-gather.13.cloned.1.call-done), kind=kOutput, calls=%fused_computation.353 | convolution fusion | flops 10066329600 | bytes 48496640 | tf_op jit(solution)/shard_map/erd,edf->erf/dot_general | solution.py:25
  497.1 28.1 %multiply_convert_fusion.1 = (bf16[10,640,512]{1,2,0:T(8,128)(2,1)}, f32[10,640,512]{1,2,0:T(8,128)}) fusion(f32[10,640,512]{1,2,0:T(8,128)} %fusion.221, bf16[10,640,1536]{2,1,0:T(8,128)(2,1)} %bitcast.505, bf16[10,1536,512]{2,1,0:T(8,128)(2,1)} %all-gather.15.cloned.1.call-done), kind=kOutput, calls=%fused_computation.60 | convolution fusion | flops 10085990400 | bytes 68157440 | tf_op jit(solution)/shard_map/erd,edf->erf/dot_general | solution.py:25
  525.2 21.2 %convolution_convert_fusion = bf16[10,640,1536]{2,1,0:T(8,128)(2,1)} fusion(bf16[10,640,512]{1,2,0:T(8,128)(2,1)} %get-tuple-element.230, bf16[10,512,1536]{2,1,0:T(8,128)(2,1)} %all-gather.17.cloned.1.call-done), kind=kOutput, calls=%fused_computation.34 | convolution fusion | flops 10076160000 | bytes 41943040 | tf_op jit(solution)/shard_map/erf,efd->erd/dot_general | solution.py:25
  546.4 18.5 %fusion.54 = f32[4,512,1536]{2,1,0:T(8,128)} fusion(bf16[10,4,160,1536]{3,2,1,0:T(8,128)(2,1)} %bitcast.540, s32[10,4,512]{2,0,1:T(8,128)S(1)} %fusion.162, bf16[10,4,160]{2,0,1:T(8,128)(2,1)S(1)} %convert_element_type.399), kind=kOutput, calls=%fused_computation.96 | convolution fusion | flops 10072883200 | bytes 32338432 | tf_op jit(solution)/shard_map/enct,encd->ntd/dot_general | solution.py:25
  571.0 26.4 %collective-permute-done.12 = bf16[512,1536]{1,0:T(8,128)(2,1)S(1)} collective-permute-done((bf16[512,1536]{1,0:T(8,128)(2,1)S(1)}, bf16[512,1536]{1,0:T(8,128)(2,1)S(1)}, u32[]{:S(2)}, u32[]{:S(2)}) %collective-permute-start.12) | collective-permute-done | bytes 1572896 | tf_op jit(solution)/shard_map/ppermute | solution.py:77
  605.8 25.4 %collective-permute-done.13 = bf16[512,1536]{1,0:T(8,128)(2,1)S(1)} collective-permute-done((bf16[512,1536]{1,0:T(8,128)(2,1)S(1)}, bf16[512,1536]{1,0:T(8,128)(2,1)S(1)}, u32[]{:S(2)}, u32[]{:S(2)}) %collective-permute-start.13) | collective-permute-done | bytes 1572896 | tf_op jit(solution)/shard_map/ppermute | solution.py:77
  645.0 47.3 %psum.22 = f32[]{:T(128)} all-reduce(f32[]{:T(128)} %convert_reduce_fusion.1), channel_id=1, replica_groups=mesh['fsdp'=8,'seq'=4] {'fsdp','seq'}, use_global_device_ids=true, to_apply=%region_19.20 | all-reduce | flops 1 | bytes 8 | tf_op jit(solution)/shard_map/psum | solution.py:180
  704.0 31.2 %collective-permute-done.18 = bf16[512,1536]{1,0:T(8,128)(2,1)S(1)} collective-permute-done((bf16[512,1536]{1,0:T(8,128)(2,1)S(1)}, bf16[512,1536]{1,0:T(8,128)(2,1)S(1)}, u32[]{:S(2)}, u32[]{:S(2)}) %collective-permute-start.18) | collective-permute-done | bytes 1572896 | tf_op jit(solution)/shard_map/ppermute | solution.py:64
  743.4 32.6 %collective-permute-done.20 = bf16[512,1536]{1,0:T(8,128)(2,1)} collective-permute-done((bf16[512,1536]{1,0:T(8,128)(2,1)S(1)}, bf16[512,1536]{1,0:T(8,128)(2,1)}, u32[]{:S(2)}, u32[]{:S(2)}) %collective-permute-start.20) | collective-permute-done | bytes 1572896 | tf_op jit(solution)/shard_map/ppermute | solution.py:65
  783.2 34.5 %all-gather.2 = f32[4,1,512]{2,1,0:T(1,128)S(1)} all-gather(f32[1,1,512]{2,1,0:T(1,128)S(1)} %bitcast.533), channel_id=2, replica_groups=mesh['fsdp'=8,'seq'=4] {'seq'}, dimensions={0}, use_global_device_ids=true | all-gather | bytes 10240 | tf_op jit(solution)/shard_map/all_gather | solution.py:245
  822.3 17.0 convert_bitcast_fusion
  839.3 16.4 copy.162
  855.7 34.7 %multiply_convert_fusion = (bf16[10,640,512]{1,2,0:T(8,128)(2,1)}, bf16[10,640,512]{1,2,0:T(8,128)(2,1)}, f32[10,640]{1,0:T(8,128)S(1)}) fusion(f32[10,640]{1,0:T(8,128)S(1)} %mul.568, f32[10,640,512]{1,2,0:T(8,128)} %fusion.221, f32[10,640,512]{1,2,0:T(8,128)} %get-tuple-element.231, bf16[10,640,512]{1,2,0:T(8,128)(2,1)} %get-tuple-element.230, ...), kind=kOutput, calls=%fused_computation.59 | convolution fusion | flops 10125305856 | bytes 81315840 | tf_op jit(solution)/shard_map/erd,efd->erf/dot_general | solution.py:25
  890.4 25.3 %fusion.222 = f32[10,640,1536]{2,1,0:T(8,128)} fusion(bf16[10,640,512]{1,2,0:T(8,128)(2,1)} %get-tuple-element.180, bf16[10,1536,512]{2,1,0:T(8,128)(2,1)} %all-gather.13.cloned.1.call-done), kind=kOutput, calls=%fused_computation.354 | convolution fusion | flops 10066329600 | bytes 61603840 | tf_op jit(solution)/shard_map/erf,edf->erd/dot_general | solution.py:25
  915.6 28.6 %add_convert_fusion = bf16[10,640,1536]{2,1,0:T(8,128)(2,1)} fusion(f32[10,640,1536]{2,1,0:T(8,128)} %fusion.222, bf16[10,640,512]{1,2,0:T(8,128)(2,1)} %get-tuple-element.179, bf16[10,1536,512]{2,1,0:T(8,128)(2,1)} %all-gather.15.cloned.1.call-done), kind=kOutput, calls=%fused_computation.5 | convolution fusion | flops 10085990400 | bytes 81264640 | tf_op jit(solution)/shard_map/erf,edf->erd/dot_general | solution.py:25
  944.2 18.4 %fusion.8 = f32[4,512,1536,1]{2,1,3,0:T(8,128)} fusion(bf16[10,4,160,1536]{3,2,1,0:T(8,128)(2,1)} %bitcast.503, s32[10,4,512]{2,0,1:T(8,128)S(1)} %fusion.162), kind=kOutput, calls=%fused_computation.25 | convolution fusion | flops 10069606400 | bytes 32325632 | tf_op jit(solution)/shard_map/enct,encd->ntd/dot_general | solution.py:25
  976.1 28.5 %collective-permute-done.24 = bf16[512,1536]{1,0:T(8,128)(2,1)S(1)} collective-permute-done((bf16[512,1536]{1,0:T(8,128)(2,1)S(1)}, bf16[512,1536]{1,0:T(8,128)(2,1)S(1)}, u32[]{:S(2)}, u32[]{:S(2)}) %collective-permute-start.24) | collective-permute-done | bytes 1572896 | tf_op jit(solution)/shard_map/ppermute | solution.py:77
  1010.9 27.1 %collective-permute-done.25 = bf16[512,1536]{1,0:T(8,128)(2,1)S(1)} collective-permute-done((bf16[512,1536]{1,0:T(8,128)(2,1)S(1)}, bf16[512,1536]{1,0:T(8,128)(2,1)S(1)}, u32[]{:S(2)}, u32[]{:S(2)}) %collective-permute-start.25) | collective-permute-done | bytes 1572896 | tf_op jit(solution)/shard_map/ppermute | solution.py:77
  1049.3 23.1 %collective-permute-done.29 = bf16[512,1536]{1,0:T(8,128)(2,1)S(1)} collective-permute-done((bf16[512,1536]{1,0:T(8,128)(2,1)S(1)}, bf16[512,1536]{1,0:T(8,128)(2,1)S(1)}, u32[]{:S(2)}, u32[]{:S(2)}) %collective-permute-start.29) | collective-permute-done | bytes 1572896 | tf_op jit(solution)/shard_map/ppermute | solution.py:78
  1135.0 12.2 fusion.40
  1151.3 12.8 fusion.15
  1179.3 13.8 fusion.5
  1193.1 15.4 fusion.7
  1212.7 16.0 fusion.1
  1228.7 16.9 fusion.3
  1305.1 20.5 %convolution_convert_fusion.3 = bf16[10,1536,512]{2,1,0:T(8,128)(2,1)} fusion(bf16[10,640,1536]{2,1,0:T(8,128)(2,1)} %bitcast.506, bf16[10,640,512]{1,2,0:T(8,128)(2,1)} %get-tuple-element.180), kind=kOutput, calls=%fused_computation.52 | convolution fusion | flops 10074193920 | bytes 41943040 | tf_op jit(solution)/shard_map/erd,erf->edf/dot_general | solution.py:25
  1325.6 20.5 %convolution_convert_fusion.2 = bf16[10,1536,512]{2,1,0:T(8,128)(2,1)} fusion(bf16[10,640,1536]{2,1,0:T(8,128)(2,1)} %bitcast.507, bf16[10,640,512]{1,2,0:T(8,128)(2,1)} %get-tuple-element.179), kind=kOutput, calls=%fused_computation.51 | convolution fusion | flops 10074193920 | bytes 41943040 | tf_op jit(solution)/shard_map/erd,erf->edf/dot_general | solution.py:25
  1346.9 20.7 %convolution_convert_fusion.1 = bf16[10,512,1536]{2,1,0:T(8,128)(2,1)} fusion(bf16[10,640,1536]{2,1,0:T(8,128)(2,1)} %bitcast.509, bf16[10,640,512]{1,2,0:T(8,128)(2,1)} %get-tuple-element.230, f32[10,640]{1,0:T(8,128)S(1)} %copy-done.80), kind=kOutput, calls=%fused_computation.50 | convolution fusion | flops 10084024320 | bytes 41968640 | tf_op jit(solution)/shard_map/erf,erd->efd/dot_general | solution.py:25
  1371.2 11.5 fusion.89
  1382.6 10.7 gather_fusion.3
  1402.0 26.5 %collective-permute-done.30 = bf16[512,1536]{1,0:T(8,128)(2,1)S(1)} collective-permute-done((bf16[512,1536]{1,0:T(8,128)(2,1)S(1)}, bf16[512,1536]{1,0:T(8,128)(2,1)S(1)}, u32[]{:S(2)}, u32[]{:S(2)}) %collective-permute-start.30) | collective-permute-done | bytes 1572896 | tf_op jit(solution)/shard_map/ppermute | solution.py:77
  1436.5 24.3 %collective-permute-done.31 = bf16[512,1536]{1,0:T(8,128)(2,1)S(1)} collective-permute-done((bf16[512,1536]{1,0:T(8,128)(2,1)S(1)}, bf16[512,1536]{1,0:T(8,128)(2,1)S(1)}, u32[]{:S(2)}, u32[]{:S(2)}) %collective-permute-start.31) | collective-permute-done | bytes 1572896 | tf_op jit(solution)/shard_map/ppermute | solution.py:77
  1476.0 44.6 %psum.21 = f32[]{:T(128)} all-reduce(f32[]{:T(128)} %get-tuple-element.170), channel_id=1, replica_groups=mesh['fsdp'=8,'seq'=4] {'fsdp','seq'}, use_global_device_ids=true, to_apply=%region_17.18 | all-reduce | flops 1 | bytes 8 | tf_op jit(solution)/shard_map/psum | solution.py:240
  1521.3 20.1 %all_gather.39 = bf16[192,2560]{1,0:T(8,128)(2,1)S(1)} all-gather(bf16[192,640]{1,0:T(8,128)(2,1)} %reduce-scatter.8.cloned.1.call-done), channel_id=1, replica_groups=mesh['fsdp'=8,'seq'=4] {'seq'}, dimensions={1}, use_global_device_ids=true | all-gather | bytes 1228800 | tf_op jit(solution)/shard_map/all_gather | solution.py:315
  1563.7 52.8 %reduce-scatter.12.cloned.1.call-done = bf16[10,192,512]{2,1,0:T(8,128)(2,1)} async-done(((bf16[10,1536,512]{2,1,0:T(8,128)(2,1)}), bf16[10,192,512]{2,1,0:T(8,128)(2,1)}) %reduce-scatter.12.cloned.1.call-update) | async-done | bytes 1966096 | tf_op jit(solution)/shard_map/reduce_scatter | solution.py:299
  1620.6 109.1 %reduce-scatter.14.cloned.1.call-done = bf16[10,64,1536]{2,1,0:T(8,128)(2,1)} async-done(((bf16[10,512,1536]{2,1,0:T(8,128)(2,1)}), bf16[10,64,1536]{2,1,0:T(8,128)(2,1)}) %reduce-scatter.14.cloned.1.call-update) | async-done | bytes 1966096 | tf_op jit(solution)/shard_map/reduce_scatter | solution.py:299
  (459 shorter events, 455.9 us)
Async XLA Ops:
  7.2 92.2 %all-gather.9.cloned.1.call-start = ((), (), s32[]{:S(2)}) async-start(), calls=%async_computation.7 | async-start | bytes 2211840 | tf_op jit(solution)/shard_map/all_gather | solution.py:171
  9.1 276.1 %all-gather.11.cloned.1.call-start = ((), (), s32[]{:S(2)}) async-start(), calls=%async_computation.8 | async-start | bytes 5308416 | tf_op jit(solution)/shard_map/all_gather | solution.py:172
  9.8 465.3 %all-gather.13.cloned.1.call-start = ((), (), s32[]{:S(2)}) async-start(), calls=%async_computation.9 | async-start | bytes 17694720 | tf_op jit(solution)/shard_map/all_gather | solution.py:173
  10.6 486.6 %all-gather.15.cloned.1.call-start = ((), (), s32[]{:S(2)}) async-start(), calls=%async_computation.10 | async-start | bytes 17694720 | tf_op jit(solution)/shard_map/all_gather | solution.py:174
  11.1 514.1 %all-gather.17.cloned.1.call-start = ((), (), s32[]{:S(2)}) async-start(), calls=%async_computation.11 | async-start | bytes 17694720 | tf_op jit(solution)/shard_map/all_gather | solution.py:175
  11.2 38.6 %collective-permute-start = (bf16[512,1536]{1,0:T(8,128)(2,1)S(1)}, bf16[512,1536]{1,0:T(8,128)(2,1)}, u32[]{:S(2)}, u32[]{:S(2)}) collective-permute-start(bf16[512,1536]{1,0:T(8,128)(2,1)S(1)} %bitcast.510), channel_id=1, source_target_pairs={{0,1},{1,2},{2,3},{4,5},{5,6},{6,7},{8,9},{9,10},{10,11},{12,13},{... | collective-permute-start | bytes 4718600 | tf_op jit(solution)/shard_map/ppermute | solution.py:64
  17.3 37.8 %collective-permute-start.1 = (bf16[512,1536]{1,0:T(8,128)(2,1)S(1)}, bf16[512,1536]{1,0:T(8,128)(2,1)}, u32[]{:S(2)}, u32[]{:S(2)}) collective-permute-start(bf16[512,1536]{1,0:T(8,128)(2,1)S(1)} %bitcast.511), channel_id=1, source_target_pairs={{1,0},{2,1},{3,2},{5,4},{6,5},{7,6},{9,8},{10,9},{11,10},{13,12},{... | collective-permute-start | bytes 4718600 | tf_op jit(solution)/shard_map/ppermute | solution.py:65
  49.8 9.1 collective-permute-start.4
  55.1 38.5 %collective-permute-start.2 = (bf16[512,1536]{1,0:T(8,128)(2,1)}, bf16[512,1536]{1,0:T(8,128)(2,1)}, u32[]{:S(2)}, u32[]{:S(2)}) collective-permute-start(bf16[512,1536]{1,0:T(8,128)(2,1)} %collective-permute-done.1), channel_id=1, source_target_pairs={{1,0},{2,1},{5,4},{6,5},{9,8},{10,9},{13,12},{14,13},{17,16},{18,1... | collective-permute-start | bytes 4718600 | tf_op jit(solution)/shard_map/ppermute | solution.py:65
  58.9 44.5 %collective-permute-start.5 = (bf16[512,1536]{1,0:T(8,128)(2,1)}, bf16[512,1536]{1,0:T(8,128)(2,1)}, u32[]{:S(2)}, u32[]{:S(2)}) collective-permute-start(bf16[512,1536]{1,0:T(8,128)(2,1)} %collective-permute-done.4), channel_id=1, source_target_pairs={{2,3},{6,7},{10,11},{14,15},{18,19},{22,23},{26,27},{30,31}} | collective-permute-start | bytes 4718600 | tf_op jit(solution)/shard_map/ppermute | solution.py:64
  93.6 36.5 %collective-permute-start.3 = (bf16[512,1536]{1,0:T(8,128)(2,1)}, bf16[512,1536]{1,0:T(8,128)(2,1)}, u32[]{:S(2)}, u32[]{:S(2)}) collective-permute-start(bf16[512,1536]{1,0:T(8,128)(2,1)} %collective-permute-done.2), channel_id=1, source_target_pairs={{1,0},{5,4},{9,8},{13,12},{17,16},{21,20},{25,24},{29,28}} | collective-permute-start | bytes 4718600 | tf_op jit(solution)/shard_map/ppermute | solution.py:65
  291.7 34.0 %collective-permute-start.6 = (bf16[512,1536]{1,0:T(8,128)(2,1)S(1)}, bf16[512,1536]{1,0:T(8,128)(2,1)S(1)}, u32[]{:S(2)}, u32[]{:S(2)}) collective-permute-start(bf16[512,1536]{1,0:T(8,128)(2,1)S(1)} %multiply_convert_fusion.3), channel_id=1, source_target_pairs={{0,1},{1,2},{2,3},{4,5},{5,6},{6,7},{8,9},{9,10},{10,11},{12,13},{... | collective-permute-start | bytes 4718600 | tf_op jit(solution)/shard_map/ppermute | solution.py:64
  293.9 36.1 %collective-permute-start.7 = (bf16[512,1536]{1,0:T(8,128)(2,1)S(1)}, bf16[512,1536]{1,0:T(8,128)(2,1)}, u32[]{:S(2)}, u32[]{:S(2)}) collective-permute-start(bf16[512,1536]{1,0:T(8,128)(2,1)S(1)} %multiply_convert_fusion.3), channel_id=1, source_target_pairs={{1,0},{2,1},{3,2},{5,4},{6,5},{7,6},{9,8},{10,9},{11,10},{13,12},{... | collective-permute-start | bytes 4718600 | tf_op jit(solution)/shard_map/ppermute | solution.py:65
  325.6 5.6 collective-permute-start.10
  330.0 76.7 %collective-permute-start.8 = (bf16[512,1536]{1,0:T(8,128)(2,1)}, bf16[512,1536]{1,0:T(8,128)(2,1)}, u32[]{:S(2)}, u32[]{:S(2)}) collective-permute-start(bf16[512,1536]{1,0:T(8,128)(2,1)} %collective-permute-done.7), channel_id=1, source_target_pairs={{1,0},{2,1},{5,4},{6,5},{9,8},{10,9},{13,12},{14,13},{17,16},{18,1... | collective-permute-start | bytes 4718600 | tf_op jit(solution)/shard_map/ppermute | solution.py:65
  331.3 79.9 %collective-permute-start.11 = (bf16[512,1536]{1,0:T(8,128)(2,1)}, bf16[512,1536]{1,0:T(8,128)(2,1)}, u32[]{:S(2)}, u32[]{:S(2)}) collective-permute-start(bf16[512,1536]{1,0:T(8,128)(2,1)} %collective-permute-done.10), channel_id=1, source_target_pairs={{2,3},{6,7},{10,11},{14,15},{18,19},{22,23},{26,27},{30,31}} | collective-permute-start | bytes 4718600 | tf_op jit(solution)/shard_map/ppermute | solution.py:64
  406.6 32.8 %collective-permute-start.9 = (bf16[512,1536]{1,0:T(8,128)(2,1)}, bf16[512,1536]{1,0:T(8,128)(2,1)S(1)}, u32[]{:S(2)}, u32[]{:S(2)}) collective-permute-start(bf16[512,1536]{1,0:T(8,128)(2,1)} %collective-permute-done.8), channel_id=1, source_target_pairs={{1,0},{5,4},{9,8},{13,12},{17,16},{21,20},{25,24},{29,28}} | collective-permute-start | bytes 4718600 | tf_op jit(solution)/shard_map/ppermute | solution.py:65
  568.2 29.3 %collective-permute-start.12 = (bf16[512,1536]{1,0:T(8,128)(2,1)S(1)}, bf16[512,1536]{1,0:T(8,128)(2,1)S(1)}, u32[]{:S(2)}, u32[]{:S(2)}) collective-permute-start(bf16[512,1536]{1,0:T(8,128)(2,1)S(1)} %get-tuple-element.199), channel_id=1, source_target_pairs={{0,1},{4,5},{8,9},{12,13},{16,17},{20,21},{24,25},{28,29}} | collective-permute-start | bytes 4718600 | tf_op jit(solution)/shard_map/ppermute | solution.py:77
  570.3 27.2 %collective-permute-start.15 = (bf16[512,1536]{1,0:T(8,128)(2,1)S(1)}, bf16[512,1536]{1,0:T(8,128)(2,1)S(1)}, u32[]{:S(2)}, u32[]{:S(2)}) collective-permute-start(bf16[512,1536]{1,0:T(8,128)(2,1)S(1)} %get-tuple-element.200), channel_id=1, source_target_pairs={{3,2},{7,6},{11,10},{15,14},{19,18},{23,22},{27,26},{31,30}} | collective-permute-start | bytes 4718600 | tf_op jit(solution)/shard_map/ppermute | solution.py:78
  600.3 30.9 %collective-permute-start.13 = (bf16[512,1536]{1,0:T(8,128)(2,1)S(1)}, bf16[512,1536]{1,0:T(8,128)(2,1)S(1)}, u32[]{:S(2)}, u32[]{:S(2)}) collective-permute-start(bf16[512,1536]{1,0:T(8,128)(2,1)S(1)} %get-tuple-element.197), channel_id=1, source_target_pairs={{0,1},{1,2},{4,5},{5,6},{8,9},{9,10},{12,13},{13,14},{16,17},{17,1... | collective-permute-start | bytes 4718600 | tf_op jit(solution)/shard_map/ppermute | solution.py:77
  604.9 26.3 %collective-permute-start.16 = (bf16[512,1536]{1,0:T(8,128)(2,1)S(1)}, bf16[512,1536]{1,0:T(8,128)(2,1)S(1)}, u32[]{:S(2)}, u32[]{:S(2)}) collective-permute-start(bf16[512,1536]{1,0:T(8,128)(2,1)S(1)} %get-tuple-element.198), channel_id=1, source_target_pairs={{2,1},{3,2},{6,5},{7,6},{10,9},{11,10},{14,13},{15,14},{18,17},{19... | collective-permute-start | bytes 4718600 | tf_op jit(solution)/shard_map/ppermute | solution.py:78
  634.0 59.0 %collective-permute-start.17 = (bf16[512,1536]{1,0:T(8,128)(2,1)}, bf16[512,1536]{1,0:T(8,128)(2,1)}, u32[]{:S(2)}, u32[]{:S(2)}) collective-permute-start(bf16[512,1536]{1,0:T(8,128)(2,1)} %get-tuple-element.196), channel_id=1, source_target_pairs={{1,0},{2,1},{3,2},{5,4},{6,5},{7,6},{9,8},{10,9},{11,10},{13,12},{... | collective-permute-start | bytes 4718600 | tf_op jit(solution)/shard_map/ppermute | solution.py:78
  635.3 57.8 %collective-permute-start.14 = (bf16[512,1536]{1,0:T(8,128)(2,1)}, bf16[512,1536]{1,0:T(8,128)(2,1)}, u32[]{:S(2)}, u32[]{:S(2)}) collective-permute-start(bf16[512,1536]{1,0:T(8,128)(2,1)} %get-tuple-element.195), channel_id=1, source_target_pairs={{0,1},{1,2},{2,3},{4,5},{5,6},{6,7},{8,9},{9,10},{10,11},{12,13},{... | collective-permute-start | bytes 4718600 | tf_op jit(solution)/shard_map/ppermute | solution.py:77
  700.0 35.2 %collective-permute-start.18 = (bf16[512,1536]{1,0:T(8,128)(2,1)S(1)}, bf16[512,1536]{1,0:T(8,128)(2,1)S(1)}, u32[]{:S(2)}, u32[]{:S(2)}) collective-permute-start(bf16[512,1536]{1,0:T(8,128)(2,1)S(1)} %get-tuple-element.177), channel_id=1, source_target_pairs={{0,1},{1,2},{2,3},{4,5},{5,6},{6,7},{8,9},{9,10},{10,11},{12,13},{... | collective-permute-start | bytes 4718600 | tf_op jit(solution)/shard_map/ppermute | solution.py:64
  702.3 37.1 %collective-permute-start.19 = (bf16[512,1536]{1,0:T(8,128)(2,1)S(1)}, bf16[512,1536]{1,0:T(8,128)(2,1)S(1)}, u32[]{:S(2)}, u32[]{:S(2)}) collective-permute-start(bf16[512,1536]{1,0:T(8,128)(2,1)S(1)} %get-tuple-element.177), channel_id=1, source_target_pairs={{1,0},{2,1},{3,2},{5,4},{6,5},{7,6},{9,8},{10,9},{11,10},{13,12},{... | collective-permute-start | bytes 4718600 | tf_op jit(solution)/shard_map/ppermute | solution.py:65
  735.2 5.5 collective-permute-start.22
  739.4 36.5 %collective-permute-start.20 = (bf16[512,1536]{1,0:T(8,128)(2,1)S(1)}, bf16[512,1536]{1,0:T(8,128)(2,1)}, u32[]{:S(2)}, u32[]{:S(2)}) collective-permute-start(bf16[512,1536]{1,0:T(8,128)(2,1)S(1)} %collective-permute-done.19), channel_id=1, source_target_pairs={{1,0},{2,1},{5,4},{6,5},{9,8},{10,9},{13,12},{14,13},{17,16},{18,1... | collective-permute-start | bytes 4718600 | tf_op jit(solution)/shard_map/ppermute | solution.py:65
  740.7 79.8 %collective-permute-start.23 = (bf16[512,1536]{1,0:T(8,128)(2,1)}, bf16[512,1536]{1,0:T(8,128)(2,1)}, u32[]{:S(2)}, u32[]{:S(2)}) collective-permute-start(bf16[512,1536]{1,0:T(8,128)(2,1)} %collective-permute-done.22), channel_id=1, source_target_pairs={{2,3},{6,7},{10,11},{14,15},{18,19},{22,23},{26,27},{30,31}} | collective-permute-start | bytes 4718600 | tf_op jit(solution)/shard_map/ppermute | solution.py:64
  776.0 44.8 %collective-permute-start.21 = (bf16[512,1536]{1,0:T(8,128)(2,1)}, bf16[512,1536]{1,0:T(8,128)(2,1)}, u32[]{:S(2)}, u32[]{:S(2)}) collective-permute-start(bf16[512,1536]{1,0:T(8,128)(2,1)} %collective-permute-done.20), channel_id=1, source_target_pairs={{1,0},{5,4},{9,8},{13,12},{17,16},{21,20},{25,24},{29,28}} | collective-permute-start | bytes 4718600 | tf_op jit(solution)/shard_map/ppermute | solution.py:65
  973.9 30.7 %collective-permute-start.24 = (bf16[512,1536]{1,0:T(8,128)(2,1)S(1)}, bf16[512,1536]{1,0:T(8,128)(2,1)S(1)}, u32[]{:S(2)}, u32[]{:S(2)}) collective-permute-start(bf16[512,1536]{1,0:T(8,128)(2,1)S(1)} %get-tuple-element.193), channel_id=1, source_target_pairs={{0,1},{4,5},{8,9},{12,13},{16,17},{20,21},{24,25},{28,29}} | collective-permute-start | bytes 4718600 | tf_op jit(solution)/shard_map/ppermute | solution.py:77
  975.3 29.3 %collective-permute-start.27 = (bf16[512,1536]{1,0:T(8,128)(2,1)S(1)}, bf16[512,1536]{1,0:T(8,128)(2,1)S(1)}, u32[]{:S(2)}, u32[]{:S(2)}) collective-permute-start(bf16[512,1536]{1,0:T(8,128)(2,1)S(1)} %get-tuple-element.194), channel_id=1, source_target_pairs={{3,2},{7,6},{11,10},{15,14},{19,18},{23,22},{27,26},{31,30}} | collective-permute-start | bytes 4718600 | tf_op jit(solution)/shard_map/ppermute | solution.py:78
  1005.4 32.6 %collective-permute-start.25 = (bf16[512,1536]{1,0:T(8,128)(2,1)S(1)}, bf16[512,1536]{1,0:T(8,128)(2,1)S(1)}, u32[]{:S(2)}, u32[]{:S(2)}) collective-permute-start(bf16[512,1536]{1,0:T(8,128)(2,1)S(1)} %get-tuple-element.191), channel_id=1, source_target_pairs={{0,1},{1,2},{4,5},{5,6},{8,9},{9,10},{12,13},{13,14},{16,17},{17,1... | collective-permute-start | bytes 4718600 | tf_op jit(solution)/shard_map/ppermute | solution.py:77
  1010.0 28.0 %collective-permute-start.28 = (bf16[512,1536]{1,0:T(8,128)(2,1)S(1)}, bf16[512,1536]{1,0:T(8,128)(2,1)S(1)}, u32[]{:S(2)}, u32[]{:S(2)}) collective-permute-start(bf16[512,1536]{1,0:T(8,128)(2,1)S(1)} %get-tuple-element.192), channel_id=1, source_target_pairs={{2,1},{3,2},{6,5},{7,6},{10,9},{11,10},{14,13},{15,14},{18,17},{19... | collective-permute-start | bytes 4718600 | tf_op jit(solution)/shard_map/ppermute | solution.py:78
  1039.1 33.3 %collective-permute-start.29 = (bf16[512,1536]{1,0:T(8,128)(2,1)S(1)}, bf16[512,1536]{1,0:T(8,128)(2,1)S(1)}, u32[]{:S(2)}, u32[]{:S(2)}) collective-permute-start(bf16[512,1536]{1,0:T(8,128)(2,1)S(1)} %get-tuple-element.190), channel_id=1, source_target_pairs={{1,0},{2,1},{3,2},{5,4},{6,5},{7,6},{9,8},{10,9},{11,10},{13,12},{... | collective-permute-start | bytes 4718600 | tf_op jit(solution)/shard_map/ppermute | solution.py:78
  1040.4 33.2 %collective-permute-start.26 = (bf16[512,1536]{1,0:T(8,128)(2,1)S(1)}, bf16[512,1536]{1,0:T(8,128)(2,1)S(1)}, u32[]{:S(2)}, u32[]{:S(2)}) collective-permute-start(bf16[512,1536]{1,0:T(8,128)(2,1)S(1)} %get-tuple-element.189), channel_id=1, source_target_pairs={{0,1},{1,2},{2,3},{4,5},{5,6},{6,7},{8,9},{9,10},{10,11},{12,13},{... | collective-permute-start | bytes 4718600 | tf_op jit(solution)/shard_map/ppermute | solution.py:77
  1080.7 35.7 %all-to-all-start.1 = ((bf16[4,512,384]{2,1,0:T(8,128)(2,1)}), bf16[4,512,384]{2,1,0:T(8,128)(2,1)}, u32[]{:S(2)}, u32[]{:S(2)}) async-start(bf16[4,512,384]{2,1,0:T(8,128)(2,1)} %fusion.137), calls=%async_computation.1 | async-start | bytes 3145728 | tf_op jit(solution)/shard_map/all_to_all | solution.py:280
  1085.6 217.1 %reduce-scatter.16.cloned.1.call-start = ((), (), s32[]{:S(2)}) async-start(), calls=%async_computation.17 | async-start | bytes 5750784
  1116.3 405.0 %reduce-scatter.8.cloned.1.call-start = ((), (), s32[]{:S(2)}) async-start(), calls=%async_computation.12 | async-start | bytes 2211840 | tf_op jit(solution)/shard_map/reduce_scatter | solution.py:299
  1302.7 251.4 %all-reduce.4.cloned.1.call-start = ((), (), s32[]{:S(2)}) async-start(), calls=%async_computation.13 | async-start | bytes 1622016 | tf_op jit(solution)/shard_map/psum | solution.py:311
  1305.0 254.5 %reduce-scatter.10.cloned.1.call-start = ((), (), s32[]{:S(2)}) async-start(), calls=%async_computation.14 | async-start | bytes 17694720 | tf_op jit(solution)/shard_map/reduce_scatter | solution.py:299
  1325.6 291.0 %reduce-scatter.12.cloned.1.call-start = ((), (), s32[]{:S(2)}) async-start(), calls=%async_computation.15 | async-start | bytes 17694720 | tf_op jit(solution)/shard_map/reduce_scatter | solution.py:299
  1346.1 383.6 %reduce-scatter.14.cloned.1.call-start = ((), (), s32[]{:S(2)}) async-start(), calls=%async_computation.16 | async-start | bytes 17694720 | tf_op jit(solution)/shard_map/reduce_scatter | solution.py:299
  1396.7 31.8 %collective-permute-start.30 = (bf16[512,1536]{1,0:T(8,128)(2,1)S(1)}, bf16[512,1536]{1,0:T(8,128)(2,1)S(1)}, u32[]{:S(2)}, u32[]{:S(2)}) collective-permute-start(bf16[512,1536]{1,0:T(8,128)(2,1)S(1)} %get-tuple-element.187), channel_id=1, source_target_pairs={{0,1},{4,5},{8,9},{12,13},{16,17},{20,21},{24,25},{28,29}} | collective-permute-start | bytes 4718600 | tf_op jit(solution)/shard_map/ppermute | solution.py:77
  1401.2 27.3 %collective-permute-start.33 = (bf16[512,1536]{1,0:T(8,128)(2,1)S(1)}, bf16[512,1536]{1,0:T(8,128)(2,1)S(1)}, u32[]{:S(2)}, u32[]{:S(2)}) collective-permute-start(bf16[512,1536]{1,0:T(8,128)(2,1)S(1)} %get-tuple-element.188), channel_id=1, source_target_pairs={{3,2},{7,6},{11,10},{15,14},{19,18},{23,22},{27,26},{31,30}} | collective-permute-start | bytes 4718600 | tf_op jit(solution)/shard_map/ppermute | solution.py:78
  1431.3 29.6 %collective-permute-start.31 = (bf16[512,1536]{1,0:T(8,128)(2,1)S(1)}, bf16[512,1536]{1,0:T(8,128)(2,1)S(1)}, u32[]{:S(2)}, u32[]{:S(2)}) collective-permute-start(bf16[512,1536]{1,0:T(8,128)(2,1)S(1)} %get-tuple-element.185), channel_id=1, source_target_pairs={{0,1},{1,2},{4,5},{5,6},{8,9},{9,10},{12,13},{13,14},{16,17},{17,1... | collective-permute-start | bytes 4718600 | tf_op jit(solution)/shard_map/ppermute | solution.py:77
  1435.7 25.1 %collective-permute-start.34 = (bf16[512,1536]{1,0:T(8,128)(2,1)S(1)}, bf16[512,1536]{1,0:T(8,128)(2,1)S(1)}, u32[]{:S(2)}, u32[]{:S(2)}) collective-permute-start(bf16[512,1536]{1,0:T(8,128)(2,1)S(1)} %get-tuple-element.186), channel_id=1, source_target_pairs={{2,1},{3,2},{6,5},{7,6},{10,9},{11,10},{14,13},{15,14},{18,17},{19... | collective-permute-start | bytes 4718600 | tf_op jit(solution)/shard_map/ppermute | solution.py:78
  1463.6 81.1 %collective-permute-start.35 = (bf16[512,1536]{1,0:T(8,128)(2,1)}, bf16[512,1536]{1,0:T(8,128)(2,1)S(1)}, u32[]{:S(2)}, u32[]{:S(2)}) collective-permute-start(bf16[512,1536]{1,0:T(8,128)(2,1)} %get-tuple-element.184), channel_id=1, source_target_pairs={{1,0},{2,1},{3,2},{5,4},{6,5},{7,6},{9,8},{10,9},{11,10},{13,12},{... | collective-permute-start | bytes 4718600 | tf_op jit(solution)/shard_map/ppermute | solution.py:78
  1465.0 79.7 %collective-permute-start.32 = (bf16[512,1536]{1,0:T(8,128)(2,1)}, bf16[512,1536]{1,0:T(8,128)(2,1)}, u32[]{:S(2)}, u32[]{:S(2)}) collective-permute-start(bf16[512,1536]{1,0:T(8,128)(2,1)} %get-tuple-element.183), channel_id=1, source_target_pairs={{0,1},{1,2},{2,3},{4,5},{5,6},{6,7},{8,9},{9,10},{10,11},{12,13},{... | collective-permute-start | bytes 4718600 | tf_op jit(solution)/shard_map/ppermute | solution.py:77
  (110 other events, 3075.0 us)
Sparse Core Ops, SparseCore 0:
  10.5 30.5 all-gather.8
  43.0 38.9 all-gather.10
  83.9 85.4 all-gather.12
  171.1 85.4 all-gather.14
  258.3 85.4 all-gather.16
  1116.4 55.9 reduce-scatter.15
  1302.8 40.0 reduce-scatter.7
  1345.9 44.5 all-reduce.3
  1394.4 109.1 reduce-scatter.9
  1507.4 109.1 reduce-scatter.11
  1620.5 109.1 reduce-scatter.13

commit v2 on v1

--- a/solution.py
+++ b/solution.py
@@ -1,6 +1,10 @@
+import functools
+
 import jax
 import jax.numpy as jnp
 from jax import lax
+from jax.experimental import pallas as pl
+from jax.experimental.pallas import tpu as pltpu
 from jax.sharding import PartitionSpec as P
 
 HEADS = 24
@@ -33,23 +37,24 @@
 def rope_tables(positions, head_dim):
     half_dim = head_dim // 2
     frequency = rope_base ** (-(2.0 * jnp.arange(half_dim, dtype=full)) / head_dim)
-    angles = positions[:, None] * frequency[None, :]
+    angles = frequency[:, None] * positions[None, :]
     return (jnp.cos(angles), jnp.sin(angles))
 
 
 def rotate(values, cosine, sine_vals):
-    half_dim = values.shape[-1] // 2
-    front_half = values[..., :half_dim]
-    back_half = values[..., half_dim:]
+    half_dim = values.shape[-2] // 2
+    front_half = values[..., :half_dim, :]
+    back_half = values[..., half_dim:, :]
     return jnp.concatenate(
         [front_half * cosine - back_half * sine_vals, back_half * cosine + front_half * sine_vals],
-        axis=-1,
-    )
-
-
-def block_ids(lengths_row, positions):
+        axis=-2,
+    )
+
+
+def block_limits(lengths_row, positions):
     block_ends = jnp.cumsum(lengths_row)
-    return jnp.sum((positions[:, None] >= block_ends[None, :]).astype(jnp.int32), axis=1)
+    open_ends = jnp.where(block_ends[None, :] > positions[:, None], block_ends[None, :], positions.shape[0])
+    return jnp.min(open_ends, axis=1).astype(jnp.int32)
 
 
 def swiglu(gate_act, up_act):
@@ -85,51 +90,159 @@
     return jnp.stack(blocks)[(me - jnp.arange(n)) % n]
 
 
-def attention_forward(query, key, value, blocks, query_rows):
-    seq_len = key.shape[0]
-    attended_list = []
-    lse_list = []
-    for row_start in range(0, seq_len, query_rows):
-        row_stop = min(seq_len, row_start + query_rows + BLOCK)
-        scores = masked_scores(query, key, blocks, row_start, row_stop, query_rows)
-        row_peak = jnp.max(scores, axis=-1, keepdims=True)
-        exp_rows = jnp.exp(scores - row_peak)
-        exp_sum = jnp.sum(exp_rows, axis=-1, keepdims=True)
-        prob_low = (exp_rows / exp_sum).astype(low)
-        attended_list.append(dot("ghqk,kgd->qghd", prob_low, value[:row_stop]))
-        lse_list.append(row_peak + jnp.log(exp_sum))
-    return jnp.concatenate(attended_list, axis=0).astype(low), lse_list
-
-
-def masked_scores(query, key, blocks, row_start, row_stop, query_rows):
-    query_blk = query[row_start : row_start + query_rows]
-    scores = dot("qghd,kgd->ghqk", query_blk, key[:row_stop]) * attn_mult
-    allowed = blocks[None, :row_stop] <= blocks[row_start : row_start + query_rows, None]
-    return jnp.where(allowed, scores, masked_score)
-
-
-def attention_backward(query, key, value, blocks, lse_list, d_heads, query_rows):
-    seq_len, kv_here = key.shape[:2]
-    key_grad = jnp.zeros((seq_len, kv_here, HEAD_DIM), full)
-    value_grad = jnp.zeros((seq_len, kv_here, HEAD_DIM), full)
-    query_grads = []
-    for block_number, row_start in enumerate(range(0, seq_len, query_rows)):
-        row_stop = min(seq_len, row_start + query_rows + BLOCK)
-        scores = masked_scores(query, key, blocks, row_start, row_stop, query_rows)
-        prob_rows = jnp.exp(scores - lse_list[block_number])
-        d_out_blk = d_heads[row_start : row_start + query_rows]
-        d_probs = dot("qghd,kgd->ghqk", d_out_blk, value[:row_stop])
-        row_delta = jnp.sum(prob_rows * d_probs, axis=-1, keepdims=True)
-        d_scores = (prob_rows * (d_probs - row_delta)).astype(low)
-        query_blk = query[row_start : row_start + query_rows]
-        query_grads.append(dot("ghqk,kgd->qghd", d_scores, key[:row_stop]) * attn_mult)
-        key_grad = key_grad.at[:row_stop].add(
-            dot("ghqk,qghd->kgd", d_scores, query_blk) * attn_mult
-        )
-        value_grad = value_grad.at[:row_stop].add(
-            dot("ghqk,qghd->kgd", prob_rows.astype(low), d_out_blk)
-        )
-    return jnp.concatenate(query_grads, axis=0), key_grad, value_grad
+def nt(a, b):
+    return lax.dot_general(a, b, (((1,), (1,)), ((), ())), preferred_element_type=full)
+
+def nn(a, b):
+    return lax.dot_general(a, b, (((1,), (0,)), ((), ())), preferred_element_type=full)
+
+def beside(ref):
+    return jnp.concatenate([ref[0, h] for h in range(GROUP)], axis=1)
+
+def key_steps(i, seq_len, query_rows, key_rows):
+    free = (i * query_rows) // key_rows
+    need = ((i + 1) * query_rows + BLOCK - 1 + key_rows - 1) // key_rows
+    return free, jnp.minimum(need, seq_len // key_rows)
+
+def forward_kernel(seq_len, query_rows, key_rows, limit_ref, q_ref, k_ref, vt_ref, low_ref, out_ref, lse_ref):
+    i = pl.program_id(1)
+    qt = beside(q_ref)
+    width = GROUP * query_rows
+    limit = jnp.concatenate([limit_ref[...]] * GROUP, axis=1)
+
+    def step(masked, j, carry):
+        peak, total, acc = carry
+        start = pl.multiple_of(j * key_rows, key_rows)
+        s = nn(k_ref[0, pl.ds(start, key_rows), :], qt)
+        if masked:
+            place = start + lax.broadcasted_iota(jnp.int32, (key_rows, 1), 0)
+            s = jnp.where(place < limit, s, masked_score)
+        new_peak = jnp.maximum(peak, jnp.max(s, axis=0, keepdims=True))
+        shrink = jnp.exp(peak - new_peak)
+        p = jnp.exp(s - new_peak)
+        total = shrink * total + jnp.sum(p, axis=0, keepdims=True)
+        acc = shrink * acc + nn(vt_ref[0, :, pl.ds(start, key_rows)], p.astype(low))
+        return new_peak, total, acc
+
+    free, need = key_steps(i, seq_len, query_rows, key_rows)
+    carry = (
+        jnp.full((1, width), masked_score, full),
+        jnp.zeros((1, width), full),
+        jnp.zeros((HEAD_DIM, width), full),
+    )
+    carry = lax.fori_loop(0, free, lambda j, c: step(False, j, c), carry)
+    peak, total, acc = lax.fori_loop(free, need, lambda j, c: step(True, j, c), carry)
+    out = acc / total
+    lse = peak + jnp.log(total)
+    for h in range(GROUP):
+        cols = slice(h * query_rows, (h + 1) * query_rows)
+        out_ref[0, h] = out[:, cols]
+        low_ref[0, pl.ds(h * HEAD_DIM, HEAD_DIM), :] = out[:, cols].astype(low)
+        lse_ref[0, h] = lse[:, cols]
+
+def attention_forward(qt, k_rows, vt, limit, shard_len):
+    kv_here, _, _, seq_len = qt.shape
+    query_rows = min(256, shard_len)
+    key_rows = min(512, seq_len)
+    per = shard_len // query_rows
+    return pl.pallas_call(
+        functools.partial(forward_kernel, seq_len, query_rows, key_rows),
+        grid=(kv_here, seq_len // query_rows),
+        in_specs=[
+            pl.BlockSpec((1, query_rows), lambda g, i: (0, i)),
+            pl.BlockSpec((1, GROUP, HEAD_DIM, query_rows), lambda g, i: (g, 0, 0, i)),
+            pl.BlockSpec((1, seq_len, HEAD_DIM), lambda g, i: (g, 0, 0)),
+            pl.BlockSpec((1, HEAD_DIM, seq_len), lambda g, i: (g, 0, 0)),
+        ],
+        out_specs=[
+            pl.BlockSpec((1, GROUP * HEAD_DIM, query_rows), lambda g, i: (i // per, g, i % per)),
+            pl.BlockSpec((1, GROUP, HEAD_DIM, query_rows), lambda g, i: (g, 0, 0, i)),
+            pl.BlockSpec((1, GROUP, 1, query_rows), lambda g, i: (g, 0, 0, i)),
+        ],
+        out_shape=[
+            jax.ShapeDtypeStruct((seq_len // shard_len, kv_here * GROUP * HEAD_DIM, shard_len), low),
+            jax.ShapeDtypeStruct((kv_here, GROUP, HEAD_DIM, seq_len), full),
+            jax.ShapeDtypeStruct((kv_here, GROUP, 1, seq_len), full),
+        ],
+        compiler_params=pltpu.CompilerParams(vmem_limit_bytes=40 * 2**20),
+        name="attention_forward",
+    )(limit, qt, k_rows, vt)
+
+def backward_kernel(seq_len, query_rows, key_rows, limit_ref, q_ref, k_ref, v_ref, kt_ref, out_ref, lse_ref, dout_ref, dq_ref, dk_ref, dv_ref, dk_acc, dv_acc):
+    i = pl.program_id(1)
+
+    @pl.when(i == 0)
+    def _():
+        dk_acc[...] = jnp.zeros_like(dk_acc)
+        dv_acc[...] = jnp.zeros_like(dv_acc)
+
+    qt = beside(q_ref)
+    limit = jnp.concatenate([limit_ref[...]] * GROUP, axis=1)
+    dout = jnp.concatenate([dout_ref[0, pl.ds(h * HEAD_DIM, HEAD_DIM), :] for h in range(GROUP)], axis=1)
+    delta = jnp.sum(dout.astype(full) * beside(out_ref), axis=0, keepdims=True)
+    lse = beside(lse_ref)
+
+    def step(masked, j, dq):
+        start = pl.multiple_of(j * key_rows, key_rows)
+        keys = pl.ds(start, key_rows)
+        s = nn(k_ref[0, keys, :], qt)
+        if masked:
+            place = start + lax.broadcasted_iota(jnp.int32, (key_rows, 1), 0)
+            s = jnp.where(place < limit, s, masked_score)
+        p = jnp.exp(s - lse)
+        dp = nn(v_ref[0, keys, :], dout)
+        ds = (p * (dp - delta)).astype(low)
+        dk_acc[:, keys] += nt(qt, ds)
+        dv_acc[:, keys] += nt(dout, p.astype(low))
+        return dq + nn(kt_ref[0, :, keys], ds)
+
+    free, need = key_steps(i, seq_len, query_rows, key_rows)
+    dq = jnp.zeros((HEAD_DIM, GROUP * query_rows), full)
+    dq = lax.fori_loop(0, free, lambda j, c: step(False, j, c), dq)
+    dq = lax.fori_loop(free, need, lambda j, c: step(True, j, c), dq) * attn_mult
+    for h in range(GROUP):
+        dq_ref[0, h] = dq[:, h * query_rows : (h + 1) * query_rows].astype(low)
+
+    @pl.when(i == pl.num_programs(1) - 1)
+    def _():
+        dk_ref[0] = dk_acc[...].astype(low)
+        dv_ref[0] = dv_acc[...].astype(low)
+
+def attention_backward(qt, k_rows, v_rows, kt, limit, out, lse, d_out):
+    kv_here, _, _, seq_len = qt.shape
+    shard_len = d_out.shape[2]
+    query_rows = min(256, shard_len)
+    key_rows = min(512, seq_len)
+    per = shard_len // query_rows
+    quarter = lambda g, i: (g, 0, 0, i)
+    whole = lambda g, i: (g, 0, 0)
+    return pl.pallas_call(
+        functools.partial(backward_kernel, seq_len, query_rows, key_rows),
+        grid=(kv_here, seq_len // query_rows),
+        in_specs=[
+            pl.BlockSpec((1, query_rows), lambda g, i: (0, i)),
+            pl.BlockSpec((1, GROUP, HEAD_DIM, query_rows), quarter),
+            pl.BlockSpec((1, seq_len, HEAD_DIM), whole),
+            pl.BlockSpec((1, seq_len, HEAD_DIM), whole),
+            pl.BlockSpec((1, HEAD_DIM, seq_len), whole),
+            pl.BlockSpec((1, GROUP, HEAD_DIM, query_rows), quarter),
+            pl.BlockSpec((1, GROUP, 1, query_rows), quarter),
+            pl.BlockSpec((1, GROUP * HEAD_DIM, query_rows), lambda g, i: (i // per, g, i % per)),
+        ],
+        out_specs=[
+            pl.BlockSpec((1, GROUP, HEAD_DIM, query_rows), quarter),
+            pl.BlockSpec((1, HEAD_DIM, seq_len), whole),
+            pl.BlockSpec((1, HEAD_DIM, seq_len), whole),
+        ],
+        out_shape=[
+            jax.ShapeDtypeStruct((kv_here, GROUP, HEAD_DIM, seq_len), low),
+            jax.ShapeDtypeStruct((kv_here, HEAD_DIM, seq_len), low),
+            jax.ShapeDtypeStruct((kv_here, HEAD_DIM, seq_len), low),
+        ],
+        scratch_shapes=[pltpu.VMEM((HEAD_DIM, seq_len), full), pltpu.VMEM((HEAD_DIM, seq_len), full)],
+        compiler_params=pltpu.CompilerParams(vmem_limit_bytes=40 * 2**20),
+        name="attention_backward",
+    )(limit, qt, k_rows, v_rows, kt, out, lse, d_out)
 
 
 def shards(
@@ -179,8 +292,8 @@
     valid_rows = valid_mask.reshape(shard_len).astype(full)
     valid_count = lax.psum(jnp.sum(valid_rows), ("fsdp", "seq"))
 
-    routes_all = lax.all_gather(routes.reshape(shard_len, top_count), "seq", axis=0)
-    routes_rel = routes_all[(me - jnp.arange(seq_devs)) % seq_devs]
+    routes_rel = jnp.stack(line_gather(routes.reshape(shard_len, top_count).T))
+    routes_rel = jnp.swapaxes(routes_rel, 1, 2)
     expert_ids = jnp.arange(expert_total, dtype=jnp.int32)
     member = jnp.any(routes_rel[:, :, :, None] == expert_ids, axis=2)
     own_member = lax.dynamic_slice_in_dim(member, me * experts_here, experts_here, 2)
@@ -191,25 +304,24 @@
     onehot = slot_of[:, :, None, :] == jnp.arange(slots, dtype=jnp.int32)[None, None, :, None]
     pick = onehot.astype(low)
 
-    x_all = by_place(line_gather(x_low)).reshape(seq_len, width).astype(full)
-    normed_one = rms_norm(x_all, full_g1).astype(low)
-    qkv_rows = dot("td,dc->tc", normed_one, full_qkv)
-    qkv_rows = qkv_rows.reshape(seq_len, kv_here, GROUP + 2, HEAD_DIM)
+    x_all = by_place(line_gather(x_low)).reshape(seq_len, width)
+    x_all, valid_count = lax.optimization_barrier((x_all, valid_count))
+    normed_one = rms_norm(x_all.astype(full), full_g1).astype(low)
+    qkv_rows = dot("td,dc->ct", normed_one, full_qkv)
+    qkv_rows = qkv_rows.reshape(kv_here, GROUP + 2, HEAD_DIM, seq_len)
     positions = jnp.arange(seq_len, dtype=jnp.int32)
     cosine, sine_vals = rope_tables(positions.astype(full), HEAD_DIM)
-    cos_rows = cosine[:, None, None, :]
-    sin_rows = sine_vals[:, None, None, :]
-    turned = rotate(qkv_rows[:, :, : GROUP + 1], cos_rows, sin_rows).astype(low)
-    query = turned[:, :, :GROUP]
-    key = turned[:, :, GROUP]
-    value = qkv_rows[:, :, GROUP + 1].astype(low)
-    blocks = block_ids(block_lengths[0], positions)
-    query_rows = min(512, seq_len)
-    attended, lse_list = attention_forward(query, key, value, blocks, query_rows)
-    attended = attended.reshape(seq_devs, shard_len, heads_w)
+    turned = rotate(qkv_rows[:, : GROUP + 1], cosine, sine_vals).astype(low)
+    query = turned[:, :GROUP] * jnp.asarray(attn_mult, low)
+    key = turned[:, GROUP]
+    value = qkv_rows[:, GROUP + 1].astype(low)
+    key_rows = jnp.swapaxes(key, 1, 2)
+    value_rows = jnp.swapaxes(value, 1, 2)
+    limit = block_limits(block_lengths[0], positions)[None]
+    attended, out_heads, lse = attention_forward(query, key_rows, value, limit, shard_len)
     attn_rows = lax.all_to_all(attended, "seq", split_axis=0, concat_axis=0, tiled=True)
-    out_rows = full_out.reshape(seq_devs, heads_w, width)
-    projected = dot("gtk,gkd->td", attn_rows, out_rows)
+    attn_rows = attn_rows.reshape(HEADS * HEAD_DIM, shard_len)
+    projected = dot("kt,kd->td", attn_rows, full_out)
     hidden = x_low.astype(full) + resid_mult * projected
     normed_two, norm_two_pull = jax.vjp(rms_norm, hidden, full_g2)
 
@@ -237,13 +349,11 @@
     activations = output_f32.astype(low).reshape(1, shard_len, width)
     error_rows = output_f32 - teacher.astype(full).reshape(shard_len, width)
     weighted = valid_rows[:, None] * error_rows
-    squares = lax.psum(jnp.sum(weighted * error_rows), ("fsdp", "seq"))
-    loss_value = squares / (valid_count * width)
+    squares = jnp.sum(weighted * error_rows)
     d_out = weighted * (tokens_all / valid_count)
 
     d_mix = resid_mult * d_out
-    mix_dot = lax.all_gather(jnp.sum(d_mix * mixture, axis=1), "seq", axis=0)
-    mix_dot = mix_dot[(me - jnp.arange(seq_devs)) % seq_devs]
+    mix_dot = jnp.stack(line_gather(jnp.sum(d_mix * mixture, axis=1)))
     d_tokens = jnp.stack(line_gather(d_mix.astype(low)))
     d_rows = dot("enct,ntd->encd", pick, d_tokens).astype(low)
     d_rows = d_rows.reshape(experts_here, seq_devs * slots, width)
@@ -272,35 +382,42 @@
     )
     router_part = dot("ntd,nte->de", tokens, d_logits)
     d_normed_two = line_scatter([d_normed_parts[k] for k in range(seq_devs)])
+    d_normed_two, gate_part, up_part, down_part = lax.optimization_barrier(
+        (d_normed_two, gate_part.astype(low), up_part.astype(low), down_part.astype(low))
+    )
+    gate_part, up_part, down_part = (
+        lax.psum_scatter(part, "fsdp", scatter_dimension=1, tiled=True)
+        for part in (gate_part, up_part, down_part)
+    )
 
     d_hidden_norm, gain_two_part = norm_two_pull(d_normed_two)
     d_hidden = d_out + d_hidden_norm
     d_proj = (resid_mult * d_hidden).astype(low)
-    d_attended = dot("td,gkd->gtk", d_proj, out_rows).astype(low)
-    d_heads = lax.all_to_all(d_attended, "seq", split_axis=0, concat_axis=0, tiled=True)
-    out_part = dot("gtk,td->gkd", attn_rows, d_proj).astype(low).reshape(HEADS * HEAD_DIM, width)
-    d_heads = d_heads.reshape(seq_len, kv_here, GROUP, HEAD_DIM)
+    d_attended = dot("kd,td->kt", full_out, d_proj).astype(low)
+    d_heads = lax.all_to_all(
+        d_attended.reshape(seq_devs, heads_w, shard_len), "seq", split_axis=0, concat_axis=0, tiled=True
+    )
+    out_part = dot("kt,td->kd", attn_rows, d_proj).astype(low)
     query_grad, key_grad, value_grad = attention_backward(
-        query, key, value, blocks, lse_list, d_heads, query_rows
-    )
-    d_turned = jnp.concatenate([query_grad, key_grad[:, :, None]], axis=2).astype(low).astype(full)
-    d_turned = rotate(d_turned, cos_rows, -sin_rows).astype(low)
-    d_qkv = jnp.concatenate([d_turned, value_grad[:, :, None].astype(low)], axis=2)
-    d_qkv = d_qkv.reshape(seq_len, group_w)
-    qkv_part = dot("td,tc->dc", normed_one, d_qkv).astype(low)
-    d_normed_parts = dot("tc,dc->td", d_qkv, full_qkv).reshape(seq_devs, shard_len, width)
+        query, key_rows, value_rows, key, limit, out_heads, lse, d_heads
+    )
+    d_turned = jnp.concatenate([query_grad, key_grad[:, None]], axis=1).astype(full)
+    d_turned = rotate(d_turned, cosine, -sine_vals).astype(low)
+    d_qkv = jnp.concatenate([d_turned, value_grad[:, None]], axis=1).reshape(group_w, seq_len)
+    qkv_part = dot("td,ct->dc", normed_one, d_qkv).astype(low)
+    d_normed_parts = dot("ct,dc->td", d_qkv, full_qkv).reshape(seq_devs, shard_len, width)
     d_normed_parts = d_normed_parts[(me - jnp.arange(seq_devs)) % seq_devs]
     d_normed_one = line_scatter([d_normed_parts[k] for k in range(seq_devs)])
     x_rows = x_low.astype(full)
     _, norm_one_pull = jax.vjp(lambda v: rms_norm(v, full_g1), x_rows)
     input_grad = (d_hidden + norm_one_pull(d_normed_one)[0]).reshape(1, shard_len, width)
 
-    def rows_sum(part, dim):
-        return lax.psum_scatter(part, "fsdp", scatter_dimension=dim, tiled=True)
-
-    gate_grad = rows_sum(gate_part.astype(low), 1).astype(full)
-    up_grad = rows_sum(up_part.astype(low), 1).astype(full)
-    down_grad = rows_sum(down_part.astype(low), 1).astype(full)
+    def rows_sum(part):
+        return lax.psum_scatter(part, "fsdp", scatter_dimension=0, tiled=True)
+
+    gate_grad = gate_part.astype(full)
+    up_grad = up_part.astype(full)
+    down_grad = down_part.astype(full)
     own_columns = jnp.zeros((width, expert_total), full)
     own_columns = lax.dynamic_update_slice_in_dim(
         own_columns, router_part, me * experts_here, 1
@@ -308,12 +425,14 @@
     dense_part = jnp.concatenate(
         [out_part, own_columns.astype(low), gain_two_part[:, None].astype(low)], axis=1
     )
-    dense_part = lax.psum(rows_sum(dense_part, 0), "seq").astype(full)
+    dense_part = lax.psum(rows_sum(dense_part), "seq").astype(full)
     out_grad = dense_part[:, :width]
     router_grad = dense_part[:, width : width + expert_total]
     gain_two_grad = dense_part[:, width + expert_total]
-    qkv_grad = lax.all_gather(rows_sum(qkv_part, 0), "seq", axis=1, tiled=True).astype(full)
+    qkv_grad = lax.all_gather(rows_sum(qkv_part), "seq", axis=1, tiled=True).astype(full)
     gain_one_grad = jnp.sum(qkv_grad * w_qkv.astype(full), axis=1) / gain_one.astype(full)
+    squares, input_grad = lax.optimization_barrier((squares, input_grad))
+    loss_value = lax.psum(squares, ("fsdp", "seq")) / (valid_count * width)
     return (
         activations,
         loss_value,

time: 1750 us -> 1670 us (0.954)
  matrix products: 512 us -> 345 us
  Pallas kernels: 0 us -> 96.2 us
  waiting for transfers between devices: 552 us -> 643 us
  other arithmetic: 182 us -> 101 us
  blocking collectives: 266 us -> 211 us
  starting transfers between devices: 97.3 us -> 136 us
    dot_general x47 -> x23, matrix products: 512 us -> 345 us  [dot(): return jnp.einsum(spec, left, right, preferred_element_type=full)]
    pallas_call x0 -> x2, Pallas kernels: none -> 96.2 us  [the longest x1 56.5 us: attention_backward(): pl.pallas_call(functools.partial(backward_kernel, seq_len, query_rows, ke...]
    all_gather x3 -> x1, blocking collectives: 127 us -> 32.2 us  [shards(): lax.all_gather(rows_sum(qkv_part), 'seq', axis=1, tiled=True).astype(full)]
    convert_element_type x9 -> x4, other arithmetic: 66.3 us -> 12.6 us  [the longest x1 4.12 us: shards(): down_grad = down_part.astype(full)]
    ppermute x9 -> x15, waiting for transfers between devices: 123 us -> 177 us  [line_gather(): lax.ppermute(lefts[-1], 'seq', [(i, i - 1) for i in range(1, n - k + 1)])]
    reduce_scatter x4, waiting for transfers between devices: 162 us -> 212 us  [the longest x3 212 us: shards(): lax.psum_scatter(part, 'fsdp', scatter_dimension=1, tiled=True)]
    psum x1, blocking collectives: 47.3 us -> 89.2 us  [shards(): valid_count = lax.psum(jnp.sum(valid_rows), ('fsdp', 'seq'))]
    reduce_sum x6 -> x1, other arithmetic: 29.1 us -> 5.06 us  [shards(): mix_dot = jnp.stack(line_gather(jnp.sum(d_mix * mixture, axis=1)))]
  transfers between devices with their start and end apart: 48 -> 60, of which waited for: 20 -> 26; matrix products, arithmetic and copies ran while one was open for 33% -> 17% of each run, Pallas kernels for 0% -> 6%
where the time goes in v2:
time: 1670 us; the launch traced here: 1660 us
  waiting for transfers between devices  643 us (39%)
  matrix products  345 us (21%)
  blocking collectives  211 us (13%)
  starting transfers between devices  136 us (8%)
  local copies, waits for them, and re-layouts  110 us (7%)
  other arithmetic  101 us (6%)
  Pallas kernels  96.2 us (6%)
  between operations  18.7 us (1%)
    dot_general x23, matrix products, dot(): return jnp.einsum(spec, left, right, preferred_element_type=full)  345 us
    reduce_scatter x3, waiting for transfers between devices, shards(): lax.psum_scatter(part, 'fsdp', scatter_dimension=1, tiled=True)  212 us
    ppermute x15, waiting for transfers between devices, line_gather(): lax.ppermute(lefts[-1], 'seq', [(i, i - 1) for i in range(1, n - k + 1)])  177 us
    ppermute x9, waiting for transfers between devices, line_scatter(): lax.ppermute(to_right.astype(low), 'seq', [(i, i + 1) for i in range(n -...  165 us
    psum x1, blocking collectives, shards(): valid_count = lax.psum(jnp.sum(valid_rows), ('fsdp', 'seq'))  89.2 us
    ppermute x9, starting transfers between devices, line_scatter(): lax.ppermute(to_right.astype(low), 'seq', [(i, i + 1) for i in range(n -...  63.1 us
    ppermute x15, waiting for transfers between devices, line_gather(): lax.ppermute(rights[-1], 'seq', [(i, i + 1) for i in range(k - 1, n - 1)])  62.4 us
    pallas_call x1, Pallas kernels, attention_backward(): pl.pallas_call(functools.partial(backward_kernel, seq_len, query_rows, ke...  56.5 us
  transfers between devices with their start and end apart: 60, of which 26 were waited for; matrix products, arithmetic and copies ran while one was open for 17% of the time, Pallas kernels for 6%

profile of v2, /device:TPU:0, one launch (start us, length us, event | category | flops | bytes accessed | tf_op | source)
XLA Modules:
  0.0 1661.4 jit_solution(1443930392778595696)
XLA Ops:
  17.5 32.2 %collective-permute-done = bf16[512,1536]{1,0:T(8,128)(2,1)S(1)} collective-permute-done((bf16[512,1536]{1,0:T(8,128)(2,1)S(1)}, bf16[512,1536]{1,0:T(8,128)(2,1)S(1)}, u32[]{:S(2)}, u32[]{:S(2)}) %collective-permute-start) | collective-permute-done | bytes 1572896 | tf_op jit(solution)/shard_map/ppermute | solution.py:69
  58.0 89.2 %psum.21 = f32[]{:T(128)} all-reduce(f32[]{:T(128)} %convert_reduce_fusion), channel_id=1, replica_groups=mesh['fsdp'=8,'seq'=4] {'fsdp','seq'}, use_global_device_ids=true, to_apply=%region_3.4 | all-reduce | flops 1 | bytes 8 | tf_op jit(solution)/shard_map/psum | solution.py:293
  147.4 10.8 all-gather
  167.7 31.8 %collective-permute-done.3 = bf16[512,1536]{1,0:T(8,128)(2,1)S(1)} collective-permute-done((bf16[512,1536]{1,0:T(8,128)(2,1)}, bf16[512,1536]{1,0:T(8,128)(2,1)S(1)}, u32[]{:S(2)}, u32[]{:S(2)}) %collective-permute-start.3) | collective-permute-done | bytes 1572896 | tf_op jit(solution)/shard_map/ppermute | solution.py:70
  214.0 7.3 fusion.57
  226.7 39.8 %attention_forward.1 = (bf16[4,384,512]{2,1,0:T(8,128)(2,1)S(1)}, f32[2,3,64,2048]{3,2,1,0:T(8,128)S(1)}, f32[2,3,1,2048]{3,2,1,0:T(1,128)S(1)}) custom-call(s32[1,2048]{1,0:T(1,128)S(1)} %bitcast.243, bf16[2,3,64,2048]{3,2,1,0:T(8,128)(2,1)S(1)} %copy.136.q_ref, bf16[2,2048,64]{2,1,0:T(8,128)(2,1)S(1)} %copy.137.k_ref, ...), custom_call_target="tpu_custom_call" | custom-call | tf_op jit(solution)/shard_map/attention_forward/pallas_call | solution.py:148
  268.2 40.2 %all_to_all.10 = bf16[4,384,512]{2,1,0:T(8,128)(2,1)} all-to-all(bf16[4,384,512]{2,1,0:T(8,128)(2,1)S(1)} %get-tuple-element.26), channel_id=1, replica_groups=mesh['fsdp'=8,'seq'=4] {'seq'}, dimensions={0} | all-to-all | bytes 3145728 | tf_op jit(solution)/shard_map/all_to_all | solution.py:322
  321.4 30.0 %collective-permute-done.12 = bf16[512,1536]{1,0:T(8,128)(2,1)} collective-permute-done((bf16[512,1536]{1,0:T(8,128)(2,1)S(1)}, bf16[512,1536]{1,0:T(8,128)(2,1)}, u32[]{:S(2)}, u32[]{:S(2)}) %collective-permute-start.12) | collective-permute-done | bytes 1572896 | tf_op jit(solution)/shard_map/ppermute | solution.py:69
  365.0 28.2 %collective-permute-done.7 = s32[8,512]{1,0:T(8,128)S(1)} collective-permute-done((s32[8,512]{1,0:T(8,128)S(1)}, s32[8,512]{1,0:T(8,128)S(1)}, u32[]{:S(2)}, u32[]{:S(2)}) %collective-permute-start.7) | collective-permute-done | bytes 16416 | tf_op jit(solution)/shard_map/ppermute | solution.py:70
  413.8 25.0 %collective-permute-done.15 = bf16[512,1536]{1,0:T(8,128)(2,1)S(1)} collective-permute-done((bf16[512,1536]{1,0:T(8,128)(2,1)}, bf16[512,1536]{1,0:T(8,128)(2,1)S(1)}, u32[]{:S(2)}, u32[]{:S(2)}) %collective-permute-start.15) | collective-permute-done | bytes 1572896 | tf_op jit(solution)/shard_map/ppermute | solution.py:70
  444.8 16.7 %convert_bitcast_fusion.1 = bf16[10,4,160,1536]{3,2,0,1:T(8,128)(2,1)} fusion(s32[10,4,512]{2,0,1:T(8,128)S(1)} %fusion.64, bf16[1,512,1536]{2,1,0:T(8,128)(2,1)S(1)} %select_bitcast_fusion.3, bf16[1,512,1536]{2,1,0:T(8,128)(2,1)S(1)} %select_bitcast_fusion.4, bf16[1,512,1536]{2,1,0:T(8,128)(2,1)S(1)} %select_bitcast_fusion.5, ...), kind=kOutput, calls=%fused_computation.10 | convolution fusion | flops 10104602624 | bytes 26034176 | tf_op jit(solution)/shard_map/enct,ntd->encd/dot_general | solution.py:29
  461.5 16.4 copy.139
  477.8 22.5 %fusion.90 = f32[10,640,512]{1,2,0:T(8,128)} fusion(bf16[10,640,1536]{2,1,0:T(8,128)(2,1)} %bitcast.251, bf16[10,1536,512]{2,1,0:T(8,128)(2,1)} %all-gather.11.cloned.1.call-done), kind=kOutput, calls=%fused_computation.211 | convolution fusion | flops 10066329600 | bytes 48496640 | tf_op jit(solution)/shard_map/erd,edf->erf/dot_general | solution.py:29
  500.3 27.9 %multiply_convert_fusion.1 = (bf16[10,640,512]{1,2,0:T(8,128)(2,1)}, f32[10,640,512]{1,2,0:T(8,128)}) fusion(f32[10,640,512]{1,2,0:T(8,128)} %fusion.90, bf16[10,640,1536]{2,1,0:T(8,128)(2,1)} %bitcast.252, bf16[10,1536,512]{2,1,0:T(8,128)(2,1)} %all-gather.13.cloned.1.call-done), kind=kOutput, calls=%fused_computation.26 | convolution fusion | flops 10085990400 | bytes 68157440 | tf_op jit(solution)/shard_map/erd,edf->erf/dot_general | solution.py:29
  528.3 21.1 %convolution_convert_fusion = bf16[10,640,1536]{2,1,0:T(8,128)(2,1)} fusion(bf16[10,640,512]{1,2,0:T(8,128)(2,1)} %get-tuple-element.141, bf16[10,512,1536]{2,1,0:T(8,128)(2,1)} %all-gather.15.cloned.1.call-done), kind=kOutput, calls=%fused_computation.11 | convolution fusion | flops 10076160000 | bytes 41943040 | tf_op jit(solution)/shard_map/erf,efd->erd/dot_general | solution.py:29
  549.4 18.7 %fusion.22 = f32[4,512,1536]{2,1,0:T(8,128)} fusion(bf16[10,4,160,1536]{3,2,1,0:T(8,128)(2,1)} %bitcast.281, s32[10,4,512]{2,0,1:T(8,128)S(1)} %fusion.64, bf16[10,4,160]{2,0,1:T(8,128)(2,1)S(1)} %convert_element_type.316), kind=kOutput, calls=%fused_computation.42 | convolution fusion | flops 10072883200 | bytes 32338432 | tf_op jit(solution)/shard_map/enct,encd->ntd/dot_general | solution.py:29
  575.6 26.5 %collective-permute-done.18 = bf16[512,1536]{1,0:T(8,128)(2,1)S(1)} collective-permute-done((bf16[512,1536]{1,0:T(8,128)(2,1)S(1)}, bf16[512,1536]{1,0:T(8,128)(2,1)S(1)}, u32[]{:S(2)}, u32[]{:S(2)}) %collective-permute-start.18) | collective-permute-done | bytes 1572896 | tf_op jit(solution)/shard_map/ppermute | solution.py:82
  610.2 25.6 %collective-permute-done.19 = bf16[512,1536]{1,0:T(8,128)(2,1)S(1)} collective-permute-done((bf16[512,1536]{1,0:T(8,128)(2,1)S(1)}, bf16[512,1536]{1,0:T(8,128)(2,1)S(1)}, u32[]{:S(2)}, u32[]{:S(2)}) %collective-permute-start.19) | collective-permute-done | bytes 1572896 | tf_op jit(solution)/shard_map/ppermute | solution.py:82
  638.6 10.6 collective-permute-start.20
  651.2 23.2 %collective-permute-done.20 = bf16[512,1536]{1,0:T(8,128)(2,1)} collective-permute-done((bf16[512,1536]{1,0:T(8,128)(2,1)}, bf16[512,1536]{1,0:T(8,128)(2,1)}, u32[]{:S(2)}, u32[]{:S(2)}) %collective-permute-start.20) | collective-permute-done | bytes 1572896 | tf_op jit(solution)/shard_map/ppermute | solution.py:82
  679.7 6.9 multiply_convert_fusion.4
  693.6 27.5 %collective-permute-done.25 = bf16[512,1536]{1,0:T(8,128)(2,1)S(1)} collective-permute-done((bf16[512,1536]{1,0:T(8,128)(2,1)S(1)}, bf16[512,1536]{1,0:T(8,128)(2,1)S(1)}, u32[]{:S(2)}, u32[]{:S(2)}) %collective-permute-start.25) | collective-permute-done | bytes 1572896 | tf_op jit(solution)/shard_map/ppermute | solution.py:70
  724.3 31.2 %collective-permute-done.26 = bf16[512,1536]{1,0:T(8,128)(2,1)} collective-permute-done((bf16[512,1536]{1,0:T(8,128)(2,1)S(1)}, bf16[512,1536]{1,0:T(8,128)(2,1)}, u32[]{:S(2)}, u32[]{:S(2)}) %collective-permute-start.26) | collective-permute-done | bytes 1572896 | tf_op jit(solution)/shard_map/ppermute | solution.py:70
  769.4 14.0 collective-permute-done.31
  798.0 16.7 %convert_bitcast_fusion = bf16[10,4,160,1536]{3,2,0,1:T(8,128)(2,1)} fusion(s32[10,4,512]{2,0,1:T(8,128)S(1)} %fusion.64, bf16[1,512,1536]{2,1,0:T(8,128)(2,1)S(1)} %select_bitcast_fusion, bf16[1,512,1536]{2,1,0:T(8,128)(2,1)S(1)} %select_bitcast_fusion.1, bf16[1,512,1536]{2,1,0:T(8,128)(2,1)S(1)} %select_bitcast_fusion.2, bf16[1,512,1536]{2,1,0:T(8,128)(2,1)} %bitcast.268), kind=kOutput, calls=%fused_computation.9 | convolution fusion | flops 10104602624 | bytes 26034176 | tf_op jit(solution)/shard_map/enct,ntd->encd/dot_general | solution.py:29
  814.8 16.4 copy.142
  831.1 34.6 %multiply_convert_fusion = (bf16[10,640,512]{1,2,0:T(8,128)(2,1)}, bf16[10,640,512]{1,2,0:T(8,128)(2,1)}, f32[10,640]{1,0:T(8,128)S(1)}) fusion(f32[10,640]{1,0:T(8,128)S(1)} %mul.432, f32[10,640,512]{1,2,0:T(8,128)} %fusion.90, f32[10,640,512]{1,2,0:T(8,128)} %get-tuple-element.142, bf16[10,640,512]{1,2,0:T(8,128)(2,1)} %get-tuple-element.141, ...), kind=kOutput, calls=%fused_computation.25 | convolution fusion | flops 10125305856 | bytes 81315840 | tf_op jit(solution)/shard_map/erd,efd->erf/dot_general | solution.py:29
  873.2 25.3 %fusion.91 = f32[10,640,1536]{2,1,0:T(8,128)} fusion(bf16[10,640,512]{1,2,0:T(8,128)(2,1)} %get-tuple-element.107, bf16[10,1536,512]{2,1,0:T(8,128)(2,1)} %all-gather.11.cloned.1.call-done), kind=kOutput, calls=%fused_computation.212 | convolution fusion | flops 10066329600 | bytes 61603840 | tf_op jit(solution)/shard_map/erf,edf->erd/dot_general | solution.py:29
  898.5 28.5 %add_convert_fusion = bf16[10,640,1536]{2,1,0:T(8,128)(2,1)} fusion(f32[10,640,1536]{2,1,0:T(8,128)} %fusion.91, bf16[10,640,512]{1,2,0:T(8,128)(2,1)} %get-tuple-element.106, bf16[10,1536,512]{2,1,0:T(8,128)(2,1)} %all-gather.13.cloned.1.call-done), kind=kOutput, calls=%fused_computation.3 | convolution fusion | flops 10085990400 | bytes 81264640 | tf_op jit(solution)/shard_map/erf,edf->erd/dot_general | solution.py:29
  927.1 18.6 %fusion.1 = f32[4,512,1536,1]{2,1,3,0:T(8,128)} fusion(bf16[10,4,160,1536]{3,2,1,0:T(8,128)(2,1)} %bitcast.245, s32[10,4,512]{2,0,1:T(8,128)S(1)} %fusion.64), kind=kOutput, calls=%fused_computation.4 | convolution fusion | flops 10069606400 | bytes 32325632 | tf_op jit(solution)/shard_map/enct,encd->ntd/dot_general | solution.py:29
  945.7 6.5 bitcast_add_fusion
  964.4 20.4 %convolution_convert_fusion.1 = bf16[10,512,1536]{2,1,0:T(8,128)(2,1)} fusion(bf16[10,640,1536]{2,1,0:T(8,128)(2,1)} %bitcast.256, bf16[10,640,512]{1,2,0:T(8,128)(2,1)} %get-tuple-element.141, f32[10,640]{1,0:T(8,128)S(1)} %mul.432), kind=kOutput, calls=%fused_computation.16 | convolution fusion | flops 10084024320 | bytes 41968640 | tf_op jit(solution)/shard_map/erf,erd->efd/dot_general | solution.py:29
  998.4 20.4 %convolution_convert_fusion.2 = bf16[10,1536,512]{2,1,0:T(8,128)(2,1)} fusion(bf16[10,640,1536]{2,1,0:T(8,128)(2,1)} %bitcast.253, bf16[10,640,512]{1,2,0:T(8,128)(2,1)} %get-tuple-element.106), kind=kOutput, calls=%fused_computation.17 | convolution fusion | flops 10074193920 | bytes 41943040 | tf_op jit(solution)/shard_map/erd,erf->edf/dot_general | solution.py:29
  1025.2 23.6 %collective-permute-start.38 = (bf16[512,1536]{1,0:T(8,128)(2,1)}, bf16[512,1536]{1,0:T(8,128)(2,1)}, u32[]{:S(2)}, u32[]{:S(2)}) collective-permute-start(bf16[512,1536]{1,0:T(8,128)(2,1)} %get-tuple-element.116), channel_id=1, source_target_pairs={{0,1},{1,2},{2,3},{4,5},{5,6},{6,7},{8,9},{9,10},{10,11},{12,13},{... | collective-permute-start | bytes 4718600 | tf_op jit(solution)/shard_map/ppermute | solution.py:82
  1050.1 20.7 %convolution_convert_fusion.3 = bf16[10,1536,512]{2,1,0:T(8,128)(2,1)} fusion(bf16[10,640,1536]{2,1,0:T(8,128)(2,1)} %bitcast.254, bf16[10,640,512]{1,2,0:T(8,128)(2,1)} %get-tuple-element.107), kind=kOutput, calls=%fused_computation.18 | convolution fusion | flops 10074193920 | bytes 41943040 | tf_op jit(solution)/shard_map/erd,erf->edf/dot_general | solution.py:29
  1083.9 7.5 copy.170
  1091.4 7.1 fusion.52
  1110.2 17.1 %all-to-all-done.1.dout_ref = bf16[4,384,512]{2,1,0:T(8,128)(2,1)} async-done(((bf16[4,384,512]{2,1,0:T(8,128)(2,1)}), bf16[4,384,512]{2,1,0:T(8,128)(2,1)}, u32[]{:S(2)}, u32[]{:S(2)}) %all-to-all-start.1) | async-done | bytes 1572896 | tf_op jit(solution)/shard_map/all_to_all | solution.py:397
  1130.4 56.5 %attention_backward.1 = (bf16[2,3,64,2048]{3,2,1,0:T(8,128)(2,1)S(1)}, bf16[2,64,2048]{2,1,0:T(8,128)(2,1)S(1)}, bf16[2,64,2048]{2,1,0:T(8,128)(2,1)S(1)}) custom-call(s32[1,2048]{1,0:T(1,128)S(1)} %bitcast.244, bf16[2,3,64,2048]{3,2,1,0:T(8,128)(2,1)S(1)} %copy.136.q_ref, bf16[2,2048,64]{2,1,0:T(8,128)(2,1)S(1)} %copy.137.k_ref, ...), custom_call_target="tpu_custom_call" | custom-call | tf_op jit(solution)/shard_map/attention_backward/pallas_call | solution.py:219
  1190.9 7.3 convolution_convert_fusion.5
  1205.2 10.2 fusion.54
  1215.4 10.9 gather_fusion.1
  1232.3 44.3 %collective-permute-done.42 = bf16[512,1536]{1,0:T(8,128)(2,1)S(1)} collective-permute-done((bf16[512,1536]{1,0:T(8,128)(2,1)S(1)}, bf16[512,1536]{1,0:T(8,128)(2,1)S(1)}, u32[]{:S(2)}, u32[]{:S(2)}) %collective-permute-start.42) | collective-permute-done | bytes 1572896 | tf_op jit(solution)/shard_map/ppermute | solution.py:82
  1284.9 43.8 %collective-permute-done.43 = bf16[512,1536]{1,0:T(8,128)(2,1)S(1)} collective-permute-done((bf16[512,1536]{1,0:T(8,128)(2,1)S(1)}, bf16[512,1536]{1,0:T(8,128)(2,1)S(1)}, u32[]{:S(2)}, u32[]{:S(2)}) %collective-permute-start.43) | collective-permute-done | bytes 1572896 | tf_op jit(solution)/shard_map/ppermute | solution.py:82
  1339.6 32.2 %all_gather.27 = bf16[192,2560]{1,0:T(8,128)(2,1)S(1)} all-gather(bf16[192,640]{1,0:T(8,128)(2,1)} %reduce-scatter.8.cloned.1.call-done), channel_id=1, replica_groups=mesh['fsdp'=8,'seq'=4] {'seq'}, dimensions={1}, use_global_device_ids=true | all-gather | bytes 1228800 | tf_op jit(solution)/shard_map/all_gather | solution.py:432
  1384.2 38.6 %psum.22 = f32[]{:T(128)} all-reduce(f32[]{:T(128)} %get-tuple-element.34), channel_id=1, replica_groups=mesh['fsdp'=8,'seq'=4] {'fsdp','seq'}, use_global_device_ids=true, to_apply=%region_17.18 | all-reduce | flops 1 | bytes 8 | tf_op jit(solution)/shard_map/psum | solution.py:435
  1433.0 103.4 %reduce-scatter.12.cloned.1.call-done = bf16[10,192,512]{2,1,0:T(8,128)(2,1)} async-done(((bf16[10,1536,512]{2,1,0:T(8,128)(2,1)}), bf16[10,192,512]{2,1,0:T(8,128)(2,1)}) %reduce-scatter.12.cloned.1.call-update) | async-done | bytes 1966096 | tf_op jit(solution)/shard_map/reduce_scatter | solution.py:389
  1540.4 109.1 %reduce-scatter.10.cloned.1.call-done = bf16[10,192,512]{2,1,0:T(8,128)(2,1)} async-done(((bf16[10,1536,512]{2,1,0:T(8,128)(2,1)}), bf16[10,192,512]{2,1,0:T(8,128)(2,1)}) %reduce-scatter.10.cloned.1.call-update) | async-done | bytes 1966096 | tf_op jit(solution)/shard_map/reduce_scatter | solution.py:389
  (335 shorter events, 299.8 us)
Async XLA Ops:
  7.2 206.8 %all-gather.7.cloned.1.call-start = ((), (), s32[]{:S(2)}) async-start(), calls=%async_computation.7 | async-start | bytes 2211840 | tf_op jit(solution)/shard_map/all_gather | solution.py:284
  9.1 299.3 %all-gather.9.cloned.1.call-start = ((), (), s32[]{:S(2)}) async-start(), calls=%async_computation.8 | async-start | bytes 5308416 | tf_op jit(solution)/shard_map/all_gather | solution.py:285
  9.8 468.0 %all-gather.11.cloned.1.call-start = ((), (), s32[]{:S(2)}) async-start(), calls=%async_computation.9 | async-start | bytes 17694720 | tf_op jit(solution)/shard_map/all_gather | solution.py:286
  10.6 489.7 %all-gather.13.cloned.1.call-start = ((), (), s32[]{:S(2)}) async-start(), calls=%async_computation.10 | async-start | bytes 17694720 | tf_op jit(solution)/shard_map/all_gather | solution.py:287
  11.2 517.1 %all-gather.15.cloned.1.call-start = ((), (), s32[]{:S(2)}) async-start(), calls=%async_computation.11 | async-start | bytes 17694720 | tf_op jit(solution)/shard_map/all_gather | solution.py:288
  11.2 38.6 %collective-permute-start = (bf16[512,1536]{1,0:T(8,128)(2,1)S(1)}, bf16[512,1536]{1,0:T(8,128)(2,1)S(1)}, u32[]{:S(2)}, u32[]{:S(2)}) collective-permute-start(bf16[512,1536]{1,0:T(8,128)(2,1)S(1)} %bitcast.257), channel_id=1, source_target_pairs={{0,1},{1,2},{2,3},{4,5},{5,6},{6,7},{8,9},{9,10},{10,11},{12,13},{... | collective-permute-start | bytes 4718600 | tf_op jit(solution)/shard_map/ppermute | solution.py:69
  16.2 37.9 %collective-permute-start.1 = (bf16[512,1536]{1,0:T(8,128)(2,1)S(1)}, bf16[512,1536]{1,0:T(8,128)(2,1)}, u32[]{:S(2)}, u32[]{:S(2)}) collective-permute-start(bf16[512,1536]{1,0:T(8,128)(2,1)S(1)} %bitcast.258), channel_id=1, source_target_pairs={{1,0},{2,1},{3,2},{5,4},{6,5},{7,6},{9,8},{10,9},{11,10},{13,12},{... | collective-permute-start | bytes 4718600 | tf_op jit(solution)/shard_map/ppermute | solution.py:70
  54.1 106.2 %collective-permute-start.2 = (bf16[512,1536]{1,0:T(8,128)(2,1)}, bf16[512,1536]{1,0:T(8,128)(2,1)}, u32[]{:S(2)}, u32[]{:S(2)}) collective-permute-start(bf16[512,1536]{1,0:T(8,128)(2,1)} %collective-permute-done.1), channel_id=1, source_target_pairs={{1,0},{2,1},{5,4},{6,5},{9,8},{10,9},{13,12},{14,13},{17,16},{18,1... | collective-permute-start | bytes 4718600 | tf_op jit(solution)/shard_map/ppermute | solution.py:70
  55.4 1142.9 %reduce-scatter.16.cloned.1.call-start = ((), (), s32[]{:S(2)}) async-start(), calls=%async_computation.17 | async-start | bytes 5750784
  56.2 109.9 %collective-permute-start.5 = (bf16[512,1536]{1,0:T(8,128)(2,1)}, bf16[512,1536]{1,0:T(8,128)(2,1)}, u32[]{:S(2)}, u32[]{:S(2)}) collective-permute-start(bf16[512,1536]{1,0:T(8,128)(2,1)} %collective-permute-done.4), channel_id=1, source_target_pairs={{2,3},{6,7},{10,11},{14,15},{18,19},{22,23},{26,27},{30,31}} | collective-permute-start | bytes 4718600 | tf_op jit(solution)/shard_map/ppermute | solution.py:69
  160.8 38.7 %collective-permute-start.3 = (bf16[512,1536]{1,0:T(8,128)(2,1)}, bf16[512,1536]{1,0:T(8,128)(2,1)S(1)}, u32[]{:S(2)}, u32[]{:S(2)}) collective-permute-start(bf16[512,1536]{1,0:T(8,128)(2,1)} %collective-permute-done.2), channel_id=1, source_target_pairs={{1,0},{5,4},{9,8},{13,12},{17,16},{21,20},{25,24},{29,28}} | collective-permute-start | bytes 4718600 | tf_op jit(solution)/shard_map/ppermute | solution.py:70
  316.8 34.7 %collective-permute-start.12 = (bf16[512,1536]{1,0:T(8,128)(2,1)S(1)}, bf16[512,1536]{1,0:T(8,128)(2,1)}, u32[]{:S(2)}, u32[]{:S(2)}) collective-permute-start(bf16[512,1536]{1,0:T(8,128)(2,1)S(1)} %multiply_convert_fusion.3), channel_id=1, source_target_pairs={{0,1},{1,2},{2,3},{4,5},{5,6},{6,7},{8,9},{9,10},{10,11},{12,13},{... | collective-permute-start | bytes 4718600 | tf_op jit(solution)/shard_map/ppermute | solution.py:69
  320.2 36.8 %collective-permute-start.13 = (bf16[512,1536]{1,0:T(8,128)(2,1)S(1)}, bf16[512,1536]{1,0:T(8,128)(2,1)}, u32[]{:S(2)}, u32[]{:S(2)}) collective-permute-start(bf16[512,1536]{1,0:T(8,128)(2,1)S(1)} %multiply_convert_fusion.3), channel_id=1, source_target_pairs={{1,0},{2,1},{3,2},{5,4},{6,5},{7,6},{9,8},{10,9},{11,10},{13,12},{... | collective-permute-start | bytes 4718600 | tf_op jit(solution)/shard_map/ppermute | solution.py:70
  351.4 53.0 %collective-permute-start.16 = (bf16[512,1536]{1,0:T(8,128)(2,1)}, bf16[512,1536]{1,0:T(8,128)(2,1)}, u32[]{:S(2)}, u32[]{:S(2)}) collective-permute-start(bf16[512,1536]{1,0:T(8,128)(2,1)} %collective-permute-done.12), channel_id=1, source_target_pairs={{1,2},{2,3},{5,6},{6,7},{9,10},{10,11},{13,14},{14,15},{17,18},{18... | collective-permute-start | bytes 4718600 | tf_op jit(solution)/shard_map/ppermute | solution.py:69
  356.9 49.0 %collective-permute-start.14 = (bf16[512,1536]{1,0:T(8,128)(2,1)}, bf16[512,1536]{1,0:T(8,128)(2,1)}, u32[]{:S(2)}, u32[]{:S(2)}) collective-permute-start(bf16[512,1536]{1,0:T(8,128)(2,1)} %collective-permute-done.13), channel_id=1, source_target_pairs={{1,0},{2,1},{5,4},{6,5},{9,8},{10,9},{13,12},{14,13},{17,16},{18,1... | collective-permute-start | bytes 4718600 | tf_op jit(solution)/shard_map/ppermute | solution.py:70
  362.8 30.4 %collective-permute-start.7 = (s32[8,512]{1,0:T(8,128)S(1)}, s32[8,512]{1,0:T(8,128)S(1)}, u32[]{:S(2)}, u32[]{:S(2)}) collective-permute-start(s32[8,512]{1,0:T(8,128)S(1)} %bitcast.273), channel_id=1, source_target_pairs={{1,0},{2,1},{3,2},{5,4},{6,5},{7,6},{9,8},{10,9},{11,10},{13,12},{... | collective-permute-start | bytes 49160 | tf_op jit(solution)/shard_map/ppermute | solution.py:70
  364.2 30.3 %collective-permute-start.10 = (s32[8,512]{1,0:T(8,128)S(1)}, s32[8,512]{1,0:T(8,128)S(1)}, u32[]{:S(2)}, u32[]{:S(2)}) collective-permute-start(s32[8,512]{1,0:T(8,128)S(1)} %collective-permute-done.6), channel_id=1, source_target_pairs={{1,2},{2,3},{5,6},{6,7},{9,10},{10,11},{13,14},{14,15},{17,18},{18... | collective-permute-start | bytes 49160 | tf_op jit(solution)/shard_map/ppermute | solution.py:69
  405.9 32.9 %collective-permute-start.15 = (bf16[512,1536]{1,0:T(8,128)(2,1)}, bf16[512,1536]{1,0:T(8,128)(2,1)S(1)}, u32[]{:S(2)}, u32[]{:S(2)}) collective-permute-start(bf16[512,1536]{1,0:T(8,128)(2,1)} %collective-permute-done.14), channel_id=1, source_target_pairs={{1,0},{5,4},{9,8},{13,12},{17,16},{21,20},{25,24},{29,28}} | collective-permute-start | bytes 4718600 | tf_op jit(solution)/shard_map/ppermute | solution.py:70
  571.5 30.6 %collective-permute-start.18 = (bf16[512,1536]{1,0:T(8,128)(2,1)S(1)}, bf16[512,1536]{1,0:T(8,128)(2,1)S(1)}, u32[]{:S(2)}, u32[]{:S(2)}) collective-permute-start(bf16[512,1536]{1,0:T(8,128)(2,1)S(1)} %get-tuple-element.126), channel_id=1, source_target_pairs={{0,1},{4,5},{8,9},{12,13},{16,17},{20,21},{24,25},{28,29}} | collective-permute-start | bytes 4718600 | tf_op jit(solution)/shard_map/ppermute | solution.py:82
  574.8 27.3 %collective-permute-start.21 = (bf16[512,1536]{1,0:T(8,128)(2,1)S(1)}, bf16[512,1536]{1,0:T(8,128)(2,1)S(1)}, u32[]{:S(2)}, u32[]{:S(2)}) collective-permute-start(bf16[512,1536]{1,0:T(8,128)(2,1)S(1)} %get-tuple-element.127), channel_id=1, source_target_pairs={{3,2},{7,6},{11,10},{15,14},{19,18},{23,22},{27,26},{31,30}} | collective-permute-start | bytes 4718600 | tf_op jit(solution)/shard_map/ppermute | solution.py:83
  604.9 30.9 %collective-permute-start.19 = (bf16[512,1536]{1,0:T(8,128)(2,1)S(1)}, bf16[512,1536]{1,0:T(8,128)(2,1)S(1)}, u32[]{:S(2)}, u32[]{:S(2)}) collective-permute-start(bf16[512,1536]{1,0:T(8,128)(2,1)S(1)} %get-tuple-element.124), channel_id=1, source_target_pairs={{0,1},{1,2},{4,5},{5,6},{8,9},{9,10},{12,13},{13,14},{16,17},{17,1... | collective-permute-start | bytes 4718600 | tf_op jit(solution)/shard_map/ppermute | solution.py:82
  609.4 26.4 %collective-permute-start.22 = (bf16[512,1536]{1,0:T(8,128)(2,1)S(1)}, bf16[512,1536]{1,0:T(8,128)(2,1)S(1)}, u32[]{:S(2)}, u32[]{:S(2)}) collective-permute-start(bf16[512,1536]{1,0:T(8,128)(2,1)S(1)} %get-tuple-element.125), channel_id=1, source_target_pairs={{2,1},{3,2},{6,5},{7,6},{10,9},{11,10},{14,13},{15,14},{18,17},{19... | collective-permute-start | bytes 4718600 | tf_op jit(solution)/shard_map/ppermute | solution.py:83
  638.6 35.9 %collective-permute-start.20 = (bf16[512,1536]{1,0:T(8,128)(2,1)}, bf16[512,1536]{1,0:T(8,128)(2,1)}, u32[]{:S(2)}, u32[]{:S(2)}) collective-permute-start(bf16[512,1536]{1,0:T(8,128)(2,1)} %get-tuple-element.122), channel_id=1, source_target_pairs={{0,1},{1,2},{2,3},{4,5},{5,6},{6,7},{8,9},{9,10},{10,11},{12,13},{... | collective-permute-start | bytes 4718600 | tf_op jit(solution)/shard_map/ppermute | solution.py:82
  649.2 30.5 %collective-permute-start.23 = (bf16[512,1536]{1,0:T(8,128)(2,1)}, bf16[512,1536]{1,0:T(8,128)(2,1)}, u32[]{:S(2)}, u32[]{:S(2)}) collective-permute-start(bf16[512,1536]{1,0:T(8,128)(2,1)} %get-tuple-element.123), channel_id=1, source_target_pairs={{1,0},{2,1},{3,2},{5,4},{6,5},{7,6},{9,8},{10,9},{11,10},{13,12},{... | collective-permute-start | bytes 4718600 | tf_op jit(solution)/shard_map/ppermute | solution.py:83
  686.6 34.6 %collective-permute-start.25 = (bf16[512,1536]{1,0:T(8,128)(2,1)S(1)}, bf16[512,1536]{1,0:T(8,128)(2,1)S(1)}, u32[]{:S(2)}, u32[]{:S(2)}) collective-permute-start(bf16[512,1536]{1,0:T(8,128)(2,1)S(1)} %get-tuple-element.104), channel_id=1, source_target_pairs={{1,0},{2,1},{3,2},{5,4},{6,5},{7,6},{9,8},{10,9},{11,10},{13,12},{... | collective-permute-start | bytes 4718600 | tf_op jit(solution)/shard_map/ppermute | solution.py:70
  687.9 34.6 %collective-permute-start.24 = (bf16[512,1536]{1,0:T(8,128)(2,1)S(1)}, bf16[512,1536]{1,0:T(8,128)(2,1)}, u32[]{:S(2)}, u32[]{:S(2)}) collective-permute-start(bf16[512,1536]{1,0:T(8,128)(2,1)S(1)} %get-tuple-element.104), channel_id=1, source_target_pairs={{0,1},{1,2},{2,3},{4,5},{5,6},{6,7},{8,9},{9,10},{10,11},{12,13},{... | collective-permute-start | bytes 4718600 | tf_op jit(solution)/shard_map/ppermute | solution.py:69
  721.1 34.4 %collective-permute-start.26 = (bf16[512,1536]{1,0:T(8,128)(2,1)S(1)}, bf16[512,1536]{1,0:T(8,128)(2,1)}, u32[]{:S(2)}, u32[]{:S(2)}) collective-permute-start(bf16[512,1536]{1,0:T(8,128)(2,1)S(1)} %collective-permute-done.25), channel_id=1, source_target_pairs={{1,0},{2,1},{5,4},{6,5},{9,8},{10,9},{13,12},{14,13},{17,16},{18,1... | collective-permute-start | bytes 4718600 | tf_op jit(solution)/shard_map/ppermute | solution.py:70
  722.4 68.5 %collective-permute-start.28 = (bf16[512,1536]{1,0:T(8,128)(2,1)}, bf16[512,1536]{1,0:T(8,128)(2,1)}, u32[]{:S(2)}, u32[]{:S(2)}) collective-permute-start(bf16[512,1536]{1,0:T(8,128)(2,1)} %collective-permute-done.24), channel_id=1, source_target_pairs={{1,2},{2,3},{5,6},{6,7},{9,10},{10,11},{13,14},{14,15},{17,18},{18... | collective-permute-start | bytes 4718600 | tf_op jit(solution)/shard_map/ppermute | solution.py:69
  755.5 40.5 %collective-permute-start.27 = (bf16[512,1536]{1,0:T(8,128)(2,1)}, bf16[512,1536]{1,0:T(8,128)(2,1)}, u32[]{:S(2)}, u32[]{:S(2)}) collective-permute-start(bf16[512,1536]{1,0:T(8,128)(2,1)} %collective-permute-done.26), channel_id=1, source_target_pairs={{1,0},{5,4},{9,8},{13,12},{17,16},{21,20},{25,24},{29,28}} | collective-permute-start | bytes 4718600 | tf_op jit(solution)/shard_map/ppermute | solution.py:70
  763.1 21.6 %collective-permute-start.30 = (f32[512]{0:T(512)S(1)}, f32[512]{0:T(512)S(1)}, u32[]{:S(2)}, u32[]{:S(2)}) collective-permute-start(f32[512]{0:T(512)S(1)} %get-tuple-element.96), channel_id=1, source_target_pairs={{0,1},{1,2},{2,3},{4,5},{5,6},{6,7},{8,9},{9,10},{10,11},{12,13},{... | collective-permute-start | bytes 6152 | tf_op jit(solution)/shard_map/ppermute | solution.py:69
  958.7 27.2 %collective-permute-start.36 = (bf16[512,1536]{1,0:T(8,128)(2,1)}, bf16[512,1536]{1,0:T(8,128)(2,1)}, u32[]{:S(2)}, u32[]{:S(2)}) collective-permute-start(bf16[512,1536]{1,0:T(8,128)(2,1)} %get-tuple-element.120), channel_id=1, source_target_pairs={{0,1},{4,5},{8,9},{12,13},{16,17},{20,21},{24,25},{28,29}} | collective-permute-start | bytes 4718600 | tf_op jit(solution)/shard_map/ppermute | solution.py:82
  962.1 23.7 %collective-permute-start.39 = (bf16[512,1536]{1,0:T(8,128)(2,1)}, bf16[512,1536]{1,0:T(8,128)(2,1)}, u32[]{:S(2)}, u32[]{:S(2)}) collective-permute-start(bf16[512,1536]{1,0:T(8,128)(2,1)} %get-tuple-element.121), channel_id=1, source_target_pairs={{3,2},{7,6},{11,10},{15,14},{19,18},{23,22},{27,26},{31,30}} | collective-permute-start | bytes 4718600 | tf_op jit(solution)/shard_map/ppermute | solution.py:83
  991.0 27.7 %collective-permute-start.37 = (bf16[512,1536]{1,0:T(8,128)(2,1)}, bf16[512,1536]{1,0:T(8,128)(2,1)}, u32[]{:S(2)}, u32[]{:S(2)}) collective-permute-start(bf16[512,1536]{1,0:T(8,128)(2,1)} %get-tuple-element.118), channel_id=1, source_target_pairs={{0,1},{1,2},{4,5},{5,6},{8,9},{9,10},{12,13},{13,14},{16,17},{17,1... | collective-permute-start | bytes 4718600 | tf_op jit(solution)/shard_map/ppermute | solution.py:82
  996.6 22.2 %collective-permute-start.40 = (bf16[512,1536]{1,0:T(8,128)(2,1)}, bf16[512,1536]{1,0:T(8,128)(2,1)}, u32[]{:S(2)}, u32[]{:S(2)}) collective-permute-start(bf16[512,1536]{1,0:T(8,128)(2,1)} %get-tuple-element.119), channel_id=1, source_target_pairs={{2,1},{3,2},{6,5},{7,6},{10,9},{11,10},{14,13},{15,14},{18,17},{19... | collective-permute-start | bytes 4718600 | tf_op jit(solution)/shard_map/ppermute | solution.py:83
  1025.2 45.7 %collective-permute-start.38 = (bf16[512,1536]{1,0:T(8,128)(2,1)}, bf16[512,1536]{1,0:T(8,128)(2,1)}, u32[]{:S(2)}, u32[]{:S(2)}) collective-permute-start(bf16[512,1536]{1,0:T(8,128)(2,1)} %get-tuple-element.116), channel_id=1, source_target_pairs={{0,1},{1,2},{2,3},{4,5},{5,6},{6,7},{8,9},{9,10},{10,11},{12,13},{... | collective-permute-start | bytes 4718600 | tf_op jit(solution)/shard_map/ppermute | solution.py:82
  1048.8 22.6 %collective-permute-start.41 = (bf16[512,1536]{1,0:T(8,128)(2,1)}, bf16[512,1536]{1,0:T(8,128)(2,1)}, u32[]{:S(2)}, u32[]{:S(2)}) collective-permute-start(bf16[512,1536]{1,0:T(8,128)(2,1)} %get-tuple-element.117), channel_id=1, source_target_pairs={{1,0},{2,1},{3,2},{5,4},{6,5},{7,6},{9,8},{10,9},{11,10},{13,12},{... | collective-permute-start | bytes 4718600 | tf_op jit(solution)/shard_map/ppermute | solution.py:83
  1101.3 26.0 %all-to-all-start.1 = ((bf16[4,384,512]{2,1,0:T(8,128)(2,1)}), bf16[4,384,512]{2,1,0:T(8,128)(2,1)}, u32[]{:S(2)}, u32[]{:S(2)}) async-start(bf16[4,384,512]{2,1,0:T(8,128)(2,1)} %bitcast.261), calls=%async_computation.1 | async-start | bytes 3145728 | tf_op jit(solution)/shard_map/all_to_all | solution.py:397
  1105.7 234.0 %reduce-scatter.8.cloned.1.call-start = ((), (), s32[]{:S(2)}) async-start(), calls=%async_computation.12 | async-start | bytes 2211840 | tf_op jit(solution)/shard_map/reduce_scatter | solution.py:416
  1198.2 225.3 %all-reduce.2.cloned.1.call-start = ((), (), s32[]{:S(2)}) async-start(), calls=%async_computation.13 | async-start | bytes 1622016 | tf_op jit(solution)/shard_map/psum | solution.py:428
  1200.6 228.3 %reduce-scatter.14.cloned.1.call-start = ((), (), s32[]{:S(2)}) async-start(), calls=%async_computation.16 | async-start | bytes 17694720 | tf_op jit(solution)/shard_map/reduce_scatter | solution.py:389
  1201.3 335.0 %reduce-scatter.12.cloned.1.call-start = ((), (), s32[]{:S(2)}) async-start(), calls=%async_computation.15 | async-start | bytes 17694720 | tf_op jit(solution)/shard_map/reduce_scatter | solution.py:389
  1201.9 447.6 %reduce-scatter.10.cloned.1.call-start = ((), (), s32[]{:S(2)}) async-start(), calls=%async_computation.14 | async-start | bytes 17694720 | tf_op jit(solution)/shard_map/reduce_scatter | solution.py:389
  1229.7 46.9 %collective-permute-start.42 = (bf16[512,1536]{1,0:T(8,128)(2,1)S(1)}, bf16[512,1536]{1,0:T(8,128)(2,1)S(1)}, u32[]{:S(2)}, u32[]{:S(2)}) collective-permute-start(bf16[512,1536]{1,0:T(8,128)(2,1)S(1)} %get-tuple-element.114), channel_id=1, source_target_pairs={{0,1},{4,5},{8,9},{12,13},{16,17},{20,21},{24,25},{28,29}} | collective-permute-start | bytes 4718600 | tf_op jit(solution)/shard_map/ppermute | solution.py:82
  1231.4 45.2 %collective-permute-start.45 = (bf16[512,1536]{1,0:T(8,128)(2,1)S(1)}, bf16[512,1536]{1,0:T(8,128)(2,1)S(1)}, u32[]{:S(2)}, u32[]{:S(2)}) collective-permute-start(bf16[512,1536]{1,0:T(8,128)(2,1)S(1)} %get-tuple-element.115), channel_id=1, source_target_pairs={{3,2},{7,6},{11,10},{15,14},{19,18},{23,22},{27,26},{31,30}} | collective-permute-start | bytes 4718600 | tf_op jit(solution)/shard_map/ppermute | solution.py:83
  1279.4 49.3 %collective-permute-start.43 = (bf16[512,1536]{1,0:T(8,128)(2,1)S(1)}, bf16[512,1536]{1,0:T(8,128)(2,1)S(1)}, u32[]{:S(2)}, u32[]{:S(2)}) collective-permute-start(bf16[512,1536]{1,0:T(8,128)(2,1)S(1)} %get-tuple-element.112), channel_id=1, source_target_pairs={{0,1},{1,2},{4,5},{5,6},{8,9},{9,10},{12,13},{13,14},{16,17},{17,1... | collective-permute-start | bytes 4718600 | tf_op jit(solution)/shard_map/ppermute | solution.py:82
  1283.9 44.8 %collective-permute-start.46 = (bf16[512,1536]{1,0:T(8,128)(2,1)S(1)}, bf16[512,1536]{1,0:T(8,128)(2,1)S(1)}, u32[]{:S(2)}, u32[]{:S(2)}) collective-permute-start(bf16[512,1536]{1,0:T(8,128)(2,1)S(1)} %get-tuple-element.113), channel_id=1, source_target_pairs={{2,1},{3,2},{6,5},{7,6},{10,9},{11,10},{14,13},{15,14},{18,17},{19... | collective-permute-start | bytes 4718600 | tf_op jit(solution)/shard_map/ppermute | solution.py:83
  1331.8 43.3 %collective-permute-start.44 = (bf16[512,1536]{1,0:T(8,128)(2,1)}, bf16[512,1536]{1,0:T(8,128)(2,1)S(1)}, u32[]{:S(2)}, u32[]{:S(2)}) collective-permute-start(bf16[512,1536]{1,0:T(8,128)(2,1)} %get-tuple-element.110), channel_id=1, source_target_pairs={{0,1},{1,2},{2,3},{4,5},{5,6},{6,7},{8,9},{9,10},{10,11},{12,13},{... | collective-permute-start | bytes 4718600 | tf_op jit(solution)/shard_map/ppermute | solution.py:82
  1337.7 37.5 %collective-permute-start.47 = (bf16[512,1536]{1,0:T(8,128)(2,1)}, bf16[512,1536]{1,0:T(8,128)(2,1)}, u32[]{:S(2)}, u32[]{:S(2)}) collective-permute-start(bf16[512,1536]{1,0:T(8,128)(2,1)} %get-tuple-element.111), channel_id=1, source_target_pairs={{1,0},{2,1},{3,2},{5,4},{6,5},{7,6},{9,8},{10,9},{11,10},{13,12},{... | collective-permute-start | bytes 4718600 | tf_op jit(solution)/shard_map/ppermute | solution.py:83
  (70 other events, 2035.8 us)
Sparse Core Ops, SparseCore 0:
  10.5 30.0 all-gather.6
  42.4 38.9 all-gather.8
  83.3 87.6 all-gather.10
  172.7 85.4 all-gather.12
  260.0 85.4 all-gather.14
  1091.5 55.9 reduce-scatter.15
  1198.3 39.8 reduce-scatter.7
  1241.3 65.1 all-reduce.1
  1310.4 112.7 reduce-scatter.13
  1427.0 109.3 reduce-scatter.11
  1540.3 109.1 reduce-scatter.9

commit v3 on v2

--- a/solution.py
+++ b/solution.py
@@ -55,10 +55,6 @@
     block_ends = jnp.cumsum(lengths_row)
     open_ends = jnp.where(block_ends[None, :] > positions[:, None], block_ends[None, :], positions.shape[0])
     return jnp.min(open_ends, axis=1).astype(jnp.int32)
-
-
-def swiglu(gate_act, up_act):
-    return jax.nn.silu(gate_act) * up_act
 
 
 def line_gather(block):
@@ -87,7 +83,49 @@
 def by_place(blocks):
     n = lax.axis_size("seq")
     me = lax.axis_index("seq")
-    return jnp.stack(blocks)[(me - jnp.arange(n)) % n]
+    placed = jnp.zeros((n,) + blocks[0].shape, blocks[0].dtype)
+    for k, block in enumerate(blocks):
+        placed = lax.dynamic_update_index_in_dim(placed, block, (me - k) % n, 0)
+    return placed
+
+
+def from_place(placed):
+    n = lax.axis_size("seq")
+    me = lax.axis_index("seq")
+    return [lax.dynamic_index_in_dim(placed, (me - k) % n, 0, keepdims=False) for k in range(n)]
+
+
+def swap(value, axis, bit):
+    return lax.ppermute(value, axis, [(i, i ^ bit) for i in range(lax.axis_size(axis))])
+
+
+def total(value, *axes):
+    for axis in axes:
+        for step in range(lax.axis_size(axis).bit_length() - 1):
+            value = value + swap(value, axis, 1 << step)
+    return value
+
+
+def halving_bits():
+    bits = [1 << step for step in range(lax.axis_size("fsdp").bit_length() - 1)]
+    return tuple(bits), tuple(bits[:1] + bits[:0:-1])
+
+
+def halving_sum(keep, send, bits):
+    for bit in bits:
+        here = swap(send, "fsdp", bit)
+        half = keep.shape[0] // 2
+        if half == 0:
+            return keep[0].astype(full) + here[0].astype(full)
+        send = (keep[half:].astype(full) + here[half:].astype(full)).astype(low)
+        keep = (keep[:half].astype(full) + here[:half].astype(full)).astype(low)
+
+
+def rows_sum(part, bits):
+    devs = lax.axis_size("fsdp")
+    order = lax.axis_index("fsdp") ^ jnp.array(halving_masks(bits), jnp.int32)
+    blocks = part.reshape(devs, part.shape[0] // devs, part.shape[1])[order]
+    return halving_sum(blocks[: devs // 2], blocks[devs // 2 :], bits)
 
 
 def nt(a, b):
@@ -95,6 +133,10 @@
 
 def nn(a, b):
     return lax.dot_general(a, b, (((1,), (0,)), ((), ())), preferred_element_type=full)
+
+def tn(a, b):
+    return lax.dot_general(a, b, (((0,), (0,)), ((), ())), preferred_element_type=full)
+
 
 def beside(ref):
     return jnp.concatenate([ref[0, h] for h in range(GROUP)], axis=1)
@@ -164,7 +206,7 @@
             jax.ShapeDtypeStruct((kv_here, GROUP, HEAD_DIM, seq_len), full),
             jax.ShapeDtypeStruct((kv_here, GROUP, 1, seq_len), full),
         ],
-        compiler_params=pltpu.CompilerParams(vmem_limit_bytes=40 * 2**20),
+        compiler_params=vmem(40),
         name="attention_forward",
     )(limit, qt, k_rows, vt)
 
@@ -240,9 +282,205 @@
             jax.ShapeDtypeStruct((kv_here, HEAD_DIM, seq_len), low),
         ],
         scratch_shapes=[pltpu.VMEM((HEAD_DIM, seq_len), full), pltpu.VMEM((HEAD_DIM, seq_len), full)],
-        compiler_params=pltpu.CompilerParams(vmem_limit_bytes=40 * 2**20),
+        compiler_params=vmem(40),
         name="attention_backward",
     )(limit, qt, k_rows, v_rows, kt, out, lse, d_out)
+
+
+def vmem(mib):
+    return pltpu.CompilerParams(vmem_limit_bytes=mib * 2**20)
+
+
+def pick_kernel(slots, slot_ref, tok_ref, out_ref, pick_ref):
+    experts, width = out_ref.shape[0], out_ref.shape[3]
+    place = lax.broadcasted_iota(jnp.int32, (slots, 1), 0)
+    for e in range(experts):
+        pick_ref[e * slots : (e + 1) * slots, :] = (place == slot_ref[0, e : e + 1, :]).astype(low)
+    for col in range(0, width, 256):
+        rows = nn(pick_ref[...], tok_ref[0, :, col : col + 256]).astype(low)
+        out_ref[:, 0, :, col : col + 256] = rows.reshape(experts, slots, 256)
+
+
+def pick_rows(slot_of, tokens, slots):
+    n, experts, shard_len = slot_of.shape
+    width = tokens.shape[2]
+    return pl.pallas_call(
+        functools.partial(pick_kernel, slots),
+        grid=(n,),
+        in_specs=[
+            pl.BlockSpec((1, experts, shard_len), lambda k: (k, 0, 0)),
+            pl.BlockSpec((1, shard_len, width), lambda k: (k, 0, 0)),
+        ],
+        out_specs=pl.BlockSpec((experts, 1, slots, width), lambda k: (0, k, 0, 0)),
+        out_shape=jax.ShapeDtypeStruct((experts, n, slots, width), low),
+        scratch_shapes=[pltpu.VMEM((experts * slots, shard_len), low)],
+        compiler_params=vmem(48),
+        name="pick_rows",
+    )(slot_of, tokens)
+
+
+def put_kernel(slots, slot_ref, gate_ref, rows_ref, out_ref, pick_ref):
+    experts, width = rows_ref.shape[0], rows_ref.shape[3]
+    place = lax.broadcasted_iota(jnp.int32, (slots, 1), 0)
+    for e in range(experts):
+        put = jnp.where(place == slot_ref[0, e : e + 1, :], gate_ref[0, e : e + 1, :], 0.0)
+        pick_ref[e * slots : (e + 1) * slots, :] = put.astype(low)
+    for col in range(0, width, 256):
+        rows = rows_ref[:, 0, :, col : col + 256].reshape(experts * slots, 256)
+        out_ref[0, :, col : col + 256] = tn(pick_ref[...], rows).astype(low)
+
+
+def put_rows(slot_of, gates, rows):
+    n, experts, shard_len = slot_of.shape
+    _, _, slots, width = rows.shape
+    return pl.pallas_call(
+        functools.partial(put_kernel, slots),
+        grid=(n,),
+        in_specs=[
+            pl.BlockSpec((1, experts, shard_len), lambda k: (k, 0, 0)),
+            pl.BlockSpec((1, experts, shard_len), lambda k: (k, 0, 0)),
+            pl.BlockSpec((experts, 1, slots, width), lambda k: (0, k, 0, 0)),
+        ],
+        out_specs=pl.BlockSpec((1, shard_len, width), lambda k: (k, 0, 0)),
+        out_shape=jax.ShapeDtypeStruct((n, shard_len, width), low),
+        scratch_shapes=[pltpu.VMEM((experts * slots, shard_len), low)],
+        compiler_params=vmem(48),
+        name="put_rows",
+    )(slot_of, gates, rows)
+
+
+def experts_kernel(x_ref, wg_ref, wu_ref, wd_ref, g_ref, u_ref, y_ref):
+    g = nn(x_ref[0], wg_ref[0])
+    u = nn(x_ref[0], wu_ref[0])
+    g_ref[0] = g.astype(low)
+    u_ref[0] = u.astype(low)
+    act = (g * jax.nn.sigmoid(g) * u).astype(low)
+    y_ref[0] = nn(act, wd_ref[0]).astype(low)
+
+
+def one(*shape):
+    return pl.BlockSpec((1,) + shape, lambda e, *_: (e, 0, 0))
+
+
+def experts_forward(rows, w_gate, w_up, w_down):
+    experts, count, width = rows.shape
+    hidden = w_gate.shape[2]
+    return pl.pallas_call(
+        experts_kernel,
+        grid=(experts,),
+        in_specs=[one(count, width), one(width, hidden), one(width, hidden), one(hidden, width)],
+        out_specs=[one(count, hidden), one(count, hidden), one(count, width)],
+        out_shape=[
+            jax.ShapeDtypeStruct((experts, count, hidden), low),
+            jax.ShapeDtypeStruct((experts, count, hidden), low),
+            jax.ShapeDtypeStruct((experts, count, width), low),
+        ],
+        compiler_params=vmem(48),
+        name="experts_forward",
+    )(rows, w_gate, w_up, w_down)
+
+
+def experts_back_kernel(
+    d_ref, gate_ref, g_ref, u_ref, wg_ref, wu_ref, wd_ref, dx_ref, dgu_ref, act_ref, dot_ref
+):
+    hidden = g_ref.shape[2]
+    d_act = nt(d_ref[0], wd_ref[0])
+    g, u = g_ref[0].astype(full), u_ref[0].astype(full)
+    gate = gate_ref[0]
+    sig = jax.nn.sigmoid(g)
+    silu = g * sig
+    act = silu * u
+    dot_ref[0] = jnp.sum(d_act * act, axis=1, keepdims=True)
+    act_ref[0] = (act * gate).astype(low)
+    d_act = d_act * gate
+    d_g = (d_act * u * (sig + silu * (1.0 - sig))).astype(low)
+    d_u = (d_act * silu).astype(low)
+    dgu_ref[0, :, :hidden] = d_g
+    dgu_ref[0, :, hidden:] = d_u
+    dx_ref[0] = (nt(d_g, wg_ref[0]) + nt(d_u, wu_ref[0])).astype(low)
+
+
+def experts_backward(d_rows, row_gates, g, u, w_gate, w_up, w_down):
+    experts, count, width = d_rows.shape
+    hidden = w_gate.shape[2]
+    return pl.pallas_call(
+        experts_back_kernel,
+        grid=(experts,),
+        in_specs=[
+            one(count, width),
+            one(count, 1),
+            one(count, hidden),
+            one(count, hidden),
+            one(width, hidden),
+            one(width, hidden),
+            one(hidden, width),
+        ],
+        out_specs=[one(count, width), one(count, 2 * hidden), one(count, hidden), one(count, 1)],
+        out_shape=[
+            jax.ShapeDtypeStruct((experts, count, width), low),
+            jax.ShapeDtypeStruct((experts, count, 2 * hidden), low),
+            jax.ShapeDtypeStruct((experts, count, hidden), low),
+            jax.ShapeDtypeStruct((experts, count, 1), full),
+        ],
+        compiler_params=vmem(56),
+        name="experts_backward",
+    )(d_rows, row_gates, g, u, w_gate, w_up, w_down)
+
+
+def halving_masks(bits):
+    masks = [0]
+    for bit in reversed(bits):
+        masks = masks + [mask ^ bit for mask in masks]
+    return masks
+
+
+def weight_grads_kernel(
+    bits_a, bits_b, me_ref, x_ref, d_ref, dgu_ref, act_ref, *refs
+):
+    outs, (gu_acc, d_acc) = refs[:8], refs[8:]
+    hidden, width = act_ref.shape[2], x_ref.shape[2]
+    me = me_ref[0]
+    gu_acc[...] = tn(x_ref[0], dgu_ref[0])
+    d_acc[...] = tn(act_ref[0], d_ref[0])
+    parts = (
+        (gu_acc, slice(0, hidden), bits_a),
+        (gu_acc, slice(hidden, 2 * hidden), bits_b),
+        (d_acc, slice(0, width // 2), bits_a),
+        (d_acc, slice(width // 2, width), bits_b),
+    )
+    for part, (acc, cols, bits) in enumerate(parts):
+        keep, send = outs[2 * part], outs[2 * part + 1]
+        rows = keep.shape[2]
+        for place, mask in enumerate(halving_masks(bits)):
+            start = pl.multiple_of((me ^ mask) * rows, rows)
+            out = keep if place < keep.shape[0] else send
+            out[place % keep.shape[0], 0] = acc[pl.ds(start, rows), cols].astype(low)
+
+
+def weight_grads(me, rows, d_rows, d_gu, act, bits_a, bits_b):
+    experts, count, width = rows.shape
+    hidden = act.shape[2]
+    devs = 2 ** len(bits_a)
+    shapes = [(width // devs, hidden)] * 2 + [(hidden // devs, width // 2)] * 2
+    out_specs, out_shape = [], []
+    for shape in shapes:
+        for _ in range(2):
+            out_specs.append(pl.BlockSpec((devs // 2, 1) + shape, lambda e, *_: (0, e, 0, 0)))
+            out_shape.append(jax.ShapeDtypeStruct((devs // 2, experts) + shape, low))
+    outs = pl.pallas_call(
+        functools.partial(weight_grads_kernel, bits_a, bits_b),
+        grid_spec=pltpu.PrefetchScalarGridSpec(
+            num_scalar_prefetch=1,
+            grid=(experts,),
+            in_specs=[one(count, width), one(count, width), one(count, 2 * hidden), one(count, hidden)],
+            out_specs=out_specs,
+            scratch_shapes=[pltpu.VMEM((width, 2 * hidden), full), pltpu.VMEM((hidden, width), full)],
+        ),
+        out_shape=out_shape,
+        compiler_params=vmem(56),
+        name="weight_grads",
+    )(me, rows, d_rows, d_gu, act)
+    return [(outs[i], outs[i + 1]) for i in range(0, 8, 2)]
 
 
 def shards(
@@ -290,22 +528,19 @@
     full_g2 = small[:, 1].astype(full)
     full_router = small[:, 2:]
     valid_rows = valid_mask.reshape(shard_len).astype(full)
-    valid_count = lax.psum(jnp.sum(valid_rows), ("fsdp", "seq"))
-
-    routes_rel = jnp.stack(line_gather(routes.reshape(shard_len, top_count).T))
-    routes_rel = jnp.swapaxes(routes_rel, 1, 2)
+
+    routes_low = jnp.concatenate([routes.reshape(shard_len, top_count).T, valid_mask], axis=0)
+    routes_rel = jnp.stack(line_gather(routes_low))
+    valid_count = total(jnp.sum(routes_rel[:, top_count]).astype(full).reshape(1, 1), "fsdp")[0, 0]
     expert_ids = jnp.arange(expert_total, dtype=jnp.int32)
-    member = jnp.any(routes_rel[:, :, :, None] == expert_ids, axis=2)
-    own_member = lax.dynamic_slice_in_dim(member, me * experts_here, experts_here, 2)
-    own_member = jnp.transpose(own_member, (2, 0, 1)).astype(low)
+    member = jnp.any(routes_rel[:, :top_count, None, :] == expert_ids[:, None], axis=1)
+    own_member = lax.dynamic_slice_in_dim(member, me * experts_here, experts_here, 1)
     earlier = jnp.arange(shard_len)[:, None] < jnp.arange(shard_len)[None, :]
-    slot_of = dot("ent,tu->enu", own_member, earlier.astype(low)).astype(jnp.int32)
-    slot_of = jnp.where(own_member > 0, slot_of, -1)
-    onehot = slot_of[:, :, None, :] == jnp.arange(slots, dtype=jnp.int32)[None, None, :, None]
-    pick = onehot.astype(low)
+    slot_of = dot("net,tu->neu", own_member.astype(low), earlier.astype(low)).astype(jnp.int32)
+    slot_of = jnp.where(own_member, slot_of, -1)
+    onehot = slot_of[:, :, None, :] == jnp.arange(slots, dtype=jnp.int32)[:, None]
 
     x_all = by_place(line_gather(x_low)).reshape(seq_len, width)
-    x_all, valid_count = lax.optimization_barrier((x_all, valid_count))
     normed_one = rms_norm(x_all.astype(full), full_g1).astype(low)
     qkv_rows = dot("td,dc->ct", normed_one, full_qkv)
     qkv_rows = qkv_rows.reshape(kv_here, GROUP + 2, HEAD_DIM, seq_len)
@@ -326,25 +561,18 @@
     normed_two, norm_two_pull = jax.vjp(rms_norm, hidden, full_g2)
 
     tokens = jnp.stack(line_gather(normed_two.astype(low)))
-    logits = dot("ntd,de->nte", tokens, full_router)
+    logits = dot("ntd,de->net", tokens, full_router)
     chosen = jnp.where(member, logits, masked_score)
-    gate_exp = jnp.where(member, jnp.exp(chosen - jnp.max(chosen, axis=2, keepdims=True)), 0.0)
-    gates = gate_exp / jnp.sum(gate_exp, axis=2, keepdims=True)
-    own_gates = lax.dynamic_slice_in_dim(gates, me * experts_here, experts_here, 2)
-    slot_gates = jnp.sum(
-        onehot.astype(full) * jnp.transpose(own_gates, (2, 0, 1))[:, :, None, :], axis=3
-    )
-    expert_in = dot("enct,ntd->encd", pick, tokens).astype(low)
-    expert_in = expert_in.reshape(experts_here, seq_devs * slots, width)
-    gate_act = dot("erd,edf->erf", expert_in, full_gate)
-    up_act = dot("erd,edf->erf", expert_in, full_up)
-    act_out, act_pull = jax.vjp(swiglu, gate_act, up_act)
-    act_low = act_out.astype(low)
-    expert_out = dot("erf,efd->erd", act_low, full_down).astype(low)
+    gate_exp = jnp.where(member, jnp.exp(chosen - jnp.max(chosen, axis=1, keepdims=True)), 0.0)
+    gates = gate_exp / jnp.sum(gate_exp, axis=1, keepdims=True)
+    own_gates = lax.dynamic_slice_in_dim(gates, me * experts_here, experts_here, 1)
+    row_gates = jnp.sum(jnp.where(onehot, own_gates[:, :, None, :], 0.0), axis=3)
+    row_gates = jnp.swapaxes(row_gates, 0, 1).reshape(experts_here, seq_devs * slots, 1)
+    expert_in = pick_rows(slot_of, tokens, slots).reshape(experts_here, seq_devs * slots, width)
+    gate_act, up_act, expert_out = experts_forward(expert_in, full_gate, full_up, full_down)
     expert_out = expert_out.reshape(experts_here, seq_devs, slots, width)
-    gated_pick = pick * slot_gates.astype(low)[..., None]
-    mix_parts = dot("enct,encd->ntd", gated_pick, expert_out)
-    mixture = line_scatter([mix_parts[k] for k in range(seq_devs)])
+    mix_parts = put_rows(slot_of, own_gates, expert_out)
+    mixture = line_scatter([mix_parts[k].astype(full) for k in range(seq_devs)])
     output_f32 = hidden + resid_mult * mixture
     activations = output_f32.astype(low).reshape(1, shard_len, width)
     error_rows = output_f32 - teacher.astype(full).reshape(shard_len, width)
@@ -355,40 +583,31 @@
     d_mix = resid_mult * d_out
     mix_dot = jnp.stack(line_gather(jnp.sum(d_mix * mixture, axis=1)))
     d_tokens = jnp.stack(line_gather(d_mix.astype(low)))
-    d_rows = dot("enct,ntd->encd", pick, d_tokens).astype(low)
-    d_rows = d_rows.reshape(experts_here, seq_devs * slots, width)
-    d_act_raw = dot("erd,efd->erf", d_rows, full_down)
-    row_gates = slot_gates.reshape(experts_here, seq_devs * slots, 1)
-    d_slot_gates = jnp.sum(d_act_raw * act_low.astype(full), axis=2)
-    down_part = dot("erf,erd->efd", (act_low.astype(full) * row_gates).astype(low), d_rows)
-    d_gate_act, d_up_act = act_pull(d_act_raw * row_gates)
-    d_gate_low = d_gate_act.astype(low)
-    d_up_low = d_up_act.astype(low)
-    gate_part = dot("erd,erf->edf", expert_in, d_gate_low)
-    up_part = dot("erd,erf->edf", expert_in, d_up_low)
-    d_expert_in = dot("erf,edf->erd", d_gate_low, full_gate)
-    d_expert_in = (d_expert_in + dot("erf,edf->erd", d_up_low, full_up)).astype(low)
+    d_rows = pick_rows(slot_of, d_tokens, slots).reshape(experts_here, seq_devs * slots, width)
+    d_expert_in, d_gate_up, act_low, d_row_gates = experts_backward(
+        d_rows, row_gates, gate_act, up_act, full_gate, full_up, full_down
+    )
     d_expert_in = d_expert_in.reshape(experts_here, seq_devs, slots, width)
-    d_gates = jnp.sum(
-        onehot.astype(full)
-        * d_slot_gates.reshape(experts_here, seq_devs, slots)[..., None],
-        axis=2,
-    )
-    d_gates = jnp.transpose(d_gates, (1, 2, 0))
-    d_logits = (own_gates * (d_gates - mix_dot[:, :, None])).astype(low)
+    d_row_gates = jnp.swapaxes(d_row_gates.reshape(experts_here, seq_devs, slots), 0, 1)
+    d_gates = jnp.sum(jnp.where(onehot, d_row_gates[..., None], 0.0), axis=2)
+    d_logits = (own_gates * (d_gates - mix_dot[:, None, :])).astype(low)
     own_router = lax.dynamic_slice_in_dim(full_router, me * experts_here, experts_here, 1)
-    d_normed_parts = dot("enct,encd->ntd", pick, d_expert_in) + dot(
-        "nte,de->ntd", d_logits, own_router
-    )
-    router_part = dot("ntd,nte->de", tokens, d_logits)
-    d_normed_two = line_scatter([d_normed_parts[k] for k in range(seq_devs)])
-    d_normed_two, gate_part, up_part, down_part = lax.optimization_barrier(
-        (d_normed_two, gate_part.astype(low), up_part.astype(low), down_part.astype(low))
-    )
-    gate_part, up_part, down_part = (
-        lax.psum_scatter(part, "fsdp", scatter_dimension=1, tiled=True)
-        for part in (gate_part, up_part, down_part)
-    )
+    d_normed_parts = put_rows(slot_of, own_member.astype(full), d_expert_in)
+    d_routed = dot("net,de->ntd", d_logits, own_router)
+    router_part = dot("ntd,net->de", tokens, d_logits)
+    d_normed_two = line_scatter(
+        [d_normed_parts[k].astype(full) + d_routed[k] for k in range(seq_devs)]
+    )
+    order_a, order_b = halving_bits()
+    expert_parts = weight_grads(
+        lax.axis_index("fsdp").reshape(1), expert_in, d_rows, d_gate_up, act_low, order_a, order_b
+    )
+    d_normed_two, expert_parts = lax.optimization_barrier((d_normed_two, expert_parts))
+    gate_grad, up_grad, down_left, down_right = (
+        halving_sum(keep, send, order)
+        for (keep, send), order in zip(expert_parts, (order_a, order_b, order_a, order_b))
+    )
+    down_grad = jnp.concatenate([down_left, down_right], axis=2)
 
     d_hidden_norm, gain_two_part = norm_two_pull(d_normed_two)
     d_hidden = d_out + d_hidden_norm
@@ -405,34 +624,39 @@
     d_turned = rotate(d_turned, cosine, -sine_vals).astype(low)
     d_qkv = jnp.concatenate([d_turned, value_grad[:, None]], axis=1).reshape(group_w, seq_len)
     qkv_part = dot("td,ct->dc", normed_one, d_qkv).astype(low)
-    d_normed_parts = dot("ct,dc->td", d_qkv, full_qkv).reshape(seq_devs, shard_len, width)
-    d_normed_parts = d_normed_parts[(me - jnp.arange(seq_devs)) % seq_devs]
-    d_normed_one = line_scatter([d_normed_parts[k] for k in range(seq_devs)])
+    d_normed_parts = dot("ct,dc->td", d_qkv, full_qkv).astype(low)
+    d_normed_parts = from_place(d_normed_parts.reshape(seq_devs, shard_len, width))
+    d_normed_one = line_scatter([part.astype(full) for part in d_normed_parts])
     x_rows = x_low.astype(full)
     _, norm_one_pull = jax.vjp(lambda v: rms_norm(v, full_g1), x_rows)
     input_grad = (d_hidden + norm_one_pull(d_normed_one)[0]).reshape(1, shard_len, width)
 
-    def rows_sum(part):
-        return lax.psum_scatter(part, "fsdp", scatter_dimension=0, tiled=True)
-
-    gate_grad = gate_part.astype(full)
-    up_grad = up_part.astype(full)
-    down_grad = down_part.astype(full)
     own_columns = jnp.zeros((width, expert_total), full)
     own_columns = lax.dynamic_update_slice_in_dim(
         own_columns, router_part, me * experts_here, 1
     )
-    dense_part = jnp.concatenate(
-        [out_part, own_columns.astype(low), gain_two_part[:, None].astype(low)], axis=1
-    )
-    dense_part = lax.psum(rows_sum(dense_part), "seq").astype(full)
-    out_grad = dense_part[:, :width]
-    router_grad = dense_part[:, width : width + expert_total]
-    gain_two_grad = dense_part[:, width + expert_total]
-    qkv_grad = lax.all_gather(rows_sum(qkv_part), "seq", axis=1, tiled=True).astype(full)
+    rest = jnp.concatenate([own_columns.astype(low), gain_two_part[:, None].astype(low)], axis=1)
+    middle = width // 2
+    dense = jnp.concatenate(
+        [
+            rows_sum(out_part[:, :middle], order_a),
+            rows_sum(jnp.concatenate([out_part[:, middle:], rest], axis=1), order_b),
+        ],
+        axis=1,
+    )
+    dense = lax.psum(dense.astype(low), "seq").astype(full)
+    out_grad = dense[:, :width]
+    router_grad = dense[:, width : width + expert_total]
+    gain_two_grad = dense[:, width + expert_total]
+    middle = group_w // 2
+    own_grad = jnp.concatenate(
+        [rows_sum(qkv_part[:, :middle], order_a), rows_sum(qkv_part[:, middle:], order_b)], axis=1
+    )
+    qkv_grad = by_place(line_gather(own_grad.astype(low)))
+    qkv_grad = jnp.swapaxes(qkv_grad, 0, 1).reshape(-1, QKV_W).astype(full)
     gain_one_grad = jnp.sum(qkv_grad * w_qkv.astype(full), axis=1) / gain_one.astype(full)
-    squares, input_grad = lax.optimization_barrier((squares, input_grad))
-    loss_value = lax.psum(squares, ("fsdp", "seq")) / (valid_count * width)
+    squares = total(squares.reshape(1, 1), "seq", "fsdp")[0, 0]
+    loss_value = squares / (valid_count * width)
     return (
         activations,
         loss_value,

time: 1670 us -> 1470 us (0.88)
  matrix products: 345 us -> 47.5 us
  Pallas kernels: 96.2 us -> 295 us
  blocking collectives: 211 us -> 58.8 us
  other arithmetic: 101 us -> 155 us
  starting transfers between devices: 136 us -> 176 us
  local copies, waits for them, and re-layouts: 110 us -> 82.7 us
  waiting for transfers between devices: 643 us -> 620 us
    dot_general x23 -> x9, matrix products: 345 us -> 42 us  [dot(): return jnp.einsum(spec, left, right, preferred_element_type=full)]
    reduce_scatter x4 -> x0, waiting for transfers between devices: 212 us -> none  [the longest x3 212 us: shards(): lax.psum_scatter(part, 'fsdp', scatter_dimension=1, tiled=True)]
    pallas_call x0 -> x7, Pallas kernels: none -> 200 us  [the longest x1 49.5 us: weight_grads(): pl.pallas_call(functools.partial(weight_grads_kernel, bits_a, bits_b), gr...]
    ppermute x0 -> x32, waiting for transfers between devices: none -> 154 us  [swap(): lax.ppermute(value, axis, [(i, i ^ bit) for i in range(lax.axis_size(axis...]
    psum x2 -> x0, blocking collectives: 128 us -> none  [the longest x1 89.2 us: shards(): valid_count = lax.psum(jnp.sum(valid_rows), ('fsdp', 'seq'))]
    psum x1, waiting for transfers between devices: 0.02 us -> 46.4 us  [shards(): dense = lax.psum(dense.astype(low), 'seq').astype(full)]
    ppermute x15 -> x18, waiting for transfers between devices: 177 us -> 220 us  [line_gather(): lax.ppermute(lefts[-1], 'seq', [(i, i - 1) for i in range(1, n - k + 1)])]
    convert_element_type x5 -> x0, local copies, waits for them, and re-layouts: 41.6 us -> none  [the longest x1 16.4 us: shards(): d_rows = dot('enct,ntd->encd', pick, d_tokens).astype(low)]
  transfers between devices with their start and end apart: 60 -> 93, of which waited for: 26 -> 40; matrix products, arithmetic and copies ran while one was open for 17% -> 14% of each run, Pallas kernels for 6% -> 11%
where the time goes in v3:
time: 1470 us; the launch traced here: 1460 us
  waiting for transfers between devices  620 us (42%)
  Pallas kernels  295 us (20%)
  starting transfers between devices  176 us (12%)
  other arithmetic  155 us (11%)
  local copies, waits for them, and re-layouts  82.7 us (6%)
  blocking collectives  58.8 us (4%)
  matrix products  47.5 us (3%)
  between operations  23.9 us (2%)
    ppermute x18, waiting for transfers between devices, line_gather(): lax.ppermute(lefts[-1], 'seq', [(i, i - 1) for i in range(1, n - k + 1)])  220 us
    ppermute x32, waiting for transfers between devices, swap(): lax.ppermute(value, axis, [(i, i ^ bit) for i in range(lax.axis_size(axis...  154 us
    ppermute x9, waiting for transfers between devices, line_scatter(): lax.ppermute(to_right.astype(low), 'seq', [(i, i + 1) for i in range(n -...  135 us
    pallas_call x1, Pallas kernels, attention_backward(): pl.pallas_call(functools.partial(backward_kernel, seq_len, query_rows, ke...  55.6 us
    ppermute x9, starting transfers between devices, line_scatter(): lax.ppermute(to_right.astype(low), 'seq', [(i, i + 1) for i in range(n -...  50 us
    pallas_call x1, Pallas kernels, weight_grads(): pl.pallas_call(functools.partial(weight_grads_kernel, bits_a, bits_b), gr...  49.5 us
    all_to_all x1, blocking collectives, shards(): lax.all_to_all(attended, 'seq', split_axis=0, concat_axis=0, tiled=True)  49.2 us
    pallas_call x1, Pallas kernels, experts_backward(): pl.pallas_call(experts_back_kernel, grid=(experts,), in_specs=[one(count,...  48.6 us
  transfers between devices with their start and end apart: 93, of which 40 were waited for; matrix products, arithmetic and copies ran while one was open for 14% of the time, Pallas kernels for 11%

profile of v3, /device:TPU:0, one launch (start us, length us, event | category | flops | bytes accessed | tf_op | source)
XLA Modules:
  0.0 1459.2 jit_solution(15447268526242275210)
XLA Ops:
  12.9 6.7 collective-permute-start
  19.6 31.3 %collective-permute-done.1 = bf16[512,1536]{1,0:T(8,128)(2,1)S(1)} collective-permute-done((bf16[512,1536]{1,0:T(8,128)(2,1)S(1)}, bf16[512,1536]{1,0:T(8,128)(2,1)S(1)}, u32[]{:S(2)}, u32[]{:S(2)}) %collective-permute-start.1) | collective-permute-done | bytes 1572896 | tf_op jit(solution)/shard_map/ppermute | solution.py:66
  54.1 34.4 %collective-permute-done.2 = bf16[512,1536]{1,0:T(8,128)(2,1)} collective-permute-done((bf16[512,1536]{1,0:T(8,128)(2,1)S(1)}, bf16[512,1536]{1,0:T(8,128)(2,1)}, u32[]{:S(2)}, u32[]{:S(2)}) %collective-permute-start.2) | collective-permute-done | bytes 1572896 | tf_op jit(solution)/shard_map/ppermute | solution.py:66
  90.2 9.6 all-gather
  111.4 14.0 collective-permute-done.3
  151.1 39.9 %attention_forward.1 = (bf16[4,384,512]{2,1,0:T(8,128)(2,1)S(1)}, f32[2,3,64,2048]{3,2,1,0:T(8,128)S(1)}, f32[2,3,1,2048]{3,2,1,0:T(1,128)S(1)}) custom-call(s32[1,2048]{1,0:T(1,128)S(1)} %bitcast.223, bf16[2,3,64,2048]{3,2,1,0:T(8,128)(2,1)S(1)} %copy.148.q_ref, bf16[2,2048,64]{2,1,0:T(8,128)(2,1)S(1)} %copy.149.k_ref, ...), custom_call_target="tpu_custom_call" | custom-call | tf_op jit(solution)/shard_map/attention_forward/pallas_call | solution.py:190
  192.6 49.2 %all_to_all.10 = bf16[4,384,512]{2,1,0:T(8,128)(2,1)} all-to-all(bf16[4,384,512]{2,1,0:T(8,128)(2,1)S(1)} %get-tuple-element.41), channel_id=1, replica_groups=mesh['fsdp'=8,'seq'=4] {'seq'}, dimensions={0} | all-to-all | bytes 3145728 | tf_op jit(solution)/shard_map/all_to_all | solution.py:557
  241.8 6.6 multiply_reduce_fusion.3
  254.7 29.9 %collective-permute-done.12 = bf16[512,1536]{1,0:T(8,128)(2,1)} collective-permute-done((bf16[512,1536]{1,0:T(8,128)(2,1)S(1)}, bf16[512,1536]{1,0:T(8,128)(2,1)}, u32[]{:S(2)}, u32[]{:S(2)}) %collective-permute-start.12) | collective-permute-done | bytes 1572896 | tf_op jit(solution)/shard_map/ppermute | solution.py:65
  298.1 28.4 %collective-permute-done.7 = s32[9,512]{1,0:T(8,128)S(1)} collective-permute-done((s32[9,512]{1,0:T(8,128)S(1)}, s32[9,512]{1,0:T(8,128)S(1)}, u32[]{:S(2)}, u32[]{:S(2)}) %collective-permute-start.7) | collective-permute-done | bytes 18464 | tf_op jit(solution)/shard_map/ppermute | solution.py:66
  346.6 26.9 %collective-permute-done.15 = bf16[512,1536]{1,0:T(8,128)(2,1)S(1)} collective-permute-done((bf16[512,1536]{1,0:T(8,128)(2,1)}, bf16[512,1536]{1,0:T(8,128)(2,1)S(1)}, u32[]{:S(2)}, u32[]{:S(2)}) %collective-permute-start.15) | collective-permute-done | bytes 1572896 | tf_op jit(solution)/shard_map/ppermute | solution.py:66
  377.1 14.5 pick_rows.2
  398.2 40.3 %experts_forward.1 = (bf16[10,640,512]{2,1,0:T(8,128)(2,1)}, bf16[10,640,512]{2,1,0:T(8,128)(2,1)}, bf16[10,640,1536]{2,1,0:T(8,128)(2,1)}) custom-call(bf16[10,640,1536]{2,1,0:T(8,128)(2,1)} %bitcast.227, bf16[10,1536,512]{2,1,0:T(8,128)(2,1)} %all-gather.11.cloned.1.call-done.wg_ref, bf16[10,1536,512]{2,1,0:T(8,128)(2,1)} %all-gather.13.cloned.1.call-done.wu_ref, ...), custom_call_target="tpu_custom_call" | custom-call | tf_op jit(solution)/shard_map/experts_forward/pallas_call | solution.py:368
  438.5 16.0 %put_rows.2 = bf16[4,512,1536]{2,1,0:T(8,128)(2,1)} custom-call(s32[4,10,512]{2,1,0:T(8,128)S(1)} %fusion.30.slot_ref, f32[4,10,512]{2,1,0:T(8,128)S(1)} %dynamic-slice_divide_fusion.gate_ref, bf16[10,4,160,1536]{3,2,1,0:T(8,128)(2,1)} %bitcast.232), custom_call_target="tpu_custom_call" | custom-call | tf_op jit(solution)/shard_map/put_rows/pallas_call | solution.py:336
  460.7 28.5 %collective-permute-done.18 = bf16[512,1536]{1,0:T(8,128)(2,1)S(1)} collective-permute-done((bf16[512,1536]{1,0:T(8,128)(2,1)S(1)}, bf16[512,1536]{1,0:T(8,128)(2,1)S(1)}, u32[]{:S(2)}, u32[]{:S(2)}) %collective-permute-start.18) | collective-permute-done | bytes 1572896 | tf_op jit(solution)/shard_map/ppermute | solution.py:78
  495.4 26.4 %collective-permute-done.19 = bf16[512,1536]{1,0:T(8,128)(2,1)S(1)} collective-permute-done((bf16[512,1536]{1,0:T(8,128)(2,1)S(1)}, bf16[512,1536]{1,0:T(8,128)(2,1)S(1)}, u32[]{:S(2)}, u32[]{:S(2)}) %collective-permute-start.19) | collective-permute-done | bytes 1572896 | tf_op jit(solution)/shard_map/ppermute | solution.py:78
  524.5 8.4 collective-permute-start.20
  546.1 12.8 collective-permute-done.20
  576.4 27.6 %collective-permute-done.33 = bf16[512,1536]{1,0:T(8,128)(2,1)S(1)} collective-permute-done((bf16[512,1536]{1,0:T(8,128)(2,1)S(1)}, bf16[512,1536]{1,0:T(8,128)(2,1)S(1)}, u32[]{:S(2)}, u32[]{:S(2)}) %collective-permute-start.33) | collective-permute-done | bytes 1572896 | tf_op jit(solution)/shard_map/ppermute | solution.py:66
  613.2 7.1 collective-permute-start.38
  620.3 15.5 %collective-permute-done.39 = f32[512]{0:T(512)S(1)} collective-permute-done((f32[512]{0:T(512)S(1)}, f32[512]{0:T(512)S(1)}, u32[]{:S(2)}, u32[]{:S(2)}) %collective-permute-start.39) | collective-permute-done | bytes 2080 | tf_op jit(solution)/shard_map/ppermute | solution.py:66
  648.6 18.5 %collective-permute-done.41 = f32[512]{0:T(512)S(1)} collective-permute-done((f32[512]{0:T(512)S(1)}, f32[512]{0:T(512)S(1)}, u32[]{:S(2)}, u32[]{:S(2)}) %collective-permute-start.41) | collective-permute-done | bytes 2080 | tf_op jit(solution)/shard_map/ppermute | solution.py:66
  675.2 14.7 %pick_rows.3 = bf16[10,4,160,1536]{3,2,1,0:T(8,128)(2,1)} custom-call(s32[4,10,512]{2,1,0:T(8,128)S(1)} %fusion.30.slot_ref, bf16[4,512,1536]{2,1,0:T(8,128)(2,1)} %pad_maximum_fusion.1.tok_ref), custom_call_target="tpu_custom_call" | custom-call | tf_op jit(solution)/shard_map/pick_rows/pallas_call | solution.py:307
  689.9 48.6 %experts_backward.1 = (bf16[10,640,1536]{2,1,0:T(8,128)(2,1)}, bf16[10,640,1024]{2,1,0:T(8,128)(2,1)}, bf16[10,640,512]{2,1,0:T(8,128)(2,1)}, f32[10,640,1]{2,1,0:T(8,128)}) custom-call(bf16[10,640,1536]{2,1,0:T(8,128)(2,1)} %bitcast.225, f32[10,640,1]{2,1,0:T(8,128)} %reshape.475.gate_ref, bf16[10,640,512]{2,1,0:T(8,128)(2,1)} %get-tuple-element.43.g_ref, ...), custom_call_target="tpu_custom_call" | custom-call | tf_op jit(solution)/shard_map/experts_backward/pallas_call | solution.py:406
  744.4 16.1 %put_rows.3 = bf16[4,512,1536]{2,1,0:T(8,128)(2,1)} custom-call(s32[4,10,512]{2,1,0:T(8,128)S(1)} %fusion.30.slot_ref, f32[4,10,512]{2,1,0:T(8,128)S(1)} %dynamic-slice_convert_fusion.gate_ref, bf16[10,4,160,1536]{3,2,1,0:T(8,128)(2,1)} %bitcast.231), custom_call_target="tpu_custom_call" | custom-call | tf_op jit(solution)/shard_map/put_rows/pallas_call | solution.py:336
  767.2 28.3 %collective-permute-done.44 = bf16[512,1536]{1,0:T(8,128)(2,1)S(1)} collective-permute-done((bf16[512,1536]{1,0:T(8,128)(2,1)S(1)}, bf16[512,1536]{1,0:T(8,128)(2,1)S(1)}, u32[]{:S(2)}, u32[]{:S(2)}) %collective-permute-start.44) | collective-permute-done | bytes 1572896 | tf_op jit(solution)/shard_map/ppermute | solution.py:78
  802.8 21.7 %collective-permute-done.45 = bf16[512,1536]{1,0:T(8,128)(2,1)S(1)} collective-permute-done((bf16[512,1536]{1,0:T(8,128)(2,1)S(1)}, bf16[512,1536]{1,0:T(8,128)(2,1)S(1)}, u32[]{:S(2)}, u32[]{:S(2)}) %collective-permute-start.45) | collective-permute-done | bytes 1572896 | tf_op jit(solution)/shard_map/ppermute | solution.py:78
  846.9 49.5 %weight_grads.1 = (bf16[4,10,192,512]{3,2,1,0:T(8,128)(2,1)}, bf16[4,10,192,512]{3,2,1,0:T(8,128)(2,1)}, bf16[4,10,192,512]{3,2,1,0:T(8,128)(2,1)}, bf16[4,10,19...) custom-call(s32[1]{0:T(128)} %bitcast.60.me_ref, ...), custom_call_target="tpu_custom_call" | custom-call | tf_op jit(solution)/shard_map/weight_grads/pallas_call | solution.py:470
  929.8 7.1 fusion.20
  939.4 5.9 all-to-all-start.1
  959.7 11.4 collective-permute-done.24
  972.3 5.9 collective-permute-start.25
  999.9 55.6 %attention_backward.1 = (bf16[2,3,64,2048]{3,2,1,0:T(8,128)(2,1)S(1)}, bf16[2,64,2048]{2,1,0:T(8,128)(2,1)S(1)}, bf16[2,64,2048]{2,1,0:T(8,128)(2,1)S(1)}) custom-call(s32[1,2048]{1,0:T(1,128)S(1)} %bitcast.224, bf16[2,3,64,2048]{3,2,1,0:T(8,128)(2,1)S(1)} %copy.148.q_ref, bf16[2,2048,64]{2,1,0:T(8,128)(2,1)S(1)} %copy.149.k_ref, ...), custom_call_target="tpu_custom_call" | custom-call | tf_op jit(solution)/shard_map/attention_backward/pallas_call | solution.py:261
  1071.4 7.4 convolution_convert_fusion.1
  1083.1 6.5 collective-permute-done.57
  1091.8 10.5 collective-permute-done.58
  1116.5 7.4 collective-permute-done.63
  1125.0 17.0 %collective-permute-done.50 = bf16[512,1536]{1,0:T(8,128)(2,1)S(1)} collective-permute-done((bf16[512,1536]{1,0:T(8,128)(2,1)S(1)}, bf16[512,1536]{1,0:T(8,128)(2,1)S(1)}, u32[]{:S(2)}, u32[]{:S(2)}) %collective-permute-start.50) | collective-permute-done | bytes 1572896 | tf_op jit(solution)/shard_map/ppermute | solution.py:78
  1158.3 46.4 %all-reduce.2.cloned.1.call-done = bf16[192,1577]{1,0:T(8,128)(2,1)} async-done(((bf16[192,1577]{1,0:T(8,128)(2,1)}), bf16[192,1577]{1,0:T(8,128)(2,1)}) %all-reduce.2.cloned.1.call-update) | async-done | bytes 605584 | tf_op jit(solution)/shard_map/psum | solution.py:647
  1228.4 5.8 add_convert_fusion.5
  1235.0 7.1 add_convert_fusion.3
  1244.0 6.7 add_convert_fusion.1
  1259.9 7.4 dynamic_update_slice.36
  1268.8 11.5 collective-permute-done.81
  1291.9 15.5 %collective-permute-start.52 = (bf16[512,1536]{1,0:T(8,128)(2,1)}, bf16[512,1536]{1,0:T(8,128)(2,1)S(1)}, u32[]{:S(2)}, u32[]{:S(2)}) collective-permute-start(bf16[512,1536]{1,0:T(8,128)(2,1)} %get-tuple-element.145), channel_id=1, source_target_pairs={{0,1},{1,2},{2,3},{4,5},{5,6},{6,7},{8,9},{9,10},{10,11},{12,13},{... | collective-permute-start | bytes 4718600 | tf_op jit(solution)/shard_map/ppermute | solution.py:78
  1309.2 82.4 %collective-permute-done.82 = bf16[1,10,64,768]{3,2,1,0:T(8,128)(2,1)S(1)} collective-permute-done((bf16[1,10,64,768]{3,2,1,0:T(8,128)(2,1)S(1)}, bf16[1,10,64,768]{3,2,1,0:T(8,128)(2,1)S(1)}, u32[]{:S(2)}, u32[]{:S(2)}) %collective-permute-start.82) | collective-permute-done | bytes 983072 | tf_op jit(solution)/shard_map/ppermute | solution.py:99
  1406.0 23.3 %collective-permute-done.55 = bf16[512,1536]{1,0:T(8,128)(2,1)S(1)} collective-permute-done((bf16[512,1536]{1,0:T(8,128)(2,1)S(1)}, bf16[512,1536]{1,0:T(8,128)(2,1)S(1)}, u32[]{:S(2)}, u32[]{:S(2)}) %collective-permute-start.55) | collective-permute-done | bytes 1572896 | tf_op jit(solution)/shard_map/ppermute | solution.py:79
  1433.4 9.1 collective-permute-done.76
  (462 shorter events, 414.1 us)
Async XLA Ops:
  7.2 101.6 %all-gather.7.cloned.1.call-start = ((), (), s32[]{:S(2)}) async-start(), calls=%async_computation.2 | async-start | bytes 2211840 | tf_op jit(solution)/shard_map/all_gather | solution.py:522
  8.9 232.9 %all-gather.9.cloned.1.call-start = ((), (), s32[]{:S(2)}) async-start(), calls=%async_computation.3 | async-start | bytes 5308416 | tf_op jit(solution)/shard_map/all_gather | solution.py:523
  9.7 388.4 %all-gather.11.cloned.1.call-start = ((), (), s32[]{:S(2)}) async-start(), calls=%async_computation.4 | async-start | bytes 17694720 | tf_op jit(solution)/shard_map/all_gather | solution.py:524
  10.5 387.7 %all-gather.13.cloned.1.call-start = ((), (), s32[]{:S(2)}) async-start(), calls=%async_computation.5 | async-start | bytes 17694720 | tf_op jit(solution)/shard_map/all_gather | solution.py:525
  11.0 387.1 %all-gather.15.cloned.1.call-start = ((), (), s32[]{:S(2)}) async-start(), calls=%async_computation.6 | async-start | bytes 17694720 | tf_op jit(solution)/shard_map/all_gather | solution.py:526
  11.6 39.3 %collective-permute-start.1 = (bf16[512,1536]{1,0:T(8,128)(2,1)S(1)}, bf16[512,1536]{1,0:T(8,128)(2,1)S(1)}, u32[]{:S(2)}, u32[]{:S(2)}) collective-permute-start(bf16[512,1536]{1,0:T(8,128)(2,1)S(1)} %bitcast.244), channel_id=1, source_target_pairs={{1,0},{2,1},{3,2},{5,4},{6,5},{7,6},{9,8},{10,9},{11,10},{13,12},{... | collective-permute-start | bytes 4718600 | tf_op jit(solution)/shard_map/ppermute | solution.py:66
  12.9 39.3 %collective-permute-start = (bf16[512,1536]{1,0:T(8,128)(2,1)S(1)}, bf16[512,1536]{1,0:T(8,128)(2,1)}, u32[]{:S(2)}, u32[]{:S(2)}) collective-permute-start(bf16[512,1536]{1,0:T(8,128)(2,1)S(1)} %bitcast.245), channel_id=1, source_target_pairs={{0,1},{1,2},{2,3},{4,5},{5,6},{6,7},{8,9},{9,10},{10,11},{12,13},{... | collective-permute-start | bytes 4718600 | tf_op jit(solution)/shard_map/ppermute | solution.py:65
  51.0 37.6 %collective-permute-start.2 = (bf16[512,1536]{1,0:T(8,128)(2,1)S(1)}, bf16[512,1536]{1,0:T(8,128)(2,1)}, u32[]{:S(2)}, u32[]{:S(2)}) collective-permute-start(bf16[512,1536]{1,0:T(8,128)(2,1)S(1)} %collective-permute-done.1), channel_id=1, source_target_pairs={{1,0},{2,1},{5,4},{6,5},{9,8},{10,9},{13,12},{14,13},{17,16},{18,1... | collective-permute-start | bytes 4718600 | tf_op jit(solution)/shard_map/ppermute | solution.py:66
  52.3 49.7 %collective-permute-start.4 = (bf16[512,1536]{1,0:T(8,128)(2,1)}, bf16[512,1536]{1,0:T(8,128)(2,1)}, u32[]{:S(2)}, u32[]{:S(2)}) collective-permute-start(bf16[512,1536]{1,0:T(8,128)(2,1)} %collective-permute-done), channel_id=1, source_target_pairs={{1,2},{2,3},{5,6},{6,7},{9,10},{10,11},{13,14},{14,15},{17,18},{18... | collective-permute-start | bytes 4718600 | tf_op jit(solution)/shard_map/ppermute | solution.py:65
  88.5 36.9 %collective-permute-start.3 = (bf16[512,1536]{1,0:T(8,128)(2,1)}, bf16[512,1536]{1,0:T(8,128)(2,1)}, u32[]{:S(2)}, u32[]{:S(2)}) collective-permute-start(bf16[512,1536]{1,0:T(8,128)(2,1)} %collective-permute-done.2), channel_id=1, source_target_pairs={{1,0},{5,4},{9,8},{13,12},{17,16},{21,20},{25,24},{29,28}} | collective-permute-start | bytes 4718600 | tf_op jit(solution)/shard_map/ppermute | solution.py:66
  250.4 34.2 %collective-permute-start.12 = (bf16[512,1536]{1,0:T(8,128)(2,1)S(1)}, bf16[512,1536]{1,0:T(8,128)(2,1)}, u32[]{:S(2)}, u32[]{:S(2)}) collective-permute-start(bf16[512,1536]{1,0:T(8,128)(2,1)S(1)} %multiply_convert_fusion.1), channel_id=1, source_target_pairs={{0,1},{1,2},{2,3},{4,5},{5,6},{6,7},{8,9},{9,10},{10,11},{12,13},{... | collective-permute-start | bytes 4718600 | tf_op jit(solution)/shard_map/ppermute | solution.py:65
  253.5 36.6 %collective-permute-start.13 = (bf16[512,1536]{1,0:T(8,128)(2,1)S(1)}, bf16[512,1536]{1,0:T(8,128)(2,1)}, u32[]{:S(2)}, u32[]{:S(2)}) collective-permute-start(bf16[512,1536]{1,0:T(8,128)(2,1)S(1)} %multiply_convert_fusion.1), channel_id=1, source_target_pairs={{1,0},{2,1},{3,2},{5,4},{6,5},{7,6},{9,8},{10,9},{11,10},{13,12},{... | collective-permute-start | bytes 4718600 | tf_op jit(solution)/shard_map/ppermute | solution.py:66
  284.7 53.4 %collective-permute-start.16 = (bf16[512,1536]{1,0:T(8,128)(2,1)}, bf16[512,1536]{1,0:T(8,128)(2,1)}, u32[]{:S(2)}, u32[]{:S(2)}) collective-permute-start(bf16[512,1536]{1,0:T(8,128)(2,1)} %collective-permute-done.12), channel_id=1, source_target_pairs={{1,2},{2,3},{5,6},{6,7},{9,10},{10,11},{13,14},{14,15},{17,18},{18... | collective-permute-start | bytes 4718600 | tf_op jit(solution)/shard_map/ppermute | solution.py:65
  290.0 49.6 %collective-permute-start.14 = (bf16[512,1536]{1,0:T(8,128)(2,1)}, bf16[512,1536]{1,0:T(8,128)(2,1)}, u32[]{:S(2)}, u32[]{:S(2)}) collective-permute-start(bf16[512,1536]{1,0:T(8,128)(2,1)} %collective-permute-done.13), channel_id=1, source_target_pairs={{1,0},{2,1},{5,4},{6,5},{9,8},{10,9},{13,12},{14,13},{17,16},{18,1... | collective-permute-start | bytes 4718600 | tf_op jit(solution)/shard_map/ppermute | solution.py:66
  339.6 33.9 %collective-permute-start.15 = (bf16[512,1536]{1,0:T(8,128)(2,1)}, bf16[512,1536]{1,0:T(8,128)(2,1)S(1)}, u32[]{:S(2)}, u32[]{:S(2)}) collective-permute-start(bf16[512,1536]{1,0:T(8,128)(2,1)} %collective-permute-done.14), channel_id=1, source_target_pairs={{1,0},{5,4},{9,8},{13,12},{17,16},{21,20},{25,24},{29,28}} | collective-permute-start | bytes 4718600 | tf_op jit(solution)/shard_map/ppermute | solution.py:66
  456.7 32.5 %collective-permute-start.18 = (bf16[512,1536]{1,0:T(8,128)(2,1)S(1)}, bf16[512,1536]{1,0:T(8,128)(2,1)S(1)}, u32[]{:S(2)}, u32[]{:S(2)}) collective-permute-start(bf16[512,1536]{1,0:T(8,128)(2,1)S(1)} %get-tuple-element.167), channel_id=1, source_target_pairs={{0,1},{4,5},{8,9},{12,13},{16,17},{20,21},{24,25},{28,29}} | collective-permute-start | bytes 4718600 | tf_op jit(solution)/shard_map/ppermute | solution.py:78
  490.0 31.9 %collective-permute-start.19 = (bf16[512,1536]{1,0:T(8,128)(2,1)S(1)}, bf16[512,1536]{1,0:T(8,128)(2,1)S(1)}, u32[]{:S(2)}, u32[]{:S(2)}) collective-permute-start(bf16[512,1536]{1,0:T(8,128)(2,1)S(1)} %get-tuple-element.165), channel_id=1, source_target_pairs={{0,1},{1,2},{4,5},{5,6},{8,9},{9,10},{12,13},{13,14},{16,17},{17,1... | collective-permute-start | bytes 4718600 | tf_op jit(solution)/shard_map/ppermute | solution.py:78
  524.5 34.4 %collective-permute-start.20 = (bf16[512,1536]{1,0:T(8,128)(2,1)}, bf16[512,1536]{1,0:T(8,128)(2,1)}, u32[]{:S(2)}, u32[]{:S(2)}) collective-permute-start(bf16[512,1536]{1,0:T(8,128)(2,1)} %get-tuple-element.163), channel_id=1, source_target_pairs={{0,1},{1,2},{2,3},{4,5},{5,6},{6,7},{8,9},{9,10},{10,11},{12,13},{... | collective-permute-start | bytes 4718600 | tf_op jit(solution)/shard_map/ppermute | solution.py:78
  532.8 31.3 %collective-permute-start.23 = (bf16[512,1536]{1,0:T(8,128)(2,1)}, bf16[512,1536]{1,0:T(8,128)(2,1)}, u32[]{:S(2)}, u32[]{:S(2)}) collective-permute-start(bf16[512,1536]{1,0:T(8,128)(2,1)} %get-tuple-element.164), channel_id=1, source_target_pairs={{1,0},{2,1},{3,2},{5,4},{6,5},{7,6},{9,8},{10,9},{11,10},{13,12},{... | collective-permute-start | bytes 4718600 | tf_op jit(solution)/shard_map/ppermute | solution.py:79
  569.4 34.6 %collective-permute-start.33 = (bf16[512,1536]{1,0:T(8,128)(2,1)S(1)}, bf16[512,1536]{1,0:T(8,128)(2,1)S(1)}, u32[]{:S(2)}, u32[]{:S(2)}) collective-permute-start(bf16[512,1536]{1,0:T(8,128)(2,1)S(1)} %get-tuple-element.147), channel_id=1, source_target_pairs={{1,0},{2,1},{3,2},{5,4},{6,5},{7,6},{9,8},{10,9},{11,10},{13,12},{... | collective-permute-start | bytes 4718600 | tf_op jit(solution)/shard_map/ppermute | solution.py:66
  570.7 34.6 %collective-permute-start.32 = (bf16[512,1536]{1,0:T(8,128)(2,1)S(1)}, bf16[512,1536]{1,0:T(8,128)(2,1)}, u32[]{:S(2)}, u32[]{:S(2)}) collective-permute-start(bf16[512,1536]{1,0:T(8,128)(2,1)S(1)} %get-tuple-element.147), channel_id=1, source_target_pairs={{0,1},{1,2},{2,3},{4,5},{5,6},{6,7},{8,9},{9,10},{10,11},{12,13},{... | collective-permute-start | bytes 4718600 | tf_op jit(solution)/shard_map/ppermute | solution.py:65
  604.0 33.7 %collective-permute-start.34 = (bf16[512,1536]{1,0:T(8,128)(2,1)S(1)}, bf16[512,1536]{1,0:T(8,128)(2,1)}, u32[]{:S(2)}, u32[]{:S(2)}) collective-permute-start(bf16[512,1536]{1,0:T(8,128)(2,1)S(1)} %collective-permute-done.33), channel_id=1, source_target_pairs={{1,0},{2,1},{5,4},{6,5},{9,8},{10,9},{13,12},{14,13},{17,16},{18,1... | collective-permute-start | bytes 4718600 | tf_op jit(solution)/shard_map/ppermute | solution.py:66
  605.3 42.2 %collective-permute-start.36 = (bf16[512,1536]{1,0:T(8,128)(2,1)}, bf16[512,1536]{1,0:T(8,128)(2,1)}, u32[]{:S(2)}, u32[]{:S(2)}) collective-permute-start(bf16[512,1536]{1,0:T(8,128)(2,1)} %collective-permute-done.32), channel_id=1, source_target_pairs={{1,2},{2,3},{5,6},{6,7},{9,10},{10,11},{13,14},{14,15},{17,18},{18... | collective-permute-start | bytes 4718600 | tf_op jit(solution)/shard_map/ppermute | solution.py:65
  637.7 31.0 %collective-permute-start.35 = (bf16[512,1536]{1,0:T(8,128)(2,1)}, bf16[512,1536]{1,0:T(8,128)(2,1)}, u32[]{:S(2)}, u32[]{:S(2)}) collective-permute-start(bf16[512,1536]{1,0:T(8,128)(2,1)} %collective-permute-done.34), channel_id=1, source_target_pairs={{1,0},{5,4},{9,8},{13,12},{17,16},{21,20},{25,24},{29,28}} | collective-permute-start | bytes 4718600 | tf_op jit(solution)/shard_map/ppermute | solution.py:66
  830.7 65.6 %collective-permute-start.46 = (bf16[512,1536]{1,0:T(8,128)(2,1)}, bf16[512,1536]{1,0:T(8,128)(2,1)}, u32[]{:S(2)}, u32[]{:S(2)}) collective-permute-start(bf16[512,1536]{1,0:T(8,128)(2,1)} %get-tuple-element.149), channel_id=1, source_target_pairs={{0,1},{1,2},{2,3},{4,5},{5,6},{6,7},{8,9},{9,10},{10,11},{12,13},{... | collective-permute-start | bytes 4718600 | tf_op jit(solution)/shard_map/ppermute | solution.py:78
  836.2 60.1 %collective-permute-start.49 = (bf16[512,1536]{1,0:T(8,128)(2,1)}, bf16[512,1536]{1,0:T(8,128)(2,1)}, u32[]{:S(2)}, u32[]{:S(2)}) collective-permute-start(bf16[512,1536]{1,0:T(8,128)(2,1)} %get-tuple-element.150), channel_id=1, source_target_pairs={{1,0},{2,1},{3,2},{5,4},{6,5},{7,6},{9,8},{10,9},{11,10},{13,12},{... | collective-permute-start | bytes 4718600 | tf_op jit(solution)/shard_map/ppermute | solution.py:79
  939.4 57.4 %all-to-all-start.1 = ((bf16[4,384,512]{2,1,0:T(8,128)(2,1)}), bf16[4,384,512]{2,1,0:T(8,128)(2,1)}, u32[]{:S(2)}, u32[]{:S(2)}) async-start(bf16[4,384,512]{2,1,0:T(8,128)(2,1)} %bitcast.260), calls=%async_computation.1 | async-start | bytes 3145728 | tf_op jit(solution)/shard_map/all_to_all | solution.py:616
  945.3 259.4 %all-reduce.2.cloned.1.call-start = ((), (), s32[]{:S(2)}) async-start(), calls=%async_computation.7 | async-start | bytes 1277952 | tf_op jit(solution)/shard_map/psum | solution.py:647
  948.4 44.6 %collective-permute-start.69 = (bf16[2,192,768]{2,1,0:T(8,128)(2,1)}, bf16[2,192,768]{2,1,0:T(8,128)(2,1)}, u32[]{:S(2)}, u32[]{:S(2)}) collective-permute-start(bf16[2,192,768]{2,1,0:T(8,128)(2,1)} %get-tuple-element.180), channel_id=1, source_target_pairs={{0,8},{4,12},{8,0},{12,4},{16,24},{20,28},{24,16},{28,20},{1,9},{5... | collective-permute-start | bytes 1769480 | tf_op jit(solution)/shard_map/ppermute | solution.py:99
  952.7 42.2 %collective-permute-start.72 = (bf16[2,192,809]{2,1,0:T(8,128)(2,1)}, bf16[2,192,809]{2,1,0:T(8,128)(2,1)}, u32[]{:S(2)}, u32[]{:S(2)}) collective-permute-start(bf16[2,192,809]{2,1,0:T(8,128)(2,1)} %get-tuple-element.178), channel_id=1, source_target_pairs={{0,16},{4,20},{8,24},{12,28},{16,0},{20,4},{24,8},{28,12},{1,17},{... | collective-permute-start | bytes 1863944 | tf_op jit(solution)/shard_map/ppermute | solution.py:99
  989.7 99.9 %collective-permute-start.28 = (f32[1,1]{1,0:T(1,128)}, f32[1,1]{1,0:T(1,128)}, u32[]{:S(2)}, u32[]{:S(2)}) collective-permute-start(f32[1,1]{1,0:T(1,128)} %add.392), channel_id=1, source_target_pairs={{0,16},{4,20},{8,24},{12,28},{16,0},{20,4},{24,8},{28,12},{1,17},{... | collective-permute-start | bytes 20 | tf_op jit(solution)/shard_map/ppermute | solution.py:99
  992.6 241.7 %collective-permute-start.74 = (bf16[4,10,192,512]{3,2,1,0:T(8,128)(2,1)}, bf16[4,10,192,512]{3,2,1,0:T(8,128)(2,1)}, u32[]{:S(2)}, u32[]{:S(2)}) collective-permute-start(bf16[4,10,192,512]{3,2,1,0:T(8,128)(2,1)} %get-tuple-element.64), channel_id=1, source_target_pairs={{0,4},{4,0},{8,12},{12,8},{16,20},{20,16},{24,28},{28,24},{1,5},{5... | collective-permute-start | bytes 23592968 | tf_op jit(solution)/shard_map/ppermute | solution.py:99
  992.6 251.4 %collective-permute-start.77 = (bf16[4,10,192,512]{3,2,1,0:T(8,128)(2,1)}, bf16[4,10,192,512]{3,2,1,0:T(8,128)(2,1)}, u32[]{:S(2)}, u32[]{:S(2)}) collective-permute-start(bf16[4,10,192,512]{3,2,1,0:T(8,128)(2,1)} %get-tuple-element.66), channel_id=1, source_target_pairs={{0,4},{4,0},{8,12},{12,8},{16,20},{20,16},{24,28},{28,24},{1,5},{5... | collective-permute-start | bytes 23592968 | tf_op jit(solution)/shard_map/ppermute | solution.py:99
  1089.6 121.2 %collective-permute-start.80 = (bf16[4,10,64,768]{3,2,1,0:T(8,128)(2,1)}, bf16[4,10,64,768]{3,2,1,0:T(8,128)(2,1)}, u32[]{:S(2)}, u32[]{:S(2)}) collective-permute-start(bf16[4,10,64,768]{3,2,1,0:T(8,128)(2,1)} %get-tuple-element.68), channel_id=1, source_target_pairs={{0,4},{4,0},{8,12},{12,8},{16,20},{20,16},{24,28},{28,24},{1,5},{5... | collective-permute-start | bytes 11796488 | tf_op jit(solution)/shard_map/ppermute | solution.py:99
  1109.1 32.9 %collective-permute-start.50 = (bf16[512,1536]{1,0:T(8,128)(2,1)S(1)}, bf16[512,1536]{1,0:T(8,128)(2,1)S(1)}, u32[]{:S(2)}, u32[]{:S(2)}) collective-permute-start(bf16[512,1536]{1,0:T(8,128)(2,1)S(1)} %dynamic-slice_bitcast_fusion), channel_id=1, source_target_pairs={{0,1},{4,5},{8,9},{12,13},{16,17},{20,21},{24,25},{28,29}} | collective-permute-start | bytes 4718600 | tf_op jit(solution)/shard_map/ppermute | solution.py:78
  1123.9 103.6 %collective-permute-start.83 = (bf16[4,10,64,768]{3,2,1,0:T(8,128)(2,1)}, bf16[4,10,64,768]{3,2,1,0:T(8,128)(2,1)}, u32[]{:S(2)}, u32[]{:S(2)}) collective-permute-start(bf16[4,10,64,768]{3,2,1,0:T(8,128)(2,1)} %get-tuple-element.70), channel_id=1, source_target_pairs={{0,4},{4,0},{8,12},{12,8},{16,20},{20,16},{24,28},{28,24},{1,5},{5... | collective-permute-start | bytes 11796488 | tf_op jit(solution)/shard_map/ppermute | solution.py:99
  1150.1 72.8 %collective-permute-start.51 = (bf16[512,1536]{1,0:T(8,128)(2,1)S(1)}, bf16[512,1536]{1,0:T(8,128)(2,1)}, u32[]{:S(2)}, u32[]{:S(2)}) collective-permute-start(bf16[512,1536]{1,0:T(8,128)(2,1)S(1)} %fusion.6), channel_id=1, source_target_pairs={{0,1},{1,2},{4,5},{5,6},{8,9},{9,10},{12,13},{13,14},{16,17},{17,1... | collective-permute-start | bytes 4718600 | tf_op jit(solution)/shard_map/ppermute | solution.py:78
  1234.2 46.1 %collective-permute-start.81 = (bf16[2,10,64,768]{3,2,1,0:T(8,128)(2,1)}, bf16[2,10,64,768]{3,2,1,0:T(8,128)(2,1)}, u32[]{:S(2)}, u32[]{:S(2)}) collective-permute-start(bf16[2,10,64,768]{3,2,1,0:T(8,128)(2,1)} %get-tuple-element.160), channel_id=1, source_target_pairs={{0,8},{4,12},{8,0},{12,4},{16,24},{20,28},{24,16},{28,20},{1,9},{5... | collective-permute-start | bytes 5898248 | tf_op jit(solution)/shard_map/ppermute | solution.py:99
  1242.1 46.1 %collective-permute-start.84 = (bf16[2,10,64,768]{3,2,1,0:T(8,128)(2,1)}, bf16[2,10,64,768]{3,2,1,0:T(8,128)(2,1)}, u32[]{:S(2)}, u32[]{:S(2)}) collective-permute-start(bf16[2,10,64,768]{3,2,1,0:T(8,128)(2,1)} %get-tuple-element.162), channel_id=1, source_target_pairs={{0,16},{4,20},{8,24},{12,28},{16,0},{20,4},{24,8},{28,12},{1,17},{... | collective-permute-start | bytes 5898248 | tf_op jit(solution)/shard_map/ppermute | solution.py:99
  1244.0 152.3 %collective-permute-start.75 = (bf16[2,10,192,512]{3,2,1,0:T(8,128)(2,1)}, bf16[2,10,192,512]{3,2,1,0:T(8,128)(2,1)}, u32[]{:S(2)}, u32[]{:S(2)}) collective-permute-start(bf16[2,10,192,512]{3,2,1,0:T(8,128)(2,1)} %get-tuple-element.158), channel_id=1, source_target_pairs={{0,8},{4,12},{8,0},{12,4},{16,24},{20,28},{24,16},{28,20},{1,9},{5... | collective-permute-start | bytes 11796488 | tf_op jit(solution)/shard_map/ppermute | solution.py:99
  1251.5 149.7 %collective-permute-start.78 = (bf16[2,10,192,512]{3,2,1,0:T(8,128)(2,1)}, bf16[2,10,192,512]{3,2,1,0:T(8,128)(2,1)}, u32[]{:S(2)}, u32[]{:S(2)}) collective-permute-start(bf16[2,10,192,512]{3,2,1,0:T(8,128)(2,1)} %get-tuple-element.156), channel_id=1, source_target_pairs={{0,16},{4,20},{8,24},{12,28},{16,0},{20,4},{24,8},{28,12},{1,17},{... | collective-permute-start | bytes 11796488 | tf_op jit(solution)/shard_map/ppermute | solution.py:99
  1254.9 37.1 %collective-permute-start.54 = (bf16[512,1536]{1,0:T(8,128)(2,1)}, bf16[512,1536]{1,0:T(8,128)(2,1)}, u32[]{:S(2)}, u32[]{:S(2)}) collective-permute-start(bf16[512,1536]{1,0:T(8,128)(2,1)} %fusion.7), channel_id=1, source_target_pairs={{2,1},{3,2},{6,5},{7,6},{10,9},{11,10},{14,13},{15,14},{18,17},{19... | collective-permute-start | bytes 4718600 | tf_op jit(solution)/shard_map/ppermute | solution.py:79
  1281.8 109.9 %collective-permute-start.82 = (bf16[1,10,64,768]{3,2,1,0:T(8,128)(2,1)S(1)}, bf16[1,10,64,768]{3,2,1,0:T(8,128)(2,1)S(1)}, u32[]{:S(2)}, u32[]{:S(2)}) collective-permute-start(bf16[1,10,64,768]{3,2,1,0:T(8,128)(2,1)S(1)} %add_convert_fusion.24), channel_id=1, source_target_pairs={{0,16},{4,20},{8,24},{12,28},{16,0},{20,4},{24,8},{28,12},{1,17},{... | collective-permute-start | bytes 2949128 | tf_op jit(solution)/shard_map/ppermute | solution.py:99
  1289.7 104.9 %collective-permute-start.85 = (bf16[1,10,64,768]{3,2,1,0:T(8,128)(2,1)S(1)}, bf16[1,10,64,768]{3,2,1,0:T(8,128)(2,1)S(1)}, u32[]{:S(2)}, u32[]{:S(2)}) collective-permute-start(bf16[1,10,64,768]{3,2,1,0:T(8,128)(2,1)S(1)} %add_convert_fusion.22), channel_id=1, source_target_pairs={{0,8},{4,12},{8,0},{12,4},{16,24},{20,28},{24,16},{28,20},{1,9},{5... | collective-permute-start | bytes 2949128 | tf_op jit(solution)/shard_map/ppermute | solution.py:99
  1291.9 114.0 %collective-permute-start.52 = (bf16[512,1536]{1,0:T(8,128)(2,1)}, bf16[512,1536]{1,0:T(8,128)(2,1)S(1)}, u32[]{:S(2)}, u32[]{:S(2)}) collective-permute-start(bf16[512,1536]{1,0:T(8,128)(2,1)} %get-tuple-element.145), channel_id=1, source_target_pairs={{0,1},{1,2},{2,3},{4,5},{5,6},{6,7},{8,9},{9,10},{10,11},{12,13},{... | collective-permute-start | bytes 4718600 | tf_op jit(solution)/shard_map/ppermute | solution.py:78
  1391.7 37.6 %collective-permute-start.55 = (bf16[512,1536]{1,0:T(8,128)(2,1)S(1)}, bf16[512,1536]{1,0:T(8,128)(2,1)S(1)}, u32[]{:S(2)}, u32[]{:S(2)}) collective-permute-start(bf16[512,1536]{1,0:T(8,128)(2,1)S(1)} %add_convert_fusion.12), channel_id=1, source_target_pairs={{1,0},{2,1},{3,2},{5,4},{6,5},{7,6},{9,8},{10,9},{11,10},{13,12},{... | collective-permute-start | bytes 4718600 | tf_op jit(solution)/shard_map/ppermute | solution.py:79
  1399.4 43.2 %collective-permute-start.76 = (bf16[1,10,192,512]{3,2,1,0:T(8,128)(2,1)S(1)}, bf16[1,10,192,512]{3,2,1,0:T(8,128)(2,1)S(1)}, u32[]{:S(2)}, u32[]{:S(2)}) collective-permute-start(bf16[1,10,192,512]{3,2,1,0:T(8,128)(2,1)S(1)} %add_convert_fusion.10), channel_id=1, source_target_pairs={{0,16},{4,20},{8,24},{12,28},{16,0},{20,4},{24,8},{28,12},{1,17},{... | collective-permute-start | bytes 5898248 | tf_op jit(solution)/shard_map/ppermute | solution.py:99
  1403.3 43.4 %collective-permute-start.79 = (bf16[1,10,192,512]{3,2,1,0:T(8,128)(2,1)S(1)}, bf16[1,10,192,512]{3,2,1,0:T(8,128)(2,1)S(1)}, u32[]{:S(2)}, u32[]{:S(2)}) collective-permute-start(bf16[1,10,192,512]{3,2,1,0:T(8,128)(2,1)S(1)} %add_convert_fusion.8), channel_id=1, source_target_pairs={{0,8},{4,12},{8,0},{12,4},{16,24},{20,28},{24,16},{28,20},{1,9},{5... | collective-permute-start | bytes 5898248 | tf_op jit(solution)/shard_map/ppermute | solution.py:99
  (113 other events, 2250.1 us)
Sparse Core Ops, SparseCore 0:
  10.5 30.0 all-gather.6
  42.4 38.9 all-gather.8
  83.3 85.4 all-gather.10
  170.5 85.4 all-gather.12
  257.8 85.4 all-gather.14
  1157.8 46.9 all-reduce.1

commit v4 on v2

--- a/solution.py
+++ b/solution.py
@@ -57,37 +57,142 @@
     return jnp.min(open_ends, axis=1).astype(jnp.int32)
 
 
-def swiglu(gate_act, up_act):
-    return jax.nn.silu(gate_act) * up_act
+def tie(*groups):
+    return lax.optimization_barrier(groups)
+
+
+def line_move(right, left, k):
+    n = lax.axis_size("seq")
+    return (
+        lax.ppermute(right, "seq", [(i, i + 1) for i in range(k - 1, n - 1)]),
+        lax.ppermute(left, "seq", [(i, i - 1) for i in range(1, n - k + 1)]),
+    )
 
 
 def line_gather(block):
     n = lax.axis_size("seq")
-    me = lax.axis_index("seq")
     rights, lefts = [block], [block]
     for k in range(1, n):
-        rights.append(lax.ppermute(rights[-1], "seq", [(i, i + 1) for i in range(k - 1, n - 1)]))
-        lefts.append(lax.ppermute(lefts[-1], "seq", [(i, i - 1) for i in range(1, n - k + 1)]))
-    return [block] + [jnp.where(me >= k, rights[k], lefts[n - k]) for k in range(1, n)]
-
-
-def line_scatter(parts):
+        right, left = line_move(rights[-1], lefts[-1], k)
+        rights.append(right)
+        lefts.append(left)
+    return nearest(rights, lefts)
+
+
+def nearest(rights, lefts):
     n = lax.axis_size("seq")
-    right = left = None
-    for k in range(n - 1, 0, -1):
-        to_right, to_left = parts[n - k], parts[k]
-        if right is not None:
-            to_right = to_right + right.astype(full)
-            to_left = to_left + left.astype(full)
-        right = lax.ppermute(to_right.astype(low), "seq", [(i, i + 1) for i in range(n - k)])
-        left = lax.ppermute(to_left.astype(low), "seq", [(i, i - 1) for i in range(k, n)])
-    return parts[0] + (right.astype(full) + left.astype(full))
+    me = lax.axis_index("seq")
+    return [rights[0]] + [jnp.where(me >= k, rights[k], lefts[n - k]) for k in range(1, n)]
+
+
+def arrival_order(n):
+    order = []
+    for me in range(n):
+        both = min(me, n - 1 - me)
+        places = [me]
+        for k in range(1, n):
+            places += [me - k] if me >= k and (k <= both or me > n - 1 - me) else []
+            places += [me + k] if me + k < n and (k <= both or me < n - 1 - me) else []
+        order.append(places)
+    return order
+
+
+def arrived(rights, lefts, turn):
+    n = lax.axis_size("seq")
+    me = lax.axis_index("seq")
+    sources = {}
+    for dev, places in enumerate(arrival_order(n)):
+        gap = dev - places[turn]
+        sources.setdefault(gap, []).append(dev)
+    block = None
+    for gap, devs in sources.items():
+        moved = rights[gap] if gap >= 0 else lefts[-gap]
+        if block is None:
+            block = moved
+        else:
+            mine = jnp.array([dev in devs for dev in range(n)])[me]
+            block = jnp.where(mine, moved, block)
+    return block
+
+
+def at_place(placed, place):
+    return lax.dynamic_index_in_dim(placed, place % lax.axis_size("seq"), 0, keepdims=False)
+
+
+def line_send(parts, k, right, left):
+    me = lax.axis_index("seq")
+    to_right, to_left = at_place(parts, me + k), at_place(parts, me - k)
+    if right is not None:
+        to_right = (to_right.astype(full) + right.astype(full)).astype(low)
+        to_left = (to_left.astype(full) + left.astype(full)).astype(low)
+    return to_right, to_left
+
+
+def line_pass(to_right, to_left, k):
+    n = lax.axis_size("seq")
+    return (
+        lax.ppermute(to_right, "seq", [(i, i + 1) for i in range(n - k)]),
+        lax.ppermute(to_left, "seq", [(i, i - 1) for i in range(k, n)]),
+    )
+
+
+def line_end(parts, right, left):
+    own = at_place(parts, lax.axis_index("seq")).astype(full)
+    return own + (right.astype(full) + left.astype(full))
 
 
 def by_place(blocks):
     n = lax.axis_size("seq")
     me = lax.axis_index("seq")
-    return jnp.stack(blocks)[(me - jnp.arange(n)) % n]
+    placed = jnp.zeros((n,) + blocks[0].shape, blocks[0].dtype)
+    for k, block in enumerate(blocks):
+        placed = lax.dynamic_update_index_in_dim(placed, block, (me - k) % n, 0)
+    return placed
+
+
+def exchange(blocks):
+    n = lax.axis_size("seq")
+    me = lax.axis_index("seq")
+    rights, lefts = [at_place(blocks, me)], [at_place(blocks, me)]
+    for k in range(1, n):
+        to_right, to_left = at_place(blocks, me + k), at_place(blocks, me - k)
+        rights.append(lax.ppermute(to_right, "seq", [(i, i + k) for i in range(n - k)]))
+        lefts.append(lax.ppermute(to_left, "seq", [(i, i - k) for i in range(k, n)]))
+    return rights, lefts
+
+
+def swap(value, axis, bit):
+    return lax.ppermute(value, axis, [(i, i ^ bit) for i in range(lax.axis_size(axis))])
+
+
+def total(value, *axes):
+    for axis in axes:
+        for step in range(lax.axis_size(axis).bit_length() - 1):
+            value = value + swap(value, axis, 1 << step)
+    return value
+
+
+def fsdp_bits():
+    bits = [1 << step for step in range(lax.axis_size("fsdp").bit_length() - 1)]
+    return tuple(bits), tuple(bits[:1] + bits[:0:-1])
+
+
+def doubling_gather(block, bits):
+    blocks = block[None]
+    for bit in bits:
+        blocks = jnp.concatenate([blocks, swap(blocks, "fsdp", bit)])
+    return blocks
+
+
+def halve(keep, here):
+    half = keep.shape[0] // 2
+    if half == 0:
+        return keep[0].astype(full) + here[0].astype(full)
+    added = [
+        (keep[cut].astype(full) + here[cut].astype(full)).astype(low)
+        for cut in (slice(half, None), slice(0, half))
+    ]
+    return tuple(added)
 
 
 def nt(a, b):
@@ -95,6 +200,10 @@
 
 def nn(a, b):
     return lax.dot_general(a, b, (((1,), (0,)), ((), ())), preferred_element_type=full)
+
+def tn(a, b):
+    return lax.dot_general(a, b, (((0,), (0,)), ((), ())), preferred_element_type=full)
+
 
 def beside(ref):
     return jnp.concatenate([ref[0, h] for h in range(GROUP)], axis=1)
@@ -164,7 +273,7 @@
             jax.ShapeDtypeStruct((kv_here, GROUP, HEAD_DIM, seq_len), full),
             jax.ShapeDtypeStruct((kv_here, GROUP, 1, seq_len), full),
         ],
-        compiler_params=pltpu.CompilerParams(vmem_limit_bytes=40 * 2**20),
+        compiler_params=vmem(40),
         name="attention_forward",
     )(limit, qt, k_rows, vt)
 
@@ -240,9 +349,304 @@
             jax.ShapeDtypeStruct((kv_here, HEAD_DIM, seq_len), low),
         ],
         scratch_shapes=[pltpu.VMEM((HEAD_DIM, seq_len), full), pltpu.VMEM((HEAD_DIM, seq_len), full)],
-        compiler_params=pltpu.CompilerParams(vmem_limit_bytes=40 * 2**20),
+        compiler_params=vmem(40),
         name="attention_backward",
     )(limit, qt, k_rows, v_rows, kt, out, lse, d_out)
+
+
+def vmem(mib):
+    return pltpu.CompilerParams(vmem_limit_bytes=mib * 2**20)
+
+
+def own_row(ref, row):
+    return ref[pl.ds(row, 1), :]
+
+
+def experts_kernel(
+    at_ref, tok_ref, slot_ref, member_ref, router_ref, wg_ref, wu_ref, wd_ref, *refs
+):
+    part_ref, x_ref, g_ref, u_ref, gates_ref, acc, gates_all = refs[-7:]
+    e, experts = pl.program_id(0), pl.num_programs(0)
+    slots = x_ref.shape[2]
+
+    @pl.when(e == 0)
+    def _():
+        member = member_ref[...] > 0
+        chosen = jnp.where(member, nt(router_ref[...], tok_ref[...]), masked_score)
+        chosen = jnp.exp(chosen - jnp.max(chosen, axis=0, keepdims=True))
+        chosen = jnp.where(member, chosen, 0.0)
+        gates_all[...] = chosen / jnp.sum(chosen, axis=0, keepdims=True)
+        acc[...] = jnp.zeros_like(acc)
+
+    gate_row = own_row(gates_all, at_ref[1] * experts + e)
+    gates_ref[pl.ds(e, 1), :] = gate_row
+    place = lax.broadcasted_iota(jnp.int32, (slots, 1), 0)
+    here = place == own_row(slot_ref, e)
+    x = nn(jnp.where(here, 1.0, 0.0).astype(low), tok_ref[...]).astype(low)
+    x_ref[0, 0] = x
+    g = nn(x, wg_ref[0])
+    u = nn(x, wu_ref[0])
+    g_ref[0, 0] = g.astype(low)
+    u_ref[0, 0] = u.astype(low)
+    act = (g * jax.nn.sigmoid(g) * u).astype(low)
+    y = nn(act, wd_ref[0]).astype(low)
+    acc[...] += tn(jnp.where(here, gate_row, 0.0).astype(low), y)
+
+    @pl.when(e == experts - 1)
+    def _():
+        part_ref[0] = acc[...].astype(low)
+
+
+def back_kernel(
+    at_ref, tok_ref, slot_ref, gates_ref, mix_ref, router_ref, g_ref, u_ref, wg_ref, wu_ref, wd_ref, *refs
+):
+    part_ref, d_ref, dgu_ref, act_ref, dlog_ref, acc, dlog_all = refs[-7:]
+    e, experts = pl.program_id(0), pl.num_programs(0)
+    slots, hidden = g_ref.shape[2:]
+
+    @pl.when(e == 0)
+    def _():
+        dlog_all[...] = jnp.zeros_like(dlog_all)
+        acc[...] = jnp.zeros_like(acc)
+
+    place = lax.broadcasted_iota(jnp.int32, (slots, 1), 0)
+    here = place == own_row(slot_ref, e)
+    pick = jnp.where(here, 1.0, 0.0).astype(low)
+    gate_row = own_row(gates_ref, e)
+    gate = jnp.sum(jnp.where(here, gate_row, 0.0), axis=1, keepdims=True)
+    d = nn(pick, tok_ref[...]).astype(low)
+    d_ref[0, 0] = d
+    d_act = nt(d, wd_ref[0])
+    g, u = g_ref[0, 0].astype(full), u_ref[0, 0].astype(full)
+    sig = jax.nn.sigmoid(g)
+    silu = g * sig
+    act = silu * u
+    d_gate = jnp.sum(d_act * act, axis=1, keepdims=True)
+    d_gate = jnp.sum(jnp.where(here, d_gate, 0.0), axis=0, keepdims=True)
+    dlog_all[pl.ds(e, 1), :] = gate_row * (d_gate - mix_ref[...])
+    act_ref[0, 0] = (act * gate).astype(low)
+    d_act = d_act * gate
+    d_g = (d_act * u * (sig + silu * (1.0 - sig))).astype(low)
+    d_u = (d_act * silu).astype(low)
+    dgu_ref[0, 0, :, :hidden] = d_g
+    dgu_ref[0, 0, :, hidden:] = d_u
+    dx = (nt(d_g, wg_ref[0]) + nt(d_u, wu_ref[0])).astype(low)
+    acc[...] += tn(pick, dx)
+
+    @pl.when(e == experts - 1)
+    def _():
+        dlog = dlog_all[...].astype(low)
+        dlog_ref[...] = dlog
+        part_ref[0] = (acc[...] + tn(dlog, router_ref[...])).astype(low)
+
+
+def by_expert(*shape):
+    return pl.BlockSpec((1,) + shape, lambda e, at: (e, 0, 0))
+
+
+def in_turn(turn, *shape):
+    return pl.BlockSpec((1, 1) + shape, lambda e, at: (e, turn, 0, 0))
+
+
+def same(*shape):
+    return pl.BlockSpec(shape, lambda e, at: (0, 0))
+
+
+def in_place(*shape):
+    return pl.BlockSpec((1,) + shape, lambda e, at: (at[0], 0, 0))
+
+
+def shard_call(kernel, name, at, inputs, in_specs, out_specs, out_shape, buffers, scratch, experts):
+    first = len(inputs) + 1
+    aliases = {first + i: i for i in range(len(buffers))}
+    return pl.pallas_call(
+        kernel,
+        grid_spec=pltpu.PrefetchScalarGridSpec(
+            num_scalar_prefetch=1,
+            grid=(experts,),
+            in_specs=in_specs + [pl.BlockSpec(memory_space=pl.ANY)] * len(buffers),
+            out_specs=out_specs,
+            scratch_shapes=scratch,
+        ),
+        out_shape=out_shape,
+        input_output_aliases=aliases,
+        compiler_params=vmem(48),
+        name=name,
+    )(at, *inputs, *buffers)
+
+
+def experts_forward(turn, devs, at, tokens, slot_of, member, router, w_gate, w_up, w_down, slots, buffers):
+    experts, width, hidden = w_gate.shape
+    count = tokens.shape[0]
+    total_experts = member.shape[0]
+    return shard_call(
+        experts_kernel,
+        "experts_forward",
+        at,
+        [tokens, slot_of, member, router, w_gate, w_up, w_down],
+        [
+            same(count, width),
+            same(experts, count),
+            same(total_experts, count),
+            same(total_experts, width),
+            by_expert(width, hidden),
+            by_expert(width, hidden),
+            by_expert(hidden, width),
+        ],
+        [
+            in_place(count, width),
+            in_turn(turn, slots, width),
+            in_turn(turn, slots, hidden),
+            in_turn(turn, slots, hidden),
+            same(experts, count),
+        ],
+        [
+            jax.ShapeDtypeStruct((devs, count, width), low),
+            jax.ShapeDtypeStruct((experts, devs, slots, width), low),
+            jax.ShapeDtypeStruct((experts, devs, slots, hidden), low),
+            jax.ShapeDtypeStruct((experts, devs, slots, hidden), low),
+            jax.ShapeDtypeStruct((experts, count), full),
+        ],
+        buffers,
+        [pltpu.VMEM((count, width), full), pltpu.VMEM((total_experts, count), full)],
+        experts,
+    )
+
+
+def experts_backward(
+    turn, devs, at, d_tokens, slot_of, gates, mix_dot, router, g, u, w_gate, w_up, w_down, buffers
+):
+    experts, width, hidden = w_gate.shape
+    count = d_tokens.shape[0]
+    slots = g.shape[2]
+    lines = router.shape[0]
+    return shard_call(
+        back_kernel,
+        "experts_backward",
+        at,
+        [d_tokens, slot_of, gates, mix_dot, router, g, u, w_gate, w_up, w_down],
+        [
+            same(count, width),
+            same(experts, count),
+            same(experts, count),
+            same(1, count),
+            same(lines, width),
+            in_turn(turn, slots, hidden),
+            in_turn(turn, slots, hidden),
+            by_expert(width, hidden),
+            by_expert(width, hidden),
+            by_expert(hidden, width),
+        ],
+        [
+            in_place(count, width),
+            in_turn(turn, slots, width),
+            in_turn(turn, slots, 2 * hidden),
+            in_turn(turn, slots, hidden),
+            same(lines, count),
+        ],
+        [
+            jax.ShapeDtypeStruct((devs, count, width), low),
+            jax.ShapeDtypeStruct((experts, devs, slots, width), low),
+            jax.ShapeDtypeStruct((experts, devs, slots, 2 * hidden), low),
+            jax.ShapeDtypeStruct((experts, devs, slots, hidden), low),
+            jax.ShapeDtypeStruct((lines, count), low),
+        ],
+        buffers,
+        [pltpu.VMEM((count, width), full), pltpu.VMEM((lines, count), full)],
+        experts,
+    )
+
+
+def halving_masks(bits):
+    masks = [0]
+    for bit in reversed(bits):
+        masks = masks + [mask ^ bit for mask in masks]
+    return masks
+
+
+def gate_up_kernel(bits_a, bits_b, me_ref, x_ref, dgu_ref, *refs):
+    outs, acc = refs[:4], refs[4]
+    hidden = outs[0].shape[3]
+    acc[...] = tn(x_ref[0], dgu_ref[0])
+    for part, bits in enumerate((bits_a, bits_b)):
+        keep, send = outs[2 * part], outs[2 * part + 1]
+        rows = keep.shape[2]
+        for place, mask in enumerate(halving_masks(bits)):
+            start = pl.multiple_of((me_ref[0] ^ mask) * rows, rows)
+            out = keep if place < keep.shape[0] else send
+            block = acc[pl.ds(start, rows), part * hidden : (part + 1) * hidden]
+            out[place % keep.shape[0], 0] = block.astype(low)
+
+
+def gate_up_grads(me, rows, d_gu, bits_a, bits_b):
+    experts, count, width = rows.shape
+    hidden = d_gu.shape[2] // 2
+    devs = 2 ** len(bits_a)
+    shape = (width // devs, hidden)
+    outs = pl.pallas_call(
+        functools.partial(gate_up_kernel, bits_a, bits_b),
+        grid_spec=pltpu.PrefetchScalarGridSpec(
+            num_scalar_prefetch=1,
+            grid=(experts,),
+            in_specs=[by_expert(count, width), by_expert(count, 2 * hidden)],
+            out_specs=[pl.BlockSpec((devs // 2, 1) + shape, lambda e, me: (0, e, 0, 0))] * 4,
+            scratch_shapes=[pltpu.VMEM((width, 2 * hidden), full)],
+        ),
+        out_shape=[jax.ShapeDtypeStruct((devs // 2, experts) + shape, low)] * 4,
+        compiler_params=vmem(48),
+        name="gate_up_grads",
+    )(me, rows, d_gu)
+    return (outs[0], outs[1]), (outs[2], outs[3])
+
+
+def down_kernel(act_ref, d_ref, out_ref):
+    out_ref[0] = tn(act_ref[0], d_ref[0]).astype(low)
+
+
+def down_grads(act, d_rows):
+    experts, count, hidden = act.shape
+    width = d_rows.shape[2]
+    one = lambda *shape: pl.BlockSpec((1,) + shape, lambda e: (e, 0, 0))
+    return pl.pallas_call(
+        down_kernel,
+        grid=(experts,),
+        in_specs=[one(count, hidden), one(count, width)],
+        out_specs=one(hidden, width),
+        out_shape=jax.ShapeDtypeStruct((experts, hidden, width), low),
+        compiler_params=vmem(48),
+        name="down_grads",
+    )(act, d_rows)
+
+
+def join_kernel(me_ref, left_ref, right_ref, out_ref):
+    half = left_ref.shape[3]
+    out_ref[:, :, :half] = left_ref[0]
+    out_ref[:, :, half:] = right_ref[0]
+
+
+def join_rows(me, left, right, bits_left, bits_right):
+    devs, experts, rows, half = left.shape
+
+    def place(bits):
+        def index(block, me_ref):
+            mask = me_ref[0] ^ block
+            spot = sum(((mask // bit) % 2) * 2**i for i, bit in enumerate(bits))
+            return (spot, 0, 0, 0)
+
+        return pl.BlockSpec((1, experts, rows, half), index)
+
+    return pl.pallas_call(
+        join_kernel,
+        grid_spec=pltpu.PrefetchScalarGridSpec(
+            num_scalar_prefetch=1,
+            grid=(devs,),
+            in_specs=[place(bits_left), place(bits_right)],
+            out_specs=pl.BlockSpec((experts, rows, 2 * half), lambda block, me_ref: (0, block, 0)),
+        ),
+        out_shape=jax.ShapeDtypeStruct((experts, devs * rows, 2 * half), low),
+        compiler_params=vmem(40),
+        name="join_rows",
+    )(me, left, right)
 
 
 def shards(
@@ -260,52 +664,61 @@
     w_up,
     w_down,
 ):
-    seq_devs = lax.axis_size("seq")
+    n = lax.axis_size("seq")
     me = lax.axis_index("seq")
+    mine = lax.axis_index("fsdp")
     seqs_here, shard_len, width = inputs.shape
     assert seqs_here == 1
-    seq_len = shard_len * seq_devs
+    seq_len = shard_len * n
     tokens_all = lax.axis_size("fsdp") * seq_len
-    kv_here = KV_HEADS // seq_devs
+    kv_here = KV_HEADS // n
     heads_w = kv_here * GROUP * HEAD_DIM
     group_w = kv_here * (GROUP + 2) * HEAD_DIM
     experts_here = w_gate.shape[0]
-    expert_total = experts_here * seq_devs
+    expert_total = experts_here * n
     top_count = routes.shape[2]
     capacity = 3 * shard_len * top_count // (2 * expert_total)
     slots = -(-capacity // 16) * 16
+    slot_rows = n * slots
+    order_a, order_b = fsdp_bits()
+    order = jnp.array(arrival_order(n), jnp.int32)[me]
     x_low = inputs.reshape(shard_len, width)
 
     own_qkv = lax.dynamic_slice_in_dim(w_qkv, me * group_w, group_w, 1)
-    small = jnp.concatenate(
-        [gain_one[:, None], gain_two[:, None], w_router], axis=1
-    )
-    small = lax.all_gather(small, "fsdp", axis=0, tiled=True)
+    small = jnp.concatenate([gain_one[:, None], gain_two[:, None], w_router], axis=1)
+    small = doubling_gather(small, order_a)
+    small = small[mine ^ jnp.arange(small.shape[0])].reshape(width, 2 + expert_total)
     full_qkv = lax.all_gather(own_qkv, "fsdp", axis=0, tiled=True)
     full_out = lax.all_gather(w_out, "fsdp", axis=0, tiled=True)
     full_gate = lax.all_gather(w_gate, "fsdp", axis=1, tiled=True)
     full_up = lax.all_gather(w_up, "fsdp", axis=1, tiled=True)
-    full_down = lax.all_gather(w_down, "fsdp", axis=1, tiled=True)
+    down_a, down_b = order_a[1:] + order_a[:1], order_b[1:] + order_b[:1]
+    full_down = join_rows(
+        mine.reshape(1),
+        doubling_gather(w_down[:, :, : width // 2], down_a),
+        doubling_gather(w_down[:, :, width // 2 :], down_b),
+        down_a,
+        down_b,
+    )
     full_g1 = small[:, 0].astype(full)
     full_g2 = small[:, 1].astype(full)
-    full_router = small[:, 2:]
+    router = small[:, 2:].T
+    own_router = lax.dynamic_slice_in_dim(router, me * experts_here, experts_here, 0)
+    own_router = jnp.pad(own_router, ((0, -experts_here % 16), (0, 0)))
     valid_rows = valid_mask.reshape(shard_len).astype(full)
-    valid_count = lax.psum(jnp.sum(valid_rows), ("fsdp", "seq"))
-
-    routes_rel = jnp.stack(line_gather(routes.reshape(shard_len, top_count).T))
-    routes_rel = jnp.swapaxes(routes_rel, 1, 2)
+
+    routes_low = jnp.concatenate([routes.reshape(shard_len, top_count).T, valid_mask], axis=0)
+    routes_all = by_place(line_gather(routes_low))[order]
+    valid_count = total(jnp.sum(routes_all[:, top_count]).astype(full).reshape(1, 1), "fsdp")[0, 0]
     expert_ids = jnp.arange(expert_total, dtype=jnp.int32)
-    member = jnp.any(routes_rel[:, :, :, None] == expert_ids, axis=2)
-    own_member = lax.dynamic_slice_in_dim(member, me * experts_here, experts_here, 2)
-    own_member = jnp.transpose(own_member, (2, 0, 1)).astype(low)
+    member = jnp.any(routes_all[:, :top_count, None, :] == expert_ids[:, None], axis=1)
+    own_member = lax.dynamic_slice_in_dim(member, me * experts_here, experts_here, 1)
     earlier = jnp.arange(shard_len)[:, None] < jnp.arange(shard_len)[None, :]
-    slot_of = dot("ent,tu->enu", own_member, earlier.astype(low)).astype(jnp.int32)
-    slot_of = jnp.where(own_member > 0, slot_of, -1)
-    onehot = slot_of[:, :, None, :] == jnp.arange(slots, dtype=jnp.int32)[None, None, :, None]
-    pick = onehot.astype(low)
+    slot_of = dot("net,tu->neu", own_member.astype(low), earlier.astype(low)).astype(jnp.int32)
+    slot_of = jnp.where(own_member, slot_of, -1)
+    member = member.astype(full)
 
     x_all = by_place(line_gather(x_low)).reshape(seq_len, width)
-    x_all, valid_count = lax.optimization_barrier((x_all, valid_count))
     normed_one = rms_norm(x_all.astype(full), full_g1).astype(low)
     qkv_rows = dot("td,dc->ct", normed_one, full_qkv)
     qkv_rows = qkv_rows.reshape(kv_here, GROUP + 2, HEAD_DIM, seq_len)
@@ -319,32 +732,35 @@
     value_rows = jnp.swapaxes(value, 1, 2)
     limit = block_limits(block_lengths[0], positions)[None]
     attended, out_heads, lse = attention_forward(query, key_rows, value, limit, shard_len)
-    attn_rows = lax.all_to_all(attended, "seq", split_axis=0, concat_axis=0, tiled=True)
-    attn_rows = attn_rows.reshape(HEADS * HEAD_DIM, shard_len)
+    moved = exchange(attended)
+    moved, slot_of, member, own_router = tie(moved, slot_of, member, own_router)
+    attn_rows = by_place(nearest(*moved)).reshape(HEADS * HEAD_DIM, shard_len)
     projected = dot("kt,kd->td", attn_rows, full_out)
     hidden = x_low.astype(full) + resid_mult * projected
     normed_two, norm_two_pull = jax.vjp(rms_norm, hidden, full_g2)
 
-    tokens = jnp.stack(line_gather(normed_two.astype(low)))
-    logits = dot("ntd,de->nte", tokens, full_router)
-    chosen = jnp.where(member, logits, masked_score)
-    gate_exp = jnp.where(member, jnp.exp(chosen - jnp.max(chosen, axis=2, keepdims=True)), 0.0)
-    gates = gate_exp / jnp.sum(gate_exp, axis=2, keepdims=True)
-    own_gates = lax.dynamic_slice_in_dim(gates, me * experts_here, experts_here, 2)
-    slot_gates = jnp.sum(
-        onehot.astype(full) * jnp.transpose(own_gates, (2, 0, 1))[:, :, None, :], axis=3
-    )
-    expert_in = dot("enct,ntd->encd", pick, tokens).astype(low)
-    expert_in = expert_in.reshape(experts_here, seq_devs * slots, width)
-    gate_act = dot("erd,edf->erf", expert_in, full_gate)
-    up_act = dot("erd,edf->erf", expert_in, full_up)
-    act_out, act_pull = jax.vjp(swiglu, gate_act, up_act)
-    act_low = act_out.astype(low)
-    expert_out = dot("erf,efd->erd", act_low, full_down).astype(low)
-    expert_out = expert_out.reshape(experts_here, seq_devs, slots, width)
-    gated_pick = pick * slot_gates.astype(low)[..., None]
-    mix_parts = dot("enct,encd->ntd", gated_pick, expert_out)
-    mixture = line_scatter([mix_parts[k] for k in range(seq_devs)])
+    tokens = [normed_two.astype(low)]
+    rights, lefts = [tokens[0]], [tokens[0]]
+    buffers, gates = [], []
+    for turn in range(n):
+        if turn < n - 1:
+            right, left, tokens[turn] = tie(rights[turn], lefts[turn], tokens[turn])
+            right, left = line_move(right, left, turn + 1)
+        *buffers, shard_gates = experts_forward(
+            turn, n, jnp.stack([order[turn], me]), tokens[turn], slot_of[turn], member[turn],
+            router, full_gate, full_up, full_down, slots, buffers,
+        )
+        if turn < n - 1:
+            right, left, shard_gates = tie(right, left, shard_gates)
+            rights.append(right)
+            lefts.append(left)
+            tokens.append(arrived(rights, lefts, turn + 1))
+        gates.append(shard_gates)
+    mix_parts, expert_in, gate_act, up_act = buffers
+    right = left = None
+    for k in range(n - 1, 0, -1):
+        right, left = line_pass(*line_send(mix_parts, k, right, left), k)
+    mixture = line_end(mix_parts, right, left)
     output_f32 = hidden + resid_mult * mixture
     activations = output_f32.astype(low).reshape(1, shard_len, width)
     error_rows = output_f32 - teacher.astype(full).reshape(shard_len, width)
@@ -353,86 +769,138 @@
     d_out = weighted * (tokens_all / valid_count)
 
     d_mix = resid_mult * d_out
-    mix_dot = jnp.stack(line_gather(jnp.sum(d_mix * mixture, axis=1)))
-    d_tokens = jnp.stack(line_gather(d_mix.astype(low)))
-    d_rows = dot("enct,ntd->encd", pick, d_tokens).astype(low)
-    d_rows = d_rows.reshape(experts_here, seq_devs * slots, width)
-    d_act_raw = dot("erd,efd->erf", d_rows, full_down)
-    row_gates = slot_gates.reshape(experts_here, seq_devs * slots, 1)
-    d_slot_gates = jnp.sum(d_act_raw * act_low.astype(full), axis=2)
-    down_part = dot("erf,erd->efd", (act_low.astype(full) * row_gates).astype(low), d_rows)
-    d_gate_act, d_up_act = act_pull(d_act_raw * row_gates)
-    d_gate_low = d_gate_act.astype(low)
-    d_up_low = d_up_act.astype(low)
-    gate_part = dot("erd,erf->edf", expert_in, d_gate_low)
-    up_part = dot("erd,erf->edf", expert_in, d_up_low)
-    d_expert_in = dot("erf,edf->erd", d_gate_low, full_gate)
-    d_expert_in = (d_expert_in + dot("erf,edf->erd", d_up_low, full_up)).astype(low)
-    d_expert_in = d_expert_in.reshape(experts_here, seq_devs, slots, width)
-    d_gates = jnp.sum(
-        onehot.astype(full)
-        * d_slot_gates.reshape(experts_here, seq_devs, slots)[..., None],
-        axis=2,
-    )
-    d_gates = jnp.transpose(d_gates, (1, 2, 0))
-    d_logits = (own_gates * (d_gates - mix_dot[:, :, None])).astype(low)
-    own_router = lax.dynamic_slice_in_dim(full_router, me * experts_here, experts_here, 1)
-    d_normed_parts = dot("enct,encd->ntd", pick, d_expert_in) + dot(
-        "nte,de->ntd", d_logits, own_router
-    )
-    router_part = dot("ntd,nte->de", tokens, d_logits)
-    d_normed_two = line_scatter([d_normed_parts[k] for k in range(seq_devs)])
-    d_normed_two, gate_part, up_part, down_part = lax.optimization_barrier(
-        (d_normed_two, gate_part.astype(low), up_part.astype(low), down_part.astype(low))
-    )
-    gate_part, up_part, down_part = (
-        lax.psum_scatter(part, "fsdp", scatter_dimension=1, tiled=True)
-        for part in (gate_part, up_part, down_part)
-    )
+    d_tokens = d_mix.astype(low)
+    mix_dot = jnp.sum(d_mix * mixture, axis=1)[None]
+    rights, lefts = [d_tokens], [d_tokens]
+    dot_rights, dot_lefts = [mix_dot], [mix_dot]
+    buffers, d_logits = [], []
+    for turn in range(n):
+        if turn < n - 1:
+            (right, left), (dot_right, dot_left), d_tokens = tie(
+                (rights[turn], lefts[turn]), (dot_rights[turn], dot_lefts[turn]), d_tokens
+            )
+            dot_right, dot_left = line_move(dot_right, dot_left, turn + 1)
+            right, left = line_move(right, left, turn + 1)
+        *buffers, shard_logits = experts_backward(
+            turn, n, jnp.stack([order[turn], me]), d_tokens, slot_of[turn], gates[turn], mix_dot,
+            own_router, gate_act, up_act, full_gate, full_up, full_down, buffers,
+        )
+        if turn < n - 1:
+            right, left, dot_right, dot_left, shard_logits = tie(
+                right, left, dot_right, dot_left, shard_logits
+            )
+            rights.append(right)
+            lefts.append(left)
+            dot_rights.append(dot_right)
+            dot_lefts.append(dot_left)
+            d_tokens = arrived(rights, lefts, turn + 1)
+            mix_dot = arrived(dot_rights, dot_lefts, turn + 1)
+        d_logits.append(shard_logits)
+    d_parts, d_rows, d_gate_up, act_low = buffers
+    expert_in = expert_in.reshape(experts_here, slot_rows, width)
+    d_rows = d_rows.reshape(experts_here, slot_rows, width)
+    d_gate_up = d_gate_up.reshape(experts_here, slot_rows, -1)
+    act_low = act_low.reshape(experts_here, slot_rows, -1)
+
+    right = left = None
+    for k in range(n - 1, 0, -1):
+        moving = line_send(d_parts, k, right, left)
+        if k == n - 1:
+            moving, expert_in, d_gate_up = tie(moving, expert_in, d_gate_up)
+            right, left = line_pass(*moving, k)
+            gate_pair, up_pair = gate_up_grads(
+                mine.reshape(1), expert_in, d_gate_up, order_a, order_b
+            )
+            right, left, gate_pair, up_pair = tie(right, left, gate_pair, up_pair)
+        elif k == n - 2:
+            moving, gate_pair, up_pair, act_low, d_rows = tie(
+                moving, gate_pair, up_pair, act_low, d_rows
+            )
+            right, left = line_pass(*moving, k)
+            gate_here = swap(gate_pair[1], "fsdp", order_a[0])
+            up_here = swap(up_pair[1], "fsdp", order_b[0])
+            down_part = down_grads(act_low, d_rows)
+            right, left, gate_here, up_here, down_part = tie(
+                right, left, gate_here, up_here, down_part
+            )
+        elif k == n - 3:
+            moving, gate_here, up_here = tie(moving, gate_here, up_here)
+            right, left = line_pass(*moving, k)
+            gate_send, gate_keep = halve(gate_pair[0], gate_here)
+            up_send, up_keep = halve(up_pair[0], up_here)
+            right, left, gate_send, up_send = tie(right, left, gate_send, up_send)
+        else:
+            right, left = line_pass(*moving, k)
+    d_normed_two = line_end(d_parts, right, left)
+    down_sum = lax.psum_scatter(down_part, "fsdp", scatter_dimension=1, tiled=True)
 
     d_hidden_norm, gain_two_part = norm_two_pull(d_normed_two)
     d_hidden = d_out + d_hidden_norm
     d_proj = (resid_mult * d_hidden).astype(low)
     d_attended = dot("kd,td->kt", full_out, d_proj).astype(low)
-    d_heads = lax.all_to_all(
-        d_attended.reshape(seq_devs, heads_w, shard_len), "seq", split_axis=0, concat_axis=0, tiled=True
-    )
+    d_attended, gate_send, up_send = tie(d_attended, gate_send, up_send)
+    moved = exchange(d_attended.reshape(n, heads_w, shard_len))
+    gate_here = swap(gate_send, "fsdp", order_a[1])
+    up_here = swap(up_send, "fsdp", order_b[1])
     out_part = dot("kt,td->kd", attn_rows, d_proj).astype(low)
+    router_part = sum(
+        dot("td,et->de", shard, shard_logits[:experts_here])
+        for shard, shard_logits in zip(tokens, d_logits)
+    )
+    moved, out_part, router_part = tie(moved, out_part, router_part)
+    d_heads = by_place(nearest(*moved))
     query_grad, key_grad, value_grad = attention_backward(
         query, key_rows, value_rows, key, limit, out_heads, lse, d_heads
+    )
+    (query_grad, key_grad, value_grad), gate_here, up_here = tie(
+        (query_grad, key_grad, value_grad), gate_here, up_here
     )
     d_turned = jnp.concatenate([query_grad, key_grad[:, None]], axis=1).astype(full)
     d_turned = rotate(d_turned, cosine, -sine_vals).astype(low)
     d_qkv = jnp.concatenate([d_turned, value_grad[:, None]], axis=1).reshape(group_w, seq_len)
+    d_parts = dot("ct,dc->td", d_qkv, full_qkv).astype(low).reshape(n, shard_len, width)
+    moving = line_send(d_parts, n - 1, None, None)
+    moving, d_qkv, gate_here, up_here = tie(moving, d_qkv, gate_here, up_here)
+    right, left = line_pass(*moving, n - 1)
     qkv_part = dot("td,ct->dc", normed_one, d_qkv).astype(low)
-    d_normed_parts = dot("ct,dc->td", d_qkv, full_qkv).reshape(seq_devs, shard_len, width)
-    d_normed_parts = d_normed_parts[(me - jnp.arange(seq_devs)) % seq_devs]
-    d_normed_one = line_scatter([d_normed_parts[k] for k in range(seq_devs)])
-    x_rows = x_low.astype(full)
-    _, norm_one_pull = jax.vjp(lambda v: rms_norm(v, full_g1), x_rows)
+    qkv_sum = lax.psum_scatter(qkv_part, "fsdp", scatter_dimension=0, tiled=True)
+    gate_send, gate_keep = halve(gate_keep, gate_here)
+    up_send, up_keep = halve(up_keep, up_here)
+    right, left, qkv_part, gate_send, up_send = tie(right, left, qkv_part, gate_send, up_send)
+    gate_here = swap(gate_send, "fsdp", order_a[2])
+    up_here = swap(up_send, "fsdp", order_b[2])
+    for k in range(n - 2, 0, -1):
+        right, left = line_pass(*line_send(d_parts, k, right, left), k)
+    d_normed_one = line_end(d_parts, right, left)
+    _, norm_one_pull = jax.vjp(lambda v: rms_norm(v, full_g1), x_low.astype(full))
     input_grad = (d_hidden + norm_one_pull(d_normed_one)[0]).reshape(1, shard_len, width)
 
-    def rows_sum(part):
-        return lax.psum_scatter(part, "fsdp", scatter_dimension=0, tiled=True)
-
-    gate_grad = gate_part.astype(full)
-    up_grad = up_part.astype(full)
-    down_grad = down_part.astype(full)
+    input_grad, gate_here, up_here, down_sum, qkv_sum = tie(
+        input_grad, gate_here, up_here, down_sum, qkv_sum
+    )
+    for bit_a, bit_b in zip(order_a[3:], order_b[3:]):
+        gate_send, gate_keep = halve(gate_keep, gate_here)
+        up_send, up_keep = halve(up_keep, up_here)
+        gate_here = swap(gate_send, "fsdp", bit_a)
+        up_here = swap(up_send, "fsdp", bit_b)
+    gate_grad = halve(gate_keep, gate_here)
+    up_grad = halve(up_keep, up_here)
+    down_grad = down_sum.astype(full)
     own_columns = jnp.zeros((width, expert_total), full)
-    own_columns = lax.dynamic_update_slice_in_dim(
-        own_columns, router_part, me * experts_here, 1
-    )
-    dense_part = jnp.concatenate(
-        [out_part, own_columns.astype(low), gain_two_part[:, None].astype(low)], axis=1
-    )
-    dense_part = lax.psum(rows_sum(dense_part), "seq").astype(full)
-    out_grad = dense_part[:, :width]
-    router_grad = dense_part[:, width : width + expert_total]
-    gain_two_grad = dense_part[:, width + expert_total]
-    qkv_grad = lax.all_gather(rows_sum(qkv_part), "seq", axis=1, tiled=True).astype(full)
+    own_columns = lax.dynamic_update_slice_in_dim(own_columns, router_part, me * experts_here, 1)
+    rest = jnp.concatenate([own_columns.astype(low), gain_two_part[:, None].astype(low)], axis=1)
+    dense = [
+        lax.psum_scatter(part, "fsdp", scatter_dimension=0, tiled=True) for part in (out_part, rest)
+    ]
+    out_sum, rest = lax.psum(dense, "seq")
+    out_grad = out_sum.astype(full)
+    router_grad = rest[:, :expert_total].astype(full)
+    gain_two_grad = rest[:, expert_total].astype(full)
+    qkv_grad = by_place(line_gather(qkv_sum))
+    qkv_grad = jnp.swapaxes(qkv_grad, 0, 1).reshape(-1, QKV_W).astype(full)
     gain_one_grad = jnp.sum(qkv_grad * w_qkv.astype(full), axis=1) / gain_one.astype(full)
-    squares, input_grad = lax.optimization_barrier((squares, input_grad))
-    loss_value = lax.psum(squares, ("fsdp", "seq")) / (valid_count * width)
+    squares = total(squares.reshape(1, 1), "seq", "fsdp")[0, 0]
+    loss_value = squares / (valid_count * width)
     return (
         activations,
         loss_value,

time: 1670 us -> 1380 us (0.83)
  matrix products: 345 us -> 32.7 us
  Pallas kernels: 96.2 us -> 394 us
  blocking collectives: 211 us -> 21.8 us
  waiting for transfers between devices: 643 us -> 456 us
  starting transfers between devices: 136 us -> 222 us
  other arithmetic: 101 us -> 155 us
  local copies, waits for them, and re-layouts: 110 us -> 61.9 us
    dot_general x23 -> x11, matrix products: 345 us -> 32.7 us  [dot(): return jnp.einsum(spec, left, right, preferred_element_type=full)]
    pallas_call x0 -> x11, Pallas kernels: none -> 300 us  [the longest x8 235 us: shard_call(): pl.pallas_call(kernel, grid_spec=pltpu.PrefetchScalarGridSpec(num_scalar_...]
    reduce_scatter x4 -> x3, waiting for transfers between devices: 212 us -> 0.03 us  [the longest x1 0.02 us: shards(): lax.psum_scatter(down_part, 'fsdp', scatter_dimension=1, tiled=True)]
    psum x2 -> x1, blocking collectives: 128 us -> 21.8 us  [shards(): out_sum, rest = lax.psum(dense, 'seq')]
    ppermute x48 -> x89, starting transfers between devices: 131 us -> 222 us  [the longest x23 65.2 us: swap(): lax.ppermute(value, axis, [(i, i ^ bit) for i in range(lax.axis_size(axis...]
    convert_element_type x6 -> x0, local copies, waits for them, and re-layouts: 44.3 us -> none  [the longest x1 16.4 us: shards(): d_rows = dot('enct,ntd->encd', pick, d_tokens).astype(low)]
    all_gather x2 -> x0, blocking collectives: 43 us -> none  [the longest x1 32.2 us: shards(): lax.all_gather(rows_sum(qkv_part), 'seq', axis=1, tiled=True).astype(full)]
    all_to_all x1 -> x0, blocking collectives: 40.2 us -> none  [shards(): lax.all_to_all(attended, 'seq', split_axis=0, concat_axis=0, tiled=True)]
  transfers between devices with their start and end apart: 60 -> 98, of which waited for: 26 -> 37; matrix products, arithmetic and copies ran while one was open for 17% -> 13% of each run, Pallas kernels for 6% -> 25%
where the time goes in v4:
time: 1380 us; the launch traced here: 1370 us
  waiting for transfers between devices  456 us (33%)
  Pallas kernels  394 us (29%)
  starting transfers between devices  222 us (16%)
  other arithmetic  155 us (11%)
  local copies, waits for them, and re-layouts  61.9 us (4%)
  matrix products  32.7 us (2%)
  between operations  24.5 us (2%)
  blocking collectives  21.8 us (2%)
    pallas_call x8, Pallas kernels, shard_call(): pl.pallas_call(kernel, grid_spec=pltpu.PrefetchScalarGridSpec(num_scalar_...  235 us
    ppermute x9, waiting for transfers between devices, line_pass(): lax.ppermute(to_right, 'seq', [(i, i + 1) for i in range(n - k)])  156 us
    ppermute x23, waiting for transfers between devices, swap(): lax.ppermute(value, axis, [(i, i ^ bit) for i in range(lax.axis_size(axis...  113 us
    ppermute x18, waiting for transfers between devices, line_move(): lax.ppermute(left, 'seq', [(i, i - 1) for i in range(1, n - k + 1)])  72.5 us
    ppermute x23, starting transfers between devices, swap(): lax.ppermute(value, axis, [(i, i ^ bit) for i in range(lax.axis_size(axis...  65.2 us
    pallas_call x1, Pallas kernels, attention_backward(): pl.pallas_call(functools.partial(backward_kernel, seq_len, query_rows, ke...  54.3 us
    ppermute x9, starting transfers between devices, line_pass(): lax.ppermute(to_right, 'seq', [(i, i + 1) for i in range(n - k)])  52.8 us
    ppermute x18, starting transfers between devices, line_move(): lax.ppermute(right, 'seq', [(i, i + 1) for i in range(k - 1, n - 1)])  40.9 us
  transfers between devices with their start and end apart: 98, of which 37 were waited for; matrix products, arithmetic and copies ran while one was open for 13% of the time, Pallas kernels for 25%

profile of v4, /device:TPU:0, one launch (start us, length us, event | category | flops | bytes accessed | tf_op | source)
XLA Modules:
  0.0 1368.7 jit_solution(6233375406098138485)
XLA Ops:
  12.4 6.7 collective-permute-start
  27.5 23.2 %collective-permute-done.1 = bf16[512,1536]{1,0:T(8,128)(2,1)} collective-permute-done((bf16[512,1536]{1,0:T(8,128)(2,1)}, bf16[512,1536]{1,0:T(8,128)(2,1)}, u32[]{:S(2)}, u32[]{:S(2)}) %collective-permute-start.1) | collective-permute-done | bytes 1572896 | tf_op jit(solution)/shard_map/ppermute | solution.py:68
  66.7 22.5 %collective-permute-done.16 = s32[9,512]{1,0:T(8,128)} collective-permute-done((s32[9,512]{1,0:T(8,128)}, s32[9,512]{1,0:T(8,128)}, u32[]{:S(2)}, u32[]{:S(2)}) %collective-permute-start.16) | collective-permute-done | bytes 18464 | tf_op jit(solution)/shard_map/ppermute | solution.py:68
  96.0 30.2 %collective-permute-done.7 = bf16[2,192,42]{1,2,0:T(8,128)(2,1)S(1)} collective-permute-done((bf16[2,192,42]{1,2,0:T(8,128)(2,1)S(1)}, bf16[2,192,42]{1,2,0:T(8,128)(2,1)S(1)}, u32[]{:S(2)}, u32[]{:S(2)}) %collective-permute-start.7) | collective-permute-done | bytes 32288 | tf_op jit(solution)/shard_map/ppermute | solution.py:165
  147.6 16.9 %collective-permute-done.23 = bf16[1,10,64,768]{3,2,1,0:T(8,128)(2,1)} collective-permute-done((bf16[1,10,64,768]{3,2,1,0:T(8,128)(2,1)S(1)}, bf16[1,10,64,768]{3,2,1,0:T(8,128)(2,1)}, u32[]{:S(2)}, u32[]{:S(2)}) %collective-permute-start.23) | collective-permute-done | bytes 983072 | tf_op jit(solution)/shard_map/ppermute | solution.py:165
  202.1 39.7 %attention_forward.1 = (bf16[4,384,512]{2,1,0:T(8,128)(2,1)S(1)}, f32[2,3,64,2048]{3,2,1,0:T(8,128)S(1)}, f32[2,3,1,2048]{3,2,1,0:T(1,128)S(1)}) custom-call(s32[1,2048]{1,0:T(1,128)S(1)} %bitcast.275, bf16[2,3,64,2048]{3,2,1,0:T(8,128)(2,1)S(1)} %copy.160.q_ref, bf16[2,2048,64]{2,1,0:T(8,128)(2,1)S(1)} %copy.161.k_ref, ...), custom_call_target="tpu_custom_call" | custom-call | tf_op jit(solution)/shard_map/attention_forward/pallas_call | solution.py:257
  246.4 7.7 collective-permute-start.11
  259.4 15.1 %collective-permute-done.13 = bf16[384,512]{1,0:T(8,128)(2,1)S(1)} collective-permute-done((bf16[384,512]{1,0:T(8,128)(2,1)S(1)}, bf16[384,512]{1,0:T(8,128)(2,1)S(1)}, u32[]{:S(2)}, u32[]{:S(2)}) %collective-permute-start.13) | collective-permute-done | bytes 393248 | tf_op jit(solution)/shard_map/ppermute | solution.py:160
  286.5 6.5 multiply_reduce_fusion.4
  294.7 8.4 collective-permute-start.21
  304.4 6.4 pad_maximum_fusion.1.right_ref
  314.7 10.1 join_rows.1.wd_ref
  331.9 26.7 %experts_forward.4 = (bf16[4,512,1536]{2,1,0:T(8,128)(2,1)}, bf16[10,4,160,1536]{3,2,1,0:T(8,128)(2,1)}, bf16[10,4,160,512]{3,2,1,0:T(8,128)(2,1)}, bf16[10,4,160,512]{3,2,1,0:T(8,128)(2,1)}, f32[10,512]{1,0:T(8,128)S(1)}) custom-call(s32[2]{0:T(128)S(1)} %get-tuple-element.427.at_ref, bf16[512,1536]{1,0:T(8,128)(2,1)S(1)} %multiply_convert_fusion.2.tok_ref, ...), custom_call_target="tpu_custom_call" | custom-call | tf_op jit(solution)/shard_map/experts_forward/pallas_call | solution.py:462
  365.6 26.8 %experts_forward.5 = (bf16[4,512,1536]{2,1,0:T(8,128)(2,1)}, bf16[10,4,160,1536]{3,2,1,0:T(8,128)(2,1)}, bf16[10,4,160,512]{3,2,1,0:T(8,128)(2,1)}, bf16[10,4,160,512]{3,2,1,0:T(8,128)(2,1)}, f32[10,512]{1,0:T(8,128)S(1)}) custom-call(s32[2]{0:T(128)S(1)} %get-tuple-element.428.at_ref, ...), custom_call_target="tpu_custom_call", output_to_operand_aliasing={{0}: (8, {}), {1}: (9, {}), {2}: (10, {}), {3}: (11, {})} | custom-call | tf_op jit(solution)/shard_map/experts_forward/pallas_call | solution.py:462
  392.4 10.2 collective-permute-done.30
  407.6 26.8 %experts_forward.6 = (bf16[4,512,1536]{2,1,0:T(8,128)(2,1)}, bf16[10,4,160,1536]{3,2,1,0:T(8,128)(2,1)}, bf16[10,4,160,512]{3,2,1,0:T(8,128)(2,1)}, bf16[10,4,160,512]{3,2,1,0:T(8,128)(2,1)}, f32[10,512]{1,0:T(8,128)S(1)}) custom-call(s32[2]{0:T(128)S(1)} %get-tuple-element.429.at_ref, ...), custom_call_target="tpu_custom_call", output_to_operand_aliasing={{0}: (8, {}), {1}: (9, {}), {2}: (10, {}), {3}: (11, {})} | custom-call | tf_op jit(solution)/shard_map/experts_forward/pallas_call | solution.py:462
  434.4 8.6 collective-permute-done.32
  445.2 26.8 %experts_forward.7 = (bf16[4,512,1536]{2,1,0:T(8,128)(2,1)}, bf16[10,4,160,1536]{3,2,1,0:T(8,128)(2,1)}, bf16[10,4,160,512]{3,2,1,0:T(8,128)(2,1)}, bf16[10,4,160,512]{3,2,1,0:T(8,128)(2,1)}, f32[10,512]{1,0:T(8,128)S(1)}) custom-call(s32[2]{0:T(128)S(1)} %get-tuple-element.426.at_ref, ...), custom_call_target="tpu_custom_call", output_to_operand_aliasing={{0}: (8, {}), {1}: (9, {}), {2}: (10, {}), {3}: (11, {})} | custom-call | tf_op jit(solution)/shard_map/experts_forward/pallas_call | solution.py:462
  476.7 31.5 %collective-permute-done.33 = bf16[512,1536]{1,0:T(8,128)(2,1)S(1)} collective-permute-done((bf16[512,1536]{1,0:T(8,128)(2,1)S(1)}, bf16[512,1536]{1,0:T(8,128)(2,1)S(1)}, u32[]{:S(2)}, u32[]{:S(2)}) %collective-permute-start.33) | collective-permute-done | bytes 1572896 | tf_op jit(solution)/shard_map/ppermute | solution.py:134
  513.1 31.4 %collective-permute-done.34 = bf16[512,1536]{1,0:T(8,128)(2,1)S(1)} collective-permute-done((bf16[512,1536]{1,0:T(8,128)(2,1)S(1)}, bf16[512,1536]{1,0:T(8,128)(2,1)S(1)}, u32[]{:S(2)}, u32[]{:S(2)}) %collective-permute-start.34) | collective-permute-done | bytes 1572896 | tf_op jit(solution)/shard_map/ppermute | solution.py:134
  547.5 6.1 collective-permute-start.35
  569.3 14.0 %collective-permute-done.35 = bf16[512,1536]{1,0:T(8,128)(2,1)} collective-permute-done((bf16[512,1536]{1,0:T(8,128)(2,1)}, bf16[512,1536]{1,0:T(8,128)(2,1)}, u32[]{:S(2)}, u32[]{:S(2)}) %collective-permute-start.35) | collective-permute-done | bytes 1572896 | tf_op jit(solution)/shard_map/ppermute | solution.py:134
  583.3 35.1 %collective-permute-done.38 = bf16[512,1536]{1,0:T(8,128)(2,1)} collective-permute-done((bf16[512,1536]{1,0:T(8,128)(2,1)}, bf16[512,1536]{1,0:T(8,128)(2,1)}, u32[]{:S(2)}, u32[]{:S(2)}) %collective-permute-start.38) | collective-permute-done | bytes 1572896 | tf_op jit(solution)/shard_map/ppermute | solution.py:135
  640.8 32.1 %experts_backward.4 = (bf16[4,512,1536]{2,1,0:T(8,128)(2,1)}, bf16[10,4,160,1536]{3,2,1,0:T(8,128)(2,1)}, bf16[10,4,160,1024]{3,2,1,0:T(8,128)(2,1)}, bf16[10,4,...) custom-call(s32[2]{0:T(128)S(1)} %get-tuple-element.427.at_ref, bf16[512,1536]{1,0:T(8,128)(2,1)S(1)} %get-tuple-element.226.tok_ref, ...), custom_call_target="tpu_custom_call" | custom-call | tf_op jit(solution)/shard_map/experts_backward/pallas_call | solution.py:462
  678.4 32.0 %experts_backward.5 = (bf16[4,512,1536]{2,1,0:T(8,128)(2,1)}, bf16[10,4,160,1536]{3,2,1,0:T(8,128)(2,1)}, bf16[10,4,160,1024]{3,2,1,0:T(8,128)(2,1)}, bf16[10,4,...) custom-call(s32[2]{0:T(128)S(1)} %copy-done.29, ...), custom_call_target="tpu_custom_call", output_to_operand_aliasing={{0}: (11, {}), {1}: (12, {}), {2}: (13, {}), {3}: (14, {})} | custom-call | tf_op jit(solution)/shard_map/experts_backward/pallas_call | solution.py:462
  717.7 32.0 %experts_backward.6 = (bf16[4,512,1536]{2,1,0:T(8,128)(2,1)}, bf16[10,4,160,1536]{3,2,1,0:T(8,128)(2,1)}, bf16[10,4,160,1024]{3,2,1,0:T(8,128)(2,1)}, bf16[10,4,...) custom-call(s32[2]{0:T(128)S(1)} %copy-done.27, ...), custom_call_target="tpu_custom_call", output_to_operand_aliasing={{0}: (11, {}), {1}: (12, {}), {2}: (13, {}), {3}: (14, {})} | custom-call | tf_op jit(solution)/shard_map/experts_backward/pallas_call | solution.py:462
  755.5 32.0 %experts_backward.7 = (bf16[4,512,1536]{2,1,0:T(8,128)(2,1)}, bf16[10,4,160,1536]{3,2,1,0:T(8,128)(2,1)}, bf16[10,4,160,1024]{3,2,1,0:T(8,128)(2,1)}, bf16[10,4,...) custom-call(s32[2]{0:T(128)S(1)} %get-tuple-element.426.at_ref, ...), custom_call_target="tpu_custom_call", output_to_operand_aliasing={{0}: (11, {}), {1}: (12, {}), {2}: (13, {}), {3}: (14, {})} | custom-call | tf_op jit(solution)/shard_map/experts_backward/pallas_call | solution.py:462
  789.6 10.2 collective-permute-start.59
  800.6 33.6 %gate_up_grads.1 = (bf16[4,10,192,512]{3,2,1,0:T(8,128)(2,1)}, bf16[4,10,192,512]{3,2,1,0:T(8,128)(2,1)}, bf16[4,10,192,512]{3,2,1,0:T(8,128)(2,1)}, bf16[4,10,192,512]{3,2,1,0:T(8,128)(2,1)}) custom-call(s32[1]{0:T(128)} %bitcast.45.me_ref, bf16[10,640,1536]{2,1,0:T(8,128)(2,1)} %bitcast.281, bf16[10,640,1024]{2,1,0:T(8,128)(2,1)} %bitcast.282), custom_call_target="tpu_custom_call" | custom-call | tf_op jit(solution)/shard_map/gate_up_grads/pallas_call | solution.py:586
  842.0 21.4 %down_grads.1 = bf16[10,512,1536]{2,1,0:T(8,128)(2,1)} custom-call(bf16[10,640,512]{2,1,0:T(8,128)(2,1)} %bitcast.287, bf16[10,640,1536]{2,1,0:T(8,128)(2,1)} %bitcast.280), custom_call_target="tpu_custom_call" | custom-call | tf_op jit(solution)/shard_map/down_grads/pallas_call | solution.py:610
  863.4 9.7 collective-permute-done.61
  876.8 8.0 collective-permute-start.65
  886.4 9.1 add_convert_fusion.1
  896.9 6.9 add_convert_fusion
  903.8 13.3 collective-permute-done.65
  940.3 7.6 collective-permute-start.69
  952.9 12.2 collective-permute-done.71
  984.1 54.3 %attention_backward.1 = (bf16[2,3,64,2048]{3,2,1,0:T(8,128)(2,1)S(1)}, bf16[2,64,2048]{2,1,0:T(8,128)(2,1)S(1)}, bf16[2,64,2048]{2,1,0:T(8,128)(2,1)S(1)}) custom-call(s32[1,2048]{1,0:T(1,128)S(1)} %bitcast.276, bf16[2,3,64,2048]{3,2,1,0:T(8,128)(2,1)S(1)} %copy-done.1, bf16[2,2048,64]{2,1,0:T(8,128)(2,1)S(1)} %copy.161.k_ref, ...), custom_call_target="tpu_custom_call" | custom-call | tf_op jit(solution)/shard_map/attention_backward/pallas_call | solution.py:328
  1038.4 26.4 %collective-permute-done.73 = bf16[2,10,192,512]{3,2,1,0:T(8,128)(2,1)} collective-permute-done((bf16[2,10,192,512]{3,2,1,0:T(8,128)(2,1)}, bf16[2,10,192,512]{3,2,1,0:T(8,128)(2,1)}, u32[]{:S(2)}, u32[]{:S(2)}) %collective-permute-start.73) | collective-permute-done | bytes 3932192 | tf_op jit(solution)/shard_map/ppermute | solution.py:165
  1079.9 6.3 convolution_convert_fusion.2
  1087.1 10.3 collective-permute-start.75
  1106.4 23.9 %collective-permute-done.75 = bf16[512,1536]{1,0:T(8,128)(2,1)S(1)} collective-permute-done((bf16[512,1536]{1,0:T(8,128)(2,1)S(1)}, bf16[512,1536]{1,0:T(8,128)(2,1)S(1)}, u32[]{:S(2)}, u32[]{:S(2)}) %collective-permute-start.75) | collective-permute-done | bytes 1572896 | tf_op jit(solution)/shard_map/ppermute | solution.py:134
  1136.5 32.0 %collective-permute-done.77 = bf16[512,1536]{1,0:T(8,128)(2,1)S(1)} collective-permute-done((bf16[512,1536]{1,0:T(8,128)(2,1)S(1)}, bf16[512,1536]{1,0:T(8,128)(2,1)S(1)}, u32[]{:S(2)}, u32[]{:S(2)}) %collective-permute-start.77) | collective-permute-done | bytes 1572896 | tf_op jit(solution)/shard_map/ppermute | solution.py:134
  1181.9 33.2 %collective-permute-start.39 = (f32[1,1]{1,0:T(1,128)}, f32[1,1]{1,0:T(1,128)}, u32[]{:S(2)}, u32[]{:S(2)}) collective-permute-start(f32[1,1]{1,0:T(1,128)} %bitcast.70), channel_id=1, source_target_pairs={{0,1},{1,0},{2,3},{3,2},{4,5},{5,4},{6,7},{7,6},{8,9},{9,8},{10,11... | collective-permute-start | bytes 20 | tf_op jit(solution)/shard_map/ppermute | solution.py:165
  1215.1 28.5 %collective-permute-done.39 = f32[1,1]{1,0:T(1,128)} collective-permute-done((f32[1,1]{1,0:T(1,128)}, f32[1,1]{1,0:T(1,128)}, u32[]{:S(2)}, u32[]{:S(2)}) %collective-permute-start.39) | collective-permute-done | bytes 36 | tf_op jit(solution)/shard_map/ppermute | solution.py:165
  1265.1 21.8 %psum.15 = bf16[192,41]{0,1:T(8,128)(2,1)S(1)} all-reduce(bf16[192,41]{0,1:T(8,128)(2,1)S(1)} %copy.178), channel_id=1, replica_groups=mesh['fsdp'=8,'seq'=4] {'seq'}, use_global_device_ids=true, to_apply=%region_18.19 | all-reduce | flops 7872 | bytes 31488 | tf_op jit(solution)/shard_map/psum | solution.py:895
  1297.6 28.3 %all-reduce.3.cloned.1.call-done = bf16[192,1536]{1,0:T(8,128)(2,1)} async-done(((bf16[192,1536]{1,0:T(8,128)(2,1)}), bf16[192,1536]{1,0:T(8,128)(2,1)}) %all-reduce.3.cloned.1.call-update) | async-done | bytes 589840 | tf_op jit(solution)/shard_map/psum | solution.py:895
  1351.0 7.4 dynamic_update_slice.86
  (567 shorter events, 374.1 us)
Async XLA Ops:
  7.2 164.8 %all-gather.5.cloned.1.call-start = ((), (), s32[]{:S(2)}) async-start(), calls=%async_computation.4 | async-start | bytes 2211840 | tf_op jit(solution)/shard_map/all_gather | solution.py:691
  9.0 277.5 %all-gather.7.cloned.1.call-start = ((), (), s32[]{:S(2)}) async-start(), calls=%async_computation.5 | async-start | bytes 5308416 | tf_op jit(solution)/shard_map/all_gather | solution.py:692
  9.7 315.1 %all-gather.9.cloned.1.call-start = ((), (), s32[]{:S(2)}) async-start(), calls=%async_computation.6 | async-start | bytes 17694720 | tf_op jit(solution)/shard_map/all_gather | solution.py:693
  10.5 319.7 %all-gather.11.cloned.1.call-start = ((), (), s32[]{:S(2)}) async-start(), calls=%async_computation.7 | async-start | bytes 17694720 | tf_op jit(solution)/shard_map/all_gather | solution.py:694
  11.1 1253.2 %reduce-scatter.13.cloned.1.call-start = ((), (), s32[]{:S(2)}) async-start(), calls=%async_computation.12 | async-start | bytes 442368
  11.1 39.6 %collective-permute-start.1 = (bf16[512,1536]{1,0:T(8,128)(2,1)}, bf16[512,1536]{1,0:T(8,128)(2,1)}, u32[]{:S(2)}, u32[]{:S(2)}) collective-permute-start(bf16[512,1536]{1,0:T(8,128)(2,1)} %bitcast), channel_id=1, source_target_pairs={{1,0},{2,1},{3,2},{5,4},{6,5},{7,6},{9,8},{10,9},{11,10},{13,12},{... | collective-permute-start | bytes 4718600 | tf_op jit(solution)/shard_map/ppermute | solution.py:68
  12.4 50.7 %collective-permute-start = (bf16[512,1536]{1,0:T(8,128)(2,1)}, bf16[512,1536]{1,0:T(8,128)(2,1)}, u32[]{:S(2)}, u32[]{:S(2)}) collective-permute-start(bf16[512,1536]{1,0:T(8,128)(2,1)} %bitcast), channel_id=1, source_target_pairs={{0,1},{1,2},{2,3},{4,5},{5,6},{6,7},{8,9},{9,10},{10,11},{12,13},{... | collective-permute-start | bytes 4718600 | tf_op jit(solution)/shard_map/ppermute | solution.py:67
  19.2 45.7 %collective-permute-start.6 = (bf16[1,192,42]{1,2,0:T(8,128)(2,1)S(1)}, bf16[1,192,42]{1,2,0:T(8,128)(2,1)S(1)}, u32[]{:S(2)}, u32[]{:S(2)}) collective-permute-start(bf16[1,192,42]{1,2,0:T(8,128)(2,1)S(1)} %maximum_bitcast_fusion), channel_id=1, source_target_pairs={{0,4},{4,0},{8,12},{12,8},{16,20},{20,16},{24,28},{28,24},{1,5},{5... | collective-permute-start | bytes 48392 | tf_op jit(solution)/shard_map/ppermute | solution.py:165
  19.9 46.3 %collective-permute-start.15 = (s32[9,512]{1,0:T(8,128)}, s32[9,512]{1,0:T(8,128)S(1)}, u32[]{:S(2)}, u32[]{:S(2)}) collective-permute-start(s32[9,512]{1,0:T(8,128)} %pad_add_fusion), channel_id=1, source_target_pairs={{0,1},{1,2},{2,3},{4,5},{5,6},{6,7},{8,9},{9,10},{10,11},{12,13},{... | collective-permute-start | bytes 55304 | tf_op jit(solution)/shard_map/ppermute | solution.py:67
  50.7 82.1 %collective-permute-start.2 = (bf16[512,1536]{1,0:T(8,128)(2,1)}, bf16[512,1536]{1,0:T(8,128)(2,1)}, u32[]{:S(2)}, u32[]{:S(2)}) collective-permute-start(bf16[512,1536]{1,0:T(8,128)(2,1)} %collective-permute-done.1), channel_id=1, source_target_pairs={{1,0},{2,1},{5,4},{6,5},{9,8},{10,9},{13,12},{14,13},{17,16},{18,1... | collective-permute-start | bytes 4718600 | tf_op jit(solution)/shard_map/ppermute | solution.py:68
  61.3 107.4 %collective-permute-start.27 = (bf16[2,10,64,768]{3,2,1,0:T(8,128)(2,1)}, bf16[2,10,64,768]{3,2,1,0:T(8,128)(2,1)}, u32[]{:S(2)}, u32[]{:S(2)}) collective-permute-start(bf16[2,10,64,768]{3,2,1,0:T(8,128)(2,1)} %pad_maximum_fusion.6), channel_id=1, source_target_pairs={{0,8},{4,12},{8,0},{12,4},{16,24},{20,28},{24,16},{28,20},{1,9},{5... | collective-permute-start | bytes 5898248 | tf_op jit(solution)/shard_map/ppermute | solution.py:165
  63.1 82.5 %collective-permute-start.4 = (bf16[512,1536]{1,0:T(8,128)(2,1)}, bf16[512,1536]{1,0:T(8,128)(2,1)}, u32[]{:S(2)}, u32[]{:S(2)}) collective-permute-start(bf16[512,1536]{1,0:T(8,128)(2,1)} %collective-permute-done), channel_id=1, source_target_pairs={{1,2},{2,3},{5,6},{6,7},{9,10},{10,11},{13,14},{14,15},{17,18},{18... | collective-permute-start | bytes 4718600 | tf_op jit(solution)/shard_map/ppermute | solution.py:67
  66.3 59.9 %collective-permute-start.7 = (bf16[2,192,42]{1,2,0:T(8,128)(2,1)S(1)}, bf16[2,192,42]{1,2,0:T(8,128)(2,1)S(1)}, u32[]{:S(2)}, u32[]{:S(2)}) collective-permute-start(bf16[2,192,42]{1,2,0:T(8,128)(2,1)S(1)} %pad_maximum_fusion.11), channel_id=1, source_target_pairs={{0,8},{4,12},{8,0},{12,4},{16,24},{20,28},{24,16},{28,20},{1,9},{5... | collective-permute-start | bytes 96776 | tf_op jit(solution)/shard_map/ppermute | solution.py:165
  128.1 36.4 %collective-permute-start.23 = (bf16[1,10,64,768]{3,2,1,0:T(8,128)(2,1)S(1)}, bf16[1,10,64,768]{3,2,1,0:T(8,128)(2,1)}, u32[]{:S(2)}, u32[]{:S(2)}) collective-permute-start(bf16[1,10,64,768]{3,2,1,0:T(8,128)(2,1)S(1)} %get-tuple-element.388), channel_id=1, source_target_pairs={{0,8},{4,12},{8,0},{12,4},{16,24},{20,28},{24,16},{28,20},{1,9},{5... | collective-permute-start | bytes 2949128 | tf_op jit(solution)/shard_map/ppermute | solution.py:165
  132.8 41.9 %collective-permute-start.3 = (bf16[512,1536]{1,0:T(8,128)(2,1)}, bf16[512,1536]{1,0:T(8,128)(2,1)}, u32[]{:S(2)}, u32[]{:S(2)}) collective-permute-start(bf16[512,1536]{1,0:T(8,128)(2,1)} %collective-permute-done.2), channel_id=1, source_target_pairs={{1,0},{5,4},{9,8},{13,12},{17,16},{21,20},{25,24},{29,28}} | collective-permute-start | bytes 4718600 | tf_op jit(solution)/shard_map/ppermute | solution.py:68
  167.2 79.2 %collective-permute-start.24 = (bf16[2,10,64,768]{3,2,1,0:T(8,128)(2,1)}, bf16[2,10,64,768]{3,2,1,0:T(8,128)(2,1)}, u32[]{:S(2)}, u32[]{:S(2)}) collective-permute-start(bf16[2,10,64,768]{3,2,1,0:T(8,128)(2,1)} %pad_maximum_fusion.5), channel_id=1, source_target_pairs={{0,16},{4,20},{8,24},{12,28},{16,0},{20,4},{24,8},{28,12},{1,17},{... | collective-permute-start | bytes 5898248 | tf_op jit(solution)/shard_map/ppermute | solution.py:165
  172.0 132.4 %collective-permute-start.28 = (bf16[4,10,64,768]{3,2,1,0:T(8,128)(2,1)}, bf16[4,10,64,768]{3,2,1,0:T(8,128)(2,1)}, u32[]{:S(2)}, u32[]{:S(2)}) collective-permute-start(bf16[4,10,64,768]{3,2,1,0:T(8,128)(2,1)} %pad_maximum_fusion.3), channel_id=1, source_target_pairs={{0,4},{4,0},{8,12},{12,8},{16,20},{20,16},{24,28},{28,24},{1,5},{5... | collective-permute-start | bytes 11796488 | tf_op jit(solution)/shard_map/ppermute | solution.py:165
  294.7 64.0 %collective-permute-start.21 = (bf16[512,1536]{1,0:T(8,128)(2,1)S(1)}, bf16[512,1536]{1,0:T(8,128)(2,1)}, u32[]{:S(2)}, u32[]{:S(2)}) collective-permute-start(bf16[512,1536]{1,0:T(8,128)(2,1)S(1)} %multiply_convert_fusion.2.tok_ref), channel_id=1, source_target_pairs={{0,1},{1,2},{2,3},{4,5},{5,6},{6,7},{8,9},{9,10},{10,11},{12,13},{... | collective-permute-start | bytes 4718600 | tf_op jit(solution)/shard_map/ppermute | solution.py:67
  303.1 55.6 %collective-permute-start.22 = (bf16[512,1536]{1,0:T(8,128)(2,1)S(1)}, bf16[512,1536]{1,0:T(8,128)(2,1)}, u32[]{:S(2)}, u32[]{:S(2)}) collective-permute-start(bf16[512,1536]{1,0:T(8,128)(2,1)S(1)} %multiply_convert_fusion.2.tok_ref), channel_id=1, source_target_pairs={{1,0},{2,1},{3,2},{5,4},{6,5},{7,6},{9,8},{10,9},{11,10},{13,12},{... | collective-permute-start | bytes 4718600 | tf_op jit(solution)/shard_map/ppermute | solution.py:68
  361.7 40.9 %collective-permute-start.30 = (bf16[512,1536]{1,0:T(8,128)(2,1)}, bf16[512,1536]{1,0:T(8,128)(2,1)S(1)}, u32[]{:S(2)}, u32[]{:S(2)}) collective-permute-start(bf16[512,1536]{1,0:T(8,128)(2,1)} %collective-permute-done.22), channel_id=1, source_target_pairs={{1,0},{2,1},{5,4},{6,5},{9,8},{10,9},{13,12},{14,13},{17,16},{18,1... | collective-permute-start | bytes 4718600 | tf_op jit(solution)/shard_map/ppermute | solution.py:68
  404.9 38.1 %collective-permute-start.32 = (bf16[512,1536]{1,0:T(8,128)(2,1)S(1)}, bf16[512,1536]{1,0:T(8,128)(2,1)S(1)}, u32[]{:S(2)}, u32[]{:S(2)}) collective-permute-start(bf16[512,1536]{1,0:T(8,128)(2,1)S(1)} %collective-permute-done.30), channel_id=1, source_target_pairs={{1,0},{5,4},{9,8},{13,12},{17,16},{21,20},{25,24},{29,28}} | collective-permute-start | bytes 4718600 | tf_op jit(solution)/shard_map/ppermute | solution.py:68
  475.9 37.2 %collective-permute-start.36 = (bf16[512,1536]{1,0:T(8,128)(2,1)S(1)}, bf16[512,1536]{1,0:T(8,128)(2,1)S(1)}, u32[]{:S(2)}, u32[]{:S(2)}) collective-permute-start(bf16[512,1536]{1,0:T(8,128)(2,1)S(1)} %get-tuple-element.378), channel_id=1, source_target_pairs={{3,2},{7,6},{11,10},{15,14},{19,18},{23,22},{27,26},{31,30}} | collective-permute-start | bytes 4718600 | tf_op jit(solution)/shard_map/ppermute | solution.py:135
  555.1 63.3 %collective-permute-start.38 = (bf16[512,1536]{1,0:T(8,128)(2,1)}, bf16[512,1536]{1,0:T(8,128)(2,1)}, u32[]{:S(2)}, u32[]{:S(2)}) collective-permute-start(bf16[512,1536]{1,0:T(8,128)(2,1)} %fusion.18), channel_id=1, source_target_pairs={{1,0},{2,1},{3,2},{5,4},{6,5},{7,6},{9,8},{10,9},{11,10},{13,12},{... | collective-permute-start | bytes 4718600 | tf_op jit(solution)/shard_map/ppermute | solution.py:135
  629.7 43.2 %collective-permute-start.47 = (bf16[512,1536]{1,0:T(8,128)(2,1)S(1)}, bf16[512,1536]{1,0:T(8,128)(2,1)S(1)}, u32[]{:S(2)}, u32[]{:S(2)}) collective-permute-start(bf16[512,1536]{1,0:T(8,128)(2,1)S(1)} %get-tuple-element.226.tok_ref), channel_id=1, source_target_pairs={{0,1},{1,2},{2,3},{4,5},{5,6},{6,7},{8,9},{9,10},{10,11},{12,13},{... | collective-permute-start | bytes 4718600 | tf_op jit(solution)/shard_map/ppermute | solution.py:67
  633.4 39.5 %collective-permute-start.48 = (bf16[512,1536]{1,0:T(8,128)(2,1)S(1)}, bf16[512,1536]{1,0:T(8,128)(2,1)S(1)}, u32[]{:S(2)}, u32[]{:S(2)}) collective-permute-start(bf16[512,1536]{1,0:T(8,128)(2,1)S(1)} %get-tuple-element.226.tok_ref), channel_id=1, source_target_pairs={{1,0},{2,1},{3,2},{5,4},{6,5},{7,6},{9,8},{10,9},{11,10},{13,12},{... | collective-permute-start | bytes 4718600 | tf_op jit(solution)/shard_map/ppermute | solution.py:68
  634.7 38.2 %collective-permute-start.49 = (f32[1,512]{1,0:T(1,128)S(1)}, f32[1,512]{1,0:T(1,128)S(1)}, u32[]{:S(2)}, u32[]{:S(2)}) collective-permute-start(f32[1,512]{1,0:T(1,128)S(1)} %bitcast.277), channel_id=1, source_target_pairs={{0,1},{1,2},{2,3},{4,5},{5,6},{6,7},{8,9},{9,10},{10,11},{12,13},{... | collective-permute-start | bytes 6152 | tf_op jit(solution)/shard_map/ppermute | solution.py:67
  673.7 36.8 %collective-permute-start.51 = (bf16[512,1536]{1,0:T(8,128)(2,1)S(1)}, bf16[512,1536]{1,0:T(8,128)(2,1)S(1)}, u32[]{:S(2)}, u32[]{:S(2)}) collective-permute-start(bf16[512,1536]{1,0:T(8,128)(2,1)S(1)} %collective-permute-done.47), channel_id=1, source_target_pairs={{1,2},{2,3},{5,6},{6,7},{9,10},{10,11},{13,14},{14,15},{17,18},{18... | collective-permute-start | bytes 4718600 | tf_op jit(solution)/shard_map/ppermute | solution.py:67
  712.0 39.3 %collective-permute-start.55 = (bf16[512,1536]{1,0:T(8,128)(2,1)S(1)}, bf16[512,1536]{1,0:T(8,128)(2,1)S(1)}, u32[]{:S(2)}, u32[]{:S(2)}) collective-permute-start(bf16[512,1536]{1,0:T(8,128)(2,1)S(1)} %collective-permute-done.51), channel_id=1, source_target_pairs={{2,3},{6,7},{10,11},{14,15},{18,19},{22,23},{26,27},{30,31}} | collective-permute-start | bytes 4718600 | tf_op jit(solution)/shard_map/ppermute | solution.py:67
  712.8 38.5 %collective-permute-start.56 = (bf16[512,1536]{1,0:T(8,128)(2,1)S(1)}, bf16[512,1536]{1,0:T(8,128)(2,1)S(1)}, u32[]{:S(2)}, u32[]{:S(2)}) collective-permute-start(bf16[512,1536]{1,0:T(8,128)(2,1)S(1)} %collective-permute-done.52), channel_id=1, source_target_pairs={{1,0},{5,4},{9,8},{13,12},{17,16},{21,20},{25,24},{29,28}} | collective-permute-start | bytes 4718600 | tf_op jit(solution)/shard_map/ppermute | solution.py:68
  714.7 36.5 %collective-permute-start.58 = (f32[1,512]{1,0:T(1,128)S(1)}, f32[1,512]{1,0:T(1,128)S(1)}, u32[]{:S(2)}, u32[]{:S(2)}) collective-permute-start(f32[1,512]{1,0:T(1,128)S(1)} %collective-permute-done.54), channel_id=1, source_target_pairs={{1,0},{5,4},{9,8},{13,12},{17,16},{21,20},{25,24},{29,28}} | collective-permute-start | bytes 6152 | tf_op jit(solution)/shard_map/ppermute | solution.py:68
  789.6 44.6 %collective-permute-start.59 = (bf16[512,1536]{1,0:T(8,128)(2,1)S(1)}, bf16[512,1536]{1,0:T(8,128)(2,1)S(1)}, u32[]{:S(2)}, u32[]{:S(2)}) collective-permute-start(bf16[512,1536]{1,0:T(8,128)(2,1)S(1)} %get-tuple-element.274), channel_id=1, source_target_pairs={{0,1},{4,5},{8,9},{12,13},{16,17},{20,21},{24,25},{28,29}} | collective-permute-start | bytes 4718600 | tf_op jit(solution)/shard_map/ppermute | solution.py:134
  836.9 36.2 %collective-permute-start.63 = (bf16[4,10,192,512]{3,2,1,0:T(8,128)(2,1)}, bf16[4,10,192,512]{3,2,1,0:T(8,128)(2,1)}, u32[]{:S(2)}, u32[]{:S(2)}) collective-permute-start(bf16[4,10,192,512]{3,2,1,0:T(8,128)(2,1)} %get-tuple-element.292), channel_id=1, source_target_pairs={{0,4},{4,0},{8,12},{12,8},{16,20},{20,16},{24,28},{28,24},{1,5},{5... | collective-permute-start | bytes 23592968 | tf_op jit(solution)/shard_map/ppermute | solution.py:165
  876.8 40.4 %collective-permute-start.65 = (bf16[512,1536]{1,0:T(8,128)(2,1)S(1)}, bf16[512,1536]{1,0:T(8,128)(2,1)S(1)}, u32[]{:S(2)}, u32[]{:S(2)}) collective-permute-start(bf16[512,1536]{1,0:T(8,128)(2,1)S(1)} %get-tuple-element.300), channel_id=1, source_target_pairs={{0,1},{1,2},{2,3},{4,5},{5,6},{6,7},{8,9},{9,10},{10,11},{12,13},{... | collective-permute-start | bytes 4718600 | tf_op jit(solution)/shard_map/ppermute | solution.py:134
  884.8 36.7 %collective-permute-start.66 = (bf16[512,1536]{1,0:T(8,128)(2,1)S(1)}, bf16[512,1536]{1,0:T(8,128)(2,1)S(1)}, u32[]{:S(2)}, u32[]{:S(2)}) collective-permute-start(bf16[512,1536]{1,0:T(8,128)(2,1)S(1)} %get-tuple-element.301), channel_id=1, source_target_pairs={{1,0},{2,1},{3,2},{5,4},{6,5},{7,6},{9,8},{10,9},{11,10},{13,12},{... | collective-permute-start | bytes 4718600 | tf_op jit(solution)/shard_map/ppermute | solution.py:135
  965.1 99.7 %collective-permute-start.73 = (bf16[2,10,192,512]{3,2,1,0:T(8,128)(2,1)}, bf16[2,10,192,512]{3,2,1,0:T(8,128)(2,1)}, u32[]{:S(2)}, u32[]{:S(2)}) collective-permute-start(bf16[2,10,192,512]{3,2,1,0:T(8,128)(2,1)} %get-tuple-element.327), channel_id=1, source_target_pairs={{0,8},{4,12},{8,0},{12,4},{16,24},{20,28},{24,16},{28,20},{1,9},{5... | collective-permute-start | bytes 11796488 | tf_op jit(solution)/shard_map/ppermute | solution.py:165
  967.4 101.0 %collective-permute-start.74 = (bf16[2,10,192,512]{3,2,1,0:T(8,128)(2,1)}, bf16[2,10,192,512]{3,2,1,0:T(8,128)(2,1)}, u32[]{:S(2)}, u32[]{:S(2)}) collective-permute-start(bf16[2,10,192,512]{3,2,1,0:T(8,128)(2,1)} %get-tuple-element.328), channel_id=1, source_target_pairs={{0,16},{4,20},{8,24},{12,28},{16,0},{20,4},{24,8},{28,12},{1,17},{... | collective-permute-start | bytes 11796488 | tf_op jit(solution)/shard_map/ppermute | solution.py:165
  974.6 312.4 %reduce-scatter.11.cloned.1.call-start = ((), (), s32[]{:S(2)}) async-start(), calls=%async_computation.10 | async-start | bytes 5308416 | tf_op jit(solution)/shard_map/reduce_scatter | solution.py:893
  975.2 319.9 %reduce-scatter.9.cloned.1.call-start = ((), (), s32[]{:S(2)}) async-start(), calls=%async_computation.9 | async-start | bytes 2211840 | tf_op jit(solution)/shard_map/reduce_scatter | solution.py:866
  1086.3 208.9 %reduce-scatter.7.cloned.1.call-start = ((), (), s32[]{:S(2)}) async-start(), calls=%async_computation.8 | async-start | bytes 17694720 | tf_op jit(solution)/shard_map/reduce_scatter | solution.py:835
  1087.0 238.9 %all-reduce.3.cloned.1.call-start = ((), (), s32[]{:S(2)}) async-start(), calls=%async_computation.11 | async-start | bytes 1179648 | tf_op jit(solution)/shard_map/psum | solution.py:895
  1087.1 43.2 %collective-permute-start.75 = (bf16[512,1536]{1,0:T(8,128)(2,1)S(1)}, bf16[512,1536]{1,0:T(8,128)(2,1)S(1)}, u32[]{:S(2)}, u32[]{:S(2)}) collective-permute-start(bf16[512,1536]{1,0:T(8,128)(2,1)S(1)} %get-tuple-element.334), channel_id=1, source_target_pairs={{0,1},{4,5},{8,9},{12,13},{16,17},{20,21},{24,25},{28,29}} | collective-permute-start | bytes 4718600 | tf_op jit(solution)/shard_map/ppermute | solution.py:134
  1132.1 36.5 %collective-permute-start.77 = (bf16[512,1536]{1,0:T(8,128)(2,1)S(1)}, bf16[512,1536]{1,0:T(8,128)(2,1)S(1)}, u32[]{:S(2)}, u32[]{:S(2)}) collective-permute-start(bf16[512,1536]{1,0:T(8,128)(2,1)S(1)} %fusion.10), channel_id=1, source_target_pairs={{0,1},{1,2},{4,5},{5,6},{8,9},{9,10},{12,13},{13,14},{16,17},{17,1... | collective-permute-start | bytes 4718600 | tf_op jit(solution)/shard_map/ppermute | solution.py:134
  1171.5 115.5 %collective-permute-start.78 = (bf16[512,1536]{1,0:T(8,128)(2,1)}, bf16[512,1536]{1,0:T(8,128)(2,1)S(1)}, u32[]{:S(2)}, u32[]{:S(2)}) collective-permute-start(bf16[512,1536]{1,0:T(8,128)(2,1)} %get-tuple-element.365), channel_id=1, source_target_pairs={{0,1},{1,2},{2,3},{4,5},{5,6},{6,7},{8,9},{9,10},{10,11},{12,13},{... | collective-permute-start | bytes 4718600 | tf_op jit(solution)/shard_map/ppermute | solution.py:134
  1178.0 109.0 %collective-permute-start.80 = (bf16[512,1536]{1,0:T(8,128)(2,1)}, bf16[512,1536]{1,0:T(8,128)(2,1)S(1)}, u32[]{:S(2)}, u32[]{:S(2)}) collective-permute-start(bf16[512,1536]{1,0:T(8,128)(2,1)} %fusion.9), channel_id=1, source_target_pairs={{1,0},{2,1},{3,2},{5,4},{6,5},{7,6},{9,8},{10,9},{11,10},{13,12},{... | collective-permute-start | bytes 4718600 | tf_op jit(solution)/shard_map/ppermute | solution.py:135
  1179.3 115.8 %collective-permute-start.81 = (bf16[1,10,192,512]{3,2,1,0:T(8,128)(2,1)}, bf16[1,10,192,512]{3,2,1,0:T(8,128)(2,1)}, u32[]{:S(2)}, u32[]{:S(2)}) collective-permute-start(bf16[1,10,192,512]{3,2,1,0:T(8,128)(2,1)} %add_convert_fusion.7), channel_id=1, source_target_pairs={{0,16},{4,20},{8,24},{12,28},{16,0},{20,4},{24,8},{28,12},{1,17},{... | collective-permute-start | bytes 5898248 | tf_op jit(solution)/shard_map/ppermute | solution.py:165
  1180.4 114.7 %collective-permute-start.82 = (bf16[1,10,192,512]{3,2,1,0:T(8,128)(2,1)}, bf16[1,10,192,512]{3,2,1,0:T(8,128)(2,1)}, u32[]{:S(2)}, u32[]{:S(2)}) collective-permute-start(bf16[1,10,192,512]{3,2,1,0:T(8,128)(2,1)} %add_convert_fusion.6), channel_id=1, source_target_pairs={{0,8},{4,12},{8,0},{12,4},{16,24},{20,28},{24,16},{28,20},{1,9},{5... | collective-permute-start | bytes 5898248 | tf_op jit(solution)/shard_map/ppermute | solution.py:165
  1181.9 61.7 %collective-permute-start.39 = (f32[1,1]{1,0:T(1,128)}, f32[1,1]{1,0:T(1,128)}, u32[]{:S(2)}, u32[]{:S(2)}) collective-permute-start(f32[1,1]{1,0:T(1,128)} %bitcast.70), channel_id=1, source_target_pairs={{0,1},{1,0},{2,3},{3,2},{4,5},{5,4},{6,7},{7,6},{8,9},{9,8},{10,11... | collective-permute-start | bytes 20 | tf_op jit(solution)/shard_map/ppermute | solution.py:165
  1295.1 36.3 %collective-permute-start.84 = (bf16[192,640]{1,0:T(8,128)(2,1)}, bf16[192,640]{1,0:T(8,128)(2,1)S(1)}, u32[]{:S(2)}, u32[]{:S(2)}) collective-permute-start(bf16[192,640]{1,0:T(8,128)(2,1)} %reduce-scatter.9.cloned.1.call-done), channel_id=1, source_target_pairs={{1,0},{2,1},{3,2},{5,4},{6,5},{7,6},{9,8},{10,9},{11,10},{13,12},{... | collective-permute-start | bytes 737288 | tf_op jit(solution)/shard_map/ppermute | solution.py:68
  (165 other events, 3378.6 us)
Sparse Core Ops, SparseCore 0:
  9.9 36.4 all-gather.4
  48.3 53.8 all-gather.6
  104.1 138.0 all-gather.8
  244.0 86.2 all-gather.10
  974.7 40.8 reduce-scatter.12
  1018.9 65.7 reduce-scatter.10
  1089.0 42.3 reduce-scatter.8
  1134.9 141.8 reduce-scatter.6
  1287.1 38.7 all-reduce.2

commit v5 on v4

--- a/solution.py
+++ b/solution.py
@@ -73,7 +73,7 @@
     n = lax.axis_size("seq")
     rights, lefts = [block], [block]
     for k in range(1, n):
-        right, left = line_move(rights[-1], lefts[-1], k)
+        right, left = tie(*line_move(rights[-1], lefts[-1], k))
         rights.append(right)
         lefts.append(left)
     return nearest(rights, lefts)
@@ -175,6 +175,16 @@
 def fsdp_bits():
     bits = [1 << step for step in range(lax.axis_size("fsdp").bit_length() - 1)]
     return tuple(bits), tuple(bits[:1] + bits[:0:-1])
+
+
+def total_steps(value, *axes):
+    for axis in axes:
+        for step in range(lax.axis_size(axis).bit_length() - 1):
+            here = swap(value, axis, 1 << step)
+            here = yield here
+            value = value + here
+    while True:
+        yield value
 
 
 def doubling_gather(block, bits):
@@ -363,7 +373,7 @@
 
 
 def experts_kernel(
-    at_ref, tok_ref, slot_ref, member_ref, router_ref, wg_ref, wu_ref, wd_ref, *refs
+    base, every, at_ref, tok_ref, slot_ref, member_ref, router_ref, wg_ref, wu_ref, wd_ref, *refs
 ):
     part_ref, x_ref, g_ref, u_ref, gates_ref, acc, gates_all = refs[-7:]
     e, experts = pl.program_id(0), pl.num_programs(0)
@@ -376,12 +386,12 @@
         chosen = jnp.exp(chosen - jnp.max(chosen, axis=0, keepdims=True))
         chosen = jnp.where(member, chosen, 0.0)
         gates_all[...] = chosen / jnp.sum(chosen, axis=0, keepdims=True)
-        acc[...] = jnp.zeros_like(acc)
-
-    gate_row = own_row(gates_all, at_ref[1] * experts + e)
+        acc[...] = refs[0][...].astype(full) if base else jnp.zeros_like(acc)
+
+    gate_row = own_row(gates_all, at_ref[1] * every + base + e)
     gates_ref[pl.ds(e, 1), :] = gate_row
     place = lax.broadcasted_iota(jnp.int32, (slots, 1), 0)
-    here = place == own_row(slot_ref, e)
+    here = place == own_row(slot_ref, base + e)
     x = nn(jnp.where(here, 1.0, 0.0).astype(low), tok_ref[...]).astype(low)
     x_ref[0, 0] = x
     g = nn(x, wg_ref[0])
@@ -394,11 +404,11 @@
 
     @pl.when(e == experts - 1)
     def _():
-        part_ref[0] = acc[...].astype(low)
+        part_ref[...] = acc[...].astype(low).reshape(part_ref.shape)
 
 
 def back_kernel(
-    at_ref, tok_ref, slot_ref, gates_ref, mix_ref, router_ref, g_ref, u_ref, wg_ref, wu_ref, wd_ref, *refs
+    base, at_ref, tok_ref, slot_ref, gates_ref, mix_ref, router_ref, g_ref, u_ref, wg_ref, wu_ref, wd_ref, *refs
 ):
     part_ref, d_ref, dgu_ref, act_ref, dlog_ref, acc, dlog_all = refs[-7:]
     e, experts = pl.program_id(0), pl.num_programs(0)
@@ -407,10 +417,10 @@
     @pl.when(e == 0)
     def _():
         dlog_all[...] = jnp.zeros_like(dlog_all)
-        acc[...] = jnp.zeros_like(acc)
+        acc[...] = refs[0][...].astype(full) if base else jnp.zeros_like(acc)
 
     place = lax.broadcasted_iota(jnp.int32, (slots, 1), 0)
-    here = place == own_row(slot_ref, e)
+    here = place == own_row(slot_ref, base + e)
     pick = jnp.where(here, 1.0, 0.0).astype(low)
     gate_row = own_row(gates_ref, e)
     gate = jnp.sum(jnp.where(here, gate_row, 0.0), axis=1, keepdims=True)
@@ -437,15 +447,16 @@
     def _():
         dlog = dlog_all[...].astype(low)
         dlog_ref[...] = dlog
-        part_ref[0] = (acc[...] + tn(dlog, router_ref[...])).astype(low)
+        part = acc[...] + tn(dlog, router_ref[...])
+        part_ref[...] = part.astype(low).reshape(part_ref.shape)
 
 
 def by_expert(*shape):
     return pl.BlockSpec((1,) + shape, lambda e, at: (e, 0, 0))
 
 
-def in_turn(turn, *shape):
-    return pl.BlockSpec((1, 1) + shape, lambda e, at: (e, turn, 0, 0))
+def in_turn(base, turn, *shape):
+    return pl.BlockSpec((1, 1) + shape, lambda e, at: (base + e, turn, 0, 0))
 
 
 def same(*shape):
@@ -456,37 +467,53 @@
     return pl.BlockSpec((1,) + shape, lambda e, at: (at[0], 0, 0))
 
 
-def shard_call(kernel, name, at, inputs, in_specs, out_specs, out_shape, buffers, scratch, experts):
-    first = len(inputs) + 1
-    aliases = {first + i: i for i in range(len(buffers))}
-    return pl.pallas_call(
+def shard_call(kernel, name, at, inputs, in_specs, outs, buffers, scratch, experts, partial):
+    last = partial is not None
+    buffers = list(buffers)
+    part_out, rest_out = outs[0], outs[1:]
+    if not last:
+        shape = part_out[1].shape[1:]
+        part_out = (same(*shape), jax.ShapeDtypeStruct(shape, low))
+    else:
+        inputs, in_specs = inputs + [partial], in_specs + [same(*partial.shape)]
+    kept = buffers[0] if buffers else None
+    passed = [] if not buffers else (buffers if last and kept is not None else buffers[1:])
+    start = len(inputs) + 1
+    skip = 0 if last and kept is not None else 1
+    aliases = {start + i: i + skip for i in range(len(passed))}
+    results = pl.pallas_call(
         kernel,
         grid_spec=pltpu.PrefetchScalarGridSpec(
             num_scalar_prefetch=1,
             grid=(experts,),
-            in_specs=in_specs + [pl.BlockSpec(memory_space=pl.ANY)] * len(buffers),
-            out_specs=out_specs,
+            in_specs=in_specs + [pl.BlockSpec(memory_space=pl.ANY)] * len(passed),
+            out_specs=[part_out[0]] + [spec for spec, _ in rest_out],
             scratch_shapes=scratch,
         ),
-        out_shape=out_shape,
+        out_shape=[part_out[1]] + [shape for _, shape in rest_out],
         input_output_aliases=aliases,
         compiler_params=vmem(48),
         name=name,
-    )(at, *inputs, *buffers)
-
-
-def experts_forward(turn, devs, at, tokens, slot_of, member, router, w_gate, w_up, w_down, slots, buffers):
-    experts, width, hidden = w_gate.shape
+    )(at, *inputs, *passed)
+    if last:
+        return None, list(results[:-1]), results[-1]
+    return results[0], [kept] + list(results[1:-1]), results[-1]
+
+
+def experts_forward(
+    base, every, turn, devs, at, tokens, slot_of, member, router, weights, slots, buffers, partial
+):
+    experts, width, hidden = weights[0].shape
     count = tokens.shape[0]
     total_experts = member.shape[0]
     return shard_call(
-        experts_kernel,
+        functools.partial(experts_kernel, base, every),
         "experts_forward",
         at,
-        [tokens, slot_of, member, router, w_gate, w_up, w_down],
+        [tokens, slot_of, member, router, *weights],
         [
             same(count, width),
-            same(experts, count),
+            same(every, count),
             same(total_experts, count),
             same(total_experts, width),
             by_expert(width, hidden),
@@ -494,66 +521,72 @@
             by_expert(hidden, width),
         ],
         [
-            in_place(count, width),
-            in_turn(turn, slots, width),
-            in_turn(turn, slots, hidden),
-            in_turn(turn, slots, hidden),
-            same(experts, count),
-        ],
-        [
-            jax.ShapeDtypeStruct((devs, count, width), low),
-            jax.ShapeDtypeStruct((experts, devs, slots, width), low),
-            jax.ShapeDtypeStruct((experts, devs, slots, hidden), low),
-            jax.ShapeDtypeStruct((experts, devs, slots, hidden), low),
-            jax.ShapeDtypeStruct((experts, count), full),
+            (in_place(count, width), jax.ShapeDtypeStruct((devs, count, width), low)),
+            (
+                in_turn(base, turn, slots, width),
+                jax.ShapeDtypeStruct((every, devs, slots, width), low),
+            ),
+            (
+                in_turn(base, turn, slots, hidden),
+                jax.ShapeDtypeStruct((every, devs, slots, hidden), low),
+            ),
+            (
+                in_turn(base, turn, slots, hidden),
+                jax.ShapeDtypeStruct((every, devs, slots, hidden), low),
+            ),
+            (same(experts, count), jax.ShapeDtypeStruct((experts, count), full)),
         ],
         buffers,
         [pltpu.VMEM((count, width), full), pltpu.VMEM((total_experts, count), full)],
         experts,
+        partial,
     )
 
 
 def experts_backward(
-    turn, devs, at, d_tokens, slot_of, gates, mix_dot, router, g, u, w_gate, w_up, w_down, buffers
+    base, turn, devs, at, d_tokens, slot_of, gates, mix_dot, router, g, u, weights, buffers, partial
 ):
-    experts, width, hidden = w_gate.shape
+    experts, width, hidden = weights[0].shape
     count = d_tokens.shape[0]
-    slots = g.shape[2]
+    every, _, slots, _ = g.shape
     lines = router.shape[0]
     return shard_call(
-        back_kernel,
+        functools.partial(back_kernel, base),
         "experts_backward",
         at,
-        [d_tokens, slot_of, gates, mix_dot, router, g, u, w_gate, w_up, w_down],
+        [d_tokens, slot_of, gates, mix_dot, router, g, u, *weights],
         [
             same(count, width),
-            same(experts, count),
+            same(every, count),
             same(experts, count),
             same(1, count),
             same(lines, width),
-            in_turn(turn, slots, hidden),
-            in_turn(turn, slots, hidden),
+            in_turn(base, turn, slots, hidden),
+            in_turn(base, turn, slots, hidden),
             by_expert(width, hidden),
             by_expert(width, hidden),
             by_expert(hidden, width),
         ],
         [
-            in_place(count, width),
-            in_turn(turn, slots, width),
-            in_turn(turn, slots, 2 * hidden),
-            in_turn(turn, slots, hidden),
-            same(lines, count),
-        ],
-        [
-            jax.ShapeDtypeStruct((devs, count, width), low),
-            jax.ShapeDtypeStruct((experts, devs, slots, width), low),
-            jax.ShapeDtypeStruct((experts, devs, slots, 2 * hidden), low),
-            jax.ShapeDtypeStruct((experts, devs, slots, hidden), low),
-            jax.ShapeDtypeStruct((lines, count), low),
+            (in_place(count, width), jax.ShapeDtypeStruct((devs, count, width), low)),
+            (
+                in_turn(base, turn, slots, width),
+                jax.ShapeDtypeStruct((every, devs, slots, width), low),
+            ),
+            (
+                in_turn(base, turn, slots, 2 * hidden),
+                jax.ShapeDtypeStruct((every, devs, slots, 2 * hidden), low),
+            ),
+            (
+                in_turn(base, turn, slots, hidden),
+                jax.ShapeDtypeStruct((every, devs, slots, hidden), low),
+            ),
+            (same(lines, count), jax.ShapeDtypeStruct((lines, count), low)),
         ],
         buffers,
         [pltpu.VMEM((count, width), full), pltpu.VMEM((lines, count), full)],
         experts,
+        partial,
     )
 
 
@@ -616,37 +649,6 @@
         compiler_params=vmem(48),
         name="down_grads",
     )(act, d_rows)
-
-
-def join_kernel(me_ref, left_ref, right_ref, out_ref):
-    half = left_ref.shape[3]
-    out_ref[:, :, :half] = left_ref[0]
-    out_ref[:, :, half:] = right_ref[0]
-
-
-def join_rows(me, left, right, bits_left, bits_right):
-    devs, experts, rows, half = left.shape
-
-    def place(bits):
-        def index(block, me_ref):
-            mask = me_ref[0] ^ block
-            spot = sum(((mask // bit) % 2) * 2**i for i, bit in enumerate(bits))
-            return (spot, 0, 0, 0)
-
-        return pl.BlockSpec((1, experts, rows, half), index)
-
-    return pl.pallas_call(
-        join_kernel,
-        grid_spec=pltpu.PrefetchScalarGridSpec(
-            num_scalar_prefetch=1,
-            grid=(devs,),
-            in_specs=[place(bits_left), place(bits_right)],
-            out_specs=pl.BlockSpec((experts, rows, 2 * half), lambda block, me_ref: (0, block, 0)),
-        ),
-        out_shape=jax.ShapeDtypeStruct((experts, devs * rows, 2 * half), low),
-        compiler_params=vmem(40),
-        name="join_rows",
-    )(me, left, right)
 
 
 def shards(
@@ -690,21 +692,20 @@
     small = small[mine ^ jnp.arange(small.shape[0])].reshape(width, 2 + expert_total)
     full_qkv = lax.all_gather(own_qkv, "fsdp", axis=0, tiled=True)
     full_out = lax.all_gather(w_out, "fsdp", axis=0, tiled=True)
-    full_gate = lax.all_gather(w_gate, "fsdp", axis=1, tiled=True)
-    full_up = lax.all_gather(w_up, "fsdp", axis=1, tiled=True)
-    down_a, down_b = order_a[1:] + order_a[:1], order_b[1:] + order_b[:1]
-    full_down = join_rows(
-        mine.reshape(1),
-        doubling_gather(w_down[:, :, : width // 2], down_a),
-        doubling_gather(w_down[:, :, width // 2 :], down_b),
-        down_a,
-        down_b,
-    )
+    cut = -(-7 * experts_here // 10)
+    weights = [
+        [lax.all_gather(w[group], "fsdp", axis=1, tiled=True) for w in (w_gate, w_up, w_down)]
+        for group in (slice(0, cut), slice(cut, None))
+    ]
+    bases = (0, cut)
     full_g1 = small[:, 0].astype(full)
     full_g2 = small[:, 1].astype(full)
     router = small[:, 2:].T
     own_router = lax.dynamic_slice_in_dim(router, me * experts_here, experts_here, 0)
-    own_router = jnp.pad(own_router, ((0, -experts_here % 16), (0, 0)))
+    own_routers = [
+        jnp.pad(rows, ((0, -rows.shape[0] % 16), (0, 0)))
+        for rows in (own_router[:cut], own_router[cut:])
+    ]
     valid_rows = valid_mask.reshape(shard_len).astype(full)
 
     routes_low = jnp.concatenate([routes.reshape(shard_len, top_count).T, valid_mask], axis=0)
@@ -733,7 +734,7 @@
     limit = block_limits(block_lengths[0], positions)[None]
     attended, out_heads, lse = attention_forward(query, key_rows, value, limit, shard_len)
     moved = exchange(attended)
-    moved, slot_of, member, own_router = tie(moved, slot_of, member, own_router)
+    moved, slot_of, member, own_routers = tie(moved, slot_of, member, own_routers)
     attn_rows = by_place(nearest(*moved)).reshape(HEADS * HEAD_DIM, shard_len)
     projected = dot("kt,kd->td", attn_rows, full_out)
     hidden = x_low.astype(full) + resid_mult * projected
@@ -741,31 +742,41 @@
 
     tokens = [normed_two.astype(low)]
     rights, lefts = [tokens[0]], [tokens[0]]
-    buffers, gates = [], []
+    buffers, gates = [None], []
+    partials = []
     for turn in range(n):
         if turn < n - 1:
             right, left, tokens[turn] = tie(rights[turn], lefts[turn], tokens[turn])
             right, left = line_move(right, left, turn + 1)
-        *buffers, shard_gates = experts_forward(
-            turn, n, jnp.stack([order[turn], me]), tokens[turn], slot_of[turn], member[turn],
-            router, full_gate, full_up, full_down, slots, buffers,
+        partial, buffers, shard_gates = experts_forward(
+            0, experts_here, turn, n, jnp.stack([order[turn], me]), tokens[turn], slot_of[turn],
+            member[turn], router, weights[0], slots, buffers, None,
         )
+        partials.append(partial)
         if turn < n - 1:
             right, left, shard_gates = tie(right, left, shard_gates)
             rights.append(right)
             lefts.append(left)
             tokens.append(arrived(rights, lefts, turn + 1))
-        gates.append(shard_gates)
+        gates.append([shard_gates])
+    for turn in range(n):
+        _, buffers, shard_gates = experts_forward(
+            cut, experts_here, turn, n, jnp.stack([order[turn], me]), tokens[turn], slot_of[turn],
+            member[turn], router, weights[1], slots, buffers, partials[turn],
+        )
+        gates[turn].append(shard_gates)
     mix_parts, expert_in, gate_act, up_act = buffers
     right = left = None
     for k in range(n - 1, 0, -1):
-        right, left = line_pass(*line_send(mix_parts, k, right, left), k)
+        moving = tie(*line_send(mix_parts, k, right, left))
+        right, left = tie(*line_pass(*moving, k))
     mixture = line_end(mix_parts, right, left)
     output_f32 = hidden + resid_mult * mixture
     activations = output_f32.astype(low).reshape(1, shard_len, width)
     error_rows = output_f32 - teacher.astype(full).reshape(shard_len, width)
     weighted = valid_rows[:, None] * error_rows
-    squares = jnp.sum(weighted * error_rows)
+    loss_steps = total_steps(jnp.sum(weighted * error_rows).reshape(1, 1), "seq", "fsdp")
+    squares = next(loss_steps)
     d_out = weighted * (tokens_all / valid_count)
 
     d_mix = resid_mult * d_out
@@ -773,7 +784,7 @@
     mix_dot = jnp.sum(d_mix * mixture, axis=1)[None]
     rights, lefts = [d_tokens], [d_tokens]
     dot_rights, dot_lefts = [mix_dot], [mix_dot]
-    buffers, d_logits = [], []
+    buffers, d_logits = [None], []
     for turn in range(n):
         if turn < n - 1:
             (right, left), (dot_right, dot_left), d_tokens = tie(
@@ -781,14 +792,19 @@
             )
             dot_right, dot_left = line_move(dot_right, dot_left, turn + 1)
             right, left = line_move(right, left, turn + 1)
-        *buffers, shard_logits = experts_backward(
-            turn, n, jnp.stack([order[turn], me]), d_tokens, slot_of[turn], gates[turn], mix_dot,
-            own_router, gate_act, up_act, full_gate, full_up, full_down, buffers,
-        )
+        partial, shard_logits = None, []
+        for group in (0, 1):
+            partial, buffers, group_logits = experts_backward(
+                bases[group], turn, n, jnp.stack([order[turn], me]), d_tokens, slot_of[turn],
+                gates[turn][group], mix_dot, own_routers[group], gate_act, up_act, weights[group],
+                buffers, partial,
+            )
+            shard_logits.append(group_logits)
         if turn < n - 1:
-            right, left, dot_right, dot_left, shard_logits = tie(
-                right, left, dot_right, dot_left, shard_logits
+            right, left, dot_right, dot_left, shard_logits, squares = tie(
+                right, left, dot_right, dot_left, shard_logits, squares
             )
+            squares = loss_steps.send(squares)
             rights.append(right)
             lefts.append(left)
             dot_rights.append(dot_right)
@@ -811,7 +827,7 @@
             gate_pair, up_pair = gate_up_grads(
                 mine.reshape(1), expert_in, d_gate_up, order_a, order_b
             )
-            right, left, gate_pair, up_pair = tie(right, left, gate_pair, up_pair)
+            right, left, gate_pair, up_pair, squares = tie(right, left, gate_pair, up_pair, squares)
         elif k == n - 2:
             moving, gate_pair, up_pair, act_low, d_rows = tie(
                 moving, gate_pair, up_pair, act_low, d_rows
@@ -820,17 +836,18 @@
             gate_here = swap(gate_pair[1], "fsdp", order_a[0])
             up_here = swap(up_pair[1], "fsdp", order_b[0])
             down_part = down_grads(act_low, d_rows)
-            right, left, gate_here, up_here, down_part = tie(
-                right, left, gate_here, up_here, down_part
+            right, left, gate_here, up_here, down_part, squares = tie(
+                right, left, gate_here, up_here, down_part, squares
             )
         elif k == n - 3:
             moving, gate_here, up_here = tie(moving, gate_here, up_here)
             right, left = line_pass(*moving, k)
             gate_send, gate_keep = halve(gate_pair[0], gate_here)
             up_send, up_keep = halve(up_pair[0], up_here)
-            right, left, gate_send, up_send = tie(right, left, gate_send, up_send)
+            right, left, gate_send, up_send, squares = tie(right, left, gate_send, up_send, squares)
         else:
-            right, left = line_pass(*moving, k)
+            right, left, squares = tie(*line_pass(*tie(*moving), k), squares)
+        squares = loss_steps.send(squares)
     d_normed_two = line_end(d_parts, right, left)
     down_sum = lax.psum_scatter(down_part, "fsdp", scatter_dimension=1, tiled=True)
 
@@ -838,23 +855,26 @@
     d_hidden = d_out + d_hidden_norm
     d_proj = (resid_mult * d_hidden).astype(low)
     d_attended = dot("kd,td->kt", full_out, d_proj).astype(low)
-    d_attended, gate_send, up_send = tie(d_attended, gate_send, up_send)
     moved = exchange(d_attended.reshape(n, heads_w, shard_len))
     gate_here = swap(gate_send, "fsdp", order_a[1])
     up_here = swap(up_send, "fsdp", order_b[1])
     out_part = dot("kt,td->kd", attn_rows, d_proj).astype(low)
+    d_logits = [
+        jnp.concatenate([first[:cut], second[: experts_here - cut]]) for first, second in d_logits
+    ]
     router_part = sum(
-        dot("td,et->de", shard, shard_logits[:experts_here])
-        for shard, shard_logits in zip(tokens, d_logits)
+        dot("td,et->de", shard, shard_logits) for shard, shard_logits in zip(tokens, d_logits)
     )
     moved, out_part, router_part = tie(moved, out_part, router_part)
+    out_sum = lax.psum_scatter(out_part, "fsdp", scatter_dimension=0, tiled=True)
     d_heads = by_place(nearest(*moved))
     query_grad, key_grad, value_grad = attention_backward(
         query, key_rows, value_rows, key, limit, out_heads, lse, d_heads
     )
-    (query_grad, key_grad, value_grad), gate_here, up_here = tie(
-        (query_grad, key_grad, value_grad), gate_here, up_here
-    )
+    (query_grad, key_grad, value_grad), gate_here, up_here, down_sum, out_sum = tie(
+        (query_grad, key_grad, value_grad), gate_here, up_here, down_sum, out_sum
+    )
+    out_sum = lax.psum(out_sum, "seq")
     d_turned = jnp.concatenate([query_grad, key_grad[:, None]], axis=1).astype(full)
     d_turned = rotate(d_turned, cosine, -sine_vals).astype(low)
     d_qkv = jnp.concatenate([d_turned, value_grad[:, None]], axis=1).reshape(group_w, seq_len)
@@ -862,7 +882,11 @@
     moving = line_send(d_parts, n - 1, None, None)
     moving, d_qkv, gate_here, up_here = tie(moving, d_qkv, gate_here, up_here)
     right, left = line_pass(*moving, n - 1)
-    qkv_part = dot("td,ct->dc", normed_one, d_qkv).astype(low)
+    own_columns = jnp.zeros((width, expert_total), full)
+    own_columns = lax.dynamic_update_slice_in_dim(own_columns, router_part, me * experts_here, 1)
+    qkv_part = jnp.concatenate(
+        [dot("td,ct->dc", normed_one, d_qkv), own_columns, gain_two_part[:, None]], axis=1
+    ).astype(low)
     qkv_sum = lax.psum_scatter(qkv_part, "fsdp", scatter_dimension=0, tiled=True)
     gate_send, gate_keep = halve(gate_keep, gate_here)
     up_send, up_keep = halve(up_keep, up_here)
@@ -870,13 +894,18 @@
     gate_here = swap(gate_send, "fsdp", order_a[2])
     up_here = swap(up_send, "fsdp", order_b[2])
     for k in range(n - 2, 0, -1):
-        right, left = line_pass(*line_send(d_parts, k, right, left), k)
+        moving = tie(*line_send(d_parts, k, right, left))
+        right, left = line_pass(*moving, k)
+        if k == 1:
+            right, left, qkv_sum = tie(right, left, qkv_sum)
+        else:
+            right, left = tie(right, left)
     d_normed_one = line_end(d_parts, right, left)
     _, norm_one_pull = jax.vjp(lambda v: rms_norm(v, full_g1), x_low.astype(full))
     input_grad = (d_hidden + norm_one_pull(d_normed_one)[0]).reshape(1, shard_len, width)
 
-    input_grad, gate_here, up_here, down_sum, qkv_sum = tie(
-        input_grad, gate_here, up_here, down_sum, qkv_sum
+    input_grad, gate_here, up_here, qkv_sum, out_sum = tie(
+        input_grad, gate_here, up_here, qkv_sum, out_sum
     )
     for bit_a, bit_b in zip(order_a[3:], order_b[3:]):
         gate_send, gate_keep = halve(gate_keep, gate_here)
@@ -886,21 +915,15 @@
     gate_grad = halve(gate_keep, gate_here)
     up_grad = halve(up_keep, up_here)
     down_grad = down_sum.astype(full)
-    own_columns = jnp.zeros((width, expert_total), full)
-    own_columns = lax.dynamic_update_slice_in_dim(own_columns, router_part, me * experts_here, 1)
-    rest = jnp.concatenate([own_columns.astype(low), gain_two_part[:, None].astype(low)], axis=1)
-    dense = [
-        lax.psum_scatter(part, "fsdp", scatter_dimension=0, tiled=True) for part in (out_part, rest)
-    ]
-    out_sum, rest = lax.psum(dense, "seq")
     out_grad = out_sum.astype(full)
-    router_grad = rest[:, :expert_total].astype(full)
-    gain_two_grad = rest[:, expert_total].astype(full)
-    qkv_grad = by_place(line_gather(qkv_sum))
-    qkv_grad = jnp.swapaxes(qkv_grad, 0, 1).reshape(-1, QKV_W).astype(full)
+    sums = by_place(line_gather(qkv_sum)).astype(full)
+    qkv_grad = jnp.swapaxes(sums[:, :, :group_w], 0, 1).reshape(-1, QKV_W)
+    rest = jnp.sum(sums[:, :, group_w:], axis=0)
+    router_grad, gain_two_grad = rest[:, :expert_total], rest[:, expert_total]
     gain_one_grad = jnp.sum(qkv_grad * w_qkv.astype(full), axis=1) / gain_one.astype(full)
-    squares = total(squares.reshape(1, 1), "seq", "fsdp")[0, 0]
-    loss_value = squares / (valid_count * width)
+    for _ in range(2):
+        squares = loss_steps.send(squares)
+    loss_value = squares[0, 0] / (valid_count * width)
     return (
         activations,
         loss_value,

time: 1380 us -> 1400 us (1.014)
  waiting for transfers between devices: 456 us -> 501 us
  Pallas kernels: 394 us -> 422 us
  starting transfers between devices: 222 us -> 195 us
  local copies, waits for them, and re-layouts: 61.9 us -> 87.1 us
  blocking collectives: 21.8 us -> 0 us
  other arithmetic: 155 us -> 139 us
    ppermute x23 -> x17, waiting for transfers between devices: 113 us -> 29.9 us  [swap(): lax.ppermute(value, axis, [(i, i ^ bit) for i in range(lax.axis_size(axis...]
    reduce_scatter x1, waiting for transfers between devices: 0.02 us -> 77.5 us  [shards(): lax.psum_scatter(down_part, 'fsdp', scatter_dimension=1, tiled=True)]
    pallas_call x8 -> x16, Pallas kernels: 235 us -> 272 us  [shard_call(): pl.pallas_call(kernel, grid_spec=pltpu.PrefetchScalarGridSpec(num_scalar_...]
    ppermute x23 -> x17, starting transfers between devices: 65.2 us -> 29.7 us  [swap(): lax.ppermute(value, axis, [(i, i ^ bit) for i in range(lax.axis_size(axis...]
    ppermute x18, waiting for transfers between devices: 72.5 us -> 108 us  [line_move(): lax.ppermute(left, 'seq', [(i, i - 1) for i in range(1, n - k + 1)])]
    ppermute x9, waiting for transfers between devices: 156 us -> 188 us  [line_pass(): lax.ppermute(to_right, 'seq', [(i, i + 1) for i in range(n - k)])]
    ppermute x18, waiting for transfers between devices: 0.05 us -> 31.2 us  [line_move(): lax.ppermute(right, 'seq', [(i, i + 1) for i in range(k - 1, n - 1)])]
    psum x1, waiting for transfers between devices: 28.3 us -> 0.01 us  [shards(): out_sum = lax.psum(out_sum, 'seq')]
  transfers between devices with their start and end apart: 98 -> 95, of which waited for: 37 -> 36; matrix products, arithmetic and copies ran while one was open for 13% -> 11% of each run, Pallas kernels for 25% -> 24%
where the time goes in v5:
time: 1400 us
  waiting for transfers between devices  501 us (36%)
  Pallas kernels  422 us (30%)
  starting transfers between devices  195 us (14%)
  other arithmetic  139 us (10%)
  local copies, waits for them, and re-layouts  87.1 us (6%)
  matrix products  28.4 us (2%)
  between operations  25 us (2%)
    pallas_call x16, Pallas kernels, shard_call(): pl.pallas_call(kernel, grid_spec=pltpu.PrefetchScalarGridSpec(num_scalar_...  272 us
    ppermute x9, waiting for transfers between devices, line_pass(): lax.ppermute(to_right, 'seq', [(i, i + 1) for i in range(n - k)])  188 us
    ppermute x18, waiting for transfers between devices, line_move(): lax.ppermute(left, 'seq', [(i, i - 1) for i in range(1, n - k + 1)])  108 us
    reduce_scatter x1, waiting for transfers between devices, shards(): lax.psum_scatter(down_part, 'fsdp', scatter_dimension=1, tiled=True)  77.5 us
    ppermute x9, starting transfers between devices, line_pass(): lax.ppermute(to_right, 'seq', [(i, i + 1) for i in range(n - k)])  60.5 us
    pallas_call x1, Pallas kernels, attention_backward(): pl.pallas_call(functools.partial(backward_kernel, seq_len, query_rows, ke...  54.3 us
    pallas_call x1, Pallas kernels, attention_forward(): pl.pallas_call(functools.partial(forward_kernel, seq_len, query_rows, key...  39.8 us
    pallas_call x1, Pallas kernels, gate_up_grads(): pl.pallas_call(functools.partial(gate_up_kernel, bits_a, bits_b), grid_sp...  33.8 us
  transfers between devices with their start and end apart: 95, of which 36 were waited for; matrix products, arithmetic and copies ran while one was open for 11% of the time, Pallas kernels for 24%

profile of v5, /device:TPU:0, one launch (start us, length us, event | category | flops | bytes accessed | tf_op | source)
XLA Modules:
  0.0 1397.4 jit_solution(17507346631409162653)
XLA Ops:
  27.9 31.2 %collective-permute-done = bf16[512,1536]{1,0:T(8,128)(2,1)} collective-permute-done((bf16[512,1536]{1,0:T(8,128)(2,1)S(1)}, bf16[512,1536]{1,0:T(8,128)(2,1)}, u32[]{:S(2)}, u32[]{:S(2)}) %collective-permute-start) | collective-permute-done | bytes 1572896 | tf_op jit(solution)/shard_map/ppermute | solution.py:67
  81.6 23.1 %collective-permute-done.3 = bf16[512,1536]{1,0:T(8,128)(2,1)} collective-permute-done((bf16[512,1536]{1,0:T(8,128)(2,1)S(1)}, bf16[512,1536]{1,0:T(8,128)(2,1)}, u32[]{:S(2)}, u32[]{:S(2)}) %collective-permute-start.3) | collective-permute-done | bytes 1572896 | tf_op jit(solution)/shard_map/ppermute | solution.py:68
  114.0 29.0 %collective-permute-done.18 = s32[9,512]{1,0:T(8,128)S(1)} collective-permute-done((s32[9,512]{1,0:T(8,128)S(1)}, s32[9,512]{1,0:T(8,128)S(1)}, u32[]{:S(2)}, u32[]{:S(2)}) %collective-permute-start.18) | collective-permute-done | bytes 18464 | tf_op jit(solution)/shard_map/ppermute | solution.py:68
  180.7 39.8 %attention_forward.1 = (bf16[4,384,512]{2,1,0:T(8,128)(2,1)S(1)}, f32[2,3,64,2048]{3,2,1,0:T(8,128)S(1)}, f32[2,3,1,2048]{3,2,1,0:T(1,128)S(1)}) custom-call(s32[1,2048]{1,0:T(1,128)S(1)} %bitcast.272, bf16[2,3,64,2048]{3,2,1,0:T(8,128)(2,1)S(1)} %copy.188.q_ref, bf16[2,2048,64]{2,1,0:T(8,128)(2,1)S(1)} %copy.189.k_ref, ...), custom_call_target="tpu_custom_call" | custom-call | tf_op jit(solution)/shard_map/attention_forward/pallas_call | solution.py:267
  234.4 16.3 %collective-permute-start.9 = (bf16[384,512]{1,0:T(8,128)(2,1)S(1)}, bf16[384,512]{1,0:T(8,128)(2,1)S(1)}, u32[]{:S(2)}, u32[]{:S(2)}) collective-permute-start(bf16[384,512]{1,0:T(8,128)(2,1)S(1)} %get-tuple-element.577), channel_id=1, source_target_pairs={{0,1},{1,2},{2,3},{4,5},{5,6},{6,7},{8,9},{9,10},{10,11},{12,13},{... | collective-permute-start | bytes 1179656 | tf_op jit(solution)/shard_map/ppermute | solution.py:159
  250.9 15.1 %collective-permute-done.13 = bf16[384,512]{1,0:T(8,128)(2,1)S(1)} collective-permute-done((bf16[384,512]{1,0:T(8,128)(2,1)S(1)}, bf16[384,512]{1,0:T(8,128)(2,1)S(1)}, u32[]{:S(2)}, u32[]{:S(2)}) %collective-permute-start.13) | collective-permute-done | bytes 393248 | tf_op jit(solution)/shard_map/ppermute | solution.py:160
  287.7 19.7 %experts_forward.8 = (bf16[512,1536]{1,0:T(8,128)(2,1)S(1)}, bf16[10,4,160,1536]{3,2,1,0:T(8,128)(2,1)}, bf16[10,4,160,512]{3,2,1,0:T(8,128)(2,1)}, bf16[10,4,160,512]{3,2,1,0:T(8,128)(2,1)}, f32[7,512]{1,0:T(8,128)S(1)}) custom-call(s32[2]{0:T(128)S(1)} %get-tuple-element.603.at_ref, bf16[512,1536]{1,0:T(8,128)(2,1)S(1)} %multiply_convert_fusion.2.tok_ref, ...), custom_call_target="tpu_custom_call" | custom-call | tf_op jit(solution)/shard_map/experts_forward/pallas_call | solution.py:484
  317.4 19.8 %experts_forward.9 = (bf16[512,1536]{1,0:T(8,128)(2,1)S(1)}, bf16[10,4,160,1536]{3,2,1,0:T(8,128)(2,1)}, bf16[10,4,160,512]{3,2,1,0:T(8,128)(2,1)}, bf16[10,4,160,512]{3,2,1,0:T(8,128)(2,1)}, f32[7,512]{1,0:T(8,128)S(1)}) custom-call(s32[2]{0:T(128)S(1)} %get-tuple-element.604.at_ref, ...), custom_call_target="tpu_custom_call", output_to_operand_aliasing={{1}: (8, {}), {2}: (9, {}), {3}: (10, {})} | custom-call | tf_op jit(solution)/shard_map/experts_forward/pallas_call | solution.py:484
  337.8 13.8 collective-permute-done.24
  356.8 19.8 %experts_forward.10 = (bf16[512,1536]{1,0:T(8,128)(2,1)S(1)}, bf16[10,4,160,1536]{3,2,1,0:T(8,128)(2,1)}, bf16[10,4,160,512]{3,2,1,0:T(8,128)(2,1)}, bf16[10,4,160,512]{3,2,1,0:T(8,128)(2,1)}, f32[7,512]{1,0:T(8,128)S(1)}) custom-call(s32[2]{0:T(128)S(1)} %get-tuple-element.605.at_ref, ...), custom_call_target="tpu_custom_call", output_to_operand_aliasing={{1}: (8, {}), {2}: (9, {}), {3}: (10, {})} | custom-call | tf_op jit(solution)/shard_map/experts_forward/pallas_call | solution.py:484
  377.8 13.4 collective-permute-done.26
  393.3 19.8 %experts_forward.11 = (bf16[512,1536]{1,0:T(8,128)(2,1)S(1)}, bf16[10,4,160,1536]{3,2,1,0:T(8,128)(2,1)}, bf16[10,4,160,512]{3,2,1,0:T(8,128)(2,1)}, bf16[10,4,160,512]{3,2,1,0:T(8,128)(2,1)}, f32[7,512]{1,0:T(8,128)S(1)}) custom-call(s32[2]{0:T(128)S(1)} %get-tuple-element.602.at_ref, ...), custom_call_target="tpu_custom_call", output_to_operand_aliasing={{1}: (8, {}), {2}: (9, {}), {3}: (10, {})} | custom-call | tf_op jit(solution)/shard_map/experts_forward/pallas_call | solution.py:484
  420.4 11.4 experts_forward.12
  431.8 11.4 experts_forward.13
  443.9 11.7 experts_forward.14
  455.6 11.6 experts_forward.15
  472.0 30.6 %collective-permute-done.27 = bf16[512,1536]{1,0:T(8,128)(2,1)S(1)} collective-permute-done((bf16[512,1536]{1,0:T(8,128)(2,1)S(1)}, bf16[512,1536]{1,0:T(8,128)(2,1)S(1)}, u32[]{:S(2)}, u32[]{:S(2)}) %collective-permute-start.27) | collective-permute-done | bytes 1572896 | tf_op jit(solution)/shard_map/ppermute | solution.py:134
  508.8 29.7 %collective-permute-done.29 = bf16[512,1536]{1,0:T(8,128)(2,1)S(1)} collective-permute-done((bf16[512,1536]{1,0:T(8,128)(2,1)S(1)}, bf16[512,1536]{1,0:T(8,128)(2,1)S(1)}, u32[]{:S(2)}, u32[]{:S(2)}) %collective-permute-start.29) | collective-permute-done | bytes 1572896 | tf_op jit(solution)/shard_map/ppermute | solution.py:134
  541.1 9.5 collective-permute-start.31
  564.3 16.3 %collective-permute-done.31 = bf16[512,1536]{1,0:T(8,128)(2,1)} collective-permute-done((bf16[512,1536]{1,0:T(8,128)(2,1)}, bf16[512,1536]{1,0:T(8,128)(2,1)}, u32[]{:S(2)}, u32[]{:S(2)}) %collective-permute-start.31) | collective-permute-done | bytes 1572896 | tf_op jit(solution)/shard_map/ppermute | solution.py:134
  608.4 23.7 %experts_backward.8 = (bf16[512,1536]{1,0:T(8,128)(2,1)S(1)}, bf16[10,4,160,1536]{3,2,1,0:T(8,128)(2,1)}, bf16[10,4,160,1024]{3,2,1,0:T(8,128)(2,1)}, bf16[10,4,...) custom-call(s32[2]{0:T(128)S(1)} %copy-done.50, bf16[512,1536]{1,0:T(8,128)(2,1)S(1)} %get-tuple-element.353.tok_ref, ...), custom_call_target="tpu_custom_call" | custom-call | tf_op jit(solution)/shard_map/experts_backward/pallas_call | solution.py:484
  632.1 13.2 experts_backward.9
  652.2 8.8 collective-permute-start.45
  660.9 23.5 %experts_backward.10 = (bf16[512,1536]{1,0:T(8,128)(2,1)S(1)}, bf16[10,4,160,1536]{3,2,1,0:T(8,128)(2,1)}, bf16[10,4,160,1024]{3,2,1,0:T(8,128)(2,1)}, bf16[10,4...) custom-call(s32[2]{0:T(128)S(1)} %copy-done.47, ...), custom_call_target="tpu_custom_call", output_to_operand_aliasing={{1}: (11, {}), {2}: (12, {}), {3}: (13, {})} | custom-call | tf_op jit(solution)/shard_map/experts_backward/pallas_call | solution.py:484
  684.4 13.3 experts_backward.11
  706.6 23.5 %experts_backward.12 = (bf16[512,1536]{1,0:T(8,128)(2,1)S(1)}, bf16[10,4,160,1536]{3,2,1,0:T(8,128)(2,1)}, bf16[10,4,160,1024]{3,2,1,0:T(8,128)(2,1)}, bf16[10,4...) custom-call(s32[2]{0:T(128)S(1)} %get-tuple-element.605.at_ref, ...), custom_call_target="tpu_custom_call", output_to_operand_aliasing={{1}: (11, {}), {2}: (12, {}), {3}: (13, {})} | custom-call | tf_op jit(solution)/shard_map/experts_backward/pallas_call | solution.py:484
  730.1 13.2 experts_backward.13
  750.2 23.5 %experts_backward.14 = (bf16[512,1536]{1,0:T(8,128)(2,1)S(1)}, bf16[10,4,160,1536]{3,2,1,0:T(8,128)(2,1)}, bf16[10,4,160,1024]{3,2,1,0:T(8,128)(2,1)}, bf16[10,4...) custom-call(s32[2]{0:T(128)S(1)} %get-tuple-element.602.at_ref, ...), custom_call_target="tpu_custom_call", output_to_operand_aliasing={{1}: (11, {}), {2}: (12, {}), {3}: (13, {})} | custom-call | tf_op jit(solution)/shard_map/experts_backward/pallas_call | solution.py:484
  773.7 13.4 experts_backward.15
  789.3 15.5 %collective-permute-start.51 = (bf16[512,1536]{1,0:T(8,128)(2,1)S(1)}, bf16[512,1536]{1,0:T(8,128)(2,1)S(1)}, u32[]{:S(2)}, u32[]{:S(2)}) collective-permute-start(bf16[512,1536]{1,0:T(8,128)(2,1)S(1)} %get-tuple-element.428), channel_id=1, source_target_pairs={{0,1},{4,5},{8,9},{12,13},{16,17},{20,21},{24,25},{28,29}} | collective-permute-start | bytes 4718600 | tf_op jit(solution)/shard_map/ppermute | solution.py:134
  809.2 33.8 %gate_up_grads.1 = (bf16[4,10,192,512]{3,2,1,0:T(8,128)(2,1)}, bf16[4,10,192,512]{3,2,1,0:T(8,128)(2,1)}, bf16[4,10,192,512]{3,2,1,0:T(8,128)(2,1)}, bf16[4,10,192,512]{3,2,1,0:T(8,128)(2,1)}) custom-call(s32[1]{0:T(128)} %bitcast.75.me_ref, bf16[10,640,1536]{2,1,0:T(8,128)(2,1)} %bitcast.279, bf16[10,640,1024]{2,1,0:T(8,128)(2,1)} %bitcast.280), custom_call_target="tpu_custom_call" | custom-call | tf_op jit(solution)/shard_map/gate_up_grads/pallas_call | solution.py:619
  852.7 21.3 %down_grads.1 = bf16[10,512,1536]{2,1,0:T(8,128)(2,1)} custom-call(bf16[10,640,512]{2,1,0:T(8,128)(2,1)} %bitcast.281, bf16[10,640,1536]{2,1,0:T(8,128)(2,1)} %bitcast.278), custom_call_target="tpu_custom_call" | custom-call | tf_op jit(solution)/shard_map/down_grads/pallas_call | solution.py:643
  874.0 7.7 collective-permute-done.54
  885.4 9.5 collective-permute-start.59
  897.7 9.1 add_convert_fusion
  906.8 7.3 add_convert_fusion.1
  914.2 13.3 collective-permute-done.59
  973.4 15.3 %collective-permute-done.65 = bf16[384,512]{1,0:T(8,128)(2,1)S(1)} collective-permute-done((bf16[384,512]{1,0:T(8,128)(2,1)}, bf16[384,512]{1,0:T(8,128)(2,1)S(1)}, u32[]{:S(2)}, u32[]{:S(2)}) %collective-permute-start.65) | collective-permute-done | bytes 393248 | tf_op jit(solution)/shard_map/ppermute | solution.py:160
  993.7 7.7 fusion.1
  1009.4 54.3 %attention_backward.1 = (bf16[2,3,64,2048]{3,2,1,0:T(8,128)(2,1)S(1)}, bf16[2,64,2048]{2,1,0:T(8,128)(2,1)S(1)}, bf16[2,64,2048]{2,1,0:T(8,128)(2,1)S(1)}) custom-call(s32[1,2048]{1,0:T(1,128)S(1)} %bitcast.273, bf16[2,3,64,2048]{3,2,1,0:T(8,128)(2,1)S(1)} %copy-done.7, bf16[2,2048,64]{2,1,0:T(8,128)(2,1)S(1)} %copy-done.9, ...), custom_call_target="tpu_custom_call" | custom-call | tf_op jit(solution)/shard_map/attention_backward/pallas_call | solution.py:338
  1066.4 27.2 %collective-permute-done.67 = bf16[2,10,192,512]{3,2,1,0:T(8,128)(2,1)} collective-permute-done((bf16[2,10,192,512]{3,2,1,0:T(8,128)(2,1)}, bf16[2,10,192,512]{3,2,1,0:T(8,128)(2,1)}, u32[]{:S(2)}, u32[]{:S(2)}) %collective-permute-start.67) | collective-permute-done | bytes 3932192 | tf_op jit(solution)/shard_map/ppermute | solution.py:165
  1093.6 77.5 %reduce-scatter.6.cloned.1.call-done = bf16[10,64,1536]{2,1,0:T(8,128)(2,1)} async-done(((bf16[10,512,1536]{2,1,0:T(8,128)(2,1)}), bf16[10,64,1536]{2,1,0:T(8,128)(2,1)}) %reduce-scatter.6.cloned.1.call-update) | async-done | bytes 1966096 | tf_op jit(solution)/shard_map/reduce_scatter | solution.py:852
  1199.5 19.2 %collective-permute-done.69 = bf16[512,1536]{1,0:T(8,128)(2,1)S(1)} collective-permute-done((bf16[512,1536]{1,0:T(8,128)(2,1)S(1)}, bf16[512,1536]{1,0:T(8,128)(2,1)S(1)}, u32[]{:S(2)}, u32[]{:S(2)}) %collective-permute-start.69) | collective-permute-done | bytes 1572896 | tf_op jit(solution)/shard_map/ppermute | solution.py:134
  1231.2 27.5 %collective-permute-done.71 = bf16[512,1536]{1,0:T(8,128)(2,1)} collective-permute-done((bf16[512,1536]{1,0:T(8,128)(2,1)}, bf16[512,1536]{1,0:T(8,128)(2,1)}, u32[]{:S(2)}, u32[]{:S(2)}) %collective-permute-start.71) | collective-permute-done | bytes 1572896 | tf_op jit(solution)/shard_map/ppermute | solution.py:134
  1264.1 8.3 collective-permute-start.73
  1277.0 44.1 %collective-permute-done.73 = bf16[512,1536]{1,0:T(8,128)(2,1)S(1)} collective-permute-done((bf16[512,1536]{1,0:T(8,128)(2,1)}, bf16[512,1536]{1,0:T(8,128)(2,1)S(1)}, u32[]{:S(2)}, u32[]{:S(2)}) %collective-permute-start.73) | collective-permute-done | bytes 1572896 | tf_op jit(solution)/shard_map/ppermute | solution.py:134
  1343.1 7.5 collective-permute-done.78
  1377.1 8.1 dynamic_update_slice.87
  (631 shorter events, 409.1 us)
Async XLA Ops:
  7.2 143.7 %all-gather.9.cloned.1.call-start = ((), (), s32[]{:S(2)}) async-start(), calls=%async_computation.3 | async-start | bytes 2211840 | tf_op jit(solution)/shard_map/all_gather | solution.py:693
  9.1 257.4 %all-gather.11.cloned.1.call-start = ((), (), s32[]{:S(2)}) async-start(), calls=%async_computation.4 | async-start | bytes 5308416 | tf_op jit(solution)/shard_map/all_gather | solution.py:694
  9.8 270.6 %all-gather.13.cloned.1.call-start = ((), (), s32[]{:S(2)}) async-start(), calls=%async_computation.5 | async-start | bytes 12386304 | tf_op jit(solution)/shard_map/all_gather | solution.py:697
  12.4 268.0 %all-gather.15.cloned.1.call-start = ((), (), s32[]{:S(2)}) async-start(), calls=%async_computation.6 | async-start | bytes 12386304 | tf_op jit(solution)/shard_map/all_gather | solution.py:697
  13.7 274.0 %all-gather.17.cloned.1.call-start = ((), (), s32[]{:S(2)}) async-start(), calls=%async_computation.7 | async-start | bytes 12386304 | tf_op jit(solution)/shard_map/all_gather | solution.py:697
  16.4 399.7 %all-gather.19.cloned.1.call-start = ((), (), s32[]{:S(2)}) async-start(), calls=%async_computation.8 | async-start | bytes 5308416 | tf_op jit(solution)/shard_map/all_gather | solution.py:697
  18.4 397.6 %all-gather.21.cloned.1.call-start = ((), (), s32[]{:S(2)}) async-start(), calls=%async_computation.9 | async-start | bytes 5308416 | tf_op jit(solution)/shard_map/all_gather | solution.py:697
  20.5 395.6 %all-gather.23.cloned.1.call-start = ((), (), s32[]{:S(2)}) async-start(), calls=%async_computation.10 | async-start | bytes 5308416 | tf_op jit(solution)/shard_map/all_gather | solution.py:697
  20.5 38.6 %collective-permute-start = (bf16[512,1536]{1,0:T(8,128)(2,1)S(1)}, bf16[512,1536]{1,0:T(8,128)(2,1)}, u32[]{:S(2)}, u32[]{:S(2)}) collective-permute-start(bf16[512,1536]{1,0:T(8,128)(2,1)S(1)} %bitcast.291), channel_id=1, source_target_pairs={{0,1},{1,2},{2,3},{4,5},{5,6},{6,7},{8,9},{9,10},{10,11},{12,13},{... | collective-permute-start | bytes 4718600 | tf_op jit(solution)/shard_map/ppermute | solution.py:67
  26.6 37.7 %collective-permute-start.1 = (bf16[512,1536]{1,0:T(8,128)(2,1)S(1)}, bf16[512,1536]{1,0:T(8,128)(2,1)S(1)}, u32[]{:S(2)}, u32[]{:S(2)}) collective-permute-start(bf16[512,1536]{1,0:T(8,128)(2,1)S(1)} %bitcast.292), channel_id=1, source_target_pairs={{1,0},{2,1},{3,2},{5,4},{6,5},{7,6},{9,8},{10,9},{11,10},{13,12},{... | collective-permute-start | bytes 4718600 | tf_op jit(solution)/shard_map/ppermute | solution.py:68
  66.2 38.5 %collective-permute-start.3 = (bf16[512,1536]{1,0:T(8,128)(2,1)S(1)}, bf16[512,1536]{1,0:T(8,128)(2,1)}, u32[]{:S(2)}, u32[]{:S(2)}) collective-permute-start(bf16[512,1536]{1,0:T(8,128)(2,1)S(1)} %collective-permute-done.1), channel_id=1, source_target_pairs={{1,0},{2,1},{5,4},{6,5},{9,8},{10,9},{13,12},{14,13},{17,16},{18,1... | collective-permute-start | bytes 4718600 | tf_op jit(solution)/shard_map/ppermute | solution.py:68
  67.5 44.4 %collective-permute-start.15 = (s32[9,512]{1,0:T(8,128)S(1)}, s32[9,512]{1,0:T(8,128)S(1)}, u32[]{:S(2)}, u32[]{:S(2)}) collective-permute-start(s32[9,512]{1,0:T(8,128)S(1)} %pad_add_fusion), channel_id=1, source_target_pairs={{0,1},{1,2},{2,3},{4,5},{5,6},{6,7},{8,9},{9,10},{10,11},{12,13},{... | collective-permute-start | bytes 55304 | tf_op jit(solution)/shard_map/ppermute | solution.py:67
  73.3 38.6 %collective-permute-start.16 = (s32[9,512]{1,0:T(8,128)S(1)}, s32[9,512]{1,0:T(8,128)S(1)}, u32[]{:S(2)}, u32[]{:S(2)}) collective-permute-start(s32[9,512]{1,0:T(8,128)S(1)} %pad_add_fusion), channel_id=1, source_target_pairs={{1,0},{2,1},{3,2},{5,4},{6,5},{7,6},{9,8},{10,9},{11,10},{13,12},{... | collective-permute-start | bytes 55304 | tf_op jit(solution)/shard_map/ppermute | solution.py:68
  76.7 1016.9 %reduce-scatter.8.cloned.1.call-start = ((), (), s32[]{:S(2)}) async-start(), calls=%async_computation.12 | async-start | bytes 5308416 | tf_op jit(solution)/shard_map/reduce_scatter | solution.py:869
  104.7 48.9 %collective-permute-start.4 = (bf16[512,1536]{1,0:T(8,128)(2,1)}, bf16[512,1536]{1,0:T(8,128)(2,1)}, u32[]{:S(2)}, u32[]{:S(2)}) collective-permute-start(bf16[512,1536]{1,0:T(8,128)(2,1)} %collective-permute-done.2), channel_id=1, source_target_pairs={{2,3},{6,7},{10,11},{14,15},{18,19},{22,23},{26,27},{30,31}} | collective-permute-start | bytes 4718600 | tf_op jit(solution)/shard_map/ppermute | solution.py:67
  106.6 47.0 %collective-permute-start.5 = (bf16[512,1536]{1,0:T(8,128)(2,1)}, bf16[512,1536]{1,0:T(8,128)(2,1)}, u32[]{:S(2)}, u32[]{:S(2)}) collective-permute-start(bf16[512,1536]{1,0:T(8,128)(2,1)} %collective-permute-done.3), channel_id=1, source_target_pairs={{1,0},{5,4},{9,8},{13,12},{17,16},{21,20},{25,24},{29,28}} | collective-permute-start | bytes 4718600 | tf_op jit(solution)/shard_map/ppermute | solution.py:68
  313.5 38.1 %collective-permute-start.24 = (bf16[512,1536]{1,0:T(8,128)(2,1)}, bf16[512,1536]{1,0:T(8,128)(2,1)S(1)}, u32[]{:S(2)}, u32[]{:S(2)}) collective-permute-start(bf16[512,1536]{1,0:T(8,128)(2,1)} %collective-permute-done.22), channel_id=1, source_target_pairs={{1,0},{2,1},{5,4},{6,5},{9,8},{10,9},{13,12},{14,13},{17,16},{18,1... | collective-permute-start | bytes 4718600 | tf_op jit(solution)/shard_map/ppermute | solution.py:68
  353.9 37.3 %collective-permute-start.26 = (bf16[512,1536]{1,0:T(8,128)(2,1)S(1)}, bf16[512,1536]{1,0:T(8,128)(2,1)S(1)}, u32[]{:S(2)}, u32[]{:S(2)}) collective-permute-start(bf16[512,1536]{1,0:T(8,128)(2,1)S(1)} %collective-permute-done.24), channel_id=1, source_target_pairs={{1,0},{5,4},{9,8},{13,12},{17,16},{21,20},{25,24},{29,28}} | collective-permute-start | bytes 4718600 | tf_op jit(solution)/shard_map/ppermute | solution.py:68
  541.1 39.5 %collective-permute-start.31 = (bf16[512,1536]{1,0:T(8,128)(2,1)}, bf16[512,1536]{1,0:T(8,128)(2,1)}, u32[]{:S(2)}, u32[]{:S(2)}) collective-permute-start(bf16[512,1536]{1,0:T(8,128)(2,1)} %get-tuple-element.345), channel_id=1, source_target_pairs={{0,1},{1,2},{2,3},{4,5},{5,6},{6,7},{8,9},{9,10},{10,11},{12,13},{... | collective-permute-start | bytes 4718600 | tf_op jit(solution)/shard_map/ppermute | solution.py:134
  597.0 48.4 %collective-permute-start.36 = (bf16[512,1536]{1,0:T(8,128)(2,1)S(1)}, bf16[512,1536]{1,0:T(8,128)(2,1)S(1)}, u32[]{:S(2)}, u32[]{:S(2)}) collective-permute-start(bf16[512,1536]{1,0:T(8,128)(2,1)S(1)} %get-tuple-element.353.tok_ref), channel_id=1, source_target_pairs={{0,1},{1,2},{2,3},{4,5},{5,6},{6,7},{8,9},{9,10},{10,11},{12,13},{... | collective-permute-start | bytes 4718600 | tf_op jit(solution)/shard_map/ppermute | solution.py:67
  598.6 46.9 %collective-permute-start.37 = (bf16[512,1536]{1,0:T(8,128)(2,1)S(1)}, bf16[512,1536]{1,0:T(8,128)(2,1)S(1)}, u32[]{:S(2)}, u32[]{:S(2)}) collective-permute-start(bf16[512,1536]{1,0:T(8,128)(2,1)S(1)} %get-tuple-element.353.tok_ref), channel_id=1, source_target_pairs={{1,0},{2,1},{3,2},{5,4},{6,5},{7,6},{9,8},{10,9},{11,10},{13,12},{... | collective-permute-start | bytes 4718600 | tf_op jit(solution)/shard_map/ppermute | solution.py:68
  599.9 45.5 %collective-permute-start.38 = (f32[1,512]{1,0:T(1,128)S(1)}, f32[1,512]{1,0:T(1,128)S(1)}, u32[]{:S(2)}, u32[]{:S(2)}) collective-permute-start(f32[1,512]{1,0:T(1,128)S(1)} %bitcast.274), channel_id=1, source_target_pairs={{0,1},{1,2},{2,3},{4,5},{5,6},{6,7},{8,9},{9,10},{10,11},{12,13},{... | collective-permute-start | bytes 6152 | tf_op jit(solution)/shard_map/ppermute | solution.py:67
  604.4 41.0 %collective-permute-start.39 = (f32[1,512]{1,0:T(1,128)S(1)}, f32[1,512]{1,0:T(1,128)S(1)}, u32[]{:S(2)}, u32[]{:S(2)}) collective-permute-start(f32[1,512]{1,0:T(1,128)S(1)} %bitcast.275), channel_id=1, source_target_pairs={{1,0},{2,1},{3,2},{5,4},{6,5},{7,6},{9,8},{10,9},{11,10},{13,12},{... | collective-permute-start | bytes 6152 | tf_op jit(solution)/shard_map/ppermute | solution.py:68
  605.7 39.7 %collective-permute-start.40 = (f32[1,1]{1,0:T(1,128)}, f32[1,1]{1,0:T(1,128)}, u32[]{:S(2)}, u32[]{:S(2)}) collective-permute-start(f32[1,1]{1,0:T(1,128)} %bitcast.67), channel_id=1, source_target_pairs={{0,1},{1,0},{2,3},{3,2},{4,5},{5,4},{6,7},{7,6},{8,9},{9,8},{10,11... | collective-permute-start | bytes 20 | tf_op jit(solution)/shard_map/ppermute | solution.py:165
  646.2 51.5 %collective-permute-start.41 = (bf16[512,1536]{1,0:T(8,128)(2,1)S(1)}, bf16[512,1536]{1,0:T(8,128)(2,1)S(1)}, u32[]{:S(2)}, u32[]{:S(2)}) collective-permute-start(bf16[512,1536]{1,0:T(8,128)(2,1)S(1)} %collective-permute-done.36), channel_id=1, source_target_pairs={{1,2},{2,3},{5,6},{6,7},{9,10},{10,11},{13,14},{14,15},{17,18},{18... | collective-permute-start | bytes 4718600 | tf_op jit(solution)/shard_map/ppermute | solution.py:67
  647.0 50.7 %collective-permute-start.42 = (bf16[512,1536]{1,0:T(8,128)(2,1)S(1)}, bf16[512,1536]{1,0:T(8,128)(2,1)S(1)}, u32[]{:S(2)}, u32[]{:S(2)}) collective-permute-start(bf16[512,1536]{1,0:T(8,128)(2,1)S(1)} %collective-permute-done.37), channel_id=1, source_target_pairs={{1,0},{2,1},{5,4},{6,5},{9,8},{10,9},{13,12},{14,13},{17,16},{18,1... | collective-permute-start | bytes 4718600 | tf_op jit(solution)/shard_map/ppermute | solution.py:68
  648.3 49.4 %collective-permute-start.43 = (f32[1,512]{1,0:T(1,128)S(1)}, f32[1,512]{1,0:T(1,128)S(1)}, u32[]{:S(2)}, u32[]{:S(2)}) collective-permute-start(f32[1,512]{1,0:T(1,128)S(1)} %collective-permute-done.38), channel_id=1, source_target_pairs={{1,2},{2,3},{5,6},{6,7},{9,10},{10,11},{13,14},{14,15},{17,18},{18... | collective-permute-start | bytes 6152 | tf_op jit(solution)/shard_map/ppermute | solution.py:67
  649.0 48.8 %collective-permute-start.44 = (f32[1,512]{1,0:T(1,128)S(1)}, f32[1,512]{1,0:T(1,128)S(1)}, u32[]{:S(2)}, u32[]{:S(2)}) collective-permute-start(f32[1,512]{1,0:T(1,128)S(1)} %collective-permute-done.39), channel_id=1, source_target_pairs={{1,0},{2,1},{5,4},{6,5},{9,8},{10,9},{13,12},{14,13},{17,16},{18,1... | collective-permute-start | bytes 6152 | tf_op jit(solution)/shard_map/ppermute | solution.py:68
  652.2 45.5 %collective-permute-start.45 = (f32[1,1]{1,0:T(1,128)}, f32[1,1]{1,0:T(1,128)}, u32[]{:S(2)}, u32[]{:S(2)}) collective-permute-start(f32[1,1]{1,0:T(1,128)} %add.445), channel_id=1, source_target_pairs={{0,2},{1,3},{2,0},{3,1},{4,6},{5,7},{6,4},{7,5},{8,10},{9,11},{10,... | collective-permute-start | bytes 20 | tf_op jit(solution)/shard_map/ppermute | solution.py:165
  699.2 47.0 %collective-permute-start.46 = (bf16[512,1536]{1,0:T(8,128)(2,1)S(1)}, bf16[512,1536]{1,0:T(8,128)(2,1)S(1)}, u32[]{:S(2)}, u32[]{:S(2)}) collective-permute-start(bf16[512,1536]{1,0:T(8,128)(2,1)S(1)} %collective-permute-done.41), channel_id=1, source_target_pairs={{2,3},{6,7},{10,11},{14,15},{18,19},{22,23},{26,27},{30,31}} | collective-permute-start | bytes 4718600 | tf_op jit(solution)/shard_map/ppermute | solution.py:67
  700.0 46.2 %collective-permute-start.47 = (bf16[512,1536]{1,0:T(8,128)(2,1)S(1)}, bf16[512,1536]{1,0:T(8,128)(2,1)S(1)}, u32[]{:S(2)}, u32[]{:S(2)}) collective-permute-start(bf16[512,1536]{1,0:T(8,128)(2,1)S(1)} %collective-permute-done.42), channel_id=1, source_target_pairs={{1,0},{5,4},{9,8},{13,12},{17,16},{21,20},{25,24},{29,28}} | collective-permute-start | bytes 4718600 | tf_op jit(solution)/shard_map/ppermute | solution.py:68
  701.3 42.0 %collective-permute-start.48 = (f32[1,512]{1,0:T(1,128)S(1)}, f32[1,512]{1,0:T(1,128)S(1)}, u32[]{:S(2)}, u32[]{:S(2)}) collective-permute-start(f32[1,512]{1,0:T(1,128)S(1)} %collective-permute-done.43), channel_id=1, source_target_pairs={{2,3},{6,7},{10,11},{14,15},{18,19},{22,23},{26,27},{30,31}} | collective-permute-start | bytes 6152 | tf_op jit(solution)/shard_map/ppermute | solution.py:67
  702.0 44.2 %collective-permute-start.49 = (f32[1,512]{1,0:T(1,128)S(1)}, f32[1,512]{1,0:T(1,128)S(1)}, u32[]{:S(2)}, u32[]{:S(2)}) collective-permute-start(f32[1,512]{1,0:T(1,128)S(1)} %collective-permute-done.44), channel_id=1, source_target_pairs={{1,0},{5,4},{9,8},{13,12},{17,16},{21,20},{25,24},{29,28}} | collective-permute-start | bytes 6152 | tf_op jit(solution)/shard_map/ppermute | solution.py:68
  705.6 37.7 %collective-permute-start.50 = (f32[1,1]{1,0:T(1,128)}, f32[1,1]{1,0:T(1,128)}, u32[]{:S(2)}, u32[]{:S(2)}) collective-permute-start(f32[1,1]{1,0:T(1,128)} %add.446), channel_id=1, source_target_pairs={{0,4},{4,0},{8,12},{12,8},{16,20},{20,16},{24,28},{28,24},{1,5},{5... | collective-permute-start | bytes 20 | tf_op jit(solution)/shard_map/ppermute | solution.py:165
  789.3 53.6 %collective-permute-start.51 = (bf16[512,1536]{1,0:T(8,128)(2,1)S(1)}, bf16[512,1536]{1,0:T(8,128)(2,1)S(1)}, u32[]{:S(2)}, u32[]{:S(2)}) collective-permute-start(bf16[512,1536]{1,0:T(8,128)(2,1)S(1)} %get-tuple-element.428), channel_id=1, source_target_pairs={{0,1},{4,5},{8,9},{12,13},{16,17},{20,21},{24,25},{28,29}} | collective-permute-start | bytes 4718600 | tf_op jit(solution)/shard_map/ppermute | solution.py:134
  804.8 38.2 %collective-permute-start.52 = (bf16[512,1536]{1,0:T(8,128)(2,1)S(1)}, bf16[512,1536]{1,0:T(8,128)(2,1)S(1)}, u32[]{:S(2)}, u32[]{:S(2)}) collective-permute-start(bf16[512,1536]{1,0:T(8,128)(2,1)S(1)} %get-tuple-element.429), channel_id=1, source_target_pairs={{3,2},{7,6},{11,10},{15,14},{19,18},{23,22},{27,26},{31,30}} | collective-permute-start | bytes 4718600 | tf_op jit(solution)/shard_map/ppermute | solution.py:135
  885.4 42.0 %collective-permute-start.59 = (bf16[512,1536]{1,0:T(8,128)(2,1)S(1)}, bf16[512,1536]{1,0:T(8,128)(2,1)S(1)}, u32[]{:S(2)}, u32[]{:S(2)}) collective-permute-start(bf16[512,1536]{1,0:T(8,128)(2,1)S(1)} %get-tuple-element.456), channel_id=1, source_target_pairs={{0,1},{1,2},{2,3},{4,5},{5,6},{6,7},{8,9},{9,10},{10,11},{12,13},{... | collective-permute-start | bytes 4718600 | tf_op jit(solution)/shard_map/ppermute | solution.py:134
  988.8 182.4 %reduce-scatter.6.cloned.1.call-start = ((), (), s32[]{:S(2)}) async-start(), calls=%async_computation.11 | async-start | bytes 17694720 | tf_op jit(solution)/shard_map/reduce_scatter | solution.py:852
  989.6 286.3 %reduce-scatter.10.cloned.1.call-start = ((), (), s32[]{:S(2)}) async-start(), calls=%async_computation.14 | async-start | bytes 2654208
  990.0 103.5 %collective-permute-start.67 = (bf16[2,10,192,512]{3,2,1,0:T(8,128)(2,1)}, bf16[2,10,192,512]{3,2,1,0:T(8,128)(2,1)}, u32[]{:S(2)}, u32[]{:S(2)}) collective-permute-start(bf16[2,10,192,512]{3,2,1,0:T(8,128)(2,1)} %get-tuple-element.484), channel_id=1, source_target_pairs={{0,8},{4,12},{8,0},{12,4},{16,24},{20,28},{24,16},{28,20},{1,9},{5... | collective-permute-start | bytes 11796488 | tf_op jit(solution)/shard_map/ppermute | solution.py:165
  990.1 103.5 %collective-permute-start.68 = (bf16[2,10,192,512]{3,2,1,0:T(8,128)(2,1)}, bf16[2,10,192,512]{3,2,1,0:T(8,128)(2,1)}, u32[]{:S(2)}, u32[]{:S(2)}) collective-permute-start(bf16[2,10,192,512]{3,2,1,0:T(8,128)(2,1)} %get-tuple-element.485), channel_id=1, source_target_pairs={{0,16},{4,20},{8,24},{12,28},{16,0},{20,4},{24,8},{28,12},{1,17},{... | collective-permute-start | bytes 11796488 | tf_op jit(solution)/shard_map/ppermute | solution.py:165
  1181.6 37.0 %collective-permute-start.69 = (bf16[512,1536]{1,0:T(8,128)(2,1)S(1)}, bf16[512,1536]{1,0:T(8,128)(2,1)S(1)}, u32[]{:S(2)}, u32[]{:S(2)}) collective-permute-start(bf16[512,1536]{1,0:T(8,128)(2,1)S(1)} %get-tuple-element.493), channel_id=1, source_target_pairs={{0,1},{4,5},{8,9},{12,13},{16,17},{20,21},{24,25},{28,29}} | collective-permute-start | bytes 4718600 | tf_op jit(solution)/shard_map/ppermute | solution.py:134
  1221.2 37.4 %collective-permute-start.71 = (bf16[512,1536]{1,0:T(8,128)(2,1)}, bf16[512,1536]{1,0:T(8,128)(2,1)}, u32[]{:S(2)}, u32[]{:S(2)}) collective-permute-start(bf16[512,1536]{1,0:T(8,128)(2,1)} %get-tuple-element.501), channel_id=1, source_target_pairs={{0,1},{1,2},{4,5},{5,6},{8,9},{9,10},{12,13},{13,14},{16,17},{17,1... | collective-permute-start | bytes 4718600 | tf_op jit(solution)/shard_map/ppermute | solution.py:134
  1231.1 104.2 %all-reduce.4.cloned.1.call-start = ((), (), s32[]{:S(2)}) async-start(), calls=%async_computation.13 | async-start | bytes 1179648 | tf_op jit(solution)/shard_map/psum | solution.py:877
  1264.1 57.1 %collective-permute-start.73 = (bf16[512,1536]{1,0:T(8,128)(2,1)}, bf16[512,1536]{1,0:T(8,128)(2,1)S(1)}, u32[]{:S(2)}, u32[]{:S(2)}) collective-permute-start(bf16[512,1536]{1,0:T(8,128)(2,1)} %get-tuple-element.505), channel_id=1, source_target_pairs={{0,1},{1,2},{2,3},{4,5},{5,6},{6,7},{8,9},{9,10},{10,11},{12,13},{... | collective-permute-start | bytes 4718600 | tf_op jit(solution)/shard_map/ppermute | solution.py:134
  1272.4 55.0 %collective-permute-start.74 = (bf16[512,1536]{1,0:T(8,128)(2,1)}, bf16[512,1536]{1,0:T(8,128)(2,1)}, u32[]{:S(2)}, u32[]{:S(2)}) collective-permute-start(bf16[512,1536]{1,0:T(8,128)(2,1)} %get-tuple-element.506), channel_id=1, source_target_pairs={{1,0},{2,1},{3,2},{5,4},{6,5},{7,6},{9,8},{10,9},{11,10},{13,12},{... | collective-permute-start | bytes 4718600 | tf_op jit(solution)/shard_map/ppermute | solution.py:135
  1273.7 61.6 %collective-permute-start.75 = (bf16[1,10,192,512]{3,2,1,0:T(8,128)(2,1)}, bf16[1,10,192,512]{3,2,1,0:T(8,128)(2,1)}, u32[]{:S(2)}, u32[]{:S(2)}) collective-permute-start(bf16[1,10,192,512]{3,2,1,0:T(8,128)(2,1)} %add_convert_fusion.7), channel_id=1, source_target_pairs={{0,16},{4,20},{8,24},{12,28},{16,0},{20,4},{24,8},{28,12},{1,17},{... | collective-permute-start | bytes 5898248 | tf_op jit(solution)/shard_map/ppermute | solution.py:165
  1275.1 60.2 %collective-permute-start.76 = (bf16[1,10,192,512]{3,2,1,0:T(8,128)(2,1)}, bf16[1,10,192,512]{3,2,1,0:T(8,128)(2,1)}, u32[]{:S(2)}, u32[]{:S(2)}) collective-permute-start(bf16[1,10,192,512]{3,2,1,0:T(8,128)(2,1)} %add_convert_fusion.6), channel_id=1, source_target_pairs={{0,8},{4,12},{8,0},{12,4},{16,24},{20,28},{24,16},{28,20},{1,9},{5... | collective-permute-start | bytes 5898248 | tf_op jit(solution)/shard_map/ppermute | solution.py:165
  (187 other events, 3360.4 us)
Sparse Core Ops, SparseCore 0:
  10.5 30.0 all-gather.8
  42.4 38.9 all-gather.10
  83.9 67.0 all-gather.12
  153.3 66.5 all-gather.14
  222.2 65.4 all-gather.16
  289.5 38.9 all-gather.18
  330.4 38.9 all-gather.20
  371.2 38.9 all-gather.22
  988.9 69.3 reduce-scatter.7
  1062.0 109.1 reduce-scatter.5
  1231.2 41.8 reduce-scatter.9
  1276.0 50.6 all-reduce.3

commit v6 on v4

--- a/solution.py
+++ b/solution.py
@@ -73,7 +73,7 @@
     n = lax.axis_size("seq")
     rights, lefts = [block], [block]
     for k in range(1, n):
-        right, left = line_move(rights[-1], lefts[-1], k)
+        right, left = tie(*line_move(rights[-1], lefts[-1], k))
         rights.append(right)
         lefts.append(left)
     return nearest(rights, lefts)
@@ -177,22 +177,48 @@
     return tuple(bits), tuple(bits[:1] + bits[:0:-1])
 
 
-def doubling_gather(block, bits):
-    blocks = block[None]
-    for bit in bits:
-        blocks = jnp.concatenate([blocks, swap(blocks, "fsdp", bit)])
-    return blocks
-
-
-def halve(keep, here):
-    half = keep.shape[0] // 2
-    if half == 0:
-        return keep[0].astype(full) + here[0].astype(full)
-    added = [
-        (keep[cut].astype(full) + here[cut].astype(full)).astype(low)
-        for cut in (slice(half, None), slice(0, half))
-    ]
-    return tuple(added)
+def total_steps(value, *axes):
+    for axis in axes:
+        for step in range(lax.axis_size(axis).bit_length() - 1):
+            here = swap(value, axis, 1 << step)
+            here = yield here
+            value = value + here
+    while True:
+        yield value
+
+
+class Halving:
+    def __init__(self, keep, send, bits):
+        self.terms, self.send, self.bits = [keep], send, list(bits)
+
+    def go(self):
+        self.terms = self.terms + [swap(self.send, "fsdp", self.bits.pop(0))]
+
+    def add(self):
+        half = self.terms[0].shape[0] // 2
+        if half:
+            self.send = sum(term[half:].astype(full) for term in self.terms).astype(low)
+            self.terms = [term[:half] for term in self.terms]
+
+    def finish(self):
+        while self.bits:
+            self.go()
+            self.add()
+        return sum(term[0].astype(full) for term in self.terms)
+
+
+def land(sums, *others):
+    tied = tie([each.terms[-1] for each in sums], *others)
+    for each, here in zip(sums, tied[0]):
+        each.terms = each.terms[:-1] + [here]
+    return tied[1:]
+
+
+def leave(sums, *others):
+    tied = tie([each.send for each in sums], *others)
+    for each, send in zip(sums, tied[0]):
+        each.send = send
+    return tied[1:]
 
 
 def nt(a, b):
@@ -362,10 +388,21 @@
     return ref[pl.ds(row, 1), :]
 
 
+def join_down(rows, block_ref, down_ref):
+    hidden, width = down_ref.shape
+    chunks = width // hidden
+    for dev in range(hidden // rows):
+        for chunk in range(chunks):
+            start = (dev * chunks + chunk) * rows
+            down_ref[dev * rows : (dev + 1) * rows, chunk * hidden : (chunk + 1) * hidden] = (
+                block_ref[0, start : start + rows, :]
+            )
+
+
 def experts_kernel(
-    at_ref, tok_ref, slot_ref, member_ref, router_ref, wg_ref, wu_ref, wd_ref, *refs
+    few, at_ref, tok_ref, slot_ref, member_ref, router_ref, wgu_ref, wd_ref, *refs
 ):
-    part_ref, x_ref, g_ref, u_ref, gates_ref, acc, gates_all = refs[-7:]
+    part_ref, x_ref, gu_ref, gates_ref, acc, gates_all, down = refs[-7:]
     e, experts = pl.program_id(0), pl.num_programs(0)
     slots = x_ref.shape[2]
 
@@ -384,12 +421,13 @@
     here = place == own_row(slot_ref, e)
     x = nn(jnp.where(here, 1.0, 0.0).astype(low), tok_ref[...]).astype(low)
     x_ref[0, 0] = x
-    g = nn(x, wg_ref[0])
-    u = nn(x, wu_ref[0])
-    g_ref[0, 0] = g.astype(low)
-    u_ref[0, 0] = u.astype(low)
+    gu = nn(x, wgu_ref[0])
+    gu_ref[0, 0] = gu.astype(low)
+    hidden = gu.shape[1] // 2
+    g, u = gu[:, :hidden], gu[:, hidden:]
     act = (g * jax.nn.sigmoid(g) * u).astype(low)
-    y = nn(act, wd_ref[0]).astype(low)
+    join_down(few, wd_ref, down)
+    y = nn(act, down[...]).astype(low)
     acc[...] += tn(jnp.where(here, gate_row, 0.0).astype(low), y)
 
     @pl.when(e == experts - 1)
@@ -398,11 +436,11 @@
 
 
 def back_kernel(
-    at_ref, tok_ref, slot_ref, gates_ref, mix_ref, router_ref, g_ref, u_ref, wg_ref, wu_ref, wd_ref, *refs
+    few, at_ref, tok_ref, slot_ref, gates_ref, mix_ref, router_ref, gu_ref, wgu_ref, wd_ref, *refs
 ):
-    part_ref, d_ref, dgu_ref, act_ref, dlog_ref, acc, dlog_all = refs[-7:]
+    part_ref, d_ref, dgu_ref, act_ref, dlog_ref, acc, dlog_all, down = refs[-8:]
     e, experts = pl.program_id(0), pl.num_programs(0)
-    slots, hidden = g_ref.shape[2:]
+    slots, hidden = gu_ref.shape[2], gu_ref.shape[3] // 2
 
     @pl.when(e == 0)
     def _():
@@ -416,8 +454,9 @@
     gate = jnp.sum(jnp.where(here, gate_row, 0.0), axis=1, keepdims=True)
     d = nn(pick, tok_ref[...]).astype(low)
     d_ref[0, 0] = d
-    d_act = nt(d, wd_ref[0])
-    g, u = g_ref[0, 0].astype(full), u_ref[0, 0].astype(full)
+    join_down(few, wd_ref, down)
+    d_act = nt(d, down[...])
+    g, u = gu_ref[0, 0, :, :hidden].astype(full), gu_ref[0, 0, :, hidden:].astype(full)
     sig = jax.nn.sigmoid(g)
     silu = g * sig
     act = silu * u
@@ -430,7 +469,7 @@
     d_u = (d_act * silu).astype(low)
     dgu_ref[0, 0, :, :hidden] = d_g
     dgu_ref[0, 0, :, hidden:] = d_u
-    dx = (nt(d_g, wg_ref[0]) + nt(d_u, wu_ref[0])).astype(low)
+    dx = nt(dgu_ref[0, 0], wgu_ref[0]).astype(low)
     acc[...] += tn(pick, dx)
 
     @pl.when(e == experts - 1)
@@ -475,67 +514,73 @@
     )(at, *inputs, *buffers)
 
 
-def experts_forward(turn, devs, at, tokens, slot_of, member, router, w_gate, w_up, w_down, slots, buffers):
-    experts, width, hidden = w_gate.shape
+def weight_specs(width, hidden):
+    return [
+        pl.BlockSpec((1, width, 2 * hidden), lambda e, at: (e, 0, 0)),
+        pl.BlockSpec((1, width, hidden), lambda e, at: (e, 0, 2)),
+    ]
+
+
+def experts_forward(turn, devs, at, tokens, slot_of, member, router, weights, few, slots, buffers):
+    experts, width, columns = weights.shape
+    hidden = columns // 3
     count = tokens.shape[0]
     total_experts = member.shape[0]
     return shard_call(
-        experts_kernel,
+        functools.partial(experts_kernel, few),
         "experts_forward",
         at,
-        [tokens, slot_of, member, router, w_gate, w_up, w_down],
+        [tokens, slot_of, member, router, weights, weights],
         [
             same(count, width),
             same(experts, count),
             same(total_experts, count),
             same(total_experts, width),
-            by_expert(width, hidden),
-            by_expert(width, hidden),
-            by_expert(hidden, width),
+            *weight_specs(width, hidden),
         ],
         [
             in_place(count, width),
             in_turn(turn, slots, width),
-            in_turn(turn, slots, hidden),
-            in_turn(turn, slots, hidden),
+            in_turn(turn, slots, 2 * hidden),
             same(experts, count),
         ],
         [
             jax.ShapeDtypeStruct((devs, count, width), low),
             jax.ShapeDtypeStruct((experts, devs, slots, width), low),
-            jax.ShapeDtypeStruct((experts, devs, slots, hidden), low),
-            jax.ShapeDtypeStruct((experts, devs, slots, hidden), low),
+            jax.ShapeDtypeStruct((experts, devs, slots, 2 * hidden), low),
             jax.ShapeDtypeStruct((experts, count), full),
         ],
         buffers,
-        [pltpu.VMEM((count, width), full), pltpu.VMEM((total_experts, count), full)],
+        [
+            pltpu.VMEM((count, width), full),
+            pltpu.VMEM((total_experts, count), full),
+            pltpu.VMEM((hidden, width), low),
+        ],
         experts,
     )
 
 
 def experts_backward(
-    turn, devs, at, d_tokens, slot_of, gates, mix_dot, router, g, u, w_gate, w_up, w_down, buffers
+    turn, devs, at, d_tokens, slot_of, gates, mix_dot, router, gu, weights, few, buffers
 ):
-    experts, width, hidden = w_gate.shape
+    experts, width, columns = weights.shape
+    hidden = columns // 3
     count = d_tokens.shape[0]
-    slots = g.shape[2]
+    slots = gu.shape[2]
     lines = router.shape[0]
     return shard_call(
-        back_kernel,
+        functools.partial(back_kernel, few),
         "experts_backward",
         at,
-        [d_tokens, slot_of, gates, mix_dot, router, g, u, w_gate, w_up, w_down],
+        [d_tokens, slot_of, gates, mix_dot, router, gu, weights, weights],
         [
             same(count, width),
             same(experts, count),
             same(experts, count),
             same(1, count),
             same(lines, width),
-            in_turn(turn, slots, hidden),
-            in_turn(turn, slots, hidden),
-            by_expert(width, hidden),
-            by_expert(width, hidden),
-            by_expert(hidden, width),
+            in_turn(turn, slots, 2 * hidden),
+            *weight_specs(width, hidden),
         ],
         [
             in_place(count, width),
@@ -552,7 +597,11 @@
             jax.ShapeDtypeStruct((lines, count), low),
         ],
         buffers,
-        [pltpu.VMEM((count, width), full), pltpu.VMEM((lines, count), full)],
+        [
+            pltpu.VMEM((count, width), full),
+            pltpu.VMEM((lines, count), full),
+            pltpu.VMEM((hidden, width), low),
+        ],
         experts,
     )
 
@@ -564,89 +613,53 @@
     return masks
 
 
-def gate_up_kernel(bits_a, bits_b, me_ref, x_ref, dgu_ref, *refs):
-    outs, acc = refs[:4], refs[4]
-    hidden = outs[0].shape[3]
-    acc[...] = tn(x_ref[0], dgu_ref[0])
+def grads_kernel(bits_a, bits_b, me_ref, x_ref, dgu_ref, act_ref, d_ref, *refs):
+    outs, gu_acc, down_acc = refs[-6:-2], refs[-2], refs[-1]
+    hidden, width = act_ref.shape[2], d_ref.shape[2]
+    gu_acc[...] = tn(x_ref[0], dgu_ref[0])
+    down_acc[...] = tn(act_ref[0], d_ref[0])
+    chunks = width // hidden
     for part, bits in enumerate((bits_a, bits_b)):
         keep, send = outs[2 * part], outs[2 * part + 1]
         rows = keep.shape[2]
+        few = rows // chunks
         for place, mask in enumerate(halving_masks(bits)):
+            out = keep if place < keep.shape[0] else send
+            spot = place % keep.shape[0]
             start = pl.multiple_of((me_ref[0] ^ mask) * rows, rows)
-            out = keep if place < keep.shape[0] else send
-            block = acc[pl.ds(start, rows), part * hidden : (part + 1) * hidden]
-            out[place % keep.shape[0], 0] = block.astype(low)
-
-
-def gate_up_grads(me, rows, d_gu, bits_a, bits_b):
+            block = gu_acc[pl.ds(start, rows), part * hidden : (part + 1) * hidden]
+            out[spot, 0, :, :hidden] = block.astype(low)
+            start = pl.multiple_of((me_ref[0] ^ mask) * few, few)
+            for chunk in range(chunks):
+                first = part * (width // 2) + chunk * (hidden // 2)
+                block = down_acc[pl.ds(start, few), first : first + hidden // 2]
+                out[spot, 0, chunk * few : (chunk + 1) * few, hidden:] = block.astype(low)
+
+
+def weight_grads(me, rows, d_gu, act, d_rows, bits_a, bits_b, first, stop, buffers):
     experts, count, width = rows.shape
-    hidden = d_gu.shape[2] // 2
+    hidden = act.shape[2]
     devs = 2 ** len(bits_a)
-    shape = (width // devs, hidden)
-    outs = pl.pallas_call(
-        functools.partial(gate_up_kernel, bits_a, bits_b),
+    shape = (width // devs, hidden + hidden // 2)
+
+    def part(*block):
+        return pl.BlockSpec((1,) + block, lambda e, me: (first + e, 0, 0))
+
+    return pl.pallas_call(
+        functools.partial(grads_kernel, bits_a, bits_b),
         grid_spec=pltpu.PrefetchScalarGridSpec(
             num_scalar_prefetch=1,
-            grid=(experts,),
-            in_specs=[by_expert(count, width), by_expert(count, 2 * hidden)],
-            out_specs=[pl.BlockSpec((devs // 2, 1) + shape, lambda e, me: (0, e, 0, 0))] * 4,
-            scratch_shapes=[pltpu.VMEM((width, 2 * hidden), full)],
+            grid=(stop - first,),
+            in_specs=[part(count, width), part(count, 2 * hidden), part(count, hidden), part(count, width)]
+            + [pl.BlockSpec(memory_space=pl.ANY)] * len(buffers),
+            out_specs=[pl.BlockSpec((devs // 2, 1) + shape, lambda e, me: (0, first + e, 0, 0))] * 4,
+            scratch_shapes=[pltpu.VMEM((width, 2 * hidden), full), pltpu.VMEM((hidden, width), full)],
         ),
         out_shape=[jax.ShapeDtypeStruct((devs // 2, experts) + shape, low)] * 4,
-        compiler_params=vmem(48),
-        name="gate_up_grads",
-    )(me, rows, d_gu)
-    return (outs[0], outs[1]), (outs[2], outs[3])
-
-
-def down_kernel(act_ref, d_ref, out_ref):
-    out_ref[0] = tn(act_ref[0], d_ref[0]).astype(low)
-
-
-def down_grads(act, d_rows):
-    experts, count, hidden = act.shape
-    width = d_rows.shape[2]
-    one = lambda *shape: pl.BlockSpec((1,) + shape, lambda e: (e, 0, 0))
-    return pl.pallas_call(
-        down_kernel,
-        grid=(experts,),
-        in_specs=[one(count, hidden), one(count, width)],
-        out_specs=one(hidden, width),
-        out_shape=jax.ShapeDtypeStruct((experts, hidden, width), low),
-        compiler_params=vmem(48),
-        name="down_grads",
-    )(act, d_rows)
-
-
-def join_kernel(me_ref, left_ref, right_ref, out_ref):
-    half = left_ref.shape[3]
-    out_ref[:, :, :half] = left_ref[0]
-    out_ref[:, :, half:] = right_ref[0]
-
-
-def join_rows(me, left, right, bits_left, bits_right):
-    devs, experts, rows, half = left.shape
-
-    def place(bits):
-        def index(block, me_ref):
-            mask = me_ref[0] ^ block
-            spot = sum(((mask // bit) % 2) * 2**i for i, bit in enumerate(bits))
-            return (spot, 0, 0, 0)
-
-        return pl.BlockSpec((1, experts, rows, half), index)
-
-    return pl.pallas_call(
-        join_kernel,
-        grid_spec=pltpu.PrefetchScalarGridSpec(
-            num_scalar_prefetch=1,
-            grid=(devs,),
-            in_specs=[place(bits_left), place(bits_right)],
-            out_specs=pl.BlockSpec((experts, rows, 2 * half), lambda block, me_ref: (0, block, 0)),
-        ),
-        out_shape=jax.ShapeDtypeStruct((experts, devs * rows, 2 * half), low),
-        compiler_params=vmem(40),
-        name="join_rows",
-    )(me, left, right)
+        input_output_aliases={5 + i: i for i in range(len(buffers))},
+        compiler_params=vmem(56),
+        name="weight_grads",
+    )(me, rows, d_gu, act, d_rows, *buffers)
 
 
 def shards(
@@ -686,20 +699,34 @@
 
     own_qkv = lax.dynamic_slice_in_dim(w_qkv, me * group_w, group_w, 1)
     small = jnp.concatenate([gain_one[:, None], gain_two[:, None], w_router], axis=1)
-    small = doubling_gather(small, order_a)
-    small = small[mine ^ jnp.arange(small.shape[0])].reshape(width, 2 + expert_total)
-    full_qkv = lax.all_gather(own_qkv, "fsdp", axis=0, tiled=True)
-    full_out = lax.all_gather(w_out, "fsdp", axis=0, tiled=True)
-    full_gate = lax.all_gather(w_gate, "fsdp", axis=1, tiled=True)
-    full_up = lax.all_gather(w_up, "fsdp", axis=1, tiled=True)
-    down_a, down_b = order_a[1:] + order_a[:1], order_b[1:] + order_b[:1]
-    full_down = join_rows(
-        mine.reshape(1),
-        doubling_gather(w_down[:, :, : width // 2], down_a),
-        doubling_gather(w_down[:, :, width // 2 :], down_b),
-        down_a,
-        down_b,
-    )
+    small = jnp.pad(small, ((0, 0), (0, -small.shape[1] % 128)))
+    first = lax.all_gather(
+        jnp.concatenate([own_qkv, small, w_out], axis=1), "fsdp", axis=0, tiled=True
+    )
+    full_qkv = first[:, :group_w]
+    small = first[:, group_w : group_w + 2 + expert_total]
+    full_out = first[:, -width:]
+    hidden_w = w_gate.shape[2]
+    down_chunks = [
+        w_down[:, :, start : start + hidden_w] for start in range(0, width, hidden_w)
+    ]
+    weights = lax.all_gather(
+        jnp.concatenate([w_gate, w_up, jnp.concatenate(down_chunks, axis=1)], axis=2),
+        "fsdp",
+        axis=1,
+        tiled=True,
+    )
+
+    routes_low = jnp.concatenate([routes.reshape(shard_len, top_count).T, valid_mask], axis=0)
+    routes_low = jnp.pad(
+        routes_low.astype(low), ((0, -routes_low.shape[0] % 16), (0, width - shard_len))
+    )
+    x_blocks = line_gather(jnp.concatenate([x_low, routes_low], axis=0))
+    routes_blocks = [
+        block[shard_len : shard_len + top_count + 1, :shard_len].astype(jnp.int32)
+        for block in x_blocks
+    ]
+    x_blocks = [block[:shard_len] for block in x_blocks]
     full_g1 = small[:, 0].astype(full)
     full_g2 = small[:, 1].astype(full)
     router = small[:, 2:].T
@@ -707,8 +734,7 @@
     own_router = jnp.pad(own_router, ((0, -experts_here % 16), (0, 0)))
     valid_rows = valid_mask.reshape(shard_len).astype(full)
 
-    routes_low = jnp.concatenate([routes.reshape(shard_len, top_count).T, valid_mask], axis=0)
-    routes_all = by_place(line_gather(routes_low))[order]
+    routes_all = by_place(routes_blocks)[order]
     valid_count = total(jnp.sum(routes_all[:, top_count]).astype(full).reshape(1, 1), "fsdp")[0, 0]
     expert_ids = jnp.arange(expert_total, dtype=jnp.int32)
     member = jnp.any(routes_all[:, :top_count, None, :] == expert_ids[:, None], axis=1)
@@ -718,7 +744,7 @@
     slot_of = jnp.where(own_member, slot_of, -1)
     member = member.astype(full)
 
-    x_all = by_place(line_gather(x_low)).reshape(seq_len, width)
+    x_all = by_place(x_blocks).reshape(seq_len, width)
     normed_one = rms_norm(x_all.astype(full), full_g1).astype(low)
     qkv_rows = dot("td,dc->ct", normed_one, full_qkv)
     qkv_rows = qkv_rows.reshape(kv_here, GROUP + 2, HEAD_DIM, seq_len)
@@ -748,7 +774,7 @@
             right, left = line_move(right, left, turn + 1)
         *buffers, shard_gates = experts_forward(
             turn, n, jnp.stack([order[turn], me]), tokens[turn], slot_of[turn], member[turn],
-            router, full_gate, full_up, full_down, slots, buffers,
+            router, weights, w_down.shape[1], slots, buffers,
         )
         if turn < n - 1:
             right, left, shard_gates = tie(right, left, shard_gates)
@@ -756,16 +782,18 @@
             lefts.append(left)
             tokens.append(arrived(rights, lefts, turn + 1))
         gates.append(shard_gates)
-    mix_parts, expert_in, gate_act, up_act = buffers
+    mix_parts, expert_in, gate_up = buffers
     right = left = None
     for k in range(n - 1, 0, -1):
-        right, left = line_pass(*line_send(mix_parts, k, right, left), k)
+        moving = tie(*line_send(mix_parts, k, right, left))
+        right, left = tie(*line_pass(*moving, k))
     mixture = line_end(mix_parts, right, left)
     output_f32 = hidden + resid_mult * mixture
     activations = output_f32.astype(low).reshape(1, shard_len, width)
     error_rows = output_f32 - teacher.astype(full).reshape(shard_len, width)
     weighted = valid_rows[:, None] * error_rows
-    squares = jnp.sum(weighted * error_rows)
+    loss_steps = total_steps(jnp.sum(weighted * error_rows).reshape(1, 1), "seq", "fsdp")
+    squares = next(loss_steps)
     d_out = weighted * (tokens_all / valid_count)
 
     d_mix = resid_mult * d_out
@@ -783,12 +811,13 @@
             right, left = line_move(right, left, turn + 1)
         *buffers, shard_logits = experts_backward(
             turn, n, jnp.stack([order[turn], me]), d_tokens, slot_of[turn], gates[turn], mix_dot,
-            own_router, gate_act, up_act, full_gate, full_up, full_down, buffers,
+            own_router, gate_up, weights, w_down.shape[1], buffers,
         )
         if turn < n - 1:
-            right, left, dot_right, dot_left, shard_logits = tie(
-                right, left, dot_right, dot_left, shard_logits
+            right, left, dot_right, dot_left, shard_logits, squares = tie(
+                right, left, dot_right, dot_left, shard_logits, squares
             )
+            squares = loss_steps.send(squares)
             rights.append(right)
             lefts.append(left)
             dot_rights.append(dot_right)
@@ -803,104 +832,106 @@
     act_low = act_low.reshape(experts_here, slot_rows, -1)
 
     right = left = None
+    grads = []
+    cut = (experts_here + 1) // 2
     for k in range(n - 1, 0, -1):
         moving = line_send(d_parts, k, right, left)
-        if k == n - 1:
-            moving, expert_in, d_gate_up = tie(moving, expert_in, d_gate_up)
+        if k >= n - 2:
+            moving, d_rows, grads = tie(moving, d_rows, grads)
             right, left = line_pass(*moving, k)
-            gate_pair, up_pair = gate_up_grads(
-                mine.reshape(1), expert_in, d_gate_up, order_a, order_b
+            part = (0, cut) if k == n - 1 else (cut, experts_here)
+            grads = weight_grads(
+                mine.reshape(1), expert_in, d_gate_up, act_low, d_rows, order_a, order_b, *part, grads
             )
-            right, left, gate_pair, up_pair = tie(right, left, gate_pair, up_pair)
-        elif k == n - 2:
-            moving, gate_pair, up_pair, act_low, d_rows = tie(
-                moving, gate_pair, up_pair, act_low, d_rows
-            )
-            right, left = line_pass(*moving, k)
-            gate_here = swap(gate_pair[1], "fsdp", order_a[0])
-            up_here = swap(up_pair[1], "fsdp", order_b[0])
-            down_part = down_grads(act_low, d_rows)
-            right, left, gate_here, up_here, down_part = tie(
-                right, left, gate_here, up_here, down_part
-            )
-        elif k == n - 3:
-            moving, gate_here, up_here = tie(moving, gate_here, up_here)
-            right, left = line_pass(*moving, k)
-            gate_send, gate_keep = halve(gate_pair[0], gate_here)
-            up_send, up_keep = halve(up_pair[0], up_here)
-            right, left, gate_send, up_send = tie(right, left, gate_send, up_send)
+            right, left, grads, squares = tie(right, left, grads, squares)
         else:
-            right, left = line_pass(*moving, k)
+            right, left, squares = tie(*line_pass(*tie(*moving), k), squares)
+        squares = loss_steps.send(squares)
+    expert_sums = [Halving(*grads[:2], order_a), Halving(*grads[2:], order_b)]
+    for each in expert_sums:
+        each.go()
     d_normed_two = line_end(d_parts, right, left)
-    down_sum = lax.psum_scatter(down_part, "fsdp", scatter_dimension=1, tiled=True)
 
     d_hidden_norm, gain_two_part = norm_two_pull(d_normed_two)
     d_hidden = d_out + d_hidden_norm
     d_proj = (resid_mult * d_hidden).astype(low)
     d_attended = dot("kd,td->kt", full_out, d_proj).astype(low)
-    d_attended, gate_send, up_send = tie(d_attended, gate_send, up_send)
     moved = exchange(d_attended.reshape(n, heads_w, shard_len))
-    gate_here = swap(gate_send, "fsdp", order_a[1])
-    up_here = swap(up_send, "fsdp", order_b[1])
+    for each in expert_sums:
+        each.add()
     out_part = dot("kt,td->kd", attn_rows, d_proj).astype(low)
     router_part = sum(
         dot("td,et->de", shard, shard_logits[:experts_here])
         for shard, shard_logits in zip(tokens, d_logits)
     )
-    moved, out_part, router_part = tie(moved, out_part, router_part)
+    moved, out_part, router_part = leave(expert_sums, moved, out_part, router_part)
+    for each in expert_sums:
+        each.go()
+    out_sum = lax.psum_scatter(out_part, "fsdp", scatter_dimension=0, tiled=True)
     d_heads = by_place(nearest(*moved))
     query_grad, key_grad, value_grad = attention_backward(
         query, key_rows, value_rows, key, limit, out_heads, lse, d_heads
     )
-    (query_grad, key_grad, value_grad), gate_here, up_here = tie(
-        (query_grad, key_grad, value_grad), gate_here, up_here
-    )
+    (query_grad, key_grad, value_grad), out_sum = tie((query_grad, key_grad, value_grad), out_sum)
+    out_sum = lax.psum(out_sum, "seq")
     d_turned = jnp.concatenate([query_grad, key_grad[:, None]], axis=1).astype(full)
     d_turned = rotate(d_turned, cosine, -sine_vals).astype(low)
     d_qkv = jnp.concatenate([d_turned, value_grad[:, None]], axis=1).reshape(group_w, seq_len)
     d_parts = dot("ct,dc->td", d_qkv, full_qkv).astype(low).reshape(n, shard_len, width)
-    moving = line_send(d_parts, n - 1, None, None)
-    moving, d_qkv, gate_here, up_here = tie(moving, d_qkv, gate_here, up_here)
-    right, left = line_pass(*moving, n - 1)
-    qkv_part = dot("td,ct->dc", normed_one, d_qkv).astype(low)
-    qkv_sum = lax.psum_scatter(qkv_part, "fsdp", scatter_dimension=0, tiled=True)
-    gate_send, gate_keep = halve(gate_keep, gate_here)
-    up_send, up_keep = halve(up_keep, up_here)
-    right, left, qkv_part, gate_send, up_send = tie(right, left, qkv_part, gate_send, up_send)
-    gate_here = swap(gate_send, "fsdp", order_a[2])
-    up_here = swap(up_send, "fsdp", order_b[2])
-    for k in range(n - 2, 0, -1):
-        right, left = line_pass(*line_send(d_parts, k, right, left), k)
+
+    right = left = None
+    for k in range(n - 1, 0, -1):
+        moving = line_send(d_parts, k, right, left)
+        if k == n - 1:
+            moving, d_qkv = tie(moving, d_qkv)
+            right, left = line_pass(*moving, k)
+            own_columns = jnp.zeros((width, expert_total), full)
+            own_columns = lax.dynamic_update_slice_in_dim(
+                own_columns, router_part, me * experts_here, 1
+            )
+            qkv_part = jnp.concatenate(
+                [dot("td,ct->dc", normed_one, d_qkv), own_columns, gain_two_part[:, None]], axis=1
+            ).astype(low)
+            qkv_sum = lax.psum_scatter(qkv_part, "fsdp", scatter_dimension=0, tiled=True)
+            right, left, qkv_part = land(expert_sums, right, left, qkv_part)
+            for each in expert_sums:
+                each.add()
+        else:
+            right, left = line_pass(*moving, k)
+            if k == n - 2:
+                for each in expert_sums:
+                    each.go()
+            if k == 1:
+                right, left, qkv_sum = tie(right, left, qkv_sum)
+            else:
+                right, left = tie(right, left)
     d_normed_one = line_end(d_parts, right, left)
+    sums = line_gather(qkv_sum)
     _, norm_one_pull = jax.vjp(lambda v: rms_norm(v, full_g1), x_low.astype(full))
     input_grad = (d_hidden + norm_one_pull(d_normed_one)[0]).reshape(1, shard_len, width)
-
-    input_grad, gate_here, up_here, down_sum, qkv_sum = tie(
-        input_grad, gate_here, up_here, down_sum, qkv_sum
-    )
-    for bit_a, bit_b in zip(order_a[3:], order_b[3:]):
-        gate_send, gate_keep = halve(gate_keep, gate_here)
-        up_send, up_keep = halve(up_keep, up_here)
-        gate_here = swap(gate_send, "fsdp", bit_a)
-        up_here = swap(up_send, "fsdp", bit_b)
-    gate_grad = halve(gate_keep, gate_here)
-    up_grad = halve(up_keep, up_here)
-    down_grad = down_sum.astype(full)
-    own_columns = jnp.zeros((width, expert_total), full)
-    own_columns = lax.dynamic_update_slice_in_dim(own_columns, router_part, me * experts_here, 1)
-    rest = jnp.concatenate([own_columns.astype(low), gain_two_part[:, None].astype(low)], axis=1)
-    dense = [
-        lax.psum_scatter(part, "fsdp", scatter_dimension=0, tiled=True) for part in (out_part, rest)
-    ]
-    out_sum, rest = lax.psum(dense, "seq")
+    input_grad, out_sum = land(expert_sums, input_grad, out_sum)
+    for each in expert_sums:
+        each.add()
+    left_sum, right_sum = (each.finish() for each in expert_sums)
+    gate_grad, up_grad = left_sum[:, :, :hidden_w], right_sum[:, :, :hidden_w]
+    few = w_down.shape[1]
+    down_grad = jnp.concatenate(
+        [
+            part[:, start : start + few, hidden_w:]
+            for part in (left_sum, right_sum)
+            for start in range(0, part.shape[1], few)
+        ],
+        axis=2,
+    )
     out_grad = out_sum.astype(full)
-    router_grad = rest[:, :expert_total].astype(full)
-    gain_two_grad = rest[:, expert_total].astype(full)
-    qkv_grad = by_place(line_gather(qkv_sum))
-    qkv_grad = jnp.swapaxes(qkv_grad, 0, 1).reshape(-1, QKV_W).astype(full)
+    sums = by_place(sums).astype(full)
+    qkv_grad = jnp.swapaxes(sums[:, :, :group_w], 0, 1).reshape(-1, QKV_W)
+    rest = jnp.sum(sums[:, :, group_w:], axis=0)
+    router_grad, gain_two_grad = rest[:, :expert_total], rest[:, expert_total]
     gain_one_grad = jnp.sum(qkv_grad * w_qkv.astype(full), axis=1) / gain_one.astype(full)
-    squares = total(squares.reshape(1, 1), "seq", "fsdp")[0, 0]
-    loss_value = squares / (valid_count * width)
+    for _ in range(2):
+        squares = loss_steps.send(squares)
+    loss_value = squares[0, 0] / (valid_count * width)
     return (
         activations,
         loss_value,

time: 1380 us -> 1280 us (0.928)
  waiting for transfers between devices: 456 us -> 395 us
  blocking collectives: 21.8 us -> 0 us
  starting transfers between devices: 222 us -> 208 us
    ppermute x23 -> x14, waiting for transfers between devices: 113 us -> 41.7 us  [swap(): lax.ppermute(value, axis, [(i, i ^ bit) for i in range(lax.axis_size(axis...]
    ppermute x18 -> x15, waiting for transfers between devices: 72.5 us -> 141 us  [line_move(): lax.ppermute(left, 'seq', [(i, i - 1) for i in range(1, n - k + 1)])]
    ppermute x23 -> x14, starting transfers between devices: 65.2 us -> 31.3 us  [swap(): lax.ppermute(value, axis, [(i, i ^ bit) for i in range(lax.axis_size(axis...]
    ppermute x6, waiting for transfers between devices: 33.7 us -> 5.13 us  [exchange(): lax.ppermute(to_left, 'seq', [(i, i - k) for i in range(k, n)])]
    ppermute x9, waiting for transfers between devices: 156 us -> 130 us  [line_pass(): lax.ppermute(to_right, 'seq', [(i, i + 1) for i in range(n - k)])]
    psum x1 -> x0, blocking collectives: 21.8 us -> none  [shards(): out_sum, rest = lax.psum(dense, 'seq')]
    psum x1, waiting for transfers between devices: 28.3 us -> 7.34 us  [shards(): out_sum = lax.psum(out_sum, 'seq')]
    reduce_scatter x3 -> x1, waiting for transfers between devices: 0.03 us -> 16.9 us  [shards(): lax.psum_scatter(out_part, 'fsdp', scatter_dimension=0, tiled=True)]
  transfers between devices with their start and end apart: 98 -> 79, of which waited for: 37 -> 34; matrix products, arithmetic and copies ran while one was open for 13% -> 14% of each run, Pallas kernels for 25% -> 26%
where the time goes in v6:
time: 1280 us; the launch traced here: 1270 us
  waiting for transfers between devices  395 us (31%)
  Pallas kernels  384 us (30%)
  starting transfers between devices  208 us (16%)
  other arithmetic  150 us (12%)
  local copies, waits for them, and re-layouts  74.5 us (6%)
  matrix products  34.7 us (3%)
  between operations  24.1 us (2%)
    pallas_call x8, Pallas kernels, shard_call(): pl.pallas_call(kernel, grid_spec=pltpu.PrefetchScalarGridSpec(num_scalar_...  235 us
    ppermute x15, waiting for transfers between devices, line_move(): lax.ppermute(left, 'seq', [(i, i - 1) for i in range(1, n - k + 1)])  141 us
    ppermute x9, waiting for transfers between devices, line_pass(): lax.ppermute(to_right, 'seq', [(i, i + 1) for i in range(n - k)])  130 us
    ppermute x9, starting transfers between devices, line_pass(): lax.ppermute(to_right, 'seq', [(i, i + 1) for i in range(n - k)])  68 us
    pallas_call x1, Pallas kernels, attention_backward(): pl.pallas_call(functools.partial(backward_kernel, seq_len, query_rows, ke...  54.4 us
    pallas_call x2, Pallas kernels, weight_grads(): pl.pallas_call(functools.partial(grads_kernel, bits_a, bits_b), grid_spec...  54.2 us
    ppermute x14, waiting for transfers between devices, swap(): lax.ppermute(value, axis, [(i, i ^ bit) for i in range(lax.axis_size(axis...  41.7 us
    ppermute x15, starting transfers between devices, line_move(): lax.ppermute(right, 'seq', [(i, i + 1) for i in range(k - 1, n - 1)])  41.4 us
  transfers between devices with their start and end apart: 79, of which 34 were waited for; matrix products, arithmetic and copies ran while one was open for 14% of the time, Pallas kernels for 26%

profile of v6, /device:TPU:0, one launch (start us, length us, event | category | flops | bytes accessed | tf_op | source)
XLA Modules:
  0.0 1270.2 jit_solution(4258855011761425550)
XLA Ops:
  15.1 6.4 maximum_maximum_fusion
  24.5 6.8 collective-permute-start
  31.3 32.4 %collective-permute-done.1 = bf16[528,1536]{1,0:T(8,128)(2,1)S(1)} collective-permute-done((bf16[528,1536]{1,0:T(8,128)(2,1)S(1)}, bf16[528,1536]{1,0:T(8,128)(2,1)S(1)}, u32[]{:S(2)}, u32[]{:S(2)}) %collective-permute-start.1) | collective-permute-done | bytes 1622048 | tf_op jit(solution)/shard_map/ppermute | solution.py:68
  68.0 40.2 %collective-permute-done.3 = bf16[528,1536]{1,0:T(8,128)(2,1)} collective-permute-done((bf16[528,1536]{1,0:T(8,128)(2,1)S(1)}, bf16[528,1536]{1,0:T(8,128)(2,1)}, u32[]{:S(2)}, u32[]{:S(2)}) %collective-permute-start.3) | collective-permute-done | bytes 1622048 | tf_op jit(solution)/shard_map/ppermute | solution.py:68
  116.5 31.0 %collective-permute-done.5 = bf16[528,1536]{1,0:T(8,128)(2,1)} collective-permute-done((bf16[528,1536]{1,0:T(8,128)(2,1)}, bf16[528,1536]{1,0:T(8,128)(2,1)}, u32[]{:S(2)}, u32[]{:S(2)}) %collective-permute-start.5) | collective-permute-done | bytes 1622048 | tf_op jit(solution)/shard_map/ppermute | solution.py:68
  178.8 39.7 %attention_forward.1 = (bf16[4,384,512]{2,1,0:T(8,128)(2,1)S(1)}, f32[2,3,64,2048]{3,2,1,0:T(8,128)S(1)}, f32[2,3,1,2048]{3,2,1,0:T(1,128)S(1)}) custom-call(s32[1,2048]{1,0:T(1,128)S(1)} %bitcast.284, bf16[2,3,64,2048]{3,2,1,0:T(8,128)(2,1)S(1)} %copy.162.q_ref, bf16[2,2048,64]{2,1,0:T(8,128)(2,1)S(1)} %copy.163.k_ref, ...), custom_call_target="tpu_custom_call" | custom-call | tf_op jit(solution)/shard_map/attention_forward/pallas_call | solution.py:283
  227.0 9.7 collective-permute-start.8
  262.4 5.4 multiply_reduce_fusion.4
  268.3 13.2 %collective-permute-start.12 = (bf16[512,1536]{1,0:T(8,128)(2,1)S(1)}, bf16[512,1536]{1,0:T(8,128)(2,1)}, u32[]{:S(2)}, u32[]{:S(2)}) collective-permute-start(bf16[512,1536]{1,0:T(8,128)(2,1)S(1)} %multiply_convert_fusion.2.tok_ref), channel_id=1, source_target_pairs={{0,1},{1,2},{2,3},{4,5},{5,6},{6,7},{8,9},{9,10},{10,11},{12,13},{... | collective-permute-start | bytes 4718600 | tf_op jit(solution)/shard_map/ppermute | solution.py:67
  287.6 26.7 %experts_forward.4 = (bf16[4,512,1536]{2,1,0:T(8,128)(2,1)}, bf16[10,4,160,1536]{3,2,1,0:T(8,128)(2,1)}, bf16[10,4,160,1024]{3,2,1,0:T(8,128)(2,1)}, f32[10,512]{1,0:T(8,128)S(1)}) custom-call(s32[2]{0:T(128)S(1)} %get-tuple-element.479.at_ref, bf16[512,1536]{1,0:T(8,128)(2,1)S(1)} %multiply_convert_fusion.2.tok_ref, ...), custom_call_target="tpu_custom_call" | custom-call | tf_op jit(solution)/shard_map/experts_forward/pallas_call | solution.py:501
  326.4 26.6 %experts_forward.5 = (bf16[4,512,1536]{2,1,0:T(8,128)(2,1)}, bf16[10,4,160,1536]{3,2,1,0:T(8,128)(2,1)}, bf16[10,4,160,1024]{3,2,1,0:T(8,128)(2,1)}, f32[10,512]{1,0:T(8,128)S(1)}) custom-call(s32[2]{0:T(128)S(1)} %get-tuple-element.480.at_ref, ...), custom_call_target="tpu_custom_call", output_to_operand_aliasing={{0}: (7, {}), {1}: (8, {}), {2}: (9, {})} | custom-call | tf_op jit(solution)/shard_map/experts_forward/pallas_call | solution.py:501
  353.1 7.7 collective-permute-done.15
  365.9 26.7 %experts_forward.6 = (bf16[4,512,1536]{2,1,0:T(8,128)(2,1)}, bf16[10,4,160,1536]{3,2,1,0:T(8,128)(2,1)}, bf16[10,4,160,1024]{3,2,1,0:T(8,128)(2,1)}, f32[10,512]{1,0:T(8,128)S(1)}) custom-call(s32[2]{0:T(128)S(1)} %get-tuple-element.481.at_ref, ...), custom_call_target="tpu_custom_call", output_to_operand_aliasing={{0}: (7, {}), {1}: (8, {}), {2}: (9, {})} | custom-call | tf_op jit(solution)/shard_map/experts_forward/pallas_call | solution.py:501
  392.6 7.5 collective-permute-done.17
  402.4 26.6 %experts_forward.7 = (bf16[4,512,1536]{2,1,0:T(8,128)(2,1)}, bf16[10,4,160,1536]{3,2,1,0:T(8,128)(2,1)}, bf16[10,4,160,1024]{3,2,1,0:T(8,128)(2,1)}, f32[10,512]{1,0:T(8,128)S(1)}) custom-call(s32[2]{0:T(128)S(1)} %get-tuple-element.478.at_ref, ...), custom_call_target="tpu_custom_call", output_to_operand_aliasing={{0}: (7, {}), {1}: (8, {}), {2}: (9, {})} | custom-call | tf_op jit(solution)/shard_map/experts_forward/pallas_call | solution.py:501
  433.7 30.4 %collective-permute-done.18 = bf16[512,1536]{1,0:T(8,128)(2,1)S(1)} collective-permute-done((bf16[512,1536]{1,0:T(8,128)(2,1)S(1)}, bf16[512,1536]{1,0:T(8,128)(2,1)S(1)}, u32[]{:S(2)}, u32[]{:S(2)}) %collective-permute-start.18) | collective-permute-done | bytes 1572896 | tf_op jit(solution)/shard_map/ppermute | solution.py:134
  470.3 29.5 %collective-permute-done.20 = bf16[512,1536]{1,0:T(8,128)(2,1)S(1)} collective-permute-done((bf16[512,1536]{1,0:T(8,128)(2,1)S(1)}, bf16[512,1536]{1,0:T(8,128)(2,1)S(1)}, u32[]{:S(2)}, u32[]{:S(2)}) %collective-permute-start.20) | collective-permute-done | bytes 1572896 | tf_op jit(solution)/shard_map/ppermute | solution.py:134
  502.4 7.5 collective-permute-start.22
  524.0 14.5 %collective-permute-done.22 = bf16[512,1536]{1,0:T(8,128)(2,1)} collective-permute-done((bf16[512,1536]{1,0:T(8,128)(2,1)}, bf16[512,1536]{1,0:T(8,128)(2,1)}, u32[]{:S(2)}, u32[]{:S(2)}) %collective-permute-start.22) | collective-permute-done | bytes 1572896 | tf_op jit(solution)/shard_map/ppermute | solution.py:134
  549.1 5.9 multiply_reduce_fusion.3
  566.6 32.2 %experts_backward.4 = (bf16[4,512,1536]{2,1,0:T(8,128)(2,1)}, bf16[10,4,160,1536]{3,2,1,0:T(8,128)(2,1)}, bf16[10,4,160,1024]{3,2,1,0:T(8,128)(2,1)}, bf16[10,4,...) custom-call(s32[2]{0:T(128)S(1)} %copy-done.33, bf16[512,1536]{1,0:T(8,128)(2,1)S(1)} %get-tuple-element.265.tok_ref, ...), custom_call_target="tpu_custom_call" | custom-call | tf_op jit(solution)/shard_map/experts_backward/pallas_call | solution.py:501
  605.7 8.7 collective-permute-start.36
  614.5 32.2 %experts_backward.5 = (bf16[4,512,1536]{2,1,0:T(8,128)(2,1)}, bf16[10,4,160,1536]{3,2,1,0:T(8,128)(2,1)}, bf16[10,4,160,1024]{3,2,1,0:T(8,128)(2,1)}, bf16[10,4,...) custom-call(s32[2]{0:T(128)S(1)} %copy-done.31, ...), custom_call_target="tpu_custom_call", output_to_operand_aliasing={{0}: (9, {}), {1}: (10, {}), {2}: (11, {}), {3}: (12, {})} | custom-call | tf_op jit(solution)/shard_map/experts_backward/pallas_call | solution.py:501
  655.5 32.2 %experts_backward.6 = (bf16[4,512,1536]{2,1,0:T(8,128)(2,1)}, bf16[10,4,160,1536]{3,2,1,0:T(8,128)(2,1)}, bf16[10,4,160,1024]{3,2,1,0:T(8,128)(2,1)}, bf16[10,4,...) custom-call(s32[2]{0:T(128)S(1)} %get-tuple-element.481.at_ref, ...), custom_call_target="tpu_custom_call", output_to_operand_aliasing={{0}: (9, {}), {1}: (10, {}), {2}: (11, {}), {3}: (12, {})} | custom-call | tf_op jit(solution)/shard_map/experts_backward/pallas_call | solution.py:501
  696.7 32.2 %experts_backward.7 = (bf16[4,512,1536]{2,1,0:T(8,128)(2,1)}, bf16[10,4,160,1536]{3,2,1,0:T(8,128)(2,1)}, bf16[10,4,160,1024]{3,2,1,0:T(8,128)(2,1)}, bf16[10,4,...) custom-call(s32[2]{0:T(128)S(1)} %get-tuple-element.478.at_ref, ...), custom_call_target="tpu_custom_call", output_to_operand_aliasing={{0}: (9, {}), {1}: (10, {}), {2}: (11, {}), {3}: (12, {})} | custom-call | tf_op jit(solution)/shard_map/experts_backward/pallas_call | solution.py:501
  732.6 13.3 %collective-permute-start.42 = (bf16[512,1536]{1,0:T(8,128)(2,1)}, bf16[512,1536]{1,0:T(8,128)(2,1)}, u32[]{:S(2)}, u32[]{:S(2)}) collective-permute-start(bf16[512,1536]{1,0:T(8,128)(2,1)} %get-tuple-element.314), channel_id=1, source_target_pairs={{0,1},{4,5},{8,9},{12,13},{16,17},{20,21},{24,25},{28,29}} | collective-permute-start | bytes 4718600 | tf_op jit(solution)/shard_map/ppermute | solution.py:134
  751.2 27.1 %weight_grads.2 = (bf16[4,10,192,768]{3,2,1,0:T(8,128)(2,1)}, bf16[4,10,192,768]{3,2,1,0:T(8,128)(2,1)}, bf16[4,10,192,768]{3,2,1,0:T(8,128)(2,1)}, bf16[4,10,192,768]{3,2,1,0:T(8,128)(2,1)}) custom-call(s32[1]{0:T(128)} %bitcast.74.me_ref, bf16[10,640,1536]{2,1,0:T(8,128)(2,1)} %bitcast.289, bf16[10,640,1024]{2,1,0:T(8,128)(2,1)} %bitcast.293, ...), custom_call_target="tpu_custom_call" | custom-call | tf_op jit(solution)/shard_map/weight_grads/pallas_call | solution.py:648
  793.2 27.1 %weight_grads.3 = (bf16[4,10,192,768]{3,2,1,0:T(8,128)(2,1)}, bf16[4,10,192,768]{3,2,1,0:T(8,128)(2,1)}, bf16[4,10,192,768]{3,2,1,0:T(8,128)(2,1)}, bf16[4,10,192,768]{3,2,1,0:T(8,128)(2,1)}) custom-call(s32[1]{0:T(128)} %bitcast.74.me_ref, ...), custom_call_target="tpu_custom_call", output_to_operand_aliasing={{0}: (5, {}), {1}: (6, {}), {2}: (7, {}), {3}: (8, {})} | custom-call | tf_op jit(solution)/shard_map/weight_grads/pallas_call | solution.py:648
  825.6 11.9 collective-permute-start.50
  841.4 29.8 %collective-permute-done.50 = bf16[512,1536]{1,0:T(8,128)(2,1)S(1)} collective-permute-done((bf16[512,1536]{1,0:T(8,128)(2,1)S(1)}, bf16[512,1536]{1,0:T(8,128)(2,1)S(1)}, u32[]{:S(2)}, u32[]{:S(2)}) %collective-permute-start.50) | collective-permute-done | bytes 1572896 | tf_op jit(solution)/shard_map/ppermute | solution.py:134
  895.7 9.0 collective-permute-start.54
  904.7 8.9 add_convert_fusion.1
  917.4 8.9 add_convert_fusion
  939.6 54.4 %attention_backward.1 = (bf16[2,3,64,2048]{3,2,1,0:T(8,128)(2,1)S(1)}, bf16[2,64,2048]{2,1,0:T(8,128)(2,1)S(1)}, bf16[2,64,2048]{2,1,0:T(8,128)(2,1)S(1)}) custom-call(s32[1,2048]{1,0:T(1,128)S(1)} %bitcast.285, bf16[2,3,64,2048]{3,2,1,0:T(8,128)(2,1)S(1)} %copy.162.q_ref, bf16[2,2048,64]{2,1,0:T(8,128)(2,1)S(1)} %copy-done.7, ...), custom_call_target="tpu_custom_call" | custom-call | tf_op jit(solution)/shard_map/attention_backward/pallas_call | solution.py:354
  996.0 16.9 %reduce-scatter.5.cloned.1.call-done = bf16[192,1536]{1,0:T(8,128)(2,1)} async-done(((bf16[1536,1536]{1,0:T(8,128)(2,1)}), bf16[192,1536]{1,0:T(8,128)(2,1)}) %reduce-scatter.5.cloned.1.call-update) | async-done | bytes 589840 | tf_op jit(solution)/shard_map/reduce_scatter | solution.py:870
  1016.2 7.9 convolution_convert_fusion
  1039.3 7.9 convolution_convert_fusion.2
  1048.7 29.9 %collective-permute-done.58 = bf16[2,10,192,768]{3,2,1,0:T(8,128)(2,1)} collective-permute-done((bf16[2,10,192,768]{3,2,1,0:T(8,128)(2,1)}, bf16[2,10,192,768]{3,2,1,0:T(8,128)(2,1)}, u32[]{:S(2)}, u32[]{:S(2)}) %collective-permute-start.58) | collective-permute-done | bytes 5898272 | tf_op jit(solution)/shard_map/ppermute | solution.py:165
  1084.9 13.1 %collective-permute-start.64 = (bf16[512,1536]{1,0:T(8,128)(2,1)}, bf16[512,1536]{1,0:T(8,128)(2,1)S(1)}, u32[]{:S(2)}, u32[]{:S(2)}) collective-permute-start(bf16[512,1536]{1,0:T(8,128)(2,1)} %get-tuple-element.412), channel_id=1, source_target_pairs={{0,1},{1,2},{4,5},{5,6},{8,9},{9,10},{12,13},{13,14},{16,17},{17,1... | collective-permute-start | bytes 4718600 | tf_op jit(solution)/shard_map/ppermute | solution.py:134
  1108.1 21.8 %collective-permute-done.64 = bf16[512,1536]{1,0:T(8,128)(2,1)S(1)} collective-permute-done((bf16[512,1536]{1,0:T(8,128)(2,1)}, bf16[512,1536]{1,0:T(8,128)(2,1)S(1)}, u32[]{:S(2)}, u32[]{:S(2)}) %collective-permute-start.64) | collective-permute-done | bytes 1572896 | tf_op jit(solution)/shard_map/ppermute | solution.py:134
  1135.6 7.0 collective-permute-start.66
  1142.6 5.4 add_convert_fusion.3
  1155.6 24.8 %collective-permute-done.67 = bf16[512,1536]{1,0:T(8,128)(2,1)S(1)} collective-permute-done((bf16[512,1536]{1,0:T(8,128)(2,1)}, bf16[512,1536]{1,0:T(8,128)(2,1)S(1)}, u32[]{:S(2)}, u32[]{:S(2)}) %collective-permute-start.67) | collective-permute-done | bytes 1572896 | tf_op jit(solution)/shard_map/ppermute | solution.py:135
  1183.2 5.9 collective-permute-start.68
  1197.1 7.3 all-reduce.5.cloned.1.call-done
  1204.4 9.0 collective-permute-done.62
  1226.1 11.0 collective-permute-done.71
  1250.2 8.1 dynamic_update_slice.87
  (498 shorter events, 347.7 us)
Async XLA Ops:
  7.2 151.0 %all-gather.3.cloned.1.call-start = ((), (), s32[]{:S(2)}) async-start(), calls=%async_computation.2 | async-start | bytes 7962624 | tf_op jit(solution)/shard_map/all_gather | solution.py:703
  12.9 273.9 %all-gather.5.cloned.1.call-start = ((), (), s32[]{:S(2)}) async-start(), calls=%async_computation.3 | async-start | bytes 53084160 | tf_op jit(solution)/shard_map/all_gather | solution.py:713
  21.6 991.3 %reduce-scatter.5.cloned.1.call-start = ((), (), s32[]{:S(2)}) async-start(), calls=%async_computation.4 | async-start | bytes 5308416 | tf_op jit(solution)/shard_map/reduce_scatter | solution.py:870
  23.2 40.4 %collective-permute-start.1 = (bf16[528,1536]{1,0:T(8,128)(2,1)S(1)}, bf16[528,1536]{1,0:T(8,128)(2,1)S(1)}, u32[]{:S(2)}, u32[]{:S(2)}) collective-permute-start(bf16[528,1536]{1,0:T(8,128)(2,1)S(1)} %pad_maximum_fusion.2), channel_id=1, source_target_pairs={{1,0},{2,1},{3,2},{5,4},{6,5},{7,6},{9,8},{10,9},{11,10},{13,12},{... | collective-permute-start | bytes 4866056 | tf_op jit(solution)/shard_map/ppermute | solution.py:68
  24.5 40.3 %collective-permute-start = (bf16[528,1536]{1,0:T(8,128)(2,1)S(1)}, bf16[528,1536]{1,0:T(8,128)(2,1)}, u32[]{:S(2)}, u32[]{:S(2)}) collective-permute-start(bf16[528,1536]{1,0:T(8,128)(2,1)S(1)} %pad_maximum_fusion.2), channel_id=1, source_target_pairs={{0,1},{1,2},{2,3},{4,5},{5,6},{6,7},{8,9},{9,10},{10,11},{12,13},{... | collective-permute-start | bytes 4866056 | tf_op jit(solution)/shard_map/ppermute | solution.py:67
  66.7 41.6 %collective-permute-start.3 = (bf16[528,1536]{1,0:T(8,128)(2,1)S(1)}, bf16[528,1536]{1,0:T(8,128)(2,1)}, u32[]{:S(2)}, u32[]{:S(2)}) collective-permute-start(bf16[528,1536]{1,0:T(8,128)(2,1)S(1)} %collective-permute-done.1), channel_id=1, source_target_pairs={{1,0},{2,1},{5,4},{6,5},{9,8},{10,9},{13,12},{14,13},{17,16},{18,1... | collective-permute-start | bytes 4866056 | tf_op jit(solution)/shard_map/ppermute | solution.py:68
  110.2 37.3 %collective-permute-start.5 = (bf16[528,1536]{1,0:T(8,128)(2,1)}, bf16[528,1536]{1,0:T(8,128)(2,1)}, u32[]{:S(2)}, u32[]{:S(2)}) collective-permute-start(bf16[528,1536]{1,0:T(8,128)(2,1)} %collective-permute-done.3), channel_id=1, source_target_pairs={{1,0},{5,4},{9,8},{13,12},{17,16},{21,20},{25,24},{29,28}} | collective-permute-start | bytes 4866056 | tf_op jit(solution)/shard_map/ppermute | solution.py:68
  268.3 46.0 %collective-permute-start.12 = (bf16[512,1536]{1,0:T(8,128)(2,1)S(1)}, bf16[512,1536]{1,0:T(8,128)(2,1)}, u32[]{:S(2)}, u32[]{:S(2)}) collective-permute-start(bf16[512,1536]{1,0:T(8,128)(2,1)S(1)} %multiply_convert_fusion.2.tok_ref), channel_id=1, source_target_pairs={{0,1},{1,2},{2,3},{4,5},{5,6},{6,7},{8,9},{9,10},{10,11},{12,13},{... | collective-permute-start | bytes 4718600 | tf_op jit(solution)/shard_map/ppermute | solution.py:67
  281.5 38.0 %collective-permute-start.13 = (bf16[512,1536]{1,0:T(8,128)(2,1)S(1)}, bf16[512,1536]{1,0:T(8,128)(2,1)}, u32[]{:S(2)}, u32[]{:S(2)}) collective-permute-start(bf16[512,1536]{1,0:T(8,128)(2,1)S(1)} %multiply_convert_fusion.2.tok_ref), channel_id=1, source_target_pairs={{1,0},{2,1},{3,2},{5,4},{6,5},{7,6},{9,8},{10,9},{11,10},{13,12},{... | collective-permute-start | bytes 4718600 | tf_op jit(solution)/shard_map/ppermute | solution.py:68
  322.5 38.4 %collective-permute-start.15 = (bf16[512,1536]{1,0:T(8,128)(2,1)}, bf16[512,1536]{1,0:T(8,128)(2,1)S(1)}, u32[]{:S(2)}, u32[]{:S(2)}) collective-permute-start(bf16[512,1536]{1,0:T(8,128)(2,1)} %collective-permute-done.13), channel_id=1, source_target_pairs={{1,0},{2,1},{5,4},{6,5},{9,8},{10,9},{13,12},{14,13},{17,16},{18,1... | collective-permute-start | bytes 4718600 | tf_op jit(solution)/shard_map/ppermute | solution.py:68
  363.2 36.9 %collective-permute-start.17 = (bf16[512,1536]{1,0:T(8,128)(2,1)S(1)}, bf16[512,1536]{1,0:T(8,128)(2,1)S(1)}, u32[]{:S(2)}, u32[]{:S(2)}) collective-permute-start(bf16[512,1536]{1,0:T(8,128)(2,1)S(1)} %collective-permute-done.15), channel_id=1, source_target_pairs={{1,0},{5,4},{9,8},{13,12},{17,16},{21,20},{25,24},{29,28}} | collective-permute-start | bytes 4718600 | tf_op jit(solution)/shard_map/ppermute | solution.py:68
  465.0 34.8 %collective-permute-start.20 = (bf16[512,1536]{1,0:T(8,128)(2,1)S(1)}, bf16[512,1536]{1,0:T(8,128)(2,1)S(1)}, u32[]{:S(2)}, u32[]{:S(2)}) collective-permute-start(bf16[512,1536]{1,0:T(8,128)(2,1)S(1)} %get-tuple-element.253), channel_id=1, source_target_pairs={{0,1},{1,2},{4,5},{5,6},{8,9},{9,10},{12,13},{13,14},{16,17},{17,1... | collective-permute-start | bytes 4718600 | tf_op jit(solution)/shard_map/ppermute | solution.py:134
  502.4 36.1 %collective-permute-start.22 = (bf16[512,1536]{1,0:T(8,128)(2,1)}, bf16[512,1536]{1,0:T(8,128)(2,1)}, u32[]{:S(2)}, u32[]{:S(2)}) collective-permute-start(bf16[512,1536]{1,0:T(8,128)(2,1)} %get-tuple-element.257), channel_id=1, source_target_pairs={{0,1},{1,2},{2,3},{4,5},{5,6},{6,7},{8,9},{9,10},{10,11},{12,13},{... | collective-permute-start | bytes 4718600 | tf_op jit(solution)/shard_map/ppermute | solution.py:134
  555.0 43.9 %collective-permute-start.27 = (bf16[512,1536]{1,0:T(8,128)(2,1)S(1)}, bf16[512,1536]{1,0:T(8,128)(2,1)S(1)}, u32[]{:S(2)}, u32[]{:S(2)}) collective-permute-start(bf16[512,1536]{1,0:T(8,128)(2,1)S(1)} %get-tuple-element.265.tok_ref), channel_id=1, source_target_pairs={{0,1},{1,2},{2,3},{4,5},{5,6},{6,7},{8,9},{9,10},{10,11},{12,13},{... | collective-permute-start | bytes 4718600 | tf_op jit(solution)/shard_map/ppermute | solution.py:67
  556.6 42.4 %collective-permute-start.28 = (bf16[512,1536]{1,0:T(8,128)(2,1)S(1)}, bf16[512,1536]{1,0:T(8,128)(2,1)S(1)}, u32[]{:S(2)}, u32[]{:S(2)}) collective-permute-start(bf16[512,1536]{1,0:T(8,128)(2,1)S(1)} %get-tuple-element.265.tok_ref), channel_id=1, source_target_pairs={{1,0},{2,1},{3,2},{5,4},{6,5},{7,6},{9,8},{10,9},{11,10},{13,12},{... | collective-permute-start | bytes 4718600 | tf_op jit(solution)/shard_map/ppermute | solution.py:68
  558.1 40.8 %collective-permute-start.29 = (f32[1,512]{1,0:T(1,128)S(1)}, f32[1,512]{1,0:T(1,128)S(1)}, u32[]{:S(2)}, u32[]{:S(2)}) collective-permute-start(f32[1,512]{1,0:T(1,128)S(1)} %bitcast.286), channel_id=1, source_target_pairs={{0,1},{1,2},{2,3},{4,5},{5,6},{6,7},{8,9},{9,10},{10,11},{12,13},{... | collective-permute-start | bytes 6152 | tf_op jit(solution)/shard_map/ppermute | solution.py:67
  562.6 36.3 %collective-permute-start.30 = (f32[1,512]{1,0:T(1,128)S(1)}, f32[1,512]{1,0:T(1,128)S(1)}, u32[]{:S(2)}, u32[]{:S(2)}) collective-permute-start(f32[1,512]{1,0:T(1,128)S(1)} %bitcast.287), channel_id=1, source_target_pairs={{1,0},{2,1},{3,2},{5,4},{6,5},{7,6},{9,8},{10,9},{11,10},{13,12},{... | collective-permute-start | bytes 6152 | tf_op jit(solution)/shard_map/ppermute | solution.py:68
  563.9 34.9 %collective-permute-start.31 = (f32[1,1]{1,0:T(1,128)}, f32[1,1]{1,0:T(1,128)}, u32[]{:S(2)}, u32[]{:S(2)}) collective-permute-start(f32[1,1]{1,0:T(1,128)} %bitcast.67), channel_id=1, source_target_pairs={{0,1},{1,0},{2,3},{3,2},{4,5},{5,4},{6,7},{7,6},{8,9},{9,8},{10,11... | collective-permute-start | bytes 20 | tf_op jit(solution)/shard_map/ppermute | solution.py:165
  599.7 46.9 %collective-permute-start.32 = (bf16[512,1536]{1,0:T(8,128)(2,1)S(1)}, bf16[512,1536]{1,0:T(8,128)(2,1)S(1)}, u32[]{:S(2)}, u32[]{:S(2)}) collective-permute-start(bf16[512,1536]{1,0:T(8,128)(2,1)S(1)} %collective-permute-done.27), channel_id=1, source_target_pairs={{1,2},{2,3},{5,6},{6,7},{9,10},{10,11},{13,14},{14,15},{17,18},{18... | collective-permute-start | bytes 4718600 | tf_op jit(solution)/shard_map/ppermute | solution.py:67
  600.5 46.1 %collective-permute-start.33 = (bf16[512,1536]{1,0:T(8,128)(2,1)S(1)}, bf16[512,1536]{1,0:T(8,128)(2,1)S(1)}, u32[]{:S(2)}, u32[]{:S(2)}) collective-permute-start(bf16[512,1536]{1,0:T(8,128)(2,1)S(1)} %collective-permute-done.28), channel_id=1, source_target_pairs={{1,0},{2,1},{5,4},{6,5},{9,8},{10,9},{13,12},{14,13},{17,16},{18,1... | collective-permute-start | bytes 4718600 | tf_op jit(solution)/shard_map/ppermute | solution.py:68
  601.8 44.8 %collective-permute-start.34 = (f32[1,512]{1,0:T(1,128)S(1)}, f32[1,512]{1,0:T(1,128)S(1)}, u32[]{:S(2)}, u32[]{:S(2)}) collective-permute-start(f32[1,512]{1,0:T(1,128)S(1)} %collective-permute-done.29), channel_id=1, source_target_pairs={{1,2},{2,3},{5,6},{6,7},{9,10},{10,11},{13,14},{14,15},{17,18},{18... | collective-permute-start | bytes 6152 | tf_op jit(solution)/shard_map/ppermute | solution.py:67
  602.5 44.2 %collective-permute-start.35 = (f32[1,512]{1,0:T(1,128)S(1)}, f32[1,512]{1,0:T(1,128)S(1)}, u32[]{:S(2)}, u32[]{:S(2)}) collective-permute-start(f32[1,512]{1,0:T(1,128)S(1)} %collective-permute-done.30), channel_id=1, source_target_pairs={{1,0},{2,1},{5,4},{6,5},{9,8},{10,9},{13,12},{14,13},{17,16},{18,1... | collective-permute-start | bytes 6152 | tf_op jit(solution)/shard_map/ppermute | solution.py:68
  605.7 40.9 %collective-permute-start.36 = (f32[1,1]{1,0:T(1,128)}, f32[1,1]{1,0:T(1,128)}, u32[]{:S(2)}, u32[]{:S(2)}) collective-permute-start(f32[1,1]{1,0:T(1,128)} %add.444), channel_id=1, source_target_pairs={{0,2},{1,3},{2,0},{3,1},{4,6},{5,7},{6,4},{7,5},{8,10},{9,11},{10,... | collective-permute-start | bytes 20 | tf_op jit(solution)/shard_map/ppermute | solution.py:165
  648.2 44.4 %collective-permute-start.37 = (bf16[512,1536]{1,0:T(8,128)(2,1)S(1)}, bf16[512,1536]{1,0:T(8,128)(2,1)S(1)}, u32[]{:S(2)}, u32[]{:S(2)}) collective-permute-start(bf16[512,1536]{1,0:T(8,128)(2,1)S(1)} %collective-permute-done.32), channel_id=1, source_target_pairs={{2,3},{6,7},{10,11},{14,15},{18,19},{22,23},{26,27},{30,31}} | collective-permute-start | bytes 4718600 | tf_op jit(solution)/shard_map/ppermute | solution.py:67
  649.0 43.6 %collective-permute-start.38 = (bf16[512,1536]{1,0:T(8,128)(2,1)S(1)}, bf16[512,1536]{1,0:T(8,128)(2,1)S(1)}, u32[]{:S(2)}, u32[]{:S(2)}) collective-permute-start(bf16[512,1536]{1,0:T(8,128)(2,1)S(1)} %collective-permute-done.33), channel_id=1, source_target_pairs={{1,0},{5,4},{9,8},{13,12},{17,16},{21,20},{25,24},{29,28}} | collective-permute-start | bytes 4718600 | tf_op jit(solution)/shard_map/ppermute | solution.py:68
  650.3 37.4 %collective-permute-start.39 = (f32[1,512]{1,0:T(1,128)S(1)}, f32[1,512]{1,0:T(1,128)S(1)}, u32[]{:S(2)}, u32[]{:S(2)}) collective-permute-start(f32[1,512]{1,0:T(1,128)S(1)} %collective-permute-done.34), channel_id=1, source_target_pairs={{2,3},{6,7},{10,11},{14,15},{18,19},{22,23},{26,27},{30,31}} | collective-permute-start | bytes 6152 | tf_op jit(solution)/shard_map/ppermute | solution.py:67
  651.0 41.6 %collective-permute-start.40 = (f32[1,512]{1,0:T(1,128)S(1)}, f32[1,512]{1,0:T(1,128)S(1)}, u32[]{:S(2)}, u32[]{:S(2)}) collective-permute-start(f32[1,512]{1,0:T(1,128)S(1)} %collective-permute-done.35), channel_id=1, source_target_pairs={{1,0},{5,4},{9,8},{13,12},{17,16},{21,20},{25,24},{29,28}} | collective-permute-start | bytes 6152 | tf_op jit(solution)/shard_map/ppermute | solution.py:68
  732.6 46.7 %collective-permute-start.42 = (bf16[512,1536]{1,0:T(8,128)(2,1)}, bf16[512,1536]{1,0:T(8,128)(2,1)}, u32[]{:S(2)}, u32[]{:S(2)}) collective-permute-start(bf16[512,1536]{1,0:T(8,128)(2,1)} %get-tuple-element.314), channel_id=1, source_target_pairs={{0,1},{4,5},{8,9},{12,13},{16,17},{20,21},{24,25},{28,29}} | collective-permute-start | bytes 4718600 | tf_op jit(solution)/shard_map/ppermute | solution.py:134
  784.1 38.2 %collective-permute-start.45 = (bf16[512,1536]{1,0:T(8,128)(2,1)}, bf16[512,1536]{1,0:T(8,128)(2,1)S(1)}, u32[]{:S(2)}, u32[]{:S(2)}) collective-permute-start(bf16[512,1536]{1,0:T(8,128)(2,1)} %get-tuple-element.331), channel_id=1, source_target_pairs={{0,1},{1,2},{4,5},{5,6},{8,9},{9,10},{12,13},{13,14},{16,17},{17,1... | collective-permute-start | bytes 4718600 | tf_op jit(solution)/shard_map/ppermute | solution.py:134
  822.3 73.4 %collective-permute-start.48 = (bf16[4,10,192,768]{3,2,1,0:T(8,128)(2,1)}, bf16[4,10,192,768]{3,2,1,0:T(8,128)(2,1)}, u32[]{:S(2)}, u32[]{:S(2)}) collective-permute-start(bf16[4,10,192,768]{3,2,1,0:T(8,128)(2,1)} %get-tuple-element.344), channel_id=1, source_target_pairs={{0,4},{4,0},{8,12},{12,8},{16,20},{20,16},{24,28},{28,24},{1,5},{5... | collective-permute-start | bytes 35389448 | tf_op jit(solution)/shard_map/ppermute | solution.py:165
  822.3 92.6 %collective-permute-start.49 = (bf16[4,10,192,768]{3,2,1,0:T(8,128)(2,1)}, bf16[4,10,192,768]{3,2,1,0:T(8,128)(2,1)}, u32[]{:S(2)}, u32[]{:S(2)}) collective-permute-start(bf16[4,10,192,768]{3,2,1,0:T(8,128)(2,1)} %get-tuple-element.346), channel_id=1, source_target_pairs={{0,4},{4,0},{8,12},{12,8},{16,20},{20,16},{24,28},{28,24},{1,5},{5... | collective-permute-start | bytes 35389448 | tf_op jit(solution)/shard_map/ppermute | solution.py:165
  825.6 45.7 %collective-permute-start.50 = (bf16[512,1536]{1,0:T(8,128)(2,1)S(1)}, bf16[512,1536]{1,0:T(8,128)(2,1)S(1)}, u32[]{:S(2)}, u32[]{:S(2)}) collective-permute-start(bf16[512,1536]{1,0:T(8,128)(2,1)S(1)} %get-tuple-element.349), channel_id=1, source_target_pairs={{0,1},{1,2},{2,3},{4,5},{5,6},{6,7},{8,9},{9,10},{10,11},{12,13},{... | collective-permute-start | bytes 4718600 | tf_op jit(solution)/shard_map/ppermute | solution.py:134
  837.5 37.9 %collective-permute-start.51 = (bf16[512,1536]{1,0:T(8,128)(2,1)S(1)}, bf16[512,1536]{1,0:T(8,128)(2,1)S(1)}, u32[]{:S(2)}, u32[]{:S(2)}) collective-permute-start(bf16[512,1536]{1,0:T(8,128)(2,1)S(1)} %get-tuple-element.350), channel_id=1, source_target_pairs={{1,0},{2,1},{3,2},{5,4},{6,5},{7,6},{9,8},{10,9},{11,10},{13,12},{... | collective-permute-start | bytes 4718600 | tf_op jit(solution)/shard_map/ppermute | solution.py:135
  888.5 37.8 %collective-permute-start.56 = (bf16[384,512]{1,0:T(8,128)(2,1)}, bf16[384,512]{1,0:T(8,128)(2,1)}, u32[]{:S(2)}, u32[]{:S(2)}) collective-permute-start(bf16[384,512]{1,0:T(8,128)(2,1)} %get-tuple-element.439), channel_id=1, source_target_pairs={{2,0},{3,1},{6,4},{7,5},{10,8},{11,9},{14,12},{15,13},{18,16},{19,... | collective-permute-start | bytes 1179656 | tf_op jit(solution)/shard_map/ppermute | solution.py:160
  889.8 36.5 %collective-permute-start.55 = (bf16[384,512]{1,0:T(8,128)(2,1)S(1)}, bf16[384,512]{1,0:T(8,128)(2,1)}, u32[]{:S(2)}, u32[]{:S(2)}) collective-permute-start(bf16[384,512]{1,0:T(8,128)(2,1)S(1)} %get-tuple-element.440), channel_id=1, source_target_pairs={{1,0},{2,1},{3,2},{5,4},{6,5},{7,6},{9,8},{10,9},{11,10},{13,12},{... | collective-permute-start | bytes 1179656 | tf_op jit(solution)/shard_map/ppermute | solution.py:160
  930.9 223.5 %reduce-scatter.7.cloned.1.call-start = ((), (), s32[]{:S(2)}) async-start(), calls=%async_computation.6 | async-start | bytes 2654208
  932.8 145.7 %collective-permute-start.58 = (bf16[2,10,192,768]{3,2,1,0:T(8,128)(2,1)}, bf16[2,10,192,768]{3,2,1,0:T(8,128)(2,1)}, u32[]{:S(2)}, u32[]{:S(2)}) collective-permute-start(bf16[2,10,192,768]{3,2,1,0:T(8,128)(2,1)} %add_convert_fusion.1), channel_id=1, source_target_pairs={{0,8},{4,12},{8,0},{12,4},{16,24},{20,28},{24,16},{28,20},{1,9},{5... | collective-permute-start | bytes 17694728 | tf_op jit(solution)/shard_map/ppermute | solution.py:165
  934.3 145.4 %collective-permute-start.59 = (bf16[2,10,192,768]{3,2,1,0:T(8,128)(2,1)}, bf16[2,10,192,768]{3,2,1,0:T(8,128)(2,1)}, u32[]{:S(2)}, u32[]{:S(2)}) collective-permute-start(bf16[2,10,192,768]{3,2,1,0:T(8,128)(2,1)} %add_convert_fusion), channel_id=1, source_target_pairs={{0,16},{4,20},{8,24},{12,28},{16,0},{20,4},{24,8},{28,12},{1,17},{... | collective-permute-start | bytes 17694728 | tf_op jit(solution)/shard_map/ppermute | solution.py:165
  1027.7 52.0 %collective-permute-start.60 = (bf16[512,1536]{1,0:T(8,128)(2,1)}, bf16[512,1536]{1,0:T(8,128)(2,1)}, u32[]{:S(2)}, u32[]{:S(2)}) collective-permute-start(bf16[512,1536]{1,0:T(8,128)(2,1)} %get-tuple-element.375), channel_id=1, source_target_pairs={{0,1},{4,5},{8,9},{12,13},{16,17},{20,21},{24,25},{28,29}} | collective-permute-start | bytes 4718600 | tf_op jit(solution)/shard_map/ppermute | solution.py:134
  1032.2 47.5 %collective-permute-start.61 = (bf16[512,1536]{1,0:T(8,128)(2,1)}, bf16[512,1536]{1,0:T(8,128)(2,1)}, u32[]{:S(2)}, u32[]{:S(2)}) collective-permute-start(bf16[512,1536]{1,0:T(8,128)(2,1)} %get-tuple-element.376), channel_id=1, source_target_pairs={{3,2},{7,6},{11,10},{15,14},{19,18},{23,22},{27,26},{31,30}} | collective-permute-start | bytes 4718600 | tf_op jit(solution)/shard_map/ppermute | solution.py:135
  1084.9 45.0 %collective-permute-start.64 = (bf16[512,1536]{1,0:T(8,128)(2,1)}, bf16[512,1536]{1,0:T(8,128)(2,1)S(1)}, u32[]{:S(2)}, u32[]{:S(2)}) collective-permute-start(bf16[512,1536]{1,0:T(8,128)(2,1)} %get-tuple-element.412), channel_id=1, source_target_pairs={{0,1},{1,2},{4,5},{5,6},{8,9},{9,10},{12,13},{13,14},{16,17},{17,1... | collective-permute-start | bytes 4718600 | tf_op jit(solution)/shard_map/ppermute | solution.py:134
  1102.2 102.2 %all-reduce.5.cloned.1.call-start = ((), (), s32[]{:S(2)}) async-start(), calls=%async_computation.5 | async-start | bytes 1179648 | tf_op jit(solution)/shard_map/psum | solution.py:876
  1107.5 96.9 %collective-permute-start.63 = (bf16[1,10,192,768]{3,2,1,0:T(8,128)(2,1)}, bf16[1,10,192,768]{3,2,1,0:T(8,128)(2,1)}, u32[]{:S(2)}, u32[]{:S(2)}) collective-permute-start(bf16[1,10,192,768]{3,2,1,0:T(8,128)(2,1)} %add_convert_fusion.2), channel_id=1, source_target_pairs={{0,8},{4,12},{8,0},{12,4},{16,24},{20,28},{24,16},{28,20},{1,9},{5... | collective-permute-start | bytes 8847368 | tf_op jit(solution)/shard_map/ppermute | solution.py:165
  1134.3 46.1 %collective-permute-start.67 = (bf16[512,1536]{1,0:T(8,128)(2,1)}, bf16[512,1536]{1,0:T(8,128)(2,1)S(1)}, u32[]{:S(2)}, u32[]{:S(2)}) collective-permute-start(bf16[512,1536]{1,0:T(8,128)(2,1)} %get-tuple-element.409), channel_id=1, source_target_pairs={{1,0},{2,1},{3,2},{5,4},{6,5},{7,6},{9,8},{10,9},{11,10},{13,12},{... | collective-permute-start | bytes 4718600 | tf_op jit(solution)/shard_map/ppermute | solution.py:135
  1135.6 46.3 %collective-permute-start.66 = (bf16[512,1536]{1,0:T(8,128)(2,1)}, bf16[512,1536]{1,0:T(8,128)(2,1)}, u32[]{:S(2)}, u32[]{:S(2)}) collective-permute-start(bf16[512,1536]{1,0:T(8,128)(2,1)} %get-tuple-element.410), channel_id=1, source_target_pairs={{0,1},{1,2},{2,3},{4,5},{5,6},{6,7},{8,9},{9,10},{10,11},{12,13},{... | collective-permute-start | bytes 4718600 | tf_op jit(solution)/shard_map/ppermute | solution.py:134
  1148.0 65.4 %collective-permute-start.62 = (bf16[1,10,192,768]{3,2,1,0:T(8,128)(2,1)}, bf16[1,10,192,768]{3,2,1,0:T(8,128)(2,1)}, u32[]{:S(2)}, u32[]{:S(2)}) collective-permute-start(bf16[1,10,192,768]{3,2,1,0:T(8,128)(2,1)} %add_convert_fusion.3), channel_id=1, source_target_pairs={{0,16},{4,20},{8,24},{12,28},{16,0},{20,4},{24,8},{28,12},{1,17},{... | collective-permute-start | bytes 8847368 | tf_op jit(solution)/shard_map/ppermute | solution.py:165
  1181.9 42.0 %collective-permute-start.69 = (bf16[192,681]{0,1:T(8,128)(2,1)S(1)}, bf16[192,681]{0,1:T(8,128)(2,1)}, u32[]{:S(2)}, u32[]{:S(2)}) collective-permute-start(bf16[192,681]{0,1:T(8,128)(2,1)S(1)} %copy.175), channel_id=1, source_target_pairs={{1,0},{2,1},{3,2},{5,4},{6,5},{7,6},{9,8},{10,9},{11,10},{13,12},{... | collective-permute-start | bytes 784520 | tf_op jit(solution)/shard_map/ppermute | solution.py:68
  1183.2 40.8 %collective-permute-start.68 = (bf16[192,681]{0,1:T(8,128)(2,1)S(1)}, bf16[192,681]{0,1:T(8,128)(2,1)}, u32[]{:S(2)}, u32[]{:S(2)}) collective-permute-start(bf16[192,681]{0,1:T(8,128)(2,1)S(1)} %copy.175), channel_id=1, source_target_pairs={{0,1},{1,2},{2,3},{4,5},{5,6},{6,7},{8,9},{9,10},{10,11},{12,13},{... | collective-permute-start | bytes 784520 | tf_op jit(solution)/shard_map/ppermute | solution.py:67
  (133 other events, 2504.9 us)
Sparse Core Ops, SparseCore 0:
  13.0 51.5 all-gather.2
  66.5 219.0 all-gather.4
  931.1 81.7 reduce-scatter.4
  1102.3 52.0 reduce-scatter.6
  1156.6 47.7 all-reduce.4

commit v7 on v6

--- a/solution.py
+++ b/solution.py
@@ -207,6 +207,13 @@
         return sum(term[0].astype(full) for term in self.terms)
 
 
+def rows_halving(part, bits):
+    devs = lax.axis_size("fsdp")
+    order = lax.axis_index("fsdp") ^ jnp.array(halving_masks(bits), jnp.int32)
+    blocks = part.reshape(devs, part.shape[0] // devs, part.shape[1])[order]
+    return Halving(blocks[: devs // 2], blocks[devs // 2 :], bits)
+
+
 def land(sums, *others):
     tied = tie([each.terms[-1] for each in sums], *others)
     for each, here in zip(sums, tied[0]):
@@ -231,8 +238,8 @@
     return lax.dot_general(a, b, (((0,), (0,)), ((), ())), preferred_element_type=full)
 
 
-def beside(ref):
-    return jnp.concatenate([ref[0, h] for h in range(GROUP)], axis=1)
+def beside(rows):
+    return jnp.concatenate([rows[h] for h in range(GROUP)], axis=1)
 
 def key_steps(i, seq_len, query_rows, key_rows):
     free = (i * query_rows) // key_rows
@@ -241,7 +248,7 @@
 
 def forward_kernel(seq_len, query_rows, key_rows, limit_ref, q_ref, k_ref, vt_ref, low_ref, out_ref, lse_ref):
     i = pl.program_id(1)
-    qt = beside(q_ref)
+    qt = beside(q_ref[0, 0])
     width = GROUP * query_rows
     limit = jnp.concatenate([limit_ref[...]] * GROUP, axis=1)
 
@@ -275,8 +282,15 @@
         low_ref[0, pl.ds(h * HEAD_DIM, HEAD_DIM), :] = out[:, cols].astype(low)
         lse_ref[0, h] = lse[:, cols]
 
-def attention_forward(qt, k_rows, vt, limit, shard_len):
-    kv_here, _, _, seq_len = qt.shape
+def query_spec(query_rows, per):
+    return pl.BlockSpec(
+        (1, 1, GROUP, HEAD_DIM, query_rows), lambda g, i: (i // per, g, 0, 0, i % per)
+    )
+
+
+def attention_forward(heads, k_rows, vt, limit):
+    kv_here, shard_len = heads.shape[1], heads.shape[4]
+    seq_len = k_rows.shape[1]
     query_rows = min(256, shard_len)
     key_rows = min(512, seq_len)
     per = shard_len // query_rows
@@ -285,7 +299,7 @@
         grid=(kv_here, seq_len // query_rows),
         in_specs=[
             pl.BlockSpec((1, query_rows), lambda g, i: (0, i)),
-            pl.BlockSpec((1, GROUP, HEAD_DIM, query_rows), lambda g, i: (g, 0, 0, i)),
+            query_spec(query_rows, per),
             pl.BlockSpec((1, seq_len, HEAD_DIM), lambda g, i: (g, 0, 0)),
             pl.BlockSpec((1, HEAD_DIM, seq_len), lambda g, i: (g, 0, 0)),
         ],
@@ -301,7 +315,7 @@
         ],
         compiler_params=vmem(40),
         name="attention_forward",
-    )(limit, qt, k_rows, vt)
+    )(limit, heads, k_rows, vt)
 
 def backward_kernel(seq_len, query_rows, key_rows, limit_ref, q_ref, k_ref, v_ref, kt_ref, out_ref, lse_ref, dout_ref, dq_ref, dk_ref, dv_ref, dk_acc, dv_acc):
     i = pl.program_id(1)
@@ -311,11 +325,11 @@
         dk_acc[...] = jnp.zeros_like(dk_acc)
         dv_acc[...] = jnp.zeros_like(dv_acc)
 
-    qt = beside(q_ref)
+    qt = beside(q_ref[0, 0])
     limit = jnp.concatenate([limit_ref[...]] * GROUP, axis=1)
     dout = jnp.concatenate([dout_ref[0, pl.ds(h * HEAD_DIM, HEAD_DIM), :] for h in range(GROUP)], axis=1)
-    delta = jnp.sum(dout.astype(full) * beside(out_ref), axis=0, keepdims=True)
-    lse = beside(lse_ref)
+    delta = jnp.sum(dout.astype(full) * beside(out_ref[0]), axis=0, keepdims=True)
+    lse = beside(lse_ref[0])
 
     def step(masked, j, dq):
         start = pl.multiple_of(j * key_rows, key_rows)
@@ -343,9 +357,9 @@
         dk_ref[0] = dk_acc[...].astype(low)
         dv_ref[0] = dv_acc[...].astype(low)
 
-def attention_backward(qt, k_rows, v_rows, kt, limit, out, lse, d_out):
-    kv_here, _, _, seq_len = qt.shape
-    shard_len = d_out.shape[2]
+def attention_backward(heads, k_rows, v_rows, kt, limit, out, lse, d_out):
+    kv_here, shard_len = heads.shape[1], heads.shape[4]
+    seq_len = k_rows.shape[1]
     query_rows = min(256, shard_len)
     key_rows = min(512, seq_len)
     per = shard_len // query_rows
@@ -356,7 +370,7 @@
         grid=(kv_here, seq_len // query_rows),
         in_specs=[
             pl.BlockSpec((1, query_rows), lambda g, i: (0, i)),
-            pl.BlockSpec((1, GROUP, HEAD_DIM, query_rows), quarter),
+            query_spec(query_rows, per),
             pl.BlockSpec((1, seq_len, HEAD_DIM), whole),
             pl.BlockSpec((1, seq_len, HEAD_DIM), whole),
             pl.BlockSpec((1, HEAD_DIM, seq_len), whole),
@@ -377,7 +391,7 @@
         scratch_shapes=[pltpu.VMEM((HEAD_DIM, seq_len), full), pltpu.VMEM((HEAD_DIM, seq_len), full)],
         compiler_params=vmem(40),
         name="attention_backward",
-    )(limit, qt, k_rows, v_rows, kt, out, lse, d_out)
+    )(limit, heads, k_rows, v_rows, kt, out, lse, d_out)
 
 
 def vmem(mib):
@@ -636,8 +650,8 @@
                 out[spot, 0, chunk * few : (chunk + 1) * few, hidden:] = block.astype(low)
 
 
-def weight_grads(me, rows, d_gu, act, d_rows, bits_a, bits_b, first, stop, buffers):
-    experts, count, width = rows.shape
+def weight_grads(me, rows, d_gu, act, d_rows, bits_a, bits_b, first, stop):
+    _, count, width = rows.shape
     hidden = act.shape[2]
     devs = 2 ** len(bits_a)
     shape = (width // devs, hidden + hidden // 2)
@@ -650,16 +664,14 @@
         grid_spec=pltpu.PrefetchScalarGridSpec(
             num_scalar_prefetch=1,
             grid=(stop - first,),
-            in_specs=[part(count, width), part(count, 2 * hidden), part(count, hidden), part(count, width)]
-            + [pl.BlockSpec(memory_space=pl.ANY)] * len(buffers),
-            out_specs=[pl.BlockSpec((devs // 2, 1) + shape, lambda e, me: (0, first + e, 0, 0))] * 4,
+            in_specs=[part(count, width), part(count, 2 * hidden), part(count, hidden), part(count, width)],
+            out_specs=[pl.BlockSpec((devs // 2, 1) + shape, lambda e, me: (0, e, 0, 0))] * 4,
             scratch_shapes=[pltpu.VMEM((width, 2 * hidden), full), pltpu.VMEM((hidden, width), full)],
         ),
-        out_shape=[jax.ShapeDtypeStruct((devs // 2, experts) + shape, low)] * 4,
-        input_output_aliases={5 + i: i for i in range(len(buffers))},
+        out_shape=[jax.ShapeDtypeStruct((devs // 2, stop - first) + shape, low)] * 4,
         compiler_params=vmem(56),
         name="weight_grads",
-    )(me, rows, d_gu, act, d_rows, *buffers)
+    )(me, rows, d_gu, act, d_rows)
 
 
 def shards(
@@ -706,6 +718,60 @@
     full_qkv = first[:, :group_w]
     small = first[:, group_w : group_w + 2 + expert_total]
     full_out = first[:, -width:]
+    full_g1 = small[:, 0].astype(full)
+    full_g2 = small[:, 1].astype(full)
+    router = small[:, 2:].T
+    own_router = lax.dynamic_slice_in_dim(router, me * experts_here, experts_here, 0)
+    own_router = jnp.pad(own_router, ((0, -experts_here % 16), (0, 0)))
+    valid_rows = valid_mask.reshape(shard_len).astype(full)
+
+    routes_low = jnp.concatenate([routes.reshape(shard_len, top_count).T, valid_mask], axis=0)
+    routes_low = jnp.pad(
+        routes_low.astype(low), ((0, -routes_low.shape[0] % 16), (0, width - shard_len))
+    )
+    block = jnp.concatenate([x_low, routes_low], axis=0)
+    positions = jnp.arange(seq_len, dtype=jnp.int32)
+    cosine, sine_vals = rope_tables(positions.astype(full), HEAD_DIM)
+    limit = block_limits(block_lengths[0], positions)[None]
+    rights, lefts = [block], [block]
+    normed_one = jnp.zeros((seq_len, width), low)
+    heads = jnp.zeros((n, kv_here, GROUP + 2, HEAD_DIM, shard_len), low)
+    routes_all = []
+    expert_weights = (w_gate, w_up, w_down)
+    for turn in range(n):
+        if turn < n - 1:
+            right, left, block = tie(rights[turn], lefts[turn], block)
+            right, left = line_move(right, left, turn + 1)
+        start = order[turn] * shard_len
+        normed = rms_norm(block[:shard_len].astype(full), full_g1).astype(low)
+        projected = dot("td,dc->ct", normed, full_qkv)
+        projected = projected.reshape(kv_here, GROUP + 2, HEAD_DIM, shard_len)
+        turned = rotate(
+            projected[:, : GROUP + 1],
+            lax.dynamic_slice_in_dim(cosine, start, shard_len, 1),
+            lax.dynamic_slice_in_dim(sine_vals, start, shard_len, 1),
+        ).astype(low)
+        turned = jnp.concatenate(
+            [
+                turned[:, :GROUP] * jnp.asarray(attn_mult, low),
+                turned[:, GROUP:],
+                projected[:, GROUP + 1 :].astype(low),
+            ],
+            axis=1,
+        )
+        heads = lax.dynamic_update_index_in_dim(heads, turned, order[turn], 0)
+        normed_one = lax.dynamic_update_slice_in_dim(normed_one, normed, start, 0)
+        routes_all.append(block[shard_len : shard_len + top_count + 1, :shard_len])
+        if turn < n - 1:
+            if turn == 0:
+                right, left, expert_weights = tie(right, left, expert_weights)
+            else:
+                right, left, heads, normed_one = tie(right, left, heads, normed_one)
+            rights.append(right)
+            lefts.append(left)
+            block = arrived(rights, lefts, turn + 1)
+
+    w_gate, w_up, w_down = expert_weights
     hidden_w = w_gate.shape[2]
     down_chunks = [
         w_down[:, :, start : start + hidden_w] for start in range(0, width, hidden_w)
@@ -717,24 +783,7 @@
         tiled=True,
     )
 
-    routes_low = jnp.concatenate([routes.reshape(shard_len, top_count).T, valid_mask], axis=0)
-    routes_low = jnp.pad(
-        routes_low.astype(low), ((0, -routes_low.shape[0] % 16), (0, width - shard_len))
-    )
-    x_blocks = line_gather(jnp.concatenate([x_low, routes_low], axis=0))
-    routes_blocks = [
-        block[shard_len : shard_len + top_count + 1, :shard_len].astype(jnp.int32)
-        for block in x_blocks
-    ]
-    x_blocks = [block[:shard_len] for block in x_blocks]
-    full_g1 = small[:, 0].astype(full)
-    full_g2 = small[:, 1].astype(full)
-    router = small[:, 2:].T
-    own_router = lax.dynamic_slice_in_dim(router, me * experts_here, experts_here, 0)
-    own_router = jnp.pad(own_router, ((0, -experts_here % 16), (0, 0)))
-    valid_rows = valid_mask.reshape(shard_len).astype(full)
-
-    routes_all = by_place(routes_blocks)[order]
+    routes_all = jnp.stack(routes_all).astype(jnp.int32)
     valid_count = total(jnp.sum(routes_all[:, top_count]).astype(full).reshape(1, 1), "fsdp")[0, 0]
     expert_ids = jnp.arange(expert_total, dtype=jnp.int32)
     member = jnp.any(routes_all[:, :top_count, None, :] == expert_ids[:, None], axis=1)
@@ -744,20 +793,11 @@
     slot_of = jnp.where(own_member, slot_of, -1)
     member = member.astype(full)
 
-    x_all = by_place(x_blocks).reshape(seq_len, width)
-    normed_one = rms_norm(x_all.astype(full), full_g1).astype(low)
-    qkv_rows = dot("td,dc->ct", normed_one, full_qkv)
-    qkv_rows = qkv_rows.reshape(kv_here, GROUP + 2, HEAD_DIM, seq_len)
-    positions = jnp.arange(seq_len, dtype=jnp.int32)
-    cosine, sine_vals = rope_tables(positions.astype(full), HEAD_DIM)
-    turned = rotate(qkv_rows[:, : GROUP + 1], cosine, sine_vals).astype(low)
-    query = turned[:, :GROUP] * jnp.asarray(attn_mult, low)
-    key = turned[:, GROUP]
-    value = qkv_rows[:, GROUP + 1].astype(low)
+    key = jnp.moveaxis(heads[:, :, GROUP], 0, 2).reshape(kv_here, HEAD_DIM, seq_len)
+    value = jnp.moveaxis(heads[:, :, GROUP + 1], 0, 2).reshape(kv_here, HEAD_DIM, seq_len)
     key_rows = jnp.swapaxes(key, 1, 2)
     value_rows = jnp.swapaxes(value, 1, 2)
-    limit = block_limits(block_lengths[0], positions)[None]
-    attended, out_heads, lse = attention_forward(query, key_rows, value, limit, shard_len)
+    attended, out_heads, lse = attention_forward(heads, key_rows, value, limit)
     moved = exchange(attended)
     moved, slot_of, member, own_router = tie(moved, slot_of, member, own_router)
     attn_rows = by_place(nearest(*moved)).reshape(HEADS * HEAD_DIM, shard_len)
@@ -832,24 +872,36 @@
     act_low = act_low.reshape(experts_here, slot_rows, -1)
 
     right = left = None
-    grads = []
     cut = (experts_here + 1) // 2
+    sums = [None, None]
     for k in range(n - 1, 0, -1):
         moving = line_send(d_parts, k, right, left)
         if k >= n - 2:
-            moving, d_rows, grads = tie(moving, d_rows, grads)
+            half = n - 1 - k
+            moving, d_rows = tie(moving, d_rows)
             right, left = line_pass(*moving, k)
-            part = (0, cut) if k == n - 1 else (cut, experts_here)
+            if half:
+                for each in sums[0]:
+                    each.go()
             grads = weight_grads(
-                mine.reshape(1), expert_in, d_gate_up, act_low, d_rows, order_a, order_b, *part, grads
+                mine.reshape(1), expert_in, d_gate_up, act_low, d_rows, order_a, order_b,
+                *((cut, experts_here) if half else (0, cut)),
             )
             right, left, grads, squares = tie(right, left, grads, squares)
+            sums[half] = [Halving(*grads[:2], order_a), Halving(*grads[2:], order_b)]
+        elif k == n - 3:
+            (moving,) = leave(sums[1], moving)
+            right, left = line_pass(*moving, k)
+            for each in sums[1]:
+                each.go()
+            for each in sums[0]:
+                each.add()
+            right, left, squares = leave(sums[0], right, left, squares)
+            for each in sums[0]:
+                each.go()
         else:
             right, left, squares = tie(*line_pass(*tie(*moving), k), squares)
         squares = loss_steps.send(squares)
-    expert_sums = [Halving(*grads[:2], order_a), Halving(*grads[2:], order_b)]
-    for each in expert_sums:
-        each.go()
     d_normed_two = line_end(d_parts, right, left)
 
     d_hidden_norm, gain_two_part = norm_two_pull(d_normed_two)
@@ -857,23 +909,27 @@
     d_proj = (resid_mult * d_hidden).astype(low)
     d_attended = dot("kd,td->kt", full_out, d_proj).astype(low)
     moved = exchange(d_attended.reshape(n, heads_w, shard_len))
-    for each in expert_sums:
+    for each in sums[1]:
         each.add()
     out_part = dot("kt,td->kd", attn_rows, d_proj).astype(low)
+    out_sum = lax.psum_scatter(out_part, "fsdp", scatter_dimension=0, tiled=True)
     router_part = sum(
         dot("td,et->de", shard, shard_logits[:experts_here])
         for shard, shard_logits in zip(tokens, d_logits)
     )
-    moved, out_part, router_part = leave(expert_sums, moved, out_part, router_part)
-    for each in expert_sums:
+    moved, out_part, router_part = leave(sums[1], moved, out_part, router_part)
+    for each in sums[1]:
         each.go()
-    out_sum = lax.psum_scatter(out_part, "fsdp", scatter_dimension=0, tiled=True)
+    (moved,) = land(sums[0], moved)
     d_heads = by_place(nearest(*moved))
+    for each in sums[0]:
+        each.add()
+    (d_heads,) = leave(sums[0], d_heads)
+    for each in sums[0]:
+        each.go()
     query_grad, key_grad, value_grad = attention_backward(
-        query, key_rows, value_rows, key, limit, out_heads, lse, d_heads
-    )
-    (query_grad, key_grad, value_grad), out_sum = tie((query_grad, key_grad, value_grad), out_sum)
-    out_sum = lax.psum(out_sum, "seq")
+        heads, key_rows, value_rows, key, limit, out_heads, lse, d_heads
+    )
     d_turned = jnp.concatenate([query_grad, key_grad[:, None]], axis=1).astype(full)
     d_turned = rotate(d_turned, cosine, -sine_vals).astype(low)
     d_qkv = jnp.concatenate([d_turned, value_grad[:, None]], axis=1).reshape(group_w, seq_len)
@@ -892,27 +948,40 @@
             qkv_part = jnp.concatenate(
                 [dot("td,ct->dc", normed_one, d_qkv), own_columns, gain_two_part[:, None]], axis=1
             ).astype(low)
-            qkv_sum = lax.psum_scatter(qkv_part, "fsdp", scatter_dimension=0, tiled=True)
-            right, left, qkv_part = land(expert_sums, right, left, qkv_part)
-            for each in expert_sums:
+            qkv_sum = rows_halving(qkv_part, order_a)
+            (right, left) = land(sums[1], right, left)
+            for each in sums[1]:
                 each.add()
+            right, left = leave(sums[1] + [qkv_sum], right, left)
+            qkv_sum.go()
+            qkv_sum.add()
+            qkv_sum.go()
+            for each in sums[1]:
+                each.go()
         else:
-            right, left = line_pass(*moving, k)
+            right, left = line_pass(*tie(*moving), k)
             if k == n - 2:
-                for each in expert_sums:
-                    each.go()
-            if k == 1:
-                right, left, qkv_sum = tie(right, left, qkv_sum)
+                right, left, out_sum = land([qkv_sum] + sums[0], right, left, out_sum)
+                qkv_sum.add()
+                qkv_sum.go()
+                for each in sums[0]:
+                    each.add()
+                out_sum = lax.psum(out_sum, "seq")
+            elif k == 1:
+                right, left = land([qkv_sum], right, left)
             else:
                 right, left = tie(right, left)
+    qkv_sum.add()
+    blocks = line_gather(qkv_sum.finish().astype(low))
     d_normed_one = line_end(d_parts, right, left)
-    sums = line_gather(qkv_sum)
     _, norm_one_pull = jax.vjp(lambda v: rms_norm(v, full_g1), x_low.astype(full))
     input_grad = (d_hidden + norm_one_pull(d_normed_one)[0]).reshape(1, shard_len, width)
-    input_grad, out_sum = land(expert_sums, input_grad, out_sum)
-    for each in expert_sums:
+    input_grad, out_sum = land(sums[1], input_grad, out_sum)
+    for each in sums[1]:
         each.add()
-    left_sum, right_sum = (each.finish() for each in expert_sums)
+    left_sum, right_sum = (
+        jnp.concatenate([sums[0][side].finish(), sums[1][side].finish()]) for side in (0, 1)
+    )
     gate_grad, up_grad = left_sum[:, :, :hidden_w], right_sum[:, :, :hidden_w]
     few = w_down.shape[1]
     down_grad = jnp.concatenate(
@@ -924,9 +993,14 @@
         axis=2,
     )
     out_grad = out_sum.astype(full)
-    sums = by_place(sums).astype(full)
-    qkv_grad = jnp.swapaxes(sums[:, :, :group_w], 0, 1).reshape(-1, QKV_W)
-    rest = jnp.sum(sums[:, :, group_w:], axis=0)
+    qkv_grad = jnp.zeros((w_qkv.shape[0], QKV_W), full)
+    rest = 0.0
+    for k, block in enumerate(blocks):
+        block = block.astype(full)
+        qkv_grad = lax.dynamic_update_slice_in_dim(
+            qkv_grad, block[:, :group_w], ((me - k) % n) * group_w, 1
+        )
+        rest = rest + block[:, group_w:]
     router_grad, gain_two_grad = rest[:, :expert_total], rest[:, expert_total]
     gain_one_grad = jnp.sum(qkv_grad * w_qkv.astype(full), axis=1) / gain_one.astype(full)
     for _ in range(2):

time: 1280 us -> 1280 us (level)
  starting transfers between devices: 208 us -> 181 us
  local copies, waits for them, and re-layouts: 74.5 us -> 55.1 us
  waiting for transfers between devices: 395 us -> 413 us
    ppermute x6, waiting for transfers between devices: 5.13 us -> 57.6 us  [exchange(): lax.ppermute(to_left, 'seq', [(i, i - k) for i in range(k, n)])]
    ppermute x15, waiting for transfers between devices: 141 us -> 104 us  [line_move(): lax.ppermute(left, 'seq', [(i, i - 1) for i in range(1, n - k + 1)])]
    ppermute x15, waiting for transfers between devices: 1.22 us -> 32.3 us  [line_move(): lax.ppermute(right, 'seq', [(i, i + 1) for i in range(k - 1, n - 1)])]
    ppermute x14 -> x23, waiting for transfers between devices: 41.7 us -> 72 us  [swap(): lax.ppermute(value, axis, [(i, i ^ bit) for i in range(lax.axis_size(axis...]
    reduce_scatter x1, waiting for transfers between devices: 16.9 us -> 0.01 us  [shards(): lax.psum_scatter(out_part, 'fsdp', scatter_dimension=0, tiled=True)]
    ppermute x9, waiting for transfers between devices: 130 us -> 114 us  [line_pass(): lax.ppermute(to_right, 'seq', [(i, i + 1) for i in range(n - k)])]
    ppermute x9, waiting for transfers between devices: 34.3 us -> 20.9 us  [line_pass(): lax.ppermute(to_left, 'seq', [(i, i - 1) for i in range(k, n)])]
    convert_element_type x4 -> x10, other arithmetic: 28.4 us -> 38.3 us  [add(): sum((term[half:].astype(full) for term in self.terms)).astype(low)]
  transfers between devices with their start and end apart: 79 -> 87, of which waited for: 34 -> 37; matrix products, arithmetic and copies ran while one was open for 14% -> 15% of each run, Pallas kernels for 26% -> 26%
where the time goes in v7:
time: 1280 us; the launch traced here: 1270 us
  waiting for transfers between devices  413 us (32%)
  Pallas kernels  384 us (30%)
  starting transfers between devices  181 us (14%)
  other arithmetic  160 us (12%)
  local copies, waits for them, and re-layouts  55.1 us (4%)
  matrix products  36.8 us (3%)
  between operations  35.2 us (3%)
    pallas_call x8, Pallas kernels, shard_call(): pl.pallas_call(kernel, grid_spec=pltpu.PrefetchScalarGridSpec(num_scalar_...  236 us
    ppermute x9, waiting for transfers between devices, line_pass(): lax.ppermute(to_right, 'seq', [(i, i + 1) for i in range(n - k)])  114 us
    ppermute x15, waiting for transfers between devices, line_move(): lax.ppermute(left, 'seq', [(i, i - 1) for i in range(1, n - k + 1)])  104 us
    ppermute x23, waiting for transfers between devices, swap(): lax.ppermute(value, axis, [(i, i ^ bit) for i in range(lax.axis_size(axis...  72 us
    ppermute x9, starting transfers between devices, line_pass(): lax.ppermute(to_right, 'seq', [(i, i + 1) for i in range(n - k)])  58.5 us
    ppermute x6, waiting for transfers between devices, exchange(): lax.ppermute(to_left, 'seq', [(i, i - k) for i in range(k, n)])  57.6 us
    pallas_call x2, Pallas kernels, weight_grads(): pl.pallas_call(functools.partial(grads_kernel, bits_a, bits_b), grid_spec...  54.1 us
    pallas_call x1, Pallas kernels, attention_backward(): pl.pallas_call(functools.partial(backward_kernel, seq_len, query_rows, ke...  54.1 us
  transfers between devices with their start and end apart: 87, of which 37 were waited for; matrix products, arithmetic and copies ran while one was open for 15% of the time, Pallas kernels for 26%

profile of v7, /device:TPU:0, one launch (start us, length us, event | category | flops | bytes accessed | tf_op | source)
XLA Modules:
  0.0 1265.2 jit_solution(1861189698746919208)
XLA Ops:
  13.7 6.3 collective-permute-start
  21.3 32.3 %collective-permute-done = bf16[528,1536]{1,0:T(8,128)(2,1)} collective-permute-done((bf16[528,1536]{1,0:T(8,128)(2,1)S(1)}, bf16[528,1536]{1,0:T(8,128)(2,1)}, u32[]{:S(2)}, u32[]{:S(2)}) %collective-permute-start) | collective-permute-done | bytes 1622048 | tf_op jit(solution)/shard_map/ppermute | solution.py:67
  53.6 5.4 collective-permute-done.1
  60.6 6.5 maximum_maximum_fusion
  104.4 26.3 %collective-permute-done.3 = bf16[528,1536]{1,0:T(8,128)(2,1)} collective-permute-done((bf16[528,1536]{1,0:T(8,128)(2,1)}, bf16[528,1536]{1,0:T(8,128)(2,1)}, u32[]{:S(2)}, u32[]{:S(2)}) %collective-permute-start.3) | collective-permute-done | bytes 1622048 | tf_op jit(solution)/shard_map/ppermute | solution.py:68
  143.6 29.4 %collective-permute-done.5 = bf16[528,1536]{1,0:T(8,128)(2,1)} collective-permute-done((bf16[528,1536]{1,0:T(8,128)(2,1)}, bf16[528,1536]{1,0:T(8,128)(2,1)}, u32[]{:S(2)}, u32[]{:S(2)}) %collective-permute-start.5) | collective-permute-done | bytes 1622048 | tf_op jit(solution)/shard_map/ppermute | solution.py:68
  189.9 39.6 %attention_forward.1 = (bf16[4,384,512]{2,1,0:T(8,128)(2,1)S(1)}, f32[2,3,64,2048]{3,2,1,0:T(8,128)S(1)}, f32[2,3,1,2048]{3,2,1,0:T(1,128)S(1)}) custom-call(s32[1,2048]{1,0:T(1,128)S(1)} %bitcast.269, bf16[4,2,5,64,512]{4,3,2,1,0:T(8,128)(2,1)S(1)} %fusion.72.q_ref, bf16[2,2048,64]{2,1,0:T(8,128)(2,1)S(1)} %copy-done.7, bf16[2,64,2048]{2,1,0:T(8,128)(2,1)S(1)} %copy-done.11), custom_call_target="tpu_custom_call" | custom-call | tf_op jit(solution)/shard_map/attention_forward/pallas_call | solution.py:297
  235.0 7.5 collective-permute-start.7
  243.8 12.8 %collective-permute-done.10 = bf16[384,512]{1,0:T(8,128)(2,1)S(1)} collective-permute-done((bf16[384,512]{1,0:T(8,128)(2,1)S(1)}, bf16[384,512]{1,0:T(8,128)(2,1)S(1)}, u32[]{:S(2)}, u32[]{:S(2)}) %collective-permute-start.10) | collective-permute-done | bytes 393248 | tf_op jit(solution)/shard_map/ppermute | solution.py:160
  260.6 9.0 collective-permute-done.9
  286.5 27.1 %experts_forward.4 = (bf16[4,512,1536]{2,1,0:T(8,128)(2,1)}, bf16[10,4,160,1536]{3,2,1,0:T(8,128)(2,1)}, bf16[10,4,160,1024]{3,2,1,0:T(8,128)(2,1)}, f32[10,512]{1,0:T(8,128)S(1)}) custom-call(s32[2]{0:T(128)S(1)} %get-tuple-element.617.at_ref, bf16[512,1536]{1,0:T(8,128)(2,1)} %multiply_convert_fusion.1.tok_ref, s32[10,512]{1,0:T(8,128)S(1)} %get-tuple-element.602.slot_ref, ...), custom_call_target="tpu_custom_call" | custom-call | tf_op jit(solution)/shard_map/experts_forward/pallas_call | solution.py:515
  321.5 26.6 %experts_forward.5 = (bf16[4,512,1536]{2,1,0:T(8,128)(2,1)}, bf16[10,4,160,1536]{3,2,1,0:T(8,128)(2,1)}, bf16[10,4,160,1024]{3,2,1,0:T(8,128)(2,1)}, f32[10,512]{1,0:T(8,128)S(1)}) custom-call(s32[2]{0:T(128)S(1)} %get-tuple-element.618.at_ref, ...), custom_call_target="tpu_custom_call", output_to_operand_aliasing={{0}: (7, {}), {1}: (8, {}), {2}: (9, {})} | custom-call | tf_op jit(solution)/shard_map/experts_forward/pallas_call | solution.py:515
  348.2 9.9 collective-permute-done.15
  362.1 26.6 %experts_forward.6 = (bf16[4,512,1536]{2,1,0:T(8,128)(2,1)}, bf16[10,4,160,1536]{3,2,1,0:T(8,128)(2,1)}, bf16[10,4,160,1024]{3,2,1,0:T(8,128)(2,1)}, f32[10,512]{1,0:T(8,128)S(1)}) custom-call(s32[2]{0:T(128)S(1)} %get-tuple-element.619.at_ref, ...), custom_call_target="tpu_custom_call", output_to_operand_aliasing={{0}: (7, {}), {1}: (8, {}), {2}: (9, {})} | custom-call | tf_op jit(solution)/shard_map/experts_forward/pallas_call | solution.py:515
  388.8 10.0 collective-permute-done.17
  400.8 26.7 %experts_forward.7 = (bf16[4,512,1536]{2,1,0:T(8,128)(2,1)}, bf16[10,4,160,1536]{3,2,1,0:T(8,128)(2,1)}, bf16[10,4,160,1024]{3,2,1,0:T(8,128)(2,1)}, f32[10,512]{1,0:T(8,128)S(1)}) custom-call(s32[2]{0:T(128)S(1)} %get-tuple-element.616.at_ref, ...), custom_call_target="tpu_custom_call", output_to_operand_aliasing={{0}: (7, {}), {1}: (8, {}), {2}: (9, {})} | custom-call | tf_op jit(solution)/shard_map/experts_forward/pallas_call | solution.py:515
  432.3 31.5 %collective-permute-done.18 = bf16[512,1536]{1,0:T(8,128)(2,1)S(1)} collective-permute-done((bf16[512,1536]{1,0:T(8,128)(2,1)S(1)}, bf16[512,1536]{1,0:T(8,128)(2,1)S(1)}, u32[]{:S(2)}, u32[]{:S(2)}) %collective-permute-start.18) | collective-permute-done | bytes 1572896 | tf_op jit(solution)/shard_map/ppermute | solution.py:134
  470.2 30.6 %collective-permute-done.20 = bf16[512,1536]{1,0:T(8,128)(2,1)S(1)} collective-permute-done((bf16[512,1536]{1,0:T(8,128)(2,1)S(1)}, bf16[512,1536]{1,0:T(8,128)(2,1)S(1)}, u32[]{:S(2)}, u32[]{:S(2)}) %collective-permute-start.20) | collective-permute-done | bytes 1572896 | tf_op jit(solution)/shard_map/ppermute | solution.py:134
  503.4 7.5 collective-permute-start.22
  523.8 16.8 %collective-permute-done.22 = bf16[512,1536]{1,0:T(8,128)(2,1)} collective-permute-done((bf16[512,1536]{1,0:T(8,128)(2,1)}, bf16[512,1536]{1,0:T(8,128)(2,1)}, u32[]{:S(2)}, u32[]{:S(2)}) %collective-permute-start.22) | collective-permute-done | bytes 1572896 | tf_op jit(solution)/shard_map/ppermute | solution.py:134
  540.6 5.3 collective-permute-done.23
  551.2 5.9 multiply_reduce_fusion.2
  568.8 32.2 %experts_backward.4 = (bf16[4,512,1536]{2,1,0:T(8,128)(2,1)}, bf16[10,4,160,1536]{3,2,1,0:T(8,128)(2,1)}, bf16[10,4,160,1024]{3,2,1,0:T(8,128)(2,1)}, bf16[10,4,...) custom-call(s32[2]{0:T(128)S(1)} %copy-done.31, bf16[512,1536]{1,0:T(8,128)(2,1)S(1)} %get-tuple-element.316.tok_ref, ...), custom_call_target="tpu_custom_call" | custom-call | tf_op jit(solution)/shard_map/experts_backward/pallas_call | solution.py:515
  607.7 8.8 collective-permute-start.36
  616.5 32.2 %experts_backward.5 = (bf16[4,512,1536]{2,1,0:T(8,128)(2,1)}, bf16[10,4,160,1536]{3,2,1,0:T(8,128)(2,1)}, bf16[10,4,160,1024]{3,2,1,0:T(8,128)(2,1)}, bf16[10,4,...) custom-call(s32[2]{0:T(128)S(1)} %copy-done.29, ...), custom_call_target="tpu_custom_call", output_to_operand_aliasing={{0}: (9, {}), {1}: (10, {}), {2}: (11, {}), {3}: (12, {})} | custom-call | tf_op jit(solution)/shard_map/experts_backward/pallas_call | solution.py:515
  657.9 32.2 %experts_backward.6 = (bf16[4,512,1536]{2,1,0:T(8,128)(2,1)}, bf16[10,4,160,1536]{3,2,1,0:T(8,128)(2,1)}, bf16[10,4,160,1024]{3,2,1,0:T(8,128)(2,1)}, bf16[10,4,...) custom-call(s32[2]{0:T(128)S(1)} %get-tuple-element.619.at_ref, ...), custom_call_target="tpu_custom_call", output_to_operand_aliasing={{0}: (9, {}), {1}: (10, {}), {2}: (11, {}), {3}: (12, {})} | custom-call | tf_op jit(solution)/shard_map/experts_backward/pallas_call | solution.py:515
  690.1 7.1 collective-permute-done.40
  701.4 32.2 %experts_backward.7 = (bf16[4,512,1536]{2,1,0:T(8,128)(2,1)}, bf16[10,4,160,1536]{3,2,1,0:T(8,128)(2,1)}, bf16[10,4,160,1024]{3,2,1,0:T(8,128)(2,1)}, bf16[10,4,...) custom-call(s32[2]{0:T(128)S(1)} %get-tuple-element.616.at_ref, ...), custom_call_target="tpu_custom_call", output_to_operand_aliasing={{0}: (9, {}), {1}: (10, {}), {2}: (11, {}), {3}: (12, {})} | custom-call | tf_op jit(solution)/shard_map/experts_backward/pallas_call | solution.py:515
  737.4 12.2 collective-permute-start.42
  755.0 27.1 %weight_grads.2 = (bf16[4,5,192,768]{3,2,1,0:T(8,128)(2,1)}, bf16[4,5,192,768]{3,2,1,0:T(8,128)(2,1)}, bf16[4,5,192,768]{3,2,1,0:T(8,128)(2,1)}, bf16[4,5,192,768]{3,2,1,0:T(8,128)(2,1)}) custom-call(s32[1]{0:T(128)} %bitcast.77.me_ref, bf16[10,640,1536]{2,1,0:T(8,128)(2,1)} %bitcast.274, bf16[10,640,1024]{2,1,0:T(8,128)(2,1)} %bitcast.278, ...), custom_call_target="tpu_custom_call" | custom-call | tf_op jit(solution)/shard_map/weight_grads/pallas_call | solution.py:662
  796.4 27.1 %weight_grads.3 = (bf16[4,5,192,768]{3,2,1,0:T(8,128)(2,1)}, bf16[4,5,192,768]{3,2,1,0:T(8,128)(2,1)}, bf16[4,5,192,768]{3,2,1,0:T(8,128)(2,1)}, bf16[4,5,192,768]{3,2,1,0:T(8,128)(2,1)}) custom-call(s32[1]{0:T(128)} %bitcast.77.me_ref, bf16[10,640,1536]{2,1,0:T(8,128)(2,1)} %bitcast.275, bf16[10,640,1024]{2,1,0:T(8,128)(2,1)} %bitcast.279, ...), custom_call_target="tpu_custom_call" | custom-call | tf_op jit(solution)/shard_map/weight_grads/pallas_call | solution.py:662
  830.7 11.4 collective-permute-start.52
  856.5 19.3 %collective-permute-done.52 = bf16[512,1536]{1,0:T(8,128)(2,1)S(1)} collective-permute-done((bf16[512,1536]{1,0:T(8,128)(2,1)S(1)}, bf16[512,1536]{1,0:T(8,128)(2,1)S(1)}, u32[]{:S(2)}, u32[]{:S(2)}) %collective-permute-start.52) | collective-permute-done | bytes 1572896 | tf_op jit(solution)/shard_map/ppermute | solution.py:134
  905.8 5.7 add_convert_fusion.2
  927.4 10.4 collective-permute-done.57
  937.8 25.5 %collective-permute-done.58 = bf16[384,512]{1,0:T(8,128)(2,1)S(1)} collective-permute-done((bf16[384,512]{1,0:T(8,128)(2,1)S(1)}, bf16[384,512]{1,0:T(8,128)(2,1)S(1)}, u32[]{:S(2)}, u32[]{:S(2)}) %collective-permute-start.58) | collective-permute-done | bytes 393248 | tf_op jit(solution)/shard_map/ppermute | solution.py:160
  974.2 54.1 %attention_backward.1 = (bf16[2,3,64,2048]{3,2,1,0:T(8,128)(2,1)S(1)}, bf16[2,64,2048]{2,1,0:T(8,128)(2,1)S(1)}, bf16[2,64,2048]{2,1,0:T(8,128)(2,1)S(1)}) custom-call(s32[1,2048]{1,0:T(1,128)S(1)} %bitcast.270, bf16[4,2,5,64,512]{4,3,2,1,0:T(8,128)(2,1)S(1)} %fusion.72.q_ref, bf16[2,2048,64]{2,1,0:T(8,128)(2,1)S(1)} %copy-done.8, ...), custom_call_target="tpu_custom_call" | custom-call | tf_op jit(solution)/shard_map/attention_backward/pallas_call | solution.py:368
  1030.3 6.9 convolution_convert_fusion
  1040.9 5.4 collective-permute-start.64
  1051.6 7.2 convolution_convert_fusion.2
  1062.7 10.4 collective-permute-done.64
  1093.5 30.0 %collective-permute-done.70 = bf16[1,5,192,768]{3,2,1,0:T(8,128)(2,1)S(1)} collective-permute-done((bf16[1,5,192,768]{3,2,1,0:T(8,128)(2,1)S(1)}, bf16[1,5,192,768]{3,2,1,0:T(8,128)(2,1)S(1)}, u32[]{:S(2)}, u32[]{:S(2)}) %collective-permute-start.70) | collective-permute-done | bytes 1474592 | tf_op jit(solution)/shard_map/ppermute | solution.py:165
  1125.0 11.4 collective-permute-done.69
  1141.6 6.7 collective-permute-start.75
  1162.9 26.2 %collective-permute-done.74 = bf16[1,192,681]{2,1,0:T(8,128)(2,1)S(1)} collective-permute-done((bf16[1,192,681]{2,1,0:T(8,128)(2,1)S(1)}, bf16[1,192,681]{2,1,0:T(8,128)(2,1)S(1)}, u32[]{:S(2)}, u32[]{:S(2)}) %collective-permute-start.74) | collective-permute-done | bytes 261536 | tf_op jit(solution)/shard_map/ppermute | solution.py:165
  1190.2 11.4 collective-permute-done.76
  1232.6 8.5 collective-permute-done.80
  1244.6 5.8 collective-permute-done.82
  (591 shorter events, 362.8 us)
Async XLA Ops:
  7.2 86.1 %all-gather.3.cloned.1.call-start = ((), (), s32[]{:S(2)}) async-start(), calls=%async_computation.1 | async-start | bytes 7962624 | tf_op jit(solution)/shard_map/all_gather | solution.py:715
  12.9 272.7 %all-gather.5.cloned.1.call-start = ((), (), s32[]{:S(2)}) async-start(), calls=%async_computation.2 | async-start | bytes 53084160 | tf_op jit(solution)/shard_map/all_gather | solution.py:779
  13.7 39.9 %collective-permute-start = (bf16[528,1536]{1,0:T(8,128)(2,1)S(1)}, bf16[528,1536]{1,0:T(8,128)(2,1)}, u32[]{:S(2)}, u32[]{:S(2)}) collective-permute-start(bf16[528,1536]{1,0:T(8,128)(2,1)S(1)} %pad_maximum_fusion.2), channel_id=1, source_target_pairs={{0,1},{1,2},{2,3},{4,5},{5,6},{6,7},{8,9},{9,10},{10,11},{12,13},{... | collective-permute-start | bytes 4866056 | tf_op jit(solution)/shard_map/ppermute | solution.py:67
  20.0 38.9 %collective-permute-start.1 = (bf16[528,1536]{1,0:T(8,128)(2,1)S(1)}, bf16[528,1536]{1,0:T(8,128)(2,1)}, u32[]{:S(2)}, u32[]{:S(2)}) collective-permute-start(bf16[528,1536]{1,0:T(8,128)(2,1)S(1)} %pad_maximum_fusion.2), channel_id=1, source_target_pairs={{1,0},{2,1},{3,2},{5,4},{6,5},{7,6},{9,8},{10,9},{11,10},{13,12},{... | collective-permute-start | bytes 4866056 | tf_op jit(solution)/shard_map/ppermute | solution.py:68
  67.2 1070.0 %reduce-scatter.2.cloned.1.call-start = ((), (), s32[]{:S(2)}) async-start(), calls=%async_computation.3 | async-start | bytes 5308416 | tf_op jit(solution)/shard_map/reduce_scatter | solution.py:915
  91.0 39.7 %collective-permute-start.3 = (bf16[528,1536]{1,0:T(8,128)(2,1)}, bf16[528,1536]{1,0:T(8,128)(2,1)}, u32[]{:S(2)}, u32[]{:S(2)}) collective-permute-start(bf16[528,1536]{1,0:T(8,128)(2,1)} %collective-permute-done.1), channel_id=1, source_target_pairs={{1,0},{2,1},{5,4},{6,5},{9,8},{10,9},{13,12},{14,13},{17,16},{18,1... | collective-permute-start | bytes 4866056 | tf_op jit(solution)/shard_map/ppermute | solution.py:68
  135.5 37.5 %collective-permute-start.5 = (bf16[528,1536]{1,0:T(8,128)(2,1)}, bf16[528,1536]{1,0:T(8,128)(2,1)}, u32[]{:S(2)}, u32[]{:S(2)}) collective-permute-start(bf16[528,1536]{1,0:T(8,128)(2,1)} %collective-permute-done.3), channel_id=1, source_target_pairs={{1,0},{5,4},{9,8},{13,12},{17,16},{21,20},{25,24},{29,28}} | collective-permute-start | bytes 4866056 | tf_op jit(solution)/shard_map/ppermute | solution.py:68
  275.6 38.5 %collective-permute-start.12 = (bf16[512,1536]{1,0:T(8,128)(2,1)}, bf16[512,1536]{1,0:T(8,128)(2,1)}, u32[]{:S(2)}, u32[]{:S(2)}) collective-permute-start(bf16[512,1536]{1,0:T(8,128)(2,1)} %multiply_convert_fusion.1.tok_ref), channel_id=1, source_target_pairs={{0,1},{1,2},{2,3},{4,5},{5,6},{6,7},{8,9},{9,10},{10,11},{12,13},{... | collective-permute-start | bytes 4718600 | tf_op jit(solution)/shard_map/ppermute | solution.py:67
  278.5 37.4 %collective-permute-start.13 = (bf16[512,1536]{1,0:T(8,128)(2,1)}, bf16[512,1536]{1,0:T(8,128)(2,1)}, u32[]{:S(2)}, u32[]{:S(2)}) collective-permute-start(bf16[512,1536]{1,0:T(8,128)(2,1)} %multiply_convert_fusion.1.tok_ref), channel_id=1, source_target_pairs={{1,0},{2,1},{3,2},{5,4},{6,5},{7,6},{9,8},{10,9},{11,10},{13,12},{... | collective-permute-start | bytes 4718600 | tf_op jit(solution)/shard_map/ppermute | solution.py:68
  318.9 39.2 %collective-permute-start.15 = (bf16[512,1536]{1,0:T(8,128)(2,1)}, bf16[512,1536]{1,0:T(8,128)(2,1)S(1)}, u32[]{:S(2)}, u32[]{:S(2)}) collective-permute-start(bf16[512,1536]{1,0:T(8,128)(2,1)} %collective-permute-done.13), channel_id=1, source_target_pairs={{1,0},{2,1},{5,4},{6,5},{9,8},{10,9},{13,12},{14,13},{17,16},{18,1... | collective-permute-start | bytes 4718600 | tf_op jit(solution)/shard_map/ppermute | solution.py:68
  360.6 38.1 %collective-permute-start.17 = (bf16[512,1536]{1,0:T(8,128)(2,1)S(1)}, bf16[512,1536]{1,0:T(8,128)(2,1)S(1)}, u32[]{:S(2)}, u32[]{:S(2)}) collective-permute-start(bf16[512,1536]{1,0:T(8,128)(2,1)S(1)} %collective-permute-done.15), channel_id=1, source_target_pairs={{1,0},{5,4},{9,8},{13,12},{17,16},{21,20},{25,24},{29,28}} | collective-permute-start | bytes 4718600 | tf_op jit(solution)/shard_map/ppermute | solution.py:68
  464.8 36.0 %collective-permute-start.20 = (bf16[512,1536]{1,0:T(8,128)(2,1)S(1)}, bf16[512,1536]{1,0:T(8,128)(2,1)S(1)}, u32[]{:S(2)}, u32[]{:S(2)}) collective-permute-start(bf16[512,1536]{1,0:T(8,128)(2,1)S(1)} %get-tuple-element.304), channel_id=1, source_target_pairs={{0,1},{1,2},{4,5},{5,6},{8,9},{9,10},{12,13},{13,14},{16,17},{17,1... | collective-permute-start | bytes 4718600 | tf_op jit(solution)/shard_map/ppermute | solution.py:134
  503.4 37.2 %collective-permute-start.22 = (bf16[512,1536]{1,0:T(8,128)(2,1)}, bf16[512,1536]{1,0:T(8,128)(2,1)}, u32[]{:S(2)}, u32[]{:S(2)}) collective-permute-start(bf16[512,1536]{1,0:T(8,128)(2,1)} %get-tuple-element.308), channel_id=1, source_target_pairs={{0,1},{1,2},{2,3},{4,5},{5,6},{6,7},{8,9},{9,10},{10,11},{12,13},{... | collective-permute-start | bytes 4718600 | tf_op jit(solution)/shard_map/ppermute | solution.py:134
  557.2 43.9 %collective-permute-start.27 = (bf16[512,1536]{1,0:T(8,128)(2,1)S(1)}, bf16[512,1536]{1,0:T(8,128)(2,1)S(1)}, u32[]{:S(2)}, u32[]{:S(2)}) collective-permute-start(bf16[512,1536]{1,0:T(8,128)(2,1)S(1)} %get-tuple-element.316.tok_ref), channel_id=1, source_target_pairs={{0,1},{1,2},{2,3},{4,5},{5,6},{6,7},{8,9},{9,10},{10,11},{12,13},{... | collective-permute-start | bytes 4718600 | tf_op jit(solution)/shard_map/ppermute | solution.py:67
  558.7 42.3 %collective-permute-start.28 = (bf16[512,1536]{1,0:T(8,128)(2,1)S(1)}, bf16[512,1536]{1,0:T(8,128)(2,1)S(1)}, u32[]{:S(2)}, u32[]{:S(2)}) collective-permute-start(bf16[512,1536]{1,0:T(8,128)(2,1)S(1)} %get-tuple-element.316.tok_ref), channel_id=1, source_target_pairs={{1,0},{2,1},{3,2},{5,4},{6,5},{7,6},{9,8},{10,9},{11,10},{13,12},{... | collective-permute-start | bytes 4718600 | tf_op jit(solution)/shard_map/ppermute | solution.py:68
  560.2 40.8 %collective-permute-start.29 = (f32[1,512]{1,0:T(1,128)S(1)}, f32[1,512]{1,0:T(1,128)S(1)}, u32[]{:S(2)}, u32[]{:S(2)}) collective-permute-start(f32[1,512]{1,0:T(1,128)S(1)} %bitcast.271), channel_id=1, source_target_pairs={{0,1},{1,2},{2,3},{4,5},{5,6},{6,7},{8,9},{9,10},{10,11},{12,13},{... | collective-permute-start | bytes 6152 | tf_op jit(solution)/shard_map/ppermute | solution.py:67
  564.8 36.3 %collective-permute-start.30 = (f32[1,512]{1,0:T(1,128)S(1)}, f32[1,512]{1,0:T(1,128)S(1)}, u32[]{:S(2)}, u32[]{:S(2)}) collective-permute-start(f32[1,512]{1,0:T(1,128)S(1)} %bitcast.272), channel_id=1, source_target_pairs={{1,0},{2,1},{3,2},{5,4},{6,5},{7,6},{9,8},{10,9},{11,10},{13,12},{... | collective-permute-start | bytes 6152 | tf_op jit(solution)/shard_map/ppermute | solution.py:68
  601.8 46.8 %collective-permute-start.32 = (bf16[512,1536]{1,0:T(8,128)(2,1)S(1)}, bf16[512,1536]{1,0:T(8,128)(2,1)S(1)}, u32[]{:S(2)}, u32[]{:S(2)}) collective-permute-start(bf16[512,1536]{1,0:T(8,128)(2,1)S(1)} %collective-permute-done.27), channel_id=1, source_target_pairs={{1,2},{2,3},{5,6},{6,7},{9,10},{10,11},{13,14},{14,15},{17,18},{18... | collective-permute-start | bytes 4718600 | tf_op jit(solution)/shard_map/ppermute | solution.py:67
  602.6 46.1 %collective-permute-start.33 = (bf16[512,1536]{1,0:T(8,128)(2,1)S(1)}, bf16[512,1536]{1,0:T(8,128)(2,1)S(1)}, u32[]{:S(2)}, u32[]{:S(2)}) collective-permute-start(bf16[512,1536]{1,0:T(8,128)(2,1)S(1)} %collective-permute-done.28), channel_id=1, source_target_pairs={{1,0},{2,1},{5,4},{6,5},{9,8},{10,9},{13,12},{14,13},{17,16},{18,1... | collective-permute-start | bytes 4718600 | tf_op jit(solution)/shard_map/ppermute | solution.py:68
  603.9 44.8 %collective-permute-start.34 = (f32[1,512]{1,0:T(1,128)S(1)}, f32[1,512]{1,0:T(1,128)S(1)}, u32[]{:S(2)}, u32[]{:S(2)}) collective-permute-start(f32[1,512]{1,0:T(1,128)S(1)} %collective-permute-done.29), channel_id=1, source_target_pairs={{1,2},{2,3},{5,6},{6,7},{9,10},{10,11},{13,14},{14,15},{17,18},{18... | collective-permute-start | bytes 6152 | tf_op jit(solution)/shard_map/ppermute | solution.py:67
  604.6 44.1 %collective-permute-start.35 = (f32[1,512]{1,0:T(1,128)S(1)}, f32[1,512]{1,0:T(1,128)S(1)}, u32[]{:S(2)}, u32[]{:S(2)}) collective-permute-start(f32[1,512]{1,0:T(1,128)S(1)} %collective-permute-done.30), channel_id=1, source_target_pairs={{1,0},{2,1},{5,4},{6,5},{9,8},{10,9},{13,12},{14,13},{17,16},{18,1... | collective-permute-start | bytes 6152 | tf_op jit(solution)/shard_map/ppermute | solution.py:68
  607.7 40.9 %collective-permute-start.36 = (f32[1,1]{1,0:T(1,128)}, f32[1,1]{1,0:T(1,128)}, u32[]{:S(2)}, u32[]{:S(2)}) collective-permute-start(f32[1,1]{1,0:T(1,128)} %add.581), channel_id=1, source_target_pairs={{0,2},{1,3},{2,0},{3,1},{4,6},{5,7},{6,4},{7,5},{8,10},{9,11},{10,... | collective-permute-start | bytes 20 | tf_op jit(solution)/shard_map/ppermute | solution.py:165
  650.5 46.7 %collective-permute-start.37 = (bf16[512,1536]{1,0:T(8,128)(2,1)S(1)}, bf16[512,1536]{1,0:T(8,128)(2,1)S(1)}, u32[]{:S(2)}, u32[]{:S(2)}) collective-permute-start(bf16[512,1536]{1,0:T(8,128)(2,1)S(1)} %collective-permute-done.32), channel_id=1, source_target_pairs={{2,3},{6,7},{10,11},{14,15},{18,19},{22,23},{26,27},{30,31}} | collective-permute-start | bytes 4718600 | tf_op jit(solution)/shard_map/ppermute | solution.py:67
  651.3 45.9 %collective-permute-start.38 = (bf16[512,1536]{1,0:T(8,128)(2,1)S(1)}, bf16[512,1536]{1,0:T(8,128)(2,1)S(1)}, u32[]{:S(2)}, u32[]{:S(2)}) collective-permute-start(bf16[512,1536]{1,0:T(8,128)(2,1)S(1)} %collective-permute-done.33), channel_id=1, source_target_pairs={{1,0},{5,4},{9,8},{13,12},{17,16},{21,20},{25,24},{29,28}} | collective-permute-start | bytes 4718600 | tf_op jit(solution)/shard_map/ppermute | solution.py:68
  652.6 37.5 %collective-permute-start.39 = (f32[1,512]{1,0:T(1,128)S(1)}, f32[1,512]{1,0:T(1,128)S(1)}, u32[]{:S(2)}, u32[]{:S(2)}) collective-permute-start(f32[1,512]{1,0:T(1,128)S(1)} %collective-permute-done.34), channel_id=1, source_target_pairs={{2,3},{6,7},{10,11},{14,15},{18,19},{22,23},{26,27},{30,31}} | collective-permute-start | bytes 6152 | tf_op jit(solution)/shard_map/ppermute | solution.py:67
  653.2 43.9 %collective-permute-start.40 = (f32[1,512]{1,0:T(1,128)S(1)}, f32[1,512]{1,0:T(1,128)S(1)}, u32[]{:S(2)}, u32[]{:S(2)}) collective-permute-start(f32[1,512]{1,0:T(1,128)S(1)} %collective-permute-done.35), channel_id=1, source_target_pairs={{1,0},{5,4},{9,8},{13,12},{17,16},{21,20},{25,24},{29,28}} | collective-permute-start | bytes 6152 | tf_op jit(solution)/shard_map/ppermute | solution.py:68
  737.4 45.7 %collective-permute-start.42 = (bf16[512,1536]{1,0:T(8,128)(2,1)}, bf16[512,1536]{1,0:T(8,128)(2,1)}, u32[]{:S(2)}, u32[]{:S(2)}) collective-permute-start(bf16[512,1536]{1,0:T(8,128)(2,1)} %get-tuple-element.365), channel_id=1, source_target_pairs={{0,1},{4,5},{8,9},{12,13},{16,17},{20,21},{24,25},{28,29}} | collective-permute-start | bytes 4718600 | tf_op jit(solution)/shard_map/ppermute | solution.py:134
  783.0 59.1 %collective-permute-start.51 = (bf16[4,5,192,768]{3,2,1,0:T(8,128)(2,1)}, bf16[4,5,192,768]{3,2,1,0:T(8,128)(2,1)}, u32[]{:S(2)}, u32[]{:S(2)}) collective-permute-start(bf16[4,5,192,768]{3,2,1,0:T(8,128)(2,1)} %get-tuple-element.397), channel_id=1, source_target_pairs={{0,4},{4,0},{8,12},{12,8},{16,20},{20,16},{24,28},{28,24},{1,5},{5... | collective-permute-start | bytes 17694728 | tf_op jit(solution)/shard_map/ppermute | solution.py:165
  783.0 69.0 %collective-permute-start.50 = (bf16[4,5,192,768]{3,2,1,0:T(8,128)(2,1)}, bf16[4,5,192,768]{3,2,1,0:T(8,128)(2,1)}, u32[]{:S(2)}, u32[]{:S(2)}) collective-permute-start(bf16[4,5,192,768]{3,2,1,0:T(8,128)(2,1)} %get-tuple-element.395), channel_id=1, source_target_pairs={{0,4},{4,0},{8,12},{12,8},{16,20},{20,16},{24,28},{28,24},{1,5},{5... | collective-permute-start | bytes 17694728 | tf_op jit(solution)/shard_map/ppermute | solution.py:165
  788.4 38.5 %collective-permute-start.45 = (bf16[512,1536]{1,0:T(8,128)(2,1)}, bf16[512,1536]{1,0:T(8,128)(2,1)S(1)}, u32[]{:S(2)}, u32[]{:S(2)}) collective-permute-start(bf16[512,1536]{1,0:T(8,128)(2,1)} %get-tuple-element.378), channel_id=1, source_target_pairs={{0,1},{1,2},{4,5},{5,6},{8,9},{9,10},{12,13},{13,14},{16,17},{17,1... | collective-permute-start | bytes 4718600 | tf_op jit(solution)/shard_map/ppermute | solution.py:134
  829.8 74.5 %collective-permute-start.49 = (bf16[4,5,192,768]{3,2,1,0:T(8,128)(2,1)}, bf16[4,5,192,768]{3,2,1,0:T(8,128)(2,1)}, u32[]{:S(2)}, u32[]{:S(2)}) collective-permute-start(bf16[4,5,192,768]{3,2,1,0:T(8,128)(2,1)} %get-tuple-element.393), channel_id=1, source_target_pairs={{0,4},{4,0},{8,12},{12,8},{16,20},{20,16},{24,28},{28,24},{1,5},{5... | collective-permute-start | bytes 17694728 | tf_op jit(solution)/shard_map/ppermute | solution.py:165
  829.9 90.9 %collective-permute-start.48 = (bf16[4,5,192,768]{3,2,1,0:T(8,128)(2,1)}, bf16[4,5,192,768]{3,2,1,0:T(8,128)(2,1)}, u32[]{:S(2)}, u32[]{:S(2)}) collective-permute-start(bf16[4,5,192,768]{3,2,1,0:T(8,128)(2,1)} %get-tuple-element.391), channel_id=1, source_target_pairs={{0,4},{4,0},{8,12},{12,8},{16,20},{20,16},{24,28},{28,24},{1,5},{5... | collective-permute-start | bytes 17694728 | tf_op jit(solution)/shard_map/ppermute | solution.py:165
  830.7 45.1 %collective-permute-start.52 = (bf16[512,1536]{1,0:T(8,128)(2,1)S(1)}, bf16[512,1536]{1,0:T(8,128)(2,1)S(1)}, u32[]{:S(2)}, u32[]{:S(2)}) collective-permute-start(bf16[512,1536]{1,0:T(8,128)(2,1)S(1)} %get-tuple-element.398), channel_id=1, source_target_pairs={{0,1},{1,2},{2,3},{4,5},{5,6},{6,7},{8,9},{9,10},{10,11},{12,13},{... | collective-permute-start | bytes 4718600 | tf_op jit(solution)/shard_map/ppermute | solution.py:134
  842.2 37.9 %collective-permute-start.53 = (bf16[512,1536]{1,0:T(8,128)(2,1)S(1)}, bf16[512,1536]{1,0:T(8,128)(2,1)S(1)}, u32[]{:S(2)}, u32[]{:S(2)}) collective-permute-start(bf16[512,1536]{1,0:T(8,128)(2,1)S(1)} %get-tuple-element.399), channel_id=1, source_target_pairs={{1,0},{2,1},{3,2},{5,4},{6,5},{7,6},{9,8},{10,9},{11,10},{13,12},{... | collective-permute-start | bytes 4718600 | tf_op jit(solution)/shard_map/ppermute | solution.py:135
  880.0 85.3 %collective-permute-start.62 = (bf16[2,5,192,768]{3,2,1,0:T(8,128)(2,1)}, bf16[2,5,192,768]{3,2,1,0:T(8,128)(2,1)}, u32[]{:S(2)}, u32[]{:S(2)}) collective-permute-start(bf16[2,5,192,768]{3,2,1,0:T(8,128)(2,1)} %add_convert_fusion.1), channel_id=1, source_target_pairs={{0,8},{4,12},{8,0},{12,4},{16,24},{20,28},{24,16},{28,20},{1,9},{5... | collective-permute-start | bytes 8847368 | tf_op jit(solution)/shard_map/ppermute | solution.py:165
  881.5 84.1 %collective-permute-start.63 = (bf16[2,5,192,768]{3,2,1,0:T(8,128)(2,1)}, bf16[2,5,192,768]{3,2,1,0:T(8,128)(2,1)}, u32[]{:S(2)}, u32[]{:S(2)}) collective-permute-start(bf16[2,5,192,768]{3,2,1,0:T(8,128)(2,1)} %add_convert_fusion), channel_id=1, source_target_pairs={{0,16},{4,20},{8,24},{12,28},{16,0},{20,4},{24,8},{28,12},{1,17},{... | collective-permute-start | bytes 8847368 | tf_op jit(solution)/shard_map/ppermute | solution.py:165
  898.0 320.0 %all-reduce.5.cloned.1.call-start = ((), (), s32[]{:S(2)}) async-start(), calls=%async_computation.4 | async-start | bytes 1179648 | tf_op jit(solution)/shard_map/psum | solution.py:969
  919.5 43.8 %collective-permute-start.58 = (bf16[384,512]{1,0:T(8,128)(2,1)S(1)}, bf16[384,512]{1,0:T(8,128)(2,1)S(1)}, u32[]{:S(2)}, u32[]{:S(2)}) collective-permute-start(bf16[384,512]{1,0:T(8,128)(2,1)S(1)} %copy-done.83), channel_id=1, source_target_pairs={{2,0},{3,1},{6,4},{7,5},{10,8},{11,9},{14,12},{15,13},{18,16},{19,... | collective-permute-start | bytes 1179656 | tf_op jit(solution)/shard_map/ppermute | solution.py:160
  920.8 42.5 %collective-permute-start.59 = (bf16[384,512]{1,0:T(8,128)(2,1)S(1)}, bf16[384,512]{1,0:T(8,128)(2,1)S(1)}, u32[]{:S(2)}, u32[]{:S(2)}) collective-permute-start(bf16[384,512]{1,0:T(8,128)(2,1)S(1)} %copy-done.82), channel_id=1, source_target_pairs={{3,0},{7,4},{11,8},{15,12},{19,16},{23,20},{27,24},{31,28}} | collective-permute-start | bytes 1179656 | tf_op jit(solution)/shard_map/ppermute | solution.py:160
  963.3 109.8 %collective-permute-start.60 = (bf16[2,5,192,768]{3,2,1,0:T(8,128)(2,1)}, bf16[2,5,192,768]{3,2,1,0:T(8,128)(2,1)}, u32[]{:S(2)}, u32[]{:S(2)}) collective-permute-start(bf16[2,5,192,768]{3,2,1,0:T(8,128)(2,1)} %add_convert_fusion.3), channel_id=1, source_target_pairs={{0,8},{4,12},{8,0},{12,4},{16,24},{20,28},{24,16},{28,20},{1,9},{5... | collective-permute-start | bytes 8847368 | tf_op jit(solution)/shard_map/ppermute | solution.py:165
  963.9 109.3 %collective-permute-start.61 = (bf16[2,5,192,768]{3,2,1,0:T(8,128)(2,1)}, bf16[2,5,192,768]{3,2,1,0:T(8,128)(2,1)}, u32[]{:S(2)}, u32[]{:S(2)}) collective-permute-start(bf16[2,5,192,768]{3,2,1,0:T(8,128)(2,1)} %add_convert_fusion.2), channel_id=1, source_target_pairs={{0,16},{4,20},{8,24},{12,28},{16,0},{20,4},{24,8},{28,12},{1,17},{... | collective-permute-start | bytes 8847368 | tf_op jit(solution)/shard_map/ppermute | solution.py:165
  1084.0 52.5 %collective-permute-start.72 = (bf16[512,1536]{1,0:T(8,128)(2,1)S(1)}, bf16[512,1536]{1,0:T(8,128)(2,1)S(1)}, u32[]{:S(2)}, u32[]{:S(2)}) collective-permute-start(bf16[512,1536]{1,0:T(8,128)(2,1)S(1)} %get-tuple-element.448), channel_id=1, source_target_pairs={{0,1},{1,2},{4,5},{5,6},{8,9},{9,10},{12,13},{13,14},{16,17},{17,1... | collective-permute-start | bytes 4718600 | tf_op jit(solution)/shard_map/ppermute | solution.py:134
  1088.4 48.8 %collective-permute-start.73 = (bf16[512,1536]{1,0:T(8,128)(2,1)S(1)}, bf16[512,1536]{1,0:T(8,128)(2,1)S(1)}, u32[]{:S(2)}, u32[]{:S(2)}) collective-permute-start(bf16[512,1536]{1,0:T(8,128)(2,1)S(1)} %get-tuple-element.449), channel_id=1, source_target_pairs={{2,1},{3,2},{6,5},{7,6},{10,9},{11,10},{14,13},{15,14},{18,17},{19... | collective-permute-start | bytes 4718600 | tf_op jit(solution)/shard_map/ppermute | solution.py:135
  1092.9 43.5 %collective-permute-start.69 = (bf16[2,192,681]{2,1,0:T(8,128)(2,1)S(1)}, bf16[2,192,681]{2,1,0:T(8,128)(2,1)S(1)}, u32[]{:S(2)}, u32[]{:S(2)}) collective-permute-start(bf16[2,192,681]{2,1,0:T(8,128)(2,1)S(1)} %add_convert_fusion.9), channel_id=1, source_target_pairs={{0,8},{4,12},{8,0},{12,4},{16,24},{20,28},{24,16},{28,20},{1,9},{5... | collective-permute-start | bytes 1569032 | tf_op jit(solution)/shard_map/ppermute | solution.py:165
  1141.6 48.6 %collective-permute-start.75 = (bf16[512,1536]{1,0:T(8,128)(2,1)}, bf16[512,1536]{1,0:T(8,128)(2,1)}, u32[]{:S(2)}, u32[]{:S(2)}) collective-permute-start(bf16[512,1536]{1,0:T(8,128)(2,1)} %get-tuple-element.453), channel_id=1, source_target_pairs={{0,1},{1,2},{2,3},{4,5},{5,6},{6,7},{8,9},{9,10},{10,11},{12,13},{... | collective-permute-start | bytes 4718600 | tf_op jit(solution)/shard_map/ppermute | solution.py:134
  1148.3 53.3 %collective-permute-start.76 = (bf16[512,1536]{1,0:T(8,128)(2,1)}, bf16[512,1536]{1,0:T(8,128)(2,1)}, u32[]{:S(2)}, u32[]{:S(2)}) collective-permute-start(bf16[512,1536]{1,0:T(8,128)(2,1)} %get-tuple-element.454), channel_id=1, source_target_pairs={{1,0},{2,1},{3,2},{5,4},{6,5},{7,6},{9,8},{10,9},{11,10},{13,12},{... | collective-permute-start | bytes 4718600 | tf_op jit(solution)/shard_map/ppermute | solution.py:135
  1149.7 68.2 %collective-permute-start.66 = (bf16[1,5,192,768]{3,2,1,0:T(8,128)(2,1)}, bf16[1,5,192,768]{3,2,1,0:T(8,128)(2,1)}, u32[]{:S(2)}, u32[]{:S(2)}) collective-permute-start(bf16[1,5,192,768]{3,2,1,0:T(8,128)(2,1)} %add_convert_fusion.5), channel_id=1, source_target_pairs={{0,16},{4,20},{8,24},{12,28},{16,0},{20,4},{24,8},{28,12},{1,17},{... | collective-permute-start | bytes 4423688 | tf_op jit(solution)/shard_map/ppermute | solution.py:165
  1151.3 66.7 %collective-permute-start.67 = (bf16[1,5,192,768]{3,2,1,0:T(8,128)(2,1)}, bf16[1,5,192,768]{3,2,1,0:T(8,128)(2,1)}, u32[]{:S(2)}, u32[]{:S(2)}) collective-permute-start(bf16[1,5,192,768]{3,2,1,0:T(8,128)(2,1)} %add_convert_fusion.4), channel_id=1, source_target_pairs={{0,8},{4,12},{8,0},{12,4},{16,24},{20,28},{24,16},{28,20},{1,9},{5... | collective-permute-start | bytes 4423688 | tf_op jit(solution)/shard_map/ppermute | solution.py:165
  (168 other events, 3338.3 us)
Sparse Core Ops, SparseCore 0:
  13.0 51.5 all-gather.2
  67.4 218.1 all-gather.4
  898.1 68.3 reduce-scatter.1
  1154.7 51.1 all-reduce.4

commit v8 on v7

--- a/solution.py
+++ b/solution.py
@@ -153,11 +153,12 @@
 def exchange(blocks):
     n = lax.axis_size("seq")
     me = lax.axis_index("seq")
-    rights, lefts = [at_place(blocks, me)], [at_place(blocks, me)]
-    for k in range(1, n):
+    own = at_place(blocks, me)
+    rights, lefts = [own] * n, [own] * n
+    for k in range(n - 1, 0, -1):
         to_right, to_left = at_place(blocks, me + k), at_place(blocks, me - k)
-        rights.append(lax.ppermute(to_right, "seq", [(i, i + k) for i in range(n - k)]))
-        lefts.append(lax.ppermute(to_left, "seq", [(i, i - k) for i in range(k, n)]))
+        rights[k] = lax.ppermute(to_right, "seq", [(i, i + k) for i in range(n - k)])
+        lefts[k] = lax.ppermute(to_left, "seq", [(i, i - k) for i in range(k, n)])
     return rights, lefts
 
 
@@ -627,51 +628,39 @@
     return masks
 
 
-def grads_kernel(bits_a, bits_b, me_ref, x_ref, dgu_ref, act_ref, d_ref, *refs):
-    outs, gu_acc, down_acc = refs[-6:-2], refs[-2], refs[-1]
-    hidden, width = act_ref.shape[2], d_ref.shape[2]
-    gu_acc[...] = tn(x_ref[0], dgu_ref[0])
-    down_acc[...] = tn(act_ref[0], d_ref[0])
+def grads_kernel(few, x_ref, dgu_ref, act_ref, d_ref, *refs):
+    out_ref, down = refs[-2], refs[-1]
+    hidden, width = down.shape
+    out_ref[0, :, : 2 * hidden] = tn(x_ref[0], dgu_ref[0]).astype(low)
+    down[...] = tn(act_ref[0], d_ref[0]).astype(low)
     chunks = width // hidden
-    for part, bits in enumerate((bits_a, bits_b)):
-        keep, send = outs[2 * part], outs[2 * part + 1]
-        rows = keep.shape[2]
-        few = rows // chunks
-        for place, mask in enumerate(halving_masks(bits)):
-            out = keep if place < keep.shape[0] else send
-            spot = place % keep.shape[0]
-            start = pl.multiple_of((me_ref[0] ^ mask) * rows, rows)
-            block = gu_acc[pl.ds(start, rows), part * hidden : (part + 1) * hidden]
-            out[spot, 0, :, :hidden] = block.astype(low)
-            start = pl.multiple_of((me_ref[0] ^ mask) * few, few)
-            for chunk in range(chunks):
-                first = part * (width // 2) + chunk * (hidden // 2)
-                block = down_acc[pl.ds(start, few), first : first + hidden // 2]
-                out[spot, 0, chunk * few : (chunk + 1) * few, hidden:] = block.astype(low)
-
-
-def weight_grads(me, rows, d_gu, act, d_rows, bits_a, bits_b, first, stop):
-    _, count, width = rows.shape
+    for dev in range(hidden // few):
+        for chunk in range(chunks):
+            start = (dev * chunks + chunk) * few
+            out_ref[0, start : start + few, 2 * hidden :] = down[
+                dev * few : (dev + 1) * few, chunk * hidden : (chunk + 1) * hidden
+            ]
+
+
+def weight_grads(rows, d_gu, act, d_rows, few, first, stop, buffers):
+    experts, count, width = rows.shape
     hidden = act.shape[2]
-    devs = 2 ** len(bits_a)
-    shape = (width // devs, hidden + hidden // 2)
 
     def part(*block):
-        return pl.BlockSpec((1,) + block, lambda e, me: (first + e, 0, 0))
+        return pl.BlockSpec((1,) + block, lambda e: (first + e, 0, 0))
 
     return pl.pallas_call(
-        functools.partial(grads_kernel, bits_a, bits_b),
-        grid_spec=pltpu.PrefetchScalarGridSpec(
-            num_scalar_prefetch=1,
-            grid=(stop - first,),
-            in_specs=[part(count, width), part(count, 2 * hidden), part(count, hidden), part(count, width)],
-            out_specs=[pl.BlockSpec((devs // 2, 1) + shape, lambda e, me: (0, e, 0, 0))] * 4,
-            scratch_shapes=[pltpu.VMEM((width, 2 * hidden), full), pltpu.VMEM((hidden, width), full)],
-        ),
-        out_shape=[jax.ShapeDtypeStruct((devs // 2, stop - first) + shape, low)] * 4,
+        functools.partial(grads_kernel, few),
+        grid=(stop - first,),
+        in_specs=[part(count, width), part(count, 2 * hidden), part(count, hidden), part(count, width)]
+        + [pl.BlockSpec(memory_space=pl.ANY)] * len(buffers),
+        out_specs=part(width, 3 * hidden),
+        out_shape=jax.ShapeDtypeStruct((experts, width, 3 * hidden), low),
+        scratch_shapes=[pltpu.VMEM((hidden, width), low)],
+        input_output_aliases={4 + i: i for i in range(len(buffers))},
         compiler_params=vmem(56),
         name="weight_grads",
-    )(me, rows, d_gu, act, d_rows)
+    )(rows, d_gu, act, d_rows, *buffers)
 
 
 def shards(
@@ -740,8 +729,7 @@
     expert_weights = (w_gate, w_up, w_down)
     for turn in range(n):
         if turn < n - 1:
-            right, left, block = tie(rights[turn], lefts[turn], block)
-            right, left = line_move(right, left, turn + 1)
+            right, left = line_move(rights[turn], lefts[turn], turn + 1)
         start = order[turn] * shard_len
         normed = rms_norm(block[:shard_len].astype(full), full_g1).astype(low)
         projected = dot("td,dc->ct", normed, full_qkv)
@@ -810,8 +798,7 @@
     buffers, gates = [], []
     for turn in range(n):
         if turn < n - 1:
-            right, left, tokens[turn] = tie(rights[turn], lefts[turn], tokens[turn])
-            right, left = line_move(right, left, turn + 1)
+            right, left = line_move(rights[turn], lefts[turn], turn + 1)
         *buffers, shard_gates = experts_forward(
             turn, n, jnp.stack([order[turn], me]), tokens[turn], slot_of[turn], member[turn],
             router, weights, w_down.shape[1], slots, buffers,
@@ -844,11 +831,8 @@
     buffers, d_logits = [], []
     for turn in range(n):
         if turn < n - 1:
-            (right, left), (dot_right, dot_left), d_tokens = tie(
-                (rights[turn], lefts[turn]), (dot_rights[turn], dot_lefts[turn]), d_tokens
-            )
-            dot_right, dot_left = line_move(dot_right, dot_left, turn + 1)
-            right, left = line_move(right, left, turn + 1)
+            dot_right, dot_left = line_move(dot_rights[turn], dot_lefts[turn], turn + 1)
+            right, left = line_move(rights[turn], lefts[turn], turn + 1)
         *buffers, shard_logits = experts_backward(
             turn, n, jnp.stack([order[turn], me]), d_tokens, slot_of[turn], gates[turn], mix_dot,
             own_router, gate_up, weights, w_down.shape[1], buffers,
@@ -873,134 +857,119 @@
 
     right = left = None
     cut = (experts_here + 1) // 2
-    sums = [None, None]
+    grads = []
     for k in range(n - 1, 0, -1):
         moving = line_send(d_parts, k, right, left)
         if k >= n - 2:
-            half = n - 1 - k
             moving, d_rows = tie(moving, d_rows)
             right, left = line_pass(*moving, k)
-            if half:
-                for each in sums[0]:
-                    each.go()
-            grads = weight_grads(
-                mine.reshape(1), expert_in, d_gate_up, act_low, d_rows, order_a, order_b,
-                *((cut, experts_here) if half else (0, cut)),
-            )
+            part = (0, cut) if k == n - 1 else (cut, experts_here)
+            grads = [
+                weight_grads(expert_in, d_gate_up, act_low, d_rows, w_down.shape[1], *part, grads)
+            ]
             right, left, grads, squares = tie(right, left, grads, squares)
-            sums[half] = [Halving(*grads[:2], order_a), Halving(*grads[2:], order_b)]
-        elif k == n - 3:
-            (moving,) = leave(sums[1], moving)
-            right, left = line_pass(*moving, k)
-            for each in sums[1]:
-                each.go()
-            for each in sums[0]:
-                each.add()
-            right, left, squares = leave(sums[0], right, left, squares)
-            for each in sums[0]:
-                each.go()
         else:
             right, left, squares = tie(*line_pass(*tie(*moving), k), squares)
         squares = loss_steps.send(squares)
+    expert_sum = lax.psum_scatter(grads[0], "fsdp", scatter_dimension=1, tiled=True)
     d_normed_two = line_end(d_parts, right, left)
 
     d_hidden_norm, gain_two_part = norm_two_pull(d_normed_two)
     d_hidden = d_out + d_hidden_norm
     d_proj = (resid_mult * d_hidden).astype(low)
+    out_part = dot("kt,td->kd", attn_rows, d_proj).astype(low)
+    middle = width // 2
+    out_sums = [
+        rows_halving(out_part[:, :middle], order_a),
+        rows_halving(out_part[:, middle:], order_b),
+    ]
     d_attended = dot("kd,td->kt", full_out, d_proj).astype(low)
+    d_attended, _ = tie(d_attended, [each.send for each in out_sums])
     moved = exchange(d_attended.reshape(n, heads_w, shard_len))
-    for each in sums[1]:
+    for each in out_sums:
+        each.go()
         each.add()
-    out_part = dot("kt,td->kd", attn_rows, d_proj).astype(low)
-    out_sum = lax.psum_scatter(out_part, "fsdp", scatter_dimension=0, tiled=True)
     router_part = sum(
         dot("td,et->de", shard, shard_logits[:experts_here])
         for shard, shard_logits in zip(tokens, d_logits)
     )
-    moved, out_part, router_part = leave(sums[1], moved, out_part, router_part)
-    for each in sums[1]:
+    moved, router_part = leave(out_sums, moved, router_part)
+    for each in out_sums:
         each.go()
-    (moved,) = land(sums[0], moved)
     d_heads = by_place(nearest(*moved))
-    for each in sums[0]:
-        each.add()
-    (d_heads,) = leave(sums[0], d_heads)
-    for each in sums[0]:
-        each.go()
     query_grad, key_grad, value_grad = attention_backward(
         heads, key_rows, value_rows, key, limit, out_heads, lse, d_heads
     )
+    ((query_grad, key_grad, value_grad),) = land(out_sums, (query_grad, key_grad, value_grad))
+    for each in out_sums:
+        each.add()
+        each.go()
     d_turned = jnp.concatenate([query_grad, key_grad[:, None]], axis=1).astype(full)
     d_turned = rotate(d_turned, cosine, -sine_vals).astype(low)
     d_qkv = jnp.concatenate([d_turned, value_grad[:, None]], axis=1).reshape(group_w, seq_len)
     d_parts = dot("ct,dc->td", d_qkv, full_qkv).astype(low).reshape(n, shard_len, width)
-
+    own_columns = jnp.zeros((width, expert_total), full)
+    own_columns = lax.dynamic_update_slice_in_dim(own_columns, router_part, me * experts_here, 1)
+    (d_parts,) = land(out_sums, d_parts)
+    for each in out_sums:
+        each.add()
+
+    out_sum = jnp.concatenate([each.finish() for each in out_sums], axis=1).astype(low)
+    out_rows = out_sum.shape[0] // n
+    out_parts = jnp.swapaxes(out_sum.reshape(out_sum.shape[0], n, width // n), 0, 1)
+    d_parts = jnp.concatenate([d_parts, out_parts.reshape(n, out_rows, width)], axis=1)
     right = left = None
     for k in range(n - 1, 0, -1):
-        moving = line_send(d_parts, k, right, left)
+        moving = tie(*line_send(d_parts, k, right, left))
         if k == n - 1:
             moving, d_qkv = tie(moving, d_qkv)
-            right, left = line_pass(*moving, k)
-            own_columns = jnp.zeros((width, expert_total), full)
-            own_columns = lax.dynamic_update_slice_in_dim(
-                own_columns, router_part, me * experts_here, 1
-            )
+        right, left = line_pass(*moving, k)
+        if k == n - 1:
             qkv_part = jnp.concatenate(
                 [dot("td,ct->dc", normed_one, d_qkv), own_columns, gain_two_part[:, None]], axis=1
             ).astype(low)
             qkv_sum = rows_halving(qkv_part, order_a)
-            (right, left) = land(sums[1], right, left)
-            for each in sums[1]:
-                each.add()
-            right, left = leave(sums[1] + [qkv_sum], right, left)
+            right, left = leave([qkv_sum], right, left)
             qkv_sum.go()
+        elif k in (n - 2, n - 3):
+            right, left = land([qkv_sum], right, left)
             qkv_sum.add()
             qkv_sum.go()
-            for each in sums[1]:
-                each.go()
         else:
-            right, left = line_pass(*tie(*moving), k)
-            if k == n - 2:
-                right, left, out_sum = land([qkv_sum] + sums[0], right, left, out_sum)
-                qkv_sum.add()
-                qkv_sum.go()
-                for each in sums[0]:
-                    each.add()
-                out_sum = lax.psum(out_sum, "seq")
-            elif k == 1:
-                right, left = land([qkv_sum], right, left)
-            else:
-                right, left = tie(right, left)
+            right, left = tie(right, left)
+    ended = line_end(d_parts, right, left)
+    d_normed_one = ended[:shard_len]
+    (ended,) = land([qkv_sum], ended)
     qkv_sum.add()
-    blocks = line_gather(qkv_sum.finish().astype(low))
-    d_normed_one = line_end(d_parts, right, left)
+    out_own = ended[shard_len:].reshape(out_sum.shape[0], width // n)
+    blocks = line_gather(jnp.concatenate([qkv_sum.finish(), out_own], axis=1).astype(low))
     _, norm_one_pull = jax.vjp(lambda v: rms_norm(v, full_g1), x_low.astype(full))
     input_grad = (d_hidden + norm_one_pull(d_normed_one)[0]).reshape(1, shard_len, width)
-    input_grad, out_sum = land(sums[1], input_grad, out_sum)
-    for each in sums[1]:
-        each.add()
-    left_sum, right_sum = (
-        jnp.concatenate([sums[0][side].finish(), sums[1][side].finish()]) for side in (0, 1)
-    )
-    gate_grad, up_grad = left_sum[:, :, :hidden_w], right_sum[:, :, :hidden_w]
+    input_grad, expert_sum = tie(input_grad, expert_sum)
+    expert_sum = expert_sum.astype(full)
+    gate_grad = expert_sum[:, :, :hidden_w]
+    up_grad = expert_sum[:, :, hidden_w : 2 * hidden_w]
     few = w_down.shape[1]
     down_grad = jnp.concatenate(
         [
-            part[:, start : start + few, hidden_w:]
-            for part in (left_sum, right_sum)
-            for start in range(0, part.shape[1], few)
+            expert_sum[:, start : start + few, 2 * hidden_w :]
+            for start in range(0, expert_sum.shape[1], few)
         ],
         axis=2,
     )
-    out_grad = out_sum.astype(full)
     qkv_grad = jnp.zeros((w_qkv.shape[0], QKV_W), full)
+    out_grad = jnp.zeros((w_out.shape[0], width), full)
     rest = 0.0
     for k, block in enumerate(blocks):
         block = block.astype(full)
+        place = (me - k) % n
         qkv_grad = lax.dynamic_update_slice_in_dim(
-            qkv_grad, block[:, :group_w], ((me - k) % n) * group_w, 1
+            qkv_grad, block[:, :group_w], place * group_w, 1
         )
-        rest = rest + block[:, group_w:]
+        out_grad = lax.dynamic_update_slice_in_dim(
+            out_grad, block[:, -(width // n) :], place * (width // n), 1
+        )
+        rest = rest + block[:, group_w : -(width // n)]
     router_grad, gain_two_grad = rest[:, :expert_total], rest[:, expert_total]
     gain_one_grad = jnp.sum(qkv_grad * w_qkv.astype(full), axis=1) / gain_one.astype(full)
     for _ in range(2):

time: 1280 us -> 1260 us (0.984)
  other arithmetic: 160 us -> 115 us
  local copies, waits for them, and re-layouts: 55.1 us -> 98.4 us
    ppermute x9, waiting for transfers between devices: 114 us -> 173 us  [line_pass(): lax.ppermute(to_right, 'seq', [(i, i + 1) for i in range(n - k)])]
    ppermute x23 -> x17, waiting for transfers between devices: 72 us -> 22.4 us  [swap(): lax.ppermute(value, axis, [(i, i ^ bit) for i in range(lax.axis_size(axis...]
    convert_element_type x10 -> x6, other arithmetic: 38.3 us -> 5.98 us  [add(): sum((term[half:].astype(full) for term in self.terms)).astype(low)]
    add x4 -> x1, other arithmetic: 15.2 us -> 1.53 us  [finish(): return sum((term[0].astype(full) for term in self.terms))]
    ppermute x15, waiting for transfers between devices: 104 us -> 90.6 us  [line_move(): lax.ppermute(left, 'seq', [(i, i - 1) for i in range(1, n - k + 1)])]
    unnamed x261 -> x244, local copies, waits for them, and re-layouts: 16.3 us -> 26.6 us
    ppermute x23 -> x17, starting transfers between devices: 34.1 us -> 29.4 us  [swap(): lax.ppermute(value, axis, [(i, i ^ bit) for i in range(lax.axis_size(axis...]
  transfers between devices with their start and end apart: 87 -> 80, of which waited for: 37 -> 38; matrix products, arithmetic and copies ran while one was open for 15% -> 16% of each run, Pallas kernels for 26% -> 26%
where the time goes in v8:
time: 1260 us; the launch traced here: 1250 us
  waiting for transfers between devices  407 us (32%)
  Pallas kernels  380 us (30%)
  starting transfers between devices  170 us (13%)
  other arithmetic  115 us (9%)
  local copies, waits for them, and re-layouts  98.4 us (8%)
  matrix products  44.3 us (4%)
  between operations  34.7 us (3%)
    pallas_call x8, Pallas kernels, shard_call(): pl.pallas_call(kernel, grid_spec=pltpu.PrefetchScalarGridSpec(num_scalar_...  236 us
    ppermute x9, waiting for transfers between devices, line_pass(): lax.ppermute(to_right, 'seq', [(i, i + 1) for i in range(n - k)])  173 us
    ppermute x15, waiting for transfers between devices, line_move(): lax.ppermute(left, 'seq', [(i, i - 1) for i in range(1, n - k + 1)])  90.6 us
    ppermute x9, starting transfers between devices, line_pass(): lax.ppermute(to_right, 'seq', [(i, i + 1) for i in range(n - k)])  59.1 us
    pallas_call x1, Pallas kernels, attention_backward(): pl.pallas_call(functools.partial(backward_kernel, seq_len, query_rows, ke...  54.1 us
    pallas_call x2, Pallas kernels, weight_grads(): pl.pallas_call(functools.partial(grads_kernel, few), grid=(stop - first,)...  50.8 us
    ppermute x6, waiting for transfers between devices, exchange(): lefts[k] = lax.ppermute(to_left, 'seq', [(i, i - k) for i in range(k, n)])  45.4 us
    dot_general x14, matrix products, dot(): return jnp.einsum(spec, left, right, preferred_element_type=full)  44.3 us
  transfers between devices with their start and end apart: 80, of which 38 were waited for; matrix products, arithmetic and copies ran while one was open for 16% of the time, Pallas kernels for 26%

profile of v8, /device:TPU:0, one launch (start us, length us, event | category | flops | bytes accessed | tf_op | source)
XLA Modules:
  0.0 1249.3 jit_solution(16970277408800825290)
XLA Ops:
  15.1 5.3 collective-permute-start
  21.7 33.3 %collective-permute-done = bf16[528,1536]{1,0:T(8,128)(2,1)S(1)} collective-permute-done((bf16[528,1536]{1,0:T(8,128)(2,1)S(1)}, bf16[528,1536]{1,0:T(8,128)(2,1)S(1)}, u32[]{:S(2)}, u32[]{:S(2)}) %collective-permute-start) | collective-permute-done | bytes 1622048 | tf_op jit(solution)/shard_map/ppermute | solution.py:67
  59.6 6.5 maximum_maximum_fusion
  108.2 14.4 %collective-permute-done.3 = bf16[528,1536]{1,0:T(8,128)(2,1)} collective-permute-done((bf16[528,1536]{1,0:T(8,128)(2,1)}, bf16[528,1536]{1,0:T(8,128)(2,1)}, u32[]{:S(2)}, u32[]{:S(2)}) %collective-permute-start.3) | collective-permute-done | bytes 1622048 | tf_op jit(solution)/shard_map/ppermute | solution.py:68
  138.2 24.6 %collective-permute-done.5 = bf16[528,1536]{1,0:T(8,128)(2,1)} collective-permute-done((bf16[528,1536]{1,0:T(8,128)(2,1)}, bf16[528,1536]{1,0:T(8,128)(2,1)}, u32[]{:S(2)}, u32[]{:S(2)}) %collective-permute-start.5) | collective-permute-done | bytes 1622048 | tf_op jit(solution)/shard_map/ppermute | solution.py:68
  179.4 39.6 %attention_forward.1 = (bf16[4,384,512]{2,1,0:T(8,128)(2,1)S(1)}, f32[2,3,64,2048]{3,2,1,0:T(8,128)S(1)}, f32[2,3,1,2048]{3,2,1,0:T(1,128)S(1)}) custom-call(s32[1,2048]{1,0:T(1,128)S(1)} %bitcast.276, bf16[4,2,5,64,512]{4,3,2,1,0:T(8,128)(2,1)S(1)} %fusion.62.q_ref, bf16[2,2048,64]{2,1,0:T(8,128)(2,1)S(1)} %copy-done.6, bf16[2,64,2048]{2,1,0:T(8,128)(2,1)S(1)} %copy-done.10), custom_call_target="tpu_custom_call" | custom-call | tf_op jit(solution)/shard_map/attention_forward/pallas_call | solution.py:298
  225.5 7.5 collective-permute-start.7
  234.3 13.7 %collective-permute-done.10 = bf16[384,512]{1,0:T(8,128)(2,1)S(1)} collective-permute-done((bf16[384,512]{1,0:T(8,128)(2,1)S(1)}, bf16[384,512]{1,0:T(8,128)(2,1)S(1)}, u32[]{:S(2)}, u32[]{:S(2)}) %collective-permute-start.10) | collective-permute-done | bytes 393248 | tf_op jit(solution)/shard_map/ppermute | solution.py:161
  251.7 9.2 collective-permute-done.9
  274.5 11.1 all-gather.5.cloned.1.call-done.wgu_ref.wd_ref
  286.5 27.1 %experts_forward.4 = (bf16[4,512,1536]{2,1,0:T(8,128)(2,1)}, bf16[10,4,160,1536]{3,2,1,0:T(8,128)(2,1)}, bf16[10,4,160,1024]{3,2,1,0:T(8,128)(2,1)}, f32[10,512]{1,0:T(8,128)S(1)}) custom-call(s32[2]{0:T(128)S(1)} %get-tuple-element.503.at_ref, bf16[512,1536]{1,0:T(8,128)(2,1)} %multiply_convert_fusion.1.tok_ref, s32[10,512]{1,0:T(8,128)S(1)} %get-tuple-element.485.slot_ref, ...), custom_call_target="tpu_custom_call" | custom-call | tf_op jit(solution)/shard_map/experts_forward/pallas_call | solution.py:516
  319.9 26.7 %experts_forward.5 = (bf16[4,512,1536]{2,1,0:T(8,128)(2,1)}, bf16[10,4,160,1536]{3,2,1,0:T(8,128)(2,1)}, bf16[10,4,160,1024]{3,2,1,0:T(8,128)(2,1)}, f32[10,512]{1,0:T(8,128)S(1)}) custom-call(s32[2]{0:T(128)S(1)} %get-tuple-element.504.at_ref, ...), custom_call_target="tpu_custom_call", output_to_operand_aliasing={{0}: (7, {}), {1}: (8, {}), {2}: (9, {})} | custom-call | tf_op jit(solution)/shard_map/experts_forward/pallas_call | solution.py:516
  346.7 9.2 collective-permute-done.15
  360.0 26.7 %experts_forward.6 = (bf16[4,512,1536]{2,1,0:T(8,128)(2,1)}, bf16[10,4,160,1536]{3,2,1,0:T(8,128)(2,1)}, bf16[10,4,160,1024]{3,2,1,0:T(8,128)(2,1)}, f32[10,512]{1,0:T(8,128)S(1)}) custom-call(s32[2]{0:T(128)S(1)} %get-tuple-element.505.at_ref, ...), custom_call_target="tpu_custom_call", output_to_operand_aliasing={{0}: (7, {}), {1}: (8, {}), {2}: (9, {})} | custom-call | tf_op jit(solution)/shard_map/experts_forward/pallas_call | solution.py:516
  386.7 7.7 collective-permute-done.17
  396.5 26.7 %experts_forward.7 = (bf16[4,512,1536]{2,1,0:T(8,128)(2,1)}, bf16[10,4,160,1536]{3,2,1,0:T(8,128)(2,1)}, bf16[10,4,160,1024]{3,2,1,0:T(8,128)(2,1)}, f32[10,512]{1,0:T(8,128)S(1)}) custom-call(s32[2]{0:T(128)S(1)} %get-tuple-element.502.at_ref, ...), custom_call_target="tpu_custom_call", output_to_operand_aliasing={{0}: (7, {}), {1}: (8, {}), {2}: (9, {})} | custom-call | tf_op jit(solution)/shard_map/experts_forward/pallas_call | solution.py:516
  427.9 31.6 %collective-permute-done.18 = bf16[512,1536]{1,0:T(8,128)(2,1)S(1)} collective-permute-done((bf16[512,1536]{1,0:T(8,128)(2,1)S(1)}, bf16[512,1536]{1,0:T(8,128)(2,1)S(1)}, u32[]{:S(2)}, u32[]{:S(2)}) %collective-permute-start.18) | collective-permute-done | bytes 1572896 | tf_op jit(solution)/shard_map/ppermute | solution.py:134
  465.8 30.7 %collective-permute-done.20 = bf16[512,1536]{1,0:T(8,128)(2,1)S(1)} collective-permute-done((bf16[512,1536]{1,0:T(8,128)(2,1)S(1)}, bf16[512,1536]{1,0:T(8,128)(2,1)S(1)}, u32[]{:S(2)}, u32[]{:S(2)}) %collective-permute-start.20) | collective-permute-done | bytes 1572896 | tf_op jit(solution)/shard_map/ppermute | solution.py:134
  499.0 7.5 collective-permute-start.22
  519.4 16.9 %collective-permute-done.22 = bf16[512,1536]{1,0:T(8,128)(2,1)} collective-permute-done((bf16[512,1536]{1,0:T(8,128)(2,1)}, bf16[512,1536]{1,0:T(8,128)(2,1)}, u32[]{:S(2)}, u32[]{:S(2)}) %collective-permute-start.22) | collective-permute-done | bytes 1572896 | tf_op jit(solution)/shard_map/ppermute | solution.py:134
  564.3 32.3 %experts_backward.4 = (bf16[4,512,1536]{2,1,0:T(8,128)(2,1)}, bf16[10,4,160,1536]{3,2,1,0:T(8,128)(2,1)}, bf16[10,4,160,1024]{3,2,1,0:T(8,128)(2,1)}, bf16[10,4,...) custom-call(s32[2]{0:T(128)S(1)} %copy-done.30, bf16[512,1536]{1,0:T(8,128)(2,1)S(1)} %get-tuple-element.410.tok_ref, ...), custom_call_target="tpu_custom_call" | custom-call | tf_op jit(solution)/shard_map/experts_backward/pallas_call | solution.py:516
  603.5 10.1 collective-permute-start.36
  613.6 32.2 %experts_backward.5 = (bf16[4,512,1536]{2,1,0:T(8,128)(2,1)}, bf16[10,4,160,1536]{3,2,1,0:T(8,128)(2,1)}, bf16[10,4,160,1024]{3,2,1,0:T(8,128)(2,1)}, bf16[10,4,...) custom-call(s32[2]{0:T(128)S(1)} %copy-done.28, ...), custom_call_target="tpu_custom_call", output_to_operand_aliasing={{0}: (9, {}), {1}: (10, {}), {2}: (11, {}), {3}: (12, {})} | custom-call | tf_op jit(solution)/shard_map/experts_backward/pallas_call | solution.py:516
  654.9 32.1 %experts_backward.6 = (bf16[4,512,1536]{2,1,0:T(8,128)(2,1)}, bf16[10,4,160,1536]{3,2,1,0:T(8,128)(2,1)}, bf16[10,4,160,1024]{3,2,1,0:T(8,128)(2,1)}, bf16[10,4,...) custom-call(s32[2]{0:T(128)S(1)} %get-tuple-element.505.at_ref, ...), custom_call_target="tpu_custom_call", output_to_operand_aliasing={{0}: (9, {}), {1}: (10, {}), {2}: (11, {}), {3}: (12, {})} | custom-call | tf_op jit(solution)/shard_map/experts_backward/pallas_call | solution.py:516
  694.5 32.2 %experts_backward.7 = (bf16[4,512,1536]{2,1,0:T(8,128)(2,1)}, bf16[10,4,160,1536]{3,2,1,0:T(8,128)(2,1)}, bf16[10,4,160,1024]{3,2,1,0:T(8,128)(2,1)}, bf16[10,4,...) custom-call(s32[2]{0:T(128)S(1)} %get-tuple-element.502.at_ref, ...), custom_call_target="tpu_custom_call", output_to_operand_aliasing={{0}: (9, {}), {1}: (10, {}), {2}: (11, {}), {3}: (12, {})} | custom-call | tf_op jit(solution)/shard_map/experts_backward/pallas_call | solution.py:516
  729.9 12.7 %collective-permute-start.42 = (bf16[512,1536]{1,0:T(8,128)(2,1)}, bf16[512,1536]{1,0:T(8,128)(2,1)S(1)}, u32[]{:S(2)}, u32[]{:S(2)}) collective-permute-start(bf16[512,1536]{1,0:T(8,128)(2,1)} %get-tuple-element.271), channel_id=1, source_target_pairs={{0,1},{4,5},{8,9},{12,13},{16,17},{20,21},{24,25},{28,29}} | collective-permute-start | bytes 4718600 | tf_op jit(solution)/shard_map/ppermute | solution.py:134
  746.9 25.4 %weight_grads.2.refs_0_ = bf16[10,1536,1536]{2,1,0:T(8,128)(2,1)} custom-call(bf16[10,640,1536]{2,1,0:T(8,128)(2,1)} %bitcast.281, bf16[10,640,1024]{2,1,0:T(8,128)(2,1)} %bitcast.285, bf16[10,640,512]{2,1,0:T(8,128)(2,1)} %bitcast.287, bf16[10,640,1536]{2,1,0:T(8,128)(2,1)} %bitcast.283), custom_call_target="tpu_custom_call" | custom-call | tf_op jit(solution)/shard_map/weight_grads/pallas_call | solution.py:652
  781.6 5.5 collective-permute-start.45
  791.6 25.3 %weight_grads.3 = bf16[10,1536,1536]{2,1,0:T(8,128)(2,1)} custom-call(bf16[10,640,1536]{2,1,0:T(8,128)(2,1)} %bitcast.282, bf16[10,640,1024]{2,1,0:T(8,128)(2,1)} %bitcast.286, bf16[10,640,512]{2,1,0:T(8,128)(2,1)} %bitcast.288, bf16[10,640,1536]{2,1,0:T(8,128)(2,1)} %bitcast.284, ...), custom_call_target="tpu_custom_call", output_to_operand_aliasing={{}: (4, {})} | custom-call | tf_op jit(solution)/shard_map/weight_grads/pallas_call | solution.py:652
  819.9 5.3 fusion.28
  825.2 11.4 collective-permute-start.48
  843.4 24.7 %collective-permute-done.48 = bf16[512,1536]{1,0:T(8,128)(2,1)} collective-permute-done((bf16[512,1536]{1,0:T(8,128)(2,1)}, bf16[512,1536]{1,0:T(8,128)(2,1)}, u32[]{:S(2)}, u32[]{:S(2)}) %collective-permute-start.48) | collective-permute-done | bytes 1572896 | tf_op jit(solution)/shard_map/ppermute | solution.py:134
  868.1 5.3 collective-permute-done.49
  878.6 5.4 fusion.21
  901.6 6.4 fusion.38
  927.8 7.6 collective-permute-done.54
  935.4 22.5 %collective-permute-done.56 = bf16[384,512]{1,0:T(8,128)(2,1)S(1)} collective-permute-done((bf16[384,512]{1,0:T(8,128)(2,1)S(1)}, bf16[384,512]{1,0:T(8,128)(2,1)S(1)}, u32[]{:S(2)}, u32[]{:S(2)}) %collective-permute-start.56) | collective-permute-done | bytes 393248 | tf_op jit(solution)/shard_map/ppermute | solution.py:161
  963.0 54.1 %attention_backward.1 = (bf16[2,3,64,2048]{3,2,1,0:T(8,128)(2,1)S(1)}, bf16[2,64,2048]{2,1,0:T(8,128)(2,1)S(1)}, bf16[2,64,2048]{2,1,0:T(8,128)(2,1)S(1)}) custom-call(s32[1,2048]{1,0:T(1,128)S(1)} %bitcast.277, bf16[4,2,5,64,512]{4,3,2,1,0:T(8,128)(2,1)S(1)} %fusion.62.q_ref, bf16[2,2048,64]{2,1,0:T(8,128)(2,1)S(1)} %copy-done.7, ...), custom_call_target="tpu_custom_call" | custom-call | tf_op jit(solution)/shard_map/attention_backward/pallas_call | solution.py:369
  1022.0 8.5 convolution_convert_fusion
  1055.4 7.2 convolution_convert_fusion.2
  1066.7 15.7 %collective-permute-done.62 = bf16[560,1536]{1,0:T(8,128)(2,1)} collective-permute-done((bf16[560,1536]{1,0:T(8,128)(2,1)}, bf16[560,1536]{1,0:T(8,128)(2,1)}, u32[]{:S(2)}, u32[]{:S(2)}) %collective-permute-start.62) | collective-permute-done | bytes 1720352 | tf_op jit(solution)/shard_map/ppermute | solution.py:134
  1094.8 28.1 %collective-permute-done.65 = bf16[560,1536]{1,0:T(8,128)(2,1)S(1)} collective-permute-done((bf16[560,1536]{1,0:T(8,128)(2,1)S(1)}, bf16[560,1536]{1,0:T(8,128)(2,1)S(1)}, u32[]{:S(2)}, u32[]{:S(2)}) %collective-permute-start.65) | collective-permute-done | bytes 1720352 | tf_op jit(solution)/shard_map/ppermute | solution.py:134
  1125.6 8.5 collective-permute-start.68
  1138.0 9.6 collective-permute-done.67
  1147.6 17.9 %collective-permute-done.68 = bf16[560,1536]{1,0:T(8,128)(2,1)S(1)} collective-permute-done((bf16[560,1536]{1,0:T(8,128)(2,1)}, bf16[560,1536]{1,0:T(8,128)(2,1)S(1)}, u32[]{:S(2)}, u32[]{:S(2)}) %collective-permute-start.68) | collective-permute-done | bytes 1720352 | tf_op jit(solution)/shard_map/ppermute | solution.py:134
  1188.1 8.6 collective-permute-done.72
  1200.9 10.8 collective-permute-done.74
  1213.8 8.8 collective-permute-done.76
  (566 shorter events, 364.6 us)
Async XLA Ops:
  7.2 83.8 %all-gather.3.cloned.1.call-start = ((), (), s32[]{:S(2)}) async-start(), calls=%async_computation.1 | async-start | bytes 7962624 | tf_op jit(solution)/shard_map/all_gather | solution.py:704
  12.9 272.7 %all-gather.5.cloned.1.call-start = ((), (), s32[]{:S(2)}) async-start(), calls=%async_computation.2 | async-start | bytes 53084160 | tf_op jit(solution)/shard_map/all_gather | solution.py:767
  15.1 39.9 %collective-permute-start = (bf16[528,1536]{1,0:T(8,128)(2,1)S(1)}, bf16[528,1536]{1,0:T(8,128)(2,1)S(1)}, u32[]{:S(2)}, u32[]{:S(2)}) collective-permute-start(bf16[528,1536]{1,0:T(8,128)(2,1)S(1)} %pad_maximum_fusion.3), channel_id=1, source_target_pairs={{0,1},{1,2},{2,3},{4,5},{5,6},{6,7},{8,9},{9,10},{10,11},{12,13},{... | collective-permute-start | bytes 4866056 | tf_op jit(solution)/shard_map/ppermute | solution.py:67
  20.4 38.9 %collective-permute-start.1 = (bf16[528,1536]{1,0:T(8,128)(2,1)S(1)}, bf16[528,1536]{1,0:T(8,128)(2,1)}, u32[]{:S(2)}, u32[]{:S(2)}) collective-permute-start(bf16[528,1536]{1,0:T(8,128)(2,1)S(1)} %pad_maximum_fusion.3), channel_id=1, source_target_pairs={{1,0},{2,1},{3,2},{5,4},{6,5},{7,6},{9,8},{10,9},{11,10},{13,12},{... | collective-permute-start | bytes 4866056 | tf_op jit(solution)/shard_map/ppermute | solution.py:68
  66.1 1165.2 %reduce-scatter.2.cloned.1.call-start = ((), (), s32[]{:S(2)}) async-start(), calls=%async_computation.3 | async-start | bytes 53084160 | tf_op jit(solution)/shard_map/reduce_scatter | solution.py:874
  84.4 38.2 %collective-permute-start.3 = (bf16[528,1536]{1,0:T(8,128)(2,1)}, bf16[528,1536]{1,0:T(8,128)(2,1)}, u32[]{:S(2)}, u32[]{:S(2)}) collective-permute-start(bf16[528,1536]{1,0:T(8,128)(2,1)} %collective-permute-done.1), channel_id=1, source_target_pairs={{1,0},{2,1},{5,4},{6,5},{9,8},{10,9},{13,12},{14,13},{17,16},{18,1... | collective-permute-start | bytes 4866056 | tf_op jit(solution)/shard_map/ppermute | solution.py:68
  85.7 36.9 %collective-permute-start.2 = (bf16[528,1536]{1,0:T(8,128)(2,1)}, bf16[528,1536]{1,0:T(8,128)(2,1)}, u32[]{:S(2)}, u32[]{:S(2)}) collective-permute-start(bf16[528,1536]{1,0:T(8,128)(2,1)} %copy-done.65), channel_id=1, source_target_pairs={{1,2},{2,3},{5,6},{6,7},{9,10},{10,11},{13,14},{14,15},{17,18},{18... | collective-permute-start | bytes 4866056 | tf_op jit(solution)/shard_map/ppermute | solution.py:67
  124.4 38.4 %collective-permute-start.5 = (bf16[528,1536]{1,0:T(8,128)(2,1)}, bf16[528,1536]{1,0:T(8,128)(2,1)}, u32[]{:S(2)}, u32[]{:S(2)}) collective-permute-start(bf16[528,1536]{1,0:T(8,128)(2,1)} %collective-permute-done.3), channel_id=1, source_target_pairs={{1,0},{5,4},{9,8},{13,12},{17,16},{21,20},{25,24},{29,28}} | collective-permute-start | bytes 4866056 | tf_op jit(solution)/shard_map/ppermute | solution.py:68
  267.9 46.3 %collective-permute-start.12 = (bf16[512,1536]{1,0:T(8,128)(2,1)}, bf16[512,1536]{1,0:T(8,128)(2,1)}, u32[]{:S(2)}, u32[]{:S(2)}) collective-permute-start(bf16[512,1536]{1,0:T(8,128)(2,1)} %multiply_convert_fusion.1.tok_ref), channel_id=1, source_target_pairs={{0,1},{1,2},{2,3},{4,5},{5,6},{6,7},{8,9},{9,10},{10,11},{12,13},{... | collective-permute-start | bytes 4718600 | tf_op jit(solution)/shard_map/ppermute | solution.py:67
  270.5 43.7 %collective-permute-start.13 = (bf16[512,1536]{1,0:T(8,128)(2,1)}, bf16[512,1536]{1,0:T(8,128)(2,1)}, u32[]{:S(2)}, u32[]{:S(2)}) collective-permute-start(bf16[512,1536]{1,0:T(8,128)(2,1)} %multiply_convert_fusion.1.tok_ref), channel_id=1, source_target_pairs={{1,0},{2,1},{3,2},{5,4},{6,5},{7,6},{9,8},{10,9},{11,10},{13,12},{... | collective-permute-start | bytes 4718600 | tf_op jit(solution)/shard_map/ppermute | solution.py:68
  314.2 32.5 %collective-permute-start.14 = (bf16[512,1536]{1,0:T(8,128)(2,1)}, bf16[512,1536]{1,0:T(8,128)(2,1)S(1)}, u32[]{:S(2)}, u32[]{:S(2)}) collective-permute-start(bf16[512,1536]{1,0:T(8,128)(2,1)} %collective-permute-done.12), channel_id=1, source_target_pairs={{1,2},{2,3},{5,6},{6,7},{9,10},{10,11},{13,14},{14,15},{17,18},{18... | collective-permute-start | bytes 4718600 | tf_op jit(solution)/shard_map/ppermute | solution.py:67
  315.0 40.9 %collective-permute-start.15 = (bf16[512,1536]{1,0:T(8,128)(2,1)}, bf16[512,1536]{1,0:T(8,128)(2,1)S(1)}, u32[]{:S(2)}, u32[]{:S(2)}) collective-permute-start(bf16[512,1536]{1,0:T(8,128)(2,1)} %collective-permute-done.13), channel_id=1, source_target_pairs={{1,0},{2,1},{5,4},{6,5},{9,8},{10,9},{13,12},{14,13},{17,16},{18,1... | collective-permute-start | bytes 4718600 | tf_op jit(solution)/shard_map/ppermute | solution.py:68
  356.7 37.6 %collective-permute-start.17 = (bf16[512,1536]{1,0:T(8,128)(2,1)S(1)}, bf16[512,1536]{1,0:T(8,128)(2,1)S(1)}, u32[]{:S(2)}, u32[]{:S(2)}) collective-permute-start(bf16[512,1536]{1,0:T(8,128)(2,1)S(1)} %collective-permute-done.15), channel_id=1, source_target_pairs={{1,0},{5,4},{9,8},{13,12},{17,16},{21,20},{25,24},{29,28}} | collective-permute-start | bytes 4718600 | tf_op jit(solution)/shard_map/ppermute | solution.py:68
  425.5 34.0 %collective-permute-start.18 = (bf16[512,1536]{1,0:T(8,128)(2,1)S(1)}, bf16[512,1536]{1,0:T(8,128)(2,1)S(1)}, u32[]{:S(2)}, u32[]{:S(2)}) collective-permute-start(bf16[512,1536]{1,0:T(8,128)(2,1)S(1)} %get-tuple-element.221), channel_id=1, source_target_pairs={{0,1},{4,5},{8,9},{12,13},{16,17},{20,21},{24,25},{28,29}} | collective-permute-start | bytes 4718600 | tf_op jit(solution)/shard_map/ppermute | solution.py:134
  427.1 32.4 %collective-permute-start.19 = (bf16[512,1536]{1,0:T(8,128)(2,1)S(1)}, bf16[512,1536]{1,0:T(8,128)(2,1)S(1)}, u32[]{:S(2)}, u32[]{:S(2)}) collective-permute-start(bf16[512,1536]{1,0:T(8,128)(2,1)S(1)} %get-tuple-element.222), channel_id=1, source_target_pairs={{3,2},{7,6},{11,10},{15,14},{19,18},{23,22},{27,26},{31,30}} | collective-permute-start | bytes 4718600 | tf_op jit(solution)/shard_map/ppermute | solution.py:135
  460.5 35.9 %collective-permute-start.20 = (bf16[512,1536]{1,0:T(8,128)(2,1)S(1)}, bf16[512,1536]{1,0:T(8,128)(2,1)S(1)}, u32[]{:S(2)}, u32[]{:S(2)}) collective-permute-start(bf16[512,1536]{1,0:T(8,128)(2,1)S(1)} %get-tuple-element.225), channel_id=1, source_target_pairs={{0,1},{1,2},{4,5},{5,6},{8,9},{9,10},{12,13},{13,14},{16,17},{17,1... | collective-permute-start | bytes 4718600 | tf_op jit(solution)/shard_map/ppermute | solution.py:134
  499.0 37.2 %collective-permute-start.22 = (bf16[512,1536]{1,0:T(8,128)(2,1)}, bf16[512,1536]{1,0:T(8,128)(2,1)}, u32[]{:S(2)}, u32[]{:S(2)}) collective-permute-start(bf16[512,1536]{1,0:T(8,128)(2,1)} %get-tuple-element.229), channel_id=1, source_target_pairs={{0,1},{1,2},{2,3},{4,5},{5,6},{6,7},{8,9},{9,10},{10,11},{12,13},{... | collective-permute-start | bytes 4718600 | tf_op jit(solution)/shard_map/ppermute | solution.py:134
  506.5 35.0 %collective-permute-start.23 = (bf16[512,1536]{1,0:T(8,128)(2,1)}, bf16[512,1536]{1,0:T(8,128)(2,1)}, u32[]{:S(2)}, u32[]{:S(2)}) collective-permute-start(bf16[512,1536]{1,0:T(8,128)(2,1)} %get-tuple-element.230), channel_id=1, source_target_pairs={{1,0},{2,1},{3,2},{5,4},{6,5},{7,6},{9,8},{10,9},{11,10},{13,12},{... | collective-permute-start | bytes 4718600 | tf_op jit(solution)/shard_map/ppermute | solution.py:135
  546.8 49.8 %collective-permute-start.27 = (bf16[512,1536]{1,0:T(8,128)(2,1)S(1)}, bf16[512,1536]{1,0:T(8,128)(2,1)}, u32[]{:S(2)}, u32[]{:S(2)}) collective-permute-start(bf16[512,1536]{1,0:T(8,128)(2,1)S(1)} %get-tuple-element.410.tok_ref), channel_id=1, source_target_pairs={{0,1},{1,2},{2,3},{4,5},{5,6},{6,7},{8,9},{9,10},{10,11},{12,13},{... | collective-permute-start | bytes 4718600 | tf_op jit(solution)/shard_map/ppermute | solution.py:67
  549.4 47.2 %collective-permute-start.28 = (bf16[512,1536]{1,0:T(8,128)(2,1)S(1)}, bf16[512,1536]{1,0:T(8,128)(2,1)S(1)}, u32[]{:S(2)}, u32[]{:S(2)}) collective-permute-start(bf16[512,1536]{1,0:T(8,128)(2,1)S(1)} %get-tuple-element.410.tok_ref), channel_id=1, source_target_pairs={{1,0},{2,1},{3,2},{5,4},{6,5},{7,6},{9,8},{10,9},{11,10},{13,12},{... | collective-permute-start | bytes 4718600 | tf_op jit(solution)/shard_map/ppermute | solution.py:68
  555.7 40.8 %collective-permute-start.29 = (f32[1,512]{1,0:T(1,128)S(1)}, f32[1,512]{1,0:T(1,128)S(1)}, u32[]{:S(2)}, u32[]{:S(2)}) collective-permute-start(f32[1,512]{1,0:T(1,128)S(1)} %bitcast.278), channel_id=1, source_target_pairs={{0,1},{1,2},{2,3},{4,5},{5,6},{6,7},{8,9},{9,10},{10,11},{12,13},{... | collective-permute-start | bytes 6152 | tf_op jit(solution)/shard_map/ppermute | solution.py:67
  560.3 36.3 %collective-permute-start.30 = (f32[1,512]{1,0:T(1,128)S(1)}, f32[1,512]{1,0:T(1,128)S(1)}, u32[]{:S(2)}, u32[]{:S(2)}) collective-permute-start(f32[1,512]{1,0:T(1,128)S(1)} %bitcast.279), channel_id=1, source_target_pairs={{1,0},{2,1},{3,2},{5,4},{6,5},{7,6},{9,8},{10,9},{11,10},{13,12},{... | collective-permute-start | bytes 6152 | tf_op jit(solution)/shard_map/ppermute | solution.py:68
  561.6 35.0 %collective-permute-start.31 = (f32[1,1]{1,0:T(1,128)}, f32[1,1]{1,0:T(1,128)}, u32[]{:S(2)}, u32[]{:S(2)}) collective-permute-start(f32[1,1]{1,0:T(1,128)} %bitcast.76), channel_id=1, source_target_pairs={{0,1},{1,0},{2,3},{3,2},{4,5},{5,4},{6,7},{7,6},{8,9},{9,8},{10,11... | collective-permute-start | bytes 20 | tf_op jit(solution)/shard_map/ppermute | solution.py:166
  596.6 49.2 %collective-permute-start.32 = (bf16[512,1536]{1,0:T(8,128)(2,1)}, bf16[512,1536]{1,0:T(8,128)(2,1)S(1)}, u32[]{:S(2)}, u32[]{:S(2)}) collective-permute-start(bf16[512,1536]{1,0:T(8,128)(2,1)} %collective-permute-done.27), channel_id=1, source_target_pairs={{1,2},{2,3},{5,6},{6,7},{9,10},{10,11},{13,14},{14,15},{17,18},{18... | collective-permute-start | bytes 4718600 | tf_op jit(solution)/shard_map/ppermute | solution.py:67
  597.5 48.3 %collective-permute-start.33 = (bf16[512,1536]{1,0:T(8,128)(2,1)S(1)}, bf16[512,1536]{1,0:T(8,128)(2,1)S(1)}, u32[]{:S(2)}, u32[]{:S(2)}) collective-permute-start(bf16[512,1536]{1,0:T(8,128)(2,1)S(1)} %collective-permute-done.28), channel_id=1, source_target_pairs={{1,0},{2,1},{5,4},{6,5},{9,8},{10,9},{13,12},{14,13},{17,16},{18,1... | collective-permute-start | bytes 4718600 | tf_op jit(solution)/shard_map/ppermute | solution.py:68
  598.8 47.0 %collective-permute-start.34 = (f32[1,512]{1,0:T(1,128)S(1)}, f32[1,512]{1,0:T(1,128)S(1)}, u32[]{:S(2)}, u32[]{:S(2)}) collective-permute-start(f32[1,512]{1,0:T(1,128)S(1)} %collective-permute-done.29), channel_id=1, source_target_pairs={{1,2},{2,3},{5,6},{6,7},{9,10},{10,11},{13,14},{14,15},{17,18},{18... | collective-permute-start | bytes 6152 | tf_op jit(solution)/shard_map/ppermute | solution.py:67
  599.5 46.4 %collective-permute-start.35 = (f32[1,512]{1,0:T(1,128)S(1)}, f32[1,512]{1,0:T(1,128)S(1)}, u32[]{:S(2)}, u32[]{:S(2)}) collective-permute-start(f32[1,512]{1,0:T(1,128)S(1)} %collective-permute-done.30), channel_id=1, source_target_pairs={{1,0},{2,1},{5,4},{6,5},{9,8},{10,9},{13,12},{14,13},{17,16},{18,1... | collective-permute-start | bytes 6152 | tf_op jit(solution)/shard_map/ppermute | solution.py:68
  603.5 42.3 %collective-permute-start.36 = (f32[1,1]{1,0:T(1,128)}, f32[1,1]{1,0:T(1,128)}, u32[]{:S(2)}, u32[]{:S(2)}) collective-permute-start(f32[1,1]{1,0:T(1,128)} %add.547), channel_id=1, source_target_pairs={{0,2},{1,3},{2,0},{3,1},{4,6},{5,7},{6,4},{7,5},{8,10},{9,11},{10,... | collective-permute-start | bytes 20 | tf_op jit(solution)/shard_map/ppermute | solution.py:166
  645.9 44.6 %collective-permute-start.37 = (bf16[512,1536]{1,0:T(8,128)(2,1)S(1)}, bf16[512,1536]{1,0:T(8,128)(2,1)S(1)}, u32[]{:S(2)}, u32[]{:S(2)}) collective-permute-start(bf16[512,1536]{1,0:T(8,128)(2,1)S(1)} %collective-permute-done.32), channel_id=1, source_target_pairs={{2,3},{6,7},{10,11},{14,15},{18,19},{22,23},{26,27},{30,31}} | collective-permute-start | bytes 4718600 | tf_op jit(solution)/shard_map/ppermute | solution.py:67
  646.7 43.8 %collective-permute-start.38 = (bf16[512,1536]{1,0:T(8,128)(2,1)S(1)}, bf16[512,1536]{1,0:T(8,128)(2,1)S(1)}, u32[]{:S(2)}, u32[]{:S(2)}) collective-permute-start(bf16[512,1536]{1,0:T(8,128)(2,1)S(1)} %collective-permute-done.33), channel_id=1, source_target_pairs={{1,0},{5,4},{9,8},{13,12},{17,16},{21,20},{25,24},{29,28}} | collective-permute-start | bytes 4718600 | tf_op jit(solution)/shard_map/ppermute | solution.py:68
  648.0 39.1 %collective-permute-start.39 = (f32[1,512]{1,0:T(1,128)S(1)}, f32[1,512]{1,0:T(1,128)S(1)}, u32[]{:S(2)}, u32[]{:S(2)}) collective-permute-start(f32[1,512]{1,0:T(1,128)S(1)} %collective-permute-done.34), channel_id=1, source_target_pairs={{2,3},{6,7},{10,11},{14,15},{18,19},{22,23},{26,27},{30,31}} | collective-permute-start | bytes 6152 | tf_op jit(solution)/shard_map/ppermute | solution.py:67
  648.6 41.9 %collective-permute-start.40 = (f32[1,512]{1,0:T(1,128)S(1)}, f32[1,512]{1,0:T(1,128)S(1)}, u32[]{:S(2)}, u32[]{:S(2)}) collective-permute-start(f32[1,512]{1,0:T(1,128)S(1)} %collective-permute-done.35), channel_id=1, source_target_pairs={{1,0},{5,4},{9,8},{13,12},{17,16},{21,20},{25,24},{29,28}} | collective-permute-start | bytes 6152 | tf_op jit(solution)/shard_map/ppermute | solution.py:68
  653.9 33.1 %collective-permute-start.41 = (f32[1,1]{1,0:T(1,128)}, f32[1,1]{1,0:T(1,128)}, u32[]{:S(2)}, u32[]{:S(2)}) collective-permute-start(f32[1,1]{1,0:T(1,128)} %add.548), channel_id=1, source_target_pairs={{0,4},{4,0},{8,12},{12,8},{16,20},{20,16},{24,28},{28,24},{1,5},{5... | collective-permute-start | bytes 20 | tf_op jit(solution)/shard_map/ppermute | solution.py:166
  729.9 47.3 %collective-permute-start.42 = (bf16[512,1536]{1,0:T(8,128)(2,1)}, bf16[512,1536]{1,0:T(8,128)(2,1)S(1)}, u32[]{:S(2)}, u32[]{:S(2)}) collective-permute-start(bf16[512,1536]{1,0:T(8,128)(2,1)} %get-tuple-element.271), channel_id=1, source_target_pairs={{0,1},{4,5},{8,9},{12,13},{16,17},{20,21},{24,25},{28,29}} | collective-permute-start | bytes 4718600 | tf_op jit(solution)/shard_map/ppermute | solution.py:134
  742.7 34.5 %collective-permute-start.43 = (bf16[512,1536]{1,0:T(8,128)(2,1)S(1)}, bf16[512,1536]{1,0:T(8,128)(2,1)S(1)}, u32[]{:S(2)}, u32[]{:S(2)}) collective-permute-start(bf16[512,1536]{1,0:T(8,128)(2,1)S(1)} %get-tuple-element.272), channel_id=1, source_target_pairs={{3,2},{7,6},{11,10},{15,14},{19,18},{23,22},{27,26},{31,30}} | collective-permute-start | bytes 4718600 | tf_op jit(solution)/shard_map/ppermute | solution.py:135
  781.6 38.2 %collective-permute-start.45 = (bf16[512,1536]{1,0:T(8,128)(2,1)}, bf16[512,1536]{1,0:T(8,128)(2,1)}, u32[]{:S(2)}, u32[]{:S(2)}) collective-permute-start(bf16[512,1536]{1,0:T(8,128)(2,1)} %get-tuple-element.280), channel_id=1, source_target_pairs={{0,1},{1,2},{4,5},{5,6},{8,9},{9,10},{12,13},{13,14},{16,17},{17,1... | collective-permute-start | bytes 4718600 | tf_op jit(solution)/shard_map/ppermute | solution.py:134
  787.1 32.7 %collective-permute-start.46 = (bf16[512,1536]{1,0:T(8,128)(2,1)}, bf16[512,1536]{1,0:T(8,128)(2,1)}, u32[]{:S(2)}, u32[]{:S(2)}) collective-permute-start(bf16[512,1536]{1,0:T(8,128)(2,1)} %get-tuple-element.281), channel_id=1, source_target_pairs={{2,1},{3,2},{6,5},{7,6},{10,9},{11,10},{14,13},{15,14},{18,17},{19... | collective-permute-start | bytes 4718600 | tf_op jit(solution)/shard_map/ppermute | solution.py:135
  825.2 42.8 %collective-permute-start.48 = (bf16[512,1536]{1,0:T(8,128)(2,1)}, bf16[512,1536]{1,0:T(8,128)(2,1)}, u32[]{:S(2)}, u32[]{:S(2)}) collective-permute-start(bf16[512,1536]{1,0:T(8,128)(2,1)} %get-tuple-element.287), channel_id=1, source_target_pairs={{0,1},{1,2},{2,3},{4,5},{5,6},{6,7},{8,9},{9,10},{10,11},{12,13},{... | collective-permute-start | bytes 4718600 | tf_op jit(solution)/shard_map/ppermute | solution.py:134
  836.6 36.7 %collective-permute-start.49 = (bf16[512,1536]{1,0:T(8,128)(2,1)}, bf16[512,1536]{1,0:T(8,128)(2,1)}, u32[]{:S(2)}, u32[]{:S(2)}) collective-permute-start(bf16[512,1536]{1,0:T(8,128)(2,1)} %get-tuple-element.288), channel_id=1, source_target_pairs={{1,0},{2,1},{3,2},{5,4},{6,5},{7,6},{9,8},{10,9},{11,10},{13,12},{... | collective-permute-start | bytes 4718600 | tf_op jit(solution)/shard_map/ppermute | solution.py:135
  920.6 37.3 %collective-permute-start.56 = (bf16[384,512]{1,0:T(8,128)(2,1)S(1)}, bf16[384,512]{1,0:T(8,128)(2,1)S(1)}, u32[]{:S(2)}, u32[]{:S(2)}) collective-permute-start(bf16[384,512]{1,0:T(8,128)(2,1)S(1)} %get-tuple-element.447), channel_id=1, source_target_pairs={{2,0},{3,1},{6,4},{7,5},{10,8},{11,9},{14,12},{15,13},{18,16},{19,... | collective-permute-start | bytes 1179656 | tf_op jit(solution)/shard_map/ppermute | solution.py:161
  921.9 36.0 %collective-permute-start.57 = (bf16[384,512]{1,0:T(8,128)(2,1)S(1)}, bf16[384,512]{1,0:T(8,128)(2,1)S(1)}, u32[]{:S(2)}, u32[]{:S(2)}) collective-permute-start(bf16[384,512]{1,0:T(8,128)(2,1)S(1)} %get-tuple-element.446), channel_id=1, source_target_pairs={{3,0},{7,4},{11,8},{15,12},{19,16},{23,20},{27,24},{31,28}} | collective-permute-start | bytes 1179656 | tf_op jit(solution)/shard_map/ppermute | solution.py:161
  957.9 59.2 %collective-permute-start.58 = (bf16[2,192,768]{2,1,0:T(8,128)(2,1)S(1)}, bf16[2,192,768]{2,1,0:T(8,128)(2,1)S(1)}, u32[]{:S(2)}, u32[]{:S(2)}) collective-permute-start(bf16[2,192,768]{2,1,0:T(8,128)(2,1)S(1)} %add_convert_fusion.3), channel_id=1, source_target_pairs={{0,8},{4,12},{8,0},{12,4},{16,24},{20,28},{24,16},{28,20},{1,9},{5... | collective-permute-start | bytes 1769480 | tf_op jit(solution)/shard_map/ppermute | solution.py:166
  959.4 57.7 %collective-permute-start.59 = (bf16[2,192,768]{2,1,0:T(8,128)(2,1)S(1)}, bf16[2,192,768]{2,1,0:T(8,128)(2,1)S(1)}, u32[]{:S(2)}, u32[]{:S(2)}) collective-permute-start(bf16[2,192,768]{2,1,0:T(8,128)(2,1)S(1)} %add_convert_fusion.2), channel_id=1, source_target_pairs={{0,16},{4,20},{8,24},{12,28},{16,0},{20,4},{24,8},{28,12},{1,17},{... | collective-permute-start | bytes 1769480 | tf_op jit(solution)/shard_map/ppermute | solution.py:166
  1047.6 34.8 %collective-permute-start.62 = (bf16[560,1536]{1,0:T(8,128)(2,1)}, bf16[560,1536]{1,0:T(8,128)(2,1)}, u32[]{:S(2)}, u32[]{:S(2)}) collective-permute-start(bf16[560,1536]{1,0:T(8,128)(2,1)} %get-tuple-element.323), channel_id=1, source_target_pairs={{0,1},{4,5},{8,9},{12,13},{16,17},{20,21},{24,25},{28,29}} | collective-permute-start | bytes 5160968 | tf_op jit(solution)/shard_map/ppermute | solution.py:134
  1050.2 32.2 %collective-permute-start.63 = (bf16[560,1536]{1,0:T(8,128)(2,1)}, bf16[560,1536]{1,0:T(8,128)(2,1)}, u32[]{:S(2)}, u32[]{:S(2)}) collective-permute-start(bf16[560,1536]{1,0:T(8,128)(2,1)} %get-tuple-element.324), channel_id=1, source_target_pairs={{3,2},{7,6},{11,10},{15,14},{19,18},{23,22},{27,26},{31,30}} | collective-permute-start | bytes 5160968 | tf_op jit(solution)/shard_map/ppermute | solution.py:135
  1086.3 36.6 %collective-permute-start.65 = (bf16[560,1536]{1,0:T(8,128)(2,1)S(1)}, bf16[560,1536]{1,0:T(8,128)(2,1)S(1)}, u32[]{:S(2)}, u32[]{:S(2)}) collective-permute-start(bf16[560,1536]{1,0:T(8,128)(2,1)S(1)} %get-tuple-element.328), channel_id=1, source_target_pairs={{0,1},{1,2},{4,5},{5,6},{8,9},{9,10},{12,13},{13,14},{16,17},{17,1... | collective-permute-start | bytes 5160968 | tf_op jit(solution)/shard_map/ppermute | solution.py:134
  1125.6 39.9 %collective-permute-start.68 = (bf16[560,1536]{1,0:T(8,128)(2,1)}, bf16[560,1536]{1,0:T(8,128)(2,1)S(1)}, u32[]{:S(2)}, u32[]{:S(2)}) collective-permute-start(bf16[560,1536]{1,0:T(8,128)(2,1)} %get-tuple-element.333), channel_id=1, source_target_pairs={{0,1},{1,2},{2,3},{4,5},{5,6},{6,7},{8,9},{9,10},{10,11},{12,13},{... | collective-permute-start | bytes 5160968 | tf_op jit(solution)/shard_map/ppermute | solution.py:134
  1134.1 35.6 %collective-permute-start.69 = (bf16[560,1536]{1,0:T(8,128)(2,1)}, bf16[560,1536]{1,0:T(8,128)(2,1)}, u32[]{:S(2)}, u32[]{:S(2)}) collective-permute-start(bf16[560,1536]{1,0:T(8,128)(2,1)} %get-tuple-element.334), channel_id=1, source_target_pairs={{1,0},{2,1},{3,2},{5,4},{6,5},{7,6},{9,8},{10,9},{11,10},{13,12},{... | collective-permute-start | bytes 5160968 | tf_op jit(solution)/shard_map/ppermute | solution.py:135
  (152 other events, 2737.0 us)
Sparse Core Ops, SparseCore 0:
  13.0 51.5 all-gather.2
  66.5 219.0 all-gather.4
  820.0 293.2 reduce-scatter.1

commit v9 on v8

--- a/solution.py
+++ b/solution.py
@@ -136,9 +136,51 @@
     )
 
 
-def line_end(parts, right, left):
-    own = at_place(parts, lax.axis_index("seq")).astype(full)
-    return own + (right.astype(full) + left.astype(full))
+class LineGather:
+    def __init__(self, halves):
+        self.rights, self.lefts = [[half] for half in halves], [[half] for half in halves]
+
+    def go(self, h):
+        step = len(self.rights[h])
+        right, left = line_move(self.rights[h][-1], self.lefts[h][-1], step)
+        self.rights[h].append(right)
+        self.lefts[h].append(left)
+
+    def land(self, h, other):
+        spot = len(self.rights[h]) - 1
+        moved = [(self.rights[part][spot], self.lefts[part][spot]) for part in range(h + 1)]
+        moved, other = tie(moved, other)
+        for part, (right, left) in enumerate(moved):
+            self.rights[part][spot], self.lefts[part][spot] = right, left
+        return other
+
+    def block(self, turn):
+        return [arrived(self.rights[h], self.lefts[h], turn) for h in (0, 1)]
+
+
+def line_scatter(parts, work):
+    n = lax.axis_size("seq")
+    me = lax.axis_index("seq")
+    middle = parts.shape[1] // 32 * 16
+    halves = [parts[:, :middle], parts[:, middle:]]
+    flying = [(None, None), (None, None)]
+    before, given = (), []
+    for k in range(n - 1, 0, -1):
+        for h in (0, 1):
+            if k < n - 1 and h:
+                flying[h], before = tie(flying[h], before)
+            elif k < n - 1:
+                flying[h], given = tie(flying[h], given)
+            before = line_send(halves[h], k, *flying[h])
+            flying[h] = line_pass(*before, k)
+        if n - 1 - k < len(work):
+            given = work[n - 1 - k](before, given)
+    sums = []
+    flying[0], given = tie(flying[0], given)
+    for h in (0, 1):
+        own = at_place(halves[h], me).astype(full)
+        sums.append(own + (flying[h][0].astype(full) + flying[h][1].astype(full)))
+    return jnp.concatenate(sums), given
 
 
 def by_place(blocks):
@@ -414,8 +456,13 @@
             )
 
 
+def pick_rows(pick, tok_ref, more_ref):
+    middle = tok_ref.shape[0]
+    return (nn(pick[:, :middle], tok_ref[...]) + nn(pick[:, middle:], more_ref[:middle, :])).astype(low)
+
+
 def experts_kernel(
-    few, at_ref, tok_ref, slot_ref, member_ref, router_ref, wgu_ref, wd_ref, *refs
+    few, at_ref, tok_ref, more_ref, slot_ref, member_ref, router_ref, wgu_ref, wd_ref, *refs
 ):
     part_ref, x_ref, gu_ref, gates_ref, acc, gates_all, down = refs[-7:]
     e, experts = pl.program_id(0), pl.num_programs(0)
@@ -424,7 +471,8 @@
     @pl.when(e == 0)
     def _():
         member = member_ref[...] > 0
-        chosen = jnp.where(member, nt(router_ref[...], tok_ref[...]), masked_score)
+        logits = [nt(router_ref[...], ref[...]) for ref in (tok_ref, more_ref)]
+        chosen = jnp.where(member, jnp.concatenate(logits, axis=1), masked_score)
         chosen = jnp.exp(chosen - jnp.max(chosen, axis=0, keepdims=True))
         chosen = jnp.where(member, chosen, 0.0)
         gates_all[...] = chosen / jnp.sum(chosen, axis=0, keepdims=True)
@@ -434,7 +482,7 @@
     gates_ref[pl.ds(e, 1), :] = gate_row
     place = lax.broadcasted_iota(jnp.int32, (slots, 1), 0)
     here = place == own_row(slot_ref, e)
-    x = nn(jnp.where(here, 1.0, 0.0).astype(low), tok_ref[...]).astype(low)
+    x = pick_rows(jnp.where(here, 1.0, 0.0).astype(low), tok_ref, more_ref)
     x_ref[0, 0] = x
     gu = nn(x, wgu_ref[0])
     gu_ref[0, 0] = gu.astype(low)
@@ -451,7 +499,7 @@
 
 
 def back_kernel(
-    few, at_ref, tok_ref, slot_ref, gates_ref, mix_ref, router_ref, gu_ref, wgu_ref, wd_ref, *refs
+    few, at_ref, tok_ref, more_ref, slot_ref, gates_ref, mix_ref, router_ref, gu_ref, wgu_ref, wd_ref, *refs
 ):
     part_ref, d_ref, dgu_ref, act_ref, dlog_ref, acc, dlog_all, down = refs[-8:]
     e, experts = pl.program_id(0), pl.num_programs(0)
@@ -467,7 +515,7 @@
     pick = jnp.where(here, 1.0, 0.0).astype(low)
     gate_row = own_row(gates_ref, e)
     gate = jnp.sum(jnp.where(here, gate_row, 0.0), axis=1, keepdims=True)
-    d = nn(pick, tok_ref[...]).astype(low)
+    d = pick_rows(pick, tok_ref, more_ref)
     d_ref[0, 0] = d
     join_down(few, wd_ref, down)
     d_act = nt(d, down[...])
@@ -539,15 +587,15 @@
 def experts_forward(turn, devs, at, tokens, slot_of, member, router, weights, few, slots, buffers):
     experts, width, columns = weights.shape
     hidden = columns // 3
-    count = tokens.shape[0]
+    count = 2 * tokens[0].shape[0]
     total_experts = member.shape[0]
     return shard_call(
         functools.partial(experts_kernel, few),
         "experts_forward",
         at,
-        [tokens, slot_of, member, router, weights, weights],
+        [*tokens, slot_of, member, router, weights, weights],
         [
-            same(count, width),
+            *(same(*half.shape) for half in tokens),
             same(experts, count),
             same(total_experts, count),
             same(total_experts, width),
@@ -580,16 +628,16 @@
 ):
     experts, width, columns = weights.shape
     hidden = columns // 3
-    count = d_tokens.shape[0]
+    count = 2 * d_tokens[0].shape[0]
     slots = gu.shape[2]
     lines = router.shape[0]
     return shard_call(
         functools.partial(back_kernel, few),
         "experts_backward",
         at,
-        [d_tokens, slot_of, gates, mix_dot, router, gu, weights, weights],
+        [*d_tokens, slot_of, gates, mix_dot, router, gu, weights, weights],
         [
-            same(count, width),
+            *(same(*half.shape) for half in d_tokens),
             same(experts, count),
             same(experts, count),
             same(1, count),
@@ -626,6 +674,39 @@
     for bit in reversed(bits):
         masks = masks + [mask ^ bit for mask in masks]
     return masks
+
+
+def out_kernel(bits_a, bits_b, me_ref, rows_ref, d_ref, *refs):
+    outs, acc = refs[:4], refs[4]
+    half = outs[0].shape[2]
+    for part, bits in enumerate((bits_a, bits_b)):
+        keep, send = outs[2 * part], outs[2 * part + 1]
+        rows = keep.shape[1]
+        acc[...] = nn(rows_ref[...], d_ref[:, part * half : (part + 1) * half])
+        for place, mask in enumerate(halving_masks(bits)):
+            out = keep if place < keep.shape[0] else send
+            start = pl.multiple_of((me_ref[0] ^ mask) * rows, rows)
+            out[place % keep.shape[0]] = acc[pl.ds(start, rows), :].astype(low)
+
+
+def out_grads(me, rows, d_proj, bits_a, bits_b):
+    (height, count), width = rows.shape, d_proj.shape[1]
+    devs = 2 ** len(bits_a)
+    shape = (devs // 2, height // devs, width // 2)
+    outs = pl.pallas_call(
+        functools.partial(out_kernel, bits_a, bits_b),
+        grid_spec=pltpu.PrefetchScalarGridSpec(
+            num_scalar_prefetch=1,
+            grid=(1,),
+            in_specs=[same(height, count), same(count, width)],
+            out_specs=[pl.BlockSpec(shape, lambda e, me: (0, 0, 0))] * 4,
+            scratch_shapes=[pltpu.VMEM((height, width // 2), full)],
+        ),
+        out_shape=[jax.ShapeDtypeStruct(shape, low)] * 4,
+        compiler_params=vmem(48),
+        name="out_grads",
+    )(me, rows, d_proj)
+    return (outs[0], outs[1]), (outs[2], outs[3])
 
 
 def grads_kernel(few, x_ref, dgu_ref, act_ref, d_ref, *refs):
@@ -718,18 +799,29 @@
     routes_low = jnp.pad(
         routes_low.astype(low), ((0, -routes_low.shape[0] % 16), (0, width - shard_len))
     )
-    block = jnp.concatenate([x_low, routes_low], axis=0)
+    middle = shard_len // 2
+    halves = (x_low[:middle], jnp.concatenate([x_low[middle:], routes_low], axis=0))
     positions = jnp.arange(seq_len, dtype=jnp.int32)
     cosine, sine_vals = rope_tables(positions.astype(full), HEAD_DIM)
     limit = block_limits(block_lengths[0], positions)[None]
-    rights, lefts = [block], [block]
     normed_one = jnp.zeros((seq_len, width), low)
     heads = jnp.zeros((n, kv_here, GROUP + 2, HEAD_DIM, shard_len), low)
     routes_all = []
-    expert_weights = (w_gate, w_up, w_down)
+    line = LineGather(halves)
+    signal = swap(x_low[:1, :128], "fsdp", order_a[0])
+    expert_weights, _ = tie((w_gate, w_up, w_down), signal)
     for turn in range(n):
-        if turn < n - 1:
-            right, left = line_move(rights[turn], lefts[turn], turn + 1)
+        if turn:
+            line.land(0, heads if turn > 1 else ())
+            if turn < n - 1:
+                line.go(0)
+            line.land(1, ())
+            if turn < n - 1:
+                line.go(1)
+        else:
+            line.go(0)
+            line.go(1)
+        block = jnp.concatenate(line.block(turn))
         start = order[turn] * shard_len
         normed = rms_norm(block[:shard_len].astype(full), full_g1).astype(low)
         projected = dot("td,dc->ct", normed, full_qkv)
@@ -750,14 +842,6 @@
         heads = lax.dynamic_update_index_in_dim(heads, turned, order[turn], 0)
         normed_one = lax.dynamic_update_slice_in_dim(normed_one, normed, start, 0)
         routes_all.append(block[shard_len : shard_len + top_count + 1, :shard_len])
-        if turn < n - 1:
-            if turn == 0:
-                right, left, expert_weights = tie(right, left, expert_weights)
-            else:
-                right, left, heads, normed_one = tie(right, left, heads, normed_one)
-            rights.append(right)
-            lefts.append(left)
-            block = arrived(rights, lefts, turn + 1)
 
     w_gate, w_up, w_down = expert_weights
     hidden_w = w_gate.shape[2]
@@ -793,28 +877,28 @@
     hidden = x_low.astype(full) + resid_mult * projected
     normed_two, norm_two_pull = jax.vjp(rms_norm, hidden, full_g2)
 
-    tokens = [normed_two.astype(low)]
-    rights, lefts = [tokens[0]], [tokens[0]]
-    buffers, gates = [], []
+    normed_low = normed_two.astype(low)
+    line = LineGather((normed_low[:middle], normed_low[middle:]))
+    buffers, gates, tokens = [], [], []
     for turn in range(n):
-        if turn < n - 1:
-            right, left = line_move(rights[turn], lefts[turn], turn + 1)
+        if turn:
+            line.land(0, gates[-1])
+            if turn < n - 1:
+                line.go(0)
+            line.land(1, ())
+            if turn < n - 1:
+                line.go(1)
+        else:
+            line.go(0)
+            line.go(1)
+        tokens.append(line.block(turn))
         *buffers, shard_gates = experts_forward(
             turn, n, jnp.stack([order[turn], me]), tokens[turn], slot_of[turn], member[turn],
             router, weights, w_down.shape[1], slots, buffers,
         )
-        if turn < n - 1:
-            right, left, shard_gates = tie(right, left, shard_gates)
-            rights.append(right)
-            lefts.append(left)
-            tokens.append(arrived(rights, lefts, turn + 1))
         gates.append(shard_gates)
     mix_parts, expert_in, gate_up = buffers
-    right = left = None
-    for k in range(n - 1, 0, -1):
-        moving = tie(*line_send(mix_parts, k, right, left))
-        right, left = tie(*line_pass(*moving, k))
-    mixture = line_end(mix_parts, right, left)
+    mixture, _ = line_scatter(mix_parts, ())
     output_f32 = hidden + resid_mult * mixture
     activations = output_f32.astype(low).reshape(1, shard_len, width)
     error_rows = output_f32 - teacher.astype(full).reshape(shard_len, width)
@@ -826,28 +910,30 @@
     d_mix = resid_mult * d_out
     d_tokens = d_mix.astype(low)
     mix_dot = jnp.sum(d_mix * mixture, axis=1)[None]
-    rights, lefts = [d_tokens], [d_tokens]
-    dot_rights, dot_lefts = [mix_dot], [mix_dot]
+    mix_high = mix_dot.astype(low)
+    mix_rows = jnp.concatenate([mix_high, (mix_dot - mix_high.astype(full)).astype(low)])
+    mix_rows = jnp.pad(mix_rows, ((0, 14), (0, width - shard_len)))
+    line = LineGather((d_tokens[:middle], jnp.concatenate([d_tokens[middle:], mix_rows])))
     buffers, d_logits = [], []
     for turn in range(n):
-        if turn < n - 1:
-            dot_right, dot_left = line_move(dot_rights[turn], dot_lefts[turn], turn + 1)
-            right, left = line_move(rights[turn], lefts[turn], turn + 1)
+        if turn:
+            line.land(0, d_logits[-1])
+            if turn < n - 1:
+                line.go(0)
+            squares = line.land(1, squares)
+            squares = loss_steps.send(squares)
+            if turn < n - 1:
+                line.go(1)
+        else:
+            line.go(0)
+            line.go(1)
+        d_block = line.block(turn)
+        mix_dot = d_block[1][middle : middle + 2, :shard_len].astype(full)
+        mix_dot = jnp.sum(mix_dot, axis=0, keepdims=True)
         *buffers, shard_logits = experts_backward(
-            turn, n, jnp.stack([order[turn], me]), d_tokens, slot_of[turn], gates[turn], mix_dot,
+            turn, n, jnp.stack([order[turn], me]), d_block, slot_of[turn], gates[turn], mix_dot,
             own_router, gate_up, weights, w_down.shape[1], buffers,
         )
-        if turn < n - 1:
-            right, left, dot_right, dot_left, shard_logits, squares = tie(
-                right, left, dot_right, dot_left, shard_logits, squares
-            )
-            squares = loss_steps.send(squares)
-            rights.append(right)
-            lefts.append(left)
-            dot_rights.append(dot_right)
-            dot_lefts.append(dot_left)
-            d_tokens = arrived(rights, lefts, turn + 1)
-            mix_dot = arrived(dot_rights, dot_lefts, turn + 1)
         d_logits.append(shard_logits)
     d_parts, d_rows, d_gate_up, act_low = buffers
     expert_in = expert_in.reshape(experts_here, slot_rows, width)
@@ -855,43 +941,43 @@
     d_gate_up = d_gate_up.reshape(experts_here, slot_rows, -1)
     act_low = act_low.reshape(experts_here, slot_rows, -1)
 
-    right = left = None
     cut = (experts_here + 1) // 2
-    grads = []
-    for k in range(n - 1, 0, -1):
-        moving = line_send(d_parts, k, right, left)
-        if k >= n - 2:
-            moving, d_rows = tie(moving, d_rows)
-            right, left = line_pass(*moving, k)
-            part = (0, cut) if k == n - 1 else (cut, experts_here)
-            grads = [
-                weight_grads(expert_in, d_gate_up, act_low, d_rows, w_down.shape[1], *part, grads)
-            ]
-            right, left, grads, squares = tie(right, left, grads, squares)
-        else:
-            right, left, squares = tie(*line_pass(*tie(*moving), k), squares)
-        squares = loss_steps.send(squares)
+
+    losses = [squares]
+
+    def some_grads(first, stop):
+        def make(before, grads):
+            inputs, _, loss = tie((expert_in, d_gate_up, act_low, d_rows), before, losses[-1])
+            losses.append(loss_steps.send(loss))
+            return [weight_grads(*inputs, w_down.shape[1], first, stop, grads)]
+
+        return make
+
+    d_normed_two, grads = line_scatter(
+        d_parts, (some_grads(0, cut), some_grads(cut, experts_here))
+    )
+    squares = losses[-1]
     expert_sum = lax.psum_scatter(grads[0], "fsdp", scatter_dimension=1, tiled=True)
-    d_normed_two = line_end(d_parts, right, left)
 
     d_hidden_norm, gain_two_part = norm_two_pull(d_normed_two)
     d_hidden = d_out + d_hidden_norm
     d_proj = (resid_mult * d_hidden).astype(low)
-    out_part = dot("kt,td->kd", attn_rows, d_proj).astype(low)
-    middle = width // 2
-    out_sums = [
-        rows_halving(out_part[:, :middle], order_a),
-        rows_halving(out_part[:, middle:], order_b),
-    ]
+    out_pairs = out_grads(mine.reshape(1), attn_rows, d_proj, order_a, order_b)
+    out_sums = [Halving(*pair, bits) for pair, bits in zip(out_pairs, (order_a, order_b))]
+    for each in out_sums:
+        each.go()
     d_attended = dot("kd,td->kt", full_out, d_proj).astype(low)
-    d_attended, _ = tie(d_attended, [each.send for each in out_sums])
+    (d_attended,) = land(out_sums, d_attended)
     moved = exchange(d_attended.reshape(n, heads_w, shard_len))
     for each in out_sums:
-        each.go()
         each.add()
     router_part = sum(
-        dot("td,et->de", shard, shard_logits[:experts_here])
+        dot("td,et->de", half, half_logits)
         for shard, shard_logits in zip(tokens, d_logits)
+        for half, half_logits in (
+            (shard[0], shard_logits[:experts_here, :middle]),
+            (shard[1], shard_logits[:experts_here, middle:]),
+        )
     )
     moved, router_part = leave(out_sums, moved, router_part)
     for each in out_sums:
@@ -918,45 +1004,55 @@
     out_rows = out_sum.shape[0] // n
     out_parts = jnp.swapaxes(out_sum.reshape(out_sum.shape[0], n, width // n), 0, 1)
     d_parts = jnp.concatenate([d_parts, out_parts.reshape(n, out_rows, width)], axis=1)
-    right = left = None
-    for k in range(n - 1, 0, -1):
-        moving = tie(*line_send(d_parts, k, right, left))
-        if k == n - 1:
-            moving, d_qkv = tie(moving, d_qkv)
-        right, left = line_pass(*moving, k)
-        if k == n - 1:
-            qkv_part = jnp.concatenate(
-                [dot("td,ct->dc", normed_one, d_qkv), own_columns, gain_two_part[:, None]], axis=1
-            ).astype(low)
-            qkv_sum = rows_halving(qkv_part, order_a)
-            right, left = leave([qkv_sum], right, left)
-            qkv_sum.go()
-        elif k in (n - 2, n - 3):
-            right, left = land([qkv_sum], right, left)
-            qkv_sum.add()
-            qkv_sum.go()
-        else:
-            right, left = tie(right, left)
-    ended = line_end(d_parts, right, left)
+    sums = {}
+
+    def first_work(before, _):
+        rows, _ = tie(d_qkv, before)
+        qkv_part = jnp.concatenate(
+            [dot("td,ct->dc", normed_one, rows), own_columns, gain_two_part[:, None]], axis=1
+        ).astype(low)
+        sums["qkv"] = rows_halving(qkv_part, order_a)
+        sums["qkv"].go()
+        return sums["qkv"].send
+
+    def next_work(before, _):
+        land([sums["qkv"]], before)
+        sums["qkv"].add()
+        sums["qkv"].go()
+        return sums["qkv"].send
+
+    ended, _ = line_scatter(d_parts, (first_work, next_work, next_work))
+    qkv_sum = sums["qkv"]
     d_normed_one = ended[:shard_len]
     (ended,) = land([qkv_sum], ended)
     qkv_sum.add()
     out_own = ended[shard_len:].reshape(out_sum.shape[0], width // n)
-    blocks = line_gather(jnp.concatenate([qkv_sum.finish(), out_own], axis=1).astype(low))
+    block = jnp.concatenate([qkv_sum.finish(), out_own], axis=1).astype(low)
+    rights, lefts = [block], [block]
     _, norm_one_pull = jax.vjp(lambda v: rms_norm(v, full_g1), x_low.astype(full))
     input_grad = (d_hidden + norm_one_pull(d_normed_one)[0]).reshape(1, shard_len, width)
-    input_grad, expert_sum = tie(input_grad, expert_sum)
-    expert_sum = expert_sum.astype(full)
-    gate_grad = expert_sum[:, :, :hidden_w]
-    up_grad = expert_sum[:, :, hidden_w : 2 * hidden_w]
     few = w_down.shape[1]
-    down_grad = jnp.concatenate(
-        [
-            expert_sum[:, start : start + few, 2 * hidden_w :]
-            for start in range(0, expert_sum.shape[1], few)
-        ],
-        axis=2,
-    )
+    last_work = [
+        lambda: expert_sum[:, :, : 2 * hidden_w].astype(full),
+        lambda: jnp.concatenate(
+            [
+                expert_sum[:, start : start + few, 2 * hidden_w :].astype(full)
+                for start in range(0, expert_sum.shape[1], few)
+            ],
+            axis=2,
+        ),
+    ]
+    done = [input_grad]
+    for k in range(1, n):
+        right, left = line_move(rights[-1], lefts[-1], k)
+        if k < 3:
+            done.append(last_work[k - 1]())
+        right, left, done[-1] = tie(right, left, done[-1])
+        rights.append(right)
+        lefts.append(left)
+    blocks = nearest(rights, lefts)
+    input_grad, gate_up_grad, down_grad = done
+    gate_grad, up_grad = gate_up_grad[:, :, :hidden_w], gate_up_grad[:, :, hidden_w:]
     qkv_grad = jnp.zeros((w_qkv.shape[0], QKV_W), full)
     out_grad = jnp.zeros((w_out.shape[0], width), full)
     rest = 0.0

time: 1260 us -> 1250 us (level)
  waiting for transfers between devices: 407 us -> 309 us
  starting transfers between devices: 170 us -> 235 us
  other arithmetic: 115 us -> 137 us
    ppermute x9 -> x18, waiting for transfers between devices: 173 us -> 137 us  [line_pass(): lax.ppermute(to_right, 'seq', [(i, i + 1) for i in range(n - k)])]
    ppermute x15 -> x21, waiting for transfers between devices: 33.4 us -> 3.71 us  [line_move(): lax.ppermute(right, 'seq', [(i, i + 1) for i in range(k - 1, n - 1)])]
    ppermute x9 -> x18, starting transfers between devices: 59.1 us -> 84.9 us  [line_pass(): lax.ppermute(to_right, 'seq', [(i, i + 1) for i in range(n - k)])]
    ppermute x15 -> x21, starting transfers between devices: 26.8 us -> 49.7 us  [line_move(): lax.ppermute(right, 'seq', [(i, i + 1) for i in range(k - 1, n - 1)])]
    ppermute x17, waiting for transfers between devices: 22.4 us -> 5.79 us  [swap(): lax.ppermute(value, axis, [(i, i ^ bit) for i in range(lax.axis_size(axis...]
    ppermute x15 -> x21, waiting for transfers between devices: 90.6 us -> 75 us  [line_move(): lax.ppermute(left, 'seq', [(i, i - 1) for i in range(1, n - k + 1)])]
    select_n x12 -> x18, other arithmetic: 23.3 us -> 34.9 us  [arrived(): block = jnp.where(mine, moved, block)]
    dot_general x14 -> x17, matrix products: 44.3 us -> 34.4 us  [dot(): return jnp.einsum(spec, left, right, preferred_element_type=full)]
  transfers between devices with their start and end apart: 80 -> 110, of which waited for: 38 -> 39; matrix products, arithmetic and copies ran while one was open for 16% -> 16% of each run, Pallas kernels for 26% -> 27%
where the time goes in v9:
time: 1250 us; the launch traced here: 1230 us
  Pallas kernels  387 us (31%)
  waiting for transfers between devices  309 us (25%)
  starting transfers between devices  235 us (19%)
  other arithmetic  137 us (11%)
  local copies, waits for them, and re-layouts  96.6 us (8%)
  between operations  35.4 us (3%)
  matrix products  34.4 us (3%)
    pallas_call x8, Pallas kernels, shard_call(): pl.pallas_call(kernel, grid_spec=pltpu.PrefetchScalarGridSpec(num_scalar_...  236 us
    ppermute x18, waiting for transfers between devices, line_pass(): lax.ppermute(to_right, 'seq', [(i, i + 1) for i in range(n - k)])  137 us
    ppermute x18, starting transfers between devices, line_pass(): lax.ppermute(to_right, 'seq', [(i, i + 1) for i in range(n - k)])  84.9 us
    ppermute x21, waiting for transfers between devices, line_move(): lax.ppermute(left, 'seq', [(i, i - 1) for i in range(1, n - k + 1)])  75 us
    pallas_call x1, Pallas kernels, attention_backward(): pl.pallas_call(functools.partial(backward_kernel, seq_len, query_rows, ke...  55 us
    pallas_call x2, Pallas kernels, weight_grads(): pl.pallas_call(functools.partial(grads_kernel, few), grid=(stop - first,)...  50.9 us
    ppermute x21, starting transfers between devices, line_move(): lax.ppermute(right, 'seq', [(i, i + 1) for i in range(k - 1, n - 1)])  49.7 us
    pallas_call x1, Pallas kernels, attention_forward(): pl.pallas_call(functools.partial(forward_kernel, seq_len, query_rows, key...  39.6 us
  transfers between devices with their start and end apart: 110, of which 39 were waited for; matrix products, arithmetic and copies ran while one was open for 16% of the time, Pallas kernels for 27%

profile of v9, /device:TPU:0, one launch (start us, length us, event | category | flops | bytes accessed | tf_op | source)
XLA Modules:
  0.0 1234.4 jit_solution(1740510576594184528)
XLA Ops:
  15.1 6.4 maximum_maximum_fusion
  23.2 6.0 collective-permute-start
  31.8 5.5 collective-permute-start.2
  63.0 6.5 collective-permute-done.3
  89.8 14.5 %collective-permute-done.7 = bf16[272,1536]{1,0:T(8,128)(2,1)} collective-permute-done((bf16[272,1536]{1,0:T(8,128)(2,1)}, bf16[272,1536]{1,0:T(8,128)(2,1)}, u32[]{:S(2)}, u32[]{:S(2)}) %collective-permute-start.7) | collective-permute-done | bytes 835616 | tf_op jit(solution)/shard_map/ppermute | solution.py:68
  121.2 16.5 %collective-permute-done.11 = bf16[272,1536]{1,0:T(8,128)(2,1)} collective-permute-done((bf16[272,1536]{1,0:T(8,128)(2,1)}, bf16[272,1536]{1,0:T(8,128)(2,1)}, u32[]{:S(2)}, u32[]{:S(2)}) %collective-permute-start.11) | collective-permute-done | bytes 835616 | tf_op jit(solution)/shard_map/ppermute | solution.py:68
  158.0 39.6 %attention_forward.1 = (bf16[4,384,512]{2,1,0:T(8,128)(2,1)S(1)}, f32[2,3,64,2048]{3,2,1,0:T(8,128)S(1)}, f32[2,3,1,2048]{3,2,1,0:T(1,128)S(1)}) custom-call(s32[1,2048]{1,0:T(1,128)S(1)} %bitcast.327, bf16[4,2,5,64,512]{4,3,2,1,0:T(8,128)(2,1)S(1)} %fusion.89.q_ref, bf16[2,2048,64]{2,1,0:T(8,128)(2,1)S(1)} %copy-done.1, bf16[2,64,2048]{2,1,0:T(8,128)(2,1)S(1)} %copy-done.17), custom_call_target="tpu_custom_call" | custom-call | tf_op jit(solution)/shard_map/attention_forward/pallas_call | solution.py:340
  213.3 5.5 collective-permute-done.13
  218.8 6.0 collective-permute-done.14
  224.8 15.5 %collective-permute-done.16 = bf16[384,512]{1,0:T(8,128)(2,1)S(1)} collective-permute-done((bf16[384,512]{1,0:T(8,128)(2,1)S(1)}, bf16[384,512]{1,0:T(8,128)(2,1)S(1)}, u32[]{:S(2)}, u32[]{:S(2)}) %collective-permute-start.16) | collective-permute-done | bytes 393248 | tf_op jit(solution)/shard_map/ppermute | solution.py:203
  251.4 5.4 collective-permute-start.22
  263.3 22.2 %all-gather.5.cloned.1.call-done.wgu_ref.wd_ref = bf16[10,1536,1536]{2,1,0:T(8,128)(2,1)} async-done(((bf16[10,192,1536]{2,1,0:T(8,128)(2,1)}), bf16[10,1536,1536]{2,1,0:T(8,128)(2,1)}) %all-gather.5.cloned.1.call-update) | async-done | bytes 47185936 | tf_op jit(solution)/shard_map/all_gather | solution.py:851
  287.1 27.1 %experts_forward.4 = (bf16[4,512,1536]{2,1,0:T(8,128)(2,1)}, bf16[10,4,160,1536]{3,2,1,0:T(8,128)(2,1)}, bf16[10,4,160,1024]{3,2,1,0:T(8,128)(2,1)}, f32[10,512]{1,0:T(8,128)S(1)}) custom-call(s32[2]{0:T(128)S(1)} %copy-done.40, bf16[256,1536]{1,0:T(8,128)(2,1)} %get-tuple-element.531.tok_ref, bf16[256,1536]{1,0:T(8,128)(2,1)} %get-tuple-element.530.more_ref, ...), custom_call_target="tpu_custom_call" | custom-call | tf_op jit(solution)/shard_map/experts_forward/pallas_call | solution.py:564
  322.8 26.6 %experts_forward.5 = (bf16[4,512,1536]{2,1,0:T(8,128)(2,1)}, bf16[10,4,160,1536]{3,2,1,0:T(8,128)(2,1)}, bf16[10,4,160,1024]{3,2,1,0:T(8,128)(2,1)}, f32[10,512]{1,0:T(8,128)S(1)}) custom-call(s32[2]{0:T(128)S(1)} %copy-done.38, bf16[256,1536]{1,0:T(8,128)(2,1)S(1)} %broadcast_select_fusion.4.tok_ref, ...), custom_call_target="tpu_custom_call", output_to_operand_aliasing={{0}: (8, {}), {1}: (9, {}), {2}: (10, {})} | custom-call | tf_op jit(solution)/shard_map/experts_forward/pallas_call | solution.py:564
  362.0 26.7 %experts_forward.6 = (bf16[4,512,1536]{2,1,0:T(8,128)(2,1)}, bf16[10,4,160,1536]{3,2,1,0:T(8,128)(2,1)}, bf16[10,4,160,1024]{3,2,1,0:T(8,128)(2,1)}, f32[10,512]{1,0:T(8,128)S(1)}) custom-call(s32[2]{0:T(128)S(1)} %get-tuple-element.586.at_ref, ...), custom_call_target="tpu_custom_call", output_to_operand_aliasing={{0}: (8, {}), {1}: (9, {}), {2}: (10, {})} | custom-call | tf_op jit(solution)/shard_map/experts_forward/pallas_call | solution.py:564
  388.7 5.5 collective-permute-done.29
  398.4 26.8 %experts_forward.7 = (bf16[4,512,1536]{2,1,0:T(8,128)(2,1)}, bf16[10,4,160,1536]{3,2,1,0:T(8,128)(2,1)}, bf16[10,4,160,1024]{3,2,1,0:T(8,128)(2,1)}, f32[10,512]{1,0:T(8,128)S(1)}) custom-call(s32[2]{0:T(128)S(1)} %get-tuple-element.583.at_ref, ...), custom_call_target="tpu_custom_call", output_to_operand_aliasing={{0}: (8, {}), {1}: (9, {}), {2}: (10, {})} | custom-call | tf_op jit(solution)/shard_map/experts_forward/pallas_call | solution.py:564
  434.3 15.0 %collective-permute-done.30 = bf16[256,1536]{1,0:T(8,128)(2,1)S(1)} collective-permute-done((bf16[256,1536]{1,0:T(8,128)(2,1)S(1)}, bf16[256,1536]{1,0:T(8,128)(2,1)S(1)}, u32[]{:S(2)}, u32[]{:S(2)}) %collective-permute-start.30) | collective-permute-done | bytes 786464 | tf_op jit(solution)/shard_map/ppermute | solution.py:134
  454.9 11.3 collective-permute-done.36
  471.7 11.3 collective-permute-done.32
  491.3 8.5 collective-permute-done.38
  522.0 10.1 collective-permute-done.40
  553.2 32.2 %experts_backward.4 = (bf16[4,512,1536]{2,1,0:T(8,128)(2,1)}, bf16[10,4,160,1536]{3,2,1,0:T(8,128)(2,1)}, bf16[10,4,160,1024]{3,2,1,0:T(8,128)(2,1)}, bf16[10,4,...) custom-call(s32[2]{0:T(128)S(1)} %copy-done.41, bf16[256,1536]{1,0:T(8,128)(2,1)S(1)} %get-tuple-element.529.tok_ref, ...), custom_call_target="tpu_custom_call" | custom-call | tf_op jit(solution)/shard_map/experts_backward/pallas_call | solution.py:564
  591.5 10.7 collective-permute-start.54
  602.9 32.1 %experts_backward.5 = (bf16[4,512,1536]{2,1,0:T(8,128)(2,1)}, bf16[10,4,160,1536]{3,2,1,0:T(8,128)(2,1)}, bf16[10,4,160,1024]{3,2,1,0:T(8,128)(2,1)}, bf16[10,4,...) custom-call(s32[2]{0:T(128)S(1)} %copy-done.39, ...), custom_call_target="tpu_custom_call", output_to_operand_aliasing={{0}: (10, {}), {1}: (11, {}), {2}: (12, {}), {3}: (13, {})} | custom-call | tf_op jit(solution)/shard_map/experts_backward/pallas_call | solution.py:564
  643.8 32.1 %experts_backward.6 = (bf16[4,512,1536]{2,1,0:T(8,128)(2,1)}, bf16[10,4,160,1536]{3,2,1,0:T(8,128)(2,1)}, bf16[10,4,160,1024]{3,2,1,0:T(8,128)(2,1)}, bf16[10,4,...) custom-call(s32[2]{0:T(128)S(1)} %get-tuple-element.586.at_ref, ...), custom_call_target="tpu_custom_call", output_to_operand_aliasing={{0}: (10, {}), {1}: (11, {}), {2}: (12, {}), {3}: (13, {})} | custom-call | tf_op jit(solution)/shard_map/experts_backward/pallas_call | solution.py:564
  676.0 12.2 collective-permute-done.58
  692.3 32.1 %experts_backward.7 = (bf16[4,512,1536]{2,1,0:T(8,128)(2,1)}, bf16[10,4,160,1536]{3,2,1,0:T(8,128)(2,1)}, bf16[10,4,160,1024]{3,2,1,0:T(8,128)(2,1)}, bf16[10,4,...) custom-call(s32[2]{0:T(128)S(1)} %get-tuple-element.583.at_ref, ...), custom_call_target="tpu_custom_call", output_to_operand_aliasing={{0}: (10, {}), {1}: (11, {}), {2}: (12, {}), {3}: (13, {})} | custom-call | tf_op jit(solution)/shard_map/experts_backward/pallas_call | solution.py:564
  729.2 10.0 collective-permute-start.63
  747.5 25.5 %weight_grads.2.refs_0_ = bf16[10,1536,1536]{2,1,0:T(8,128)(2,1)} custom-call(bf16[10,640,1536]{2,1,0:T(8,128)(2,1)} %bitcast.335, bf16[10,640,1024]{2,1,0:T(8,128)(2,1)} %bitcast.337, bf16[10,640,512]{2,1,0:T(8,128)(2,1)} %bitcast.339, bf16[10,640,1536]{2,1,0:T(8,128)(2,1)} %bitcast.333), custom_call_target="tpu_custom_call" | custom-call | tf_op jit(solution)/shard_map/weight_grads/pallas_call | solution.py:733
  784.4 25.4 %weight_grads.3 = bf16[10,1536,1536]{2,1,0:T(8,128)(2,1)} custom-call(bf16[10,640,1536]{2,1,0:T(8,128)(2,1)} %bitcast.336, bf16[10,640,1024]{2,1,0:T(8,128)(2,1)} %bitcast.338, bf16[10,640,512]{2,1,0:T(8,128)(2,1)} %bitcast.340, bf16[10,640,1536]{2,1,0:T(8,128)(2,1)} %bitcast.334, ...), custom_call_target="tpu_custom_call", output_to_operand_aliasing={{}: (4, {})} | custom-call | tf_op jit(solution)/shard_map/weight_grads/pallas_call | solution.py:733
  817.4 14.2 %collective-permute-done.68 = bf16[256,1536]{1,0:T(8,128)(2,1)S(1)} collective-permute-done((bf16[256,1536]{1,0:T(8,128)(2,1)S(1)}, bf16[256,1536]{1,0:T(8,128)(2,1)S(1)}, u32[]{:S(2)}, u32[]{:S(2)}) %collective-permute-start.68) | collective-permute-done | bytes 786464 | tf_op jit(solution)/shard_map/ppermute | solution.py:134
  848.0 11.8 collective-permute-done.70
  860.3 7.7 collective-permute-start.72
  871.7 8.9 collective-permute-done.72
  891.4 5.4 out_grads.1
  926.4 7.6 collective-permute-done.78
  934.0 17.6 %collective-permute-done.80 = bf16[384,512]{1,0:T(8,128)(2,1)} collective-permute-done((bf16[384,512]{1,0:T(8,128)(2,1)}, bf16[384,512]{1,0:T(8,128)(2,1)}, u32[]{:S(2)}, u32[]{:S(2)}) %collective-permute-start.80) | collective-permute-done | bytes 393248 | tf_op jit(solution)/shard_map/ppermute | solution.py:203
  964.8 55.0 %attention_backward.1 = (bf16[2,3,64,2048]{3,2,1,0:T(8,128)(2,1)S(1)}, bf16[2,64,2048]{2,1,0:T(8,128)(2,1)S(1)}, bf16[2,64,2048]{2,1,0:T(8,128)(2,1)S(1)}) custom-call(s32[1,2048]{1,0:T(1,128)S(1)} %bitcast.328, bf16[4,2,5,64,512]{4,3,2,1,0:T(8,128)(2,1)S(1)} %fusion.89.q_ref, bf16[2,2048,64]{2,1,0:T(8,128)(2,1)S(1)} %copy-done.2, ...), custom_call_target="tpu_custom_call" | custom-call | tf_op jit(solution)/shard_map/attention_backward/pallas_call | solution.py:411
  1025.9 9.8 convolution_convert_fusion
  1072.2 15.2 %collective-permute-done.86 = bf16[272,1536]{1,0:T(8,128)(2,1)} collective-permute-done((bf16[272,1536]{1,0:T(8,128)(2,1)}, bf16[272,1536]{1,0:T(8,128)(2,1)}, u32[]{:S(2)}, u32[]{:S(2)}) %collective-permute-start.86) | collective-permute-done | bytes 835616 | tf_op jit(solution)/shard_map/ppermute | solution.py:134
  1106.4 7.1 collective-permute-done.88
  1115.1 9.5 collective-permute-start.93
  1125.8 6.6 collective-permute-done.96
  1134.1 8.6 collective-permute-start.98
  1152.4 12.9 %collective-permute-done.98 = bf16[288,1536]{1,0:T(8,128)(2,1)S(1)} collective-permute-done((bf16[288,1536]{1,0:T(8,128)(2,1)}, bf16[288,1536]{1,0:T(8,128)(2,1)S(1)}, u32[]{:S(2)}, u32[]{:S(2)}) %collective-permute-start.98) | collective-permute-done | bytes 884768 | tf_op jit(solution)/shard_map/ppermute | solution.py:134
  1174.1 7.7 collective-permute-start.101
  1207.6 8.8 collective-permute-done.106
  (735 shorter events, 453.8 us)
Async XLA Ops:
  7.2 70.0 %all-gather.3.cloned.1.call-start = ((), (), s32[]{:S(2)}) async-start(), calls=%async_computation.1 | async-start | bytes 7962624 | tf_op jit(solution)/shard_map/all_gather | solution.py:785
  12.9 272.7 %all-gather.5.cloned.1.call-start = ((), (), s32[]{:S(2)}) async-start(), calls=%async_computation.2 | async-start | bytes 53084160 | tf_op jit(solution)/shard_map/all_gather | solution.py:851
  21.5 1168.3 %reduce-scatter.2.cloned.1.call-start = ((), (), s32[]{:S(2)}) async-start(), calls=%async_computation.3 | async-start | bytes 53084160 | tf_op jit(solution)/shard_map/reduce_scatter | solution.py:960
  69.5 34.8 %collective-permute-start.7 = (bf16[272,1536]{1,0:T(8,128)(2,1)}, bf16[272,1536]{1,0:T(8,128)(2,1)}, u32[]{:S(2)}, u32[]{:S(2)}) collective-permute-start(bf16[272,1536]{1,0:T(8,128)(2,1)} %collective-permute-done.3), channel_id=1, source_target_pairs={{1,0},{2,1},{5,4},{6,5},{9,8},{10,9},{13,12},{14,13},{17,16},{18,1... | collective-permute-start | bytes 2506760 | tf_op jit(solution)/shard_map/ppermute | solution.py:68
  70.8 33.5 %collective-permute-start.6 = (bf16[272,1536]{1,0:T(8,128)(2,1)}, bf16[272,1536]{1,0:T(8,128)(2,1)}, u32[]{:S(2)}, u32[]{:S(2)}) collective-permute-start(bf16[272,1536]{1,0:T(8,128)(2,1)} %collective-permute-done.2), channel_id=1, source_target_pairs={{1,2},{2,3},{5,6},{6,7},{9,10},{10,11},{13,14},{14,15},{17,18},{18... | collective-permute-start | bytes 2506760 | tf_op jit(solution)/shard_map/ppermute | solution.py:67
  206.6 33.7 %collective-permute-start.16 = (bf16[384,512]{1,0:T(8,128)(2,1)S(1)}, bf16[384,512]{1,0:T(8,128)(2,1)S(1)}, u32[]{:S(2)}, u32[]{:S(2)}) collective-permute-start(bf16[384,512]{1,0:T(8,128)(2,1)S(1)} %get-tuple-element.533), channel_id=1, source_target_pairs={{2,0},{3,1},{6,4},{7,5},{10,8},{11,9},{14,12},{15,13},{18,16},{19,... | collective-permute-start | bytes 1179656 | tf_op jit(solution)/shard_map/ppermute | solution.py:203
  248.0 66.8 %collective-permute-start.18 = (bf16[256,1536]{1,0:T(8,128)(2,1)}, bf16[256,1536]{1,0:T(8,128)(2,1)}, u32[]{:S(2)}, u32[]{:S(2)}) collective-permute-start(bf16[256,1536]{1,0:T(8,128)(2,1)} %get-tuple-element.531.tok_ref), channel_id=1, source_target_pairs={{0,1},{1,2},{2,3},{4,5},{5,6},{6,7},{8,9},{9,10},{10,11},{12,13},{... | collective-permute-start | bytes 2359304 | tf_op jit(solution)/shard_map/ppermute | solution.py:67
  250.2 64.6 %collective-permute-start.19 = (bf16[256,1536]{1,0:T(8,128)(2,1)}, bf16[256,1536]{1,0:T(8,128)(2,1)}, u32[]{:S(2)}, u32[]{:S(2)}) collective-permute-start(bf16[256,1536]{1,0:T(8,128)(2,1)} %get-tuple-element.531.tok_ref), channel_id=1, source_target_pairs={{1,0},{2,1},{3,2},{5,4},{6,5},{7,6},{9,8},{10,9},{11,10},{13,12},{... | collective-permute-start | bytes 2359304 | tf_op jit(solution)/shard_map/ppermute | solution.py:68
  251.4 65.5 %collective-permute-start.22 = (bf16[256,1536]{1,0:T(8,128)(2,1)}, bf16[256,1536]{1,0:T(8,128)(2,1)}, u32[]{:S(2)}, u32[]{:S(2)}) collective-permute-start(bf16[256,1536]{1,0:T(8,128)(2,1)} %get-tuple-element.530.more_ref), channel_id=1, source_target_pairs={{0,1},{1,2},{2,3},{4,5},{5,6},{6,7},{8,9},{9,10},{10,11},{12,13},{... | collective-permute-start | bytes 2359304 | tf_op jit(solution)/shard_map/ppermute | solution.py:67
  256.9 60.1 %collective-permute-start.23 = (bf16[256,1536]{1,0:T(8,128)(2,1)}, bf16[256,1536]{1,0:T(8,128)(2,1)}, u32[]{:S(2)}, u32[]{:S(2)}) collective-permute-start(bf16[256,1536]{1,0:T(8,128)(2,1)} %get-tuple-element.530.more_ref), channel_id=1, source_target_pairs={{1,0},{2,1},{3,2},{5,4},{6,5},{7,6},{9,8},{10,9},{11,10},{13,12},{... | collective-permute-start | bytes 2359304 | tf_op jit(solution)/shard_map/ppermute | solution.py:68
  314.8 34.6 %collective-permute-start.20 = (bf16[256,1536]{1,0:T(8,128)(2,1)}, bf16[256,1536]{1,0:T(8,128)(2,1)S(1)}, u32[]{:S(2)}, u32[]{:S(2)}) collective-permute-start(bf16[256,1536]{1,0:T(8,128)(2,1)} %collective-permute-done.18), channel_id=1, source_target_pairs={{1,2},{2,3},{5,6},{6,7},{9,10},{10,11},{13,14},{14,15},{17,18},{18... | collective-permute-start | bytes 2359304 | tf_op jit(solution)/shard_map/ppermute | solution.py:67
  315.7 33.8 %collective-permute-start.21 = (bf16[256,1536]{1,0:T(8,128)(2,1)}, bf16[256,1536]{1,0:T(8,128)(2,1)S(1)}, u32[]{:S(2)}, u32[]{:S(2)}) collective-permute-start(bf16[256,1536]{1,0:T(8,128)(2,1)} %collective-permute-done.19), channel_id=1, source_target_pairs={{1,0},{2,1},{5,4},{6,5},{9,8},{10,9},{13,12},{14,13},{17,16},{18,1... | collective-permute-start | bytes 2359304 | tf_op jit(solution)/shard_map/ppermute | solution.py:68
  317.0 34.5 %collective-permute-start.26 = (bf16[256,1536]{1,0:T(8,128)(2,1)}, bf16[256,1536]{1,0:T(8,128)(2,1)S(1)}, u32[]{:S(2)}, u32[]{:S(2)}) collective-permute-start(bf16[256,1536]{1,0:T(8,128)(2,1)} %collective-permute-done.22), channel_id=1, source_target_pairs={{1,2},{2,3},{5,6},{6,7},{9,10},{10,11},{13,14},{14,15},{17,18},{18... | collective-permute-start | bytes 2359304 | tf_op jit(solution)/shard_map/ppermute | solution.py:67
  317.7 38.8 %collective-permute-start.27 = (bf16[256,1536]{1,0:T(8,128)(2,1)}, bf16[256,1536]{1,0:T(8,128)(2,1)S(1)}, u32[]{:S(2)}, u32[]{:S(2)}) collective-permute-start(bf16[256,1536]{1,0:T(8,128)(2,1)} %collective-permute-done.23), channel_id=1, source_target_pairs={{1,0},{2,1},{5,4},{6,5},{9,8},{10,9},{13,12},{14,13},{17,16},{18,1... | collective-permute-start | bytes 2359304 | tf_op jit(solution)/shard_map/ppermute | solution.py:68
  349.5 39.2 %collective-permute-start.24 = (bf16[256,1536]{1,0:T(8,128)(2,1)S(1)}, bf16[256,1536]{1,0:T(8,128)(2,1)S(1)}, u32[]{:S(2)}, u32[]{:S(2)}) collective-permute-start(bf16[256,1536]{1,0:T(8,128)(2,1)S(1)} %collective-permute-done.20), channel_id=1, source_target_pairs={{2,3},{6,7},{10,11},{14,15},{18,19},{22,23},{26,27},{30,31}} | collective-permute-start | bytes 2359304 | tf_op jit(solution)/shard_map/ppermute | solution.py:67
  350.2 38.5 %collective-permute-start.25 = (bf16[256,1536]{1,0:T(8,128)(2,1)S(1)}, bf16[256,1536]{1,0:T(8,128)(2,1)S(1)}, u32[]{:S(2)}, u32[]{:S(2)}) collective-permute-start(bf16[256,1536]{1,0:T(8,128)(2,1)S(1)} %collective-permute-done.21), channel_id=1, source_target_pairs={{1,0},{5,4},{9,8},{13,12},{17,16},{21,20},{25,24},{29,28}} | collective-permute-start | bytes 2359304 | tf_op jit(solution)/shard_map/ppermute | solution.py:68
  357.2 36.9 %collective-permute-start.29 = (bf16[256,1536]{1,0:T(8,128)(2,1)S(1)}, bf16[256,1536]{1,0:T(8,128)(2,1)S(1)}, u32[]{:S(2)}, u32[]{:S(2)}) collective-permute-start(bf16[256,1536]{1,0:T(8,128)(2,1)S(1)} %collective-permute-done.27), channel_id=1, source_target_pairs={{1,0},{5,4},{9,8},{13,12},{17,16},{21,20},{25,24},{29,28}} | collective-permute-start | bytes 2359304 | tf_op jit(solution)/shard_map/ppermute | solution.py:68
  432.2 33.9 %collective-permute-start.36 = (bf16[256,1536]{1,0:T(8,128)(2,1)S(1)}, bf16[256,1536]{1,0:T(8,128)(2,1)S(1)}, u32[]{:S(2)}, u32[]{:S(2)}) collective-permute-start(bf16[256,1536]{1,0:T(8,128)(2,1)S(1)} %get-tuple-element.515), channel_id=1, source_target_pairs={{0,1},{4,5},{8,9},{12,13},{16,17},{20,21},{24,25},{28,29}} | collective-permute-start | bytes 2359304 | tf_op jit(solution)/shard_map/ppermute | solution.py:134
  484.6 35.3 %collective-permute-start.34 = (bf16[256,1536]{1,0:T(8,128)(2,1)}, bf16[256,1536]{1,0:T(8,128)(2,1)}, u32[]{:S(2)}, u32[]{:S(2)}) collective-permute-start(bf16[256,1536]{1,0:T(8,128)(2,1)} %get-tuple-element.507), channel_id=1, source_target_pairs={{0,1},{1,2},{2,3},{4,5},{5,6},{6,7},{8,9},{9,10},{10,11},{12,13},{... | collective-permute-start | bytes 2359304 | tf_op jit(solution)/shard_map/ppermute | solution.py:134
  538.5 49.0 %collective-permute-start.47 = (bf16[272,1536]{1,0:T(8,128)(2,1)S(1)}, bf16[272,1536]{1,0:T(8,128)(2,1)S(1)}, u32[]{:S(2)}, u32[]{:S(2)}) collective-permute-start(bf16[272,1536]{1,0:T(8,128)(2,1)S(1)} %fusion.85.more_ref), channel_id=1, source_target_pairs={{0,1},{1,2},{2,3},{4,5},{5,6},{6,7},{8,9},{9,10},{10,11},{12,13},{... | collective-permute-start | bytes 2506760 | tf_op jit(solution)/shard_map/ppermute | solution.py:67
  543.0 44.5 %collective-permute-start.48 = (bf16[272,1536]{1,0:T(8,128)(2,1)S(1)}, bf16[272,1536]{1,0:T(8,128)(2,1)S(1)}, u32[]{:S(2)}, u32[]{:S(2)}) collective-permute-start(bf16[272,1536]{1,0:T(8,128)(2,1)S(1)} %fusion.85.more_ref), channel_id=1, source_target_pairs={{1,0},{2,1},{3,2},{5,4},{6,5},{7,6},{9,8},{10,9},{11,10},{13,12},{... | collective-permute-start | bytes 2506760 | tf_op jit(solution)/shard_map/ppermute | solution.py:68
  544.3 41.1 %collective-permute-start.45 = (bf16[256,1536]{1,0:T(8,128)(2,1)S(1)}, bf16[256,1536]{1,0:T(8,128)(2,1)S(1)}, u32[]{:S(2)}, u32[]{:S(2)}) collective-permute-start(bf16[256,1536]{1,0:T(8,128)(2,1)S(1)} %get-tuple-element.529.tok_ref), channel_id=1, source_target_pairs={{0,1},{1,2},{2,3},{4,5},{5,6},{6,7},{8,9},{9,10},{10,11},{12,13},{... | collective-permute-start | bytes 2359304 | tf_op jit(solution)/shard_map/ppermute | solution.py:67
  549.2 36.2 %collective-permute-start.46 = (bf16[256,1536]{1,0:T(8,128)(2,1)S(1)}, bf16[256,1536]{1,0:T(8,128)(2,1)S(1)}, u32[]{:S(2)}, u32[]{:S(2)}) collective-permute-start(bf16[256,1536]{1,0:T(8,128)(2,1)S(1)} %get-tuple-element.529.tok_ref), channel_id=1, source_target_pairs={{1,0},{2,1},{3,2},{5,4},{6,5},{7,6},{9,8},{10,9},{11,10},{13,12},{... | collective-permute-start | bytes 2359304 | tf_op jit(solution)/shard_map/ppermute | solution.py:68
  550.5 36.9 %collective-permute-start.49 = (f32[1,1]{1,0:T(1,128)}, f32[1,1]{1,0:T(1,128)}, u32[]{:S(2)}, u32[]{:S(2)}) collective-permute-start(f32[1,1]{1,0:T(1,128)} %bitcast.81), channel_id=1, source_target_pairs={{0,1},{1,0},{2,3},{3,2},{4,5},{5,4},{6,7},{7,6},{8,9},{9,8},{10,11... | collective-permute-start | bytes 20 | tf_op jit(solution)/shard_map/ppermute | solution.py:208
  585.4 49.6 %collective-permute-start.50 = (bf16[256,1536]{1,0:T(8,128)(2,1)S(1)}, bf16[256,1536]{1,0:T(8,128)(2,1)S(1)}, u32[]{:S(2)}, u32[]{:S(2)}) collective-permute-start(bf16[256,1536]{1,0:T(8,128)(2,1)S(1)} %collective-permute-done.45), channel_id=1, source_target_pairs={{1,2},{2,3},{5,6},{6,7},{9,10},{10,11},{13,14},{14,15},{17,18},{18... | collective-permute-start | bytes 2359304 | tf_op jit(solution)/shard_map/ppermute | solution.py:67
  586.2 48.9 %collective-permute-start.51 = (bf16[256,1536]{1,0:T(8,128)(2,1)S(1)}, bf16[256,1536]{1,0:T(8,128)(2,1)S(1)}, u32[]{:S(2)}, u32[]{:S(2)}) collective-permute-start(bf16[256,1536]{1,0:T(8,128)(2,1)S(1)} %collective-permute-done.46), channel_id=1, source_target_pairs={{1,0},{2,1},{5,4},{6,5},{9,8},{10,9},{13,12},{14,13},{17,16},{18,1... | collective-permute-start | bytes 2359304 | tf_op jit(solution)/shard_map/ppermute | solution.py:68
  587.5 49.6 %collective-permute-start.52 = (bf16[272,1536]{1,0:T(8,128)(2,1)S(1)}, bf16[272,1536]{1,0:T(8,128)(2,1)S(1)}, u32[]{:S(2)}, u32[]{:S(2)}) collective-permute-start(bf16[272,1536]{1,0:T(8,128)(2,1)S(1)} %collective-permute-done.47), channel_id=1, source_target_pairs={{1,2},{2,3},{5,6},{6,7},{9,10},{10,11},{13,14},{14,15},{17,18},{18... | collective-permute-start | bytes 2506760 | tf_op jit(solution)/shard_map/ppermute | solution.py:67
  588.2 48.9 %collective-permute-start.53 = (bf16[272,1536]{1,0:T(8,128)(2,1)S(1)}, bf16[272,1536]{1,0:T(8,128)(2,1)S(1)}, u32[]{:S(2)}, u32[]{:S(2)}) collective-permute-start(bf16[272,1536]{1,0:T(8,128)(2,1)S(1)} %collective-permute-done.48), channel_id=1, source_target_pairs={{1,0},{2,1},{5,4},{6,5},{9,8},{10,9},{13,12},{14,13},{17,16},{18,1... | collective-permute-start | bytes 2506760 | tf_op jit(solution)/shard_map/ppermute | solution.py:68
  591.5 45.6 %collective-permute-start.54 = (f32[1,1]{1,0:T(1,128)}, f32[1,1]{1,0:T(1,128)}, u32[]{:S(2)}, u32[]{:S(2)}) collective-permute-start(f32[1,1]{1,0:T(1,128)} %add.686), channel_id=1, source_target_pairs={{0,2},{1,3},{2,0},{3,1},{4,6},{5,7},{6,4},{7,5},{8,10},{9,11},{10,... | collective-permute-start | bytes 20 | tf_op jit(solution)/shard_map/ppermute | solution.py:208
  635.1 40.9 %collective-permute-start.55 = (bf16[256,1536]{1,0:T(8,128)(2,1)S(1)}, bf16[256,1536]{1,0:T(8,128)(2,1)S(1)}, u32[]{:S(2)}, u32[]{:S(2)}) collective-permute-start(bf16[256,1536]{1,0:T(8,128)(2,1)S(1)} %collective-permute-done.50), channel_id=1, source_target_pairs={{2,3},{6,7},{10,11},{14,15},{18,19},{22,23},{26,27},{30,31}} | collective-permute-start | bytes 2359304 | tf_op jit(solution)/shard_map/ppermute | solution.py:67
  635.8 40.2 %collective-permute-start.56 = (bf16[256,1536]{1,0:T(8,128)(2,1)S(1)}, bf16[256,1536]{1,0:T(8,128)(2,1)S(1)}, u32[]{:S(2)}, u32[]{:S(2)}) collective-permute-start(bf16[256,1536]{1,0:T(8,128)(2,1)S(1)} %collective-permute-done.51), channel_id=1, source_target_pairs={{1,0},{5,4},{9,8},{13,12},{17,16},{21,20},{25,24},{29,28}} | collective-permute-start | bytes 2359304 | tf_op jit(solution)/shard_map/ppermute | solution.py:68
  637.1 38.8 %collective-permute-start.57 = (bf16[272,1536]{1,0:T(8,128)(2,1)S(1)}, bf16[272,1536]{1,0:T(8,128)(2,1)S(1)}, u32[]{:S(2)}, u32[]{:S(2)}) collective-permute-start(bf16[272,1536]{1,0:T(8,128)(2,1)S(1)} %collective-permute-done.52), channel_id=1, source_target_pairs={{2,3},{6,7},{10,11},{14,15},{18,19},{22,23},{26,27},{30,31}} | collective-permute-start | bytes 2506760 | tf_op jit(solution)/shard_map/ppermute | solution.py:67
  637.8 50.3 %collective-permute-start.58 = (bf16[272,1536]{1,0:T(8,128)(2,1)S(1)}, bf16[272,1536]{1,0:T(8,128)(2,1)S(1)}, u32[]{:S(2)}, u32[]{:S(2)}) collective-permute-start(bf16[272,1536]{1,0:T(8,128)(2,1)S(1)} %collective-permute-done.53), channel_id=1, source_target_pairs={{1,0},{5,4},{9,8},{13,12},{17,16},{21,20},{25,24},{29,28}} | collective-permute-start | bytes 2506760 | tf_op jit(solution)/shard_map/ppermute | solution.py:68
  641.4 34.6 %collective-permute-start.59 = (f32[1,1]{1,0:T(1,128)}, f32[1,1]{1,0:T(1,128)}, u32[]{:S(2)}, u32[]{:S(2)}) collective-permute-start(f32[1,1]{1,0:T(1,128)} %add.687), channel_id=1, source_target_pairs={{0,4},{4,0},{8,12},{12,8},{16,20},{20,16},{24,28},{28,24},{1,5},{5... | collective-permute-start | bytes 20 | tf_op jit(solution)/shard_map/ppermute | solution.py:208
  729.2 43.8 %collective-permute-start.63 = (bf16[256,1536]{1,0:T(8,128)(2,1)}, bf16[256,1536]{1,0:T(8,128)(2,1)}, u32[]{:S(2)}, u32[]{:S(2)}) collective-permute-start(bf16[256,1536]{1,0:T(8,128)(2,1)} %get-tuple-element.501), channel_id=1, source_target_pairs={{0,1},{4,5},{8,9},{12,13},{16,17},{20,21},{24,25},{28,29}} | collective-permute-start | bytes 2359304 | tf_op jit(solution)/shard_map/ppermute | solution.py:134
  739.2 33.8 %collective-permute-start.64 = (bf16[256,1536]{1,0:T(8,128)(2,1)}, bf16[256,1536]{1,0:T(8,128)(2,1)}, u32[]{:S(2)}, u32[]{:S(2)}) collective-permute-start(bf16[256,1536]{1,0:T(8,128)(2,1)} %get-tuple-element.500), channel_id=1, source_target_pairs={{3,2},{7,6},{11,10},{15,14},{19,18},{23,22},{27,26},{31,30}} | collective-permute-start | bytes 2359304 | tf_op jit(solution)/shard_map/ppermute | solution.py:135
  745.4 37.3 %collective-permute-start.61 = (bf16[256,1536]{1,0:T(8,128)(2,1)}, bf16[256,1536]{1,0:T(8,128)(2,1)S(1)}, u32[]{:S(2)}, u32[]{:S(2)}) collective-permute-start(bf16[256,1536]{1,0:T(8,128)(2,1)} %get-tuple-element.503), channel_id=1, source_target_pairs={{0,1},{4,5},{8,9},{12,13},{16,17},{20,21},{24,25},{28,29}} | collective-permute-start | bytes 2359304 | tf_op jit(solution)/shard_map/ppermute | solution.py:134
  746.8 36.0 %collective-permute-start.62 = (bf16[256,1536]{1,0:T(8,128)(2,1)}, bf16[256,1536]{1,0:T(8,128)(2,1)S(1)}, u32[]{:S(2)}, u32[]{:S(2)}) collective-permute-start(bf16[256,1536]{1,0:T(8,128)(2,1)} %get-tuple-element.502), channel_id=1, source_target_pairs={{3,2},{7,6},{11,10},{15,14},{19,18},{23,22},{27,26},{31,30}} | collective-permute-start | bytes 2359304 | tf_op jit(solution)/shard_map/ppermute | solution.py:135
  776.0 33.7 %collective-permute-start.66 = (bf16[256,1536]{1,0:T(8,128)(2,1)}, bf16[256,1536]{1,0:T(8,128)(2,1)}, u32[]{:S(2)}, u32[]{:S(2)}) collective-permute-start(bf16[256,1536]{1,0:T(8,128)(2,1)} %get-tuple-element.499), channel_id=1, source_target_pairs={{0,1},{1,2},{4,5},{5,6},{8,9},{9,10},{12,13},{13,14},{16,17},{17,1... | collective-permute-start | bytes 2359304 | tf_op jit(solution)/shard_map/ppermute | solution.py:134
  916.2 35.4 %collective-permute-start.80 = (bf16[384,512]{1,0:T(8,128)(2,1)}, bf16[384,512]{1,0:T(8,128)(2,1)}, u32[]{:S(2)}, u32[]{:S(2)}) collective-permute-start(bf16[384,512]{1,0:T(8,128)(2,1)} %get-tuple-element.522), channel_id=1, source_target_pairs={{2,0},{3,1},{6,4},{7,5},{10,8},{11,9},{14,12},{15,13},{18,16},{19,... | collective-permute-start | bytes 1179656 | tf_op jit(solution)/shard_map/ppermute | solution.py:203
  917.9 33.7 %collective-permute-start.81 = (bf16[384,512]{1,0:T(8,128)(2,1)}, bf16[384,512]{1,0:T(8,128)(2,1)S(1)}, u32[]{:S(2)}, u32[]{:S(2)}) collective-permute-start(bf16[384,512]{1,0:T(8,128)(2,1)} %get-tuple-element.521), channel_id=1, source_target_pairs={{3,0},{7,4},{11,8},{15,12},{19,16},{23,20},{27,24},{31,28}} | collective-permute-start | bytes 1179656 | tf_op jit(solution)/shard_map/ppermute | solution.py:203
  951.6 68.2 %collective-permute-start.82 = (bf16[2,192,768]{2,1,0:T(8,128)(2,1)}, bf16[2,192,768]{2,1,0:T(8,128)(2,1)}, u32[]{:S(2)}, u32[]{:S(2)}) collective-permute-start(bf16[2,192,768]{2,1,0:T(8,128)(2,1)} %add_convert_fusion.3), channel_id=1, source_target_pairs={{0,8},{4,12},{8,0},{12,4},{16,24},{20,28},{24,16},{28,20},{1,9},{5... | collective-permute-start | bytes 1769480 | tf_op jit(solution)/shard_map/ppermute | solution.py:208
  952.5 67.3 %collective-permute-start.83 = (bf16[2,192,768]{2,1,0:T(8,128)(2,1)}, bf16[2,192,768]{2,1,0:T(8,128)(2,1)}, u32[]{:S(2)}, u32[]{:S(2)}) collective-permute-start(bf16[2,192,768]{2,1,0:T(8,128)(2,1)} %add_convert_fusion.2), channel_id=1, source_target_pairs={{0,16},{4,20},{8,24},{12,28},{16,0},{20,4},{24,8},{28,12},{1,17},{... | collective-permute-start | bytes 1769480 | tf_op jit(solution)/shard_map/ppermute | solution.py:208
  1050.4 44.8 %collective-permute-start.91 = (bf16[288,1536]{1,0:T(8,128)(2,1)}, bf16[288,1536]{1,0:T(8,128)(2,1)}, u32[]{:S(2)}, u32[]{:S(2)}) collective-permute-start(bf16[288,1536]{1,0:T(8,128)(2,1)} %get-tuple-element.485), channel_id=1, source_target_pairs={{0,1},{4,5},{8,9},{12,13},{16,17},{20,21},{24,25},{28,29}} | collective-permute-start | bytes 2654216 | tf_op jit(solution)/shard_map/ppermute | solution.py:134
  1052.9 42.4 %collective-permute-start.92 = (bf16[288,1536]{1,0:T(8,128)(2,1)}, bf16[288,1536]{1,0:T(8,128)(2,1)}, u32[]{:S(2)}, u32[]{:S(2)}) collective-permute-start(bf16[288,1536]{1,0:T(8,128)(2,1)} %get-tuple-element.484), channel_id=1, source_target_pairs={{3,2},{7,6},{11,10},{15,14},{19,18},{23,22},{27,26},{31,30}} | collective-permute-start | bytes 2654216 | tf_op jit(solution)/shard_map/ppermute | solution.py:135
  1097.4 35.1 %collective-permute-start.96 = (bf16[288,1536]{1,0:T(8,128)(2,1)S(1)}, bf16[288,1536]{1,0:T(8,128)(2,1)S(1)}, u32[]{:S(2)}, u32[]{:S(2)}) collective-permute-start(bf16[288,1536]{1,0:T(8,128)(2,1)S(1)} %get-tuple-element.483), channel_id=1, source_target_pairs={{0,1},{1,2},{4,5},{5,6},{8,9},{9,10},{12,13},{13,14},{16,17},{17,1... | collective-permute-start | bytes 2654216 | tf_op jit(solution)/shard_map/ppermute | solution.py:134
  1105.5 39.4 %collective-permute-start.95 = (bf16[2,192,681]{2,1,0:T(8,128)(2,1)}, bf16[2,192,681]{2,1,0:T(8,128)(2,1)}, u32[]{:S(2)}, u32[]{:S(2)}) collective-permute-start(bf16[2,192,681]{2,1,0:T(8,128)(2,1)} %add_convert_fusion.1), channel_id=1, source_target_pairs={{0,8},{4,12},{8,0},{12,4},{16,24},{20,28},{24,16},{28,20},{1,9},{5... | collective-permute-start | bytes 1569032 | tf_op jit(solution)/shard_map/ppermute | solution.py:208
  1115.1 35.4 %collective-permute-start.93 = (bf16[272,1536]{1,0:T(8,128)(2,1)}, bf16[272,1536]{1,0:T(8,128)(2,1)}, u32[]{:S(2)}, u32[]{:S(2)}) collective-permute-start(bf16[272,1536]{1,0:T(8,128)(2,1)} %get-tuple-element.487), channel_id=1, source_target_pairs={{0,1},{1,2},{2,3},{4,5},{5,6},{6,7},{8,9},{9,10},{10,11},{12,13},{... | collective-permute-start | bytes 2506760 | tf_op jit(solution)/shard_map/ppermute | solution.py:134
  (221 other events, 3758.5 us)
Sparse Core Ops, SparseCore 0:
  13.0 51.5 all-gather.2
  66.5 218.9 all-gather.4
  836.7 300.3 reduce-scatter.1

commit v10 on v9

--- a/solution.py
+++ b/solution.py
@@ -136,9 +136,33 @@
     )
 
 
+class Doubling:
+    def __init__(self, block, bits):
+        self.blocks, self.order, self.bits = block[None], bits, list(bits)
+        self.away = self.late = False
+
+    def go(self):
+        self.here, self.away = swap(self.blocks, "fsdp", self.bits.pop(0)), True
+
+    def land(self, other):
+        other, here = tie(other, self.here)
+        self.blocks, self.away = jnp.concatenate([self.blocks, here]), False
+        return other
+
+    def rows(self):
+        while self.bits or self.away:
+            if not self.away:
+                self.go()
+            self.land(())
+        mask = lax.axis_index("fsdp") ^ jnp.arange(self.blocks.shape[0])
+        spot = sum(((mask // bit) % 2) << i for i, bit in enumerate(self.order))
+        return self.blocks[spot].reshape(-1, self.blocks.shape[2])
+
+
 class LineGather:
     def __init__(self, halves):
         self.rights, self.lefts = [[half] for half in halves], [[half] for half in halves]
+        self.landed = [0, 0]
 
     def go(self, h):
         step = len(self.rights[h])
@@ -147,39 +171,48 @@
         self.lefts[h].append(left)
 
     def land(self, h, other):
-        spot = len(self.rights[h]) - 1
+        spot = self.landed[h] = len(self.rights[h]) - 1
+        if isinstance(other, Doubling):
+            (self.rights[h][spot], self.lefts[h][spot]) = other.land(
+                (self.rights[h][spot], self.lefts[h][spot])
+            )
+            other = ()
         moved = [(self.rights[part][spot], self.lefts[part][spot]) for part in range(h + 1)]
         moved, other = tie(moved, other)
         for part, (right, left) in enumerate(moved):
             self.rights[part][spot], self.lefts[part][spot] = right, left
         return other
 
+    def hold(self, other):
+        came = [(self.rights[h][-1 - self.ahead(h)], self.lefts[h][-1 - self.ahead(h)]) for h in (0, 1)]
+        return tie(other, came)[0]
+
+    def ahead(self, h):
+        return len(self.rights[h]) - 1 - self.landed[h]
+
     def block(self, turn):
         return [arrived(self.rights[h], self.lefts[h], turn) for h in (0, 1)]
 
 
-def line_scatter(parts, work):
+def line_scatter(halves, work):
     n = lax.axis_size("seq")
     me = lax.axis_index("seq")
-    middle = parts.shape[1] // 32 * 16
-    halves = [parts[:, :middle], parts[:, middle:]]
-    flying = [(None, None), (None, None)]
+    flying = [(None, None)] * len(halves)
     before, given = (), []
     for k in range(n - 1, 0, -1):
-        for h in (0, 1):
+        for h, half in enumerate(halves):
             if k < n - 1 and h:
                 flying[h], before = tie(flying[h], before)
             elif k < n - 1:
                 flying[h], given = tie(flying[h], given)
-            before = line_send(halves[h], k, *flying[h])
+            before = line_send(half, k, *flying[h])
             flying[h] = line_pass(*before, k)
         if n - 1 - k < len(work):
             given = work[n - 1 - k](before, given)
     sums = []
     flying[0], given = tie(flying[0], given)
-    for h in (0, 1):
-        own = at_place(halves[h], me).astype(full)
-        sums.append(own + (flying[h][0].astype(full) + flying[h][1].astype(full)))
+    for half, (right, left) in zip(halves, flying):
+        sums.append(at_place(half, me).astype(full) + (right.astype(full) + left.astype(full)))
     return jnp.concatenate(sums), given
 
 
@@ -360,7 +393,10 @@
         name="attention_forward",
     )(limit, heads, k_rows, vt)
 
-def backward_kernel(seq_len, query_rows, key_rows, limit_ref, q_ref, k_ref, v_ref, kt_ref, out_ref, lse_ref, dout_ref, dq_ref, dk_ref, dv_ref, dk_acc, dv_acc):
+def backward_kernel(
+    seq_len, query_rows, key_rows, per, me_ref, limit_ref, q_ref, k_ref, v_ref, kt_ref, out_ref, lse_ref, *refs
+):
+    blocks, (dq_ref, dk_ref, dv_ref, dk_acc, dv_acc, held) = refs[:-6], refs[-6:]
     i = pl.program_id(1)
 
     @pl.when(i == 0)
@@ -370,7 +406,15 @@
 
     qt = beside(q_ref[0, 0])
     limit = jnp.concatenate([limit_ref[...]] * GROUP, axis=1)
-    dout = jnp.concatenate([dout_ref[0, pl.ds(h * HEAD_DIM, HEAD_DIM), :] for h in range(GROUP)], axis=1)
+    devs = (len(blocks) + 1) // 2
+    gap = me_ref[0] - i // per
+    for spot, block in enumerate(blocks):
+
+        @pl.when(gap == (spot if spot < devs else devs - 1 - spot))
+        def _():
+            held[...] = block[...]
+
+    dout = jnp.concatenate([held[pl.ds(h * HEAD_DIM, HEAD_DIM), :] for h in range(GROUP)], axis=1)
     delta = jnp.sum(dout.astype(full) * beside(out_ref[0]), axis=0, keepdims=True)
     lse = beside(lse_ref[0])
 
@@ -400,41 +444,53 @@
         dk_ref[0] = dk_acc[...].astype(low)
         dv_ref[0] = dv_acc[...].astype(low)
 
-def attention_backward(heads, k_rows, v_rows, kt, limit, out, lse, d_out):
+def attention_backward(heads, k_rows, v_rows, kt, limit, out, lse, me, rights, lefts):
+    blocks = [*rights, *lefts[1:]]
     kv_here, shard_len = heads.shape[1], heads.shape[4]
     seq_len = k_rows.shape[1]
     query_rows = min(256, shard_len)
     key_rows = min(512, seq_len)
     per = shard_len // query_rows
-    quarter = lambda g, i: (g, 0, 0, i)
-    whole = lambda g, i: (g, 0, 0)
+    quarter = lambda g, i, me: (g, 0, 0, i)
+    whole = lambda g, i, me: (g, 0, 0)
     return pl.pallas_call(
-        functools.partial(backward_kernel, seq_len, query_rows, key_rows),
-        grid=(kv_here, seq_len // query_rows),
-        in_specs=[
-            pl.BlockSpec((1, query_rows), lambda g, i: (0, i)),
-            query_spec(query_rows, per),
-            pl.BlockSpec((1, seq_len, HEAD_DIM), whole),
-            pl.BlockSpec((1, seq_len, HEAD_DIM), whole),
-            pl.BlockSpec((1, HEAD_DIM, seq_len), whole),
-            pl.BlockSpec((1, GROUP, HEAD_DIM, query_rows), quarter),
-            pl.BlockSpec((1, GROUP, 1, query_rows), quarter),
-            pl.BlockSpec((1, GROUP * HEAD_DIM, query_rows), lambda g, i: (i // per, g, i % per)),
-        ],
-        out_specs=[
-            pl.BlockSpec((1, GROUP, HEAD_DIM, query_rows), quarter),
-            pl.BlockSpec((1, HEAD_DIM, seq_len), whole),
-            pl.BlockSpec((1, HEAD_DIM, seq_len), whole),
-        ],
+        functools.partial(backward_kernel, seq_len, query_rows, key_rows, per),
+        grid_spec=pltpu.PrefetchScalarGridSpec(
+            num_scalar_prefetch=1,
+            grid=(kv_here, seq_len // query_rows),
+            in_specs=[
+                pl.BlockSpec((1, query_rows), lambda g, i, me: (0, i)),
+                pl.BlockSpec(
+                    (1, 1, GROUP, HEAD_DIM, query_rows),
+                    lambda g, i, me: (i // per, g, 0, 0, i % per),
+                ),
+                pl.BlockSpec((1, seq_len, HEAD_DIM), whole),
+                pl.BlockSpec((1, seq_len, HEAD_DIM), whole),
+                pl.BlockSpec((1, HEAD_DIM, seq_len), whole),
+                pl.BlockSpec((1, GROUP, HEAD_DIM, query_rows), quarter),
+                pl.BlockSpec((1, GROUP, 1, query_rows), quarter),
+            ]
+            + [pl.BlockSpec((GROUP * HEAD_DIM, query_rows), lambda g, i, me: (g, i % per))]
+            * len(blocks),
+            out_specs=[
+                pl.BlockSpec((1, GROUP, HEAD_DIM, query_rows), quarter),
+                pl.BlockSpec((1, HEAD_DIM, seq_len), whole),
+                pl.BlockSpec((1, HEAD_DIM, seq_len), whole),
+            ],
+            scratch_shapes=[
+                pltpu.VMEM((HEAD_DIM, seq_len), full),
+                pltpu.VMEM((HEAD_DIM, seq_len), full),
+                pltpu.VMEM((GROUP * HEAD_DIM, query_rows), low),
+            ],
+        ),
         out_shape=[
             jax.ShapeDtypeStruct((kv_here, GROUP, HEAD_DIM, seq_len), low),
             jax.ShapeDtypeStruct((kv_here, HEAD_DIM, seq_len), low),
             jax.ShapeDtypeStruct((kv_here, HEAD_DIM, seq_len), low),
         ],
-        scratch_shapes=[pltpu.VMEM((HEAD_DIM, seq_len), full), pltpu.VMEM((HEAD_DIM, seq_len), full)],
         compiler_params=vmem(40),
         name="attention_backward",
-    )(limit, heads, k_rows, v_rows, kt, out, lse, d_out)
+    )(me, limit, heads, k_rows, v_rows, kt, out, lse, *blocks)
 
 
 def vmem(mib):
@@ -452,7 +508,7 @@
         for chunk in range(chunks):
             start = (dev * chunks + chunk) * rows
             down_ref[dev * rows : (dev + 1) * rows, chunk * hidden : (chunk + 1) * hidden] = (
-                block_ref[0, start : start + rows, :]
+                block_ref[start : start + rows, :]
             )
 
 
@@ -462,13 +518,13 @@
 
 
 def experts_kernel(
-    few, at_ref, tok_ref, more_ref, slot_ref, member_ref, router_ref, wgu_ref, wd_ref, *refs
+    few, pair, at_ref, tok_ref, more_ref, slot_ref, member_ref, router_ref, wgu_ref, wd_ref, *refs
 ):
     part_ref, x_ref, gu_ref, gates_ref, acc, gates_all, down = refs[-7:]
-    e, experts = pl.program_id(0), pl.num_programs(0)
+    step, steps = pl.program_id(0), pl.num_programs(0)
     slots = x_ref.shape[2]
 
-    @pl.when(e == 0)
+    @pl.when(step == 0)
     def _():
         member = member_ref[...] > 0
         logits = [nt(router_ref[...], ref[...]) for ref in (tok_ref, more_ref)]
@@ -478,64 +534,72 @@
         gates_all[...] = chosen / jnp.sum(chosen, axis=0, keepdims=True)
         acc[...] = jnp.zeros_like(acc)
 
-    gate_row = own_row(gates_all, at_ref[1] * experts + e)
-    gates_ref[pl.ds(e, 1), :] = gate_row
     place = lax.broadcasted_iota(jnp.int32, (slots, 1), 0)
-    here = place == own_row(slot_ref, e)
-    x = pick_rows(jnp.where(here, 1.0, 0.0).astype(low), tok_ref, more_ref)
-    x_ref[0, 0] = x
-    gu = nn(x, wgu_ref[0])
-    gu_ref[0, 0] = gu.astype(low)
-    hidden = gu.shape[1] // 2
-    g, u = gu[:, :hidden], gu[:, hidden:]
-    act = (g * jax.nn.sigmoid(g) * u).astype(low)
-    join_down(few, wd_ref, down)
-    y = nn(act, down[...]).astype(low)
-    acc[...] += tn(jnp.where(here, gate_row, 0.0).astype(low), y)
-
-    @pl.when(e == experts - 1)
+    puts, ys = [], []
+    for i in range(pair):
+        e = step * pair + i
+        gate_row = own_row(gates_all, at_ref[1] * (steps * pair) + e)
+        gates_ref[pl.ds(e, 1), :] = gate_row
+        here = place == own_row(slot_ref, e)
+        x = pick_rows(jnp.where(here, 1.0, 0.0).astype(low), tok_ref, more_ref)
+        x_ref[i, 0] = x
+        gu = nn(x, wgu_ref[i])
+        gu_ref[i, 0] = gu.astype(low)
+        hidden = gu.shape[1] // 2
+        g, u = gu[:, :hidden], gu[:, hidden:]
+        act = (g * jax.nn.sigmoid(g) * u).astype(low)
+        join_down(few, wd_ref.at[i], down.at[i])
+        ys.append(nn(act, down[i]).astype(low))
+        puts.append(jnp.where(here, gate_row, 0.0).astype(low))
+    acc[...] += tn(jnp.concatenate(puts), jnp.concatenate(ys))
+
+    @pl.when(step == steps - 1)
     def _():
         part_ref[0] = acc[...].astype(low)
 
 
 def back_kernel(
-    few, at_ref, tok_ref, more_ref, slot_ref, gates_ref, mix_ref, router_ref, gu_ref, wgu_ref, wd_ref, *refs
+    few, pair, at_ref, tok_ref, more_ref, slot_ref, gates_ref, mix_ref, router_ref, gu_ref, wgu_ref, wd_ref, *refs
 ):
     part_ref, d_ref, dgu_ref, act_ref, dlog_ref, acc, dlog_all, down = refs[-8:]
-    e, experts = pl.program_id(0), pl.num_programs(0)
+    step, steps = pl.program_id(0), pl.num_programs(0)
     slots, hidden = gu_ref.shape[2], gu_ref.shape[3] // 2
 
-    @pl.when(e == 0)
+    @pl.when(step == 0)
     def _():
         dlog_all[...] = jnp.zeros_like(dlog_all)
         acc[...] = jnp.zeros_like(acc)
 
     place = lax.broadcasted_iota(jnp.int32, (slots, 1), 0)
-    here = place == own_row(slot_ref, e)
-    pick = jnp.where(here, 1.0, 0.0).astype(low)
-    gate_row = own_row(gates_ref, e)
-    gate = jnp.sum(jnp.where(here, gate_row, 0.0), axis=1, keepdims=True)
-    d = pick_rows(pick, tok_ref, more_ref)
-    d_ref[0, 0] = d
-    join_down(few, wd_ref, down)
-    d_act = nt(d, down[...])
-    g, u = gu_ref[0, 0, :, :hidden].astype(full), gu_ref[0, 0, :, hidden:].astype(full)
-    sig = jax.nn.sigmoid(g)
-    silu = g * sig
-    act = silu * u
-    d_gate = jnp.sum(d_act * act, axis=1, keepdims=True)
-    d_gate = jnp.sum(jnp.where(here, d_gate, 0.0), axis=0, keepdims=True)
-    dlog_all[pl.ds(e, 1), :] = gate_row * (d_gate - mix_ref[...])
-    act_ref[0, 0] = (act * gate).astype(low)
-    d_act = d_act * gate
-    d_g = (d_act * u * (sig + silu * (1.0 - sig))).astype(low)
-    d_u = (d_act * silu).astype(low)
-    dgu_ref[0, 0, :, :hidden] = d_g
-    dgu_ref[0, 0, :, hidden:] = d_u
-    dx = nt(dgu_ref[0, 0], wgu_ref[0]).astype(low)
-    acc[...] += tn(pick, dx)
-
-    @pl.when(e == experts - 1)
+    puts, dxs = [], []
+    for i in range(pair):
+        e = step * pair + i
+        here = place == own_row(slot_ref, e)
+        pick = jnp.where(here, 1.0, 0.0).astype(low)
+        gate_row = own_row(gates_ref, e)
+        gate = jnp.sum(jnp.where(here, gate_row, 0.0), axis=1, keepdims=True)
+        d = pick_rows(pick, tok_ref, more_ref)
+        d_ref[i, 0] = d
+        join_down(few, wd_ref.at[i], down.at[i])
+        d_act = nt(d, down[i])
+        g, u = gu_ref[i, 0, :, :hidden].astype(full), gu_ref[i, 0, :, hidden:].astype(full)
+        sig = jax.nn.sigmoid(g)
+        silu = g * sig
+        act = silu * u
+        d_gate = jnp.sum(d_act * act, axis=1, keepdims=True)
+        d_gate = jnp.sum(jnp.where(here, d_gate, 0.0), axis=0, keepdims=True)
+        dlog_all[pl.ds(e, 1), :] = gate_row * (d_gate - mix_ref[...])
+        act_ref[i, 0] = (act * gate).astype(low)
+        d_act = d_act * gate
+        d_g = (d_act * u * (sig + silu * (1.0 - sig))).astype(low)
+        d_u = (d_act * silu).astype(low)
+        dgu_ref[i, 0, :, :hidden] = d_g
+        dgu_ref[i, 0, :, hidden:] = d_u
+        dxs.append(nt(dgu_ref[i, 0], wgu_ref[i]).astype(low))
+        puts.append(pick)
+    acc[...] += tn(jnp.concatenate(puts), jnp.concatenate(dxs))
+
+    @pl.when(step == steps - 1)
     def _():
         dlog = dlog_all[...].astype(low)
         dlog_ref[...] = dlog
@@ -546,8 +610,8 @@
     return pl.BlockSpec((1,) + shape, lambda e, at: (e, 0, 0))
 
 
-def in_turn(turn, *shape):
-    return pl.BlockSpec((1, 1) + shape, lambda e, at: (e, turn, 0, 0))
+def in_turn(pair, turn, *shape):
+    return pl.BlockSpec((pair, 1) + shape, lambda e, at: (e, turn, 0, 0))
 
 
 def same(*shape):
@@ -577,20 +641,21 @@
     )(at, *inputs, *buffers)
 
 
-def weight_specs(width, hidden):
+def weight_specs(pair, width, hidden):
     return [
-        pl.BlockSpec((1, width, 2 * hidden), lambda e, at: (e, 0, 0)),
-        pl.BlockSpec((1, width, hidden), lambda e, at: (e, 0, 2)),
+        pl.BlockSpec((pair, width, 2 * hidden), lambda e, at: (e, 0, 0)),
+        pl.BlockSpec((pair, width, hidden), lambda e, at: (e, 0, 2)),
     ]
 
 
 def experts_forward(turn, devs, at, tokens, slot_of, member, router, weights, few, slots, buffers):
     experts, width, columns = weights.shape
     hidden = columns // 3
+    pair = 1 + (experts + 1) % 2
     count = 2 * tokens[0].shape[0]
     total_experts = member.shape[0]
     return shard_call(
-        functools.partial(experts_kernel, few),
+        functools.partial(experts_kernel, few, pair),
         "experts_forward",
         at,
         [*tokens, slot_of, member, router, weights, weights],
@@ -599,12 +664,12 @@
             same(experts, count),
             same(total_experts, count),
             same(total_experts, width),
-            *weight_specs(width, hidden),
+            *weight_specs(pair, width, hidden),
         ],
         [
             in_place(count, width),
-            in_turn(turn, slots, width),
-            in_turn(turn, slots, 2 * hidden),
+            in_turn(pair, turn, slots, width),
+            in_turn(pair, turn, slots, 2 * hidden),
             same(experts, count),
         ],
         [
@@ -617,9 +682,9 @@
         [
             pltpu.VMEM((count, width), full),
             pltpu.VMEM((total_experts, count), full),
-            pltpu.VMEM((hidden, width), low),
+            pltpu.VMEM((pair, hidden, width), low),
         ],
-        experts,
+        experts // pair,
     )
 
 
@@ -628,11 +693,12 @@
 ):
     experts, width, columns = weights.shape
     hidden = columns // 3
+    pair = 1 + (experts + 1) % 2
     count = 2 * d_tokens[0].shape[0]
     slots = gu.shape[2]
     lines = router.shape[0]
     return shard_call(
-        functools.partial(back_kernel, few),
+        functools.partial(back_kernel, few, pair),
         "experts_backward",
         at,
         [*d_tokens, slot_of, gates, mix_dot, router, gu, weights, weights],
@@ -642,14 +708,14 @@
             same(experts, count),
             same(1, count),
             same(lines, width),
-            in_turn(turn, slots, 2 * hidden),
-            *weight_specs(width, hidden),
+            in_turn(pair, turn, slots, 2 * hidden),
+            *weight_specs(pair, width, hidden),
         ],
         [
             in_place(count, width),
-            in_turn(turn, slots, width),
-            in_turn(turn, slots, 2 * hidden),
-            in_turn(turn, slots, hidden),
+            in_turn(pair, turn, slots, width),
+            in_turn(pair, turn, slots, 2 * hidden),
+            in_turn(pair, turn, slots, hidden),
             same(lines, count),
         ],
         [
@@ -663,9 +729,9 @@
         [
             pltpu.VMEM((count, width), full),
             pltpu.VMEM((lines, count), full),
-            pltpu.VMEM((hidden, width), low),
+            pltpu.VMEM((pair, hidden, width), low),
         ],
-        experts,
+        experts // pair,
     )
 
 
@@ -779,20 +845,23 @@
     order = jnp.array(arrival_order(n), jnp.int32)[me]
     x_low = inputs.reshape(shard_len, width)
 
+    hidden_w = w_gate.shape[2]
+    down_chunks = [
+        w_down[:, :, start : start + hidden_w] for start in range(0, width, hidden_w)
+    ]
+    weights = lax.all_gather(
+        jnp.concatenate([w_gate, w_up, jnp.concatenate(down_chunks, axis=1)], axis=2),
+        "fsdp",
+        axis=1,
+        tiled=True,
+    )
+
     own_qkv = lax.dynamic_slice_in_dim(w_qkv, me * group_w, group_w, 1)
     small = jnp.concatenate([gain_one[:, None], gain_two[:, None], w_router], axis=1)
     small = jnp.pad(small, ((0, 0), (0, -small.shape[1] % 128)))
-    first = lax.all_gather(
-        jnp.concatenate([own_qkv, small, w_out], axis=1), "fsdp", axis=0, tiled=True
-    )
-    full_qkv = first[:, :group_w]
-    small = first[:, group_w : group_w + 2 + expert_total]
-    full_out = first[:, -width:]
-    full_g1 = small[:, 0].astype(full)
-    full_g2 = small[:, 1].astype(full)
-    router = small[:, 2:].T
-    own_router = lax.dynamic_slice_in_dim(router, me * experts_here, experts_here, 0)
-    own_router = jnp.pad(own_router, ((0, -experts_here % 16), (0, 0)))
+    plane_first = order_a[1:] + order_a[:1]
+    first = Doubling(jnp.concatenate([own_qkv, small], axis=1), plane_first)
+    out = Doubling(w_out, plane_first)
     valid_rows = valid_mask.reshape(shard_len).astype(full)
 
     routes_low = jnp.concatenate([routes.reshape(shard_len, top_count).T, valid_mask], axis=0)
@@ -808,20 +877,36 @@
     heads = jnp.zeros((n, kv_here, GROUP + 2, HEAD_DIM, shard_len), low)
     routes_all = []
     line = LineGather(halves)
-    signal = swap(x_low[:1, :128], "fsdp", order_a[0])
-    expert_weights, _ = tie((w_gate, w_up, w_down), signal)
+    line.go(0)
+    line.go(1)
+    first.go()
+    x_blocks = [line.block(0)]
+    for turn in range(1, n):
+        for h in (0, 1):
+            if first.away:
+                line.land(h, first)
+                (first if first.bits else out).go()
+            elif out.away and not out.late:
+                line.land(h, out)
+                out.go()
+                out.late = True
+            else:
+                line.land(h, ())
+            if turn < n - 1:
+                line.go(h)
+        x_blocks.append(line.block(turn))
+    first = first.rows()
+    full_qkv = first[:, :group_w]
+    small = first[:, group_w : group_w + 2 + expert_total]
+    full_g1 = small[:, 0].astype(full)
+    full_g2 = small[:, 1].astype(full)
+    router = small[:, 2:].T
+    own_router = lax.dynamic_slice_in_dim(router, me * experts_here, experts_here, 0)
+    own_router = jnp.pad(own_router, ((0, -experts_here % 16), (0, 0)))
     for turn in range(n):
-        if turn:
-            line.land(0, heads if turn > 1 else ())
-            if turn < n - 1:
-                line.go(0)
-            line.land(1, ())
-            if turn < n - 1:
-                line.go(1)
-        else:
-            line.go(0)
-            line.go(1)
-        block = jnp.concatenate(line.block(turn))
+        if turn == n - 1:
+            x_blocks[turn], heads, normed_one = tie(x_blocks[turn], heads, normed_one)
+        block = jnp.concatenate(x_blocks[turn])
         start = order[turn] * shard_len
         normed = rms_norm(block[:shard_len].astype(full), full_g1).astype(low)
         projected = dot("td,dc->ct", normed, full_qkv)
@@ -843,18 +928,6 @@
         normed_one = lax.dynamic_update_slice_in_dim(normed_one, normed, start, 0)
         routes_all.append(block[shard_len : shard_len + top_count + 1, :shard_len])
 
-    w_gate, w_up, w_down = expert_weights
-    hidden_w = w_gate.shape[2]
-    down_chunks = [
-        w_down[:, :, start : start + hidden_w] for start in range(0, width, hidden_w)
-    ]
-    weights = lax.all_gather(
-        jnp.concatenate([w_gate, w_up, jnp.concatenate(down_chunks, axis=1)], axis=2),
-        "fsdp",
-        axis=1,
-        tiled=True,
-    )
-
     routes_all = jnp.stack(routes_all).astype(jnp.int32)
     valid_count = total(jnp.sum(routes_all[:, top_count]).astype(full).reshape(1, 1), "fsdp")[0, 0]
     expert_ids = jnp.arange(expert_total, dtype=jnp.int32)
@@ -870,8 +943,13 @@
     key_rows = jnp.swapaxes(key, 1, 2)
     value_rows = jnp.swapaxes(value, 1, 2)
     attended, out_heads, lse = attention_forward(heads, key_rows, value, limit)
+    if out.away:
+        attended = out.land(attended)
     moved = exchange(attended)
-    moved, slot_of, member, own_router = tie(moved, slot_of, member, own_router)
+    full_out = out.rows()
+    moved, slot_of, member, own_router, valid_count, full_out = tie(
+        moved, slot_of, member, own_router, valid_count, full_out
+    )
     attn_rows = by_place(nearest(*moved)).reshape(HEADS * HEAD_DIM, shard_len)
     projected = dot("kt,kd->td", attn_rows, full_out)
     hidden = x_low.astype(full) + resid_mult * projected
@@ -880,25 +958,27 @@
     normed_low = normed_two.astype(low)
     line = LineGather((normed_low[:middle], normed_low[middle:]))
     buffers, gates, tokens = [], [], []
+    line.go(0)
+    line.go(1)
+    other = ()
     for turn in range(n):
-        if turn:
-            line.land(0, gates[-1])
-            if turn < n - 1:
-                line.go(0)
-            line.land(1, ())
-            if turn < n - 1:
-                line.go(1)
+        if turn < n - 1:
+            for h in (0, 1):
+                other = line.land(h, other)
+                if turn < n - 2:
+                    line.go(h)
+            line_slots = line.hold(slot_of[turn])
         else:
-            line.go(0)
-            line.go(1)
+            line_slots = slot_of[turn]
         tokens.append(line.block(turn))
         *buffers, shard_gates = experts_forward(
-            turn, n, jnp.stack([order[turn], me]), tokens[turn], slot_of[turn], member[turn],
+            turn, n, jnp.stack([order[turn], me]), tokens[turn], line_slots, member[turn],
             router, weights, w_down.shape[1], slots, buffers,
         )
         gates.append(shard_gates)
+        other = shard_gates
     mix_parts, expert_in, gate_up = buffers
-    mixture, _ = line_scatter(mix_parts, ())
+    mixture, _ = line_scatter([mix_parts[:, :middle], mix_parts[:, middle:]], ())
     output_f32 = hidden + resid_mult * mixture
     activations = output_f32.astype(low).reshape(1, shard_len, width)
     error_rows = output_f32 - teacher.astype(full).reshape(shard_len, width)
@@ -920,8 +1000,7 @@
             line.land(0, d_logits[-1])
             if turn < n - 1:
                 line.go(0)
-            squares = line.land(1, squares)
-            squares = loss_steps.send(squares)
+            line.land(1, ())
             if turn < n - 1:
                 line.go(1)
         else:
@@ -943,20 +1022,16 @@
 
     cut = (experts_here + 1) // 2
 
-    losses = [squares]
-
     def some_grads(first, stop):
         def make(before, grads):
-            inputs, _, loss = tie((expert_in, d_gate_up, act_low, d_rows), before, losses[-1])
-            losses.append(loss_steps.send(loss))
+            inputs, _ = tie((expert_in, d_gate_up, act_low, d_rows), before)
             return [weight_grads(*inputs, w_down.shape[1], first, stop, grads)]
 
         return make
 
     d_normed_two, grads = line_scatter(
-        d_parts, (some_grads(0, cut), some_grads(cut, experts_here))
-    )
-    squares = losses[-1]
+        [d_parts], (some_grads(0, cut), some_grads(cut, experts_here))
+    )
     expert_sum = lax.psum_scatter(grads[0], "fsdp", scatter_dimension=1, tiled=True)
 
     d_hidden_norm, gain_two_part = norm_two_pull(d_normed_two)
@@ -979,14 +1054,17 @@
             (shard[1], shard_logits[:experts_here, middle:]),
         )
     )
-    moved, router_part = leave(out_sums, moved, router_part)
+    moved, router_part, squares = leave(out_sums, moved, router_part, squares)
+    squares = loss_steps.send(squares)
     for each in out_sums:
         each.go()
-    d_heads = by_place(nearest(*moved))
     query_grad, key_grad, value_grad = attention_backward(
-        heads, key_rows, value_rows, key, limit, out_heads, lse, d_heads
-    )
-    ((query_grad, key_grad, value_grad),) = land(out_sums, (query_grad, key_grad, value_grad))
+        heads, key_rows, value_rows, key, limit, out_heads, lse, me.reshape(1), *moved
+    )
+    (query_grad, key_grad, value_grad), squares = land(
+        out_sums, (query_grad, key_grad, value_grad), squares
+    )
+    squares = loss_steps.send(squares)
     for each in out_sums:
         each.add()
         each.go()
@@ -1003,7 +1081,10 @@
     out_sum = jnp.concatenate([each.finish() for each in out_sums], axis=1).astype(low)
     out_rows = out_sum.shape[0] // n
     out_parts = jnp.swapaxes(out_sum.reshape(out_sum.shape[0], n, width // n), 0, 1)
-    d_parts = jnp.concatenate([d_parts, out_parts.reshape(n, out_rows, width)], axis=1)
+    d_parts = [
+        d_parts[:, :middle],
+        jnp.concatenate([d_parts[:, middle:], out_parts.reshape(n, out_rows, width)], axis=1),
+    ]
     sums = {}
 
     def first_work(before, _):
@@ -1047,7 +1128,8 @@
         right, left = line_move(rights[-1], lefts[-1], k)
         if k < 3:
             done.append(last_work[k - 1]())
-        right, left, done[-1] = tie(right, left, done[-1])
+        right, left, done[-1], squares = tie(right, left, done[-1], squares)
+        squares = loss_steps.send(squares)
         rights.append(right)
         lefts.append(left)
     blocks = nearest(rights, lefts)
@@ -1068,7 +1150,7 @@
         rest = rest + block[:, group_w : -(width // n)]
     router_grad, gain_two_grad = rest[:, :expert_total], rest[:, expert_total]
     gain_one_grad = jnp.sum(qkv_grad * w_qkv.astype(full), axis=1) / gain_one.astype(full)
-    for _ in range(2):
+    for _ in range(4):
         squares = loss_steps.send(squares)
     loss_value = squares[0, 0] / (valid_count * width)
     return (

time: 1250 us -> 1240 us (level)
  waiting for transfers between devices: 309 us -> 279 us
  local copies, waits for them, and re-layouts: 96.6 us -> 114 us
    ppermute x18 -> x15, waiting for transfers between devices: 137 us -> 114 us  [line_pass(): lax.ppermute(to_right, 'seq', [(i, i + 1) for i in range(n - k)])]
    ppermute x21, waiting for transfers between devices: 3.71 us -> 26 us  [line_move(): lax.ppermute(right, 'seq', [(i, i + 1) for i in range(k - 1, n - 1)])]
    all_gather x1, waiting for transfers between devices: 22.2 us -> 0.01 us  [shards(): lax.all_gather(jnp.concatenate([w_gate, w_up, jnp.concatenate(down_chunks...]
    concatenate x2 -> x6, other arithmetic: 3.84 us -> 17.4 us  [land(): self.blocks, self.away = (jnp.concatenate([self.blocks, here]), False)]
    ppermute x6, waiting for transfers between devices: 24.6 us -> 11.4 us  [exchange(): lax.ppermute(to_right, 'seq', [(i, i + k) for i in range(n - k)])]
    select_n x18 -> x11, other arithmetic: 34.9 us -> 30.3 us  [arrived(): block = jnp.where(mine, moved, block)]
    ppermute x18 -> x15, starting transfers between devices: 84.9 us -> 80.7 us  [line_pass(): lax.ppermute(to_right, 'seq', [(i, i + 1) for i in range(n - k)])]
    unnamed x321 -> x295, local copies, waits for them, and re-layouts: 33.3 us -> 34.9 us
  transfers between devices with their start and end apart: 110 -> 109, of which waited for: 39 -> 36; matrix products, arithmetic and copies ran while one was open for 16% -> 17% of each run, Pallas kernels for 27% -> 24%
where the time goes in v10:
time: 1240 us; the launch traced here: 1230 us
  Pallas kernels  382 us (31%)
  waiting for transfers between devices  279 us (22%)
  starting transfers between devices  236 us (19%)
  other arithmetic  149 us (12%)
  local copies, waits for them, and re-layouts  114 us (9%)
  matrix products  38.4 us (3%)
  between operations  34.2 us (3%)
    pallas_call x8, Pallas kernels, shard_call(): pl.pallas_call(kernel, grid_spec=pltpu.PrefetchScalarGridSpec(num_scalar_...  230 us
    ppermute x15, waiting for transfers between devices, line_pass(): lax.ppermute(to_right, 'seq', [(i, i + 1) for i in range(n - k)])  114 us
    ppermute x15, starting transfers between devices, line_pass(): lax.ppermute(to_right, 'seq', [(i, i + 1) for i in range(n - k)])  80.7 us
    ppermute x21, waiting for transfers between devices, line_move(): lax.ppermute(left, 'seq', [(i, i - 1) for i in range(1, n - k + 1)])  70.6 us
    pallas_call x1, Pallas kernels, attention_backward(): pl.pallas_call(functools.partial(backward_kernel, seq_len, query_rows, ke...  55.9 us
    ppermute x21, starting transfers between devices, line_move(): lax.ppermute(right, 'seq', [(i, i + 1) for i in range(k - 1, n - 1)])  52.5 us
    pallas_call x2, Pallas kernels, weight_grads(): pl.pallas_call(functools.partial(grads_kernel, few), grid=(stop - first,)...  50.8 us
    pallas_call x1, Pallas kernels, attention_forward(): pl.pallas_call(functools.partial(forward_kernel, seq_len, query_rows, key...  40 us
  transfers between devices with their start and end apart: 109, of which 36 were waited for; matrix products, arithmetic and copies ran while one was open for 17% of the time, Pallas kernels for 24%

profile of v10, /device:TPU:0, one launch (start us, length us, event | category | flops | bytes accessed | tf_op | source)
XLA Modules:
  0.0 1232.8 jit_solution(9696294288979484300)
XLA Ops:
  10.0 6.4 maximum_maximum_fusion
  28.6 5.7 collective-permute-start.5
  49.6 8.1 collective-permute-done.5
  61.8 11.2 collective-permute-done.7
  96.2 7.7 collective-permute-done.12
  107.5 15.6 %collective-permute-done.4 = bf16[256,1536]{1,0:T(8,128)(2,1)} collective-permute-done((bf16[256,1536]{1,0:T(8,128)(2,1)}, bf16[256,1536]{1,0:T(8,128)(2,1)}, u32[]{:S(2)}, u32[]{:S(2)}) %collective-permute-start.4) | collective-permute-done | bytes 786464 | tf_op jit(solution)/shard_map/ppermute | solution.py:68
  145.8 16.0 %collective-permute-done.15 = bf16[272,1536]{1,0:T(8,128)(2,1)} collective-permute-done((bf16[272,1536]{1,0:T(8,128)(2,1)}, bf16[272,1536]{1,0:T(8,128)(2,1)}, u32[]{:S(2)}, u32[]{:S(2)}) %collective-permute-start.15) | collective-permute-done | bytes 835616 | tf_op jit(solution)/shard_map/ppermute | solution.py:68
  167.1 5.8 select_select_fusion.2
  190.1 40.0 %attention_forward.1 = (bf16[4,384,512]{2,1,0:T(8,128)(2,1)S(1)}, f32[2,3,64,2048]{3,2,1,0:T(8,128)S(1)}, f32[2,3,1,2048]{3,2,1,0:T(1,128)S(1)}) custom-call(s32[1,2048]{1,0:T(1,128)S(1)} %bitcast.316, bf16[4,2,5,64,512]{4,3,2,1,0:T(8,128)(2,1)S(1)} %fusion.73.q_ref, bf16[2,2048,64]{2,1,0:T(8,128)(2,1)S(1)} %copy-done.1, bf16[2,64,2048]{2,1,0:T(8,128)(2,1)S(1)} %copy-done.22), custom_call_target="tpu_custom_call" | custom-call | tf_op jit(solution)/shard_map/attention_forward/pallas_call | solution.py:373
  275.4 5.4 gather_fusion.1
  280.8 20.0 %collective-permute-done.21 = bf16[384,512]{1,0:T(8,128)(2,1)} collective-permute-done((bf16[384,512]{1,0:T(8,128)(2,1)}, bf16[384,512]{1,0:T(8,128)(2,1)}, u32[]{:S(2)}, u32[]{:S(2)}) %collective-permute-start.21) | collective-permute-done | bytes 393248 | tf_op jit(solution)/shard_map/ppermute | solution.py:236
  304.4 5.5 multiply_reduce_fusion.3
  316.2 5.4 collective-permute-start.31
  322.9 8.2 collective-permute-done.27
  344.4 8.9 collective-permute-done.32
  361.6 25.2 %experts_forward.4 = (bf16[4,512,1536]{2,1,0:T(8,128)(2,1)}, bf16[10,4,160,1536]{3,2,1,0:T(8,128)(2,1)}, bf16[10,4,160,1024]{3,2,1,0:T(8,128)(2,1)}, f32[10,512]{1,0:T(8,128)S(1)}) custom-call(s32[2]{0:T(128)S(1)} %get-tuple-element.598.at_ref, bf16[256,1536]{1,0:T(8,128)(2,1)S(1)} %copy-done.19, bf16[256,1536]{1,0:T(8,128)(2,1)S(1)} %get-tuple-element.540.more_ref, ...), custom_call_target="tpu_custom_call" | custom-call | tf_op jit(solution)/shard_map/experts_forward/pallas_call | solution.py:628
  395.1 25.5 %experts_forward.5 = (bf16[4,512,1536]{2,1,0:T(8,128)(2,1)}, bf16[10,4,160,1536]{3,2,1,0:T(8,128)(2,1)}, bf16[10,4,160,1024]{3,2,1,0:T(8,128)(2,1)}, f32[10,512]{1,0:T(8,128)S(1)}) custom-call(s32[2]{0:T(128)S(1)} %get-tuple-element.599.at_ref, ...), custom_call_target="tpu_custom_call", output_to_operand_aliasing={{0}: (8, {}), {1}: (9, {}), {2}: (10, {})} | custom-call | tf_op jit(solution)/shard_map/experts_forward/pallas_call | solution.py:628
  429.2 25.2 %experts_forward.6 = (bf16[4,512,1536]{2,1,0:T(8,128)(2,1)}, bf16[10,4,160,1536]{3,2,1,0:T(8,128)(2,1)}, bf16[10,4,160,1024]{3,2,1,0:T(8,128)(2,1)}, f32[10,512]{1,0:T(8,128)S(1)}) custom-call(s32[2]{0:T(128)S(1)} %get-tuple-element.600.at_ref, ...), custom_call_target="tpu_custom_call", output_to_operand_aliasing={{0}: (8, {}), {1}: (9, {}), {2}: (10, {})} | custom-call | tf_op jit(solution)/shard_map/experts_forward/pallas_call | solution.py:628
  454.4 25.3 %experts_forward.7 = (bf16[4,512,1536]{2,1,0:T(8,128)(2,1)}, bf16[10,4,160,1536]{3,2,1,0:T(8,128)(2,1)}, bf16[10,4,160,1024]{3,2,1,0:T(8,128)(2,1)}, f32[10,512]{1,0:T(8,128)S(1)}) custom-call(s32[2]{0:T(128)S(1)} %get-tuple-element.597.at_ref, ...), custom_call_target="tpu_custom_call", output_to_operand_aliasing={{0}: (8, {}), {1}: (9, {}), {2}: (10, {})} | custom-call | tf_op jit(solution)/shard_map/experts_forward/pallas_call | solution.py:628
  491.7 14.6 %collective-permute-done.39 = bf16[256,1536]{1,0:T(8,128)(2,1)S(1)} collective-permute-done((bf16[256,1536]{1,0:T(8,128)(2,1)S(1)}, bf16[256,1536]{1,0:T(8,128)(2,1)S(1)}, u32[]{:S(2)}, u32[]{:S(2)}) %collective-permute-start.39) | collective-permute-done | bytes 786464 | tf_op jit(solution)/shard_map/ppermute | solution.py:134
  511.9 11.3 collective-permute-done.45
  528.8 11.3 collective-permute-done.41
  548.2 8.7 collective-permute-done.47
  565.1 8.4 collective-permute-done.43
  575.5 6.4 collective-permute-done.49
  600.3 32.1 %experts_backward.4 = (bf16[4,512,1536]{2,1,0:T(8,128)(2,1)}, bf16[10,4,160,1536]{3,2,1,0:T(8,128)(2,1)}, bf16[10,4,160,1024]{3,2,1,0:T(8,128)(2,1)}, bf16[10,4,...) custom-call(s32[2]{0:T(128)S(1)} %get-tuple-element.598.at_ref, bf16[256,1536]{1,0:T(8,128)(2,1)S(1)} %get-tuple-element.535.tok_ref, ...), custom_call_target="tpu_custom_call" | custom-call | tf_op jit(solution)/shard_map/experts_backward/pallas_call | solution.py:628
  638.3 32.2 %experts_backward.5 = (bf16[4,512,1536]{2,1,0:T(8,128)(2,1)}, bf16[10,4,160,1536]{3,2,1,0:T(8,128)(2,1)}, bf16[10,4,160,1024]{3,2,1,0:T(8,128)(2,1)}, bf16[10,4,...) custom-call(s32[2]{0:T(128)S(1)} %get-tuple-element.599.at_ref, ...), custom_call_target="tpu_custom_call", output_to_operand_aliasing={{0}: (10, {}), {1}: (11, {}), {2}: (12, {}), {3}: (13, {})} | custom-call | tf_op jit(solution)/shard_map/experts_backward/pallas_call | solution.py:628
  677.5 32.2 %experts_backward.6 = (bf16[4,512,1536]{2,1,0:T(8,128)(2,1)}, bf16[10,4,160,1536]{3,2,1,0:T(8,128)(2,1)}, bf16[10,4,160,1024]{3,2,1,0:T(8,128)(2,1)}, bf16[10,4,...) custom-call(s32[2]{0:T(128)S(1)} %get-tuple-element.600.at_ref, ...), custom_call_target="tpu_custom_call", output_to_operand_aliasing={{0}: (10, {}), {1}: (11, {}), {2}: (12, {}), {3}: (13, {})} | custom-call | tf_op jit(solution)/shard_map/experts_backward/pallas_call | solution.py:628
  713.8 32.2 %experts_backward.7 = (bf16[4,512,1536]{2,1,0:T(8,128)(2,1)}, bf16[10,4,160,1536]{3,2,1,0:T(8,128)(2,1)}, bf16[10,4,160,1024]{3,2,1,0:T(8,128)(2,1)}, bf16[10,4,...) custom-call(s32[2]{0:T(128)S(1)} %get-tuple-element.597.at_ref, ...), custom_call_target="tpu_custom_call", output_to_operand_aliasing={{0}: (10, {}), {1}: (11, {}), {2}: (12, {}), {3}: (13, {})} | custom-call | tf_op jit(solution)/shard_map/experts_backward/pallas_call | solution.py:628
  749.2 12.4 %collective-permute-start.63 = (bf16[512,1536]{1,0:T(8,128)(2,1)}, bf16[512,1536]{1,0:T(8,128)(2,1)S(1)}, u32[]{:S(2)}, u32[]{:S(2)}) collective-permute-start(bf16[512,1536]{1,0:T(8,128)(2,1)} %get-tuple-element.487), channel_id=1, source_target_pairs={{0,1},{4,5},{8,9},{12,13},{16,17},{20,21},{24,25},{28,29}} | collective-permute-start | bytes 4718600 | tf_op jit(solution)/shard_map/ppermute | solution.py:134
  762.6 25.5 %weight_grads.2.refs_0_ = bf16[10,1536,1536]{2,1,0:T(8,128)(2,1)} custom-call(bf16[10,640,1536]{2,1,0:T(8,128)(2,1)} %bitcast.322, bf16[10,640,1024]{2,1,0:T(8,128)(2,1)} %bitcast.326, bf16[10,640,512]{2,1,0:T(8,128)(2,1)} %bitcast.328, bf16[10,640,1536]{2,1,0:T(8,128)(2,1)} %bitcast.324), custom_call_target="tpu_custom_call" | custom-call | tf_op jit(solution)/shard_map/weight_grads/pallas_call | solution.py:799
  798.4 25.4 %weight_grads.3 = bf16[10,1536,1536]{2,1,0:T(8,128)(2,1)} custom-call(bf16[10,640,1536]{2,1,0:T(8,128)(2,1)} %bitcast.323, bf16[10,640,1024]{2,1,0:T(8,128)(2,1)} %bitcast.327, bf16[10,640,512]{2,1,0:T(8,128)(2,1)} %bitcast.329, bf16[10,640,1536]{2,1,0:T(8,128)(2,1)} %bitcast.325, ...), custom_call_target="tpu_custom_call", output_to_operand_aliasing={{}: (4, {})} | custom-call | tf_op jit(solution)/shard_map/weight_grads/pallas_call | solution.py:799
  832.1 20.5 %collective-permute-done.67 = bf16[512,1536]{1,0:T(8,128)(2,1)} collective-permute-done((bf16[512,1536]{1,0:T(8,128)(2,1)S(1)}, bf16[512,1536]{1,0:T(8,128)(2,1)}, u32[]{:S(2)}, u32[]{:S(2)}) %collective-permute-start.67) | collective-permute-done | bytes 1572896 | tf_op jit(solution)/shard_map/ppermute | solution.py:134
  866.4 6.1 multiply_convert_fusion
  872.6 5.8 out_grads.1
  879.4 6.4 convolution_convert_fusion.2
  908.3 6.7 collective-permute-done.73.refs_3_
  916.5 16.5 %collective-permute-done.75.refs_5_ = bf16[384,512]{1,0:T(8,128)(2,1)S(1)} collective-permute-done((bf16[384,512]{1,0:T(8,128)(2,1)S(1)}, bf16[384,512]{1,0:T(8,128)(2,1)S(1)}, u32[]{:S(2)}, u32[]{:S(2)}) %collective-permute-start.75) | collective-permute-done | bytes 393248 | tf_op jit(solution)/shard_map/ppermute | solution.py:236
  958.4 55.9 %attention_backward.1 = (bf16[2,3,64,2048]{3,2,1,0:T(8,128)(2,1)S(1)}, bf16[2,64,2048]{2,1,0:T(8,128)(2,1)S(1)}, bf16[2,64,2048]{2,1,0:T(8,128)(2,1)S(1)}) custom-call(s32[1]{0:T(128)} %bitcast.58.me_ref, s32[1,2048]{1,0:T(1,128)S(1)} %bitcast.317, bf16[4,2,5,64,512]{4,3,2,1,0:T(8,128)(2,1)S(1)} %fusion.73.q_ref, bf16[2,2048,64]{2,1,0:T(8,128)(2,1)S(1)} %copy-done.2, ...), custom_call_target="tpu_custom_call" | custom-call | tf_op jit(solution)/shard_map/attention_backward/pallas_call | solution.py:456
  1022.7 7.1 convolution_convert_fusion
  1053.1 7.2 convolution_convert_fusion.1
  1067.5 10.8 collective-permute-done.86
  1088.3 5.7 collective-permute-start.89
  1106.7 10.5 collective-permute-start.94
  1125.2 10.5 collective-permute-start.96
  1144.5 10.1 collective-permute-done.96
  1160.0 9.6 collective-permute-start.98
  1204.4 6.4 collective-permute-done.105
  (696 shorter events, 479.1 us)
Async XLA Ops:
  7.2 351.7 %all-gather.2.cloned.1.call-start = ((), (), s32[]{:S(2)}) async-start(), calls=%async_computation.1 | async-start | bytes 53084160 | tf_op jit(solution)/shard_map/all_gather | solution.py:852
  16.5 1163.5 %reduce-scatter.2.cloned.1.call-start = ((), (), s32[]{:S(2)}) async-start(), calls=%async_computation.2 | async-start | bytes 53084160 | tf_op jit(solution)/shard_map/reduce_scatter | solution.py:1035
  35.6 58.8 %collective-permute-start.13 = (bf16[1,192,1536]{2,1,0:T(8,128)(2,1)}, bf16[1,192,1536]{2,1,0:T(8,128)(2,1)}, u32[]{:S(2)}, u32[]{:S(2)}) collective-permute-start(bf16[1,192,1536]{2,1,0:T(8,128)(2,1)} %bitcast.333), channel_id=1, source_target_pairs={{0,8},{4,12},{8,0},{12,4},{16,24},{20,28},{24,16},{28,20},{1,9},{5... | collective-permute-start | bytes 1769480 | tf_op jit(solution)/shard_map/ppermute | solution.py:241
  76.0 47.1 %collective-permute-start.8 = (bf16[4,192,768]{2,1,0:T(8,128)(2,1)}, bf16[4,192,768]{2,1,0:T(8,128)(2,1)}, u32[]{:S(2)}, u32[]{:S(2)}) collective-permute-start(bf16[4,192,768]{2,1,0:T(8,128)(2,1)} %pad_maximum_fusion.11), channel_id=1, source_target_pairs={{0,4},{4,0},{8,12},{12,8},{16,20},{20,16},{24,28},{28,24},{1,5},{5... | collective-permute-start | bytes 3538952 | tf_op jit(solution)/shard_map/ppermute | solution.py:241
  106.0 124.7 %collective-permute-start.16 = (bf16[2,192,1536]{2,1,0:T(8,128)(2,1)}, bf16[2,192,1536]{2,1,0:T(8,128)(2,1)}, u32[]{:S(2)}, u32[]{:S(2)}) collective-permute-start(bf16[2,192,1536]{2,1,0:T(8,128)(2,1)} %pad_maximum_fusion.12), channel_id=1, source_target_pairs={{0,16},{4,20},{8,24},{12,28},{16,0},{20,4},{24,8},{28,12},{1,17},{... | collective-permute-start | bytes 3538952 | tf_op jit(solution)/shard_map/ppermute | solution.py:241
  127.6 34.2 %collective-permute-start.15 = (bf16[272,1536]{1,0:T(8,128)(2,1)}, bf16[272,1536]{1,0:T(8,128)(2,1)}, u32[]{:S(2)}, u32[]{:S(2)}) collective-permute-start(bf16[272,1536]{1,0:T(8,128)(2,1)} %collective-permute-done.12), channel_id=1, source_target_pairs={{1,0},{5,4},{9,8},{13,12},{17,16},{21,20},{25,24},{29,28}} | collective-permute-start | bytes 2506760 | tf_op jit(solution)/shard_map/ppermute | solution.py:68
  235.1 32.4 %collective-permute-start.26 = (bf16[4,192,1536]{2,1,0:T(8,128)(2,1)}, bf16[4,192,1536]{2,1,0:T(8,128)(2,1)}, u32[]{:S(2)}, u32[]{:S(2)}) collective-permute-start(bf16[4,192,1536]{2,1,0:T(8,128)(2,1)} %pad_maximum_fusion.5), channel_id=1, source_target_pairs={{0,4},{4,0},{8,12},{12,8},{16,20},{20,16},{24,28},{28,24},{1,5},{5... | collective-permute-start | bytes 7077896 | tf_op jit(solution)/shard_map/ppermute | solution.py:241
  248.7 32.0 %collective-permute-start.18 = (bf16[384,512]{1,0:T(8,128)(2,1)}, bf16[384,512]{1,0:T(8,128)(2,1)}, u32[]{:S(2)}, u32[]{:S(2)}) collective-permute-start(bf16[384,512]{1,0:T(8,128)(2,1)} %get-tuple-element.546), channel_id=1, source_target_pairs={{0,2},{1,3},{4,6},{5,7},{8,10},{9,11},{12,14},{13,15},{16,18},{17,... | collective-permute-start | bytes 1179656 | tf_op jit(solution)/shard_map/ppermute | solution.py:235
  267.6 33.2 %collective-permute-start.21 = (bf16[384,512]{1,0:T(8,128)(2,1)}, bf16[384,512]{1,0:T(8,128)(2,1)}, u32[]{:S(2)}, u32[]{:S(2)}) collective-permute-start(bf16[384,512]{1,0:T(8,128)(2,1)} %get-tuple-element.543), channel_id=1, source_target_pairs={{2,0},{3,1},{6,4},{7,5},{10,8},{11,9},{14,12},{15,13},{18,16},{19,... | collective-permute-start | bytes 1179656 | tf_op jit(solution)/shard_map/ppermute | solution.py:236
  268.9 31.9 %collective-permute-start.22 = (bf16[384,512]{1,0:T(8,128)(2,1)}, bf16[384,512]{1,0:T(8,128)(2,1)}, u32[]{:S(2)}, u32[]{:S(2)}) collective-permute-start(bf16[384,512]{1,0:T(8,128)(2,1)} %get-tuple-element.542), channel_id=1, source_target_pairs={{3,0},{7,4},{11,8},{15,12},{19,16},{23,20},{27,24},{31,28}} | collective-permute-start | bytes 1179656 | tf_op jit(solution)/shard_map/ppermute | solution.py:236
  321.6 31.7 %collective-permute-start.32 = (bf16[256,1536]{1,0:T(8,128)(2,1)S(1)}, bf16[256,1536]{1,0:T(8,128)(2,1)}, u32[]{:S(2)}, u32[]{:S(2)}) collective-permute-start(bf16[256,1536]{1,0:T(8,128)(2,1)S(1)} %get-tuple-element.540.more_ref), channel_id=1, source_target_pairs={{1,0},{2,1},{3,2},{5,4},{6,5},{7,6},{9,8},{10,9},{11,10},{13,12},{... | collective-permute-start | bytes 2359304 | tf_op jit(solution)/shard_map/ppermute | solution.py:68
  336.5 50.9 %collective-permute-start.29 = (bf16[256,1536]{1,0:T(8,128)(2,1)}, bf16[256,1536]{1,0:T(8,128)(2,1)}, u32[]{:S(2)}, u32[]{:S(2)}) collective-permute-start(bf16[256,1536]{1,0:T(8,128)(2,1)} %collective-permute-done.27), channel_id=1, source_target_pairs={{1,2},{2,3},{5,6},{6,7},{9,10},{10,11},{13,14},{14,15},{17,18},{18... | collective-permute-start | bytes 2359304 | tf_op jit(solution)/shard_map/ppermute | solution.py:67
  338.1 49.4 %collective-permute-start.30 = (bf16[256,1536]{1,0:T(8,128)(2,1)}, bf16[256,1536]{1,0:T(8,128)(2,1)}, u32[]{:S(2)}, u32[]{:S(2)}) collective-permute-start(bf16[256,1536]{1,0:T(8,128)(2,1)} %collective-permute-done.28), channel_id=1, source_target_pairs={{1,0},{2,1},{5,4},{6,5},{9,8},{10,9},{13,12},{14,13},{17,16},{18,1... | collective-permute-start | bytes 2359304 | tf_op jit(solution)/shard_map/ppermute | solution.py:68
  353.4 36.1 %collective-permute-start.35 = (bf16[256,1536]{1,0:T(8,128)(2,1)}, bf16[256,1536]{1,0:T(8,128)(2,1)}, u32[]{:S(2)}, u32[]{:S(2)}) collective-permute-start(bf16[256,1536]{1,0:T(8,128)(2,1)} %collective-permute-done.31), channel_id=1, source_target_pairs={{1,2},{2,3},{5,6},{6,7},{9,10},{10,11},{13,14},{14,15},{17,18},{18... | collective-permute-start | bytes 2359304 | tf_op jit(solution)/shard_map/ppermute | solution.py:67
  354.9 34.6 %collective-permute-start.36 = (bf16[256,1536]{1,0:T(8,128)(2,1)}, bf16[256,1536]{1,0:T(8,128)(2,1)}, u32[]{:S(2)}, u32[]{:S(2)}) collective-permute-start(bf16[256,1536]{1,0:T(8,128)(2,1)} %collective-permute-done.32), channel_id=1, source_target_pairs={{1,0},{2,1},{5,4},{6,5},{9,8},{10,9},{13,12},{14,13},{17,16},{18,1... | collective-permute-start | bytes 2359304 | tf_op jit(solution)/shard_map/ppermute | solution.py:68
  387.5 33.1 %collective-permute-start.33 = (bf16[256,1536]{1,0:T(8,128)(2,1)}, bf16[256,1536]{1,0:T(8,128)(2,1)S(1)}, u32[]{:S(2)}, u32[]{:S(2)}) collective-permute-start(bf16[256,1536]{1,0:T(8,128)(2,1)} %collective-permute-done.29), channel_id=1, source_target_pairs={{2,3},{6,7},{10,11},{14,15},{18,19},{22,23},{26,27},{30,31}} | collective-permute-start | bytes 2359304 | tf_op jit(solution)/shard_map/ppermute | solution.py:67
  388.2 32.4 %collective-permute-start.34 = (bf16[256,1536]{1,0:T(8,128)(2,1)}, bf16[256,1536]{1,0:T(8,128)(2,1)S(1)}, u32[]{:S(2)}, u32[]{:S(2)}) collective-permute-start(bf16[256,1536]{1,0:T(8,128)(2,1)} %collective-permute-done.30), channel_id=1, source_target_pairs={{1,0},{5,4},{9,8},{13,12},{17,16},{21,20},{25,24},{29,28}} | collective-permute-start | bytes 2359304 | tf_op jit(solution)/shard_map/ppermute | solution.py:68
  489.3 33.9 %collective-permute-start.45 = (bf16[256,1536]{1,0:T(8,128)(2,1)S(1)}, bf16[256,1536]{1,0:T(8,128)(2,1)S(1)}, u32[]{:S(2)}, u32[]{:S(2)}) collective-permute-start(bf16[256,1536]{1,0:T(8,128)(2,1)S(1)} %get-tuple-element.519), channel_id=1, source_target_pairs={{0,1},{4,5},{8,9},{12,13},{16,17},{20,21},{24,25},{28,29}} | collective-permute-start | bytes 2359304 | tf_op jit(solution)/shard_map/ppermute | solution.py:134
  490.6 32.6 %collective-permute-start.46 = (bf16[256,1536]{1,0:T(8,128)(2,1)S(1)}, bf16[256,1536]{1,0:T(8,128)(2,1)S(1)}, u32[]{:S(2)}, u32[]{:S(2)}) collective-permute-start(bf16[256,1536]{1,0:T(8,128)(2,1)S(1)} %get-tuple-element.518), channel_id=1, source_target_pairs={{3,2},{7,6},{11,10},{15,14},{19,18},{23,22},{27,26},{31,30}} | collective-permute-start | bytes 2359304 | tf_op jit(solution)/shard_map/ppermute | solution.py:135
  506.8 33.3 %collective-permute-start.41 = (bf16[256,1536]{1,0:T(8,128)(2,1)S(1)}, bf16[256,1536]{1,0:T(8,128)(2,1)S(1)}, u32[]{:S(2)}, u32[]{:S(2)}) collective-permute-start(bf16[256,1536]{1,0:T(8,128)(2,1)S(1)} %get-tuple-element.515), channel_id=1, source_target_pairs={{0,1},{1,2},{4,5},{5,6},{8,9},{9,10},{12,13},{13,14},{16,17},{17,1... | collective-permute-start | bytes 2359304 | tf_op jit(solution)/shard_map/ppermute | solution.py:134
  523.6 33.3 %collective-permute-start.47 = (bf16[256,1536]{1,0:T(8,128)(2,1)S(1)}, bf16[256,1536]{1,0:T(8,128)(2,1)S(1)}, u32[]{:S(2)}, u32[]{:S(2)}) collective-permute-start(bf16[256,1536]{1,0:T(8,128)(2,1)S(1)} %get-tuple-element.513), channel_id=1, source_target_pairs={{0,1},{1,2},{4,5},{5,6},{8,9},{9,10},{12,13},{13,14},{16,17},{17,1... | collective-permute-start | bytes 2359304 | tf_op jit(solution)/shard_map/ppermute | solution.py:134
  541.7 31.8 %collective-permute-start.43 = (bf16[256,1536]{1,0:T(8,128)(2,1)}, bf16[256,1536]{1,0:T(8,128)(2,1)}, u32[]{:S(2)}, u32[]{:S(2)}) collective-permute-start(bf16[256,1536]{1,0:T(8,128)(2,1)} %get-tuple-element.511), channel_id=1, source_target_pairs={{0,1},{1,2},{2,3},{4,5},{5,6},{6,7},{8,9},{9,10},{10,11},{12,13},{... | collective-permute-start | bytes 2359304 | tf_op jit(solution)/shard_map/ppermute | solution.py:134
  588.3 46.1 %collective-permute-start.55 = (bf16[272,1536]{1,0:T(8,128)(2,1)S(1)}, bf16[272,1536]{1,0:T(8,128)(2,1)S(1)}, u32[]{:S(2)}, u32[]{:S(2)}) collective-permute-start(bf16[272,1536]{1,0:T(8,128)(2,1)S(1)} %fusion.69.more_ref), channel_id=1, source_target_pairs={{0,1},{1,2},{2,3},{4,5},{5,6},{6,7},{8,9},{9,10},{10,11},{12,13},{... | collective-permute-start | bytes 2506760 | tf_op jit(solution)/shard_map/ppermute | solution.py:67
  592.8 41.7 %collective-permute-start.56 = (bf16[272,1536]{1,0:T(8,128)(2,1)S(1)}, bf16[272,1536]{1,0:T(8,128)(2,1)S(1)}, u32[]{:S(2)}, u32[]{:S(2)}) collective-permute-start(bf16[272,1536]{1,0:T(8,128)(2,1)S(1)} %fusion.69.more_ref), channel_id=1, source_target_pairs={{1,0},{2,1},{3,2},{5,4},{6,5},{7,6},{9,8},{10,9},{11,10},{13,12},{... | collective-permute-start | bytes 2506760 | tf_op jit(solution)/shard_map/ppermute | solution.py:68
  594.1 38.4 %collective-permute-start.51 = (bf16[256,1536]{1,0:T(8,128)(2,1)S(1)}, bf16[256,1536]{1,0:T(8,128)(2,1)S(1)}, u32[]{:S(2)}, u32[]{:S(2)}) collective-permute-start(bf16[256,1536]{1,0:T(8,128)(2,1)S(1)} %get-tuple-element.535.tok_ref), channel_id=1, source_target_pairs={{0,1},{1,2},{2,3},{4,5},{5,6},{6,7},{8,9},{9,10},{10,11},{12,13},{... | collective-permute-start | bytes 2359304 | tf_op jit(solution)/shard_map/ppermute | solution.py:67
  599.0 33.5 %collective-permute-start.52 = (bf16[256,1536]{1,0:T(8,128)(2,1)S(1)}, bf16[256,1536]{1,0:T(8,128)(2,1)S(1)}, u32[]{:S(2)}, u32[]{:S(2)}) collective-permute-start(bf16[256,1536]{1,0:T(8,128)(2,1)S(1)} %get-tuple-element.535.tok_ref), channel_id=1, source_target_pairs={{1,0},{2,1},{3,2},{5,4},{6,5},{7,6},{9,8},{10,9},{11,10},{13,12},{... | collective-permute-start | bytes 2359304 | tf_op jit(solution)/shard_map/ppermute | solution.py:68
  632.5 38.0 %collective-permute-start.53 = (bf16[256,1536]{1,0:T(8,128)(2,1)S(1)}, bf16[256,1536]{1,0:T(8,128)(2,1)S(1)}, u32[]{:S(2)}, u32[]{:S(2)}) collective-permute-start(bf16[256,1536]{1,0:T(8,128)(2,1)S(1)} %collective-permute-done.51), channel_id=1, source_target_pairs={{1,2},{2,3},{5,6},{6,7},{9,10},{10,11},{13,14},{14,15},{17,18},{18... | collective-permute-start | bytes 2359304 | tf_op jit(solution)/shard_map/ppermute | solution.py:67
  633.2 37.3 %collective-permute-start.54 = (bf16[256,1536]{1,0:T(8,128)(2,1)S(1)}, bf16[256,1536]{1,0:T(8,128)(2,1)S(1)}, u32[]{:S(2)}, u32[]{:S(2)}) collective-permute-start(bf16[256,1536]{1,0:T(8,128)(2,1)S(1)} %collective-permute-done.52), channel_id=1, source_target_pairs={{1,0},{2,1},{5,4},{6,5},{9,8},{10,9},{13,12},{14,13},{17,16},{18,1... | collective-permute-start | bytes 2359304 | tf_op jit(solution)/shard_map/ppermute | solution.py:68
  634.5 38.0 %collective-permute-start.59 = (bf16[272,1536]{1,0:T(8,128)(2,1)S(1)}, bf16[272,1536]{1,0:T(8,128)(2,1)S(1)}, u32[]{:S(2)}, u32[]{:S(2)}) collective-permute-start(bf16[272,1536]{1,0:T(8,128)(2,1)S(1)} %collective-permute-done.55), channel_id=1, source_target_pairs={{1,2},{2,3},{5,6},{6,7},{9,10},{10,11},{13,14},{14,15},{17,18},{18... | collective-permute-start | bytes 2506760 | tf_op jit(solution)/shard_map/ppermute | solution.py:67
  635.2 37.3 %collective-permute-start.60 = (bf16[272,1536]{1,0:T(8,128)(2,1)S(1)}, bf16[272,1536]{1,0:T(8,128)(2,1)S(1)}, u32[]{:S(2)}, u32[]{:S(2)}) collective-permute-start(bf16[272,1536]{1,0:T(8,128)(2,1)S(1)} %collective-permute-done.56), channel_id=1, source_target_pairs={{1,0},{2,1},{5,4},{6,5},{9,8},{10,9},{13,12},{14,13},{17,16},{18,1... | collective-permute-start | bytes 2506760 | tf_op jit(solution)/shard_map/ppermute | solution.py:68
  670.5 39.2 %collective-permute-start.57 = (bf16[256,1536]{1,0:T(8,128)(2,1)S(1)}, bf16[256,1536]{1,0:T(8,128)(2,1)S(1)}, u32[]{:S(2)}, u32[]{:S(2)}) collective-permute-start(bf16[256,1536]{1,0:T(8,128)(2,1)S(1)} %collective-permute-done.53), channel_id=1, source_target_pairs={{2,3},{6,7},{10,11},{14,15},{18,19},{22,23},{26,27},{30,31}} | collective-permute-start | bytes 2359304 | tf_op jit(solution)/shard_map/ppermute | solution.py:67
  671.2 38.4 %collective-permute-start.58 = (bf16[256,1536]{1,0:T(8,128)(2,1)S(1)}, bf16[256,1536]{1,0:T(8,128)(2,1)S(1)}, u32[]{:S(2)}, u32[]{:S(2)}) collective-permute-start(bf16[256,1536]{1,0:T(8,128)(2,1)S(1)} %collective-permute-done.54), channel_id=1, source_target_pairs={{1,0},{5,4},{9,8},{13,12},{17,16},{21,20},{25,24},{29,28}} | collective-permute-start | bytes 2359304 | tf_op jit(solution)/shard_map/ppermute | solution.py:68
  672.6 37.1 %collective-permute-start.61 = (bf16[272,1536]{1,0:T(8,128)(2,1)S(1)}, bf16[272,1536]{1,0:T(8,128)(2,1)S(1)}, u32[]{:S(2)}, u32[]{:S(2)}) collective-permute-start(bf16[272,1536]{1,0:T(8,128)(2,1)S(1)} %collective-permute-done.59), channel_id=1, source_target_pairs={{2,3},{6,7},{10,11},{14,15},{18,19},{22,23},{26,27},{30,31}} | collective-permute-start | bytes 2506760 | tf_op jit(solution)/shard_map/ppermute | solution.py:67
  673.3 36.4 %collective-permute-start.62 = (bf16[272,1536]{1,0:T(8,128)(2,1)S(1)}, bf16[272,1536]{1,0:T(8,128)(2,1)S(1)}, u32[]{:S(2)}, u32[]{:S(2)}) collective-permute-start(bf16[272,1536]{1,0:T(8,128)(2,1)S(1)} %collective-permute-done.60), channel_id=1, source_target_pairs={{1,0},{5,4},{9,8},{13,12},{17,16},{21,20},{25,24},{29,28}} | collective-permute-start | bytes 2506760 | tf_op jit(solution)/shard_map/ppermute | solution.py:68
  749.2 38.9 %collective-permute-start.63 = (bf16[512,1536]{1,0:T(8,128)(2,1)}, bf16[512,1536]{1,0:T(8,128)(2,1)S(1)}, u32[]{:S(2)}, u32[]{:S(2)}) collective-permute-start(bf16[512,1536]{1,0:T(8,128)(2,1)} %get-tuple-element.487), channel_id=1, source_target_pairs={{0,1},{4,5},{8,9},{12,13},{16,17},{20,21},{24,25},{28,29}} | collective-permute-start | bytes 4718600 | tf_op jit(solution)/shard_map/ppermute | solution.py:134
  792.5 31.2 %collective-permute-start.65 = (bf16[512,1536]{1,0:T(8,128)(2,1)}, bf16[512,1536]{1,0:T(8,128)(2,1)}, u32[]{:S(2)}, u32[]{:S(2)}) collective-permute-start(bf16[512,1536]{1,0:T(8,128)(2,1)} %get-tuple-element.485), channel_id=1, source_target_pairs={{0,1},{1,2},{4,5},{5,6},{8,9},{9,10},{12,13},{13,14},{16,17},{17,1... | collective-permute-start | bytes 4718600 | tf_op jit(solution)/shard_map/ppermute | solution.py:134
  857.2 40.7 %collective-permute-start.77 = (f32[1,1]{1,0:T(1,128)}, f32[1,1]{1,0:T(1,128)}, u32[]{:S(2)}, u32[]{:S(2)}) collective-permute-start(f32[1,1]{1,0:T(1,128)} %bitcast.88), channel_id=1, source_target_pairs={{0,1},{1,0},{2,3},{3,2},{4,5},{5,4},{6,7},{7,6},{8,9},{9,8},{10,11... | collective-permute-start | bytes 20 | tf_op jit(solution)/shard_map/ppermute | solution.py:241
  898.0 35.0 %collective-permute-start.75 = (bf16[384,512]{1,0:T(8,128)(2,1)S(1)}, bf16[384,512]{1,0:T(8,128)(2,1)S(1)}, u32[]{:S(2)}, u32[]{:S(2)}) collective-permute-start(bf16[384,512]{1,0:T(8,128)(2,1)S(1)} %get-tuple-element.528), channel_id=1, source_target_pairs={{2,0},{3,1},{6,4},{7,5},{10,8},{11,9},{14,12},{15,13},{18,16},{19,... | collective-permute-start | bytes 1179656 | tf_op jit(solution)/shard_map/ppermute | solution.py:236
  899.3 34.4 %collective-permute-start.76 = (bf16[384,512]{1,0:T(8,128)(2,1)S(1)}, bf16[384,512]{1,0:T(8,128)(2,1)S(1)}, u32[]{:S(2)}, u32[]{:S(2)}) collective-permute-start(bf16[384,512]{1,0:T(8,128)(2,1)S(1)} %get-tuple-element.527), channel_id=1, source_target_pairs={{3,0},{7,4},{11,8},{15,12},{19,16},{23,20},{27,24},{31,28}} | collective-permute-start | bytes 1179656 | tf_op jit(solution)/shard_map/ppermute | solution.py:236
  934.5 79.9 %collective-permute-start.78 = (bf16[2,192,768]{2,1,0:T(8,128)(2,1)}, bf16[2,192,768]{2,1,0:T(8,128)(2,1)}, u32[]{:S(2)}, u32[]{:S(2)}) collective-permute-start(bf16[2,192,768]{2,1,0:T(8,128)(2,1)} %add_convert_fusion.3), channel_id=1, source_target_pairs={{0,8},{4,12},{8,0},{12,4},{16,24},{20,28},{24,16},{28,20},{1,9},{5... | collective-permute-start | bytes 1769480 | tf_op jit(solution)/shard_map/ppermute | solution.py:241
  935.5 78.9 %collective-permute-start.79 = (bf16[2,192,768]{2,1,0:T(8,128)(2,1)}, bf16[2,192,768]{2,1,0:T(8,128)(2,1)}, u32[]{:S(2)}, u32[]{:S(2)}) collective-permute-start(bf16[2,192,768]{2,1,0:T(8,128)(2,1)} %add_convert_fusion.2), channel_id=1, source_target_pairs={{0,16},{4,20},{8,24},{12,28},{16,0},{20,4},{24,8},{28,12},{1,17},{... | collective-permute-start | bytes 1769480 | tf_op jit(solution)/shard_map/ppermute | solution.py:241
  941.8 72.5 %collective-permute-start.80 = (f32[1,1]{1,0:T(1,128)}, f32[1,1]{1,0:T(1,128)}, u32[]{:S(2)}, u32[]{:S(2)}) collective-permute-start(f32[1,1]{1,0:T(1,128)} %add.757), channel_id=1, source_target_pairs={{0,2},{1,3},{2,0},{3,1},{4,6},{5,7},{6,4},{7,5},{8,10},{9,11},{10,... | collective-permute-start | bytes 20 | tf_op jit(solution)/shard_map/ppermute | solution.py:241
  1042.9 43.7 %collective-permute-start.84 = (bf16[304,1536]{1,0:T(8,128)(2,1)}, bf16[304,1536]{1,0:T(8,128)(2,1)S(1)}, u32[]{:S(2)}, u32[]{:S(2)}) collective-permute-start(bf16[304,1536]{1,0:T(8,128)(2,1)} %get-tuple-element.501), channel_id=1, source_target_pairs={{0,1},{4,5},{8,9},{12,13},{16,17},{20,21},{24,25},{28,29}} | collective-permute-start | bytes 2801672 | tf_op jit(solution)/shard_map/ppermute | solution.py:134
  1044.5 42.2 %collective-permute-start.85 = (bf16[304,1536]{1,0:T(8,128)(2,1)}, bf16[304,1536]{1,0:T(8,128)(2,1)}, u32[]{:S(2)}, u32[]{:S(2)}) collective-permute-start(bf16[304,1536]{1,0:T(8,128)(2,1)} %get-tuple-element.500), channel_id=1, source_target_pairs={{3,2},{7,6},{11,10},{15,14},{19,18},{23,22},{27,26},{31,30}} | collective-permute-start | bytes 2801672 | tf_op jit(solution)/shard_map/ppermute | solution.py:135
  1088.3 35.5 %collective-permute-start.89 = (bf16[304,1536]{1,0:T(8,128)(2,1)S(1)}, bf16[304,1536]{1,0:T(8,128)(2,1)S(1)}, u32[]{:S(2)}, u32[]{:S(2)}) collective-permute-start(bf16[304,1536]{1,0:T(8,128)(2,1)S(1)} %get-tuple-element.499), channel_id=1, source_target_pairs={{0,1},{1,2},{4,5},{5,6},{8,9},{9,10},{12,13},{13,14},{16,17},{17,1... | collective-permute-start | bytes 2801672 | tf_op jit(solution)/shard_map/ppermute | solution.py:134
  1096.6 41.1 %collective-permute-start.88 = (bf16[2,192,681]{2,1,0:T(8,128)(2,1)S(1)}, bf16[2,192,681]{2,1,0:T(8,128)(2,1)}, u32[]{:S(2)}, u32[]{:S(2)}) collective-permute-start(bf16[2,192,681]{2,1,0:T(8,128)(2,1)S(1)} %add_convert_fusion.1), channel_id=1, source_target_pairs={{0,8},{4,12},{8,0},{12,4},{16,24},{20,28},{24,16},{28,20},{1,9},{5... | collective-permute-start | bytes 1569032 | tf_op jit(solution)/shard_map/ppermute | solution.py:241
  1106.7 34.1 %collective-permute-start.94 = (bf16[256,1536]{1,0:T(8,128)(2,1)}, bf16[256,1536]{1,0:T(8,128)(2,1)}, u32[]{:S(2)}, u32[]{:S(2)}) collective-permute-start(bf16[256,1536]{1,0:T(8,128)(2,1)} %get-tuple-element.503), channel_id=1, source_target_pairs={{0,1},{1,2},{2,3},{4,5},{5,6},{6,7},{8,9},{9,10},{10,11},{12,13},{... | collective-permute-start | bytes 2359304 | tf_op jit(solution)/shard_map/ppermute | solution.py:134
  1137.6 45.4 %collective-permute-start.100 = (f32[1,1]{1,0:T(1,128)}, f32[1,1]{1,0:T(1,128)}, u32[]{:S(2)}, u32[]{:S(2)}) collective-permute-start(f32[1,1]{1,0:T(1,128)} %add.758), channel_id=1, source_target_pairs={{0,4},{4,0},{8,12},{12,8},{16,20},{20,16},{24,28},{28,24},{1,5},{5... | collective-permute-start | bytes 20 | tf_op jit(solution)/shard_map/ppermute | solution.py:241
  (207 other events, 4113.8 us)
Sparse Core Ops, SparseCore 0:
  16.5 251.9 all-gather.1
  856.8 302.6 reduce-scatter.1

commit v11 on v10

--- a/solution.py
+++ b/solution.py
@@ -136,29 +136,6 @@
     )
 
 
-class Doubling:
-    def __init__(self, block, bits):
-        self.blocks, self.order, self.bits = block[None], bits, list(bits)
-        self.away = self.late = False
-
-    def go(self):
-        self.here, self.away = swap(self.blocks, "fsdp", self.bits.pop(0)), True
-
-    def land(self, other):
-        other, here = tie(other, self.here)
-        self.blocks, self.away = jnp.concatenate([self.blocks, here]), False
-        return other
-
-    def rows(self):
-        while self.bits or self.away:
-            if not self.away:
-                self.go()
-            self.land(())
-        mask = lax.axis_index("fsdp") ^ jnp.arange(self.blocks.shape[0])
-        spot = sum(((mask // bit) % 2) << i for i, bit in enumerate(self.order))
-        return self.blocks[spot].reshape(-1, self.blocks.shape[2])
-
-
 class LineGather:
     def __init__(self, halves):
         self.rights, self.lefts = [[half] for half in halves], [[half] for half in halves]
@@ -172,11 +149,6 @@
 
     def land(self, h, other):
         spot = self.landed[h] = len(self.rights[h]) - 1
-        if isinstance(other, Doubling):
-            (self.rights[h][spot], self.lefts[h][spot]) = other.land(
-                (self.rights[h][spot], self.lefts[h][spot])
-            )
-            other = ()
         moved = [(self.rights[part][spot], self.lefts[part][spot]) for part in range(h + 1)]
         moved, other = tie(moved, other)
         for part, (right, left) in enumerate(moved):
@@ -389,7 +361,7 @@
             jax.ShapeDtypeStruct((kv_here, GROUP, HEAD_DIM, seq_len), full),
             jax.ShapeDtypeStruct((kv_here, GROUP, 1, seq_len), full),
         ],
-        compiler_params=vmem(40),
+        compiler_params=vmem(60),
         name="attention_forward",
     )(limit, heads, k_rows, vt)
 
@@ -488,7 +460,7 @@
             jax.ShapeDtypeStruct((kv_here, HEAD_DIM, seq_len), low),
             jax.ShapeDtypeStruct((kv_here, HEAD_DIM, seq_len), low),
         ],
-        compiler_params=vmem(40),
+        compiler_params=vmem(60),
         name="attention_backward",
     )(me, limit, heads, k_rows, v_rows, kt, out, lse, *blocks)
 
@@ -845,6 +817,22 @@
     order = jnp.array(arrival_order(n), jnp.int32)[me]
     x_low = inputs.reshape(shard_len, width)
 
+    own_qkv = lax.dynamic_slice_in_dim(w_qkv, me * group_w, group_w, 1)
+    small = jnp.concatenate([gain_one[:, None], gain_two[:, None], w_router], axis=1)
+    small = jnp.pad(small, ((0, 0), (0, -small.shape[1] % 128)))
+    first = lax.all_gather(
+        jnp.concatenate([own_qkv, small, w_out], axis=1), "fsdp", axis=0, tiled=True
+    )
+    full_qkv = first[:, :group_w]
+    small = first[:, group_w : group_w + 2 + expert_total]
+    full_out = first[:, -width:]
+    full_g1 = small[:, 0].astype(full)
+    full_g2 = small[:, 1].astype(full)
+    router = small[:, 2:].T
+    own_router = lax.dynamic_slice_in_dim(router, me * experts_here, experts_here, 0)
+    own_router = jnp.pad(own_router, ((0, -experts_here % 16), (0, 0)))
+    valid_rows = valid_mask.reshape(shard_len).astype(full)
+
     hidden_w = w_gate.shape[2]
     down_chunks = [
         w_down[:, :, start : start + hidden_w] for start in range(0, width, hidden_w)
@@ -856,14 +844,6 @@
         tiled=True,
     )
 
-    own_qkv = lax.dynamic_slice_in_dim(w_qkv, me * group_w, group_w, 1)
-    small = jnp.concatenate([gain_one[:, None], gain_two[:, None], w_router], axis=1)
-    small = jnp.pad(small, ((0, 0), (0, -small.shape[1] % 128)))
-    plane_first = order_a[1:] + order_a[:1]
-    first = Doubling(jnp.concatenate([own_qkv, small], axis=1), plane_first)
-    out = Doubling(w_out, plane_first)
-    valid_rows = valid_mask.reshape(shard_len).astype(full)
-
     routes_low = jnp.concatenate([routes.reshape(shard_len, top_count).T, valid_mask], axis=0)
     routes_low = jnp.pad(
         routes_low.astype(low), ((0, -routes_low.shape[0] % 16), (0, width - shard_len))
@@ -877,36 +857,18 @@
     heads = jnp.zeros((n, kv_here, GROUP + 2, HEAD_DIM, shard_len), low)
     routes_all = []
     line = LineGather(halves)
-    line.go(0)
-    line.go(1)
-    first.go()
-    x_blocks = [line.block(0)]
-    for turn in range(1, n):
-        for h in (0, 1):
-            if first.away:
-                line.land(h, first)
-                (first if first.bits else out).go()
-            elif out.away and not out.late:
-                line.land(h, out)
-                out.go()
-                out.late = True
-            else:
-                line.land(h, ())
+    for turn in range(n):
+        if turn:
+            line.land(0, heads if turn > 1 else ())
             if turn < n - 1:
-                line.go(h)
-        x_blocks.append(line.block(turn))
-    first = first.rows()
-    full_qkv = first[:, :group_w]
-    small = first[:, group_w : group_w + 2 + expert_total]
-    full_g1 = small[:, 0].astype(full)
-    full_g2 = small[:, 1].astype(full)
-    router = small[:, 2:].T
-    own_router = lax.dynamic_slice_in_dim(router, me * experts_here, experts_here, 0)
-    own_router = jnp.pad(own_router, ((0, -experts_here % 16), (0, 0)))
-    for turn in range(n):
-        if turn == n - 1:
-            x_blocks[turn], heads, normed_one = tie(x_blocks[turn], heads, normed_one)
-        block = jnp.concatenate(x_blocks[turn])
+                line.go(0)
+            line.land(1, ())
+            if turn < n - 1:
+                line.go(1)
+        else:
+            line.go(0)
+            line.go(1)
+        block = jnp.concatenate(line.block(turn))
         start = order[turn] * shard_len
         normed = rms_norm(block[:shard_len].astype(full), full_g1).astype(low)
         projected = dot("td,dc->ct", normed, full_qkv)
@@ -943,13 +905,8 @@
     key_rows = jnp.swapaxes(key, 1, 2)
     value_rows = jnp.swapaxes(value, 1, 2)
     attended, out_heads, lse = attention_forward(heads, key_rows, value, limit)
-    if out.away:
-        attended = out.land(attended)
     moved = exchange(attended)
-    full_out = out.rows()
-    moved, slot_of, member, own_router, valid_count, full_out = tie(
-        moved, slot_of, member, own_router, valid_count, full_out
-    )
+    moved, slot_of, member, own_router = tie(moved, slot_of, member, own_router)
     attn_rows = by_place(nearest(*moved)).reshape(HEADS * HEAD_DIM, shard_len)
     projected = dot("kt,kd->td", attn_rows, full_out)
     hidden = x_low.astype(full) + resid_mult * projected
@@ -1054,7 +1011,10 @@
             (shard[1], shard_logits[:experts_here, middle:]),
         )
     )
-    moved, router_part, squares = leave(out_sums, moved, router_part, squares)
+    own_columns = jnp.zeros((width, expert_total), full)
+    own_columns = lax.dynamic_update_slice_in_dim(own_columns, router_part, me * experts_here, 1)
+    own_columns = jnp.concatenate([own_columns, gain_two_part[:, None]], axis=1).astype(low)
+    moved, own_columns, squares = leave(out_sums, moved, own_columns, squares)
     squares = loss_steps.send(squares)
     for each in out_sums:
         each.go()
@@ -1072,8 +1032,6 @@
     d_turned = rotate(d_turned, cosine, -sine_vals).astype(low)
     d_qkv = jnp.concatenate([d_turned, value_grad[:, None]], axis=1).reshape(group_w, seq_len)
     d_parts = dot("ct,dc->td", d_qkv, full_qkv).astype(low).reshape(n, shard_len, width)
-    own_columns = jnp.zeros((width, expert_total), full)
-    own_columns = lax.dynamic_update_slice_in_dim(own_columns, router_part, me * experts_here, 1)
     (d_parts,) = land(out_sums, d_parts)
     for each in out_sums:
         each.add()
@@ -1090,8 +1048,8 @@
     def first_work(before, _):
         rows, _ = tie(d_qkv, before)
         qkv_part = jnp.concatenate(
-            [dot("td,ct->dc", normed_one, rows), own_columns, gain_two_part[:, None]], axis=1
-        ).astype(low)
+            [dot("td,ct->dc", normed_one, rows).astype(low), own_columns], axis=1
+        )
         sums["qkv"] = rows_halving(qkv_part, order_a)
         sums["qkv"].go()
         return sums["qkv"].send
@@ -1132,15 +1090,14 @@
         squares = loss_steps.send(squares)
         rights.append(right)
         lefts.append(left)
-    blocks = nearest(rights, lefts)
     input_grad, gate_up_grad, down_grad = done
     gate_grad, up_grad = gate_up_grad[:, :, :hidden_w], gate_up_grad[:, :, hidden_w:]
     qkv_grad = jnp.zeros((w_qkv.shape[0], QKV_W), full)
     out_grad = jnp.zeros((w_out.shape[0], width), full)
     rest = 0.0
-    for k, block in enumerate(blocks):
-        block = block.astype(full)
-        place = (me - k) % n
+    for turn in range(n):
+        block = arrived(rights, lefts, turn).astype(full)
+        place = order[turn]
         qkv_grad = lax.dynamic_update_slice_in_dim(
             qkv_grad, block[:, :group_w], place * group_w, 1
         )

time: 1240 us -> 1170 us (0.944)
  local copies, waits for them, and re-layouts: 114 us -> 79.1 us
  waiting for transfers between devices: 279 us -> 249 us
    ppermute x15, waiting for transfers between devices: 114 us -> 96.5 us  [line_pass(): lax.ppermute(to_right, 'seq', [(i, i + 1) for i in range(n - k)])]
    ppermute x6, waiting for transfers between devices: 11.4 us -> 27.8 us  [exchange(): lax.ppermute(to_right, 'seq', [(i, i + k) for i in range(n - k)])]
    concatenate x7 -> x3, other arithmetic: 19.1 us -> 4.19 us  [the longest x1 2.04 us: shards(): jnp.concatenate([own_qkv, small, w_out], axis=1)]
    unnamed x295 -> x251, local copies, waits for them, and re-layouts: 34.9 us -> 22.3 us
    ppermute x23 -> x17, starting transfers between devices: 30.5 us -> 20.2 us  [swap(): lax.ppermute(value, axis, [(i, i ^ bit) for i in range(lax.axis_size(axis...]
    select_n x11 -> x16, other arithmetic: 30.3 us -> 35.1 us  [arrived(): block = jnp.where(mine, moved, block)]
  transfers between devices with their start and end apart: 109 -> 104, of which waited for: 36 -> 38; matrix products, arithmetic and copies ran while one was open for 17% -> 16% of each run, Pallas kernels for 24% -> 26%
where the time goes in v11:
time: 1170 us; the launch traced here: 1160 us
  Pallas kernels  386 us (33%)
  waiting for transfers between devices  249 us (21%)
  starting transfers between devices  234 us (20%)
  other arithmetic  139 us (12%)
  local copies, waits for them, and re-layouts  79.1 us (7%)
  between operations  39.7 us (3%)
  matrix products  38.5 us (3%)
    pallas_call x8, Pallas kernels, shard_call(): pl.pallas_call(kernel, grid_spec=pltpu.PrefetchScalarGridSpec(num_scalar_...  230 us
    ppermute x15, waiting for transfers between devices, line_pass(): lax.ppermute(to_right, 'seq', [(i, i + 1) for i in range(n - k)])  96.5 us
    ppermute x15, starting transfers between devices, line_pass(): lax.ppermute(to_right, 'seq', [(i, i + 1) for i in range(n - k)])  89.5 us
    ppermute x21, waiting for transfers between devices, line_move(): lax.ppermute(left, 'seq', [(i, i - 1) for i in range(1, n - k + 1)])  59.9 us
    pallas_call x1, Pallas kernels, attention_backward(): pl.pallas_call(functools.partial(backward_kernel, seq_len, query_rows, ke...  58.4 us
    pallas_call x2, Pallas kernels, weight_grads(): pl.pallas_call(functools.partial(grads_kernel, few), grid=(stop - first,)...  50.8 us
    ppermute x21, starting transfers between devices, line_move(): lax.ppermute(right, 'seq', [(i, i + 1) for i in range(k - 1, n - 1)])  50.6 us
    pallas_call x1, Pallas kernels, attention_forward(): pl.pallas_call(functools.partial(forward_kernel, seq_len, query_rows, key...  41.7 us
  transfers between devices with their start and end apart: 104, of which 38 were waited for; matrix products, arithmetic and copies ran while one was open for 16% of the time, Pallas kernels for 26%

profile of v11, /device:TPU:0, one launch (start us, length us, event | category | flops | bytes accessed | tf_op | source)
XLA Modules:
  0.0 1164.8 jit_solution(3810744658695272172)
XLA Ops:
  15.1 6.4 maximum_maximum_fusion
  23.2 6.0 collective-permute-start
  31.8 5.5 collective-permute-start.2
  63.0 6.6 collective-permute-done.3
  90.0 14.4 %collective-permute-done.7 = bf16[272,1536]{1,0:T(8,128)(2,1)} collective-permute-done((bf16[272,1536]{1,0:T(8,128)(2,1)}, bf16[272,1536]{1,0:T(8,128)(2,1)}, u32[]{:S(2)}, u32[]{:S(2)}) %collective-permute-start.7) | collective-permute-done | bytes 835616 | tf_op jit(solution)/shard_map/ppermute | solution.py:68
  121.2 16.5 %collective-permute-done.11 = bf16[272,1536]{1,0:T(8,128)(2,1)} collective-permute-done((bf16[272,1536]{1,0:T(8,128)(2,1)}, bf16[272,1536]{1,0:T(8,128)(2,1)}, u32[]{:S(2)}, u32[]{:S(2)}) %collective-permute-start.11) | collective-permute-done | bytes 835616 | tf_op jit(solution)/shard_map/ppermute | solution.py:68
  153.0 41.7 %attention_forward.1 = (bf16[4,384,512]{2,1,0:T(8,128)(2,1)}, f32[2,3,64,2048]{3,2,1,0:T(8,128)}, f32[2,3,1,2048]{3,2,1,0:T(1,128)}) custom-call(s32[1,2048]{1,0:T(1,128)} %bitcast.334, bf16[4,2,5,64,512]{4,3,2,1,0:T(8,128)(2,1)} %copy-done.15, bf16[2,2048,64]{2,1,0:T(8,128)(2,1)} %copy.175.k_ref, bf16[2,64,2048]{2,1,0:T(8,128)(2,1)} %copy.176.vt_ref), custom_call_target="tpu_custom_call" | custom-call | tf_op jit(solution)/shard_map/attention_forward/pallas_call | solution.py:345
  216.0 6.1 collective-permute-done.14
  222.2 16.0 %collective-permute-done.16 = bf16[384,512]{1,0:T(8,128)(2,1)S(1)} collective-permute-done((bf16[384,512]{1,0:T(8,128)(2,1)S(1)}, bf16[384,512]{1,0:T(8,128)(2,1)S(1)}, u32[]{:S(2)}, u32[]{:S(2)}) %collective-permute-start.16) | collective-permute-done | bytes 393248 | tf_op jit(solution)/shard_map/ppermute | solution.py:208
  250.0 5.4 collective-permute-start.22
  256.7 9.1 collective-permute-done.18
  265.8 5.3 collective-permute-done.19
  273.9 5.8 collective-permute-done.22
  279.7 8.3 collective-permute-done.23
  293.7 25.2 %experts_forward.4 = (bf16[4,512,1536]{2,1,0:T(8,128)(2,1)}, bf16[10,4,160,1536]{3,2,1,0:T(8,128)(2,1)}, bf16[10,4,160,1024]{3,2,1,0:T(8,128)(2,1)}, f32[10,512]{1,0:T(8,128)S(1)}) custom-call(s32[2]{0:T(128)S(1)} %get-tuple-element.577.at_ref, bf16[256,1536]{1,0:T(8,128)(2,1)S(1)} %get-tuple-element.521.tok_ref, ...), custom_call_target="tpu_custom_call" | custom-call | tf_op jit(solution)/shard_map/experts_forward/pallas_call | solution.py:600
  321.7 10.0 collective-permute-start.29
  334.3 25.2 %experts_forward.5 = (bf16[4,512,1536]{2,1,0:T(8,128)(2,1)}, bf16[10,4,160,1536]{3,2,1,0:T(8,128)(2,1)}, bf16[10,4,160,1024]{3,2,1,0:T(8,128)(2,1)}, f32[10,512]{1,0:T(8,128)S(1)}) custom-call(s32[2]{0:T(128)S(1)} %get-tuple-element.578.at_ref, ...), custom_call_target="tpu_custom_call", output_to_operand_aliasing={{0}: (8, {}), {1}: (9, {}), {2}: (10, {})} | custom-call | tf_op jit(solution)/shard_map/experts_forward/pallas_call | solution.py:600
  368.0 25.2 %experts_forward.6 = (bf16[4,512,1536]{2,1,0:T(8,128)(2,1)}, bf16[10,4,160,1536]{3,2,1,0:T(8,128)(2,1)}, bf16[10,4,160,1024]{3,2,1,0:T(8,128)(2,1)}, f32[10,512]{1,0:T(8,128)S(1)}) custom-call(s32[2]{0:T(128)S(1)} %get-tuple-element.579.at_ref, ...), custom_call_target="tpu_custom_call", output_to_operand_aliasing={{0}: (8, {}), {1}: (9, {}), {2}: (10, {})} | custom-call | tf_op jit(solution)/shard_map/experts_forward/pallas_call | solution.py:600
  393.3 25.2 %experts_forward.7 = (bf16[4,512,1536]{2,1,0:T(8,128)(2,1)}, bf16[10,4,160,1536]{3,2,1,0:T(8,128)(2,1)}, bf16[10,4,160,1024]{3,2,1,0:T(8,128)(2,1)}, f32[10,512]{1,0:T(8,128)S(1)}) custom-call(s32[2]{0:T(128)S(1)} %get-tuple-element.576.at_ref, ...), custom_call_target="tpu_custom_call", output_to_operand_aliasing={{0}: (8, {}), {1}: (9, {}), {2}: (10, {})} | custom-call | tf_op jit(solution)/shard_map/experts_forward/pallas_call | solution.py:600
  422.1 6.0 collective-permute-start.30
  431.5 14.6 %collective-permute-done.30 = bf16[256,1536]{1,0:T(8,128)(2,1)S(1)} collective-permute-done((bf16[256,1536]{1,0:T(8,128)(2,1)S(1)}, bf16[256,1536]{1,0:T(8,128)(2,1)S(1)}, u32[]{:S(2)}, u32[]{:S(2)}) %collective-permute-start.30) | collective-permute-done | bytes 786464 | tf_op jit(solution)/shard_map/ppermute | solution.py:134
  451.6 11.3 collective-permute-done.36
  468.5 11.3 collective-permute-done.32
  480.2 5.3 collective-permute-start.34
  486.9 9.7 collective-permute-done.38
  497.9 5.3 collective-permute-start.40
  541.5 32.2 %experts_backward.4 = (bf16[4,512,1536]{2,1,0:T(8,128)(2,1)}, bf16[10,4,160,1536]{3,2,1,0:T(8,128)(2,1)}, bf16[10,4,160,1024]{3,2,1,0:T(8,128)(2,1)}, bf16[10,4,...) custom-call(s32[2]{0:T(128)S(1)} %get-tuple-element.577.at_ref, bf16[256,1536]{1,0:T(8,128)(2,1)S(1)} %get-tuple-element.515.tok_ref, ...), custom_call_target="tpu_custom_call" | custom-call | tf_op jit(solution)/shard_map/experts_backward/pallas_call | solution.py:600
  579.4 32.2 %experts_backward.5 = (bf16[4,512,1536]{2,1,0:T(8,128)(2,1)}, bf16[10,4,160,1536]{3,2,1,0:T(8,128)(2,1)}, bf16[10,4,160,1024]{3,2,1,0:T(8,128)(2,1)}, bf16[10,4,...) custom-call(s32[2]{0:T(128)S(1)} %get-tuple-element.578.at_ref, ...), custom_call_target="tpu_custom_call", output_to_operand_aliasing={{0}: (10, {}), {1}: (11, {}), {2}: (12, {}), {3}: (13, {})} | custom-call | tf_op jit(solution)/shard_map/experts_backward/pallas_call | solution.py:600
  618.4 32.2 %experts_backward.6 = (bf16[4,512,1536]{2,1,0:T(8,128)(2,1)}, bf16[10,4,160,1536]{3,2,1,0:T(8,128)(2,1)}, bf16[10,4,160,1024]{3,2,1,0:T(8,128)(2,1)}, bf16[10,4,...) custom-call(s32[2]{0:T(128)S(1)} %get-tuple-element.579.at_ref, ...), custom_call_target="tpu_custom_call", output_to_operand_aliasing={{0}: (10, {}), {1}: (11, {}), {2}: (12, {}), {3}: (13, {})} | custom-call | tf_op jit(solution)/shard_map/experts_backward/pallas_call | solution.py:600
  655.3 32.2 %experts_backward.7 = (bf16[4,512,1536]{2,1,0:T(8,128)(2,1)}, bf16[10,4,160,1536]{3,2,1,0:T(8,128)(2,1)}, bf16[10,4,160,1024]{3,2,1,0:T(8,128)(2,1)}, bf16[10,4,...) custom-call(s32[2]{0:T(128)S(1)} %get-tuple-element.576.at_ref, ...), custom_call_target="tpu_custom_call", output_to_operand_aliasing={{0}: (10, {}), {1}: (11, {}), {2}: (12, {}), {3}: (13, {})} | custom-call | tf_op jit(solution)/shard_map/experts_backward/pallas_call | solution.py:600
  689.6 11.8 %collective-permute-start.57 = (bf16[512,1536]{1,0:T(8,128)(2,1)S(1)}, bf16[512,1536]{1,0:T(8,128)(2,1)S(1)}, u32[]{:S(2)}, u32[]{:S(2)}) collective-permute-start(bf16[512,1536]{1,0:T(8,128)(2,1)S(1)} %get-tuple-element.469), channel_id=1, source_target_pairs={{0,1},{4,5},{8,9},{12,13},{16,17},{20,21},{24,25},{28,29}} | collective-permute-start | bytes 4718600 | tf_op jit(solution)/shard_map/ppermute | solution.py:134
  702.4 25.5 %weight_grads.2.refs_0_ = bf16[10,1536,1536]{2,1,0:T(8,128)(2,1)} custom-call(bf16[10,640,1536]{2,1,0:T(8,128)(2,1)} %bitcast.306, bf16[10,640,1024]{2,1,0:T(8,128)(2,1)} %bitcast.308, bf16[10,640,512]{2,1,0:T(8,128)(2,1)} %bitcast.310, bf16[10,640,1536]{2,1,0:T(8,128)(2,1)} %bitcast.304), custom_call_target="tpu_custom_call" | custom-call | tf_op jit(solution)/shard_map/weight_grads/pallas_call | solution.py:771
  737.6 25.4 %weight_grads.3 = bf16[10,1536,1536]{2,1,0:T(8,128)(2,1)} custom-call(bf16[10,640,1536]{2,1,0:T(8,128)(2,1)} %bitcast.307, bf16[10,640,1024]{2,1,0:T(8,128)(2,1)} %bitcast.309, bf16[10,640,512]{2,1,0:T(8,128)(2,1)} %bitcast.311, bf16[10,640,1536]{2,1,0:T(8,128)(2,1)} %bitcast.305, ...), custom_call_target="tpu_custom_call", output_to_operand_aliasing={{}: (4, {})} | custom-call | tf_op jit(solution)/shard_map/weight_grads/pallas_call | solution.py:771
  766.1 5.4 collective-permute-start.61
  773.3 21.4 %collective-permute-done.61 = bf16[512,1536]{1,0:T(8,128)(2,1)S(1)} collective-permute-done((bf16[512,1536]{1,0:T(8,128)(2,1)S(1)}, bf16[512,1536]{1,0:T(8,128)(2,1)S(1)}, u32[]{:S(2)}, u32[]{:S(2)}) %collective-permute-start.61) | collective-permute-done | bytes 1572896 | tf_op jit(solution)/shard_map/ppermute | solution.py:134
  817.5 5.8 out_grads.1
  824.3 6.2 fusion.33
  854.7 7.8 collective-permute-done.67.refs_3_
  862.5 15.8 %collective-permute-done.69.refs_5_ = bf16[384,512]{1,0:T(8,128)(2,1)S(1)} collective-permute-done((bf16[384,512]{1,0:T(8,128)(2,1)}, bf16[384,512]{1,0:T(8,128)(2,1)S(1)}, u32[]{:S(2)}, u32[]{:S(2)}) %collective-permute-start.69) | collective-permute-done | bytes 393248 | tf_op jit(solution)/shard_map/ppermute | solution.py:208
  887.1 58.4 %attention_backward.1 = (bf16[2,3,64,2048]{3,2,1,0:T(8,128)(2,1)}, bf16[2,64,2048]{2,1,0:T(8,128)(2,1)}, bf16[2,64,2048]{2,1,0:T(8,128)(2,1)}) custom-call(s32[1]{0:T(128)} %bitcast.51.me_ref, s32[1,2048]{1,0:T(1,128)} %bitcast.335, bf16[4,2,5,64,512]{4,3,2,1,0:T(8,128)(2,1)} %copy-done.15, bf16[2,2048,64]{2,1,0:T(8,128)(2,1)} %copy.175.k_ref, ...), custom_call_target="tpu_custom_call" | custom-call | tf_op jit(solution)/shard_map/attention_backward/pallas_call | solution.py:428
  951.9 9.5 convolution_convert_fusion
  983.0 7.4 convolution_convert_fusion.1
  1001.7 7.9 collective-permute-done.80
  1019.1 7.9 collective-permute-start.83
  1035.8 12.0 %collective-permute-start.88 = (bf16[256,1536]{1,0:T(8,128)(2,1)}, bf16[256,1536]{1,0:T(8,128)(2,1)}, u32[]{:S(2)}, u32[]{:S(2)}) collective-permute-start(bf16[256,1536]{1,0:T(8,128)(2,1)} %get-tuple-element.485), channel_id=1, source_target_pairs={{0,1},{1,2},{2,3},{4,5},{5,6},{6,7},{8,9},{9,10},{10,11},{12,13},{... | collective-permute-start | bytes 2359304 | tf_op jit(solution)/shard_map/ppermute | solution.py:134
  1055.9 12.1 %collective-permute-start.90 = (bf16[304,1536]{1,0:T(8,128)(2,1)}, bf16[304,1536]{1,0:T(8,128)(2,1)}, u32[]{:S(2)}, u32[]{:S(2)}) collective-permute-start(bf16[304,1536]{1,0:T(8,128)(2,1)} %get-tuple-element.479), channel_id=1, source_target_pairs={{0,1},{1,2},{2,3},{4,5},{5,6},{6,7},{8,9},{9,10},{10,11},{12,13},{... | collective-permute-start | bytes 2801672 | tf_op jit(solution)/shard_map/ppermute | solution.py:134
  1079.7 6.8 collective-permute-done.90
  1099.3 7.4 collective-permute-start.92
  (636 shorter events, 414.8 us)
Async XLA Ops:
  7.2 70.5 %all-gather.3.cloned.1.call-start = ((), (), s32[]{:S(2)}) async-start(), calls=%async_computation.1 | async-start | bytes 7962624 | tf_op jit(solution)/shard_map/all_gather | solution.py:823
  12.9 280.8 %all-gather.5.cloned.1.call-start = ((), (), s32[]{:S(2)}) async-start(), calls=%async_computation.2 | async-start | bytes 53084160 | tf_op jit(solution)/shard_map/all_gather | solution.py:840
  21.5 1094.7 %reduce-scatter.2.cloned.1.call-start = ((), (), s32[]{:S(2)}) async-start(), calls=%async_computation.3 | async-start | bytes 53084160 | tf_op jit(solution)/shard_map/reduce_scatter | solution.py:992
  23.2 34.8 %collective-permute-start = (bf16[256,1536]{1,0:T(8,128)(2,1)S(1)}, bf16[256,1536]{1,0:T(8,128)(2,1)}, u32[]{:S(2)}, u32[]{:S(2)}) collective-permute-start(bf16[256,1536]{1,0:T(8,128)(2,1)S(1)} %get-tuple-element.529), channel_id=1, source_target_pairs={{0,1},{1,2},{2,3},{4,5},{5,6},{6,7},{8,9},{9,10},{10,11},{12,13},{... | collective-permute-start | bytes 2359304 | tf_op jit(solution)/shard_map/ppermute | solution.py:67
  37.2 32.3 %collective-permute-start.3 = (bf16[272,1536]{1,0:T(8,128)(2,1)S(1)}, bf16[272,1536]{1,0:T(8,128)(2,1)}, u32[]{:S(2)}, u32[]{:S(2)}) collective-permute-start(bf16[272,1536]{1,0:T(8,128)(2,1)S(1)} %pad_maximum_fusion.9), channel_id=1, source_target_pairs={{1,0},{2,1},{3,2},{5,4},{6,5},{7,6},{9,8},{10,9},{11,10},{13,12},{... | collective-permute-start | bytes 2506760 | tf_op jit(solution)/shard_map/ppermute | solution.py:68
  69.6 34.8 %collective-permute-start.7 = (bf16[272,1536]{1,0:T(8,128)(2,1)}, bf16[272,1536]{1,0:T(8,128)(2,1)}, u32[]{:S(2)}, u32[]{:S(2)}) collective-permute-start(bf16[272,1536]{1,0:T(8,128)(2,1)} %collective-permute-done.3), channel_id=1, source_target_pairs={{1,0},{2,1},{5,4},{6,5},{9,8},{10,9},{13,12},{14,13},{17,16},{18,1... | collective-permute-start | bytes 2506760 | tf_op jit(solution)/shard_map/ppermute | solution.py:68
  70.9 33.5 %collective-permute-start.6 = (bf16[272,1536]{1,0:T(8,128)(2,1)}, bf16[272,1536]{1,0:T(8,128)(2,1)}, u32[]{:S(2)}, u32[]{:S(2)}) collective-permute-start(bf16[272,1536]{1,0:T(8,128)(2,1)} %collective-permute-done.2), channel_id=1, source_target_pairs={{1,2},{2,3},{5,6},{6,7},{9,10},{10,11},{13,14},{14,15},{17,18},{18... | collective-permute-start | bytes 2506760 | tf_op jit(solution)/shard_map/ppermute | solution.py:67
  88.7 32.5 %collective-permute-start.9 = (bf16[256,1536]{1,0:T(8,128)(2,1)}, bf16[256,1536]{1,0:T(8,128)(2,1)}, u32[]{:S(2)}, u32[]{:S(2)}) collective-permute-start(bf16[256,1536]{1,0:T(8,128)(2,1)} %collective-permute-done.5), channel_id=1, source_target_pairs={{1,0},{5,4},{9,8},{13,12},{17,16},{21,20},{25,24},{29,28}} | collective-permute-start | bytes 2359304 | tf_op jit(solution)/shard_map/ppermute | solution.py:68
  105.9 31.8 %collective-permute-start.11 = (bf16[272,1536]{1,0:T(8,128)(2,1)}, bf16[272,1536]{1,0:T(8,128)(2,1)}, u32[]{:S(2)}, u32[]{:S(2)}) collective-permute-start(bf16[272,1536]{1,0:T(8,128)(2,1)} %collective-permute-done.7), channel_id=1, source_target_pairs={{1,0},{5,4},{9,8},{13,12},{17,16},{21,20},{25,24},{29,28}} | collective-permute-start | bytes 2506760 | tf_op jit(solution)/shard_map/ppermute | solution.py:68
  204.3 33.8 %collective-permute-start.16 = (bf16[384,512]{1,0:T(8,128)(2,1)S(1)}, bf16[384,512]{1,0:T(8,128)(2,1)S(1)}, u32[]{:S(2)}, u32[]{:S(2)}) collective-permute-start(bf16[384,512]{1,0:T(8,128)(2,1)S(1)} %get-tuple-element.523), channel_id=1, source_target_pairs={{2,0},{3,1},{6,4},{7,5},{10,8},{11,9},{14,12},{15,13},{18,16},{19,... | collective-permute-start | bytes 1179656 | tf_op jit(solution)/shard_map/ppermute | solution.py:208
  255.5 32.6 %collective-permute-start.23 = (bf16[256,1536]{1,0:T(8,128)(2,1)S(1)}, bf16[256,1536]{1,0:T(8,128)(2,1)}, u32[]{:S(2)}, u32[]{:S(2)}) collective-permute-start(bf16[256,1536]{1,0:T(8,128)(2,1)S(1)} %get-tuple-element.520.more_ref), channel_id=1, source_target_pairs={{1,0},{2,1},{3,2},{5,4},{6,5},{7,6},{9,8},{10,9},{11,10},{13,12},{... | collective-permute-start | bytes 2359304 | tf_op jit(solution)/shard_map/ppermute | solution.py:68
  271.1 47.8 %collective-permute-start.20 = (bf16[256,1536]{1,0:T(8,128)(2,1)}, bf16[256,1536]{1,0:T(8,128)(2,1)}, u32[]{:S(2)}, u32[]{:S(2)}) collective-permute-start(bf16[256,1536]{1,0:T(8,128)(2,1)} %collective-permute-done.18), channel_id=1, source_target_pairs={{1,2},{2,3},{5,6},{6,7},{9,10},{10,11},{13,14},{14,15},{17,18},{18... | collective-permute-start | bytes 2359304 | tf_op jit(solution)/shard_map/ppermute | solution.py:67
  272.6 46.3 %collective-permute-start.21 = (bf16[256,1536]{1,0:T(8,128)(2,1)S(1)}, bf16[256,1536]{1,0:T(8,128)(2,1)}, u32[]{:S(2)}, u32[]{:S(2)}) collective-permute-start(bf16[256,1536]{1,0:T(8,128)(2,1)S(1)} %collective-permute-done.19), channel_id=1, source_target_pairs={{1,0},{2,1},{5,4},{6,5},{9,8},{10,9},{13,12},{14,13},{17,16},{18,1... | collective-permute-start | bytes 2359304 | tf_op jit(solution)/shard_map/ppermute | solution.py:68
  288.1 32.9 %collective-permute-start.26 = (bf16[256,1536]{1,0:T(8,128)(2,1)}, bf16[256,1536]{1,0:T(8,128)(2,1)}, u32[]{:S(2)}, u32[]{:S(2)}) collective-permute-start(bf16[256,1536]{1,0:T(8,128)(2,1)} %collective-permute-done.22), channel_id=1, source_target_pairs={{1,2},{2,3},{5,6},{6,7},{9,10},{10,11},{13,14},{14,15},{17,18},{18... | collective-permute-start | bytes 2359304 | tf_op jit(solution)/shard_map/ppermute | solution.py:67
  318.9 40.7 %collective-permute-start.24 = (bf16[256,1536]{1,0:T(8,128)(2,1)}, bf16[256,1536]{1,0:T(8,128)(2,1)S(1)}, u32[]{:S(2)}, u32[]{:S(2)}) collective-permute-start(bf16[256,1536]{1,0:T(8,128)(2,1)} %collective-permute-done.20), channel_id=1, source_target_pairs={{2,3},{6,7},{10,11},{14,15},{18,19},{22,23},{26,27},{30,31}} | collective-permute-start | bytes 2359304 | tf_op jit(solution)/shard_map/ppermute | solution.py:67
  319.6 40.0 %collective-permute-start.25 = (bf16[256,1536]{1,0:T(8,128)(2,1)}, bf16[256,1536]{1,0:T(8,128)(2,1)S(1)}, u32[]{:S(2)}, u32[]{:S(2)}) collective-permute-start(bf16[256,1536]{1,0:T(8,128)(2,1)} %collective-permute-done.21), channel_id=1, source_target_pairs={{1,0},{5,4},{9,8},{13,12},{17,16},{21,20},{25,24},{29,28}} | collective-permute-start | bytes 2359304 | tf_op jit(solution)/shard_map/ppermute | solution.py:68
  320.9 38.6 %collective-permute-start.28 = (bf16[256,1536]{1,0:T(8,128)(2,1)}, bf16[256,1536]{1,0:T(8,128)(2,1)S(1)}, u32[]{:S(2)}, u32[]{:S(2)}) collective-permute-start(bf16[256,1536]{1,0:T(8,128)(2,1)} %collective-permute-done.26), channel_id=1, source_target_pairs={{2,3},{6,7},{10,11},{14,15},{18,19},{22,23},{26,27},{30,31}} | collective-permute-start | bytes 2359304 | tf_op jit(solution)/shard_map/ppermute | solution.py:67
  321.7 37.9 %collective-permute-start.29 = (bf16[256,1536]{1,0:T(8,128)(2,1)}, bf16[256,1536]{1,0:T(8,128)(2,1)S(1)}, u32[]{:S(2)}, u32[]{:S(2)}) collective-permute-start(bf16[256,1536]{1,0:T(8,128)(2,1)} %collective-permute-done.27), channel_id=1, source_target_pairs={{1,0},{5,4},{9,8},{13,12},{17,16},{21,20},{25,24},{29,28}} | collective-permute-start | bytes 2359304 | tf_op jit(solution)/shard_map/ppermute | solution.py:68
  429.0 33.9 %collective-permute-start.36 = (bf16[256,1536]{1,0:T(8,128)(2,1)S(1)}, bf16[256,1536]{1,0:T(8,128)(2,1)S(1)}, u32[]{:S(2)}, u32[]{:S(2)}) collective-permute-start(bf16[256,1536]{1,0:T(8,128)(2,1)S(1)} %get-tuple-element.501), channel_id=1, source_target_pairs={{0,1},{4,5},{8,9},{12,13},{16,17},{20,21},{24,25},{28,29}} | collective-permute-start | bytes 2359304 | tf_op jit(solution)/shard_map/ppermute | solution.py:134
  430.8 32.2 %collective-permute-start.37 = (bf16[256,1536]{1,0:T(8,128)(2,1)S(1)}, bf16[256,1536]{1,0:T(8,128)(2,1)S(1)}, u32[]{:S(2)}, u32[]{:S(2)}) collective-permute-start(bf16[256,1536]{1,0:T(8,128)(2,1)S(1)} %get-tuple-element.500), channel_id=1, source_target_pairs={{3,2},{7,6},{11,10},{15,14},{19,18},{23,22},{27,26},{31,30}} | collective-permute-start | bytes 2359304 | tf_op jit(solution)/shard_map/ppermute | solution.py:135
  446.5 33.3 %collective-permute-start.32 = (bf16[256,1536]{1,0:T(8,128)(2,1)S(1)}, bf16[256,1536]{1,0:T(8,128)(2,1)S(1)}, u32[]{:S(2)}, u32[]{:S(2)}) collective-permute-start(bf16[256,1536]{1,0:T(8,128)(2,1)S(1)} %get-tuple-element.497), channel_id=1, source_target_pairs={{0,1},{1,2},{4,5},{5,6},{8,9},{9,10},{12,13},{13,14},{16,17},{17,1... | collective-permute-start | bytes 2359304 | tf_op jit(solution)/shard_map/ppermute | solution.py:134
  463.3 33.3 %collective-permute-start.38 = (bf16[256,1536]{1,0:T(8,128)(2,1)S(1)}, bf16[256,1536]{1,0:T(8,128)(2,1)S(1)}, u32[]{:S(2)}, u32[]{:S(2)}) collective-permute-start(bf16[256,1536]{1,0:T(8,128)(2,1)S(1)} %get-tuple-element.495), channel_id=1, source_target_pairs={{0,1},{1,2},{4,5},{5,6},{8,9},{9,10},{12,13},{13,14},{16,17},{17,1... | collective-permute-start | bytes 2359304 | tf_op jit(solution)/shard_map/ppermute | solution.py:134
  480.2 36.1 %collective-permute-start.34 = (bf16[256,1536]{1,0:T(8,128)(2,1)S(1)}, bf16[256,1536]{1,0:T(8,128)(2,1)}, u32[]{:S(2)}, u32[]{:S(2)}) collective-permute-start(bf16[256,1536]{1,0:T(8,128)(2,1)S(1)} %get-tuple-element.493), channel_id=1, source_target_pairs={{0,1},{1,2},{2,3},{4,5},{5,6},{6,7},{8,9},{9,10},{10,11},{12,13},{... | collective-permute-start | bytes 2359304 | tf_op jit(solution)/shard_map/ppermute | solution.py:134
  529.9 45.9 %collective-permute-start.49 = (bf16[272,1536]{1,0:T(8,128)(2,1)S(1)}, bf16[272,1536]{1,0:T(8,128)(2,1)S(1)}, u32[]{:S(2)}, u32[]{:S(2)}) collective-permute-start(bf16[272,1536]{1,0:T(8,128)(2,1)S(1)} %fusion.81.more_ref), channel_id=1, source_target_pairs={{0,1},{1,2},{2,3},{4,5},{5,6},{6,7},{8,9},{9,10},{10,11},{12,13},{... | collective-permute-start | bytes 2506760 | tf_op jit(solution)/shard_map/ppermute | solution.py:67
  534.3 41.4 %collective-permute-start.50 = (bf16[272,1536]{1,0:T(8,128)(2,1)S(1)}, bf16[272,1536]{1,0:T(8,128)(2,1)S(1)}, u32[]{:S(2)}, u32[]{:S(2)}) collective-permute-start(bf16[272,1536]{1,0:T(8,128)(2,1)S(1)} %fusion.81.more_ref), channel_id=1, source_target_pairs={{1,0},{2,1},{3,2},{5,4},{6,5},{7,6},{9,8},{10,9},{11,10},{13,12},{... | collective-permute-start | bytes 2506760 | tf_op jit(solution)/shard_map/ppermute | solution.py:68
  535.6 38.1 %collective-permute-start.45 = (bf16[256,1536]{1,0:T(8,128)(2,1)S(1)}, bf16[256,1536]{1,0:T(8,128)(2,1)S(1)}, u32[]{:S(2)}, u32[]{:S(2)}) collective-permute-start(bf16[256,1536]{1,0:T(8,128)(2,1)S(1)} %get-tuple-element.515.tok_ref), channel_id=1, source_target_pairs={{0,1},{1,2},{2,3},{4,5},{5,6},{6,7},{8,9},{9,10},{10,11},{12,13},{... | collective-permute-start | bytes 2359304 | tf_op jit(solution)/shard_map/ppermute | solution.py:67
  540.2 33.5 %collective-permute-start.46 = (bf16[256,1536]{1,0:T(8,128)(2,1)S(1)}, bf16[256,1536]{1,0:T(8,128)(2,1)S(1)}, u32[]{:S(2)}, u32[]{:S(2)}) collective-permute-start(bf16[256,1536]{1,0:T(8,128)(2,1)S(1)} %get-tuple-element.515.tok_ref), channel_id=1, source_target_pairs={{1,0},{2,1},{3,2},{5,4},{6,5},{7,6},{9,8},{10,9},{11,10},{13,12},{... | collective-permute-start | bytes 2359304 | tf_op jit(solution)/shard_map/ppermute | solution.py:68
  573.7 37.9 %collective-permute-start.47 = (bf16[256,1536]{1,0:T(8,128)(2,1)S(1)}, bf16[256,1536]{1,0:T(8,128)(2,1)S(1)}, u32[]{:S(2)}, u32[]{:S(2)}) collective-permute-start(bf16[256,1536]{1,0:T(8,128)(2,1)S(1)} %collective-permute-done.45), channel_id=1, source_target_pairs={{1,2},{2,3},{5,6},{6,7},{9,10},{10,11},{13,14},{14,15},{17,18},{18... | collective-permute-start | bytes 2359304 | tf_op jit(solution)/shard_map/ppermute | solution.py:67
  574.4 37.2 %collective-permute-start.48 = (bf16[256,1536]{1,0:T(8,128)(2,1)S(1)}, bf16[256,1536]{1,0:T(8,128)(2,1)S(1)}, u32[]{:S(2)}, u32[]{:S(2)}) collective-permute-start(bf16[256,1536]{1,0:T(8,128)(2,1)S(1)} %collective-permute-done.46), channel_id=1, source_target_pairs={{1,0},{2,1},{5,4},{6,5},{9,8},{10,9},{13,12},{14,13},{17,16},{18,1... | collective-permute-start | bytes 2359304 | tf_op jit(solution)/shard_map/ppermute | solution.py:68
  575.7 37.9 %collective-permute-start.53 = (bf16[272,1536]{1,0:T(8,128)(2,1)S(1)}, bf16[272,1536]{1,0:T(8,128)(2,1)S(1)}, u32[]{:S(2)}, u32[]{:S(2)}) collective-permute-start(bf16[272,1536]{1,0:T(8,128)(2,1)S(1)} %collective-permute-done.49), channel_id=1, source_target_pairs={{1,2},{2,3},{5,6},{6,7},{9,10},{10,11},{13,14},{14,15},{17,18},{18... | collective-permute-start | bytes 2506760 | tf_op jit(solution)/shard_map/ppermute | solution.py:67
  576.5 37.2 %collective-permute-start.54 = (bf16[272,1536]{1,0:T(8,128)(2,1)S(1)}, bf16[272,1536]{1,0:T(8,128)(2,1)S(1)}, u32[]{:S(2)}, u32[]{:S(2)}) collective-permute-start(bf16[272,1536]{1,0:T(8,128)(2,1)S(1)} %collective-permute-done.50), channel_id=1, source_target_pairs={{1,0},{2,1},{5,4},{6,5},{9,8},{10,9},{13,12},{14,13},{17,16},{18,1... | collective-permute-start | bytes 2506760 | tf_op jit(solution)/shard_map/ppermute | solution.py:68
  611.6 39.0 %collective-permute-start.51 = (bf16[256,1536]{1,0:T(8,128)(2,1)S(1)}, bf16[256,1536]{1,0:T(8,128)(2,1)S(1)}, u32[]{:S(2)}, u32[]{:S(2)}) collective-permute-start(bf16[256,1536]{1,0:T(8,128)(2,1)S(1)} %collective-permute-done.47), channel_id=1, source_target_pairs={{2,3},{6,7},{10,11},{14,15},{18,19},{22,23},{26,27},{30,31}} | collective-permute-start | bytes 2359304 | tf_op jit(solution)/shard_map/ppermute | solution.py:67
  612.3 38.3 %collective-permute-start.52 = (bf16[256,1536]{1,0:T(8,128)(2,1)S(1)}, bf16[256,1536]{1,0:T(8,128)(2,1)S(1)}, u32[]{:S(2)}, u32[]{:S(2)}) collective-permute-start(bf16[256,1536]{1,0:T(8,128)(2,1)S(1)} %collective-permute-done.48), channel_id=1, source_target_pairs={{1,0},{5,4},{9,8},{13,12},{17,16},{21,20},{25,24},{29,28}} | collective-permute-start | bytes 2359304 | tf_op jit(solution)/shard_map/ppermute | solution.py:68
  613.6 37.0 %collective-permute-start.55 = (bf16[272,1536]{1,0:T(8,128)(2,1)S(1)}, bf16[272,1536]{1,0:T(8,128)(2,1)S(1)}, u32[]{:S(2)}, u32[]{:S(2)}) collective-permute-start(bf16[272,1536]{1,0:T(8,128)(2,1)S(1)} %collective-permute-done.53), channel_id=1, source_target_pairs={{2,3},{6,7},{10,11},{14,15},{18,19},{22,23},{26,27},{30,31}} | collective-permute-start | bytes 2506760 | tf_op jit(solution)/shard_map/ppermute | solution.py:67
  614.4 36.8 %collective-permute-start.56 = (bf16[272,1536]{1,0:T(8,128)(2,1)S(1)}, bf16[272,1536]{1,0:T(8,128)(2,1)S(1)}, u32[]{:S(2)}, u32[]{:S(2)}) collective-permute-start(bf16[272,1536]{1,0:T(8,128)(2,1)S(1)} %collective-permute-done.54), channel_id=1, source_target_pairs={{1,0},{5,4},{9,8},{13,12},{17,16},{21,20},{25,24},{29,28}} | collective-permute-start | bytes 2506760 | tf_op jit(solution)/shard_map/ppermute | solution.py:68
  689.6 38.2 %collective-permute-start.57 = (bf16[512,1536]{1,0:T(8,128)(2,1)S(1)}, bf16[512,1536]{1,0:T(8,128)(2,1)S(1)}, u32[]{:S(2)}, u32[]{:S(2)}) collective-permute-start(bf16[512,1536]{1,0:T(8,128)(2,1)S(1)} %get-tuple-element.469), channel_id=1, source_target_pairs={{0,1},{4,5},{8,9},{12,13},{16,17},{20,21},{24,25},{28,29}} | collective-permute-start | bytes 4718600 | tf_op jit(solution)/shard_map/ppermute | solution.py:134
  802.8 39.9 %collective-permute-start.71 = (f32[1,1]{1,0:T(1,128)}, f32[1,1]{1,0:T(1,128)}, u32[]{:S(2)}, u32[]{:S(2)}) collective-permute-start(f32[1,1]{1,0:T(1,128)} %bitcast.81), channel_id=1, source_target_pairs={{0,1},{1,0},{2,3},{3,2},{4,5},{5,4},{6,7},{7,6},{8,9},{9,8},{10,11... | collective-permute-start | bytes 20 | tf_op jit(solution)/shard_map/ppermute | solution.py:213
  842.7 35.5 %collective-permute-start.69 = (bf16[384,512]{1,0:T(8,128)(2,1)}, bf16[384,512]{1,0:T(8,128)(2,1)S(1)}, u32[]{:S(2)}, u32[]{:S(2)}) collective-permute-start(bf16[384,512]{1,0:T(8,128)(2,1)} %get-tuple-element.508), channel_id=1, source_target_pairs={{2,0},{3,1},{6,4},{7,5},{10,8},{11,9},{14,12},{15,13},{18,16},{19,... | collective-permute-start | bytes 1179656 | tf_op jit(solution)/shard_map/ppermute | solution.py:208
  846.2 32.0 %collective-permute-start.70 = (bf16[384,512]{1,0:T(8,128)(2,1)}, bf16[384,512]{1,0:T(8,128)(2,1)S(1)}, u32[]{:S(2)}, u32[]{:S(2)}) collective-permute-start(bf16[384,512]{1,0:T(8,128)(2,1)} %get-tuple-element.507), channel_id=1, source_target_pairs={{3,0},{7,4},{11,8},{15,12},{19,16},{23,20},{27,24},{31,28}} | collective-permute-start | bytes 1179656 | tf_op jit(solution)/shard_map/ppermute | solution.py:208
  878.2 67.3 %collective-permute-start.72 = (bf16[2,192,768]{2,1,0:T(8,128)(2,1)}, bf16[2,192,768]{2,1,0:T(8,128)(2,1)}, u32[]{:S(2)}, u32[]{:S(2)}) collective-permute-start(bf16[2,192,768]{2,1,0:T(8,128)(2,1)} %add_convert_fusion.3), channel_id=1, source_target_pairs={{0,8},{4,12},{8,0},{12,4},{16,24},{20,28},{24,16},{28,20},{1,9},{5... | collective-permute-start | bytes 1769480 | tf_op jit(solution)/shard_map/ppermute | solution.py:213
  879.8 65.8 %collective-permute-start.73 = (bf16[2,192,768]{2,1,0:T(8,128)(2,1)S(1)}, bf16[2,192,768]{2,1,0:T(8,128)(2,1)}, u32[]{:S(2)}, u32[]{:S(2)}) collective-permute-start(bf16[2,192,768]{2,1,0:T(8,128)(2,1)S(1)} %add_convert_fusion.2), channel_id=1, source_target_pairs={{0,16},{4,20},{8,24},{12,28},{16,0},{20,4},{24,8},{28,12},{1,17},{... | collective-permute-start | bytes 1769480 | tf_op jit(solution)/shard_map/ppermute | solution.py:213
  885.8 59.8 %collective-permute-start.74 = (f32[1,1]{1,0:T(1,128)}, f32[1,1]{1,0:T(1,128)}, u32[]{:S(2)}, u32[]{:S(2)}) collective-permute-start(f32[1,1]{1,0:T(1,128)} %add.661), channel_id=1, source_target_pairs={{0,2},{1,3},{2,0},{3,1},{4,6},{5,7},{6,4},{7,5},{8,10},{9,11},{10,... | collective-permute-start | bytes 20 | tf_op jit(solution)/shard_map/ppermute | solution.py:213
  973.5 43.5 %collective-permute-start.78 = (bf16[304,1536]{1,0:T(8,128)(2,1)}, bf16[304,1536]{1,0:T(8,128)(2,1)}, u32[]{:S(2)}, u32[]{:S(2)}) collective-permute-start(bf16[304,1536]{1,0:T(8,128)(2,1)} %get-tuple-element.483), channel_id=1, source_target_pairs={{0,1},{4,5},{8,9},{12,13},{16,17},{20,21},{24,25},{28,29}} | collective-permute-start | bytes 2801672 | tf_op jit(solution)/shard_map/ppermute | solution.py:134
  976.0 41.0 %collective-permute-start.79 = (bf16[304,1536]{1,0:T(8,128)(2,1)}, bf16[304,1536]{1,0:T(8,128)(2,1)}, u32[]{:S(2)}, u32[]{:S(2)}) collective-permute-start(bf16[304,1536]{1,0:T(8,128)(2,1)} %get-tuple-element.482), channel_id=1, source_target_pairs={{3,2},{7,6},{11,10},{15,14},{19,18},{23,22},{27,26},{31,30}} | collective-permute-start | bytes 2801672 | tf_op jit(solution)/shard_map/ppermute | solution.py:135
  1019.1 35.1 %collective-permute-start.83 = (bf16[304,1536]{1,0:T(8,128)(2,1)S(1)}, bf16[304,1536]{1,0:T(8,128)(2,1)S(1)}, u32[]{:S(2)}, u32[]{:S(2)}) collective-permute-start(bf16[304,1536]{1,0:T(8,128)(2,1)S(1)} %get-tuple-element.481), channel_id=1, source_target_pairs={{0,1},{1,2},{4,5},{5,6},{8,9},{9,10},{12,13},{13,14},{16,17},{17,1... | collective-permute-start | bytes 2801672 | tf_op jit(solution)/shard_map/ppermute | solution.py:134
  1030.3 44.9 %collective-permute-start.82 = (bf16[2,192,681]{2,1,0:T(8,128)(2,1)}, bf16[2,192,681]{2,1,0:T(8,128)(2,1)}, u32[]{:S(2)}, u32[]{:S(2)}) collective-permute-start(bf16[2,192,681]{2,1,0:T(8,128)(2,1)} %add_convert_fusion.1), channel_id=1, source_target_pairs={{0,8},{4,12},{8,0},{12,4},{16,24},{20,28},{24,16},{28,20},{1,9},{5... | collective-permute-start | bytes 1569032 | tf_op jit(solution)/shard_map/ppermute | solution.py:213
  1035.8 41.7 %collective-permute-start.88 = (bf16[256,1536]{1,0:T(8,128)(2,1)}, bf16[256,1536]{1,0:T(8,128)(2,1)}, u32[]{:S(2)}, u32[]{:S(2)}) collective-permute-start(bf16[256,1536]{1,0:T(8,128)(2,1)} %get-tuple-element.485), channel_id=1, source_target_pairs={{0,1},{1,2},{2,3},{4,5},{5,6},{6,7},{8,9},{9,10},{10,11},{12,13},{... | collective-permute-start | bytes 2359304 | tf_op jit(solution)/shard_map/ppermute | solution.py:134
  1075.2 44.2 %collective-permute-start.94 = (f32[1,1]{1,0:T(1,128)}, f32[1,1]{1,0:T(1,128)}, u32[]{:S(2)}, u32[]{:S(2)}) collective-permute-start(f32[1,1]{1,0:T(1,128)} %add.662), channel_id=1, source_target_pairs={{0,4},{4,0},{8,12},{12,8},{16,20},{20,16},{24,28},{28,24},{1,5},{5... | collective-permute-start | bytes 20 | tf_op jit(solution)/shard_map/ppermute | solution.py:213
  (180 other events, 3015.7 us)
Sparse Core Ops, SparseCore 0:
  13.0 51.5 all-gather.2
  66.5 219.0 all-gather.4
  799.1 301.7 reduce-scatter.1

commit v12 on v11

--- a/solution.py
+++ b/solution.py
@@ -97,20 +97,19 @@
     return order
 
 
+def arrivals(n, turn):
+    return [dev - places[turn] for dev, places in enumerate(arrival_order(n))]
+
+
 def arrived(rights, lefts, turn):
-    n = lax.axis_size("seq")
-    me = lax.axis_index("seq")
-    sources = {}
-    for dev, places in enumerate(arrival_order(n)):
-        gap = dev - places[turn]
-        sources.setdefault(gap, []).append(dev)
+    gaps = arrivals(lax.axis_size("seq"), turn)
     block = None
-    for gap, devs in sources.items():
+    for gap in sorted(set(gaps)):
         moved = rights[gap] if gap >= 0 else lefts[-gap]
         if block is None:
             block = moved
         else:
-            mine = jnp.array([dev in devs for dev in range(n)])[me]
+            mine = jnp.array([each == gap for each in gaps])[lax.axis_index("seq")]
             block = jnp.where(mine, moved, block)
     return block
 
@@ -119,9 +118,7 @@
     return lax.dynamic_index_in_dim(placed, place % lax.axis_size("seq"), 0, keepdims=False)
 
 
-def line_send(parts, k, right, left):
-    me = lax.axis_index("seq")
-    to_right, to_left = at_place(parts, me + k), at_place(parts, me - k)
+def line_send(to_right, to_left, right, left):
     if right is not None:
         to_right = (to_right.astype(full) + right.astype(full)).astype(low)
         to_left = (to_left.astype(full) + left.astype(full)).astype(low)
@@ -136,6 +133,29 @@
     )
 
 
+class Doubling:
+    def __init__(self, block, bits):
+        self.blocks, self.order, self.bits = block[None], bits, list(bits)
+        self.away = False
+
+    def go(self):
+        self.here, self.away = swap(self.blocks, "fsdp", self.bits.pop(0)), True
+
+    def land(self, other):
+        other, here = tie(other, self.here)
+        self.blocks, self.away = jnp.concatenate([self.blocks, here]), False
+        return other
+
+    def rows(self):
+        while self.bits or self.away:
+            if not self.away:
+                self.go()
+            self.land(())
+        mask = lax.axis_index("fsdp") ^ jnp.arange(self.blocks.shape[0])
+        spot = sum(((mask // bit) % 2) << i for i, bit in enumerate(self.order))
+        return self.blocks[spot].reshape(-1, self.blocks.shape[2])
+
+
 class LineGather:
     def __init__(self, halves):
         self.rights, self.lefts = [[half] for half in halves], [[half] for half in halves]
@@ -149,6 +169,11 @@
 
     def land(self, h, other):
         spot = self.landed[h] = len(self.rights[h]) - 1
+        if isinstance(other, Doubling):
+            self.rights[h][spot], self.lefts[h][spot] = other.land(
+                (self.rights[h][spot], self.lefts[h][spot])
+            )
+            other = ()
         moved = [(self.rights[part][spot], self.lefts[part][spot]) for part in range(h + 1)]
         moved, other = tie(moved, other)
         for part, (right, left) in enumerate(moved):
@@ -162,29 +187,40 @@
     def ahead(self, h):
         return len(self.rights[h]) - 1 - self.landed[h]
 
+    def choice(self, turn):
+        gaps = arrivals(lax.axis_size("seq"), turn)
+        places = sorted(set(gaps))
+        return jnp.array([places.index(gap) for gap in gaps], jnp.int32)[lax.axis_index("seq")]
+
+    def blocks(self, turn):
+        places = sorted(set(arrivals(lax.axis_size("seq"), turn)))
+        return [
+            [rights[gap] if gap >= 0 else lefts[-gap] for gap in places]
+            for rights, lefts in zip(self.rights, self.lefts)
+        ]
+
     def block(self, turn):
         return [arrived(self.rights[h], self.lefts[h], turn) for h in (0, 1)]
 
 
-def line_scatter(halves, work):
+def line_scatter(count, get, work):
     n = lax.axis_size("seq")
-    me = lax.axis_index("seq")
-    flying = [(None, None)] * len(halves)
+    flying = [(None, None)] * count
     before, given = (), []
     for k in range(n - 1, 0, -1):
-        for h, half in enumerate(halves):
+        for h in range(count):
             if k < n - 1 and h:
                 flying[h], before = tie(flying[h], before)
             elif k < n - 1:
                 flying[h], given = tie(flying[h], given)
-            before = line_send(half, k, *flying[h])
+            before = line_send(get(h, k), get(h, -k), *flying[h])
             flying[h] = line_pass(*before, k)
         if n - 1 - k < len(work):
             given = work[n - 1 - k](before, given)
     sums = []
     flying[0], given = tie(flying[0], given)
-    for half, (right, left) in zip(halves, flying):
-        sums.append(at_place(half, me).astype(full) + (right.astype(full) + left.astype(full)))
+    for h, (right, left) in enumerate(flying):
+        sums.append(get(h, 0).astype(full) + (right.astype(full) + left.astype(full)))
     return jnp.concatenate(sums), given
 
 
@@ -489,15 +525,31 @@
     return (nn(pick[:, :middle], tok_ref[...]) + nn(pick[:, middle:], more_ref[:middle, :])).astype(low)
 
 
+def take_tokens(choices, at_ref, refs, tok_ref, more_ref, sems):
+    for choice in range(choices):
+
+        @pl.when(at_ref[2] == choice)
+        def _():
+            copies = [
+                pltpu.make_async_copy(refs[choice], tok_ref, sems.at[0]),
+                pltpu.make_async_copy(refs[choices + choice], more_ref, sems.at[1]),
+            ]
+            for copy in copies:
+                copy.start()
+            for copy in copies:
+                copy.wait()
+
+
 def experts_kernel(
-    few, pair, at_ref, tok_ref, more_ref, slot_ref, member_ref, router_ref, wgu_ref, wd_ref, *refs
+    few, pair, choices, at_ref, slot_ref, member_ref, router_ref, wgu_ref, wd_ref, *refs
 ):
-    part_ref, x_ref, gu_ref, gates_ref, acc, gates_all, down = refs[-7:]
+    part_ref, x_ref, gu_ref, gates_ref, acc, gates_all, down, tok_ref, more_ref, sems = refs[-10:]
     step, steps = pl.program_id(0), pl.num_programs(0)
     slots = x_ref.shape[2]
 
     @pl.when(step == 0)
     def _():
+        take_tokens(choices, at_ref, refs, tok_ref, more_ref, sems)
         member = member_ref[...] > 0
         logits = [nt(router_ref[...], ref[...]) for ref in (tok_ref, more_ref)]
         chosen = jnp.where(member, jnp.concatenate(logits, axis=1), masked_score)
@@ -531,17 +583,21 @@
 
 
 def back_kernel(
-    few, pair, at_ref, tok_ref, more_ref, slot_ref, gates_ref, mix_ref, router_ref, gu_ref, wgu_ref, wd_ref, *refs
+    few, pair, choices, at_ref, slot_ref, gates_ref, router_ref, gu_ref, wgu_ref, wd_ref, *refs
 ):
-    part_ref, d_ref, dgu_ref, act_ref, dlog_ref, acc, dlog_all, down = refs[-8:]
+    part_ref, d_ref, dgu_ref, act_ref, dlog_ref, acc, dlog_all, down, tok_ref, more_ref, sems = refs[-11:]
     step, steps = pl.program_id(0), pl.num_programs(0)
     slots, hidden = gu_ref.shape[2], gu_ref.shape[3] // 2
 
     @pl.when(step == 0)
     def _():
+        take_tokens(choices, at_ref, refs, tok_ref, more_ref, sems)
         dlog_all[...] = jnp.zeros_like(dlog_all)
         acc[...] = jnp.zeros_like(acc)
 
+    middle, count = tok_ref.shape[0], slot_ref.shape[1]
+    mix = more_ref[middle : middle + 2, :count].astype(full)
+    mix = mix[0:1, :] + mix[1:2, :]
     place = lax.broadcasted_iota(jnp.int32, (slots, 1), 0)
     puts, dxs = [], []
     for i in range(pair):
@@ -560,7 +616,7 @@
         act = silu * u
         d_gate = jnp.sum(d_act * act, axis=1, keepdims=True)
         d_gate = jnp.sum(jnp.where(here, d_gate, 0.0), axis=0, keepdims=True)
-        dlog_all[pl.ds(e, 1), :] = gate_row * (d_gate - mix_ref[...])
+        dlog_all[pl.ds(e, 1), :] = gate_row * (d_gate - mix)
         act_ref[i, 0] = (act * gate).astype(low)
         d_act = d_act * gate
         d_g = (d_act * u * (sig + silu * (1.0 - sig))).astype(low)
@@ -602,7 +658,8 @@
         grid_spec=pltpu.PrefetchScalarGridSpec(
             num_scalar_prefetch=1,
             grid=(experts,),
-            in_specs=in_specs + [pl.BlockSpec(memory_space=pl.ANY)] * len(buffers),
+            in_specs=in_specs
+            + [pl.BlockSpec(memory_space=pl.ANY)] * (len(inputs) + len(buffers) - len(in_specs)),
             out_specs=out_specs,
             scratch_shapes=scratch,
         ),
@@ -624,15 +681,14 @@
     experts, width, columns = weights.shape
     hidden = columns // 3
     pair = 1 + (experts + 1) % 2
-    count = 2 * tokens[0].shape[0]
+    count = slot_of.shape[1]
     total_experts = member.shape[0]
     return shard_call(
-        functools.partial(experts_kernel, few, pair),
+        functools.partial(experts_kernel, few, pair, len(tokens[0])),
         "experts_forward",
         at,
-        [*tokens, slot_of, member, router, weights, weights],
+        [slot_of, member, router, weights, weights, *tokens[0], *tokens[1]],
         [
-            *(same(*half.shape) for half in tokens),
             same(experts, count),
             same(total_experts, count),
             same(total_experts, width),
@@ -655,30 +711,30 @@
             pltpu.VMEM((count, width), full),
             pltpu.VMEM((total_experts, count), full),
             pltpu.VMEM((pair, hidden, width), low),
+            *(pltpu.VMEM(half[0].shape, low) for half in tokens),
+            pltpu.SemaphoreType.DMA((2,)),
         ],
         experts // pair,
     )
 
 
 def experts_backward(
-    turn, devs, at, d_tokens, slot_of, gates, mix_dot, router, gu, weights, few, buffers
+    turn, devs, at, d_tokens, slot_of, gates, router, gu, weights, few, buffers
 ):
     experts, width, columns = weights.shape
     hidden = columns // 3
     pair = 1 + (experts + 1) % 2
-    count = 2 * d_tokens[0].shape[0]
+    count = slot_of.shape[1]
     slots = gu.shape[2]
     lines = router.shape[0]
     return shard_call(
-        functools.partial(back_kernel, few, pair),
+        functools.partial(back_kernel, few, pair, len(d_tokens[0])),
         "experts_backward",
         at,
-        [*d_tokens, slot_of, gates, mix_dot, router, gu, weights, weights],
+        [slot_of, gates, router, gu, weights, weights, *d_tokens[0], *d_tokens[1]],
         [
-            *(same(*half.shape) for half in d_tokens),
             same(experts, count),
             same(experts, count),
-            same(1, count),
             same(lines, width),
             in_turn(pair, turn, slots, 2 * hidden),
             *weight_specs(pair, width, hidden),
@@ -702,6 +758,8 @@
             pltpu.VMEM((count, width), full),
             pltpu.VMEM((lines, count), full),
             pltpu.VMEM((pair, hidden, width), low),
+            *(pltpu.VMEM(half[0].shape, low) for half in d_tokens),
+            pltpu.SemaphoreType.DMA((2,)),
         ],
         experts // pair,
     )
@@ -821,11 +879,11 @@
     small = jnp.concatenate([gain_one[:, None], gain_two[:, None], w_router], axis=1)
     small = jnp.pad(small, ((0, 0), (0, -small.shape[1] % 128)))
     first = lax.all_gather(
-        jnp.concatenate([own_qkv, small, w_out], axis=1), "fsdp", axis=0, tiled=True
-    )
+        jnp.concatenate([own_qkv, small], axis=1), "fsdp", axis=0, tiled=True
+    )
+    out = Doubling(w_out, order_a[1:] + order_a[:1])
     full_qkv = first[:, :group_w]
     small = first[:, group_w : group_w + 2 + expert_total]
-    full_out = first[:, -width:]
     full_g1 = small[:, 0].astype(full)
     full_g2 = small[:, 1].astype(full)
     router = small[:, 2:].T
@@ -834,15 +892,6 @@
     valid_rows = valid_mask.reshape(shard_len).astype(full)
 
     hidden_w = w_gate.shape[2]
-    down_chunks = [
-        w_down[:, :, start : start + hidden_w] for start in range(0, width, hidden_w)
-    ]
-    weights = lax.all_gather(
-        jnp.concatenate([w_gate, w_up, jnp.concatenate(down_chunks, axis=1)], axis=2),
-        "fsdp",
-        axis=1,
-        tiled=True,
-    )
 
     routes_low = jnp.concatenate([routes.reshape(shard_len, top_count).T, valid_mask], axis=0)
     routes_low = jnp.pad(
@@ -857,16 +906,20 @@
     heads = jnp.zeros((n, kv_here, GROUP + 2, HEAD_DIM, shard_len), low)
     routes_all = []
     line = LineGather(halves)
+    line.go(0)
+    line.go(1)
+    out.go()
     for turn in range(n):
         if turn:
             line.land(0, heads if turn > 1 else ())
-            if turn < n - 1:
-                line.go(0)
+        if 0 < turn < n - 1:
+            line.go(0)
+        if turn == 2:
+            line.land(1, out)
+            out.go()
+        elif turn:
             line.land(1, ())
-            if turn < n - 1:
-                line.go(1)
-        else:
-            line.go(0)
+        if 0 < turn < n - 1:
             line.go(1)
         block = jnp.concatenate(line.block(turn))
         start = order[turn] * shard_len
@@ -890,6 +943,16 @@
         normed_one = lax.dynamic_update_slice_in_dim(normed_one, normed, start, 0)
         routes_all.append(block[shard_len : shard_len + top_count + 1, :shard_len])
 
+    down_chunks = [
+        w_down[:, :, start : start + hidden_w] for start in range(0, width, hidden_w)
+    ]
+    weights = lax.all_gather(
+        jnp.concatenate([w_gate, w_up, jnp.concatenate(down_chunks, axis=1)], axis=2),
+        "fsdp",
+        axis=1,
+        tiled=True,
+    )
+
     routes_all = jnp.stack(routes_all).astype(jnp.int32)
     valid_count = total(jnp.sum(routes_all[:, top_count]).astype(full).reshape(1, 1), "fsdp")[0, 0]
     expert_ids = jnp.arange(expert_total, dtype=jnp.int32)
@@ -905,8 +968,10 @@
     key_rows = jnp.swapaxes(key, 1, 2)
     value_rows = jnp.swapaxes(value, 1, 2)
     attended, out_heads, lse = attention_forward(heads, key_rows, value, limit)
+    attended = out.land(attended)
     moved = exchange(attended)
-    moved, slot_of, member, own_router = tie(moved, slot_of, member, own_router)
+    full_out = out.rows()
+    moved, slot_of, member, own_router, full_out = tie(moved, slot_of, member, own_router, full_out)
     attn_rows = by_place(nearest(*moved)).reshape(HEADS * HEAD_DIM, shard_len)
     projected = dot("kt,kd->td", attn_rows, full_out)
     hidden = x_low.astype(full) + resid_mult * projected
@@ -929,13 +994,14 @@
             line_slots = slot_of[turn]
         tokens.append(line.block(turn))
         *buffers, shard_gates = experts_forward(
-            turn, n, jnp.stack([order[turn], me]), tokens[turn], line_slots, member[turn],
-            router, weights, w_down.shape[1], slots, buffers,
+            turn, n, jnp.stack([order[turn], me, line.choice(turn)]), line.blocks(turn), line_slots,
+            member[turn], router, weights, w_down.shape[1], slots, buffers,
         )
         gates.append(shard_gates)
         other = shard_gates
     mix_parts, expert_in, gate_up = buffers
-    mixture, _ = line_scatter([mix_parts[:, :middle], mix_parts[:, middle:]], ())
+    cuts = (slice(0, middle), slice(middle, None))
+    mixture, _ = line_scatter(2, lambda h, shift: at_place(mix_parts[:, cuts[h]], me + shift), ())
     output_f32 = hidden + resid_mult * mixture
     activations = output_f32.astype(low).reshape(1, shard_len, width)
     error_rows = output_f32 - teacher.astype(full).reshape(shard_len, width)
@@ -963,12 +1029,9 @@
         else:
             line.go(0)
             line.go(1)
-        d_block = line.block(turn)
-        mix_dot = d_block[1][middle : middle + 2, :shard_len].astype(full)
-        mix_dot = jnp.sum(mix_dot, axis=0, keepdims=True)
         *buffers, shard_logits = experts_backward(
-            turn, n, jnp.stack([order[turn], me]), d_block, slot_of[turn], gates[turn], mix_dot,
-            own_router, gate_up, weights, w_down.shape[1], buffers,
+            turn, n, jnp.stack([order[turn], me, line.choice(turn)]), line.blocks(turn), slot_of[turn],
+            gates[turn], own_router, gate_up, weights, w_down.shape[1], buffers,
         )
         d_logits.append(shard_logits)
     d_parts, d_rows, d_gate_up, act_low = buffers
@@ -987,21 +1050,22 @@
         return make
 
     d_normed_two, grads = line_scatter(
-        [d_parts], (some_grads(0, cut), some_grads(cut, experts_here))
+        1,
+        lambda h, shift: at_place(d_parts, me + shift),
+        (some_grads(0, cut), some_grads(cut, experts_here)),
     )
     expert_sum = lax.psum_scatter(grads[0], "fsdp", scatter_dimension=1, tiled=True)
 
     d_hidden_norm, gain_two_part = norm_two_pull(d_normed_two)
     d_hidden = d_out + d_hidden_norm
     d_proj = (resid_mult * d_hidden).astype(low)
+    d_attended = dot("kd,td->kt", full_out, d_proj).astype(low)
+    moved = exchange(d_attended.reshape(n, heads_w, shard_len))
+    d_proj, _ = tie(d_proj, d_attended)
     out_pairs = out_grads(mine.reshape(1), attn_rows, d_proj, order_a, order_b)
     out_sums = [Halving(*pair, bits) for pair, bits in zip(out_pairs, (order_a, order_b))]
     for each in out_sums:
         each.go()
-    d_attended = dot("kd,td->kt", full_out, d_proj).astype(low)
-    (d_attended,) = land(out_sums, d_attended)
-    moved = exchange(d_attended.reshape(n, heads_w, shard_len))
-    for each in out_sums:
         each.add()
     router_part = sum(
         dot("td,et->de", half, half_logits)
@@ -1031,7 +1095,13 @@
     d_turned = jnp.concatenate([query_grad, key_grad[:, None]], axis=1).astype(full)
     d_turned = rotate(d_turned, cosine, -sine_vals).astype(low)
     d_qkv = jnp.concatenate([d_turned, value_grad[:, None]], axis=1).reshape(group_w, seq_len)
-    d_parts = dot("ct,dc->td", d_qkv, full_qkv).astype(low).reshape(n, shard_len, width)
+
+    def d_part(rows, shift):
+        start = (me + shift) % n * shard_len
+        rows = lax.dynamic_slice_in_dim(rows, start, shard_len, 1)
+        return dot("ct,dc->td", rows, full_qkv).astype(low)
+
+    d_parts = {shift: d_part(d_qkv, shift) for shift in {1, n - 1}}
     (d_parts,) = land(out_sums, d_parts)
     for each in out_sums:
         each.add()
@@ -1039,14 +1109,21 @@
     out_sum = jnp.concatenate([each.finish() for each in out_sums], axis=1).astype(low)
     out_rows = out_sum.shape[0] // n
     out_parts = jnp.swapaxes(out_sum.reshape(out_sum.shape[0], n, width // n), 0, 1)
-    d_parts = [
-        d_parts[:, :middle],
-        jnp.concatenate([d_parts[:, middle:], out_parts.reshape(n, out_rows, width)], axis=1),
-    ]
+    out_parts = out_parts.reshape(n, out_rows, width)
+
+    def get(h, shift):
+        part = d_parts[shift % n]
+        if h == 0:
+            return part[:middle]
+        return jnp.concatenate([part[middle:], at_place(out_parts, me + shift)])
+
     sums = {}
 
     def first_work(before, _):
         rows, _ = tie(d_qkv, before)
+        for shift in range(n):
+            if shift not in d_parts:
+                d_parts[shift] = d_part(rows, shift)
         qkv_part = jnp.concatenate(
             [dot("td,ct->dc", normed_one, rows).astype(low), own_columns], axis=1
         )
@@ -1060,7 +1137,7 @@
         sums["qkv"].go()
         return sums["qkv"].send
 
-    ended, _ = line_scatter(d_parts, (first_work, next_work, next_work))
+    ended, _ = line_scatter(2, get, (first_work, next_work, next_work))
     qkv_sum = sums["qkv"]
     d_normed_one = ended[:shard_len]
     (ended,) = land([qkv_sum], ended)
@@ -1094,19 +1171,18 @@
     gate_grad, up_grad = gate_up_grad[:, :, :hidden_w], gate_up_grad[:, :, hidden_w:]
     qkv_grad = jnp.zeros((w_qkv.shape[0], QKV_W), full)
     out_grad = jnp.zeros((w_out.shape[0], width), full)
-    rest = 0.0
+    rest = gain_sum = 0.0
     for turn in range(n):
         block = arrived(rights, lefts, turn).astype(full)
-        place = order[turn]
-        qkv_grad = lax.dynamic_update_slice_in_dim(
-            qkv_grad, block[:, :group_w], place * group_w, 1
-        )
-        out_grad = lax.dynamic_update_slice_in_dim(
-            out_grad, block[:, -(width // n) :], place * (width // n), 1
-        )
+        own_part, out_part = block[:, :group_w], block[:, -(width // n) :]
+        start = order[turn] * group_w
+        qkv_grad = lax.dynamic_update_slice_in_dim(qkv_grad, own_part, start, 1)
+        out_grad = lax.dynamic_update_slice_in_dim(out_grad, out_part, order[turn] * (width // n), 1)
+        own_part = own_part * lax.dynamic_slice_in_dim(w_qkv, start, group_w, 1).astype(full)
+        gain_sum = gain_sum + jnp.sum(own_part, axis=1)
         rest = rest + block[:, group_w : -(width // n)]
     router_grad, gain_two_grad = rest[:, :expert_total], rest[:, expert_total]
-    gain_one_grad = jnp.sum(qkv_grad * w_qkv.astype(full), axis=1) / gain_one.astype(full)
+    gain_one_grad = gain_sum / gain_one.astype(full)
     for _ in range(4):
         squares = loss_steps.send(squares)
     loss_value = squares[0, 0] / (valid_count * width)

time: 1170 us -> 1210 us (1.034)
  waiting for transfers between devices: 249 us -> 290 us
  starting transfers between devices: 234 us -> 215 us
  other arithmetic: 139 us -> 121 us
  local copies, waits for them, and re-layouts: 79.1 us -> 94.6 us
    ppermute x21, waiting for transfers between devices: 59.9 us -> 87.5 us  [line_move(): lax.ppermute(left, 'seq', [(i, i - 1) for i in range(1, n - k + 1)])]
    select_n x16 -> x6, other arithmetic: 35.1 us -> 12.9 us  [arrived(): block = jnp.where(mine, moved, block)]
    ppermute x15, waiting for transfers between devices: 96.5 us -> 117 us  [line_pass(): lax.ppermute(to_right, 'seq', [(i, i + 1) for i in range(n - k)])]
    ppermute x15, starting transfers between devices: 89.5 us -> 71.8 us  [line_pass(): lax.ppermute(to_right, 'seq', [(i, i + 1) for i in range(n - k)])]
    ppermute x6, waiting for transfers between devices: 27.8 us -> 14.2 us  [exchange(): lax.ppermute(to_right, 'seq', [(i, i + k) for i in range(n - k)])]
    unnamed x251 -> x319, local copies, waits for them, and re-layouts: 22.3 us -> 30.3 us
    dot_general x17 -> x20, matrix products: 38.5 us -> 43.1 us  [dot(): return jnp.einsum(spec, left, right, preferred_element_type=full)]
    ppermute x17 -> x20, starting transfers between devices: 20.2 us -> 24.5 us  [swap(): lax.ppermute(value, axis, [(i, i ^ bit) for i in range(lax.axis_size(axis...]
  transfers between devices with their start and end apart: 104 -> 107, of which waited for: 38 -> 42; matrix products, arithmetic and copies ran while one was open for 16% -> 16% of each run, Pallas kernels for 26% -> 26%
where the time goes in v12:
time: 1210 us; the launch traced here: 1190 us
  Pallas kernels  391 us (32%)
  waiting for transfers between devices  290 us (24%)
  starting transfers between devices  215 us (18%)
  other arithmetic  121 us (10%)
  local copies, waits for them, and re-layouts  94.6 us (8%)
  matrix products  43.1 us (4%)
  between operations  40.3 us (3%)
    pallas_call x8, Pallas kernels, shard_call(): pl.pallas_call(kernel, grid_spec=pltpu.PrefetchScalarGridSpec(num_scalar_...  234 us
    ppermute x15, waiting for transfers between devices, line_pass(): lax.ppermute(to_right, 'seq', [(i, i + 1) for i in range(n - k)])  117 us
    ppermute x21, waiting for transfers between devices, line_move(): lax.ppermute(left, 'seq', [(i, i - 1) for i in range(1, n - k + 1)])  87.5 us
    ppermute x15, starting transfers between devices, line_pass(): lax.ppermute(to_right, 'seq', [(i, i + 1) for i in range(n - k)])  71.8 us
    pallas_call x1, Pallas kernels, attention_backward(): pl.pallas_call(functools.partial(backward_kernel, seq_len, query_rows, ke...  58.4 us
    pallas_call x2, Pallas kernels, weight_grads(): pl.pallas_call(functools.partial(grads_kernel, few), grid=(stop - first,)...  50.9 us
    ppermute x21, starting transfers between devices, line_move(): lax.ppermute(right, 'seq', [(i, i + 1) for i in range(k - 1, n - 1)])  49.5 us
    dot_general x20, matrix products, dot(): return jnp.einsum(spec, left, right, preferred_element_type=full)  43.1 us
  transfers between devices with their start and end apart: 107, of which 42 were waited for; matrix products, arithmetic and copies ran while one was open for 16% of the time, Pallas kernels for 26%

profile of v12, /device:TPU:0, one launch (start us, length us, event | category | flops | bytes accessed | tf_op | source)
XLA Modules:
  0.0 1194.2 jit_solution(8609254267265598998)
XLA Ops:
  14.2 6.4 maximum_maximum_fusion
  22.2 6.0 collective-permute-start
  31.1 5.5 collective-permute-start.2
  62.1 6.5 collective-permute-done.3
  75.5 26.3 %collective-permute-done.7 = bf16[272,1536]{1,0:T(8,128)(2,1)} collective-permute-done((bf16[272,1536]{1,0:T(8,128)(2,1)}, bf16[272,1536]{1,0:T(8,128)(2,1)}, u32[]{:S(2)}, u32[]{:S(2)}) %collective-permute-start.7) | collective-permute-done | bytes 835616 | tf_op jit(solution)/shard_map/ppermute | solution.py:68
  124.6 11.1 collective-permute-done.10
  135.8 15.2 %collective-permute-done.12 = bf16[272,1536]{1,0:T(8,128)(2,1)S(1)} collective-permute-done((bf16[272,1536]{1,0:T(8,128)(2,1)}, bf16[272,1536]{1,0:T(8,128)(2,1)S(1)}, u32[]{:S(2)}, u32[]{:S(2)}) %collective-permute-start.12) | collective-permute-done | bytes 835616 | tf_op jit(solution)/shard_map/ppermute | solution.py:68
  165.0 41.5 %attention_forward.1 = (bf16[4,384,512]{2,1,0:T(8,128)(2,1)}, f32[2,3,64,2048]{3,2,1,0:T(8,128)}, f32[2,3,1,2048]{3,2,1,0:T(1,128)}) custom-call(s32[1,2048]{1,0:T(1,128)} %bitcast.301, bf16[4,2,5,64,512]{4,3,2,1,0:T(8,128)(2,1)} %copy-done.33, bf16[2,2048,64]{2,1,0:T(8,128)(2,1)} %copy.167.k_ref, bf16[2,64,2048]{2,1,0:T(8,128)(2,1)} %copy.168.vt_ref), custom_call_target="tpu_custom_call" | custom-call | tf_op jit(solution)/shard_map/attention_forward/pallas_call | solution.py:381
  243.0 17.0 %collective-permute-done.18 = bf16[384,512]{1,0:T(8,128)(2,1)} collective-permute-done((bf16[384,512]{1,0:T(8,128)(2,1)S(1)}, bf16[384,512]{1,0:T(8,128)(2,1)}, u32[]{:S(2)}, u32[]{:S(2)}) %collective-permute-start.18) | collective-permute-done | bytes 393248 | tf_op jit(solution)/shard_map/ppermute | solution.py:244
  263.7 5.5 multiply_reduce_fusion.3
  275.3 5.4 collective-permute-start.25
  282.9 7.2 collective-permute-done.21.refs_1_
  290.2 5.3 collective-permute-done.22.refs_0_.refs_1_
  298.4 7.7 collective-permute-done.25.refs_3_
  306.1 6.3 collective-permute-done.26.refs_2_.refs_4_
  321.9 25.4 %experts_forward.4 = (bf16[4,512,1536]{2,1,0:T(8,128)(2,1)}, bf16[10,4,160,1536]{3,2,1,0:T(8,128)(2,1)}, bf16[10,4,160,1024]{3,2,1,0:T(8,128)(2,1)}, f32[10,512]{1,0:T(8,128)S(1)}) custom-call(s32[3]{0:T(128)S(1)} %get-tuple-element.587.at_ref, s32[10,512]{1,0:T(8,128)S(1)} %copy-done.16, f32[40,512]{1,0:T(8,128)S(1)} %copy-done.15, ...), custom_call_target="tpu_custom_call" | custom-call | tf_op jit(solution)/shard_map/experts_forward/pallas_call | solution.py:656
  355.4 25.5 %experts_forward.5 = (bf16[4,512,1536]{2,1,0:T(8,128)(2,1)}, bf16[10,4,160,1536]{3,2,1,0:T(8,128)(2,1)}, bf16[10,4,160,1024]{3,2,1,0:T(8,128)(2,1)}, f32[10,512]{1,0:T(8,128)S(1)}) custom-call(s32[3]{0:T(128)S(1)} %get-tuple-element.588.at_ref, ...), custom_call_target="tpu_custom_call", output_to_operand_aliasing={{0}: (10, {}), {1}: (11, {}), {2}: (12, {})} | custom-call | tf_op jit(solution)/shard_map/experts_forward/pallas_call | solution.py:656
  384.1 28.3 %experts_forward.6 = (bf16[4,512,1536]{2,1,0:T(8,128)(2,1)}, bf16[10,4,160,1536]{3,2,1,0:T(8,128)(2,1)}, bf16[10,4,160,1024]{3,2,1,0:T(8,128)(2,1)}, f32[10,512]{1,0:T(8,128)S(1)}) custom-call(s32[3]{0:T(128)S(1)} %get-tuple-element.589.at_ref, ...), custom_call_target="tpu_custom_call", output_to_operand_aliasing={{0}: (12, {}), {1}: (13, {}), {2}: (14, {})} | custom-call | tf_op jit(solution)/shard_map/experts_forward/pallas_call | solution.py:656
  412.5 25.4 %experts_forward.7 = (bf16[4,512,1536]{2,1,0:T(8,128)(2,1)}, bf16[10,4,160,1536]{3,2,1,0:T(8,128)(2,1)}, bf16[10,4,160,1024]{3,2,1,0:T(8,128)(2,1)}, f32[10,512]{1,0:T(8,128)S(1)}) custom-call(s32[3]{0:T(128)S(1)} %get-tuple-element.586.at_ref, s32[10,512]{1,0:T(8,128)S(1)} %copy-done.18, ...), custom_call_target="tpu_custom_call", output_to_operand_aliasing={{0}: (14, {}), {1}: (15, {}), {2}: (16, {})} | custom-call | tf_op jit(solution)/shard_map/experts_forward/pallas_call | solution.py:656
  450.2 14.6 %collective-permute-done.33 = bf16[256,1536]{1,0:T(8,128)(2,1)S(1)} collective-permute-done((bf16[256,1536]{1,0:T(8,128)(2,1)S(1)}, bf16[256,1536]{1,0:T(8,128)(2,1)S(1)}, u32[]{:S(2)}, u32[]{:S(2)}) %collective-permute-start.33) | collective-permute-done | bytes 786464 | tf_op jit(solution)/shard_map/ppermute | solution.py:131
  470.4 11.3 collective-permute-done.39
  487.2 11.3 collective-permute-done.35
  506.8 8.6 collective-permute-done.41
  537.2 8.2 collective-permute-done.43
  563.5 32.3 %experts_backward.4 = (bf16[4,512,1536]{2,1,0:T(8,128)(2,1)}, bf16[10,4,160,1536]{3,2,1,0:T(8,128)(2,1)}, bf16[10,4,160,1024]{3,2,1,0:T(8,128)(2,1)}, bf16[10,4,...) custom-call(s32[3]{0:T(128)S(1)} %copy-done.29, s32[10,512]{1,0:T(8,128)S(1)} %copy-done.17, f32[10,512]{1,0:T(8,128)S(1)} %copy-done.23, ...), custom_call_target="tpu_custom_call" | custom-call | tf_op jit(solution)/shard_map/experts_backward/pallas_call | solution.py:656
  600.1 32.3 %experts_backward.5 = (bf16[4,512,1536]{2,1,0:T(8,128)(2,1)}, bf16[10,4,160,1536]{3,2,1,0:T(8,128)(2,1)}, bf16[10,4,160,1024]{3,2,1,0:T(8,128)(2,1)}, bf16[10,4,...) custom-call(s32[3]{0:T(128)S(1)} %get-tuple-element.588.at_ref, ...), custom_call_target="tpu_custom_call", output_to_operand_aliasing={{0}: (11, {}), {1}: (12, {}), {2}: (13, {}), {3}: (14, {})} | custom-call | tf_op jit(solution)/shard_map/experts_backward/pallas_call | solution.py:656
  637.7 32.2 %experts_backward.6 = (bf16[4,512,1536]{2,1,0:T(8,128)(2,1)}, bf16[10,4,160,1536]{3,2,1,0:T(8,128)(2,1)}, bf16[10,4,160,1024]{3,2,1,0:T(8,128)(2,1)}, bf16[10,4,...) custom-call(s32[3]{0:T(128)S(1)} %copy-done.27, ...), custom_call_target="tpu_custom_call", output_to_operand_aliasing={{0}: (13, {}), {1}: (14, {}), {2}: (15, {}), {3}: (16, {})} | custom-call | tf_op jit(solution)/shard_map/experts_backward/pallas_call | solution.py:656
  674.4 32.3 %experts_backward.7 = (bf16[4,512,1536]{2,1,0:T(8,128)(2,1)}, bf16[10,4,160,1536]{3,2,1,0:T(8,128)(2,1)}, bf16[10,4,160,1024]{3,2,1,0:T(8,128)(2,1)}, bf16[10,4,...) custom-call(s32[3]{0:T(128)S(1)} %get-tuple-element.586.at_ref, ...), custom_call_target="tpu_custom_call", output_to_operand_aliasing={{0}: (15, {}), {1}: (16, {}), {2}: (17, {}), {3}: (18, {})} | custom-call | tf_op jit(solution)/shard_map/experts_backward/pallas_call | solution.py:656
  710.0 6.4 collective-permute-start.60
  717.4 25.5 %weight_grads.2.refs_0_ = bf16[10,1536,1536]{2,1,0:T(8,128)(2,1)} custom-call(bf16[10,640,1536]{2,1,0:T(8,128)(2,1)} %bitcast.261, bf16[10,640,1024]{2,1,0:T(8,128)(2,1)} %bitcast.265, bf16[10,640,512]{2,1,0:T(8,128)(2,1)} %bitcast.267, bf16[10,640,1536]{2,1,0:T(8,128)(2,1)} %bitcast.263), custom_call_target="tpu_custom_call" | custom-call | tf_op jit(solution)/shard_map/weight_grads/pallas_call | solution.py:829
  749.2 5.5 collective-permute-start.62
  756.5 25.4 %weight_grads.3 = bf16[10,1536,1536]{2,1,0:T(8,128)(2,1)} custom-call(bf16[10,640,1536]{2,1,0:T(8,128)(2,1)} %bitcast.262, bf16[10,640,1024]{2,1,0:T(8,128)(2,1)} %bitcast.266, bf16[10,640,512]{2,1,0:T(8,128)(2,1)} %bitcast.268, bf16[10,640,1536]{2,1,0:T(8,128)(2,1)} %bitcast.264, ...), custom_call_target="tpu_custom_call", output_to_operand_aliasing={{}: (4, {})} | custom-call | tf_op jit(solution)/shard_map/weight_grads/pallas_call | solution.py:829
  785.5 8.4 collective-permute-start.64
  795.8 22.8 %collective-permute-done.64 = bf16[512,1536]{1,0:T(8,128)(2,1)} collective-permute-done((bf16[512,1536]{1,0:T(8,128)(2,1)S(1)}, bf16[512,1536]{1,0:T(8,128)(2,1)}, u32[]{:S(2)}, u32[]{:S(2)}) %collective-permute-start.64) | collective-permute-done | bytes 1572896 | tf_op jit(solution)/shard_map/ppermute | solution.py:131
  818.5 5.5 collective-permute-done.65
  847.4 6.1 multiply_convert_fusion
  856.3 6.7 out_grads.1
  891.8 6.3 collective-permute-done.70.refs_3_
  898.1 9.9 collective-permute-done.71.refs_4_
  908.0 14.7 %collective-permute-done.72.refs_5_ = bf16[384,512]{1,0:T(8,128)(2,1)} collective-permute-done((bf16[384,512]{1,0:T(8,128)(2,1)}, bf16[384,512]{1,0:T(8,128)(2,1)}, u32[]{:S(2)}, u32[]{:S(2)}) %collective-permute-start.72) | collective-permute-done | bytes 393248 | tf_op jit(solution)/shard_map/ppermute | solution.py:244
  931.5 58.4 %attention_backward.1 = (bf16[2,3,64,2048]{3,2,1,0:T(8,128)(2,1)}, bf16[2,64,2048]{2,1,0:T(8,128)(2,1)}, bf16[2,64,2048]{2,1,0:T(8,128)(2,1)}) custom-call(s32[1]{0:T(128)} %bitcast.54.me_ref, s32[1,2048]{1,0:T(1,128)} %bitcast.302, bf16[4,2,5,64,512]{4,3,2,1,0:T(8,128)(2,1)} %copy-done.33, bf16[2,2048,64]{2,1,0:T(8,128)(2,1)} %copy.167.k_ref, ...), custom_call_target="tpu_custom_call" | custom-call | tf_op jit(solution)/shard_map/attention_backward/pallas_call | solution.py:464
  1054.4 10.2 collective-permute-done.88
  1066.3 7.0 collective-permute-start.91
  1073.3 11.3 collective-permute-done.86
  1086.4 7.0 collective-permute-start.93
  1105.1 11.1 collective-permute-done.93
  1122.4 8.9 collective-permute-start.95
  1153.9 5.4 collective-permute-done.99
  (715 shorter events, 430.9 us)
Async XLA Ops:
  7.2 98.4 %all-gather.3.cloned.1.call-start = ((), (), s32[]{:S(2)}) async-start(), calls=%async_computation.1 | async-start | bytes 2654208 | tf_op jit(solution)/shard_map/all_gather | solution.py:881
  11.4 306.6 %all-gather.5.cloned.1.call-start = ((), (), s32[]{:S(2)}) async-start(), calls=%async_computation.2 | async-start | bytes 53084160 | tf_op jit(solution)/shard_map/all_gather | solution.py:949
  20.6 1118.9 %reduce-scatter.2.cloned.1.call-start = ((), (), s32[]{:S(2)}) async-start(), calls=%async_computation.3 | async-start | bytes 53084160 | tf_op jit(solution)/shard_map/reduce_scatter | solution.py:1057
  22.2 35.6 %collective-permute-start = (bf16[256,1536]{1,0:T(8,128)(2,1)S(1)}, bf16[256,1536]{1,0:T(8,128)(2,1)}, u32[]{:S(2)}, u32[]{:S(2)}) collective-permute-start(bf16[256,1536]{1,0:T(8,128)(2,1)S(1)} %get-tuple-element.529), channel_id=1, source_target_pairs={{0,1},{1,2},{2,3},{4,5},{5,6},{6,7},{8,9},{9,10},{10,11},{12,13},{... | collective-permute-start | bytes 2359304 | tf_op jit(solution)/shard_map/ppermute | solution.py:67
  37.9 37.6 %collective-permute-start.8 = (bf16[1,192,1536]{2,1,0:T(8,128)(2,1)}, bf16[1,192,1536]{2,1,0:T(8,128)(2,1)S(1)}, u32[]{:S(2)}, u32[]{:S(2)}) collective-permute-start(bf16[1,192,1536]{2,1,0:T(8,128)(2,1)} %bitcast.15), channel_id=1, source_target_pairs={{0,8},{4,12},{8,0},{12,4},{16,24},{20,28},{24,16},{28,20},{1,9},{5... | collective-permute-start | bytes 1769480 | tf_op jit(solution)/shard_map/ppermute | solution.py:249
  57.9 55.3 %collective-permute-start.4 = (bf16[256,1536]{1,0:T(8,128)(2,1)}, bf16[256,1536]{1,0:T(8,128)(2,1)}, u32[]{:S(2)}, u32[]{:S(2)}) collective-permute-start(bf16[256,1536]{1,0:T(8,128)(2,1)} %collective-permute-done), channel_id=1, source_target_pairs={{1,2},{2,3},{5,6},{6,7},{9,10},{10,11},{13,14},{14,15},{17,18},{18... | collective-permute-start | bytes 2359304 | tf_op jit(solution)/shard_map/ppermute | solution.py:67
  59.5 53.7 %collective-permute-start.5 = (bf16[256,1536]{1,0:T(8,128)(2,1)}, bf16[256,1536]{1,0:T(8,128)(2,1)}, u32[]{:S(2)}, u32[]{:S(2)}) collective-permute-start(bf16[256,1536]{1,0:T(8,128)(2,1)} %collective-permute-done.1), channel_id=1, source_target_pairs={{1,0},{2,1},{5,4},{6,5},{9,8},{10,9},{13,12},{14,13},{17,16},{18,1... | collective-permute-start | bytes 2359304 | tf_op jit(solution)/shard_map/ppermute | solution.py:68
  68.6 33.2 %collective-permute-start.7 = (bf16[272,1536]{1,0:T(8,128)(2,1)}, bf16[272,1536]{1,0:T(8,128)(2,1)}, u32[]{:S(2)}, u32[]{:S(2)}) collective-permute-start(bf16[272,1536]{1,0:T(8,128)(2,1)} %collective-permute-done.3), channel_id=1, source_target_pairs={{1,0},{2,1},{5,4},{6,5},{9,8},{10,9},{13,12},{14,13},{17,16},{18,1... | collective-permute-start | bytes 2506760 | tf_op jit(solution)/shard_map/ppermute | solution.py:68
  104.0 102.5 %collective-permute-start.13 = (bf16[2,192,1536]{2,1,0:T(8,128)(2,1)}, bf16[2,192,1536]{2,1,0:T(8,128)(2,1)}, u32[]{:S(2)}, u32[]{:S(2)}) collective-permute-start(bf16[2,192,1536]{2,1,0:T(8,128)(2,1)} %pad_maximum_fusion.10), channel_id=1, source_target_pairs={{0,16},{4,20},{8,24},{12,28},{16,0},{20,4},{24,8},{28,12},{1,17},{... | collective-permute-start | bytes 3538952 | tf_op jit(solution)/shard_map/ppermute | solution.py:249
  115.9 35.0 %collective-permute-start.12 = (bf16[272,1536]{1,0:T(8,128)(2,1)}, bf16[272,1536]{1,0:T(8,128)(2,1)S(1)}, u32[]{:S(2)}, u32[]{:S(2)}) collective-permute-start(bf16[272,1536]{1,0:T(8,128)(2,1)} %collective-permute-done.7), channel_id=1, source_target_pairs={{1,0},{5,4},{9,8},{13,12},{17,16},{21,20},{25,24},{29,28}} | collective-permute-start | bytes 2506760 | tf_op jit(solution)/shard_map/ppermute | solution.py:68
  223.8 36.3 %collective-permute-start.18 = (bf16[384,512]{1,0:T(8,128)(2,1)S(1)}, bf16[384,512]{1,0:T(8,128)(2,1)}, u32[]{:S(2)}, u32[]{:S(2)}) collective-permute-start(bf16[384,512]{1,0:T(8,128)(2,1)S(1)} %get-tuple-element.523), channel_id=1, source_target_pairs={{2,0},{3,1},{6,4},{7,5},{10,8},{11,9},{14,12},{15,13},{18,16},{19,... | collective-permute-start | bytes 1179656 | tf_op jit(solution)/shard_map/ppermute | solution.py:244
  226.4 33.6 %collective-permute-start.19 = (bf16[384,512]{1,0:T(8,128)(2,1)S(1)}, bf16[384,512]{1,0:T(8,128)(2,1)}, u32[]{:S(2)}, u32[]{:S(2)}) collective-permute-start(bf16[384,512]{1,0:T(8,128)(2,1)S(1)} %get-tuple-element.522), channel_id=1, source_target_pairs={{3,0},{7,4},{11,8},{15,12},{19,16},{23,20},{27,24},{31,28}} | collective-permute-start | bytes 1179656 | tf_op jit(solution)/shard_map/ppermute | solution.py:244
  295.5 51.8 %collective-permute-start.23 = (bf16[256,1536]{1,0:T(8,128)(2,1)}, bf16[256,1536]{1,0:T(8,128)(2,1)}, u32[]{:S(2)}, u32[]{:S(2)}) collective-permute-start(bf16[256,1536]{1,0:T(8,128)(2,1)} %collective-permute-done.21.refs_1_), channel_id=1, source_target_pairs={{1,2},{2,3},{5,6},{6,7},{9,10},{10,11},{13,14},{14,15},{17,18},{18... | collective-permute-start | bytes 2359304 | tf_op jit(solution)/shard_map/ppermute | solution.py:67
  297.1 50.3 %collective-permute-start.24 = (bf16[256,1536]{1,0:T(8,128)(2,1)S(1)}, bf16[256,1536]{1,0:T(8,128)(2,1)}, u32[]{:S(2)}, u32[]{:S(2)}) collective-permute-start(bf16[256,1536]{1,0:T(8,128)(2,1)S(1)} %collective-permute-done.22.refs_0_.refs_1_), channel_id=1, source_target_pairs={{1,0},{2,1},{5,4},{6,5},{9,8},{10,9},{13,12},{14,13},{17,16},{18,1... | collective-permute-start | bytes 2359304 | tf_op jit(solution)/shard_map/ppermute | solution.py:68
  312.3 37.0 %collective-permute-start.29 = (bf16[256,1536]{1,0:T(8,128)(2,1)}, bf16[256,1536]{1,0:T(8,128)(2,1)S(1)}, u32[]{:S(2)}, u32[]{:S(2)}) collective-permute-start(bf16[256,1536]{1,0:T(8,128)(2,1)} %collective-permute-done.25.refs_3_), channel_id=1, source_target_pairs={{1,2},{2,3},{5,6},{6,7},{9,10},{10,11},{13,14},{14,15},{17,18},{18... | collective-permute-start | bytes 2359304 | tf_op jit(solution)/shard_map/ppermute | solution.py:67
  313.1 36.3 %collective-permute-start.30 = (bf16[256,1536]{1,0:T(8,128)(2,1)S(1)}, bf16[256,1536]{1,0:T(8,128)(2,1)S(1)}, u32[]{:S(2)}, u32[]{:S(2)}) collective-permute-start(bf16[256,1536]{1,0:T(8,128)(2,1)S(1)} %collective-permute-done.26.refs_2_.refs_4_), channel_id=1, source_target_pairs={{1,0},{2,1},{5,4},{6,5},{9,8},{10,9},{13,12},{14,13},{17,16},{18,1... | collective-permute-start | bytes 2359304 | tf_op jit(solution)/shard_map/ppermute | solution.py:68
  347.4 33.6 %collective-permute-start.27 = (bf16[256,1536]{1,0:T(8,128)(2,1)}, bf16[256,1536]{1,0:T(8,128)(2,1)S(1)}, u32[]{:S(2)}, u32[]{:S(2)}) collective-permute-start(bf16[256,1536]{1,0:T(8,128)(2,1)} %collective-permute-done.23.refs_2_), channel_id=1, source_target_pairs={{2,3},{6,7},{10,11},{14,15},{18,19},{22,23},{26,27},{30,31}} | collective-permute-start | bytes 2359304 | tf_op jit(solution)/shard_map/ppermute | solution.py:67
  348.1 32.9 %collective-permute-start.28 = (bf16[256,1536]{1,0:T(8,128)(2,1)}, bf16[256,1536]{1,0:T(8,128)(2,1)S(1)}, u32[]{:S(2)}, u32[]{:S(2)}) collective-permute-start(bf16[256,1536]{1,0:T(8,128)(2,1)} %collective-permute-done.24.refs_0_.refs_1_), channel_id=1, source_target_pairs={{1,0},{5,4},{9,8},{13,12},{17,16},{21,20},{25,24},{29,28}} | collective-permute-start | bytes 2359304 | tf_op jit(solution)/shard_map/ppermute | solution.py:68
  350.1 34.0 %collective-permute-start.32 = (bf16[256,1536]{1,0:T(8,128)(2,1)S(1)}, bf16[256,1536]{1,0:T(8,128)(2,1)S(1)}, u32[]{:S(2)}, u32[]{:S(2)}) collective-permute-start(bf16[256,1536]{1,0:T(8,128)(2,1)S(1)} %collective-permute-done.30.refs_3_.refs_5_), channel_id=1, source_target_pairs={{1,0},{5,4},{9,8},{13,12},{17,16},{21,20},{25,24},{29,28}} | collective-permute-start | bytes 2359304 | tf_op jit(solution)/shard_map/ppermute | solution.py:68
  447.7 33.9 %collective-permute-start.39 = (bf16[256,1536]{1,0:T(8,128)(2,1)S(1)}, bf16[256,1536]{1,0:T(8,128)(2,1)S(1)}, u32[]{:S(2)}, u32[]{:S(2)}) collective-permute-start(bf16[256,1536]{1,0:T(8,128)(2,1)S(1)} %get-tuple-element.499), channel_id=1, source_target_pairs={{0,1},{4,5},{8,9},{12,13},{16,17},{20,21},{24,25},{28,29}} | collective-permute-start | bytes 2359304 | tf_op jit(solution)/shard_map/ppermute | solution.py:131
  465.2 33.3 %collective-permute-start.35 = (bf16[256,1536]{1,0:T(8,128)(2,1)S(1)}, bf16[256,1536]{1,0:T(8,128)(2,1)S(1)}, u32[]{:S(2)}, u32[]{:S(2)}) collective-permute-start(bf16[256,1536]{1,0:T(8,128)(2,1)S(1)} %get-tuple-element.495), channel_id=1, source_target_pairs={{0,1},{1,2},{4,5},{5,6},{8,9},{9,10},{12,13},{13,14},{16,17},{17,1... | collective-permute-start | bytes 2359304 | tf_op jit(solution)/shard_map/ppermute | solution.py:131
  482.1 33.3 %collective-permute-start.41 = (bf16[256,1536]{1,0:T(8,128)(2,1)S(1)}, bf16[256,1536]{1,0:T(8,128)(2,1)S(1)}, u32[]{:S(2)}, u32[]{:S(2)}) collective-permute-start(bf16[256,1536]{1,0:T(8,128)(2,1)S(1)} %get-tuple-element.493), channel_id=1, source_target_pairs={{0,1},{1,2},{4,5},{5,6},{8,9},{9,10},{12,13},{13,14},{16,17},{17,1... | collective-permute-start | bytes 2359304 | tf_op jit(solution)/shard_map/ppermute | solution.py:131
  500.0 35.1 %collective-permute-start.37 = (bf16[256,1536]{1,0:T(8,128)(2,1)}, bf16[256,1536]{1,0:T(8,128)(2,1)}, u32[]{:S(2)}, u32[]{:S(2)}) collective-permute-start(bf16[256,1536]{1,0:T(8,128)(2,1)} %get-tuple-element.491), channel_id=1, source_target_pairs={{0,1},{1,2},{2,3},{4,5},{5,6},{6,7},{8,9},{9,10},{10,11},{12,13},{... | collective-permute-start | bytes 2359304 | tf_op jit(solution)/shard_map/ppermute | solution.py:131
  551.9 44.0 %collective-permute-start.52 = (bf16[272,1536]{1,0:T(8,128)(2,1)S(1)}, bf16[272,1536]{1,0:T(8,128)(2,1)S(1)}, u32[]{:S(2)}, u32[]{:S(2)}) collective-permute-start(bf16[272,1536]{1,0:T(8,128)(2,1)S(1)} %pad_maximum_fusion.14.refs_1_), channel_id=1, source_target_pairs={{0,1},{1,2},{2,3},{4,5},{5,6},{6,7},{8,9},{9,10},{10,11},{12,13},{... | collective-permute-start | bytes 2506760 | tf_op jit(solution)/shard_map/ppermute | solution.py:67
  556.3 39.5 %collective-permute-start.53 = (bf16[272,1536]{1,0:T(8,128)(2,1)S(1)}, bf16[272,1536]{1,0:T(8,128)(2,1)S(1)}, u32[]{:S(2)}, u32[]{:S(2)}) collective-permute-start(bf16[272,1536]{1,0:T(8,128)(2,1)S(1)} %pad_maximum_fusion.14.refs_1_), channel_id=1, source_target_pairs={{1,0},{2,1},{3,2},{5,4},{6,5},{7,6},{9,8},{10,9},{11,10},{13,12},{... | collective-permute-start | bytes 2506760 | tf_op jit(solution)/shard_map/ppermute | solution.py:68
  557.6 38.2 %collective-permute-start.48 = (bf16[256,1536]{1,0:T(8,128)(2,1)S(1)}, bf16[256,1536]{1,0:T(8,128)(2,1)S(1)}, u32[]{:S(2)}, u32[]{:S(2)}) collective-permute-start(bf16[256,1536]{1,0:T(8,128)(2,1)S(1)} %get-tuple-element.519.refs_0_), channel_id=1, source_target_pairs={{0,1},{1,2},{2,3},{4,5},{5,6},{6,7},{8,9},{9,10},{10,11},{12,13},{... | collective-permute-start | bytes 2359304 | tf_op jit(solution)/shard_map/ppermute | solution.py:67
  562.2 33.6 %collective-permute-start.49 = (bf16[256,1536]{1,0:T(8,128)(2,1)S(1)}, bf16[256,1536]{1,0:T(8,128)(2,1)S(1)}, u32[]{:S(2)}, u32[]{:S(2)}) collective-permute-start(bf16[256,1536]{1,0:T(8,128)(2,1)S(1)} %get-tuple-element.519.refs_0_), channel_id=1, source_target_pairs={{1,0},{2,1},{3,2},{5,4},{6,5},{7,6},{9,8},{10,9},{11,10},{13,12},{... | collective-permute-start | bytes 2359304 | tf_op jit(solution)/shard_map/ppermute | solution.py:68
  595.8 37.8 %collective-permute-start.56 = (bf16[272,1536]{1,0:T(8,128)(2,1)S(1)}, bf16[272,1536]{1,0:T(8,128)(2,1)S(1)}, u32[]{:S(2)}, u32[]{:S(2)}) collective-permute-start(bf16[272,1536]{1,0:T(8,128)(2,1)S(1)} %collective-permute-done.52.refs_3_), channel_id=1, source_target_pairs={{1,2},{2,3},{5,6},{6,7},{9,10},{10,11},{13,14},{14,15},{17,18},{18... | collective-permute-start | bytes 2506760 | tf_op jit(solution)/shard_map/ppermute | solution.py:67
  596.6 37.1 %collective-permute-start.57 = (bf16[272,1536]{1,0:T(8,128)(2,1)S(1)}, bf16[272,1536]{1,0:T(8,128)(2,1)S(1)}, u32[]{:S(2)}, u32[]{:S(2)}) collective-permute-start(bf16[272,1536]{1,0:T(8,128)(2,1)S(1)} %collective-permute-done.53.refs_2_.refs_4_), channel_id=1, source_target_pairs={{1,0},{2,1},{5,4},{6,5},{9,8},{10,9},{13,12},{14,13},{17,16},{18,1... | collective-permute-start | bytes 2506760 | tf_op jit(solution)/shard_map/ppermute | solution.py:68
  597.9 34.5 %collective-permute-start.50 = (bf16[256,1536]{1,0:T(8,128)(2,1)S(1)}, bf16[256,1536]{1,0:T(8,128)(2,1)S(1)}, u32[]{:S(2)}, u32[]{:S(2)}) collective-permute-start(bf16[256,1536]{1,0:T(8,128)(2,1)S(1)} %collective-permute-done.48.refs_1_), channel_id=1, source_target_pairs={{1,2},{2,3},{5,6},{6,7},{9,10},{10,11},{13,14},{14,15},{17,18},{18... | collective-permute-start | bytes 2359304 | tf_op jit(solution)/shard_map/ppermute | solution.py:67
  598.6 35.0 %collective-permute-start.51 = (bf16[256,1536]{1,0:T(8,128)(2,1)S(1)}, bf16[256,1536]{1,0:T(8,128)(2,1)S(1)}, u32[]{:S(2)}, u32[]{:S(2)}) collective-permute-start(bf16[256,1536]{1,0:T(8,128)(2,1)S(1)} %collective-permute-done.49.refs_0_.refs_1_), channel_id=1, source_target_pairs={{1,0},{2,1},{5,4},{6,5},{9,8},{10,9},{13,12},{14,13},{17,16},{18,1... | collective-permute-start | bytes 2359304 | tf_op jit(solution)/shard_map/ppermute | solution.py:68
  633.6 39.9 %collective-permute-start.58 = (bf16[272,1536]{1,0:T(8,128)(2,1)S(1)}, bf16[272,1536]{1,0:T(8,128)(2,1)S(1)}, u32[]{:S(2)}, u32[]{:S(2)}) collective-permute-start(bf16[272,1536]{1,0:T(8,128)(2,1)S(1)} %collective-permute-done.56.refs_5_.refs_6_), channel_id=1, source_target_pairs={{2,3},{6,7},{10,11},{14,15},{18,19},{22,23},{26,27},{30,31}} | collective-permute-start | bytes 2506760 | tf_op jit(solution)/shard_map/ppermute | solution.py:67
  634.3 39.2 %collective-permute-start.59 = (bf16[272,1536]{1,0:T(8,128)(2,1)S(1)}, bf16[272,1536]{1,0:T(8,128)(2,1)S(1)}, u32[]{:S(2)}, u32[]{:S(2)}) collective-permute-start(bf16[272,1536]{1,0:T(8,128)(2,1)S(1)} %collective-permute-done.57.refs_3_.refs_5_), channel_id=1, source_target_pairs={{1,0},{5,4},{9,8},{13,12},{17,16},{21,20},{25,24},{29,28}} | collective-permute-start | bytes 2506760 | tf_op jit(solution)/shard_map/ppermute | solution.py:68
  635.6 34.3 %collective-permute-start.54 = (bf16[256,1536]{1,0:T(8,128)(2,1)S(1)}, bf16[256,1536]{1,0:T(8,128)(2,1)S(1)}, u32[]{:S(2)}, u32[]{:S(2)}) collective-permute-start(bf16[256,1536]{1,0:T(8,128)(2,1)S(1)} %collective-permute-done.50.refs_2_), channel_id=1, source_target_pairs={{2,3},{6,7},{10,11},{14,15},{18,19},{22,23},{26,27},{30,31}} | collective-permute-start | bytes 2359304 | tf_op jit(solution)/shard_map/ppermute | solution.py:67
  636.3 37.2 %collective-permute-start.55 = (bf16[256,1536]{1,0:T(8,128)(2,1)S(1)}, bf16[256,1536]{1,0:T(8,128)(2,1)S(1)}, u32[]{:S(2)}, u32[]{:S(2)}) collective-permute-start(bf16[256,1536]{1,0:T(8,128)(2,1)S(1)} %collective-permute-done.51.refs_0_.refs_1_), channel_id=1, source_target_pairs={{1,0},{5,4},{9,8},{13,12},{17,16},{21,20},{25,24},{29,28}} | collective-permute-start | bytes 2359304 | tf_op jit(solution)/shard_map/ppermute | solution.py:68
  710.0 34.8 %collective-permute-start.60 = (bf16[512,1536]{1,0:T(8,128)(2,1)}, bf16[512,1536]{1,0:T(8,128)(2,1)S(1)}, u32[]{:S(2)}, u32[]{:S(2)}) collective-permute-start(bf16[512,1536]{1,0:T(8,128)(2,1)} %get-tuple-element.479), channel_id=1, source_target_pairs={{0,1},{4,5},{8,9},{12,13},{16,17},{20,21},{24,25},{28,29}} | collective-permute-start | bytes 4718600 | tf_op jit(solution)/shard_map/ppermute | solution.py:131
  785.5 33.0 %collective-permute-start.64 = (bf16[512,1536]{1,0:T(8,128)(2,1)S(1)}, bf16[512,1536]{1,0:T(8,128)(2,1)}, u32[]{:S(2)}, u32[]{:S(2)}) collective-permute-start(bf16[512,1536]{1,0:T(8,128)(2,1)S(1)} %get-tuple-element.475), channel_id=1, source_target_pairs={{0,1},{1,2},{2,3},{4,5},{5,6},{6,7},{8,9},{9,10},{10,11},{12,13},{... | collective-permute-start | bytes 4718600 | tf_op jit(solution)/shard_map/ppermute | solution.py:131
  833.7 45.7 %collective-permute-start.74 = (f32[1,1]{1,0:T(1,128)}, f32[1,1]{1,0:T(1,128)}, u32[]{:S(2)}, u32[]{:S(2)}) collective-permute-start(f32[1,1]{1,0:T(1,128)} %bitcast.85), channel_id=1, source_target_pairs={{0,1},{1,0},{2,3},{3,2},{4,5},{5,4},{6,7},{7,6},{8,9},{9,8},{10,11... | collective-permute-start | bytes 20 | tf_op jit(solution)/shard_map/ppermute | solution.py:249
  884.6 38.1 %collective-permute-start.72 = (bf16[384,512]{1,0:T(8,128)(2,1)}, bf16[384,512]{1,0:T(8,128)(2,1)}, u32[]{:S(2)}, u32[]{:S(2)}) collective-permute-start(bf16[384,512]{1,0:T(8,128)(2,1)} %get-tuple-element.512), channel_id=1, source_target_pairs={{2,0},{3,1},{6,4},{7,5},{10,8},{11,9},{14,12},{15,13},{18,16},{19,... | collective-permute-start | bytes 1179656 | tf_op jit(solution)/shard_map/ppermute | solution.py:244
  886.0 36.8 %collective-permute-start.73 = (bf16[384,512]{1,0:T(8,128)(2,1)}, bf16[384,512]{1,0:T(8,128)(2,1)}, u32[]{:S(2)}, u32[]{:S(2)}) collective-permute-start(bf16[384,512]{1,0:T(8,128)(2,1)} %get-tuple-element.511), channel_id=1, source_target_pairs={{3,0},{7,4},{11,8},{15,12},{19,16},{23,20},{27,24},{31,28}} | collective-permute-start | bytes 1179656 | tf_op jit(solution)/shard_map/ppermute | solution.py:244
  922.7 67.1 %collective-permute-start.75 = (bf16[2,192,768]{2,1,0:T(8,128)(2,1)}, bf16[2,192,768]{2,1,0:T(8,128)(2,1)}, u32[]{:S(2)}, u32[]{:S(2)}) collective-permute-start(bf16[2,192,768]{2,1,0:T(8,128)(2,1)} %add_convert_fusion.9), channel_id=1, source_target_pairs={{0,8},{4,12},{8,0},{12,4},{16,24},{20,28},{24,16},{28,20},{1,9},{5... | collective-permute-start | bytes 1769480 | tf_op jit(solution)/shard_map/ppermute | solution.py:249
  922.7 67.1 %collective-permute-start.76 = (bf16[2,192,768]{2,1,0:T(8,128)(2,1)}, bf16[2,192,768]{2,1,0:T(8,128)(2,1)}, u32[]{:S(2)}, u32[]{:S(2)}) collective-permute-start(bf16[2,192,768]{2,1,0:T(8,128)(2,1)} %add_convert_fusion.8), channel_id=1, source_target_pairs={{0,16},{4,20},{8,24},{12,28},{16,0},{20,4},{24,8},{28,12},{1,17},{... | collective-permute-start | bytes 1769480 | tf_op jit(solution)/shard_map/ppermute | solution.py:249
  930.1 59.8 %collective-permute-start.77 = (f32[1,1]{1,0:T(1,128)}, f32[1,1]{1,0:T(1,128)}, u32[]{:S(2)}, u32[]{:S(2)}) collective-permute-start(f32[1,1]{1,0:T(1,128)} %add.773), channel_id=1, source_target_pairs={{0,2},{1,3},{2,0},{3,1},{4,6},{5,7},{6,4},{7,5},{8,10},{9,11},{10,... | collective-permute-start | bytes 20 | tf_op jit(solution)/shard_map/ppermute | solution.py:249
  1013.0 34.4 %collective-permute-start.82 = (bf16[304,1536]{1,0:T(8,128)(2,1)}, bf16[304,1536]{1,0:T(8,128)(2,1)}, u32[]{:S(2)}, u32[]{:S(2)}) collective-permute-start(bf16[304,1536]{1,0:T(8,128)(2,1)} %pad_maximum_fusion.12), channel_id=1, source_target_pairs={{3,2},{7,6},{11,10},{15,14},{19,18},{23,22},{27,26},{31,30}} | collective-permute-start | bytes 2801672 | tf_op jit(solution)/shard_map/ppermute | solution.py:132
  1049.4 35.2 %collective-permute-start.86 = (bf16[304,1536]{1,0:T(8,128)(2,1)S(1)}, bf16[304,1536]{1,0:T(8,128)(2,1)S(1)}, u32[]{:S(2)}, u32[]{:S(2)}) collective-permute-start(bf16[304,1536]{1,0:T(8,128)(2,1)S(1)} %get-tuple-element.543), channel_id=1, source_target_pairs={{0,1},{1,2},{4,5},{5,6},{8,9},{9,10},{12,13},{13,14},{16,17},{17,1... | collective-permute-start | bytes 2801672 | tf_op jit(solution)/shard_map/ppermute | solution.py:131
  1053.0 43.0 %collective-permute-start.85 = (bf16[2,192,681]{2,1,0:T(8,128)(2,1)S(1)}, bf16[2,192,681]{2,1,0:T(8,128)(2,1)S(1)}, u32[]{:S(2)}, u32[]{:S(2)}) collective-permute-start(bf16[2,192,681]{2,1,0:T(8,128)(2,1)S(1)} %add_convert_fusion.7), channel_id=1, source_target_pairs={{0,8},{4,12},{8,0},{12,4},{16,24},{20,28},{24,16},{28,20},{1,9},{5... | collective-permute-start | bytes 1569032 | tf_op jit(solution)/shard_map/ppermute | solution.py:249
  1066.3 35.2 %collective-permute-start.91 = (bf16[256,1536]{1,0:T(8,128)(2,1)S(1)}, bf16[256,1536]{1,0:T(8,128)(2,1)S(1)}, u32[]{:S(2)}, u32[]{:S(2)}) collective-permute-start(bf16[256,1536]{1,0:T(8,128)(2,1)S(1)} %add_convert_fusion.6), channel_id=1, source_target_pairs={{0,1},{1,2},{2,3},{4,5},{5,6},{6,7},{8,9},{9,10},{10,11},{12,13},{... | collective-permute-start | bytes 2359304 | tf_op jit(solution)/shard_map/ppermute | solution.py:131
  1096.0 46.6 %collective-permute-start.97 = (f32[1,1]{1,0:T(1,128)}, f32[1,1]{1,0:T(1,128)}, u32[]{:S(2)}, u32[]{:S(2)}) collective-permute-start(f32[1,1]{1,0:T(1,128)} %add.774), channel_id=1, source_target_pairs={{0,4},{4,0},{8,12},{12,8},{16,20},{20,16},{24,28},{28,24},{1,5},{5... | collective-permute-start | bytes 20 | tf_op jit(solution)/shard_map/ppermute | solution.py:249
  (217 other events, 4319.2 us)
Sparse Core Ops, SparseCore 0:
  11.5 33.2 all-gather.2
  46.7 241.8 all-gather.4
  824.2 300.4 reduce-scatter.1

commit v13 on v11

--- a/solution.py
+++ b/solution.py
@@ -119,9 +119,7 @@
     return lax.dynamic_index_in_dim(placed, place % lax.axis_size("seq"), 0, keepdims=False)
 
 
-def line_send(parts, k, right, left):
-    me = lax.axis_index("seq")
-    to_right, to_left = at_place(parts, me + k), at_place(parts, me - k)
+def line_send(to_right, to_left, right, left):
     if right is not None:
         to_right = (to_right.astype(full) + right.astype(full)).astype(low)
         to_left = (to_left.astype(full) + left.astype(full)).astype(low)
@@ -166,25 +164,24 @@
         return [arrived(self.rights[h], self.lefts[h], turn) for h in (0, 1)]
 
 
-def line_scatter(halves, work):
+def line_scatter(count, get, work):
     n = lax.axis_size("seq")
-    me = lax.axis_index("seq")
-    flying = [(None, None)] * len(halves)
+    flying = [(None, None)] * count
     before, given = (), []
     for k in range(n - 1, 0, -1):
-        for h, half in enumerate(halves):
+        for h in range(count):
             if k < n - 1 and h:
                 flying[h], before = tie(flying[h], before)
             elif k < n - 1:
                 flying[h], given = tie(flying[h], given)
-            before = line_send(half, k, *flying[h])
+            before = line_send(get(h, k), get(h, -k), *flying[h])
             flying[h] = line_pass(*before, k)
         if n - 1 - k < len(work):
             given = work[n - 1 - k](before, given)
     sums = []
     flying[0], given = tie(flying[0], given)
-    for half, (right, left) in zip(halves, flying):
-        sums.append(at_place(half, me).astype(full) + (right.astype(full) + left.astype(full)))
+    for h, (right, left) in enumerate(flying):
+        sums.append(get(h, 0).astype(full) + (right.astype(full) + left.astype(full)))
     return jnp.concatenate(sums), given
 
 
@@ -935,7 +932,8 @@
         gates.append(shard_gates)
         other = shard_gates
     mix_parts, expert_in, gate_up = buffers
-    mixture, _ = line_scatter([mix_parts[:, :middle], mix_parts[:, middle:]], ())
+    cuts = (slice(0, middle), slice(middle, None))
+    mixture, _ = line_scatter(2, lambda h, shift: at_place(mix_parts[:, cuts[h]], me + shift), ())
     output_f32 = hidden + resid_mult * mixture
     activations = output_f32.astype(low).reshape(1, shard_len, width)
     error_rows = output_f32 - teacher.astype(full).reshape(shard_len, width)
@@ -987,21 +985,22 @@
         return make
 
     d_normed_two, grads = line_scatter(
-        [d_parts], (some_grads(0, cut), some_grads(cut, experts_here))
+        1,
+        lambda h, shift: at_place(d_parts, me + shift),
+        (some_grads(0, cut), some_grads(cut, experts_here)),
     )
     expert_sum = lax.psum_scatter(grads[0], "fsdp", scatter_dimension=1, tiled=True)
 
     d_hidden_norm, gain_two_part = norm_two_pull(d_normed_two)
     d_hidden = d_out + d_hidden_norm
     d_proj = (resid_mult * d_hidden).astype(low)
+    d_attended = dot("kd,td->kt", full_out, d_proj).astype(low)
+    moved = exchange(d_attended.reshape(n, heads_w, shard_len))
+    moved[0][1], d_proj, d_logits = tie(moved[0][1], d_proj, d_logits)
     out_pairs = out_grads(mine.reshape(1), attn_rows, d_proj, order_a, order_b)
     out_sums = [Halving(*pair, bits) for pair, bits in zip(out_pairs, (order_a, order_b))]
     for each in out_sums:
         each.go()
-    d_attended = dot("kd,td->kt", full_out, d_proj).astype(low)
-    (d_attended,) = land(out_sums, d_attended)
-    moved = exchange(d_attended.reshape(n, heads_w, shard_len))
-    for each in out_sums:
         each.add()
     router_part = sum(
         dot("td,et->de", half, half_logits)
@@ -1031,7 +1030,13 @@
     d_turned = jnp.concatenate([query_grad, key_grad[:, None]], axis=1).astype(full)
     d_turned = rotate(d_turned, cosine, -sine_vals).astype(low)
     d_qkv = jnp.concatenate([d_turned, value_grad[:, None]], axis=1).reshape(group_w, seq_len)
-    d_parts = dot("ct,dc->td", d_qkv, full_qkv).astype(low).reshape(n, shard_len, width)
+
+    def d_part(rows, shift):
+        start = (me + shift) % n * shard_len
+        rows = lax.dynamic_slice_in_dim(rows, start, shard_len, 1)
+        return dot("ct,dc->td", rows, full_qkv).astype(low)
+
+    d_parts = {shift: d_part(d_qkv, shift) for shift in {1, n - 1}}
     (d_parts,) = land(out_sums, d_parts)
     for each in out_sums:
         each.add()
@@ -1039,14 +1044,21 @@
     out_sum = jnp.concatenate([each.finish() for each in out_sums], axis=1).astype(low)
     out_rows = out_sum.shape[0] // n
     out_parts = jnp.swapaxes(out_sum.reshape(out_sum.shape[0], n, width // n), 0, 1)
-    d_parts = [
-        d_parts[:, :middle],
-        jnp.concatenate([d_parts[:, middle:], out_parts.reshape(n, out_rows, width)], axis=1),
-    ]
+    out_parts = out_parts.reshape(n, out_rows, width)
+
+    def get(h, shift):
+        part = d_parts[shift % n]
+        if h == 0:
+            return part[:middle]
+        return jnp.concatenate([part[middle:], at_place(out_parts, me + shift)])
+
     sums = {}
 
     def first_work(before, _):
         rows, _ = tie(d_qkv, before)
+        for shift in range(n):
+            if shift not in d_parts:
+                d_parts[shift] = d_part(rows, shift)
         qkv_part = jnp.concatenate(
             [dot("td,ct->dc", normed_one, rows).astype(low), own_columns], axis=1
         )
@@ -1060,7 +1072,7 @@
         sums["qkv"].go()
         return sums["qkv"].send
 
-    ended, _ = line_scatter(d_parts, (first_work, next_work, next_work))
+    ended, _ = line_scatter(2, get, (first_work, next_work, next_work))
     qkv_sum = sums["qkv"]
     d_normed_one = ended[:shard_len]
     (ended,) = land([qkv_sum], ended)

time: 1170 us -> 1180 us (level)
  waiting for transfers between devices: 249 us -> 288 us
  other arithmetic: 139 us -> 127 us
  starting transfers between devices: 234 us -> 222 us
    ppermute x15, waiting for transfers between devices: 96.5 us -> 127 us  [line_pass(): lax.ppermute(to_right, 'seq', [(i, i + 1) for i in range(n - k)])]
    ppermute x6, waiting for transfers between devices: 31.8 us -> 57.2 us  [exchange(): lefts[k] = lax.ppermute(to_left, 'seq', [(i, i - k) for i in range(k, n)])]
    ppermute x15, starting transfers between devices: 89.5 us -> 74 us  [line_pass(): lax.ppermute(to_right, 'seq', [(i, i + 1) for i in range(n - k)])]
    ppermute x6, waiting for transfers between devices: 27.8 us -> 13.2 us  [exchange(): lax.ppermute(to_right, 'seq', [(i, i + k) for i in range(n - k)])]
    dot_general x17 -> x20, matrix products: 38.5 us -> 34.8 us  [dot(): return jnp.einsum(spec, left, right, preferred_element_type=full)]
  transfers between devices with their start and end apart: 104 -> 104, of which waited for: 38 -> 37; matrix products, arithmetic and copies ran while one was open for 16% -> 14% of each run, Pallas kernels for 26% -> 26%
where the time goes in v13:
time: 1180 us; the launch traced here: 1170 us
  Pallas kernels  387 us (33%)
  waiting for transfers between devices  288 us (24%)
  starting transfers between devices  222 us (19%)
  other arithmetic  127 us (11%)
  local copies, waits for them, and re-layouts  72.7 us (6%)
  between operations  40.6 us (3%)
  matrix products  34.8 us (3%)
    pallas_call x8, Pallas kernels, shard_call(): pl.pallas_call(kernel, grid_spec=pltpu.PrefetchScalarGridSpec(num_scalar_...  230 us
    ppermute x15, waiting for transfers between devices, line_pass(): lax.ppermute(to_right, 'seq', [(i, i + 1) for i in range(n - k)])  127 us
    ppermute x15, starting transfers between devices, line_pass(): lax.ppermute(to_right, 'seq', [(i, i + 1) for i in range(n - k)])  74 us
    ppermute x21, waiting for transfers between devices, line_move(): lax.ppermute(left, 'seq', [(i, i - 1) for i in range(1, n - k + 1)])  59.3 us
    pallas_call x1, Pallas kernels, attention_backward(): pl.pallas_call(functools.partial(backward_kernel, seq_len, query_rows, ke...  58.4 us
    ppermute x6, waiting for transfers between devices, exchange(): lefts[k] = lax.ppermute(to_left, 'seq', [(i, i - k) for i in range(k, n)])  57.2 us
    pallas_call x2, Pallas kernels, weight_grads(): pl.pallas_call(functools.partial(grads_kernel, few), grid=(stop - first,)...  50.9 us
    ppermute x21, starting transfers between devices, line_move(): lax.ppermute(right, 'seq', [(i, i + 1) for i in range(k - 1, n - 1)])  50.3 us
  transfers between devices with their start and end apart: 104, of which 37 were waited for; matrix products, arithmetic and copies ran while one was open for 14% of the time, Pallas kernels for 26%

profile of v13, /device:TPU:0, one launch (start us, length us, event | category | flops | bytes accessed | tf_op | source)
XLA Modules:
  0.0 1172.9 jit_solution(2109911885381315209)
XLA Ops:
  15.1 6.4 maximum_maximum_fusion
  23.2 6.0 collective-permute-start
  31.8 5.4 collective-permute-start.2
  63.0 6.5 collective-permute-done.3
  90.4 13.9 %collective-permute-done.7 = bf16[272,1536]{1,0:T(8,128)(2,1)} collective-permute-done((bf16[272,1536]{1,0:T(8,128)(2,1)}, bf16[272,1536]{1,0:T(8,128)(2,1)}, u32[]{:S(2)}, u32[]{:S(2)}) %collective-permute-start.7) | collective-permute-done | bytes 835616 | tf_op jit(solution)/shard_map/ppermute | solution.py:68
  121.2 16.5 %collective-permute-done.11 = bf16[272,1536]{1,0:T(8,128)(2,1)} collective-permute-done((bf16[272,1536]{1,0:T(8,128)(2,1)}, bf16[272,1536]{1,0:T(8,128)(2,1)}, u32[]{:S(2)}, u32[]{:S(2)}) %collective-permute-start.11) | collective-permute-done | bytes 835616 | tf_op jit(solution)/shard_map/ppermute | solution.py:68
  152.8 41.7 %attention_forward.1 = (bf16[4,384,512]{2,1,0:T(8,128)(2,1)}, f32[2,3,64,2048]{3,2,1,0:T(8,128)}, f32[2,3,1,2048]{3,2,1,0:T(1,128)}) custom-call(s32[1,2048]{1,0:T(1,128)} %bitcast.306, bf16[4,2,5,64,512]{4,3,2,1,0:T(8,128)(2,1)} %copy-done.15, bf16[2,2048,64]{2,1,0:T(8,128)(2,1)} %copy.170.k_ref, bf16[2,64,2048]{2,1,0:T(8,128)(2,1)} %copy.171.vt_ref), custom_call_target="tpu_custom_call" | custom-call | tf_op jit(solution)/shard_map/attention_forward/pallas_call | solution.py:342
  210.7 5.1 collective-permute-done.13
  215.9 6.1 collective-permute-done.14
  221.9 16.1 %collective-permute-done.16 = bf16[384,512]{1,0:T(8,128)(2,1)S(1)} collective-permute-done((bf16[384,512]{1,0:T(8,128)(2,1)S(1)}, bf16[384,512]{1,0:T(8,128)(2,1)S(1)}, u32[]{:S(2)}, u32[]{:S(2)}) %collective-permute-start.16) | collective-permute-done | bytes 393248 | tf_op jit(solution)/shard_map/ppermute | solution.py:205
  249.9 5.5 collective-permute-start.22
  256.7 9.0 collective-permute-done.18
  265.7 5.3 collective-permute-done.19
  273.8 5.8 collective-permute-done.22
  279.6 8.3 collective-permute-done.23
  293.6 25.3 %experts_forward.4 = (bf16[4,512,1536]{2,1,0:T(8,128)(2,1)}, bf16[10,4,160,1536]{3,2,1,0:T(8,128)(2,1)}, bf16[10,4,160,1024]{3,2,1,0:T(8,128)(2,1)}, f32[10,512]{1,0:T(8,128)S(1)}) custom-call(s32[2]{0:T(128)S(1)} %get-tuple-element.586.at_ref, bf16[256,1536]{1,0:T(8,128)(2,1)S(1)} %get-tuple-element.521.tok_ref, ...), custom_call_target="tpu_custom_call" | custom-call | tf_op jit(solution)/shard_map/experts_forward/pallas_call | solution.py:597
  321.6 10.0 collective-permute-start.29
  334.2 25.2 %experts_forward.5 = (bf16[4,512,1536]{2,1,0:T(8,128)(2,1)}, bf16[10,4,160,1536]{3,2,1,0:T(8,128)(2,1)}, bf16[10,4,160,1024]{3,2,1,0:T(8,128)(2,1)}, f32[10,512]{1,0:T(8,128)S(1)}) custom-call(s32[2]{0:T(128)S(1)} %get-tuple-element.587.at_ref, ...), custom_call_target="tpu_custom_call", output_to_operand_aliasing={{0}: (8, {}), {1}: (9, {}), {2}: (10, {})} | custom-call | tf_op jit(solution)/shard_map/experts_forward/pallas_call | solution.py:597
  367.8 25.2 %experts_forward.6 = (bf16[4,512,1536]{2,1,0:T(8,128)(2,1)}, bf16[10,4,160,1536]{3,2,1,0:T(8,128)(2,1)}, bf16[10,4,160,1024]{3,2,1,0:T(8,128)(2,1)}, f32[10,512]{1,0:T(8,128)S(1)}) custom-call(s32[2]{0:T(128)S(1)} %get-tuple-element.588.at_ref, ...), custom_call_target="tpu_custom_call", output_to_operand_aliasing={{0}: (8, {}), {1}: (9, {}), {2}: (10, {})} | custom-call | tf_op jit(solution)/shard_map/experts_forward/pallas_call | solution.py:597
  393.0 25.2 %experts_forward.7 = (bf16[4,512,1536]{2,1,0:T(8,128)(2,1)}, bf16[10,4,160,1536]{3,2,1,0:T(8,128)(2,1)}, bf16[10,4,160,1024]{3,2,1,0:T(8,128)(2,1)}, f32[10,512]{1,0:T(8,128)S(1)}) custom-call(s32[2]{0:T(128)S(1)} %get-tuple-element.585.at_ref, ...), custom_call_target="tpu_custom_call", output_to_operand_aliasing={{0}: (8, {}), {1}: (9, {}), {2}: (10, {})} | custom-call | tf_op jit(solution)/shard_map/experts_forward/pallas_call | solution.py:597
  421.9 6.0 collective-permute-start.30
  431.3 14.6 %collective-permute-done.30 = bf16[256,1536]{1,0:T(8,128)(2,1)S(1)} collective-permute-done((bf16[256,1536]{1,0:T(8,128)(2,1)S(1)}, bf16[256,1536]{1,0:T(8,128)(2,1)S(1)}, u32[]{:S(2)}, u32[]{:S(2)}) %collective-permute-start.30) | collective-permute-done | bytes 786464 | tf_op jit(solution)/shard_map/ppermute | solution.py:132
  451.4 11.3 collective-permute-done.36
  468.3 11.3 collective-permute-done.32
  480.0 5.3 collective-permute-start.34
  486.7 9.7 collective-permute-done.38
  497.7 5.3 collective-permute-start.40
  541.3 32.1 %experts_backward.4 = (bf16[4,512,1536]{2,1,0:T(8,128)(2,1)}, bf16[10,4,160,1536]{3,2,1,0:T(8,128)(2,1)}, bf16[10,4,160,1024]{3,2,1,0:T(8,128)(2,1)}, bf16[10,4,...) custom-call(s32[2]{0:T(128)S(1)} %get-tuple-element.586.at_ref, bf16[256,1536]{1,0:T(8,128)(2,1)S(1)} %get-tuple-element.515.tok_ref, ...), custom_call_target="tpu_custom_call" | custom-call | tf_op jit(solution)/shard_map/experts_backward/pallas_call | solution.py:597
  579.1 32.2 %experts_backward.5 = (bf16[4,512,1536]{2,1,0:T(8,128)(2,1)}, bf16[10,4,160,1536]{3,2,1,0:T(8,128)(2,1)}, bf16[10,4,160,1024]{3,2,1,0:T(8,128)(2,1)}, bf16[10,4,...) custom-call(s32[2]{0:T(128)S(1)} %get-tuple-element.587.at_ref, ...), custom_call_target="tpu_custom_call", output_to_operand_aliasing={{0}: (10, {}), {1}: (11, {}), {2}: (12, {}), {3}: (13, {})} | custom-call | tf_op jit(solution)/shard_map/experts_backward/pallas_call | solution.py:597
  618.1 32.2 %experts_backward.6 = (bf16[4,512,1536]{2,1,0:T(8,128)(2,1)}, bf16[10,4,160,1536]{3,2,1,0:T(8,128)(2,1)}, bf16[10,4,160,1024]{3,2,1,0:T(8,128)(2,1)}, bf16[10,4,...) custom-call(s32[2]{0:T(128)S(1)} %get-tuple-element.588.at_ref, ...), custom_call_target="tpu_custom_call", output_to_operand_aliasing={{0}: (10, {}), {1}: (11, {}), {2}: (12, {}), {3}: (13, {})} | custom-call | tf_op jit(solution)/shard_map/experts_backward/pallas_call | solution.py:597
  655.0 32.2 %experts_backward.7 = (bf16[4,512,1536]{2,1,0:T(8,128)(2,1)}, bf16[10,4,160,1536]{3,2,1,0:T(8,128)(2,1)}, bf16[10,4,160,1024]{3,2,1,0:T(8,128)(2,1)}, bf16[10,4,...) custom-call(s32[2]{0:T(128)S(1)} %get-tuple-element.585.at_ref, ...), custom_call_target="tpu_custom_call", output_to_operand_aliasing={{0}: (10, {}), {1}: (11, {}), {2}: (12, {}), {3}: (13, {})} | custom-call | tf_op jit(solution)/shard_map/experts_backward/pallas_call | solution.py:597
  689.3 11.7 collective-permute-start.57
  702.0 25.5 %weight_grads.2.refs_0_ = bf16[10,1536,1536]{2,1,0:T(8,128)(2,1)} custom-call(bf16[10,640,1536]{2,1,0:T(8,128)(2,1)} %bitcast.270, bf16[10,640,1024]{2,1,0:T(8,128)(2,1)} %bitcast.272, bf16[10,640,512]{2,1,0:T(8,128)(2,1)} %bitcast.274, bf16[10,640,1536]{2,1,0:T(8,128)(2,1)} %bitcast.268), custom_call_target="tpu_custom_call" | custom-call | tf_op jit(solution)/shard_map/weight_grads/pallas_call | solution.py:768
  737.2 25.4 %weight_grads.3 = bf16[10,1536,1536]{2,1,0:T(8,128)(2,1)} custom-call(bf16[10,640,1536]{2,1,0:T(8,128)(2,1)} %bitcast.271, bf16[10,640,1024]{2,1,0:T(8,128)(2,1)} %bitcast.273, bf16[10,640,512]{2,1,0:T(8,128)(2,1)} %bitcast.275, bf16[10,640,1536]{2,1,0:T(8,128)(2,1)} %bitcast.269, ...), custom_call_target="tpu_custom_call", output_to_operand_aliasing={{}: (4, {})} | custom-call | tf_op jit(solution)/shard_map/weight_grads/pallas_call | solution.py:768
  765.8 5.5 collective-permute-start.61
  773.0 21.4 %collective-permute-done.61 = bf16[512,1536]{1,0:T(8,128)(2,1)S(1)} collective-permute-done((bf16[512,1536]{1,0:T(8,128)(2,1)S(1)}, bf16[512,1536]{1,0:T(8,128)(2,1)S(1)}, u32[]{:S(2)}, u32[]{:S(2)}) %collective-permute-start.61) | collective-permute-done | bytes 1572896 | tf_op jit(solution)/shard_map/ppermute | solution.py:132
  811.8 5.7 multiply_convert_fusion
  832.0 6.7 out_grads.1
  851.2 13.9 %collective-permute-done.68.refs_4_ = bf16[384,512]{1,0:T(8,128)(2,1)S(1)} collective-permute-done((bf16[384,512]{1,0:T(8,128)(2,1)}, bf16[384,512]{1,0:T(8,128)(2,1)S(1)}, u32[]{:S(2)}, u32[]{:S(2)}) %collective-permute-start.68) | collective-permute-done | bytes 393248 | tf_op jit(solution)/shard_map/ppermute | solution.py:205
  865.1 27.2 %collective-permute-done.69.refs_5_ = bf16[384,512]{1,0:T(8,128)(2,1)S(1)} collective-permute-done((bf16[384,512]{1,0:T(8,128)(2,1)}, bf16[384,512]{1,0:T(8,128)(2,1)S(1)}, u32[]{:S(2)}, u32[]{:S(2)}) %collective-permute-start.69) | collective-permute-done | bytes 393248 | tf_op jit(solution)/shard_map/ppermute | solution.py:205
  900.8 58.4 %attention_backward.1 = (bf16[2,3,64,2048]{3,2,1,0:T(8,128)(2,1)}, bf16[2,64,2048]{2,1,0:T(8,128)(2,1)}, bf16[2,64,2048]{2,1,0:T(8,128)(2,1)}) custom-call(s32[1]{0:T(128)} %bitcast.51.me_ref, s32[1,2048]{1,0:T(1,128)} %bitcast.307, bf16[4,2,5,64,512]{4,3,2,1,0:T(8,128)(2,1)} %copy-done.15, bf16[2,2048,64]{2,1,0:T(8,128)(2,1)} %copy.170.k_ref, ...), custom_call_target="tpu_custom_call" | custom-call | tf_op jit(solution)/shard_map/attention_backward/pallas_call | solution.py:425
  1009.9 16.5 %collective-permute-done.80 = bf16[256,1536]{1,0:T(8,128)(2,1)} collective-permute-done((bf16[256,1536]{1,0:T(8,128)(2,1)}, bf16[256,1536]{1,0:T(8,128)(2,1)}, u32[]{:S(2)}, u32[]{:S(2)}) %collective-permute-start.80) | collective-permute-done | bytes 786464 | tf_op jit(solution)/shard_map/ppermute | solution.py:132
  1039.9 10.6 collective-permute-done.85
  1052.3 7.0 collective-permute-start.88
  1059.3 11.3 collective-permute-done.83
  1072.3 7.0 collective-permute-start.90
  1090.1 13.3 %collective-permute-done.90 = bf16[304,1536]{1,0:T(8,128)(2,1)S(1)} collective-permute-done((bf16[304,1536]{1,0:T(8,128)(2,1)S(1)}, bf16[304,1536]{1,0:T(8,128)(2,1)S(1)}, u32[]{:S(2)}, u32[]{:S(2)}) %collective-permute-start.90) | collective-permute-done | bytes 933920 | tf_op jit(solution)/shard_map/ppermute | solution.py:132
  1109.6 7.1 collective-permute-start.92
  (659 shorter events, 397.3 us)
Async XLA Ops:
  7.2 70.4 %all-gather.3.cloned.1.call-start = ((), (), s32[]{:S(2)}) async-start(), calls=%async_computation.1 | async-start | bytes 7962624 | tf_op jit(solution)/shard_map/all_gather | solution.py:820
  12.9 280.7 %all-gather.5.cloned.1.call-start = ((), (), s32[]{:S(2)}) async-start(), calls=%async_computation.2 | async-start | bytes 53084160 | tf_op jit(solution)/shard_map/all_gather | solution.py:837
  21.5 1103.1 %reduce-scatter.2.cloned.1.call-start = ((), (), s32[]{:S(2)}) async-start(), calls=%async_computation.3 | async-start | bytes 53084160 | tf_op jit(solution)/shard_map/reduce_scatter | solution.py:992
  23.2 34.1 %collective-permute-start = (bf16[256,1536]{1,0:T(8,128)(2,1)S(1)}, bf16[256,1536]{1,0:T(8,128)(2,1)}, u32[]{:S(2)}, u32[]{:S(2)}) collective-permute-start(bf16[256,1536]{1,0:T(8,128)(2,1)S(1)} %get-tuple-element.529), channel_id=1, source_target_pairs={{0,1},{1,2},{2,3},{4,5},{5,6},{6,7},{8,9},{9,10},{10,11},{12,13},{... | collective-permute-start | bytes 2359304 | tf_op jit(solution)/shard_map/ppermute | solution.py:67
  37.2 32.3 %collective-permute-start.3 = (bf16[272,1536]{1,0:T(8,128)(2,1)S(1)}, bf16[272,1536]{1,0:T(8,128)(2,1)}, u32[]{:S(2)}, u32[]{:S(2)}) collective-permute-start(bf16[272,1536]{1,0:T(8,128)(2,1)S(1)} %pad_maximum_fusion.11), channel_id=1, source_target_pairs={{1,0},{2,1},{3,2},{5,4},{6,5},{7,6},{9,8},{10,9},{11,10},{13,12},{... | collective-permute-start | bytes 2506760 | tf_op jit(solution)/shard_map/ppermute | solution.py:68
  69.5 34.8 %collective-permute-start.7 = (bf16[272,1536]{1,0:T(8,128)(2,1)}, bf16[272,1536]{1,0:T(8,128)(2,1)}, u32[]{:S(2)}, u32[]{:S(2)}) collective-permute-start(bf16[272,1536]{1,0:T(8,128)(2,1)} %collective-permute-done.3), channel_id=1, source_target_pairs={{1,0},{2,1},{5,4},{6,5},{9,8},{10,9},{13,12},{14,13},{17,16},{18,1... | collective-permute-start | bytes 2506760 | tf_op jit(solution)/shard_map/ppermute | solution.py:68
  70.8 33.5 %collective-permute-start.6 = (bf16[272,1536]{1,0:T(8,128)(2,1)}, bf16[272,1536]{1,0:T(8,128)(2,1)}, u32[]{:S(2)}, u32[]{:S(2)}) collective-permute-start(bf16[272,1536]{1,0:T(8,128)(2,1)} %collective-permute-done.2), channel_id=1, source_target_pairs={{1,2},{2,3},{5,6},{6,7},{9,10},{10,11},{13,14},{14,15},{17,18},{18... | collective-permute-start | bytes 2506760 | tf_op jit(solution)/shard_map/ppermute | solution.py:67
  204.2 33.8 %collective-permute-start.16 = (bf16[384,512]{1,0:T(8,128)(2,1)S(1)}, bf16[384,512]{1,0:T(8,128)(2,1)S(1)}, u32[]{:S(2)}, u32[]{:S(2)}) collective-permute-start(bf16[384,512]{1,0:T(8,128)(2,1)S(1)} %get-tuple-element.523), channel_id=1, source_target_pairs={{2,0},{3,1},{6,4},{7,5},{10,8},{11,9},{14,12},{15,13},{18,16},{19,... | collective-permute-start | bytes 1179656 | tf_op jit(solution)/shard_map/ppermute | solution.py:205
  255.4 32.6 %collective-permute-start.23 = (bf16[256,1536]{1,0:T(8,128)(2,1)S(1)}, bf16[256,1536]{1,0:T(8,128)(2,1)}, u32[]{:S(2)}, u32[]{:S(2)}) collective-permute-start(bf16[256,1536]{1,0:T(8,128)(2,1)S(1)} %get-tuple-element.520.more_ref), channel_id=1, source_target_pairs={{1,0},{2,1},{3,2},{5,4},{6,5},{7,6},{9,8},{10,9},{11,10},{13,12},{... | collective-permute-start | bytes 2359304 | tf_op jit(solution)/shard_map/ppermute | solution.py:68
  271.0 47.9 %collective-permute-start.20 = (bf16[256,1536]{1,0:T(8,128)(2,1)}, bf16[256,1536]{1,0:T(8,128)(2,1)}, u32[]{:S(2)}, u32[]{:S(2)}) collective-permute-start(bf16[256,1536]{1,0:T(8,128)(2,1)} %collective-permute-done.18), channel_id=1, source_target_pairs={{1,2},{2,3},{5,6},{6,7},{9,10},{10,11},{13,14},{14,15},{17,18},{18... | collective-permute-start | bytes 2359304 | tf_op jit(solution)/shard_map/ppermute | solution.py:67
  272.5 46.3 %collective-permute-start.21 = (bf16[256,1536]{1,0:T(8,128)(2,1)S(1)}, bf16[256,1536]{1,0:T(8,128)(2,1)}, u32[]{:S(2)}, u32[]{:S(2)}) collective-permute-start(bf16[256,1536]{1,0:T(8,128)(2,1)S(1)} %collective-permute-done.19), channel_id=1, source_target_pairs={{1,0},{2,1},{5,4},{6,5},{9,8},{10,9},{13,12},{14,13},{17,16},{18,1... | collective-permute-start | bytes 2359304 | tf_op jit(solution)/shard_map/ppermute | solution.py:68
  287.9 33.0 %collective-permute-start.26 = (bf16[256,1536]{1,0:T(8,128)(2,1)}, bf16[256,1536]{1,0:T(8,128)(2,1)}, u32[]{:S(2)}, u32[]{:S(2)}) collective-permute-start(bf16[256,1536]{1,0:T(8,128)(2,1)} %collective-permute-done.22), channel_id=1, source_target_pairs={{1,2},{2,3},{5,6},{6,7},{9,10},{10,11},{13,14},{14,15},{17,18},{18... | collective-permute-start | bytes 2359304 | tf_op jit(solution)/shard_map/ppermute | solution.py:67
  318.9 40.5 %collective-permute-start.24 = (bf16[256,1536]{1,0:T(8,128)(2,1)}, bf16[256,1536]{1,0:T(8,128)(2,1)S(1)}, u32[]{:S(2)}, u32[]{:S(2)}) collective-permute-start(bf16[256,1536]{1,0:T(8,128)(2,1)} %collective-permute-done.20), channel_id=1, source_target_pairs={{2,3},{6,7},{10,11},{14,15},{18,19},{22,23},{26,27},{30,31}} | collective-permute-start | bytes 2359304 | tf_op jit(solution)/shard_map/ppermute | solution.py:67
  319.6 39.8 %collective-permute-start.25 = (bf16[256,1536]{1,0:T(8,128)(2,1)}, bf16[256,1536]{1,0:T(8,128)(2,1)S(1)}, u32[]{:S(2)}, u32[]{:S(2)}) collective-permute-start(bf16[256,1536]{1,0:T(8,128)(2,1)} %collective-permute-done.21), channel_id=1, source_target_pairs={{1,0},{5,4},{9,8},{13,12},{17,16},{21,20},{25,24},{29,28}} | collective-permute-start | bytes 2359304 | tf_op jit(solution)/shard_map/ppermute | solution.py:68
  320.9 38.5 %collective-permute-start.28 = (bf16[256,1536]{1,0:T(8,128)(2,1)}, bf16[256,1536]{1,0:T(8,128)(2,1)S(1)}, u32[]{:S(2)}, u32[]{:S(2)}) collective-permute-start(bf16[256,1536]{1,0:T(8,128)(2,1)} %collective-permute-done.26), channel_id=1, source_target_pairs={{2,3},{6,7},{10,11},{14,15},{18,19},{22,23},{26,27},{30,31}} | collective-permute-start | bytes 2359304 | tf_op jit(solution)/shard_map/ppermute | solution.py:67
  321.6 37.8 %collective-permute-start.29 = (bf16[256,1536]{1,0:T(8,128)(2,1)}, bf16[256,1536]{1,0:T(8,128)(2,1)S(1)}, u32[]{:S(2)}, u32[]{:S(2)}) collective-permute-start(bf16[256,1536]{1,0:T(8,128)(2,1)} %collective-permute-done.27), channel_id=1, source_target_pairs={{1,0},{5,4},{9,8},{13,12},{17,16},{21,20},{25,24},{29,28}} | collective-permute-start | bytes 2359304 | tf_op jit(solution)/shard_map/ppermute | solution.py:68
  428.8 33.9 %collective-permute-start.36 = (bf16[256,1536]{1,0:T(8,128)(2,1)S(1)}, bf16[256,1536]{1,0:T(8,128)(2,1)S(1)}, u32[]{:S(2)}, u32[]{:S(2)}) collective-permute-start(bf16[256,1536]{1,0:T(8,128)(2,1)S(1)} %get-tuple-element.495), channel_id=1, source_target_pairs={{0,1},{4,5},{8,9},{12,13},{16,17},{20,21},{24,25},{28,29}} | collective-permute-start | bytes 2359304 | tf_op jit(solution)/shard_map/ppermute | solution.py:132
  430.5 32.2 %collective-permute-start.37 = (bf16[256,1536]{1,0:T(8,128)(2,1)S(1)}, bf16[256,1536]{1,0:T(8,128)(2,1)S(1)}, u32[]{:S(2)}, u32[]{:S(2)}) collective-permute-start(bf16[256,1536]{1,0:T(8,128)(2,1)S(1)} %get-tuple-element.494), channel_id=1, source_target_pairs={{3,2},{7,6},{11,10},{15,14},{19,18},{23,22},{27,26},{31,30}} | collective-permute-start | bytes 2359304 | tf_op jit(solution)/shard_map/ppermute | solution.py:133
  446.3 33.3 %collective-permute-start.32 = (bf16[256,1536]{1,0:T(8,128)(2,1)S(1)}, bf16[256,1536]{1,0:T(8,128)(2,1)S(1)}, u32[]{:S(2)}, u32[]{:S(2)}) collective-permute-start(bf16[256,1536]{1,0:T(8,128)(2,1)S(1)} %get-tuple-element.491), channel_id=1, source_target_pairs={{0,1},{1,2},{4,5},{5,6},{8,9},{9,10},{12,13},{13,14},{16,17},{17,1... | collective-permute-start | bytes 2359304 | tf_op jit(solution)/shard_map/ppermute | solution.py:132
  463.1 33.3 %collective-permute-start.38 = (bf16[256,1536]{1,0:T(8,128)(2,1)S(1)}, bf16[256,1536]{1,0:T(8,128)(2,1)S(1)}, u32[]{:S(2)}, u32[]{:S(2)}) collective-permute-start(bf16[256,1536]{1,0:T(8,128)(2,1)S(1)} %get-tuple-element.489), channel_id=1, source_target_pairs={{0,1},{1,2},{4,5},{5,6},{8,9},{9,10},{12,13},{13,14},{16,17},{17,1... | collective-permute-start | bytes 2359304 | tf_op jit(solution)/shard_map/ppermute | solution.py:132
  480.0 36.3 %collective-permute-start.34 = (bf16[256,1536]{1,0:T(8,128)(2,1)S(1)}, bf16[256,1536]{1,0:T(8,128)(2,1)}, u32[]{:S(2)}, u32[]{:S(2)}) collective-permute-start(bf16[256,1536]{1,0:T(8,128)(2,1)S(1)} %get-tuple-element.487), channel_id=1, source_target_pairs={{0,1},{1,2},{2,3},{4,5},{5,6},{6,7},{8,9},{9,10},{10,11},{12,13},{... | collective-permute-start | bytes 2359304 | tf_op jit(solution)/shard_map/ppermute | solution.py:132
  529.7 45.8 %collective-permute-start.49 = (bf16[272,1536]{1,0:T(8,128)(2,1)S(1)}, bf16[272,1536]{1,0:T(8,128)(2,1)S(1)}, u32[]{:S(2)}, u32[]{:S(2)}) collective-permute-start(bf16[272,1536]{1,0:T(8,128)(2,1)S(1)} %fusion.52.more_ref), channel_id=1, source_target_pairs={{0,1},{1,2},{2,3},{4,5},{5,6},{6,7},{8,9},{9,10},{10,11},{12,13},{... | collective-permute-start | bytes 2506760 | tf_op jit(solution)/shard_map/ppermute | solution.py:67
  534.1 41.4 %collective-permute-start.50 = (bf16[272,1536]{1,0:T(8,128)(2,1)S(1)}, bf16[272,1536]{1,0:T(8,128)(2,1)S(1)}, u32[]{:S(2)}, u32[]{:S(2)}) collective-permute-start(bf16[272,1536]{1,0:T(8,128)(2,1)S(1)} %fusion.52.more_ref), channel_id=1, source_target_pairs={{1,0},{2,1},{3,2},{5,4},{6,5},{7,6},{9,8},{10,9},{11,10},{13,12},{... | collective-permute-start | bytes 2506760 | tf_op jit(solution)/shard_map/ppermute | solution.py:68
  535.4 38.1 %collective-permute-start.45 = (bf16[256,1536]{1,0:T(8,128)(2,1)S(1)}, bf16[256,1536]{1,0:T(8,128)(2,1)S(1)}, u32[]{:S(2)}, u32[]{:S(2)}) collective-permute-start(bf16[256,1536]{1,0:T(8,128)(2,1)S(1)} %get-tuple-element.515.tok_ref), channel_id=1, source_target_pairs={{0,1},{1,2},{2,3},{4,5},{5,6},{6,7},{8,9},{9,10},{10,11},{12,13},{... | collective-permute-start | bytes 2359304 | tf_op jit(solution)/shard_map/ppermute | solution.py:67
  540.0 33.5 %collective-permute-start.46 = (bf16[256,1536]{1,0:T(8,128)(2,1)S(1)}, bf16[256,1536]{1,0:T(8,128)(2,1)S(1)}, u32[]{:S(2)}, u32[]{:S(2)}) collective-permute-start(bf16[256,1536]{1,0:T(8,128)(2,1)S(1)} %get-tuple-element.515.tok_ref), channel_id=1, source_target_pairs={{1,0},{2,1},{3,2},{5,4},{6,5},{7,6},{9,8},{10,9},{11,10},{13,12},{... | collective-permute-start | bytes 2359304 | tf_op jit(solution)/shard_map/ppermute | solution.py:68
  573.5 37.8 %collective-permute-start.47 = (bf16[256,1536]{1,0:T(8,128)(2,1)S(1)}, bf16[256,1536]{1,0:T(8,128)(2,1)S(1)}, u32[]{:S(2)}, u32[]{:S(2)}) collective-permute-start(bf16[256,1536]{1,0:T(8,128)(2,1)S(1)} %collective-permute-done.45), channel_id=1, source_target_pairs={{1,2},{2,3},{5,6},{6,7},{9,10},{10,11},{13,14},{14,15},{17,18},{18... | collective-permute-start | bytes 2359304 | tf_op jit(solution)/shard_map/ppermute | solution.py:67
  574.2 37.1 %collective-permute-start.48 = (bf16[256,1536]{1,0:T(8,128)(2,1)S(1)}, bf16[256,1536]{1,0:T(8,128)(2,1)S(1)}, u32[]{:S(2)}, u32[]{:S(2)}) collective-permute-start(bf16[256,1536]{1,0:T(8,128)(2,1)S(1)} %collective-permute-done.46), channel_id=1, source_target_pairs={{1,0},{2,1},{5,4},{6,5},{9,8},{10,9},{13,12},{14,13},{17,16},{18,1... | collective-permute-start | bytes 2359304 | tf_op jit(solution)/shard_map/ppermute | solution.py:68
  575.5 37.8 %collective-permute-start.53 = (bf16[272,1536]{1,0:T(8,128)(2,1)S(1)}, bf16[272,1536]{1,0:T(8,128)(2,1)S(1)}, u32[]{:S(2)}, u32[]{:S(2)}) collective-permute-start(bf16[272,1536]{1,0:T(8,128)(2,1)S(1)} %collective-permute-done.49), channel_id=1, source_target_pairs={{1,2},{2,3},{5,6},{6,7},{9,10},{10,11},{13,14},{14,15},{17,18},{18... | collective-permute-start | bytes 2506760 | tf_op jit(solution)/shard_map/ppermute | solution.py:67
  576.3 37.1 %collective-permute-start.54 = (bf16[272,1536]{1,0:T(8,128)(2,1)S(1)}, bf16[272,1536]{1,0:T(8,128)(2,1)S(1)}, u32[]{:S(2)}, u32[]{:S(2)}) collective-permute-start(bf16[272,1536]{1,0:T(8,128)(2,1)S(1)} %collective-permute-done.50), channel_id=1, source_target_pairs={{1,0},{2,1},{5,4},{6,5},{9,8},{10,9},{13,12},{14,13},{17,16},{18,1... | collective-permute-start | bytes 2506760 | tf_op jit(solution)/shard_map/ppermute | solution.py:68
  611.3 39.0 %collective-permute-start.51 = (bf16[256,1536]{1,0:T(8,128)(2,1)S(1)}, bf16[256,1536]{1,0:T(8,128)(2,1)S(1)}, u32[]{:S(2)}, u32[]{:S(2)}) collective-permute-start(bf16[256,1536]{1,0:T(8,128)(2,1)S(1)} %collective-permute-done.47), channel_id=1, source_target_pairs={{2,3},{6,7},{10,11},{14,15},{18,19},{22,23},{26,27},{30,31}} | collective-permute-start | bytes 2359304 | tf_op jit(solution)/shard_map/ppermute | solution.py:67
  612.0 38.3 %collective-permute-start.52 = (bf16[256,1536]{1,0:T(8,128)(2,1)S(1)}, bf16[256,1536]{1,0:T(8,128)(2,1)S(1)}, u32[]{:S(2)}, u32[]{:S(2)}) collective-permute-start(bf16[256,1536]{1,0:T(8,128)(2,1)S(1)} %collective-permute-done.48), channel_id=1, source_target_pairs={{1,0},{5,4},{9,8},{13,12},{17,16},{21,20},{25,24},{29,28}} | collective-permute-start | bytes 2359304 | tf_op jit(solution)/shard_map/ppermute | solution.py:68
  613.3 37.0 %collective-permute-start.55 = (bf16[272,1536]{1,0:T(8,128)(2,1)S(1)}, bf16[272,1536]{1,0:T(8,128)(2,1)S(1)}, u32[]{:S(2)}, u32[]{:S(2)}) collective-permute-start(bf16[272,1536]{1,0:T(8,128)(2,1)S(1)} %collective-permute-done.53), channel_id=1, source_target_pairs={{2,3},{6,7},{10,11},{14,15},{18,19},{22,23},{26,27},{30,31}} | collective-permute-start | bytes 2506760 | tf_op jit(solution)/shard_map/ppermute | solution.py:67
  614.0 36.9 %collective-permute-start.56 = (bf16[272,1536]{1,0:T(8,128)(2,1)S(1)}, bf16[272,1536]{1,0:T(8,128)(2,1)S(1)}, u32[]{:S(2)}, u32[]{:S(2)}) collective-permute-start(bf16[272,1536]{1,0:T(8,128)(2,1)S(1)} %collective-permute-done.54), channel_id=1, source_target_pairs={{1,0},{5,4},{9,8},{13,12},{17,16},{21,20},{25,24},{29,28}} | collective-permute-start | bytes 2506760 | tf_op jit(solution)/shard_map/ppermute | solution.py:68
  689.3 38.1 %collective-permute-start.57 = (bf16[512,1536]{1,0:T(8,128)(2,1)S(1)}, bf16[512,1536]{1,0:T(8,128)(2,1)S(1)}, u32[]{:S(2)}, u32[]{:S(2)}) collective-permute-start(bf16[512,1536]{1,0:T(8,128)(2,1)S(1)} %get-tuple-element.475), channel_id=1, source_target_pairs={{0,1},{4,5},{8,9},{12,13},{16,17},{20,21},{24,25},{28,29}} | collective-permute-start | bytes 4718600 | tf_op jit(solution)/shard_map/ppermute | solution.py:132
  844.7 47.6 %collective-permute-start.69 = (bf16[384,512]{1,0:T(8,128)(2,1)}, bf16[384,512]{1,0:T(8,128)(2,1)S(1)}, u32[]{:S(2)}, u32[]{:S(2)}) collective-permute-start(bf16[384,512]{1,0:T(8,128)(2,1)} %get-tuple-element.508), channel_id=1, source_target_pairs={{2,0},{3,1},{6,4},{7,5},{10,8},{11,9},{14,12},{15,13},{18,16},{19,... | collective-permute-start | bytes 1179656 | tf_op jit(solution)/shard_map/ppermute | solution.py:205
  846.0 46.3 %collective-permute-start.70 = (bf16[384,512]{1,0:T(8,128)(2,1)}, bf16[384,512]{1,0:T(8,128)(2,1)S(1)}, u32[]{:S(2)}, u32[]{:S(2)}) collective-permute-start(bf16[384,512]{1,0:T(8,128)(2,1)} %get-tuple-element.507), channel_id=1, source_target_pairs={{3,0},{7,4},{11,8},{15,12},{19,16},{23,20},{27,24},{31,28}} | collective-permute-start | bytes 1179656 | tf_op jit(solution)/shard_map/ppermute | solution.py:205
  892.3 66.9 %collective-permute-start.72 = (bf16[2,192,768]{2,1,0:T(8,128)(2,1)}, bf16[2,192,768]{2,1,0:T(8,128)(2,1)}, u32[]{:S(2)}, u32[]{:S(2)}) collective-permute-start(bf16[2,192,768]{2,1,0:T(8,128)(2,1)} %add_convert_fusion.9), channel_id=1, source_target_pairs={{0,8},{4,12},{8,0},{12,4},{16,24},{20,28},{24,16},{28,20},{1,9},{5... | collective-permute-start | bytes 1769480 | tf_op jit(solution)/shard_map/ppermute | solution.py:210
  894.2 65.0 %collective-permute-start.73 = (bf16[2,192,768]{2,1,0:T(8,128)(2,1)S(1)}, bf16[2,192,768]{2,1,0:T(8,128)(2,1)}, u32[]{:S(2)}, u32[]{:S(2)}) collective-permute-start(bf16[2,192,768]{2,1,0:T(8,128)(2,1)S(1)} %add_convert_fusion.8), channel_id=1, source_target_pairs={{0,16},{4,20},{8,24},{12,28},{16,0},{20,4},{24,8},{28,12},{1,17},{... | collective-permute-start | bytes 1769480 | tf_op jit(solution)/shard_map/ppermute | solution.py:210
  899.4 59.8 %collective-permute-start.74 = (f32[1,1]{1,0:T(1,128)}, f32[1,1]{1,0:T(1,128)}, u32[]{:S(2)}, u32[]{:S(2)}) collective-permute-start(f32[1,1]{1,0:T(1,128)} %add.675), channel_id=1, source_target_pairs={{0,2},{1,3},{2,0},{3,1},{4,6},{5,7},{6,4},{7,5},{8,10},{9,11},{10,... | collective-permute-start | bytes 20 | tf_op jit(solution)/shard_map/ppermute | solution.py:210
  985.4 47.9 %collective-permute-start.79 = (bf16[304,1536]{1,0:T(8,128)(2,1)}, bf16[304,1536]{1,0:T(8,128)(2,1)}, u32[]{:S(2)}, u32[]{:S(2)}) collective-permute-start(bf16[304,1536]{1,0:T(8,128)(2,1)} %pad_maximum_fusion.9), channel_id=1, source_target_pairs={{3,2},{7,6},{11,10},{15,14},{19,18},{23,22},{27,26},{31,30}} | collective-permute-start | bytes 2801672 | tf_op jit(solution)/shard_map/ppermute | solution.py:133
  990.0 43.3 %collective-permute-start.78 = (bf16[304,1536]{1,0:T(8,128)(2,1)}, bf16[304,1536]{1,0:T(8,128)(2,1)}, u32[]{:S(2)}, u32[]{:S(2)}) collective-permute-start(bf16[304,1536]{1,0:T(8,128)(2,1)} %pad_maximum_fusion.8), channel_id=1, source_target_pairs={{0,1},{4,5},{8,9},{12,13},{16,17},{20,21},{24,25},{28,29}} | collective-permute-start | bytes 2801672 | tf_op jit(solution)/shard_map/ppermute | solution.py:132
  992.3 34.2 %collective-permute-start.80 = (bf16[256,1536]{1,0:T(8,128)(2,1)}, bf16[256,1536]{1,0:T(8,128)(2,1)}, u32[]{:S(2)}, u32[]{:S(2)}) collective-permute-start(bf16[256,1536]{1,0:T(8,128)(2,1)} %get-tuple-element.505), channel_id=1, source_target_pairs={{0,1},{4,5},{8,9},{12,13},{16,17},{20,21},{24,25},{28,29}} | collective-permute-start | bytes 2359304 | tf_op jit(solution)/shard_map/ppermute | solution.py:132
  1035.4 35.2 %collective-permute-start.83 = (bf16[304,1536]{1,0:T(8,128)(2,1)S(1)}, bf16[304,1536]{1,0:T(8,128)(2,1)S(1)}, u32[]{:S(2)}, u32[]{:S(2)}) collective-permute-start(bf16[304,1536]{1,0:T(8,128)(2,1)S(1)} %get-tuple-element.542), channel_id=1, source_target_pairs={{0,1},{1,2},{4,5},{5,6},{8,9},{9,10},{12,13},{13,14},{16,17},{17,1... | collective-permute-start | bytes 2801672 | tf_op jit(solution)/shard_map/ppermute | solution.py:132
  1038.3 32.3 %collective-permute-start.84 = (bf16[304,1536]{1,0:T(8,128)(2,1)S(1)}, bf16[304,1536]{1,0:T(8,128)(2,1)S(1)}, u32[]{:S(2)}, u32[]{:S(2)}) collective-permute-start(bf16[304,1536]{1,0:T(8,128)(2,1)S(1)} %get-tuple-element.541), channel_id=1, source_target_pairs={{2,1},{3,2},{6,5},{7,6},{10,9},{11,10},{14,13},{15,14},{18,17},{19... | collective-permute-start | bytes 2801672 | tf_op jit(solution)/shard_map/ppermute | solution.py:133
  1039.2 43.4 %collective-permute-start.82 = (bf16[2,192,681]{2,1,0:T(8,128)(2,1)S(1)}, bf16[2,192,681]{2,1,0:T(8,128)(2,1)S(1)}, u32[]{:S(2)}, u32[]{:S(2)}) collective-permute-start(bf16[2,192,681]{2,1,0:T(8,128)(2,1)S(1)} %add_convert_fusion.7), channel_id=1, source_target_pairs={{0,8},{4,12},{8,0},{12,4},{16,24},{20,28},{24,16},{28,20},{1,9},{5... | collective-permute-start | bytes 1569032 | tf_op jit(solution)/shard_map/ppermute | solution.py:210
  1050.8 32.9 %collective-permute-start.89 = (bf16[256,1536]{1,0:T(8,128)(2,1)S(1)}, bf16[256,1536]{1,0:T(8,128)(2,1)S(1)}, u32[]{:S(2)}, u32[]{:S(2)}) collective-permute-start(bf16[256,1536]{1,0:T(8,128)(2,1)S(1)} %add_convert_fusion.5), channel_id=1, source_target_pairs={{1,0},{2,1},{3,2},{5,4},{6,5},{7,6},{9,8},{10,9},{11,10},{13,12},{... | collective-permute-start | bytes 2359304 | tf_op jit(solution)/shard_map/ppermute | solution.py:133
  1052.3 35.2 %collective-permute-start.88 = (bf16[256,1536]{1,0:T(8,128)(2,1)S(1)}, bf16[256,1536]{1,0:T(8,128)(2,1)S(1)}, u32[]{:S(2)}, u32[]{:S(2)}) collective-permute-start(bf16[256,1536]{1,0:T(8,128)(2,1)S(1)} %add_convert_fusion.6), channel_id=1, source_target_pairs={{0,1},{1,2},{2,3},{4,5},{5,6},{6,7},{8,9},{9,10},{10,11},{12,13},{... | collective-permute-start | bytes 2359304 | tf_op jit(solution)/shard_map/ppermute | solution.py:132
  1082.6 45.0 %collective-permute-start.94 = (f32[1,1]{1,0:T(1,128)}, f32[1,1]{1,0:T(1,128)}, u32[]{:S(2)}, u32[]{:S(2)}) collective-permute-start(f32[1,1]{1,0:T(1,128)} %add.676), channel_id=1, source_target_pairs={{0,4},{4,0},{8,12},{12,8},{16,20},{20,16},{24,28},{28,24},{1,5},{5... | collective-permute-start | bytes 20 | tf_op jit(solution)/shard_map/ppermute | solution.py:210
  (186 other events, 3147.8 us)
Sparse Core Ops, SparseCore 0:
  13.0 51.5 all-gather.2
  66.5 219.0 all-gather.4
  798.8 301.9 reduce-scatter.1

commit v14 on v13

--- a/solution.py
+++ b/solution.py
@@ -994,13 +994,14 @@
     d_hidden_norm, gain_two_part = norm_two_pull(d_normed_two)
     d_hidden = d_out + d_hidden_norm
     d_proj = (resid_mult * d_hidden).astype(low)
-    d_attended = dot("kd,td->kt", full_out, d_proj).astype(low)
-    moved = exchange(d_attended.reshape(n, heads_w, shard_len))
-    moved[0][1], d_proj, d_logits = tie(moved[0][1], d_proj, d_logits)
     out_pairs = out_grads(mine.reshape(1), attn_rows, d_proj, order_a, order_b)
     out_sums = [Halving(*pair, bits) for pair, bits in zip(out_pairs, (order_a, order_b))]
     for each in out_sums:
         each.go()
+    d_attended = dot("kd,td->kt", full_out, d_proj).astype(low)
+    (d_attended,) = land(out_sums, d_attended)
+    moved = exchange(d_attended.reshape(n, heads_w, shard_len))
+    for each in out_sums:
         each.add()
     router_part = sum(
         dot("td,et->de", half, half_logits)
@@ -1010,8 +1011,9 @@
             (shard[1], shard_logits[:experts_here, middle:]),
         )
     )
-    own_columns = jnp.zeros((width, expert_total), full)
-    own_columns = lax.dynamic_update_slice_in_dim(own_columns, router_part, me * experts_here, 1)
+    own_columns = jnp.where(
+        expert_ids // experts_here == me, jnp.concatenate([router_part] * n, axis=1), 0.0
+    )
     own_columns = jnp.concatenate([own_columns, gain_two_part[:, None]], axis=1).astype(low)
     moved, own_columns, squares = leave(out_sums, moved, own_columns, squares)
     squares = loss_steps.send(squares)
@@ -1094,31 +1096,41 @@
         ),
     ]
     done = [input_grad]
+    grads = [
+        jnp.zeros((w_qkv.shape[0], QKV_W), full),
+        jnp.zeros((w_out.shape[0], width), full),
+        jnp.zeros((w_qkv.shape[0], block.shape[1] - group_w - width // n), full),
+        jnp.zeros((w_qkv.shape[0],), full),
+    ]
+
+    def write(grads, turn):
+        qkv_grad, out_grad, rest, gain_sum = grads
+        came = arrived(rights, lefts, turn).astype(full)
+        own_part, start = came[:, :group_w], order[turn] * group_w
+        own_qkv = lax.dynamic_slice_in_dim(w_qkv, start, group_w, 1).astype(full)
+        return [
+            lax.dynamic_update_slice_in_dim(qkv_grad, own_part, start, 1),
+            lax.dynamic_update_slice_in_dim(
+                out_grad, came[:, -(width // n) :], order[turn] * (width // n), 1
+            ),
+            rest + came[:, group_w : -(width // n)],
+            gain_sum + jnp.sum(own_part * own_qkv, axis=1),
+        ]
+
     for k in range(1, n):
         right, left = line_move(rights[-1], lefts[-1], k)
+        grads = write(grads, k - 1)
         if k < 3:
             done.append(last_work[k - 1]())
-        right, left, done[-1], squares = tie(right, left, done[-1], squares)
+        right, left, done[-1], squares, grads = tie(right, left, done[-1], squares, grads)
         squares = loss_steps.send(squares)
         rights.append(right)
         lefts.append(left)
+    qkv_grad, out_grad, rest, gain_sum = write(grads, n - 1)
     input_grad, gate_up_grad, down_grad = done
     gate_grad, up_grad = gate_up_grad[:, :, :hidden_w], gate_up_grad[:, :, hidden_w:]
-    qkv_grad = jnp.zeros((w_qkv.shape[0], QKV_W), full)
-    out_grad = jnp.zeros((w_out.shape[0], width), full)
-    rest = 0.0
-    for turn in range(n):
-        block = arrived(rights, lefts, turn).astype(full)
-        place = order[turn]
-        qkv_grad = lax.dynamic_update_slice_in_dim(
-            qkv_grad, block[:, :group_w], place * group_w, 1
-        )
-        out_grad = lax.dynamic_update_slice_in_dim(
-            out_grad, block[:, -(width // n) :], place * (width // n), 1
-        )
-        rest = rest + block[:, group_w : -(width // n)]
     router_grad, gain_two_grad = rest[:, :expert_total], rest[:, expert_total]
-    gain_one_grad = jnp.sum(qkv_grad * w_qkv.astype(full), axis=1) / gain_one.astype(full)
+    gain_one_grad = gain_sum / gain_one.astype(full)
     for _ in range(4):
         squares = loss_steps.send(squares)
     loss_value = squares[0, 0] / (valid_count * width)

time: 1180 us -> 1180 us (level)
    ppermute x6, waiting for transfers between devices: 57.2 us -> 31.5 us  [exchange(): lefts[k] = lax.ppermute(to_left, 'seq', [(i, i - k) for i in range(k, n)])]
    ppermute x6, waiting for transfers between devices: 13.2 us -> 29.3 us  [exchange(): lax.ppermute(to_right, 'seq', [(i, i + k) for i in range(n - k)])]
  transfers between devices with their start and end apart: 104 -> 104, of which waited for: 37 -> 39; matrix products, arithmetic and copies ran while one was open for 14% -> 14% of each run, Pallas kernels for 26% -> 26%
where the time goes in v14:
time: 1180 us; the launch traced here: 1170 us
  Pallas kernels  386 us (33%)
  waiting for transfers between devices  283 us (24%)
  starting transfers between devices  221 us (19%)
  other arithmetic  123 us (10%)
  local copies, waits for them, and re-layouts  73.9 us (6%)
  between operations  40.2 us (3%)
  matrix products  38.6 us (3%)
    pallas_call x8, Pallas kernels, shard_call(): pl.pallas_call(kernel, grid_spec=pltpu.PrefetchScalarGridSpec(num_scalar_...  230 us
    ppermute x15, waiting for transfers between devices, line_pass(): lax.ppermute(to_right, 'seq', [(i, i + 1) for i in range(n - k)])  128 us
    ppermute x15, starting transfers between devices, line_pass(): lax.ppermute(to_right, 'seq', [(i, i + 1) for i in range(n - k)])  74.3 us
    ppermute x21, waiting for transfers between devices, line_move(): lax.ppermute(left, 'seq', [(i, i - 1) for i in range(1, n - k + 1)])  62.3 us
    pallas_call x1, Pallas kernels, attention_backward(): pl.pallas_call(functools.partial(backward_kernel, seq_len, query_rows, ke...  58.4 us
    pallas_call x2, Pallas kernels, weight_grads(): pl.pallas_call(functools.partial(grads_kernel, few), grid=(stop - first,)...  50.8 us
    ppermute x21, starting transfers between devices, line_move(): lax.ppermute(right, 'seq', [(i, i + 1) for i in range(k - 1, n - 1)])  50.3 us
    pallas_call x1, Pallas kernels, attention_forward(): pl.pallas_call(functools.partial(forward_kernel, seq_len, query_rows, key...  41.7 us
  transfers between devices with their start and end apart: 104, of which 39 were waited for; matrix products, arithmetic and copies ran while one was open for 14% of the time, Pallas kernels for 26%

profile of v14, /device:TPU:0, one launch (start us, length us, event | category | flops | bytes accessed | tf_op | source)
XLA Modules:
  0.0 1165.7 jit_solution(10091642897186844271)
XLA Ops:
  15.1 6.4 maximum_maximum_fusion
  23.2 6.0 collective-permute-start
  31.8 5.5 collective-permute-start.2
  63.0 6.5 collective-permute-done.3
  89.8 14.5 %collective-permute-done.7 = bf16[272,1536]{1,0:T(8,128)(2,1)} collective-permute-done((bf16[272,1536]{1,0:T(8,128)(2,1)}, bf16[272,1536]{1,0:T(8,128)(2,1)}, u32[]{:S(2)}, u32[]{:S(2)}) %collective-permute-start.7) | collective-permute-done | bytes 835616 | tf_op jit(solution)/shard_map/ppermute | solution.py:68
  121.2 16.5 %collective-permute-done.11 = bf16[272,1536]{1,0:T(8,128)(2,1)} collective-permute-done((bf16[272,1536]{1,0:T(8,128)(2,1)}, bf16[272,1536]{1,0:T(8,128)(2,1)}, u32[]{:S(2)}, u32[]{:S(2)}) %collective-permute-start.11) | collective-permute-done | bytes 835616 | tf_op jit(solution)/shard_map/ppermute | solution.py:68
  153.0 41.7 %attention_forward.1 = (bf16[4,384,512]{2,1,0:T(8,128)(2,1)}, f32[2,3,64,2048]{3,2,1,0:T(8,128)}, f32[2,3,1,2048]{3,2,1,0:T(1,128)}) custom-call(s32[1,2048]{1,0:T(1,128)} %bitcast.304, bf16[4,2,5,64,512]{4,3,2,1,0:T(8,128)(2,1)} %copy-done.15, bf16[2,2048,64]{2,1,0:T(8,128)(2,1)} %copy.174.k_ref, bf16[2,64,2048]{2,1,0:T(8,128)(2,1)} %copy.175.vt_ref), custom_call_target="tpu_custom_call" | custom-call | tf_op jit(solution)/shard_map/attention_forward/pallas_call | solution.py:342
  216.0 6.1 collective-permute-done.14
  222.2 16.0 %collective-permute-done.16 = bf16[384,512]{1,0:T(8,128)(2,1)S(1)} collective-permute-done((bf16[384,512]{1,0:T(8,128)(2,1)S(1)}, bf16[384,512]{1,0:T(8,128)(2,1)S(1)}, u32[]{:S(2)}, u32[]{:S(2)}) %collective-permute-start.16) | collective-permute-done | bytes 393248 | tf_op jit(solution)/shard_map/ppermute | solution.py:205
  250.1 5.5 collective-permute-start.22
  256.8 9.1 collective-permute-done.18
  274.0 5.8 collective-permute-done.22
  279.8 8.3 collective-permute-done.23
  293.7 25.2 %experts_forward.4 = (bf16[4,512,1536]{2,1,0:T(8,128)(2,1)}, bf16[10,4,160,1536]{3,2,1,0:T(8,128)(2,1)}, bf16[10,4,160,1024]{3,2,1,0:T(8,128)(2,1)}, f32[10,512]{1,0:T(8,128)S(1)}) custom-call(s32[2]{0:T(128)S(1)} %get-tuple-element.609.at_ref, bf16[256,1536]{1,0:T(8,128)(2,1)S(1)} %get-tuple-element.539.tok_ref, ...), custom_call_target="tpu_custom_call" | custom-call | tf_op jit(solution)/shard_map/experts_forward/pallas_call | solution.py:597
  321.7 10.0 collective-permute-start.29
  334.2 25.2 %experts_forward.5 = (bf16[4,512,1536]{2,1,0:T(8,128)(2,1)}, bf16[10,4,160,1536]{3,2,1,0:T(8,128)(2,1)}, bf16[10,4,160,1024]{3,2,1,0:T(8,128)(2,1)}, f32[10,512]{1,0:T(8,128)S(1)}) custom-call(s32[2]{0:T(128)S(1)} %get-tuple-element.610.at_ref, ...), custom_call_target="tpu_custom_call", output_to_operand_aliasing={{0}: (8, {}), {1}: (9, {}), {2}: (10, {})} | custom-call | tf_op jit(solution)/shard_map/experts_forward/pallas_call | solution.py:597
  368.0 25.2 %experts_forward.6 = (bf16[4,512,1536]{2,1,0:T(8,128)(2,1)}, bf16[10,4,160,1536]{3,2,1,0:T(8,128)(2,1)}, bf16[10,4,160,1024]{3,2,1,0:T(8,128)(2,1)}, f32[10,512]{1,0:T(8,128)S(1)}) custom-call(s32[2]{0:T(128)S(1)} %get-tuple-element.611.at_ref, ...), custom_call_target="tpu_custom_call", output_to_operand_aliasing={{0}: (8, {}), {1}: (9, {}), {2}: (10, {})} | custom-call | tf_op jit(solution)/shard_map/experts_forward/pallas_call | solution.py:597
  393.2 25.2 %experts_forward.7 = (bf16[4,512,1536]{2,1,0:T(8,128)(2,1)}, bf16[10,4,160,1536]{3,2,1,0:T(8,128)(2,1)}, bf16[10,4,160,1024]{3,2,1,0:T(8,128)(2,1)}, f32[10,512]{1,0:T(8,128)S(1)}) custom-call(s32[2]{0:T(128)S(1)} %get-tuple-element.608.at_ref, ...), custom_call_target="tpu_custom_call", output_to_operand_aliasing={{0}: (8, {}), {1}: (9, {}), {2}: (10, {})} | custom-call | tf_op jit(solution)/shard_map/experts_forward/pallas_call | solution.py:597
  422.1 6.1 collective-permute-start.30
  431.5 14.6 %collective-permute-done.30 = bf16[256,1536]{1,0:T(8,128)(2,1)S(1)} collective-permute-done((bf16[256,1536]{1,0:T(8,128)(2,1)S(1)}, bf16[256,1536]{1,0:T(8,128)(2,1)S(1)}, u32[]{:S(2)}, u32[]{:S(2)}) %collective-permute-start.30) | collective-permute-done | bytes 786464 | tf_op jit(solution)/shard_map/ppermute | solution.py:132
  451.6 11.3 collective-permute-done.36
  468.5 11.3 collective-permute-done.32
  480.2 5.3 collective-permute-start.34
  486.9 9.7 collective-permute-done.38
  518.0 5.5 collective-permute-done.40
  541.6 32.2 %experts_backward.4 = (bf16[4,512,1536]{2,1,0:T(8,128)(2,1)}, bf16[10,4,160,1536]{3,2,1,0:T(8,128)(2,1)}, bf16[10,4,160,1024]{3,2,1,0:T(8,128)(2,1)}, bf16[10,4,...) custom-call(s32[2]{0:T(128)S(1)} %get-tuple-element.609.at_ref, bf16[256,1536]{1,0:T(8,128)(2,1)S(1)} %get-tuple-element.533.tok_ref, ...), custom_call_target="tpu_custom_call" | custom-call | tf_op jit(solution)/shard_map/experts_backward/pallas_call | solution.py:597
  579.3 32.2 %experts_backward.5 = (bf16[4,512,1536]{2,1,0:T(8,128)(2,1)}, bf16[10,4,160,1536]{3,2,1,0:T(8,128)(2,1)}, bf16[10,4,160,1024]{3,2,1,0:T(8,128)(2,1)}, bf16[10,4,...) custom-call(s32[2]{0:T(128)S(1)} %get-tuple-element.610.at_ref, ...), custom_call_target="tpu_custom_call", output_to_operand_aliasing={{0}: (10, {}), {1}: (11, {}), {2}: (12, {}), {3}: (13, {})} | custom-call | tf_op jit(solution)/shard_map/experts_backward/pallas_call | solution.py:597
  618.4 32.2 %experts_backward.6 = (bf16[4,512,1536]{2,1,0:T(8,128)(2,1)}, bf16[10,4,160,1536]{3,2,1,0:T(8,128)(2,1)}, bf16[10,4,160,1024]{3,2,1,0:T(8,128)(2,1)}, bf16[10,4,...) custom-call(s32[2]{0:T(128)S(1)} %get-tuple-element.611.at_ref, ...), custom_call_target="tpu_custom_call", output_to_operand_aliasing={{0}: (10, {}), {1}: (11, {}), {2}: (12, {}), {3}: (13, {})} | custom-call | tf_op jit(solution)/shard_map/experts_backward/pallas_call | solution.py:597
  655.2 32.2 %experts_backward.7 = (bf16[4,512,1536]{2,1,0:T(8,128)(2,1)}, bf16[10,4,160,1536]{3,2,1,0:T(8,128)(2,1)}, bf16[10,4,160,1024]{3,2,1,0:T(8,128)(2,1)}, bf16[10,4,...) custom-call(s32[2]{0:T(128)S(1)} %get-tuple-element.608.at_ref, ...), custom_call_target="tpu_custom_call", output_to_operand_aliasing={{0}: (10, {}), {1}: (11, {}), {2}: (12, {}), {3}: (13, {})} | custom-call | tf_op jit(solution)/shard_map/experts_backward/pallas_call | solution.py:597
  689.5 11.9 %collective-permute-start.57 = (bf16[512,1536]{1,0:T(8,128)(2,1)S(1)}, bf16[512,1536]{1,0:T(8,128)(2,1)S(1)}, u32[]{:S(2)}, u32[]{:S(2)}) collective-permute-start(bf16[512,1536]{1,0:T(8,128)(2,1)S(1)} %get-tuple-element.493), channel_id=1, source_target_pairs={{0,1},{4,5},{8,9},{12,13},{16,17},{20,21},{24,25},{28,29}} | collective-permute-start | bytes 4718600 | tf_op jit(solution)/shard_map/ppermute | solution.py:132
  702.4 25.4 %weight_grads.2.refs_0_ = bf16[10,1536,1536]{2,1,0:T(8,128)(2,1)} custom-call(bf16[10,640,1536]{2,1,0:T(8,128)(2,1)} %bitcast.270, bf16[10,640,1024]{2,1,0:T(8,128)(2,1)} %bitcast.272, bf16[10,640,512]{2,1,0:T(8,128)(2,1)} %bitcast.274, bf16[10,640,1536]{2,1,0:T(8,128)(2,1)} %bitcast.268), custom_call_target="tpu_custom_call" | custom-call | tf_op jit(solution)/shard_map/weight_grads/pallas_call | solution.py:768
  737.5 25.4 %weight_grads.3 = bf16[10,1536,1536]{2,1,0:T(8,128)(2,1)} custom-call(bf16[10,640,1536]{2,1,0:T(8,128)(2,1)} %bitcast.271, bf16[10,640,1024]{2,1,0:T(8,128)(2,1)} %bitcast.273, bf16[10,640,512]{2,1,0:T(8,128)(2,1)} %bitcast.275, bf16[10,640,1536]{2,1,0:T(8,128)(2,1)} %bitcast.269, ...), custom_call_target="tpu_custom_call", output_to_operand_aliasing={{}: (4, {})} | custom-call | tf_op jit(solution)/shard_map/weight_grads/pallas_call | solution.py:768
  766.1 5.3 collective-permute-start.61
  773.1 21.3 %collective-permute-done.61 = bf16[512,1536]{1,0:T(8,128)(2,1)S(1)} collective-permute-done((bf16[512,1536]{1,0:T(8,128)(2,1)S(1)}, bf16[512,1536]{1,0:T(8,128)(2,1)S(1)}, u32[]{:S(2)}, u32[]{:S(2)}) %collective-permute-start.61) | collective-permute-done | bytes 1572896 | tf_op jit(solution)/shard_map/ppermute | solution.py:132
  821.0 5.8 out_grads.1
  827.9 6.1 fusion.33
  850.6 6.7 collective-permute-done.66.refs_2_
  857.3 7.4 collective-permute-done.67.refs_3_
  864.7 15.5 %collective-permute-done.69.refs_5_ = bf16[384,512]{1,0:T(8,128)(2,1)S(1)} collective-permute-done((bf16[384,512]{1,0:T(8,128)(2,1)S(1)}, bf16[384,512]{1,0:T(8,128)(2,1)S(1)}, u32[]{:S(2)}, u32[]{:S(2)}) %collective-permute-start.69) | collective-permute-done | bytes 393248 | tf_op jit(solution)/shard_map/ppermute | solution.py:205
  890.0 58.4 %attention_backward.1 = (bf16[2,3,64,2048]{3,2,1,0:T(8,128)(2,1)}, bf16[2,64,2048]{2,1,0:T(8,128)(2,1)}, bf16[2,64,2048]{2,1,0:T(8,128)(2,1)}) custom-call(s32[1]{0:T(128)} %bitcast.51.me_ref, s32[1,2048]{1,0:T(1,128)} %bitcast.305, bf16[4,2,5,64,512]{4,3,2,1,0:T(8,128)(2,1)} %copy-done.15, bf16[2,2048,64]{2,1,0:T(8,128)(2,1)} %copy.174.k_ref, ...), custom_call_target="tpu_custom_call" | custom-call | tf_op jit(solution)/shard_map/attention_backward/pallas_call | solution.py:425
  999.0 16.1 %collective-permute-done.80 = bf16[256,1536]{1,0:T(8,128)(2,1)} collective-permute-done((bf16[256,1536]{1,0:T(8,128)(2,1)}, bf16[256,1536]{1,0:T(8,128)(2,1)}, u32[]{:S(2)}, u32[]{:S(2)}) %collective-permute-start.80) | collective-permute-done | bytes 786464 | tf_op jit(solution)/shard_map/ppermute | solution.py:132
  1029.7 9.5 collective-permute-done.85
  1040.9 7.0 collective-permute-start.88
  1047.9 11.3 collective-permute-done.83
  1061.0 7.0 collective-permute-start.90
  1078.7 13.3 %collective-permute-done.90 = bf16[304,1536]{1,0:T(8,128)(2,1)S(1)} collective-permute-done((bf16[304,1536]{1,0:T(8,128)(2,1)S(1)}, bf16[304,1536]{1,0:T(8,128)(2,1)S(1)}, u32[]{:S(2)}, u32[]{:S(2)}) %collective-permute-start.90) | collective-permute-done | bytes 933920 | tf_op jit(solution)/shard_map/ppermute | solution.py:132
  1098.2 7.1 collective-permute-start.92
  1143.2 7.0 collective-permute-done.99
  (664 shorter events, 406.8 us)
Async XLA Ops:
  7.2 70.4 %all-gather.3.cloned.1.call-start = ((), (), s32[]{:S(2)}) async-start(), calls=%async_computation.1 | async-start | bytes 7962624 | tf_op jit(solution)/shard_map/all_gather | solution.py:820
  12.9 280.9 %all-gather.5.cloned.1.call-start = ((), (), s32[]{:S(2)}) async-start(), calls=%async_computation.2 | async-start | bytes 53084160 | tf_op jit(solution)/shard_map/all_gather | solution.py:837
  21.5 1093.7 %reduce-scatter.2.cloned.1.call-start = ((), (), s32[]{:S(2)}) async-start(), calls=%async_computation.3 | async-start | bytes 53084160 | tf_op jit(solution)/shard_map/reduce_scatter | solution.py:992
  23.2 34.6 %collective-permute-start = (bf16[256,1536]{1,0:T(8,128)(2,1)S(1)}, bf16[256,1536]{1,0:T(8,128)(2,1)}, u32[]{:S(2)}, u32[]{:S(2)}) collective-permute-start(bf16[256,1536]{1,0:T(8,128)(2,1)S(1)} %get-tuple-element.547), channel_id=1, source_target_pairs={{0,1},{1,2},{2,3},{4,5},{5,6},{6,7},{8,9},{9,10},{10,11},{12,13},{... | collective-permute-start | bytes 2359304 | tf_op jit(solution)/shard_map/ppermute | solution.py:67
  37.3 32.3 %collective-permute-start.3 = (bf16[272,1536]{1,0:T(8,128)(2,1)S(1)}, bf16[272,1536]{1,0:T(8,128)(2,1)}, u32[]{:S(2)}, u32[]{:S(2)}) collective-permute-start(bf16[272,1536]{1,0:T(8,128)(2,1)S(1)} %pad_maximum_fusion.11), channel_id=1, source_target_pairs={{1,0},{2,1},{3,2},{5,4},{6,5},{7,6},{9,8},{10,9},{11,10},{13,12},{... | collective-permute-start | bytes 2506760 | tf_op jit(solution)/shard_map/ppermute | solution.py:68
  69.6 34.8 %collective-permute-start.7 = (bf16[272,1536]{1,0:T(8,128)(2,1)}, bf16[272,1536]{1,0:T(8,128)(2,1)}, u32[]{:S(2)}, u32[]{:S(2)}) collective-permute-start(bf16[272,1536]{1,0:T(8,128)(2,1)} %collective-permute-done.3), channel_id=1, source_target_pairs={{1,0},{2,1},{5,4},{6,5},{9,8},{10,9},{13,12},{14,13},{17,16},{18,1... | collective-permute-start | bytes 2506760 | tf_op jit(solution)/shard_map/ppermute | solution.py:68
  70.8 33.5 %collective-permute-start.6 = (bf16[272,1536]{1,0:T(8,128)(2,1)}, bf16[272,1536]{1,0:T(8,128)(2,1)}, u32[]{:S(2)}, u32[]{:S(2)}) collective-permute-start(bf16[272,1536]{1,0:T(8,128)(2,1)} %collective-permute-done.2), channel_id=1, source_target_pairs={{1,2},{2,3},{5,6},{6,7},{9,10},{10,11},{13,14},{14,15},{17,18},{18... | collective-permute-start | bytes 2506760 | tf_op jit(solution)/shard_map/ppermute | solution.py:67
  88.6 32.6 %collective-permute-start.9 = (bf16[256,1536]{1,0:T(8,128)(2,1)}, bf16[256,1536]{1,0:T(8,128)(2,1)}, u32[]{:S(2)}, u32[]{:S(2)}) collective-permute-start(bf16[256,1536]{1,0:T(8,128)(2,1)} %collective-permute-done.5), channel_id=1, source_target_pairs={{1,0},{5,4},{9,8},{13,12},{17,16},{21,20},{25,24},{29,28}} | collective-permute-start | bytes 2359304 | tf_op jit(solution)/shard_map/ppermute | solution.py:68
  204.3 33.8 %collective-permute-start.16 = (bf16[384,512]{1,0:T(8,128)(2,1)S(1)}, bf16[384,512]{1,0:T(8,128)(2,1)S(1)}, u32[]{:S(2)}, u32[]{:S(2)}) collective-permute-start(bf16[384,512]{1,0:T(8,128)(2,1)S(1)} %get-tuple-element.541), channel_id=1, source_target_pairs={{2,0},{3,1},{6,4},{7,5},{10,8},{11,9},{14,12},{15,13},{18,16},{19,... | collective-permute-start | bytes 1179656 | tf_op jit(solution)/shard_map/ppermute | solution.py:205
  255.5 32.6 %collective-permute-start.23 = (bf16[256,1536]{1,0:T(8,128)(2,1)S(1)}, bf16[256,1536]{1,0:T(8,128)(2,1)}, u32[]{:S(2)}, u32[]{:S(2)}) collective-permute-start(bf16[256,1536]{1,0:T(8,128)(2,1)S(1)} %get-tuple-element.538.more_ref), channel_id=1, source_target_pairs={{1,0},{2,1},{3,2},{5,4},{6,5},{7,6},{9,8},{10,9},{11,10},{13,12},{... | collective-permute-start | bytes 2359304 | tf_op jit(solution)/shard_map/ppermute | solution.py:68
  271.1 47.8 %collective-permute-start.20 = (bf16[256,1536]{1,0:T(8,128)(2,1)}, bf16[256,1536]{1,0:T(8,128)(2,1)}, u32[]{:S(2)}, u32[]{:S(2)}) collective-permute-start(bf16[256,1536]{1,0:T(8,128)(2,1)} %collective-permute-done.18), channel_id=1, source_target_pairs={{1,2},{2,3},{5,6},{6,7},{9,10},{10,11},{13,14},{14,15},{17,18},{18... | collective-permute-start | bytes 2359304 | tf_op jit(solution)/shard_map/ppermute | solution.py:67
  272.7 46.2 %collective-permute-start.21 = (bf16[256,1536]{1,0:T(8,128)(2,1)S(1)}, bf16[256,1536]{1,0:T(8,128)(2,1)}, u32[]{:S(2)}, u32[]{:S(2)}) collective-permute-start(bf16[256,1536]{1,0:T(8,128)(2,1)S(1)} %collective-permute-done.19), channel_id=1, source_target_pairs={{1,0},{2,1},{5,4},{6,5},{9,8},{10,9},{13,12},{14,13},{17,16},{18,1... | collective-permute-start | bytes 2359304 | tf_op jit(solution)/shard_map/ppermute | solution.py:68
  288.1 32.8 %collective-permute-start.26 = (bf16[256,1536]{1,0:T(8,128)(2,1)}, bf16[256,1536]{1,0:T(8,128)(2,1)}, u32[]{:S(2)}, u32[]{:S(2)}) collective-permute-start(bf16[256,1536]{1,0:T(8,128)(2,1)} %collective-permute-done.22), channel_id=1, source_target_pairs={{1,2},{2,3},{5,6},{6,7},{9,10},{10,11},{13,14},{14,15},{17,18},{18... | collective-permute-start | bytes 2359304 | tf_op jit(solution)/shard_map/ppermute | solution.py:67
  318.9 40.5 %collective-permute-start.24 = (bf16[256,1536]{1,0:T(8,128)(2,1)}, bf16[256,1536]{1,0:T(8,128)(2,1)S(1)}, u32[]{:S(2)}, u32[]{:S(2)}) collective-permute-start(bf16[256,1536]{1,0:T(8,128)(2,1)} %collective-permute-done.20), channel_id=1, source_target_pairs={{2,3},{6,7},{10,11},{14,15},{18,19},{22,23},{26,27},{30,31}} | collective-permute-start | bytes 2359304 | tf_op jit(solution)/shard_map/ppermute | solution.py:67
  319.6 39.8 %collective-permute-start.25 = (bf16[256,1536]{1,0:T(8,128)(2,1)}, bf16[256,1536]{1,0:T(8,128)(2,1)S(1)}, u32[]{:S(2)}, u32[]{:S(2)}) collective-permute-start(bf16[256,1536]{1,0:T(8,128)(2,1)} %collective-permute-done.21), channel_id=1, source_target_pairs={{1,0},{5,4},{9,8},{13,12},{17,16},{21,20},{25,24},{29,28}} | collective-permute-start | bytes 2359304 | tf_op jit(solution)/shard_map/ppermute | solution.py:68
  321.0 38.5 %collective-permute-start.28 = (bf16[256,1536]{1,0:T(8,128)(2,1)}, bf16[256,1536]{1,0:T(8,128)(2,1)S(1)}, u32[]{:S(2)}, u32[]{:S(2)}) collective-permute-start(bf16[256,1536]{1,0:T(8,128)(2,1)} %collective-permute-done.26), channel_id=1, source_target_pairs={{2,3},{6,7},{10,11},{14,15},{18,19},{22,23},{26,27},{30,31}} | collective-permute-start | bytes 2359304 | tf_op jit(solution)/shard_map/ppermute | solution.py:67
  321.7 37.8 %collective-permute-start.29 = (bf16[256,1536]{1,0:T(8,128)(2,1)}, bf16[256,1536]{1,0:T(8,128)(2,1)S(1)}, u32[]{:S(2)}, u32[]{:S(2)}) collective-permute-start(bf16[256,1536]{1,0:T(8,128)(2,1)} %collective-permute-done.27), channel_id=1, source_target_pairs={{1,0},{5,4},{9,8},{13,12},{17,16},{21,20},{25,24},{29,28}} | collective-permute-start | bytes 2359304 | tf_op jit(solution)/shard_map/ppermute | solution.py:68
  429.0 33.9 %collective-permute-start.36 = (bf16[256,1536]{1,0:T(8,128)(2,1)S(1)}, bf16[256,1536]{1,0:T(8,128)(2,1)S(1)}, u32[]{:S(2)}, u32[]{:S(2)}) collective-permute-start(bf16[256,1536]{1,0:T(8,128)(2,1)S(1)} %get-tuple-element.513), channel_id=1, source_target_pairs={{0,1},{4,5},{8,9},{12,13},{16,17},{20,21},{24,25},{28,29}} | collective-permute-start | bytes 2359304 | tf_op jit(solution)/shard_map/ppermute | solution.py:132
  430.7 32.2 %collective-permute-start.37 = (bf16[256,1536]{1,0:T(8,128)(2,1)S(1)}, bf16[256,1536]{1,0:T(8,128)(2,1)S(1)}, u32[]{:S(2)}, u32[]{:S(2)}) collective-permute-start(bf16[256,1536]{1,0:T(8,128)(2,1)S(1)} %get-tuple-element.512), channel_id=1, source_target_pairs={{3,2},{7,6},{11,10},{15,14},{19,18},{23,22},{27,26},{31,30}} | collective-permute-start | bytes 2359304 | tf_op jit(solution)/shard_map/ppermute | solution.py:133
  446.5 33.3 %collective-permute-start.32 = (bf16[256,1536]{1,0:T(8,128)(2,1)S(1)}, bf16[256,1536]{1,0:T(8,128)(2,1)S(1)}, u32[]{:S(2)}, u32[]{:S(2)}) collective-permute-start(bf16[256,1536]{1,0:T(8,128)(2,1)S(1)} %get-tuple-element.509), channel_id=1, source_target_pairs={{0,1},{1,2},{4,5},{5,6},{8,9},{9,10},{12,13},{13,14},{16,17},{17,1... | collective-permute-start | bytes 2359304 | tf_op jit(solution)/shard_map/ppermute | solution.py:132
  463.3 33.3 %collective-permute-start.38 = (bf16[256,1536]{1,0:T(8,128)(2,1)S(1)}, bf16[256,1536]{1,0:T(8,128)(2,1)S(1)}, u32[]{:S(2)}, u32[]{:S(2)}) collective-permute-start(bf16[256,1536]{1,0:T(8,128)(2,1)S(1)} %get-tuple-element.507), channel_id=1, source_target_pairs={{0,1},{1,2},{4,5},{5,6},{8,9},{9,10},{12,13},{13,14},{16,17},{17,1... | collective-permute-start | bytes 2359304 | tf_op jit(solution)/shard_map/ppermute | solution.py:132
  480.2 35.8 %collective-permute-start.34 = (bf16[256,1536]{1,0:T(8,128)(2,1)S(1)}, bf16[256,1536]{1,0:T(8,128)(2,1)}, u32[]{:S(2)}, u32[]{:S(2)}) collective-permute-start(bf16[256,1536]{1,0:T(8,128)(2,1)S(1)} %get-tuple-element.505), channel_id=1, source_target_pairs={{0,1},{1,2},{2,3},{4,5},{5,6},{6,7},{8,9},{9,10},{10,11},{12,13},{... | collective-permute-start | bytes 2359304 | tf_op jit(solution)/shard_map/ppermute | solution.py:132
  529.9 45.8 %collective-permute-start.49 = (bf16[272,1536]{1,0:T(8,128)(2,1)S(1)}, bf16[272,1536]{1,0:T(8,128)(2,1)S(1)}, u32[]{:S(2)}, u32[]{:S(2)}) collective-permute-start(bf16[272,1536]{1,0:T(8,128)(2,1)S(1)} %fusion.52.more_ref), channel_id=1, source_target_pairs={{0,1},{1,2},{2,3},{4,5},{5,6},{6,7},{8,9},{9,10},{10,11},{12,13},{... | collective-permute-start | bytes 2506760 | tf_op jit(solution)/shard_map/ppermute | solution.py:67
  534.4 41.4 %collective-permute-start.50 = (bf16[272,1536]{1,0:T(8,128)(2,1)S(1)}, bf16[272,1536]{1,0:T(8,128)(2,1)S(1)}, u32[]{:S(2)}, u32[]{:S(2)}) collective-permute-start(bf16[272,1536]{1,0:T(8,128)(2,1)S(1)} %fusion.52.more_ref), channel_id=1, source_target_pairs={{1,0},{2,1},{3,2},{5,4},{6,5},{7,6},{9,8},{10,9},{11,10},{13,12},{... | collective-permute-start | bytes 2506760 | tf_op jit(solution)/shard_map/ppermute | solution.py:68
  535.7 38.1 %collective-permute-start.45 = (bf16[256,1536]{1,0:T(8,128)(2,1)S(1)}, bf16[256,1536]{1,0:T(8,128)(2,1)S(1)}, u32[]{:S(2)}, u32[]{:S(2)}) collective-permute-start(bf16[256,1536]{1,0:T(8,128)(2,1)S(1)} %get-tuple-element.533.tok_ref), channel_id=1, source_target_pairs={{0,1},{1,2},{2,3},{4,5},{5,6},{6,7},{8,9},{9,10},{10,11},{12,13},{... | collective-permute-start | bytes 2359304 | tf_op jit(solution)/shard_map/ppermute | solution.py:67
  540.3 33.5 %collective-permute-start.46 = (bf16[256,1536]{1,0:T(8,128)(2,1)S(1)}, bf16[256,1536]{1,0:T(8,128)(2,1)S(1)}, u32[]{:S(2)}, u32[]{:S(2)}) collective-permute-start(bf16[256,1536]{1,0:T(8,128)(2,1)S(1)} %get-tuple-element.533.tok_ref), channel_id=1, source_target_pairs={{1,0},{2,1},{3,2},{5,4},{6,5},{7,6},{9,8},{10,9},{11,10},{13,12},{... | collective-permute-start | bytes 2359304 | tf_op jit(solution)/shard_map/ppermute | solution.py:68
  573.8 37.7 %collective-permute-start.47 = (bf16[256,1536]{1,0:T(8,128)(2,1)S(1)}, bf16[256,1536]{1,0:T(8,128)(2,1)S(1)}, u32[]{:S(2)}, u32[]{:S(2)}) collective-permute-start(bf16[256,1536]{1,0:T(8,128)(2,1)S(1)} %collective-permute-done.45), channel_id=1, source_target_pairs={{1,2},{2,3},{5,6},{6,7},{9,10},{10,11},{13,14},{14,15},{17,18},{18... | collective-permute-start | bytes 2359304 | tf_op jit(solution)/shard_map/ppermute | solution.py:67
  574.5 37.0 %collective-permute-start.48 = (bf16[256,1536]{1,0:T(8,128)(2,1)S(1)}, bf16[256,1536]{1,0:T(8,128)(2,1)S(1)}, u32[]{:S(2)}, u32[]{:S(2)}) collective-permute-start(bf16[256,1536]{1,0:T(8,128)(2,1)S(1)} %collective-permute-done.46), channel_id=1, source_target_pairs={{1,0},{2,1},{5,4},{6,5},{9,8},{10,9},{13,12},{14,13},{17,16},{18,1... | collective-permute-start | bytes 2359304 | tf_op jit(solution)/shard_map/ppermute | solution.py:68
  575.8 37.7 %collective-permute-start.53 = (bf16[272,1536]{1,0:T(8,128)(2,1)S(1)}, bf16[272,1536]{1,0:T(8,128)(2,1)S(1)}, u32[]{:S(2)}, u32[]{:S(2)}) collective-permute-start(bf16[272,1536]{1,0:T(8,128)(2,1)S(1)} %collective-permute-done.49), channel_id=1, source_target_pairs={{1,2},{2,3},{5,6},{6,7},{9,10},{10,11},{13,14},{14,15},{17,18},{18... | collective-permute-start | bytes 2506760 | tf_op jit(solution)/shard_map/ppermute | solution.py:67
  576.5 37.0 %collective-permute-start.54 = (bf16[272,1536]{1,0:T(8,128)(2,1)S(1)}, bf16[272,1536]{1,0:T(8,128)(2,1)S(1)}, u32[]{:S(2)}, u32[]{:S(2)}) collective-permute-start(bf16[272,1536]{1,0:T(8,128)(2,1)S(1)} %collective-permute-done.50), channel_id=1, source_target_pairs={{1,0},{2,1},{5,4},{6,5},{9,8},{10,9},{13,12},{14,13},{17,16},{18,1... | collective-permute-start | bytes 2506760 | tf_op jit(solution)/shard_map/ppermute | solution.py:68
  611.5 39.1 %collective-permute-start.51 = (bf16[256,1536]{1,0:T(8,128)(2,1)S(1)}, bf16[256,1536]{1,0:T(8,128)(2,1)S(1)}, u32[]{:S(2)}, u32[]{:S(2)}) collective-permute-start(bf16[256,1536]{1,0:T(8,128)(2,1)S(1)} %collective-permute-done.47), channel_id=1, source_target_pairs={{2,3},{6,7},{10,11},{14,15},{18,19},{22,23},{26,27},{30,31}} | collective-permute-start | bytes 2359304 | tf_op jit(solution)/shard_map/ppermute | solution.py:67
  612.2 38.4 %collective-permute-start.52 = (bf16[256,1536]{1,0:T(8,128)(2,1)S(1)}, bf16[256,1536]{1,0:T(8,128)(2,1)S(1)}, u32[]{:S(2)}, u32[]{:S(2)}) collective-permute-start(bf16[256,1536]{1,0:T(8,128)(2,1)S(1)} %collective-permute-done.48), channel_id=1, source_target_pairs={{1,0},{5,4},{9,8},{13,12},{17,16},{21,20},{25,24},{29,28}} | collective-permute-start | bytes 2359304 | tf_op jit(solution)/shard_map/ppermute | solution.py:68
  613.5 37.1 %collective-permute-start.55 = (bf16[272,1536]{1,0:T(8,128)(2,1)S(1)}, bf16[272,1536]{1,0:T(8,128)(2,1)S(1)}, u32[]{:S(2)}, u32[]{:S(2)}) collective-permute-start(bf16[272,1536]{1,0:T(8,128)(2,1)S(1)} %collective-permute-done.53), channel_id=1, source_target_pairs={{2,3},{6,7},{10,11},{14,15},{18,19},{22,23},{26,27},{30,31}} | collective-permute-start | bytes 2506760 | tf_op jit(solution)/shard_map/ppermute | solution.py:67
  614.3 36.7 %collective-permute-start.56 = (bf16[272,1536]{1,0:T(8,128)(2,1)S(1)}, bf16[272,1536]{1,0:T(8,128)(2,1)S(1)}, u32[]{:S(2)}, u32[]{:S(2)}) collective-permute-start(bf16[272,1536]{1,0:T(8,128)(2,1)S(1)} %collective-permute-done.54), channel_id=1, source_target_pairs={{1,0},{5,4},{9,8},{13,12},{17,16},{21,20},{25,24},{29,28}} | collective-permute-start | bytes 2506760 | tf_op jit(solution)/shard_map/ppermute | solution.py:68
  689.5 38.4 %collective-permute-start.57 = (bf16[512,1536]{1,0:T(8,128)(2,1)S(1)}, bf16[512,1536]{1,0:T(8,128)(2,1)S(1)}, u32[]{:S(2)}, u32[]{:S(2)}) collective-permute-start(bf16[512,1536]{1,0:T(8,128)(2,1)S(1)} %get-tuple-element.493), channel_id=1, source_target_pairs={{0,1},{4,5},{8,9},{12,13},{16,17},{20,21},{24,25},{28,29}} | collective-permute-start | bytes 4718600 | tf_op jit(solution)/shard_map/ppermute | solution.py:132
  807.6 37.8 %collective-permute-start.71 = (f32[1,1]{1,0:T(1,128)}, f32[1,1]{1,0:T(1,128)}, u32[]{:S(2)}, u32[]{:S(2)}) collective-permute-start(f32[1,1]{1,0:T(1,128)} %bitcast.81), channel_id=1, source_target_pairs={{0,1},{1,0},{2,3},{3,2},{4,5},{5,4},{6,7},{7,6},{8,9},{9,8},{10,11... | collective-permute-start | bytes 20 | tf_op jit(solution)/shard_map/ppermute | solution.py:210
  845.4 34.7 %collective-permute-start.69 = (bf16[384,512]{1,0:T(8,128)(2,1)S(1)}, bf16[384,512]{1,0:T(8,128)(2,1)S(1)}, u32[]{:S(2)}, u32[]{:S(2)}) collective-permute-start(bf16[384,512]{1,0:T(8,128)(2,1)S(1)} %get-tuple-element.526), channel_id=1, source_target_pairs={{2,0},{3,1},{6,4},{7,5},{10,8},{11,9},{14,12},{15,13},{18,16},{19,... | collective-permute-start | bytes 1179656 | tf_op jit(solution)/shard_map/ppermute | solution.py:205
  880.2 68.2 %collective-permute-start.72 = (bf16[2,192,768]{2,1,0:T(8,128)(2,1)S(1)}, bf16[2,192,768]{2,1,0:T(8,128)(2,1)}, u32[]{:S(2)}, u32[]{:S(2)}) collective-permute-start(bf16[2,192,768]{2,1,0:T(8,128)(2,1)S(1)} %add_convert_fusion.9), channel_id=1, source_target_pairs={{0,8},{4,12},{8,0},{12,4},{16,24},{20,28},{24,16},{28,20},{1,9},{5... | collective-permute-start | bytes 1769480 | tf_op jit(solution)/shard_map/ppermute | solution.py:210
  881.7 66.7 %collective-permute-start.73 = (bf16[2,192,768]{2,1,0:T(8,128)(2,1)S(1)}, bf16[2,192,768]{2,1,0:T(8,128)(2,1)}, u32[]{:S(2)}, u32[]{:S(2)}) collective-permute-start(bf16[2,192,768]{2,1,0:T(8,128)(2,1)S(1)} %add_convert_fusion.8), channel_id=1, source_target_pairs={{0,16},{4,20},{8,24},{12,28},{16,0},{20,4},{24,8},{28,12},{1,17},{... | collective-permute-start | bytes 1769480 | tf_op jit(solution)/shard_map/ppermute | solution.py:210
  888.6 59.8 %collective-permute-start.74 = (f32[1,1]{1,0:T(1,128)}, f32[1,1]{1,0:T(1,128)}, u32[]{:S(2)}, u32[]{:S(2)}) collective-permute-start(f32[1,1]{1,0:T(1,128)} %add.688), channel_id=1, source_target_pairs={{0,2},{1,3},{2,0},{3,1},{4,6},{5,7},{6,4},{7,5},{8,10},{9,11},{10,... | collective-permute-start | bytes 20 | tf_op jit(solution)/shard_map/ppermute | solution.py:210
  974.0 48.0 %collective-permute-start.79 = (bf16[304,1536]{1,0:T(8,128)(2,1)}, bf16[304,1536]{1,0:T(8,128)(2,1)}, u32[]{:S(2)}, u32[]{:S(2)}) collective-permute-start(bf16[304,1536]{1,0:T(8,128)(2,1)} %pad_maximum_fusion.9), channel_id=1, source_target_pairs={{3,2},{7,6},{11,10},{15,14},{19,18},{23,22},{27,26},{31,30}} | collective-permute-start | bytes 2801672 | tf_op jit(solution)/shard_map/ppermute | solution.py:133
  978.7 43.3 %collective-permute-start.78 = (bf16[304,1536]{1,0:T(8,128)(2,1)}, bf16[304,1536]{1,0:T(8,128)(2,1)}, u32[]{:S(2)}, u32[]{:S(2)}) collective-permute-start(bf16[304,1536]{1,0:T(8,128)(2,1)} %pad_maximum_fusion.8), channel_id=1, source_target_pairs={{0,1},{4,5},{8,9},{12,13},{16,17},{20,21},{24,25},{28,29}} | collective-permute-start | bytes 2801672 | tf_op jit(solution)/shard_map/ppermute | solution.py:132
  981.0 34.2 %collective-permute-start.80 = (bf16[256,1536]{1,0:T(8,128)(2,1)}, bf16[256,1536]{1,0:T(8,128)(2,1)}, u32[]{:S(2)}, u32[]{:S(2)}) collective-permute-start(bf16[256,1536]{1,0:T(8,128)(2,1)} %get-tuple-element.523), channel_id=1, source_target_pairs={{0,1},{4,5},{8,9},{12,13},{16,17},{20,21},{24,25},{28,29}} | collective-permute-start | bytes 2359304 | tf_op jit(solution)/shard_map/ppermute | solution.py:132
  1024.1 35.1 %collective-permute-start.83 = (bf16[304,1536]{1,0:T(8,128)(2,1)S(1)}, bf16[304,1536]{1,0:T(8,128)(2,1)S(1)}, u32[]{:S(2)}, u32[]{:S(2)}) collective-permute-start(bf16[304,1536]{1,0:T(8,128)(2,1)S(1)} %get-tuple-element.566), channel_id=1, source_target_pairs={{0,1},{1,2},{4,5},{5,6},{8,9},{9,10},{12,13},{13,14},{16,17},{17,1... | collective-permute-start | bytes 2801672 | tf_op jit(solution)/shard_map/ppermute | solution.py:132
  1028.2 43.2 %collective-permute-start.82 = (bf16[2,192,681]{2,1,0:T(8,128)(2,1)S(1)}, bf16[2,192,681]{2,1,0:T(8,128)(2,1)S(1)}, u32[]{:S(2)}, u32[]{:S(2)}) collective-permute-start(bf16[2,192,681]{2,1,0:T(8,128)(2,1)S(1)} %add_convert_fusion.7), channel_id=1, source_target_pairs={{0,8},{4,12},{8,0},{12,4},{16,24},{20,28},{24,16},{28,20},{1,9},{5... | collective-permute-start | bytes 1569032 | tf_op jit(solution)/shard_map/ppermute | solution.py:210
  1039.4 33.0 %collective-permute-start.89 = (bf16[256,1536]{1,0:T(8,128)(2,1)S(1)}, bf16[256,1536]{1,0:T(8,128)(2,1)S(1)}, u32[]{:S(2)}, u32[]{:S(2)}) collective-permute-start(bf16[256,1536]{1,0:T(8,128)(2,1)S(1)} %add_convert_fusion.5), channel_id=1, source_target_pairs={{1,0},{2,1},{3,2},{5,4},{6,5},{7,6},{9,8},{10,9},{11,10},{13,12},{... | collective-permute-start | bytes 2359304 | tf_op jit(solution)/shard_map/ppermute | solution.py:133
  1040.9 35.2 %collective-permute-start.88 = (bf16[256,1536]{1,0:T(8,128)(2,1)S(1)}, bf16[256,1536]{1,0:T(8,128)(2,1)S(1)}, u32[]{:S(2)}, u32[]{:S(2)}) collective-permute-start(bf16[256,1536]{1,0:T(8,128)(2,1)S(1)} %add_convert_fusion.6), channel_id=1, source_target_pairs={{0,1},{1,2},{2,3},{4,5},{5,6},{6,7},{8,9},{9,10},{10,11},{12,13},{... | collective-permute-start | bytes 2359304 | tf_op jit(solution)/shard_map/ppermute | solution.py:132
  1071.4 46.9 %collective-permute-start.94 = (f32[1,1]{1,0:T(1,128)}, f32[1,1]{1,0:T(1,128)}, u32[]{:S(2)}, u32[]{:S(2)}) collective-permute-start(f32[1,1]{1,0:T(1,128)} %add.689), channel_id=1, source_target_pairs={{0,4},{4,0},{8,12},{12,8},{16,20},{20,16},{24,28},{28,24},{1,5},{5... | collective-permute-start | bytes 20 | tf_op jit(solution)/shard_map/ppermute | solution.py:210
  (186 other events, 3290.8 us)
Sparse Core Ops, SparseCore 0:
  13.0 51.5 all-gather.2
  66.5 219.0 all-gather.4
  798.8 302.0 reduce-scatter.1

commit v15 on v14

--- a/solution.py
+++ b/solution.py
@@ -1081,56 +1081,25 @@
     qkv_sum.add()
     out_own = ended[shard_len:].reshape(out_sum.shape[0], width // n)
     block = jnp.concatenate([qkv_sum.finish(), out_own], axis=1).astype(low)
-    rights, lefts = [block], [block]
+    block, expert_sum, squares = tie(block, expert_sum, squares)
+    blocks = lax.all_gather(block, "seq", axis=0)
     _, norm_one_pull = jax.vjp(lambda v: rms_norm(v, full_g1), x_low.astype(full))
     input_grad = (d_hidden + norm_one_pull(d_normed_one)[0]).reshape(1, shard_len, width)
     few = w_down.shape[1]
-    last_work = [
-        lambda: expert_sum[:, :, : 2 * hidden_w].astype(full),
-        lambda: jnp.concatenate(
-            [
-                expert_sum[:, start : start + few, 2 * hidden_w :].astype(full)
-                for start in range(0, expert_sum.shape[1], few)
-            ],
-            axis=2,
-        ),
-    ]
-    done = [input_grad]
-    grads = [
-        jnp.zeros((w_qkv.shape[0], QKV_W), full),
-        jnp.zeros((w_out.shape[0], width), full),
-        jnp.zeros((w_qkv.shape[0], block.shape[1] - group_w - width // n), full),
-        jnp.zeros((w_qkv.shape[0],), full),
-    ]
-
-    def write(grads, turn):
-        qkv_grad, out_grad, rest, gain_sum = grads
-        came = arrived(rights, lefts, turn).astype(full)
-        own_part, start = came[:, :group_w], order[turn] * group_w
-        own_qkv = lax.dynamic_slice_in_dim(w_qkv, start, group_w, 1).astype(full)
-        return [
-            lax.dynamic_update_slice_in_dim(qkv_grad, own_part, start, 1),
-            lax.dynamic_update_slice_in_dim(
-                out_grad, came[:, -(width // n) :], order[turn] * (width // n), 1
-            ),
-            rest + came[:, group_w : -(width // n)],
-            gain_sum + jnp.sum(own_part * own_qkv, axis=1),
-        ]
-
-    for k in range(1, n):
-        right, left = line_move(rights[-1], lefts[-1], k)
-        grads = write(grads, k - 1)
-        if k < 3:
-            done.append(last_work[k - 1]())
-        right, left, done[-1], squares, grads = tie(right, left, done[-1], squares, grads)
-        squares = loss_steps.send(squares)
-        rights.append(right)
-        lefts.append(left)
-    qkv_grad, out_grad, rest, gain_sum = write(grads, n - 1)
-    input_grad, gate_up_grad, down_grad = done
-    gate_grad, up_grad = gate_up_grad[:, :, :hidden_w], gate_up_grad[:, :, hidden_w:]
+    gate_grad = expert_sum[:, :, :hidden_w].astype(full)
+    up_grad = expert_sum[:, :, hidden_w : 2 * hidden_w].astype(full)
+    down_grad = jnp.concatenate(
+        [
+            expert_sum[:, start : start + few, 2 * hidden_w :].astype(full)
+            for start in range(0, expert_sum.shape[1], few)
+        ],
+        axis=2,
+    )
+    qkv_grad = jnp.concatenate([came[:, :group_w] for came in blocks], axis=1).astype(full)
+    out_grad = jnp.concatenate([came[:, -(width // n) :] for came in blocks], axis=1).astype(full)
+    rest = jnp.sum(blocks[:, :, group_w : -(width // n)].astype(full), axis=0)
     router_grad, gain_two_grad = rest[:, :expert_total], rest[:, expert_total]
-    gain_one_grad = gain_sum / gain_one.astype(full)
+    gain_one_grad = jnp.sum(qkv_grad * w_qkv.astype(full), axis=1) / gain_one.astype(full)
     for _ in range(4):
         squares = loss_steps.send(squares)
     loss_value = squares[0, 0] / (valid_count * width)

time: 1180 us -> 1160 us (0.983); the launches traced: 1170 us -> 1160 us
  waiting for transfers between devices: 283 us -> 305 us
  starting transfers between devices: 221 us -> 209 us
    all_gather x0 -> x1, waiting for transfers between devices: none -> 24.2 us  [shards(): blocks = lax.all_gather(block, 'seq', axis=0)]
    ppermute x21 -> x18, starting transfers between devices: 50.3 us -> 41.8 us  [line_move(): lax.ppermute(right, 'seq', [(i, i + 1) for i in range(k - 1, n - 1)])]
    ppermute x21 -> x18, waiting for transfers between devices: 62.3 us -> 55.6 us  [line_move(): lax.ppermute(left, 'seq', [(i, i - 1) for i in range(1, n - k + 1)])]
    ppermute x21 -> x18, starting transfers between devices: 36.4 us -> 32.3 us  [line_move(): lax.ppermute(left, 'seq', [(i, i - 1) for i in range(1, n - k + 1)])]
    unnamed x263 -> x259, local copies, waits for them, and re-layouts: 25.3 us -> 22.7 us
  transfers between devices with their start and end apart: 104 -> 99, of which waited for: 39 -> 39; matrix products, arithmetic and copies ran while one was open for 14% -> 13% of each run, Pallas kernels for 26% -> 26%
where the time goes in v15:
time: 1160 us
  Pallas kernels  387 us (33%)
  waiting for transfers between devices  305 us (26%)
  starting transfers between devices  209 us (18%)
  other arithmetic  122 us (11%)
  local copies, waits for them, and re-layouts  62.6 us (5%)
  matrix products  38.3 us (3%)
  between operations  34.9 us (3%)
    pallas_call x8, Pallas kernels, shard_call(): pl.pallas_call(kernel, grid_spec=pltpu.PrefetchScalarGridSpec(num_scalar_...  230 us
    ppermute x15, waiting for transfers between devices, line_pass(): lax.ppermute(to_right, 'seq', [(i, i + 1) for i in range(n - k)])  128 us
    ppermute x15, starting transfers between devices, line_pass(): lax.ppermute(to_right, 'seq', [(i, i + 1) for i in range(n - k)])  74.1 us
    pallas_call x1, Pallas kernels, attention_backward(): pl.pallas_call(functools.partial(backward_kernel, seq_len, query_rows, ke...  58.9 us
    ppermute x18, waiting for transfers between devices, line_move(): lax.ppermute(left, 'seq', [(i, i - 1) for i in range(1, n - k + 1)])  55.6 us
    pallas_call x2, Pallas kernels, weight_grads(): pl.pallas_call(functools.partial(grads_kernel, few), grid=(stop - first,)...  50.8 us
    ppermute x18, starting transfers between devices, line_move(): lax.ppermute(right, 'seq', [(i, i + 1) for i in range(k - 1, n - 1)])  41.8 us
    pallas_call x1, Pallas kernels, attention_forward(): pl.pallas_call(functools.partial(forward_kernel, seq_len, query_rows, key...  41.7 us
  transfers between devices with their start and end apart: 99, of which 39 were waited for; matrix products, arithmetic and copies ran while one was open for 13% of the time, Pallas kernels for 26%

profile of v15, /device:TPU:0, one launch (start us, length us, event | category | flops | bytes accessed | tf_op | source)
XLA Modules:
  0.0 1158.3 jit_solution(5372924714638483864)
XLA Ops:
  15.1 6.4 maximum_maximum_fusion
  23.2 6.0 collective-permute-start
  31.8 5.5 collective-permute-start.2
  63.0 6.5 collective-permute-done.3
  90.0 14.4 %collective-permute-done.7 = bf16[272,1536]{1,0:T(8,128)(2,1)} collective-permute-done((bf16[272,1536]{1,0:T(8,128)(2,1)}, bf16[272,1536]{1,0:T(8,128)(2,1)}, u32[]{:S(2)}, u32[]{:S(2)}) %collective-permute-start.7) | collective-permute-done | bytes 835616 | tf_op jit(solution)/shard_map/ppermute | solution.py:68
  121.2 16.5 %collective-permute-done.11 = bf16[272,1536]{1,0:T(8,128)(2,1)} collective-permute-done((bf16[272,1536]{1,0:T(8,128)(2,1)}, bf16[272,1536]{1,0:T(8,128)(2,1)}, u32[]{:S(2)}, u32[]{:S(2)}) %collective-permute-start.11) | collective-permute-done | bytes 835616 | tf_op jit(solution)/shard_map/ppermute | solution.py:68
  153.1 41.7 %attention_forward.1 = (bf16[4,384,512]{2,1,0:T(8,128)(2,1)}, f32[2,3,64,2048]{3,2,1,0:T(8,128)}, f32[2,3,1,2048]{3,2,1,0:T(1,128)}) custom-call(s32[1,2048]{1,0:T(1,128)} %bitcast.308, bf16[4,2,5,64,512]{4,3,2,1,0:T(8,128)(2,1)} %copy-done.15, bf16[2,2048,64]{2,1,0:T(8,128)(2,1)} %copy.141.k_ref, bf16[2,64,2048]{2,1,0:T(8,128)(2,1)} %copy.142.vt_ref), custom_call_target="tpu_custom_call" | custom-call | tf_op jit(solution)/shard_map/attention_forward/pallas_call | solution.py:342
  216.1 6.2 collective-permute-done.14
  222.3 15.9 %collective-permute-done.16 = bf16[384,512]{1,0:T(8,128)(2,1)S(1)} collective-permute-done((bf16[384,512]{1,0:T(8,128)(2,1)S(1)}, bf16[384,512]{1,0:T(8,128)(2,1)S(1)}, u32[]{:S(2)}, u32[]{:S(2)}) %collective-permute-start.16) | collective-permute-done | bytes 393248 | tf_op jit(solution)/shard_map/ppermute | solution.py:205
  250.1 5.4 collective-permute-start.22
  256.9 9.1 collective-permute-done.18
  265.9 5.3 collective-permute-done.19
  274.0 5.8 collective-permute-done.22
  279.9 8.3 collective-permute-done.23
  293.8 25.2 %experts_forward.4 = (bf16[4,512,1536]{2,1,0:T(8,128)(2,1)}, bf16[10,4,160,1536]{3,2,1,0:T(8,128)(2,1)}, bf16[10,4,160,1024]{3,2,1,0:T(8,128)(2,1)}, f32[10,512]{1,0:T(8,128)S(1)}) custom-call(s32[2]{0:T(128)S(1)} %get-tuple-element.545.at_ref, bf16[256,1536]{1,0:T(8,128)(2,1)S(1)} %get-tuple-element.485.tok_ref, ...), custom_call_target="tpu_custom_call" | custom-call | tf_op jit(solution)/shard_map/experts_forward/pallas_call | solution.py:597
  321.7 10.0 collective-permute-start.29
  334.5 25.2 %experts_forward.5 = (bf16[4,512,1536]{2,1,0:T(8,128)(2,1)}, bf16[10,4,160,1536]{3,2,1,0:T(8,128)(2,1)}, bf16[10,4,160,1024]{3,2,1,0:T(8,128)(2,1)}, f32[10,512]{1,0:T(8,128)S(1)}) custom-call(s32[2]{0:T(128)S(1)} %get-tuple-element.546.at_ref, ...), custom_call_target="tpu_custom_call", output_to_operand_aliasing={{0}: (8, {}), {1}: (9, {}), {2}: (10, {})} | custom-call | tf_op jit(solution)/shard_map/experts_forward/pallas_call | solution.py:597
  368.1 25.2 %experts_forward.6 = (bf16[4,512,1536]{2,1,0:T(8,128)(2,1)}, bf16[10,4,160,1536]{3,2,1,0:T(8,128)(2,1)}, bf16[10,4,160,1024]{3,2,1,0:T(8,128)(2,1)}, f32[10,512]{1,0:T(8,128)S(1)}) custom-call(s32[2]{0:T(128)S(1)} %get-tuple-element.547.at_ref, ...), custom_call_target="tpu_custom_call", output_to_operand_aliasing={{0}: (8, {}), {1}: (9, {}), {2}: (10, {})} | custom-call | tf_op jit(solution)/shard_map/experts_forward/pallas_call | solution.py:597
  393.4 25.2 %experts_forward.7 = (bf16[4,512,1536]{2,1,0:T(8,128)(2,1)}, bf16[10,4,160,1536]{3,2,1,0:T(8,128)(2,1)}, bf16[10,4,160,1024]{3,2,1,0:T(8,128)(2,1)}, f32[10,512]{1,0:T(8,128)S(1)}) custom-call(s32[2]{0:T(128)S(1)} %get-tuple-element.544.at_ref, ...), custom_call_target="tpu_custom_call", output_to_operand_aliasing={{0}: (8, {}), {1}: (9, {}), {2}: (10, {})} | custom-call | tf_op jit(solution)/shard_map/experts_forward/pallas_call | solution.py:597
  422.2 6.1 collective-permute-start.30
  431.6 14.6 %collective-permute-done.30 = bf16[256,1536]{1,0:T(8,128)(2,1)S(1)} collective-permute-done((bf16[256,1536]{1,0:T(8,128)(2,1)S(1)}, bf16[256,1536]{1,0:T(8,128)(2,1)S(1)}, u32[]{:S(2)}, u32[]{:S(2)}) %collective-permute-start.30) | collective-permute-done | bytes 786464 | tf_op jit(solution)/shard_map/ppermute | solution.py:132
  451.8 11.3 collective-permute-done.36
  468.7 11.3 collective-permute-done.32
  480.4 5.3 collective-permute-start.34
  487.1 9.7 collective-permute-done.38
  541.7 32.1 %experts_backward.4 = (bf16[4,512,1536]{2,1,0:T(8,128)(2,1)}, bf16[10,4,160,1536]{3,2,1,0:T(8,128)(2,1)}, bf16[10,4,160,1024]{3,2,1,0:T(8,128)(2,1)}, bf16[10,4,...) custom-call(s32[2]{0:T(128)S(1)} %get-tuple-element.545.at_ref, bf16[256,1536]{1,0:T(8,128)(2,1)S(1)} %get-tuple-element.479.tok_ref, ...), custom_call_target="tpu_custom_call" | custom-call | tf_op jit(solution)/shard_map/experts_backward/pallas_call | solution.py:597
  579.7 32.2 %experts_backward.5 = (bf16[4,512,1536]{2,1,0:T(8,128)(2,1)}, bf16[10,4,160,1536]{3,2,1,0:T(8,128)(2,1)}, bf16[10,4,160,1024]{3,2,1,0:T(8,128)(2,1)}, bf16[10,4,...) custom-call(s32[2]{0:T(128)S(1)} %get-tuple-element.546.at_ref, ...), custom_call_target="tpu_custom_call", output_to_operand_aliasing={{0}: (10, {}), {1}: (11, {}), {2}: (12, {}), {3}: (13, {})} | custom-call | tf_op jit(solution)/shard_map/experts_backward/pallas_call | solution.py:597
  618.6 32.2 %experts_backward.6 = (bf16[4,512,1536]{2,1,0:T(8,128)(2,1)}, bf16[10,4,160,1536]{3,2,1,0:T(8,128)(2,1)}, bf16[10,4,160,1024]{3,2,1,0:T(8,128)(2,1)}, bf16[10,4,...) custom-call(s32[2]{0:T(128)S(1)} %get-tuple-element.547.at_ref, ...), custom_call_target="tpu_custom_call", output_to_operand_aliasing={{0}: (10, {}), {1}: (11, {}), {2}: (12, {}), {3}: (13, {})} | custom-call | tf_op jit(solution)/shard_map/experts_backward/pallas_call | solution.py:597
  655.8 32.2 %experts_backward.7 = (bf16[4,512,1536]{2,1,0:T(8,128)(2,1)}, bf16[10,4,160,1536]{3,2,1,0:T(8,128)(2,1)}, bf16[10,4,160,1024]{3,2,1,0:T(8,128)(2,1)}, bf16[10,4,...) custom-call(s32[2]{0:T(128)S(1)} %get-tuple-element.544.at_ref, ...), custom_call_target="tpu_custom_call", output_to_operand_aliasing={{0}: (10, {}), {1}: (11, {}), {2}: (12, {}), {3}: (13, {})} | custom-call | tf_op jit(solution)/shard_map/experts_backward/pallas_call | solution.py:597
  690.0 11.6 collective-permute-start.57
  702.6 25.4 %weight_grads.2.refs_0_ = bf16[10,1536,1536]{2,1,0:T(8,128)(2,1)} custom-call(bf16[10,640,1536]{2,1,0:T(8,128)(2,1)} %bitcast.271, bf16[10,640,1024]{2,1,0:T(8,128)(2,1)} %bitcast.273, bf16[10,640,512]{2,1,0:T(8,128)(2,1)} %bitcast.275, bf16[10,640,1536]{2,1,0:T(8,128)(2,1)} %bitcast.269), custom_call_target="tpu_custom_call" | custom-call | tf_op jit(solution)/shard_map/weight_grads/pallas_call | solution.py:768
  737.8 25.4 %weight_grads.3 = bf16[10,1536,1536]{2,1,0:T(8,128)(2,1)} custom-call(bf16[10,640,1536]{2,1,0:T(8,128)(2,1)} %bitcast.272, bf16[10,640,1024]{2,1,0:T(8,128)(2,1)} %bitcast.274, bf16[10,640,512]{2,1,0:T(8,128)(2,1)} %bitcast.276, bf16[10,640,1536]{2,1,0:T(8,128)(2,1)} %bitcast.270, ...), custom_call_target="tpu_custom_call", output_to_operand_aliasing={{}: (4, {})} | custom-call | tf_op jit(solution)/shard_map/weight_grads/pallas_call | solution.py:768
  766.4 5.6 collective-permute-start.61
  773.3 21.9 %collective-permute-done.61 = bf16[512,1536]{1,0:T(8,128)(2,1)S(1)} collective-permute-done((bf16[512,1536]{1,0:T(8,128)(2,1)S(1)}, bf16[512,1536]{1,0:T(8,128)(2,1)S(1)}, u32[]{:S(2)}, u32[]{:S(2)}) %collective-permute-start.61) | collective-permute-done | bytes 1572896 | tf_op jit(solution)/shard_map/ppermute | solution.py:132
  816.2 5.8 out_grads.1
  823.0 6.2 fusion.33
  845.1 6.7 collective-permute-done.66.refs_2_
  851.7 7.4 collective-permute-done.67.refs_3_
  859.1 17.1 %collective-permute-done.69.refs_5_ = bf16[384,512]{1,0:T(8,128)(2,1)S(1)} collective-permute-done((bf16[384,512]{1,0:T(8,128)(2,1)S(1)}, bf16[384,512]{1,0:T(8,128)(2,1)S(1)}, u32[]{:S(2)}, u32[]{:S(2)}) %collective-permute-start.69) | collective-permute-done | bytes 393248 | tf_op jit(solution)/shard_map/ppermute | solution.py:205
  884.6 58.9 %attention_backward.1 = (bf16[2,3,64,2048]{3,2,1,0:T(8,128)(2,1)}, bf16[2,64,2048]{2,1,0:T(8,128)(2,1)}, bf16[2,64,2048]{2,1,0:T(8,128)(2,1)}) custom-call(s32[1]{0:T(128)} %bitcast.51.me_ref, s32[1,2048]{1,0:T(1,128)} %bitcast.309, bf16[4,2,5,64,512]{4,3,2,1,0:T(8,128)(2,1)} %copy-done.15, bf16[2,2048,64]{2,1,0:T(8,128)(2,1)} %copy.141.k_ref, ...), custom_call_target="tpu_custom_call" | custom-call | tf_op jit(solution)/shard_map/attention_backward/pallas_call | solution.py:425
  994.1 15.5 %collective-permute-done.80 = bf16[256,1536]{1,0:T(8,128)(2,1)} collective-permute-done((bf16[256,1536]{1,0:T(8,128)(2,1)}, bf16[256,1536]{1,0:T(8,128)(2,1)}, u32[]{:S(2)}, u32[]{:S(2)}) %collective-permute-start.80) | collective-permute-done | bytes 786464 | tf_op jit(solution)/shard_map/ppermute | solution.py:132
  1022.7 11.0 collective-permute-done.85
  1035.4 7.0 collective-permute-start.88
  1042.3 11.3 collective-permute-done.83
  1055.4 7.2 collective-permute-start.90
  1071.8 13.5 %collective-permute-done.90 = bf16[304,1536]{1,0:T(8,128)(2,1)S(1)} collective-permute-done((bf16[304,1536]{1,0:T(8,128)(2,1)S(1)}, bf16[304,1536]{1,0:T(8,128)(2,1)S(1)}, u32[]{:S(2)}, u32[]{:S(2)}) %collective-permute-start.90) | collective-permute-done | bytes 933920 | tf_op jit(solution)/shard_map/ppermute | solution.py:132
  1091.4 6.5 reduce-scatter.2.cloned.1.call-done
  1117.6 24.2 %all-gather.9.cloned.1.call-done = bf16[768,1065]{1,0:T(8,128)(2,1)} async-done(((bf16[192,1065]{1,0:T(8,128)(2,1)}), bf16[768,1065]{1,0:T(8,128)(2,1)}) %all-gather.9.cloned.1.call-update) | async-done | bytes 1635856 | tf_op jit(solution)/shard_map/all_gather | solution.py:1085
  (637 shorter events, 384.5 us)
Async XLA Ops:
  7.2 70.6 %all-gather.5.cloned.1.call-start = ((), (), s32[]{:S(2)}) async-start(), calls=%async_computation.1 | async-start | bytes 7962624 | tf_op jit(solution)/shard_map/all_gather | solution.py:820
  12.9 280.9 %all-gather.7.cloned.1.call-start = ((), (), s32[]{:S(2)}) async-start(), calls=%async_computation.2 | async-start | bytes 53084160 | tf_op jit(solution)/shard_map/all_gather | solution.py:837
  21.5 1076.3 %reduce-scatter.2.cloned.1.call-start = ((), (), s32[]{:S(2)}) async-start(), calls=%async_computation.3 | async-start | bytes 53084160 | tf_op jit(solution)/shard_map/reduce_scatter | solution.py:992
  23.2 34.5 %collective-permute-start = (bf16[256,1536]{1,0:T(8,128)(2,1)S(1)}, bf16[256,1536]{1,0:T(8,128)(2,1)}, u32[]{:S(2)}, u32[]{:S(2)}) collective-permute-start(bf16[256,1536]{1,0:T(8,128)(2,1)S(1)} %get-tuple-element.493), channel_id=1, source_target_pairs={{0,1},{1,2},{2,3},{4,5},{5,6},{6,7},{8,9},{9,10},{10,11},{12,13},{... | collective-permute-start | bytes 2359304 | tf_op jit(solution)/shard_map/ppermute | solution.py:67
  69.6 34.8 %collective-permute-start.7 = (bf16[272,1536]{1,0:T(8,128)(2,1)}, bf16[272,1536]{1,0:T(8,128)(2,1)}, u32[]{:S(2)}, u32[]{:S(2)}) collective-permute-start(bf16[272,1536]{1,0:T(8,128)(2,1)} %collective-permute-done.3), channel_id=1, source_target_pairs={{1,0},{2,1},{5,4},{6,5},{9,8},{10,9},{13,12},{14,13},{17,16},{18,1... | collective-permute-start | bytes 2506760 | tf_op jit(solution)/shard_map/ppermute | solution.py:68
  70.9 33.5 %collective-permute-start.6 = (bf16[272,1536]{1,0:T(8,128)(2,1)}, bf16[272,1536]{1,0:T(8,128)(2,1)}, u32[]{:S(2)}, u32[]{:S(2)}) collective-permute-start(bf16[272,1536]{1,0:T(8,128)(2,1)} %collective-permute-done.2), channel_id=1, source_target_pairs={{1,2},{2,3},{5,6},{6,7},{9,10},{10,11},{13,14},{14,15},{17,18},{18... | collective-permute-start | bytes 2506760 | tf_op jit(solution)/shard_map/ppermute | solution.py:67
  88.7 32.5 %collective-permute-start.9 = (bf16[256,1536]{1,0:T(8,128)(2,1)}, bf16[256,1536]{1,0:T(8,128)(2,1)}, u32[]{:S(2)}, u32[]{:S(2)}) collective-permute-start(bf16[256,1536]{1,0:T(8,128)(2,1)} %collective-permute-done.5), channel_id=1, source_target_pairs={{1,0},{5,4},{9,8},{13,12},{17,16},{21,20},{25,24},{29,28}} | collective-permute-start | bytes 2359304 | tf_op jit(solution)/shard_map/ppermute | solution.py:68
  204.4 33.8 %collective-permute-start.16 = (bf16[384,512]{1,0:T(8,128)(2,1)S(1)}, bf16[384,512]{1,0:T(8,128)(2,1)S(1)}, u32[]{:S(2)}, u32[]{:S(2)}) collective-permute-start(bf16[384,512]{1,0:T(8,128)(2,1)S(1)} %get-tuple-element.487), channel_id=1, source_target_pairs={{2,0},{3,1},{6,4},{7,5},{10,8},{11,9},{14,12},{15,13},{18,16},{19,... | collective-permute-start | bytes 1179656 | tf_op jit(solution)/shard_map/ppermute | solution.py:205
  255.6 32.6 %collective-permute-start.23 = (bf16[256,1536]{1,0:T(8,128)(2,1)S(1)}, bf16[256,1536]{1,0:T(8,128)(2,1)}, u32[]{:S(2)}, u32[]{:S(2)}) collective-permute-start(bf16[256,1536]{1,0:T(8,128)(2,1)S(1)} %get-tuple-element.484.more_ref), channel_id=1, source_target_pairs={{1,0},{2,1},{3,2},{5,4},{6,5},{7,6},{9,8},{10,9},{11,10},{13,12},{... | collective-permute-start | bytes 2359304 | tf_op jit(solution)/shard_map/ppermute | solution.py:68
  271.2 47.8 %collective-permute-start.20 = (bf16[256,1536]{1,0:T(8,128)(2,1)}, bf16[256,1536]{1,0:T(8,128)(2,1)}, u32[]{:S(2)}, u32[]{:S(2)}) collective-permute-start(bf16[256,1536]{1,0:T(8,128)(2,1)} %collective-permute-done.18), channel_id=1, source_target_pairs={{1,2},{2,3},{5,6},{6,7},{9,10},{10,11},{13,14},{14,15},{17,18},{18... | collective-permute-start | bytes 2359304 | tf_op jit(solution)/shard_map/ppermute | solution.py:67
  272.8 46.2 %collective-permute-start.21 = (bf16[256,1536]{1,0:T(8,128)(2,1)S(1)}, bf16[256,1536]{1,0:T(8,128)(2,1)}, u32[]{:S(2)}, u32[]{:S(2)}) collective-permute-start(bf16[256,1536]{1,0:T(8,128)(2,1)S(1)} %collective-permute-done.19), channel_id=1, source_target_pairs={{1,0},{2,1},{5,4},{6,5},{9,8},{10,9},{13,12},{14,13},{17,16},{18,1... | collective-permute-start | bytes 2359304 | tf_op jit(solution)/shard_map/ppermute | solution.py:68
  288.2 32.8 %collective-permute-start.26 = (bf16[256,1536]{1,0:T(8,128)(2,1)}, bf16[256,1536]{1,0:T(8,128)(2,1)}, u32[]{:S(2)}, u32[]{:S(2)}) collective-permute-start(bf16[256,1536]{1,0:T(8,128)(2,1)} %collective-permute-done.22), channel_id=1, source_target_pairs={{1,2},{2,3},{5,6},{6,7},{9,10},{10,11},{13,14},{14,15},{17,18},{18... | collective-permute-start | bytes 2359304 | tf_op jit(solution)/shard_map/ppermute | solution.py:67
  319.0 40.8 %collective-permute-start.24 = (bf16[256,1536]{1,0:T(8,128)(2,1)}, bf16[256,1536]{1,0:T(8,128)(2,1)S(1)}, u32[]{:S(2)}, u32[]{:S(2)}) collective-permute-start(bf16[256,1536]{1,0:T(8,128)(2,1)} %collective-permute-done.20), channel_id=1, source_target_pairs={{2,3},{6,7},{10,11},{14,15},{18,19},{22,23},{26,27},{30,31}} | collective-permute-start | bytes 2359304 | tf_op jit(solution)/shard_map/ppermute | solution.py:67
  319.7 40.1 %collective-permute-start.25 = (bf16[256,1536]{1,0:T(8,128)(2,1)}, bf16[256,1536]{1,0:T(8,128)(2,1)S(1)}, u32[]{:S(2)}, u32[]{:S(2)}) collective-permute-start(bf16[256,1536]{1,0:T(8,128)(2,1)} %collective-permute-done.21), channel_id=1, source_target_pairs={{1,0},{5,4},{9,8},{13,12},{17,16},{21,20},{25,24},{29,28}} | collective-permute-start | bytes 2359304 | tf_op jit(solution)/shard_map/ppermute | solution.py:68
  321.0 38.7 %collective-permute-start.28 = (bf16[256,1536]{1,0:T(8,128)(2,1)}, bf16[256,1536]{1,0:T(8,128)(2,1)S(1)}, u32[]{:S(2)}, u32[]{:S(2)}) collective-permute-start(bf16[256,1536]{1,0:T(8,128)(2,1)} %collective-permute-done.26), channel_id=1, source_target_pairs={{2,3},{6,7},{10,11},{14,15},{18,19},{22,23},{26,27},{30,31}} | collective-permute-start | bytes 2359304 | tf_op jit(solution)/shard_map/ppermute | solution.py:67
  321.7 38.0 %collective-permute-start.29 = (bf16[256,1536]{1,0:T(8,128)(2,1)}, bf16[256,1536]{1,0:T(8,128)(2,1)S(1)}, u32[]{:S(2)}, u32[]{:S(2)}) collective-permute-start(bf16[256,1536]{1,0:T(8,128)(2,1)} %collective-permute-done.27), channel_id=1, source_target_pairs={{1,0},{5,4},{9,8},{13,12},{17,16},{21,20},{25,24},{29,28}} | collective-permute-start | bytes 2359304 | tf_op jit(solution)/shard_map/ppermute | solution.py:68
  429.2 33.9 %collective-permute-start.36 = (bf16[256,1536]{1,0:T(8,128)(2,1)S(1)}, bf16[256,1536]{1,0:T(8,128)(2,1)S(1)}, u32[]{:S(2)}, u32[]{:S(2)}) collective-permute-start(bf16[256,1536]{1,0:T(8,128)(2,1)S(1)} %get-tuple-element.451), channel_id=1, source_target_pairs={{0,1},{4,5},{8,9},{12,13},{16,17},{20,21},{24,25},{28,29}} | collective-permute-start | bytes 2359304 | tf_op jit(solution)/shard_map/ppermute | solution.py:132
  446.6 33.3 %collective-permute-start.32 = (bf16[256,1536]{1,0:T(8,128)(2,1)S(1)}, bf16[256,1536]{1,0:T(8,128)(2,1)S(1)}, u32[]{:S(2)}, u32[]{:S(2)}) collective-permute-start(bf16[256,1536]{1,0:T(8,128)(2,1)S(1)} %get-tuple-element.447), channel_id=1, source_target_pairs={{0,1},{1,2},{4,5},{5,6},{8,9},{9,10},{12,13},{13,14},{16,17},{17,1... | collective-permute-start | bytes 2359304 | tf_op jit(solution)/shard_map/ppermute | solution.py:132
  463.5 33.3 %collective-permute-start.38 = (bf16[256,1536]{1,0:T(8,128)(2,1)S(1)}, bf16[256,1536]{1,0:T(8,128)(2,1)S(1)}, u32[]{:S(2)}, u32[]{:S(2)}) collective-permute-start(bf16[256,1536]{1,0:T(8,128)(2,1)S(1)} %get-tuple-element.445), channel_id=1, source_target_pairs={{0,1},{1,2},{4,5},{5,6},{8,9},{9,10},{12,13},{13,14},{16,17},{17,1... | collective-permute-start | bytes 2359304 | tf_op jit(solution)/shard_map/ppermute | solution.py:132
  480.4 36.3 %collective-permute-start.34 = (bf16[256,1536]{1,0:T(8,128)(2,1)S(1)}, bf16[256,1536]{1,0:T(8,128)(2,1)}, u32[]{:S(2)}, u32[]{:S(2)}) collective-permute-start(bf16[256,1536]{1,0:T(8,128)(2,1)S(1)} %get-tuple-element.443), channel_id=1, source_target_pairs={{0,1},{1,2},{2,3},{4,5},{5,6},{6,7},{8,9},{9,10},{10,11},{12,13},{... | collective-permute-start | bytes 2359304 | tf_op jit(solution)/shard_map/ppermute | solution.py:132
  530.1 45.8 %collective-permute-start.49 = (bf16[272,1536]{1,0:T(8,128)(2,1)S(1)}, bf16[272,1536]{1,0:T(8,128)(2,1)S(1)}, u32[]{:S(2)}, u32[]{:S(2)}) collective-permute-start(bf16[272,1536]{1,0:T(8,128)(2,1)S(1)} %fusion.52.more_ref), channel_id=1, source_target_pairs={{0,1},{1,2},{2,3},{4,5},{5,6},{6,7},{8,9},{9,10},{10,11},{12,13},{... | collective-permute-start | bytes 2506760 | tf_op jit(solution)/shard_map/ppermute | solution.py:67
  534.5 41.4 %collective-permute-start.50 = (bf16[272,1536]{1,0:T(8,128)(2,1)S(1)}, bf16[272,1536]{1,0:T(8,128)(2,1)S(1)}, u32[]{:S(2)}, u32[]{:S(2)}) collective-permute-start(bf16[272,1536]{1,0:T(8,128)(2,1)S(1)} %fusion.52.more_ref), channel_id=1, source_target_pairs={{1,0},{2,1},{3,2},{5,4},{6,5},{7,6},{9,8},{10,9},{11,10},{13,12},{... | collective-permute-start | bytes 2506760 | tf_op jit(solution)/shard_map/ppermute | solution.py:68
  535.8 38.1 %collective-permute-start.45 = (bf16[256,1536]{1,0:T(8,128)(2,1)S(1)}, bf16[256,1536]{1,0:T(8,128)(2,1)S(1)}, u32[]{:S(2)}, u32[]{:S(2)}) collective-permute-start(bf16[256,1536]{1,0:T(8,128)(2,1)S(1)} %get-tuple-element.479.tok_ref), channel_id=1, source_target_pairs={{0,1},{1,2},{2,3},{4,5},{5,6},{6,7},{8,9},{9,10},{10,11},{12,13},{... | collective-permute-start | bytes 2359304 | tf_op jit(solution)/shard_map/ppermute | solution.py:67
  540.4 33.5 %collective-permute-start.46 = (bf16[256,1536]{1,0:T(8,128)(2,1)S(1)}, bf16[256,1536]{1,0:T(8,128)(2,1)S(1)}, u32[]{:S(2)}, u32[]{:S(2)}) collective-permute-start(bf16[256,1536]{1,0:T(8,128)(2,1)S(1)} %get-tuple-element.479.tok_ref), channel_id=1, source_target_pairs={{1,0},{2,1},{3,2},{5,4},{6,5},{7,6},{9,8},{10,9},{11,10},{13,12},{... | collective-permute-start | bytes 2359304 | tf_op jit(solution)/shard_map/ppermute | solution.py:68
  573.9 38.0 %collective-permute-start.47 = (bf16[256,1536]{1,0:T(8,128)(2,1)S(1)}, bf16[256,1536]{1,0:T(8,128)(2,1)S(1)}, u32[]{:S(2)}, u32[]{:S(2)}) collective-permute-start(bf16[256,1536]{1,0:T(8,128)(2,1)S(1)} %collective-permute-done.45), channel_id=1, source_target_pairs={{1,2},{2,3},{5,6},{6,7},{9,10},{10,11},{13,14},{14,15},{17,18},{18... | collective-permute-start | bytes 2359304 | tf_op jit(solution)/shard_map/ppermute | solution.py:67
  574.6 37.2 %collective-permute-start.48 = (bf16[256,1536]{1,0:T(8,128)(2,1)S(1)}, bf16[256,1536]{1,0:T(8,128)(2,1)S(1)}, u32[]{:S(2)}, u32[]{:S(2)}) collective-permute-start(bf16[256,1536]{1,0:T(8,128)(2,1)S(1)} %collective-permute-done.46), channel_id=1, source_target_pairs={{1,0},{2,1},{5,4},{6,5},{9,8},{10,9},{13,12},{14,13},{17,16},{18,1... | collective-permute-start | bytes 2359304 | tf_op jit(solution)/shard_map/ppermute | solution.py:68
  575.9 37.9 %collective-permute-start.53 = (bf16[272,1536]{1,0:T(8,128)(2,1)S(1)}, bf16[272,1536]{1,0:T(8,128)(2,1)S(1)}, u32[]{:S(2)}, u32[]{:S(2)}) collective-permute-start(bf16[272,1536]{1,0:T(8,128)(2,1)S(1)} %collective-permute-done.49), channel_id=1, source_target_pairs={{1,2},{2,3},{5,6},{6,7},{9,10},{10,11},{13,14},{14,15},{17,18},{18... | collective-permute-start | bytes 2506760 | tf_op jit(solution)/shard_map/ppermute | solution.py:67
  576.6 37.2 %collective-permute-start.54 = (bf16[272,1536]{1,0:T(8,128)(2,1)S(1)}, bf16[272,1536]{1,0:T(8,128)(2,1)S(1)}, u32[]{:S(2)}, u32[]{:S(2)}) collective-permute-start(bf16[272,1536]{1,0:T(8,128)(2,1)S(1)} %collective-permute-done.50), channel_id=1, source_target_pairs={{1,0},{2,1},{5,4},{6,5},{9,8},{10,9},{13,12},{14,13},{17,16},{18,1... | collective-permute-start | bytes 2506760 | tf_op jit(solution)/shard_map/ppermute | solution.py:68
  611.8 39.0 %collective-permute-start.51 = (bf16[256,1536]{1,0:T(8,128)(2,1)S(1)}, bf16[256,1536]{1,0:T(8,128)(2,1)S(1)}, u32[]{:S(2)}, u32[]{:S(2)}) collective-permute-start(bf16[256,1536]{1,0:T(8,128)(2,1)S(1)} %collective-permute-done.47), channel_id=1, source_target_pairs={{2,3},{6,7},{10,11},{14,15},{18,19},{22,23},{26,27},{30,31}} | collective-permute-start | bytes 2359304 | tf_op jit(solution)/shard_map/ppermute | solution.py:67
  612.6 38.3 %collective-permute-start.52 = (bf16[256,1536]{1,0:T(8,128)(2,1)S(1)}, bf16[256,1536]{1,0:T(8,128)(2,1)S(1)}, u32[]{:S(2)}, u32[]{:S(2)}) collective-permute-start(bf16[256,1536]{1,0:T(8,128)(2,1)S(1)} %collective-permute-done.48), channel_id=1, source_target_pairs={{1,0},{5,4},{9,8},{13,12},{17,16},{21,20},{25,24},{29,28}} | collective-permute-start | bytes 2359304 | tf_op jit(solution)/shard_map/ppermute | solution.py:68
  613.9 37.0 %collective-permute-start.55 = (bf16[272,1536]{1,0:T(8,128)(2,1)S(1)}, bf16[272,1536]{1,0:T(8,128)(2,1)S(1)}, u32[]{:S(2)}, u32[]{:S(2)}) collective-permute-start(bf16[272,1536]{1,0:T(8,128)(2,1)S(1)} %collective-permute-done.53), channel_id=1, source_target_pairs={{2,3},{6,7},{10,11},{14,15},{18,19},{22,23},{26,27},{30,31}} | collective-permute-start | bytes 2506760 | tf_op jit(solution)/shard_map/ppermute | solution.py:67
  614.6 36.9 %collective-permute-start.56 = (bf16[272,1536]{1,0:T(8,128)(2,1)S(1)}, bf16[272,1536]{1,0:T(8,128)(2,1)S(1)}, u32[]{:S(2)}, u32[]{:S(2)}) collective-permute-start(bf16[272,1536]{1,0:T(8,128)(2,1)S(1)} %collective-permute-done.54), channel_id=1, source_target_pairs={{1,0},{5,4},{9,8},{13,12},{17,16},{21,20},{25,24},{29,28}} | collective-permute-start | bytes 2506760 | tf_op jit(solution)/shard_map/ppermute | solution.py:68
  690.0 38.0 %collective-permute-start.57 = (bf16[512,1536]{1,0:T(8,128)(2,1)S(1)}, bf16[512,1536]{1,0:T(8,128)(2,1)S(1)}, u32[]{:S(2)}, u32[]{:S(2)}) collective-permute-start(bf16[512,1536]{1,0:T(8,128)(2,1)S(1)} %get-tuple-element.429), channel_id=1, source_target_pairs={{0,1},{4,5},{8,9},{12,13},{16,17},{20,21},{24,25},{28,29}} | collective-permute-start | bytes 4718600 | tf_op jit(solution)/shard_map/ppermute | solution.py:132
  799.5 342.4 %all-gather.9.cloned.1.call-start = ((), (), s32[]{:S(2)}) async-start(), calls=%async_computation.4 | async-start | bytes 2211840 | tf_op jit(solution)/shard_map/all_gather | solution.py:1085
  803.2 38.1 %collective-permute-start.71 = (f32[1,1]{1,0:T(1,128)}, f32[1,1]{1,0:T(1,128)}, u32[]{:S(2)}, u32[]{:S(2)}) collective-permute-start(f32[1,1]{1,0:T(1,128)} %bitcast.81), channel_id=1, source_target_pairs={{0,1},{1,0},{2,3},{3,2},{4,5},{5,4},{6,7},{7,6},{8,9},{9,8},{10,11... | collective-permute-start | bytes 20 | tf_op jit(solution)/shard_map/ppermute | solution.py:210
  841.3 34.9 %collective-permute-start.69 = (bf16[384,512]{1,0:T(8,128)(2,1)S(1)}, bf16[384,512]{1,0:T(8,128)(2,1)S(1)}, u32[]{:S(2)}, u32[]{:S(2)}) collective-permute-start(bf16[384,512]{1,0:T(8,128)(2,1)S(1)} %get-tuple-element.472), channel_id=1, source_target_pairs={{2,0},{3,1},{6,4},{7,5},{10,8},{11,9},{14,12},{15,13},{18,16},{19,... | collective-permute-start | bytes 1179656 | tf_op jit(solution)/shard_map/ppermute | solution.py:205
  843.3 33.0 %collective-permute-start.70 = (bf16[384,512]{1,0:T(8,128)(2,1)S(1)}, bf16[384,512]{1,0:T(8,128)(2,1)S(1)}, u32[]{:S(2)}, u32[]{:S(2)}) collective-permute-start(bf16[384,512]{1,0:T(8,128)(2,1)S(1)} %get-tuple-element.471), channel_id=1, source_target_pairs={{3,0},{7,4},{11,8},{15,12},{19,16},{23,20},{27,24},{31,28}} | collective-permute-start | bytes 1179656 | tf_op jit(solution)/shard_map/ppermute | solution.py:205
  876.3 67.2 %collective-permute-start.72 = (bf16[2,192,768]{2,1,0:T(8,128)(2,1)S(1)}, bf16[2,192,768]{2,1,0:T(8,128)(2,1)}, u32[]{:S(2)}, u32[]{:S(2)}) collective-permute-start(bf16[2,192,768]{2,1,0:T(8,128)(2,1)S(1)} %add_convert_fusion.9), channel_id=1, source_target_pairs={{0,8},{4,12},{8,0},{12,4},{16,24},{20,28},{24,16},{28,20},{1,9},{5... | collective-permute-start | bytes 1769480 | tf_op jit(solution)/shard_map/ppermute | solution.py:210
  877.7 65.9 %collective-permute-start.73 = (bf16[2,192,768]{2,1,0:T(8,128)(2,1)S(1)}, bf16[2,192,768]{2,1,0:T(8,128)(2,1)}, u32[]{:S(2)}, u32[]{:S(2)}) collective-permute-start(bf16[2,192,768]{2,1,0:T(8,128)(2,1)S(1)} %add_convert_fusion.8), channel_id=1, source_target_pairs={{0,16},{4,20},{8,24},{12,28},{16,0},{20,4},{24,8},{28,12},{1,17},{... | collective-permute-start | bytes 1769480 | tf_op jit(solution)/shard_map/ppermute | solution.py:210
  883.2 60.3 %collective-permute-start.74 = (f32[1,1]{1,0:T(1,128)}, f32[1,1]{1,0:T(1,128)}, u32[]{:S(2)}, u32[]{:S(2)}) collective-permute-start(f32[1,1]{1,0:T(1,128)} %add.636), channel_id=1, source_target_pairs={{0,2},{1,3},{2,0},{3,1},{4,6},{5,7},{6,4},{7,5},{8,10},{9,11},{10,... | collective-permute-start | bytes 20 | tf_op jit(solution)/shard_map/ppermute | solution.py:210
  969.6 46.8 %collective-permute-start.79 = (bf16[304,1536]{1,0:T(8,128)(2,1)}, bf16[304,1536]{1,0:T(8,128)(2,1)}, u32[]{:S(2)}, u32[]{:S(2)}) collective-permute-start(bf16[304,1536]{1,0:T(8,128)(2,1)} %pad_maximum_fusion.9), channel_id=1, source_target_pairs={{3,2},{7,6},{11,10},{15,14},{19,18},{23,22},{27,26},{31,30}} | collective-permute-start | bytes 2801672 | tf_op jit(solution)/shard_map/ppermute | solution.py:133
  974.3 42.1 %collective-permute-start.78 = (bf16[304,1536]{1,0:T(8,128)(2,1)}, bf16[304,1536]{1,0:T(8,128)(2,1)}, u32[]{:S(2)}, u32[]{:S(2)}) collective-permute-start(bf16[304,1536]{1,0:T(8,128)(2,1)} %pad_maximum_fusion.8), channel_id=1, source_target_pairs={{0,1},{4,5},{8,9},{12,13},{16,17},{20,21},{24,25},{28,29}} | collective-permute-start | bytes 2801672 | tf_op jit(solution)/shard_map/ppermute | solution.py:132
  976.6 33.0 %collective-permute-start.80 = (bf16[256,1536]{1,0:T(8,128)(2,1)}, bf16[256,1536]{1,0:T(8,128)(2,1)}, u32[]{:S(2)}, u32[]{:S(2)}) collective-permute-start(bf16[256,1536]{1,0:T(8,128)(2,1)} %get-tuple-element.469), channel_id=1, source_target_pairs={{0,1},{4,5},{8,9},{12,13},{16,17},{20,21},{24,25},{28,29}} | collective-permute-start | bytes 2359304 | tf_op jit(solution)/shard_map/ppermute | solution.py:132
  1018.5 35.2 %collective-permute-start.83 = (bf16[304,1536]{1,0:T(8,128)(2,1)S(1)}, bf16[304,1536]{1,0:T(8,128)(2,1)S(1)}, u32[]{:S(2)}, u32[]{:S(2)}) collective-permute-start(bf16[304,1536]{1,0:T(8,128)(2,1)S(1)} %get-tuple-element.504), channel_id=1, source_target_pairs={{0,1},{1,2},{4,5},{5,6},{8,9},{9,10},{12,13},{13,14},{16,17},{17,1... | collective-permute-start | bytes 2801672 | tf_op jit(solution)/shard_map/ppermute | solution.py:132
  1021.2 32.4 %collective-permute-start.84 = (bf16[304,1536]{1,0:T(8,128)(2,1)S(1)}, bf16[304,1536]{1,0:T(8,128)(2,1)S(1)}, u32[]{:S(2)}, u32[]{:S(2)}) collective-permute-start(bf16[304,1536]{1,0:T(8,128)(2,1)S(1)} %get-tuple-element.503), channel_id=1, source_target_pairs={{2,1},{3,2},{6,5},{7,6},{10,9},{11,10},{14,13},{15,14},{18,17},{19... | collective-permute-start | bytes 2801672 | tf_op jit(solution)/shard_map/ppermute | solution.py:133
  1022.1 43.8 %collective-permute-start.82 = (bf16[2,192,681]{2,1,0:T(8,128)(2,1)S(1)}, bf16[2,192,681]{2,1,0:T(8,128)(2,1)S(1)}, u32[]{:S(2)}, u32[]{:S(2)}) collective-permute-start(bf16[2,192,681]{2,1,0:T(8,128)(2,1)S(1)} %add_convert_fusion.7), channel_id=1, source_target_pairs={{0,8},{4,12},{8,0},{12,4},{16,24},{20,28},{24,16},{28,20},{1,9},{5... | collective-permute-start | bytes 1569032 | tf_op jit(solution)/shard_map/ppermute | solution.py:210
  1033.8 33.2 %collective-permute-start.89 = (bf16[256,1536]{1,0:T(8,128)(2,1)S(1)}, bf16[256,1536]{1,0:T(8,128)(2,1)S(1)}, u32[]{:S(2)}, u32[]{:S(2)}) collective-permute-start(bf16[256,1536]{1,0:T(8,128)(2,1)S(1)} %add_convert_fusion.5), channel_id=1, source_target_pairs={{1,0},{2,1},{3,2},{5,4},{6,5},{7,6},{9,8},{10,9},{11,10},{13,12},{... | collective-permute-start | bytes 2359304 | tf_op jit(solution)/shard_map/ppermute | solution.py:133
  1035.4 35.2 %collective-permute-start.88 = (bf16[256,1536]{1,0:T(8,128)(2,1)S(1)}, bf16[256,1536]{1,0:T(8,128)(2,1)S(1)}, u32[]{:S(2)}, u32[]{:S(2)}) collective-permute-start(bf16[256,1536]{1,0:T(8,128)(2,1)S(1)} %add_convert_fusion.6), channel_id=1, source_target_pairs={{0,1},{1,2},{2,3},{4,5},{5,6},{6,7},{8,9},{9,10},{10,11},{12,13},{... | collective-permute-start | bytes 2359304 | tf_op jit(solution)/shard_map/ppermute | solution.py:132
  (179 other events, 3221.7 us)
Sparse Core Ops, SparseCore 0:
  13.0 51.5 all-gather.4
  66.5 219.0 all-gather.6
  799.6 298.2 reduce-scatter.1
  1099.8 41.9 all-gather.8

commit v16 on v15

--- a/solution.py
+++ b/solution.py
@@ -97,20 +97,19 @@
     return order
 
 
+def arrivals(n, turn):
+    return [dev - places[turn] for dev, places in enumerate(arrival_order(n))]
+
+
 def arrived(rights, lefts, turn):
-    n = lax.axis_size("seq")
-    me = lax.axis_index("seq")
-    sources = {}
-    for dev, places in enumerate(arrival_order(n)):
-        gap = dev - places[turn]
-        sources.setdefault(gap, []).append(dev)
+    gaps = arrivals(lax.axis_size("seq"), turn)
     block = None
-    for gap, devs in sources.items():
+    for gap in sorted(set(gaps)):
         moved = rights[gap] if gap >= 0 else lefts[-gap]
         if block is None:
             block = moved
         else:
-            mine = jnp.array([dev in devs for dev in range(n)])[me]
+            mine = jnp.array([each == gap for each in gaps])[lax.axis_index("seq")]
             block = jnp.where(mine, moved, block)
     return block
 
@@ -159,6 +158,18 @@
 
     def ahead(self, h):
         return len(self.rights[h]) - 1 - self.landed[h]
+
+    def choice(self, turn):
+        gaps = arrivals(lax.axis_size("seq"), turn)
+        places = sorted(set(gaps))
+        return jnp.array([places.index(gap) for gap in gaps], jnp.int32)[lax.axis_index("seq")]
+
+    def blocks(self, turn):
+        places = sorted(set(arrivals(lax.axis_size("seq"), turn)))
+        return [
+            [rights[gap] if gap >= 0 else lefts[-gap] for gap in places]
+            for rights, lefts in zip(self.rights, self.lefts)
+        ]
 
     def block(self, turn):
         return [arrived(self.rights[h], self.lefts[h], turn) for h in (0, 1)]
@@ -486,15 +497,31 @@
     return (nn(pick[:, :middle], tok_ref[...]) + nn(pick[:, middle:], more_ref[:middle, :])).astype(low)
 
 
+def take_tokens(choices, at_ref, refs, tok_ref, more_ref, sems):
+    for choice in range(choices):
+
+        @pl.when(at_ref[2] == choice)
+        def _():
+            copies = [
+                pltpu.make_async_copy(refs[choice], tok_ref, sems.at[0]),
+                pltpu.make_async_copy(refs[choices + choice], more_ref, sems.at[1]),
+            ]
+            for copy in copies:
+                copy.start()
+            for copy in copies:
+                copy.wait()
+
+
 def experts_kernel(
-    few, pair, at_ref, tok_ref, more_ref, slot_ref, member_ref, router_ref, wgu_ref, wd_ref, *refs
+    few, pair, choices, at_ref, slot_ref, member_ref, router_ref, wgu_ref, wd_ref, *refs
 ):
-    part_ref, x_ref, gu_ref, gates_ref, acc, gates_all, down = refs[-7:]
+    part_ref, x_ref, gu_ref, gates_ref, acc, gates_all, down, tok_ref, more_ref, sems = refs[-10:]
     step, steps = pl.program_id(0), pl.num_programs(0)
     slots = x_ref.shape[2]
 
     @pl.when(step == 0)
     def _():
+        take_tokens(choices, at_ref, refs, tok_ref, more_ref, sems)
         member = member_ref[...] > 0
         logits = [nt(router_ref[...], ref[...]) for ref in (tok_ref, more_ref)]
         chosen = jnp.where(member, jnp.concatenate(logits, axis=1), masked_score)
@@ -528,17 +555,21 @@
 
 
 def back_kernel(
-    few, pair, at_ref, tok_ref, more_ref, slot_ref, gates_ref, mix_ref, router_ref, gu_ref, wgu_ref, wd_ref, *refs
+    few, pair, choices, at_ref, slot_ref, gates_ref, router_ref, gu_ref, wgu_ref, wd_ref, *refs
 ):
-    part_ref, d_ref, dgu_ref, act_ref, dlog_ref, acc, dlog_all, down = refs[-8:]
+    part_ref, d_ref, dgu_ref, act_ref, dlog_ref, acc, dlog_all, down, tok_ref, more_ref, sems = refs[-11:]
     step, steps = pl.program_id(0), pl.num_programs(0)
     slots, hidden = gu_ref.shape[2], gu_ref.shape[3] // 2
 
     @pl.when(step == 0)
     def _():
+        take_tokens(choices, at_ref, refs, tok_ref, more_ref, sems)
         dlog_all[...] = jnp.zeros_like(dlog_all)
         acc[...] = jnp.zeros_like(acc)
 
+    middle, count = tok_ref.shape[0], slot_ref.shape[1]
+    mix = more_ref[middle : middle + 2, :count].astype(full)
+    mix = mix[0:1, :] + mix[1:2, :]
     place = lax.broadcasted_iota(jnp.int32, (slots, 1), 0)
     puts, dxs = [], []
     for i in range(pair):
@@ -557,7 +588,7 @@
         act = silu * u
         d_gate = jnp.sum(d_act * act, axis=1, keepdims=True)
         d_gate = jnp.sum(jnp.where(here, d_gate, 0.0), axis=0, keepdims=True)
-        dlog_all[pl.ds(e, 1), :] = gate_row * (d_gate - mix_ref[...])
+        dlog_all[pl.ds(e, 1), :] = gate_row * (d_gate - mix)
         act_ref[i, 0] = (act * gate).astype(low)
         d_act = d_act * gate
         d_g = (d_act * u * (sig + silu * (1.0 - sig))).astype(low)
@@ -599,7 +630,8 @@
         grid_spec=pltpu.PrefetchScalarGridSpec(
             num_scalar_prefetch=1,
             grid=(experts,),
-            in_specs=in_specs + [pl.BlockSpec(memory_space=pl.ANY)] * len(buffers),
+            in_specs=in_specs
+            + [pl.BlockSpec(memory_space=pl.ANY)] * (len(inputs) + len(buffers) - len(in_specs)),
             out_specs=out_specs,
             scratch_shapes=scratch,
         ),
@@ -621,15 +653,14 @@
     experts, width, columns = weights.shape
     hidden = columns // 3
     pair = 1 + (experts + 1) % 2
-    count = 2 * tokens[0].shape[0]
+    count = slot_of.shape[1]
     total_experts = member.shape[0]
     return shard_call(
-        functools.partial(experts_kernel, few, pair),
+        functools.partial(experts_kernel, few, pair, len(tokens[0])),
         "experts_forward",
         at,
-        [*tokens, slot_of, member, router, weights, weights],
+        [slot_of, member, router, weights, weights, *tokens[0], *tokens[1]],
         [
-            *(same(*half.shape) for half in tokens),
             same(experts, count),
             same(total_experts, count),
             same(total_experts, width),
@@ -652,30 +683,30 @@
             pltpu.VMEM((count, width), full),
             pltpu.VMEM((total_experts, count), full),
             pltpu.VMEM((pair, hidden, width), low),
+            *(pltpu.VMEM(half[0].shape, low) for half in tokens),
+            pltpu.SemaphoreType.DMA((2,)),
         ],
         experts // pair,
     )
 
 
 def experts_backward(
-    turn, devs, at, d_tokens, slot_of, gates, mix_dot, router, gu, weights, few, buffers
+    turn, devs, at, d_tokens, slot_of, gates, router, gu, weights, few, buffers
 ):
     experts, width, columns = weights.shape
     hidden = columns // 3
     pair = 1 + (experts + 1) % 2
-    count = 2 * d_tokens[0].shape[0]
+    count = slot_of.shape[1]
     slots = gu.shape[2]
     lines = router.shape[0]
     return shard_call(
-        functools.partial(back_kernel, few, pair),
+        functools.partial(back_kernel, few, pair, len(d_tokens[0])),
         "experts_backward",
         at,
-        [*d_tokens, slot_of, gates, mix_dot, router, gu, weights, weights],
+        [slot_of, gates, router, gu, weights, weights, *d_tokens[0], *d_tokens[1]],
         [
-            *(same(*half.shape) for half in d_tokens),
             same(experts, count),
             same(experts, count),
-            same(1, count),
             same(lines, width),
             in_turn(pair, turn, slots, 2 * hidden),
             *weight_specs(pair, width, hidden),
@@ -699,6 +730,8 @@
             pltpu.VMEM((count, width), full),
             pltpu.VMEM((lines, count), full),
             pltpu.VMEM((pair, hidden, width), low),
+            *(pltpu.VMEM(half[0].shape, low) for half in d_tokens),
+            pltpu.SemaphoreType.DMA((2,)),
         ],
         experts // pair,
     )
@@ -911,7 +944,7 @@
 
     normed_low = normed_two.astype(low)
     line = LineGather((normed_low[:middle], normed_low[middle:]))
-    buffers, gates, tokens = [], [], []
+    buffers, gates = [], []
     line.go(0)
     line.go(1)
     other = ()
@@ -924,16 +957,20 @@
             line_slots = line.hold(slot_of[turn])
         else:
             line_slots = slot_of[turn]
-        tokens.append(line.block(turn))
         *buffers, shard_gates = experts_forward(
-            turn, n, jnp.stack([order[turn], me]), tokens[turn], line_slots, member[turn],
-            router, weights, w_down.shape[1], slots, buffers,
+            turn, n, jnp.stack([order[turn], me, line.choice(turn)]), line.blocks(turn), line_slots,
+            member[turn], router, weights, w_down.shape[1], slots, buffers,
         )
         gates.append(shard_gates)
         other = shard_gates
     mix_parts, expert_in, gate_up = buffers
+    token_line = line
     cuts = (slice(0, middle), slice(middle, None))
-    mixture, _ = line_scatter(2, lambda h, shift: at_place(mix_parts[:, cuts[h]], me + shift), ())
+    mixture, tokens = line_scatter(
+        2,
+        lambda h, shift: at_place(mix_parts[:, cuts[h]], me + shift),
+        (lambda before, given: [token_line.block(turn) for turn in range(n)],),
+    )
     output_f32 = hidden + resid_mult * mixture
     activations = output_f32.astype(low).reshape(1, shard_len, width)
     error_rows = output_f32 - teacher.astype(full).reshape(shard_len, width)
@@ -961,12 +998,9 @@
         else:
             line.go(0)
             line.go(1)
-        d_block = line.block(turn)
-        mix_dot = d_block[1][middle : middle + 2, :shard_len].astype(full)
-        mix_dot = jnp.sum(mix_dot, axis=0, keepdims=True)
         *buffers, shard_logits = experts_backward(
-            turn, n, jnp.stack([order[turn], me]), d_block, slot_of[turn], gates[turn], mix_dot,
-            own_router, gate_up, weights, w_down.shape[1], buffers,
+            turn, n, jnp.stack([order[turn], me, line.choice(turn)]), line.blocks(turn), slot_of[turn],
+            gates[turn], own_router, gate_up, weights, w_down.shape[1], buffers,
         )
         d_logits.append(shard_logits)
     d_parts, d_rows, d_gate_up, act_low = buffers

time: 1160 us -> 1170 us (level)
  local copies, waits for them, and re-layouts: 62.6 us -> 74.5 us
    select_n x16 -> x8, other arithmetic: 35.3 us -> 27 us  [arrived(): block = jnp.where(mine, moved, block)]
    unnamed x259 -> x311, local copies, waits for them, and re-layouts: 22.7 us -> 29.2 us
  transfers between devices with their start and end apart: 99 -> 99, of which waited for: 39 -> 39; matrix products, arithmetic and copies ran while one was open for 13% -> 14% of each run, Pallas kernels for 26% -> 26%
where the time goes in v16:
time: 1170 us; the launch traced here: 1160 us
  Pallas kernels  391 us (33%)
  waiting for transfers between devices  299 us (26%)
  starting transfers between devices  208 us (18%)
  other arithmetic  116 us (10%)
  local copies, waits for them, and re-layouts  74.5 us (6%)
  matrix products  40.3 us (3%)
  between operations  35.2 us (3%)
    pallas_call x8, Pallas kernels, shard_call(): pl.pallas_call(kernel, grid_spec=pltpu.PrefetchScalarGridSpec(num_scalar_...  234 us
    ppermute x15, waiting for transfers between devices, line_pass(): lax.ppermute(to_right, 'seq', [(i, i + 1) for i in range(n - k)])  124 us
    ppermute x15, starting transfers between devices, line_pass(): lax.ppermute(to_right, 'seq', [(i, i + 1) for i in range(n - k)])  70.7 us
    pallas_call x1, Pallas kernels, attention_backward(): pl.pallas_call(functools.partial(backward_kernel, seq_len, query_rows, ke...  58.5 us
    ppermute x18, waiting for transfers between devices, line_move(): lax.ppermute(left, 'seq', [(i, i - 1) for i in range(1, n - k + 1)])  56.8 us
    pallas_call x2, Pallas kernels, weight_grads(): pl.pallas_call(functools.partial(grads_kernel, few), grid=(stop - first,)...  51 us
    pallas_call x1, Pallas kernels, attention_forward(): pl.pallas_call(functools.partial(forward_kernel, seq_len, query_rows, key...  41.7 us
    ppermute x18, starting transfers between devices, line_move(): lax.ppermute(right, 'seq', [(i, i + 1) for i in range(k - 1, n - 1)])  41.4 us
  transfers between devices with their start and end apart: 99, of which 39 were waited for; matrix products, arithmetic and copies ran while one was open for 14% of the time, Pallas kernels for 26%

profile of v16, /device:TPU:0, one launch (start us, length us, event | category | flops | bytes accessed | tf_op | source)
XLA Modules:
  0.0 1164.0 jit_solution(1477947008239740389)
XLA Ops:
  15.1 6.4 maximum_maximum_fusion
  23.2 6.0 collective-permute-start
  31.8 5.5 collective-permute-start.2
  63.0 6.5 collective-permute-done.3
  90.6 13.7 %collective-permute-done.7 = bf16[272,1536]{1,0:T(8,128)(2,1)} collective-permute-done((bf16[272,1536]{1,0:T(8,128)(2,1)}, bf16[272,1536]{1,0:T(8,128)(2,1)}, u32[]{:S(2)}, u32[]{:S(2)}) %collective-permute-start.7) | collective-permute-done | bytes 835616 | tf_op jit(solution)/shard_map/ppermute | solution.py:68
  121.2 16.5 %collective-permute-done.11 = bf16[272,1536]{1,0:T(8,128)(2,1)} collective-permute-done((bf16[272,1536]{1,0:T(8,128)(2,1)}, bf16[272,1536]{1,0:T(8,128)(2,1)}, u32[]{:S(2)}, u32[]{:S(2)}) %collective-permute-start.11) | collective-permute-done | bytes 835616 | tf_op jit(solution)/shard_map/ppermute | solution.py:68
  152.9 41.7 %attention_forward.1 = (bf16[4,384,512]{2,1,0:T(8,128)(2,1)}, f32[2,3,64,2048]{3,2,1,0:T(8,128)}, f32[2,3,1,2048]{3,2,1,0:T(1,128)}) custom-call(s32[1,2048]{1,0:T(1,128)} %bitcast.305, bf16[4,2,5,64,512]{4,3,2,1,0:T(8,128)(2,1)} %copy-done.25, bf16[2,2048,64]{2,1,0:T(8,128)(2,1)} %copy.137.k_ref, bf16[2,64,2048]{2,1,0:T(8,128)(2,1)} %copy.138.vt_ref), custom_call_target="tpu_custom_call" | custom-call | tf_op jit(solution)/shard_map/attention_forward/pallas_call | solution.py:353
  215.9 6.1 collective-permute-done.14
  222.0 16.0 %collective-permute-done.16 = bf16[384,512]{1,0:T(8,128)(2,1)S(1)} collective-permute-done((bf16[384,512]{1,0:T(8,128)(2,1)S(1)}, bf16[384,512]{1,0:T(8,128)(2,1)S(1)}, u32[]{:S(2)}, u32[]{:S(2)}) %collective-permute-start.16) | collective-permute-done | bytes 393248 | tf_op jit(solution)/shard_map/ppermute | solution.py:216
  250.8 5.4 collective-permute-start.22
  258.4 7.3 collective-permute-done.18.refs_1_
  265.6 5.3 collective-permute-done.19.refs_0_.refs_1_
  273.0 6.6 collective-permute-done.22.refs_3_
  279.6 8.3 collective-permute-done.23.refs_2_.refs_4_
  298.2 25.4 %experts_forward.4 = (bf16[4,512,1536]{2,1,0:T(8,128)(2,1)}, bf16[10,4,160,1536]{3,2,1,0:T(8,128)(2,1)}, bf16[10,4,160,1024]{3,2,1,0:T(8,128)(2,1)}, f32[10,512]{1,0:T(8,128)S(1)}) custom-call(s32[3]{0:T(128)S(1)} %get-tuple-element.593.at_ref, s32[10,512]{1,0:T(8,128)S(1)} %copy-done.8, f32[40,512]{1,0:T(8,128)S(1)} %copy-done.7, ...), custom_call_target="tpu_custom_call" | custom-call | tf_op jit(solution)/shard_map/experts_forward/pallas_call | solution.py:628
  326.9 10.0 collective-permute-start.29
  340.8 25.4 %experts_forward.5 = (bf16[4,512,1536]{2,1,0:T(8,128)(2,1)}, bf16[10,4,160,1536]{3,2,1,0:T(8,128)(2,1)}, bf16[10,4,160,1024]{3,2,1,0:T(8,128)(2,1)}, f32[10,512]{1,0:T(8,128)S(1)}) custom-call(s32[3]{0:T(128)S(1)} %get-tuple-element.594.at_ref, ...), custom_call_target="tpu_custom_call", output_to_operand_aliasing={{0}: (10, {}), {1}: (11, {}), {2}: (12, {})} | custom-call | tf_op jit(solution)/shard_map/experts_forward/pallas_call | solution.py:628
  366.3 6.3 select_select_fusion.2
  372.6 28.3 %experts_forward.6 = (bf16[4,512,1536]{2,1,0:T(8,128)(2,1)}, bf16[10,4,160,1536]{3,2,1,0:T(8,128)(2,1)}, bf16[10,4,160,1024]{3,2,1,0:T(8,128)(2,1)}, f32[10,512]{1,0:T(8,128)S(1)}) custom-call(s32[3]{0:T(128)S(1)} %get-tuple-element.595.at_ref, ...), custom_call_target="tpu_custom_call", output_to_operand_aliasing={{0}: (12, {}), {1}: (13, {}), {2}: (14, {})} | custom-call | tf_op jit(solution)/shard_map/experts_forward/pallas_call | solution.py:628
  401.0 25.4 %experts_forward.7 = (bf16[4,512,1536]{2,1,0:T(8,128)(2,1)}, bf16[10,4,160,1536]{3,2,1,0:T(8,128)(2,1)}, bf16[10,4,160,1024]{3,2,1,0:T(8,128)(2,1)}, f32[10,512]{1,0:T(8,128)S(1)}) custom-call(s32[3]{0:T(128)S(1)} %get-tuple-element.592.at_ref, s32[10,512]{1,0:T(8,128)S(1)} %copy-done.10, ...), custom_call_target="tpu_custom_call", output_to_operand_aliasing={{0}: (14, {}), {1}: (15, {}), {2}: (16, {})} | custom-call | tf_op jit(solution)/shard_map/experts_forward/pallas_call | solution.py:628
  429.8 8.1 collective-permute-start.30
  446.0 9.9 collective-permute-done.30
  461.5 11.3 collective-permute-done.36
  478.4 11.3 collective-permute-done.32
  490.0 5.3 collective-permute-start.34
  496.8 9.7 collective-permute-done.38
  506.9 5.3 collective-permute-start.40
  551.5 32.4 %experts_backward.4 = (bf16[4,512,1536]{2,1,0:T(8,128)(2,1)}, bf16[10,4,160,1536]{3,2,1,0:T(8,128)(2,1)}, bf16[10,4,160,1024]{3,2,1,0:T(8,128)(2,1)}, bf16[10,4,...) custom-call(s32[3]{0:T(128)S(1)} %copy-done.21, s32[10,512]{1,0:T(8,128)S(1)} %copy-done.9, f32[10,512]{1,0:T(8,128)S(1)} %copy-done.15, ...), custom_call_target="tpu_custom_call" | custom-call | tf_op jit(solution)/shard_map/experts_backward/pallas_call | solution.py:628
  588.0 32.3 %experts_backward.5 = (bf16[4,512,1536]{2,1,0:T(8,128)(2,1)}, bf16[10,4,160,1536]{3,2,1,0:T(8,128)(2,1)}, bf16[10,4,160,1024]{3,2,1,0:T(8,128)(2,1)}, bf16[10,4,...) custom-call(s32[3]{0:T(128)S(1)} %get-tuple-element.594.at_ref, ...), custom_call_target="tpu_custom_call", output_to_operand_aliasing={{0}: (11, {}), {1}: (12, {}), {2}: (13, {}), {3}: (14, {})} | custom-call | tf_op jit(solution)/shard_map/experts_backward/pallas_call | solution.py:628
  624.6 32.3 %experts_backward.6 = (bf16[4,512,1536]{2,1,0:T(8,128)(2,1)}, bf16[10,4,160,1536]{3,2,1,0:T(8,128)(2,1)}, bf16[10,4,160,1024]{3,2,1,0:T(8,128)(2,1)}, bf16[10,4,...) custom-call(s32[3]{0:T(128)S(1)} %copy-done.19, ...), custom_call_target="tpu_custom_call", output_to_operand_aliasing={{0}: (13, {}), {1}: (14, {}), {2}: (15, {}), {3}: (16, {})} | custom-call | tf_op jit(solution)/shard_map/experts_backward/pallas_call | solution.py:628
  660.2 32.3 %experts_backward.7 = (bf16[4,512,1536]{2,1,0:T(8,128)(2,1)}, bf16[10,4,160,1536]{3,2,1,0:T(8,128)(2,1)}, bf16[10,4,160,1024]{3,2,1,0:T(8,128)(2,1)}, bf16[10,4,...) custom-call(s32[3]{0:T(128)S(1)} %get-tuple-element.592.at_ref, ...), custom_call_target="tpu_custom_call", output_to_operand_aliasing={{0}: (15, {}), {1}: (16, {}), {2}: (17, {}), {3}: (18, {})} | custom-call | tf_op jit(solution)/shard_map/experts_backward/pallas_call | solution.py:628
  696.3 9.9 collective-permute-start.57
  708.2 25.6 %weight_grads.2.refs_0_ = bf16[10,1536,1536]{2,1,0:T(8,128)(2,1)} custom-call(bf16[10,640,1536]{2,1,0:T(8,128)(2,1)} %bitcast.264, bf16[10,640,1024]{2,1,0:T(8,128)(2,1)} %bitcast.268, bf16[10,640,512]{2,1,0:T(8,128)(2,1)} %bitcast.270, bf16[10,640,1536]{2,1,0:T(8,128)(2,1)} %bitcast.266), custom_call_target="tpu_custom_call" | custom-call | tf_op jit(solution)/shard_map/weight_grads/pallas_call | solution.py:801
  742.5 25.4 %weight_grads.3 = bf16[10,1536,1536]{2,1,0:T(8,128)(2,1)} custom-call(bf16[10,640,1536]{2,1,0:T(8,128)(2,1)} %bitcast.265, bf16[10,640,1024]{2,1,0:T(8,128)(2,1)} %bitcast.269, bf16[10,640,512]{2,1,0:T(8,128)(2,1)} %bitcast.271, bf16[10,640,1536]{2,1,0:T(8,128)(2,1)} %bitcast.267, ...), custom_call_target="tpu_custom_call", output_to_operand_aliasing={{}: (4, {})} | custom-call | tf_op jit(solution)/shard_map/weight_grads/pallas_call | solution.py:801
  776.6 22.4 %collective-permute-done.61 = bf16[512,1536]{1,0:T(8,128)(2,1)S(1)} collective-permute-done((bf16[512,1536]{1,0:T(8,128)(2,1)S(1)}, bf16[512,1536]{1,0:T(8,128)(2,1)S(1)}, u32[]{:S(2)}, u32[]{:S(2)}) %collective-permute-start.61) | collective-permute-done | bytes 1572896 | tf_op jit(solution)/shard_map/ppermute | solution.py:131
  819.8 5.9 out_grads.1
  826.7 6.1 fusion.33
  854.2 7.6 collective-permute-done.67.refs_3_
  861.9 16.6 %collective-permute-done.69.refs_5_ = bf16[384,512]{1,0:T(8,128)(2,1)S(1)} collective-permute-done((bf16[384,512]{1,0:T(8,128)(2,1)S(1)}, bf16[384,512]{1,0:T(8,128)(2,1)S(1)}, u32[]{:S(2)}, u32[]{:S(2)}) %collective-permute-start.69) | collective-permute-done | bytes 393248 | tf_op jit(solution)/shard_map/ppermute | solution.py:216
  889.4 58.5 %attention_backward.1 = (bf16[2,3,64,2048]{3,2,1,0:T(8,128)(2,1)}, bf16[2,64,2048]{2,1,0:T(8,128)(2,1)}, bf16[2,64,2048]{2,1,0:T(8,128)(2,1)}) custom-call(s32[1]{0:T(128)} %bitcast.51.me_ref, s32[1,2048]{1,0:T(1,128)} %bitcast.306, bf16[4,2,5,64,512]{4,3,2,1,0:T(8,128)(2,1)} %copy-done.25, bf16[2,2048,64]{2,1,0:T(8,128)(2,1)} %copy.137.k_ref, ...), custom_call_target="tpu_custom_call" | custom-call | tf_op jit(solution)/shard_map/attention_backward/pallas_call | solution.py:436
  1000.8 15.5 %collective-permute-done.80 = bf16[256,1536]{1,0:T(8,128)(2,1)} collective-permute-done((bf16[256,1536]{1,0:T(8,128)(2,1)}, bf16[256,1536]{1,0:T(8,128)(2,1)}, u32[]{:S(2)}, u32[]{:S(2)}) %collective-permute-start.80) | collective-permute-done | bytes 786464 | tf_op jit(solution)/shard_map/ppermute | solution.py:131
  1029.3 11.1 collective-permute-done.85
  1042.1 7.0 collective-permute-start.88
  1049.1 11.3 collective-permute-done.83
  1062.2 7.2 collective-permute-start.90
  1078.5 13.7 %collective-permute-done.90 = bf16[304,1536]{1,0:T(8,128)(2,1)S(1)} collective-permute-done((bf16[304,1536]{1,0:T(8,128)(2,1)S(1)}, bf16[304,1536]{1,0:T(8,128)(2,1)S(1)}, u32[]{:S(2)}, u32[]{:S(2)}) %collective-permute-start.90) | collective-permute-done | bytes 933920 | tf_op jit(solution)/shard_map/ppermute | solution.py:131
  1098.2 6.4 reduce-scatter.2.cloned.1.call-done
  1124.7 22.8 %all-gather.9.cloned.1.call-done = bf16[768,1065]{1,0:T(8,128)(2,1)} async-done(((bf16[192,1065]{1,0:T(8,128)(2,1)}), bf16[768,1065]{1,0:T(8,128)(2,1)}) %all-gather.9.cloned.1.call-update) | async-done | bytes 1635856 | tf_op jit(solution)/shard_map/all_gather | solution.py:1119
  (681 shorter events, 393.6 us)
Async XLA Ops:
  7.2 70.0 %all-gather.5.cloned.1.call-start = ((), (), s32[]{:S(2)}) async-start(), calls=%async_computation.1 | async-start | bytes 7962624 | tf_op jit(solution)/shard_map/all_gather | solution.py:853
  12.9 281.4 %all-gather.7.cloned.1.call-start = ((), (), s32[]{:S(2)}) async-start(), calls=%async_computation.2 | async-start | bytes 53084160 | tf_op jit(solution)/shard_map/all_gather | solution.py:870
  21.5 1083.1 %reduce-scatter.2.cloned.1.call-start = ((), (), s32[]{:S(2)}) async-start(), calls=%async_computation.3 | async-start | bytes 53084160 | tf_op jit(solution)/shard_map/reduce_scatter | solution.py:1026
  23.2 33.8 %collective-permute-start = (bf16[256,1536]{1,0:T(8,128)(2,1)S(1)}, bf16[256,1536]{1,0:T(8,128)(2,1)}, u32[]{:S(2)}, u32[]{:S(2)}) collective-permute-start(bf16[256,1536]{1,0:T(8,128)(2,1)S(1)} %get-tuple-element.539), channel_id=1, source_target_pairs={{0,1},{1,2},{2,3},{4,5},{5,6},{6,7},{8,9},{9,10},{10,11},{12,13},{... | collective-permute-start | bytes 2359304 | tf_op jit(solution)/shard_map/ppermute | solution.py:67
  69.6 34.8 %collective-permute-start.7 = (bf16[272,1536]{1,0:T(8,128)(2,1)}, bf16[272,1536]{1,0:T(8,128)(2,1)}, u32[]{:S(2)}, u32[]{:S(2)}) collective-permute-start(bf16[272,1536]{1,0:T(8,128)(2,1)} %collective-permute-done.3), channel_id=1, source_target_pairs={{1,0},{2,1},{5,4},{6,5},{9,8},{10,9},{13,12},{14,13},{17,16},{18,1... | collective-permute-start | bytes 2506760 | tf_op jit(solution)/shard_map/ppermute | solution.py:68
  70.9 33.5 %collective-permute-start.6 = (bf16[272,1536]{1,0:T(8,128)(2,1)}, bf16[272,1536]{1,0:T(8,128)(2,1)}, u32[]{:S(2)}, u32[]{:S(2)}) collective-permute-start(bf16[272,1536]{1,0:T(8,128)(2,1)} %collective-permute-done.2), channel_id=1, source_target_pairs={{1,2},{2,3},{5,6},{6,7},{9,10},{10,11},{13,14},{14,15},{17,18},{18... | collective-permute-start | bytes 2506760 | tf_op jit(solution)/shard_map/ppermute | solution.py:67
  204.2 33.8 %collective-permute-start.16 = (bf16[384,512]{1,0:T(8,128)(2,1)S(1)}, bf16[384,512]{1,0:T(8,128)(2,1)S(1)}, u32[]{:S(2)}, u32[]{:S(2)}) collective-permute-start(bf16[384,512]{1,0:T(8,128)(2,1)S(1)} %get-tuple-element.533), channel_id=1, source_target_pairs={{2,0},{3,1},{6,4},{7,5},{10,8},{11,9},{14,12},{15,13},{18,16},{19,... | collective-permute-start | bytes 1179656 | tf_op jit(solution)/shard_map/ppermute | solution.py:216
  271.0 53.2 %collective-permute-start.20 = (bf16[256,1536]{1,0:T(8,128)(2,1)}, bf16[256,1536]{1,0:T(8,128)(2,1)S(1)}, u32[]{:S(2)}, u32[]{:S(2)}) collective-permute-start(bf16[256,1536]{1,0:T(8,128)(2,1)} %collective-permute-done.18.refs_1_), channel_id=1, source_target_pairs={{1,2},{2,3},{5,6},{6,7},{9,10},{10,11},{13,14},{14,15},{17,18},{18... | collective-permute-start | bytes 2359304 | tf_op jit(solution)/shard_map/ppermute | solution.py:67
  271.7 52.5 %collective-permute-start.21 = (bf16[256,1536]{1,0:T(8,128)(2,1)S(1)}, bf16[256,1536]{1,0:T(8,128)(2,1)S(1)}, u32[]{:S(2)}, u32[]{:S(2)}) collective-permute-start(bf16[256,1536]{1,0:T(8,128)(2,1)S(1)} %collective-permute-done.19.refs_0_.refs_1_), channel_id=1, source_target_pairs={{1,0},{2,1},{5,4},{6,5},{9,8},{10,9},{13,12},{14,13},{17,16},{18,1... | collective-permute-start | bytes 2359304 | tf_op jit(solution)/shard_map/ppermute | solution.py:68
  287.8 38.4 %collective-permute-start.26 = (bf16[256,1536]{1,0:T(8,128)(2,1)}, bf16[256,1536]{1,0:T(8,128)(2,1)}, u32[]{:S(2)}, u32[]{:S(2)}) collective-permute-start(bf16[256,1536]{1,0:T(8,128)(2,1)} %collective-permute-done.22.refs_3_), channel_id=1, source_target_pairs={{1,2},{2,3},{5,6},{6,7},{9,10},{10,11},{13,14},{14,15},{17,18},{18... | collective-permute-start | bytes 2359304 | tf_op jit(solution)/shard_map/ppermute | solution.py:67
  289.4 36.8 %collective-permute-start.27 = (bf16[256,1536]{1,0:T(8,128)(2,1)S(1)}, bf16[256,1536]{1,0:T(8,128)(2,1)}, u32[]{:S(2)}, u32[]{:S(2)}) collective-permute-start(bf16[256,1536]{1,0:T(8,128)(2,1)S(1)} %collective-permute-done.23.refs_2_.refs_4_), channel_id=1, source_target_pairs={{1,0},{2,1},{5,4},{6,5},{9,8},{10,9},{13,12},{14,13},{17,16},{18,1... | collective-permute-start | bytes 2359304 | tf_op jit(solution)/shard_map/ppermute | solution.py:68
  324.2 42.1 %collective-permute-start.24 = (bf16[256,1536]{1,0:T(8,128)(2,1)S(1)}, bf16[256,1536]{1,0:T(8,128)(2,1)S(1)}, u32[]{:S(2)}, u32[]{:S(2)}) collective-permute-start(bf16[256,1536]{1,0:T(8,128)(2,1)S(1)} %collective-permute-done.20.refs_2_), channel_id=1, source_target_pairs={{2,3},{6,7},{10,11},{14,15},{18,19},{22,23},{26,27},{30,31}} | collective-permute-start | bytes 2359304 | tf_op jit(solution)/shard_map/ppermute | solution.py:67
  324.9 41.4 %collective-permute-start.25 = (bf16[256,1536]{1,0:T(8,128)(2,1)S(1)}, bf16[256,1536]{1,0:T(8,128)(2,1)S(1)}, u32[]{:S(2)}, u32[]{:S(2)}) collective-permute-start(bf16[256,1536]{1,0:T(8,128)(2,1)S(1)} %collective-permute-done.21.refs_0_.refs_1_), channel_id=1, source_target_pairs={{1,0},{5,4},{9,8},{13,12},{17,16},{21,20},{25,24},{29,28}} | collective-permute-start | bytes 2359304 | tf_op jit(solution)/shard_map/ppermute | solution.py:68
  326.2 40.1 %collective-permute-start.28 = (bf16[256,1536]{1,0:T(8,128)(2,1)}, bf16[256,1536]{1,0:T(8,128)(2,1)S(1)}, u32[]{:S(2)}, u32[]{:S(2)}) collective-permute-start(bf16[256,1536]{1,0:T(8,128)(2,1)} %collective-permute-done.26.refs_5_.refs_6_), channel_id=1, source_target_pairs={{2,3},{6,7},{10,11},{14,15},{18,19},{22,23},{26,27},{30,31}} | collective-permute-start | bytes 2359304 | tf_op jit(solution)/shard_map/ppermute | solution.py:67
  326.9 39.4 %collective-permute-start.29 = (bf16[256,1536]{1,0:T(8,128)(2,1)}, bf16[256,1536]{1,0:T(8,128)(2,1)S(1)}, u32[]{:S(2)}, u32[]{:S(2)}) collective-permute-start(bf16[256,1536]{1,0:T(8,128)(2,1)} %collective-permute-done.27.refs_3_.refs_5_), channel_id=1, source_target_pairs={{1,0},{5,4},{9,8},{13,12},{17,16},{21,20},{25,24},{29,28}} | collective-permute-start | bytes 2359304 | tf_op jit(solution)/shard_map/ppermute | solution.py:68
  438.8 33.9 %collective-permute-start.36 = (bf16[256,1536]{1,0:T(8,128)(2,1)S(1)}, bf16[256,1536]{1,0:T(8,128)(2,1)S(1)}, u32[]{:S(2)}, u32[]{:S(2)}) collective-permute-start(bf16[256,1536]{1,0:T(8,128)(2,1)S(1)} %get-tuple-element.497), channel_id=1, source_target_pairs={{0,1},{4,5},{8,9},{12,13},{16,17},{20,21},{24,25},{28,29}} | collective-permute-start | bytes 2359304 | tf_op jit(solution)/shard_map/ppermute | solution.py:131
  440.4 32.4 %collective-permute-start.37 = (bf16[256,1536]{1,0:T(8,128)(2,1)S(1)}, bf16[256,1536]{1,0:T(8,128)(2,1)S(1)}, u32[]{:S(2)}, u32[]{:S(2)}) collective-permute-start(bf16[256,1536]{1,0:T(8,128)(2,1)S(1)} %get-tuple-element.496), channel_id=1, source_target_pairs={{3,2},{7,6},{11,10},{15,14},{19,18},{23,22},{27,26},{31,30}} | collective-permute-start | bytes 2359304 | tf_op jit(solution)/shard_map/ppermute | solution.py:132
  456.3 33.3 %collective-permute-start.32 = (bf16[256,1536]{1,0:T(8,128)(2,1)S(1)}, bf16[256,1536]{1,0:T(8,128)(2,1)S(1)}, u32[]{:S(2)}, u32[]{:S(2)}) collective-permute-start(bf16[256,1536]{1,0:T(8,128)(2,1)S(1)} %get-tuple-element.493), channel_id=1, source_target_pairs={{0,1},{1,2},{4,5},{5,6},{8,9},{9,10},{12,13},{13,14},{16,17},{17,1... | collective-permute-start | bytes 2359304 | tf_op jit(solution)/shard_map/ppermute | solution.py:131
  473.2 33.3 %collective-permute-start.38 = (bf16[256,1536]{1,0:T(8,128)(2,1)S(1)}, bf16[256,1536]{1,0:T(8,128)(2,1)S(1)}, u32[]{:S(2)}, u32[]{:S(2)}) collective-permute-start(bf16[256,1536]{1,0:T(8,128)(2,1)S(1)} %get-tuple-element.491), channel_id=1, source_target_pairs={{0,1},{1,2},{4,5},{5,6},{8,9},{9,10},{12,13},{13,14},{16,17},{17,1... | collective-permute-start | bytes 2359304 | tf_op jit(solution)/shard_map/ppermute | solution.py:131
  490.0 35.5 %collective-permute-start.34 = (bf16[256,1536]{1,0:T(8,128)(2,1)S(1)}, bf16[256,1536]{1,0:T(8,128)(2,1)}, u32[]{:S(2)}, u32[]{:S(2)}) collective-permute-start(bf16[256,1536]{1,0:T(8,128)(2,1)S(1)} %get-tuple-element.489), channel_id=1, source_target_pairs={{0,1},{1,2},{2,3},{4,5},{5,6},{6,7},{8,9},{9,10},{10,11},{12,13},{... | collective-permute-start | bytes 2359304 | tf_op jit(solution)/shard_map/ppermute | solution.py:131
  538.9 45.0 %collective-permute-start.49 = (bf16[272,1536]{1,0:T(8,128)(2,1)S(1)}, bf16[272,1536]{1,0:T(8,128)(2,1)S(1)}, u32[]{:S(2)}, u32[]{:S(2)}) collective-permute-start(bf16[272,1536]{1,0:T(8,128)(2,1)S(1)} %pad_maximum_fusion.12.refs_1_), channel_id=1, source_target_pairs={{0,1},{1,2},{2,3},{4,5},{5,6},{6,7},{8,9},{9,10},{10,11},{12,13},{... | collective-permute-start | bytes 2506760 | tf_op jit(solution)/shard_map/ppermute | solution.py:67
  543.4 40.5 %collective-permute-start.50 = (bf16[272,1536]{1,0:T(8,128)(2,1)S(1)}, bf16[272,1536]{1,0:T(8,128)(2,1)S(1)}, u32[]{:S(2)}, u32[]{:S(2)}) collective-permute-start(bf16[272,1536]{1,0:T(8,128)(2,1)S(1)} %pad_maximum_fusion.12.refs_1_), channel_id=1, source_target_pairs={{1,0},{2,1},{3,2},{5,4},{6,5},{7,6},{9,8},{10,9},{11,10},{13,12},{... | collective-permute-start | bytes 2506760 | tf_op jit(solution)/shard_map/ppermute | solution.py:68
  544.7 39.1 %collective-permute-start.45 = (bf16[256,1536]{1,0:T(8,128)(2,1)S(1)}, bf16[256,1536]{1,0:T(8,128)(2,1)S(1)}, u32[]{:S(2)}, u32[]{:S(2)}) collective-permute-start(bf16[256,1536]{1,0:T(8,128)(2,1)S(1)} %get-tuple-element.525.refs_0_), channel_id=1, source_target_pairs={{0,1},{1,2},{2,3},{4,5},{5,6},{6,7},{8,9},{9,10},{10,11},{12,13},{... | collective-permute-start | bytes 2359304 | tf_op jit(solution)/shard_map/ppermute | solution.py:67
  549.7 34.2 %collective-permute-start.46 = (bf16[256,1536]{1,0:T(8,128)(2,1)S(1)}, bf16[256,1536]{1,0:T(8,128)(2,1)S(1)}, u32[]{:S(2)}, u32[]{:S(2)}) collective-permute-start(bf16[256,1536]{1,0:T(8,128)(2,1)S(1)} %get-tuple-element.525.refs_0_), channel_id=1, source_target_pairs={{1,0},{2,1},{3,2},{5,4},{6,5},{7,6},{9,8},{10,9},{11,10},{13,12},{... | collective-permute-start | bytes 2359304 | tf_op jit(solution)/shard_map/ppermute | solution.py:68
  583.9 36.4 %collective-permute-start.53 = (bf16[272,1536]{1,0:T(8,128)(2,1)S(1)}, bf16[272,1536]{1,0:T(8,128)(2,1)S(1)}, u32[]{:S(2)}, u32[]{:S(2)}) collective-permute-start(bf16[272,1536]{1,0:T(8,128)(2,1)S(1)} %collective-permute-done.49.refs_3_), channel_id=1, source_target_pairs={{1,2},{2,3},{5,6},{6,7},{9,10},{10,11},{13,14},{14,15},{17,18},{18... | collective-permute-start | bytes 2506760 | tf_op jit(solution)/shard_map/ppermute | solution.py:67
  584.6 35.7 %collective-permute-start.54 = (bf16[272,1536]{1,0:T(8,128)(2,1)S(1)}, bf16[272,1536]{1,0:T(8,128)(2,1)S(1)}, u32[]{:S(2)}, u32[]{:S(2)}) collective-permute-start(bf16[272,1536]{1,0:T(8,128)(2,1)S(1)} %collective-permute-done.50.refs_2_.refs_4_), channel_id=1, source_target_pairs={{1,0},{2,1},{5,4},{6,5},{9,8},{10,9},{13,12},{14,13},{17,16},{18,1... | collective-permute-start | bytes 2506760 | tf_op jit(solution)/shard_map/ppermute | solution.py:68
  585.9 34.3 %collective-permute-start.47 = (bf16[256,1536]{1,0:T(8,128)(2,1)S(1)}, bf16[256,1536]{1,0:T(8,128)(2,1)S(1)}, u32[]{:S(2)}, u32[]{:S(2)}) collective-permute-start(bf16[256,1536]{1,0:T(8,128)(2,1)S(1)} %collective-permute-done.45.refs_1_), channel_id=1, source_target_pairs={{1,2},{2,3},{5,6},{6,7},{9,10},{10,11},{13,14},{14,15},{17,18},{18... | collective-permute-start | bytes 2359304 | tf_op jit(solution)/shard_map/ppermute | solution.py:67
  586.7 33.6 %collective-permute-start.48 = (bf16[256,1536]{1,0:T(8,128)(2,1)S(1)}, bf16[256,1536]{1,0:T(8,128)(2,1)S(1)}, u32[]{:S(2)}, u32[]{:S(2)}) collective-permute-start(bf16[256,1536]{1,0:T(8,128)(2,1)S(1)} %collective-permute-done.46.refs_0_.refs_1_), channel_id=1, source_target_pairs={{1,0},{2,1},{5,4},{6,5},{9,8},{10,9},{13,12},{14,13},{17,16},{18,1... | collective-permute-start | bytes 2359304 | tf_op jit(solution)/shard_map/ppermute | solution.py:68
  620.3 39.0 %collective-permute-start.55 = (bf16[272,1536]{1,0:T(8,128)(2,1)S(1)}, bf16[272,1536]{1,0:T(8,128)(2,1)S(1)}, u32[]{:S(2)}, u32[]{:S(2)}) collective-permute-start(bf16[272,1536]{1,0:T(8,128)(2,1)S(1)} %collective-permute-done.53.refs_5_.refs_6_), channel_id=1, source_target_pairs={{2,3},{6,7},{10,11},{14,15},{18,19},{22,23},{26,27},{30,31}} | collective-permute-start | bytes 2506760 | tf_op jit(solution)/shard_map/ppermute | solution.py:67
  621.0 38.3 %collective-permute-start.56 = (bf16[272,1536]{1,0:T(8,128)(2,1)S(1)}, bf16[272,1536]{1,0:T(8,128)(2,1)S(1)}, u32[]{:S(2)}, u32[]{:S(2)}) collective-permute-start(bf16[272,1536]{1,0:T(8,128)(2,1)S(1)} %collective-permute-done.54.refs_3_.refs_5_), channel_id=1, source_target_pairs={{1,0},{5,4},{9,8},{13,12},{17,16},{21,20},{25,24},{29,28}} | collective-permute-start | bytes 2506760 | tf_op jit(solution)/shard_map/ppermute | solution.py:68
  622.3 34.5 %collective-permute-start.51 = (bf16[256,1536]{1,0:T(8,128)(2,1)S(1)}, bf16[256,1536]{1,0:T(8,128)(2,1)S(1)}, u32[]{:S(2)}, u32[]{:S(2)}) collective-permute-start(bf16[256,1536]{1,0:T(8,128)(2,1)S(1)} %collective-permute-done.47.refs_2_), channel_id=1, source_target_pairs={{2,3},{6,7},{10,11},{14,15},{18,19},{22,23},{26,27},{30,31}} | collective-permute-start | bytes 2359304 | tf_op jit(solution)/shard_map/ppermute | solution.py:67
  623.0 36.3 %collective-permute-start.52 = (bf16[256,1536]{1,0:T(8,128)(2,1)S(1)}, bf16[256,1536]{1,0:T(8,128)(2,1)S(1)}, u32[]{:S(2)}, u32[]{:S(2)}) collective-permute-start(bf16[256,1536]{1,0:T(8,128)(2,1)S(1)} %collective-permute-done.48.refs_0_.refs_1_), channel_id=1, source_target_pairs={{1,0},{5,4},{9,8},{13,12},{17,16},{21,20},{25,24},{29,28}} | collective-permute-start | bytes 2359304 | tf_op jit(solution)/shard_map/ppermute | solution.py:68
  696.3 37.6 %collective-permute-start.57 = (bf16[512,1536]{1,0:T(8,128)(2,1)}, bf16[512,1536]{1,0:T(8,128)(2,1)S(1)}, u32[]{:S(2)}, u32[]{:S(2)}) collective-permute-start(bf16[512,1536]{1,0:T(8,128)(2,1)} %get-tuple-element.475), channel_id=1, source_target_pairs={{0,1},{4,5},{8,9},{12,13},{16,17},{20,21},{24,25},{28,29}} | collective-permute-start | bytes 4718600 | tf_op jit(solution)/shard_map/ppermute | solution.py:131
  802.2 345.3 %all-gather.9.cloned.1.call-start = ((), (), s32[]{:S(2)}) async-start(), calls=%async_computation.4 | async-start | bytes 2211840 | tf_op jit(solution)/shard_map/all_gather | solution.py:1119
  806.0 37.8 %collective-permute-start.71 = (f32[1,1]{1,0:T(1,128)}, f32[1,1]{1,0:T(1,128)}, u32[]{:S(2)}, u32[]{:S(2)}) collective-permute-start(f32[1,1]{1,0:T(1,128)} %bitcast.82), channel_id=1, source_target_pairs={{0,1},{1,0},{2,3},{3,2},{4,5},{5,4},{6,7},{7,6},{8,9},{9,8},{10,11... | collective-permute-start | bytes 20 | tf_op jit(solution)/shard_map/ppermute | solution.py:221
  843.7 34.7 %collective-permute-start.69 = (bf16[384,512]{1,0:T(8,128)(2,1)S(1)}, bf16[384,512]{1,0:T(8,128)(2,1)S(1)}, u32[]{:S(2)}, u32[]{:S(2)}) collective-permute-start(bf16[384,512]{1,0:T(8,128)(2,1)S(1)} %get-tuple-element.518), channel_id=1, source_target_pairs={{2,0},{3,1},{6,4},{7,5},{10,8},{11,9},{14,12},{15,13},{18,16},{19,... | collective-permute-start | bytes 1179656 | tf_op jit(solution)/shard_map/ppermute | solution.py:216
  845.8 32.7 %collective-permute-start.70 = (bf16[384,512]{1,0:T(8,128)(2,1)S(1)}, bf16[384,512]{1,0:T(8,128)(2,1)S(1)}, u32[]{:S(2)}, u32[]{:S(2)}) collective-permute-start(bf16[384,512]{1,0:T(8,128)(2,1)S(1)} %get-tuple-element.517), channel_id=1, source_target_pairs={{3,0},{7,4},{11,8},{15,12},{19,16},{23,20},{27,24},{31,28}} | collective-permute-start | bytes 1179656 | tf_op jit(solution)/shard_map/ppermute | solution.py:216
  878.5 69.4 %collective-permute-start.72 = (bf16[2,192,768]{2,1,0:T(8,128)(2,1)}, bf16[2,192,768]{2,1,0:T(8,128)(2,1)}, u32[]{:S(2)}, u32[]{:S(2)}) collective-permute-start(bf16[2,192,768]{2,1,0:T(8,128)(2,1)} %add_convert_fusion.9), channel_id=1, source_target_pairs={{0,8},{4,12},{8,0},{12,4},{16,24},{20,28},{24,16},{28,20},{1,9},{5... | collective-permute-start | bytes 1769480 | tf_op jit(solution)/shard_map/ppermute | solution.py:221
  880.9 67.0 %collective-permute-start.73 = (bf16[2,192,768]{2,1,0:T(8,128)(2,1)}, bf16[2,192,768]{2,1,0:T(8,128)(2,1)}, u32[]{:S(2)}, u32[]{:S(2)}) collective-permute-start(bf16[2,192,768]{2,1,0:T(8,128)(2,1)} %add_convert_fusion.8), channel_id=1, source_target_pairs={{0,16},{4,20},{8,24},{12,28},{16,0},{20,4},{24,8},{28,12},{1,17},{... | collective-permute-start | bytes 1769480 | tf_op jit(solution)/shard_map/ppermute | solution.py:221
  888.0 59.9 %collective-permute-start.74 = (f32[1,1]{1,0:T(1,128)}, f32[1,1]{1,0:T(1,128)}, u32[]{:S(2)}, u32[]{:S(2)}) collective-permute-start(f32[1,1]{1,0:T(1,128)} %add.632), channel_id=1, source_target_pairs={{0,2},{1,3},{2,0},{3,1},{4,6},{5,7},{6,4},{7,5},{8,10},{9,11},{10,... | collective-permute-start | bytes 20 | tf_op jit(solution)/shard_map/ppermute | solution.py:221
  976.3 46.9 %collective-permute-start.79 = (bf16[304,1536]{1,0:T(8,128)(2,1)}, bf16[304,1536]{1,0:T(8,128)(2,1)}, u32[]{:S(2)}, u32[]{:S(2)}) collective-permute-start(bf16[304,1536]{1,0:T(8,128)(2,1)} %pad_maximum_fusion.9), channel_id=1, source_target_pairs={{3,2},{7,6},{11,10},{15,14},{19,18},{23,22},{27,26},{31,30}} | collective-permute-start | bytes 2801672 | tf_op jit(solution)/shard_map/ppermute | solution.py:132
  980.9 42.3 %collective-permute-start.78 = (bf16[304,1536]{1,0:T(8,128)(2,1)}, bf16[304,1536]{1,0:T(8,128)(2,1)}, u32[]{:S(2)}, u32[]{:S(2)}) collective-permute-start(bf16[304,1536]{1,0:T(8,128)(2,1)} %pad_maximum_fusion.8), channel_id=1, source_target_pairs={{0,1},{4,5},{8,9},{12,13},{16,17},{20,21},{24,25},{28,29}} | collective-permute-start | bytes 2801672 | tf_op jit(solution)/shard_map/ppermute | solution.py:131
  983.1 33.2 %collective-permute-start.80 = (bf16[256,1536]{1,0:T(8,128)(2,1)}, bf16[256,1536]{1,0:T(8,128)(2,1)}, u32[]{:S(2)}, u32[]{:S(2)}) collective-permute-start(bf16[256,1536]{1,0:T(8,128)(2,1)} %get-tuple-element.515), channel_id=1, source_target_pairs={{0,1},{4,5},{8,9},{12,13},{16,17},{20,21},{24,25},{28,29}} | collective-permute-start | bytes 2359304 | tf_op jit(solution)/shard_map/ppermute | solution.py:131
  1025.2 35.2 %collective-permute-start.83 = (bf16[304,1536]{1,0:T(8,128)(2,1)S(1)}, bf16[304,1536]{1,0:T(8,128)(2,1)S(1)}, u32[]{:S(2)}, u32[]{:S(2)}) collective-permute-start(bf16[304,1536]{1,0:T(8,128)(2,1)S(1)} %get-tuple-element.552), channel_id=1, source_target_pairs={{0,1},{1,2},{4,5},{5,6},{8,9},{9,10},{12,13},{13,14},{16,17},{17,1... | collective-permute-start | bytes 2801672 | tf_op jit(solution)/shard_map/ppermute | solution.py:131
  1027.9 32.5 %collective-permute-start.84 = (bf16[304,1536]{1,0:T(8,128)(2,1)S(1)}, bf16[304,1536]{1,0:T(8,128)(2,1)S(1)}, u32[]{:S(2)}, u32[]{:S(2)}) collective-permute-start(bf16[304,1536]{1,0:T(8,128)(2,1)S(1)} %get-tuple-element.551), channel_id=1, source_target_pairs={{2,1},{3,2},{6,5},{7,6},{10,9},{11,10},{14,13},{15,14},{18,17},{19... | collective-permute-start | bytes 2801672 | tf_op jit(solution)/shard_map/ppermute | solution.py:132
  1028.8 43.9 %collective-permute-start.82 = (bf16[2,192,681]{2,1,0:T(8,128)(2,1)S(1)}, bf16[2,192,681]{2,1,0:T(8,128)(2,1)S(1)}, u32[]{:S(2)}, u32[]{:S(2)}) collective-permute-start(bf16[2,192,681]{2,1,0:T(8,128)(2,1)S(1)} %add_convert_fusion.7), channel_id=1, source_target_pairs={{0,8},{4,12},{8,0},{12,4},{16,24},{20,28},{24,16},{28,20},{1,9},{5... | collective-permute-start | bytes 1569032 | tf_op jit(solution)/shard_map/ppermute | solution.py:221
  1040.6 33.2 %collective-permute-start.89 = (bf16[256,1536]{1,0:T(8,128)(2,1)S(1)}, bf16[256,1536]{1,0:T(8,128)(2,1)S(1)}, u32[]{:S(2)}, u32[]{:S(2)}) collective-permute-start(bf16[256,1536]{1,0:T(8,128)(2,1)S(1)} %add_convert_fusion.5), channel_id=1, source_target_pairs={{1,0},{2,1},{3,2},{5,4},{6,5},{7,6},{9,8},{10,9},{11,10},{13,12},{... | collective-permute-start | bytes 2359304 | tf_op jit(solution)/shard_map/ppermute | solution.py:132
  1042.1 35.2 %collective-permute-start.88 = (bf16[256,1536]{1,0:T(8,128)(2,1)S(1)}, bf16[256,1536]{1,0:T(8,128)(2,1)S(1)}, u32[]{:S(2)}, u32[]{:S(2)}) collective-permute-start(bf16[256,1536]{1,0:T(8,128)(2,1)S(1)} %add_convert_fusion.6), channel_id=1, source_target_pairs={{0,1},{1,2},{2,3},{4,5},{5,6},{6,7},{8,9},{9,10},{10,11},{12,13},{... | collective-permute-start | bytes 2359304 | tf_op jit(solution)/shard_map/ppermute | solution.py:131
  (205 other events, 3540.6 us)
Sparse Core Ops, SparseCore 0:
  13.0 51.5 all-gather.4
  66.5 219.0 all-gather.6
  802.3 302.3 reduce-scatter.1
  1106.6 40.7 all-gather.8
